TPU v7x, 32 devices: a whole 2x2x4 slice. The times are simulated.
32 devices in a mesh: cam: 8 (over y, x, core), head: 4 (over z).
Axes of the slice: x: 2, y: 2, z: 4, core: 2. Of those that a mesh axis runs over, the one named last changes fastest.
Arguments:
- queries: bfloat16 [16384, 1024], P('cam', 'head'), may hold values from -24 to 24
- keys: bfloat16 [16384, 1024], P('cam', 'head'), may hold values from -24 to 24
- values: bfloat16 [16384, 1024], P('cam', 'head'), may hold values from -6 to 6
- rates: float32 [16384, 4], P('cam', 'head'), may hold values from 0.1 to 1
- w_one: bfloat16 [4, 256, 256], P('head'), may hold values from -0.375 to 0.375
- w_three: bfloat16 [4, 256, 256], P('head'), may hold values from -0.375 to 0.375
- w_two: bfloat16 [4, 256, 256], P('head'), may hold values from -0.375 to 0.375
- gain: float32 [1024], P('head'), may hold values from 0.5 to 1.5
- order: int32 [8, 2048], P('cam'), may hold values from 0 to 2047, as said below
Outputs:
- mixed: bfloat16 [16384, 1024], P('cam', 'head')
Inputs may be any that keep to these rules, and one draw needn't show every extreme that they name: `order`: each row is an ordering of 0 to 2047; every timestamp holds exactly 32 tokens of every camera.
All inputs are finite; a program needn't handle non-finite values.
Results may differ from a plain program's by a relative error of at most 0.0085.
Values may be sent and summed in bfloat16 or wider, within the bound.
No kernel may reach another device: no remote copies, remote signals or barrier semaphores. Data moves between devices by JAX's collectives and lax.ppermute only.
A program may use at most 64 MiB of HBM per device.

v0:
```python
import jax
import jax.numpy as jnp
from jax import lax
from jax.sharding import PartitionSpec as P

PATCHES = 32


EPSILON = 1e-06


def hidden_parts(tokens, first, third):
    h_one = jnp.einsum("nhd,hkd->nhk", tokens, first, preferred_element_type=jnp.float32)
    h_three = jnp.einsum("nhd,hkd->nhk", tokens, third, preferred_element_type=jnp.float32)
    return (h_one, h_three)


def gradients(key_rows, value_rows, rates, first, third, second):
    h_one, h_three = hidden_parts(key_rows, first, third)
    sigma = jax.nn.sigmoid(h_one)
    active = (h_one * sigma * h_three).astype(jnp.bfloat16)
    error = (-rates[:, :, None] * value_rows.astype(jnp.float32)).astype(jnp.bfloat16)
    grad_second = jnp.einsum("nhd,nhk->hdk", error, active, preferred_element_type=jnp.float32)
    back = jnp.einsum("nhd,hdk->nhk", error, second, preferred_element_type=jnp.float32)
    back_one = (back * h_three * sigma * (1.0 + h_one * (1.0 - sigma))).astype(jnp.bfloat16)
    back_three = (back * h_one * sigma).astype(jnp.bfloat16)
    grad_first = jnp.einsum("nhk,nhd->hkd", back_one, key_rows, preferred_element_type=jnp.float32)
    grad_third = jnp.einsum(
        "nhk,nhd->hkd", back_three, key_rows, preferred_element_type=jnp.float32
    )
    return (grad_first, grad_third, grad_second)


def weight_scale(weight):
    wf = weight.astype(jnp.float32)
    return jnp.sqrt(jnp.mean(wf * wf, axis=(1, 2)))


def renew(weight, grad, weight_rms, grad_total, entries):
    wf = weight.astype(jnp.float32)
    scale = weight_rms / jnp.sqrt(grad_total / entries + EPSILON)
    moved = wf - scale[:, None, None] * grad
    ratio = jnp.sqrt(jnp.sum(wf * wf, axis=-1, keepdims=True)) / jnp.sqrt(
        jnp.sum(moved * moved, axis=-1, keepdims=True) + EPSILON
    )
    return (moved * ratio).astype(jnp.bfloat16)


def attend(parts, local, head_size):
    query_all, key_all, value_all = parts
    cams, frames, patches, width = query_all.shape

    def one_frame(blocks):
        query_block, key_block, value_block = blocks
        query_rows = query_block.reshape(cams * patches, local, head_size)
        key_rows = key_block.reshape(cams * patches, local, head_size)
        value_rows = value_block.reshape(cams * patches, local, head_size)
        scores = jnp.einsum(
            "qhd,khd->hqk", query_rows, key_rows, preferred_element_type=jnp.float32
        ) * head_size ** (-0.5)
        scores = scores - jnp.max(scores, axis=-1, keepdims=True)
        expo = jnp.exp(scores)
        probs = (expo / jnp.sum(expo, axis=-1, keepdims=True)).astype(jnp.bfloat16)
        result = jnp.einsum("hqk,khd->qhd", probs, value_rows, preferred_element_type=jnp.float32)
        return result.astype(jnp.bfloat16).reshape(cams, patches, width)

    moved = (
        jnp.moveaxis(query_all, 1, 0),
        jnp.moveaxis(key_all, 1, 0),
        jnp.moveaxis(value_all, 1, 0),
    )
    return jnp.moveaxis(lax.map(one_frame, moved), 0, 1)


def per_device(queries, keys, values, rates, w_one, w_three, w_two, gain, order):
    count, width = queries.shape
    local = w_one.shape[0]
    head_size = w_one.shape[2]
    cams = lax.axis_size("cam")
    owned = count // (cams * PATCHES)
    slots = order[0]
    inverse = jnp.zeros((count,), jnp.int32).at[slots].set(jnp.arange(count, dtype=jnp.int32))
    sorted_query = jnp.take(queries, inverse, axis=0).reshape(cams, owned, PATCHES, width)
    sorted_keys = jnp.take(keys, inverse, axis=0).reshape(cams, owned, PATCHES, width)
    sorted_value = jnp.take(values, inverse, axis=0).reshape(cams, owned, PATCHES, width)
    arrived = (
        lax.all_to_all(sorted_query, "cam", split_axis=0, concat_axis=0, tiled=True),
        lax.all_to_all(sorted_keys, "cam", split_axis=0, concat_axis=0, tiled=True),
        lax.all_to_all(sorted_value, "cam", split_axis=0, concat_axis=0, tiled=True),
    )
    returned = lax.all_to_all(
        attend(arrived, local, head_size), "cam", split_axis=0, concat_axis=0, tiled=True
    )
    attended = jnp.take(returned.reshape(count, width), slots, axis=0)
    key_rows = keys.reshape(count, local, head_size)
    value_rows = values.reshape(count, local, head_size)
    grad_first, grad_third, grad_second = gradients(
        key_rows, value_rows, rates, w_one, w_three, w_two
    )
    weights = (w_one, w_three, w_two)
    scales = tuple((weight_scale(weight) for weight in weights))
    summed = lax.psum((grad_first, grad_third, grad_second), "cam")
    renewed = []
    for weight, grad, scale_now in zip(weights, summed, scales):
        total = jnp.sum(grad * grad, axis=(1, 2))
        renewed.append(renew(weight, grad, scale_now, total, weight.shape[1] * weight.shape[2]))
    new_first, new_third, new_second = renewed
    query_rows = queries.reshape(count, local, head_size)
    q_one, q_three = hidden_parts(query_rows, new_first, new_third)
    q_active = (q_one * jax.nn.sigmoid(q_one) * q_three).astype(jnp.bfloat16)
    readout = jnp.einsum(
        "nhk,hdk->nhd", q_active, new_second, preferred_element_type=jnp.float32
    ).reshape(count, width)
    total_sq = lax.psum(jnp.sum(readout * readout, axis=1), "head")
    full_width = width * lax.axis_size("head")
    inv_norm = 1.0 / jnp.sqrt(total_sq / full_width + EPSILON)
    mixed = readout * inv_norm[:, None] * gain[None, :] + attended.astype(jnp.float32)
    return mixed.astype(jnp.bfloat16)


def solution(mesh):
    in_specs = (
        P("cam", "head"),
        P("cam", "head"),
        P("cam", "head"),
        P("cam", "head"),
        P("head", None, None),
        P("head", None, None),
        P("head", None, None),
        P("head"),
        P("cam", None),
    )
    out_specs = P("cam", "head")
    return jax.shard_map(
        per_device, mesh=mesh, in_specs=in_specs, out_specs=out_specs, check_vma=False
    )
```

profile of v0, /device:TPU:0, one launch (start us, length us, event | category | flops | bytes accessed | tf_op | source)
XLA Modules:
  0.0 210.7 jit_solution(13549510900019919728)
XLA Ops:
  7.3 8.0 %scatter_custom_fusion = s32[2048]{0:T(1024)S(1)} fusion(s32[2048]{0:T(1024)S(1)} %bitcast.143, s32[2048]{0:T(1024)S(1)} %iota.3, s32[]{:T(128)} %copy.48), kind=kCustom, calls=%fused_computation.83 | custom fusion | bytes 8196 | tf_op jit(solution)/shard_map/scatter | solution.py:82
  15.4 8.1 %gather_fusion = bf16[2048,256]{1,0:T(8,128)(2,1)S(1)} fusion(bf16[2048,256]{1,0:T(8,128)(2,1)} %param.15, s32[2048]{0:T(1024)S(1)} %fusion.34), kind=kCustom, calls=%fused_computation.clone | custom fusion | bytes 2105344 | tf_op jit(solution)/shard_map/jit(_take)/gather | solution.py:85
  23.5 9.0 %gather_fusion.1 = bf16[2048,256]{1,0:T(8,128)(2,1)} fusion(bf16[2048,256]{1,0:T(8,128)(2,1)S(1)} %copy-done.2, s32[2048]{0:T(1024)S(1)} %fusion.34), kind=kCustom, calls=%fused_computation.1.clone | custom fusion | bytes 2105344 | tf_op jit(solution)/shard_map/jit(_take)/gather | solution.py:83
  32.5 9.0 %gather_fusion.2 = bf16[2048,256]{1,0:T(8,128)(2,1)} fusion(bf16[2048,256]{1,0:T(8,128)(2,1)S(1)} %copy-done, s32[2048]{0:T(1024)S(1)} %fusion.34), kind=kCustom, calls=%fused_computation.2.clone | custom fusion | bytes 2105344 | tf_op jit(solution)/shard_map/jit(_take)/gather | solution.py:84
  41.6 3.1 %broadcast_select_fusion = (bf16[2048,256]{1,0:T(8,128)(2,1)}, bf16[2048,256]{1,0:T(8,128)(2,1)}, bf16[2048,256]{1,0:T(8,128)(2,1)}) fusion(bf16[2048,256]{1,0:T(8,128)(2,1)} %gather_fusion.2, pred[2048]{0:T(1024)(128)(4,1)S(1)} %compare_and_fusion.1, bf16[2048,256]{1,0:T(8,128)(2,1)} %gather_fusion.1, bf16[2048,256]{1,0:T(8,128)(2,1)S(1)} %gather_fusion), kind=kLoop, calls=%fused_computation.39 | loop fusion | flops 1572864 | bytes 6293504 | tf_op jit(solution)/shard_map/jit(_take)/select_n | solution.py:84
  44.7 5.3 %all-to-all-start = ((bf16[8,8,32,256]{3,2,1,0:T(8,128)(2,1)}), bf16[8,8,32,256]{3,2,1,0:T(8,128)(2,1)}, u32[]{:S(2)}, u32[]{:S(2)}) async-start(bf16[8,8,32,256]{3,2,1,0:T(8,128)(2,1)} %bitcast.44), calls=%async_computation | async-start | bytes 2097152 | tf_op jit(solution)/shard_map/all_to_all | solution.py:89
  52.8 1.8 convolution_bitcast_fusion.8
  54.6 1.4 convolution_bitcast_fusion.6
  56.0 1.7 convolution_bitcast_fusion.7
  60.3 5.2 %all-to-all-done = bf16[8,8,32,256]{3,2,1,0:T(8,128)(2,1)} async-done(((bf16[8,8,32,256]{3,2,1,0:T(8,128)(2,1)}), bf16[8,8,32,256]{3,2,1,0:T(8,128)(2,1)}, u32[]{:S(2)}, u32[]{:S(2)}) %all-to-all-start) | async-done | bytes 1048608 | tf_op jit(solution)/shard_map/all_to_all | solution.py:89
  65.5 4.2 %all-to-all-start.1 = ((bf16[8,8,32,256]{3,2,1,0:T(8,128)(2,1)}), bf16[8,8,32,256]{3,2,1,0:T(8,128)(2,1)}, u32[]{:S(2)}, u32[]{:S(2)}) async-start(bf16[8,8,32,256]{3,2,1,0:T(8,128)(2,1)} %bitcast.46), calls=%async_computation.1 | async-start | bytes 2097152 | tf_op jit(solution)/shard_map/all_to_all | solution.py:87
  71.1 47.8 %all-reduce.3.cloned.1.call-done = (f32[1,256,256]{2,1,0:T(8,128)}, f32[1,256,256]{2,1,0:T(8,128)}, f32[1,256,256]{2,1,0:T(8,128)}) async-done(((f32[1,256,256]{2,1,0:T(8,128)}, f32[1,256,256]{2,1,0:T(8,128)}, f32[1,256,256]{2,1,0:T(8,128)}), (f32[1,256,256]{2,1,0:T(8,128)}, f32[1,256,256]{2,1,0:T(8,128)}, f32[1,256,256]{2,1,0:T(8,128)})) %all-reduce.3.cloned.1.call-update) | async-done | bytes 786448 | tf_op jit(solution)/shard_map/psum | solution.py:102
  118.9 1.7 multiply_reduce_fusion.6
  121.3 1.6 multiply_reduce_fusion.4
  123.6 1.6 multiply_reduce_fusion.2
  125.9 4.3 %all-to-all-start.2 = ((bf16[8,8,32,256]{3,2,1,0:T(8,128)(2,1)}), bf16[8,8,32,256]{3,2,1,0:T(8,128)(2,1)}, u32[]{:S(2)}, u32[]{:S(2)}) async-start(bf16[8,8,32,256]{3,2,1,0:T(8,128)(2,1)} %bitcast.48), calls=%async_computation.2 | async-start | bytes 2097152 | tf_op jit(solution)/shard_map/all_to_all | solution.py:88
  131.7 13.8 %all-to-all-done.2 = bf16[8,8,32,256]{3,2,1,0:T(8,128)(2,1)} async-done(((bf16[8,8,32,256]{3,2,1,0:T(8,128)(2,1)}), bf16[8,8,32,256]{3,2,1,0:T(8,128)(2,1)}, u32[]{:S(2)}, u32[]{:S(2)}) %all-to-all-start.2) | async-done | bytes 1048608 | tf_op jit(solution)/shard_map/all_to_all | solution.py:88
  145.5 25.2 %while.10 = (s32[]{:T(128)}, bf16[8,8,32,256]{3,2,0,1:T(8,128)(2,1)}, bf16[8,8,32,256]{3,2,0,1:T(8,128)(2,1)}, bf16[8,8,32,256]{3,2,0,1:T(8,128)(2,1)}, bf16[8,8,32,256]{3,2,0,1:T(8,128)(2,1)}, /*index=5*/s32[]{:T(128)}) while((s32[]{:T(128)}, bf16[8,8,32,256]{3,2,0,1:T(8,128)(2,1)}, bf16[8,8,32,256]{3,2,0,1:T(8,128)(2,1)}, ...), condition=%wide.region_21.23_spmd, body=%wide.region_18.22_spmd.sunk | while | flops 67632640 | bytes 2365005 | solution.py:72
  145.5 1.0 constant_dynamic-slice_fusion.6
  148.7 1.0 constant_dynamic-slice_fusion.6
  151.9 1.0 constant_dynamic-slice_fusion.6
  155.0 1.0 constant_dynamic-slice_fusion.6
  158.2 1.0 constant_dynamic-slice_fusion.6
  161.3 1.0 constant_dynamic-slice_fusion.6
  164.5 1.0 constant_dynamic-slice_fusion.6
  170.8 3.6 %all-to-all-start.3 = ((bf16[8,8,32,256]{3,2,1,0:T(8,128)(2,1)}), bf16[8,8,32,256]{3,2,1,0:T(8,128)(2,1)S(1)}, u32[]{:S(2)}, u32[]{:S(2)}) async-start(bf16[8,8,32,256]{3,2,1,0:T(8,128)(2,1)} %bitcast.50), calls=%async_computation.3 | async-start | bytes 2097152 | tf_op jit(solution)/shard_map/all_to_all | solution.py:91
  174.3 1.8 convolution_bitcast_fusion.2
  176.2 4.2 %multiply_reduce_fusion = (f32[2048]{0:T(1024)S(1)}, f32[2048,256]{0,1:T(8,128)}) fusion(bf16[2048,256]{1,0:T(8,128)(2,1)S(1)} %copy-done.2, f32[2048,1,256]{0,2,1:T(8,128)} %convolution_bitcast_fusion.2, f32[1,256,256]{2,1,0:T(8,128)} %get-tuple-element.57, bf16[1,256,256]{2,1,0:T(8,128)(2,1)} %param.18, f32[256]{0:T(256)} %rsqrt_multiply_fusion, ...), kind=kOutput, calls=%fused_computation.26 | convolution fusion | flops 541718528 | bytes 6039560 | tf_op jit(solution)/shard_map/nhk,hdk->nhd/dot_general | solution.py:111
  180.4 11.8 %psum.31 = f32[2048]{0:T(1024)S(1)} all-reduce(f32[2048]{0:T(1024)S(1)} %get-tuple-element.65), channel_id=1, replica_groups=mesh['cam'=8,'head'=4] {'head'}, use_global_device_ids=true, to_apply=%region_16.17 | all-reduce | flops 2048 | bytes 16384 | tf_op jit(solution)/shard_map/psum | solution.py:114
  192.3 7.5 %gather_fusion.3 = bf16[2048,256]{1,0:T(8,128)(2,1)S(1)} fusion(bf16[2048,256]{1,0:T(8,128)(2,1)S(1)} %bitcast.134, s32[2048]{0:T(1024)S(1)} %fusion.35), kind=kCustom, calls=%fused_computation.3.clone | custom fusion | bytes 2105344 | tf_op jit(solution)/shard_map/jit(_take)/gather | solution.py:94
  200.5 2.1 add_convert_fusion
  202.5 1.3 copy.30
  (90 shorter events, 26.0 us)
Async XLA Ops:
  6.5 26.0 %copy-start = (bf16[2048,256]{1,0:T(8,128)(2,1)S(1)}, bf16[2048,256]{1,0:T(8,128)(2,1)}, u32[]{:S(2)}) copy-start(bf16[2048,256]{1,0:T(8,128)(2,1)} %param.14) | copy-start | bytes 3145732
  15.4 8.1 %copy-start.2 = (bf16[2048,256]{1,0:T(8,128)(2,1)S(1)}, bf16[2048,256]{1,0:T(8,128)(2,1)}, u32[]{:S(2)}) copy-start(bf16[2048,256]{1,0:T(8,128)(2,1)} %param.13) | copy-start | bytes 3145732
  44.7 5.4 %copy-start.10 = (f32[2048,1]{0,1:T(1,128)S(1)}, f32[2048,1]{0,1:T(1,128)}, u32[]{:S(2)}) copy-start(f32[2048,1]{0,1:T(1,128)} %param.16) | copy-start | bytes 24580
  44.7 5.4 %copy-start.4 = (bf16[1,256,256]{2,1,0:T(8,128)(2,1)S(1)}, bf16[1,256,256]{2,1,0:T(8,128)(2,1)}, u32[]{:S(2)}) copy-start(bf16[1,256,256]{2,1,0:T(8,128)(2,1)} %param.17) | copy-start | bytes 393220
  44.7 20.8 %all-to-all-start = ((bf16[8,8,32,256]{3,2,1,0:T(8,128)(2,1)}), bf16[8,8,32,256]{3,2,1,0:T(8,128)(2,1)}, u32[]{:S(2)}, u32[]{:S(2)}) async-start(bf16[8,8,32,256]{3,2,1,0:T(8,128)(2,1)} %bitcast.44), calls=%async_computation | async-start | bytes 2097152 | tf_op jit(solution)/shard_map/all_to_all | solution.py:89
  50.0 0.9 copy-start.5
  50.0 68.9 %all-reduce.3.cloned.1.call-start = ((), (), s32[]{:S(2)}) async-start(), calls=%async_computation.4 | async-start | bytes 1572864 | tf_op jit(solution)/shard_map/psum | solution.py:102
  50.9 1.2 copy-start.1
  50.9 1.2 copy-start.6
  57.7 13.3 %copy-start.9 = (s32[1,2048]{1,0:T(1,128)S(1)}, s32[1,2048]{1,0:T(1,128)}, u32[]{:S(2)}) copy-start(s32[1,2048]{1,0:T(1,128)} %param.21) | copy-start | bytes 24580
  65.5 60.3 %all-to-all-start.1 = ((bf16[8,8,32,256]{3,2,1,0:T(8,128)(2,1)}), bf16[8,8,32,256]{3,2,1,0:T(8,128)(2,1)}, u32[]{:S(2)}, u32[]{:S(2)}) async-start(bf16[8,8,32,256]{3,2,1,0:T(8,128)(2,1)} %bitcast.46), calls=%async_computation.1 | async-start | bytes 2097152 | tf_op jit(solution)/shard_map/all_to_all | solution.py:87
  118.9 11.2 %copy-start.8 = (f32[1,256,256]{2,1,0:T(8,128)S(1)}, f32[1,256,256]{2,1,0:T(8,128)}, u32[]{:S(2)}) copy-start(f32[1,256,256]{2,1,0:T(8,128)} %get-tuple-element.57) | copy-start | bytes 786436
  118.9 11.4 %copy-start.3 = (f32[1,256,256]{2,1,0:T(8,128)S(1)}, f32[1,256,256]{2,1,0:T(8,128)}, u32[]{:S(2)}) copy-start(f32[1,256,256]{2,1,0:T(8,128)} %get-tuple-element.55) | copy-start | bytes 786436
  118.9 11.4 %copy-start.7 = (f32[1,256,256]{2,1,0:T(8,128)S(1)}, f32[1,256,256]{2,1,0:T(8,128)}, u32[]{:S(2)}) copy-start(f32[1,256,256]{2,1,0:T(8,128)} %get-tuple-element.56) | copy-start | bytes 786436
  125.9 19.7 %all-to-all-start.2 = ((bf16[8,8,32,256]{3,2,1,0:T(8,128)(2,1)}), bf16[8,8,32,256]{3,2,1,0:T(8,128)(2,1)}, u32[]{:S(2)}, u32[]{:S(2)}) async-start(bf16[8,8,32,256]{3,2,1,0:T(8,128)(2,1)} %bitcast.48), calls=%async_computation.2 | async-start | bytes 2097152 | tf_op jit(solution)/shard_map/all_to_all | solution.py:88
  170.8 21.5 %all-to-all-start.3 = ((bf16[8,8,32,256]{3,2,1,0:T(8,128)(2,1)}), bf16[8,8,32,256]{3,2,1,0:T(8,128)(2,1)S(1)}, u32[]{:S(2)}, u32[]{:S(2)}) async-start(bf16[8,8,32,256]{3,2,1,0:T(8,128)(2,1)} %bitcast.50), calls=%async_computation.3 | async-start | bytes 2097152 | tf_op jit(solution)/shard_map/all_to_all | solution.py:91
  199.8 0.7 copy-start.11
Sparse Core Ops, SparseCore 0:
  57.9 60.9 all-reduce.2
where the time goes:
time: 212 us; the launch traced here: 211 us
  waiting for transfers between devices  66.9 us (32%)
  local copies, waits for them, and re-layouts  65.4 us (31%)
  between operations  17.5 us (8%)
  starting transfers between devices  17.4 us (8%)
  matrix products  16.5 us (8%)
  other arithmetic  15.1 us (7%)
  blocking collectives  11.8 us (6%)
    psum x1, waiting for transfers between devices, per_device(): summed = lax.psum((grad_first, grad_third, grad_second), 'cam')  47.8 us
    dynamic_slice x16, local copies, waits for them, and re-layouts, attend(): return jnp.moveaxis(lax.map(one_frame, moved), 0, 1)  15.2 us
    all_to_all x1, waiting for transfers between devices, per_device(): lax.all_to_all(sorted_keys, 'cam', split_axis=0, concat_axis=0, tiled=True)  13.8 us
    psum x1, blocking collectives, per_device(): total_sq = lax.psum(jnp.sum(readout * readout, axis=1), 'head')  11.8 us
    gather x1, local copies, waits for them, and re-layouts, per_device(): jnp.take(keys, inverse, axis=0).reshape(cams, owned, PATCHES, width)  9.05 us
    gather x1, local copies, waits for them, and re-layouts, per_device(): jnp.take(queries, inverse, axis=0).reshape(cams, owned, PATCHES, width)  8.98 us
    gather x2, local copies, waits for them, and re-layouts, per_device(): attended = jnp.take(returned.reshape(count, width), slots, axis=0)  8.14 us
    gather x1, local copies, waits for them, and re-layouts, per_device(): jnp.take(values, inverse, axis=0).reshape(cams, owned, PATCHES, width)  8.09 us
  transfers between devices with their start and end apart: 5, of which 3 were waited for; matrix products, arithmetic and copies ran while one was open for 10% of the time, Pallas kernels for 0%

commit v1 on v0

v1 whole, which is shorter than its diff:
```python
import functools

import jax
import jax.numpy as jnp
from jax import lax
from jax.experimental import pallas as pl
from jax.experimental.pallas import tpu as pltpu
from jax.sharding import PartitionSpec as P

PATCHES = 32
EPSILON = 1e-06
LANES = 128
CHUNKS = 2
MIB = 1024 * 1024
F32 = jnp.float32
BF16 = jnp.bfloat16


def dot(a, b):
    return lax.dot_general(a, b, (((1,), (0,)), ((), ())), preferred_element_type=F32)


def dot_bt(a, b):
    return lax.dot_general(a, b, (((1,), (1,)), ((), ())), preferred_element_type=F32)


def dot_at(a, b):
    return lax.dot_general(a, b, (((0,), (0,)), ((), ())), preferred_element_type=F32)


def params():
    return pltpu.CompilerParams(vmem_limit_bytes=40 * MIB)


def full(count):
    return [pl.BlockSpec(memory_space=pltpu.VMEM)] * count


def cost(flops, moved, exps=0):
    return pl.CostEstimate(flops=int(flops), bytes_accessed=int(moved), transcendentals=int(exps))


def power_of_two(n):
    return n & (n - 1) == 0


def peer(me, step, n):
    if power_of_two(n):
        return me ^ step
    ahead = me + step
    return jnp.where(ahead >= n, ahead - n, ahead)


def routes(step, n):
    if power_of_two(n):
        return [(at, at ^ step) for at in range(n)]
    return [(at, (at + step) % n) for at in range(n)]


def column(row):
    return jnp.broadcast_to(row, (LANES, LANES)).T


def sort_kernel(n, start, rows, owned_rows, order_ref, q_ref, k_ref, v_ref, *rest):
    outs, onehot = rest[:n], rest[n]
    me = lax.axis_index("cam")
    count, width = q_ref.shape
    group = onehot.shape[0] // rows
    order = order_ref[...]
    for first in range(0, n, group):
        for at in range(group):
            base = peer(me, first + at, n) * owned_rows + start
            slot = lax.broadcasted_iota(jnp.int32, (rows, count), 0) + base
            onehot[at * rows : (at + 1) * rows, :] = (slot == order).astype(F32).astype(BF16)
        for which, ref in enumerate((q_ref, k_ref, v_ref)):
            picked = dot(onehot[...], ref[...]).astype(BF16)
            for at in range(group):
                outs[first + at][:, which * width : (which + 1) * width] = picked[
                    at * rows : (at + 1) * rows
                ]


def sort_tokens(order, q, k, v, n, start, rows, owned_rows):
    count, width = q.shape
    group = max(1, min(n, 512 // rows))
    while n % group:
        group -= 1
    return pl.pallas_call(
        functools.partial(sort_kernel, n, start, rows, owned_rows),
        out_shape=[jax.ShapeDtypeStruct((rows, 3 * width), BF16)] * n,
        in_specs=full(4),
        out_specs=full(n),
        scratch_shapes=[pltpu.VMEM((group * rows, count), BF16)],
        compiler_params=params(),
        cost_estimate=cost(6 * n * rows * count * width, 6 * count * width),
        name="sort_tokens",
    )(order, q, k, v)


def attend_kernel(n, scale, *refs):
    ins, outs = refs[:n], refs[n : 2 * n]
    q_all, k_all, v_all = refs[2 * n :]
    rows = ins[0].shape[0]
    width = outs[0].shape[1]
    group = n * PATCHES
    block = min(group, 256)
    for stamp in range(rows // PATCHES):
        here = slice(stamp * PATCHES, (stamp + 1) * PATCHES)
        for cam in range(n):
            there = slice(cam * PATCHES, (cam + 1) * PATCHES)
            q_all[there, :] = ins[cam][here, 0:width]
            k_all[there, :] = ins[cam][here, width : 2 * width]
            v_all[there, :] = ins[cam][here, 2 * width : 3 * width]
        for low in range(0, group, block):
            scores = dot_bt(q_all[low : low + block, :], k_all[...]) * scale
            scores = scores - jnp.max(scores, axis=-1, keepdims=True)
            expo = jnp.exp(scores)
            probs = (expo / jnp.sum(expo, axis=-1, keepdims=True)).astype(BF16)
            result = dot(probs, v_all[...]).astype(BF16)
            for cam in range(low // PATCHES, (low + block) // PATCHES):
                at = cam * PATCHES - low
                outs[cam][here, :] = result[at : at + PATCHES]


def attend(blocks, n, width):
    rows = blocks[0].shape[0]
    group = n * PATCHES
    return pl.pallas_call(
        functools.partial(attend_kernel, n, width**-0.5),
        out_shape=[jax.ShapeDtypeStruct((rows, width), BF16)] * n,
        in_specs=full(n),
        out_specs=full(n),
        scratch_shapes=[pltpu.VMEM((group, width), BF16)] * 3,
        compiler_params=params(),
        cost_estimate=cost(
            4 * n * rows * group * width, 8 * n * rows * width, n * rows * group
        ),
        name="attend",
    )(*blocks)


def grads_kernel(n, split, k_ref, v_ref, rate_ref, one_ref, three_ref, two_ref, *rest):
    outs, total = rest[:-1], rest[-1]
    step = pl.program_id(0)
    hid, width = one_ref.shape[1:]

    @pl.when(step == 0)
    def _():
        total[...] = jnp.zeros_like(total)

    k = k_ref[...]
    one, three, two = one_ref[0], three_ref[0], two_ref[0]
    h_one = dot_bt(k, one)
    h_three = dot_bt(k, three)
    sigma = jax.nn.sigmoid(h_one)
    gated = h_one * sigma
    active = (gated * h_three).astype(BF16)
    pieces = []
    for low in range(0, k.shape[0], LANES):
        rate = column(rate_ref[:, low : low + LANES])
        rate = jnp.concatenate([rate] * (width // LANES), axis=1)
        pieces.append((-rate * v_ref[low : low + LANES, :].astype(F32)).astype(BF16))
    error = jnp.concatenate(pieces, axis=0)
    back = dot(error, two)
    back_one = (back * h_three * sigma * (1.0 + h_one * (1.0 - sigma))).astype(BF16)
    back_three = (back * gated).astype(BF16)
    total[0:hid, :] += dot_at(back_one, k)
    total[hid : 2 * hid, :] += dot_at(back_three, k)
    total[2 * hid :, :] += dot_at(error, active)

    @pl.when(step == pl.num_programs(0) - 1)
    def _():
        if split:
            half = total.shape[0] // 2
            core = lax.axis_index("cam") & 1
            outs[0][...] = total[pl.ds(pl.multiple_of(core * half, half), half), :]
            outs[1][...] = total[pl.ds(pl.multiple_of((1 - core) * half, half), half), :]
        else:
            outs[0][...] = total[...]


def gradients(k, v, rate, one, three, two, n):
    count, width = k.shape
    hid = one.shape[1]
    tile = min(count, 512)
    split = n > 1 and power_of_two(n)
    assert hid == width
    rows = 3 * hid
    parts = 2 if split else 1
    weight = pl.BlockSpec((1, hid, width), lambda i: (0, 0, 0))
    return pl.pallas_call(
        functools.partial(grads_kernel, n, split),
        grid=(count // tile,),
        out_shape=[jax.ShapeDtypeStruct((rows // parts, width), F32)] * parts,
        in_specs=[
            pl.BlockSpec((tile, width), lambda i: (i, 0)),
            pl.BlockSpec((tile, width), lambda i: (i, 0)),
            pl.BlockSpec((1, tile), lambda i: (0, i)),
            weight,
            weight,
            weight,
        ],
        out_specs=[pl.BlockSpec((rows // parts, width), lambda i: (0, 0))] * parts,
        scratch_shapes=[pltpu.VMEM((rows, width), F32)],
        compiler_params=params(),
        cost_estimate=cost(12 * count * width * hid, 8 * count * width, count * hid),
        name="gradients",
    )(k, v, rate, one, three, two)


def sum_over_cams(parts, n):
    if len(parts) == 1:
        return [lax.psum(parts[0], "cam")]
    keep, send = parts
    bits = n.bit_length() - 1
    mine = keep + lax.ppermute(send, "cam", routes(1, n))
    span = bits - 1
    for step in range(span):
        pairs = []
        for at in range(n):
            bit = 1 + (step + (at & 1)) % span
            pairs.append((at, at ^ (1 << bit)))
        mine = mine + lax.ppermute(mine, "cam", pairs)
    return [mine, lax.ppermute(mine, "cam", routes(1, n))]


def readout_kernel(parts, q_ref, one_ref, three_ref, two_ref, *rest):
    grads, (y_ref, sq_ref, total, fresh) = rest[:parts], rest[parts:]
    step = pl.program_id(0)
    hid, width = one_ref.shape[1:]

    @pl.when(step == 0)
    def _():
        if parts == 2:
            half = total.shape[0] // 2
            core = lax.axis_index("cam") & 1
            total[pl.ds(pl.multiple_of(core * half, half), half), :] = grads[0][...]
            total[pl.ds(pl.multiple_of((1 - core) * half, half), half), :] = grads[1][...]
        else:
            total[...] = grads[0][...]
        entries = hid * width
        for which, ref in enumerate((one_ref, three_ref, two_ref)):
            grad = total[which * hid : (which + 1) * hid, :]
            weight = ref[0].astype(F32)
            row_sq = jnp.sum(weight * weight, axis=1, keepdims=True)
            weight_sq = jnp.sum(row_sq, axis=0, keepdims=True)
            grad_sq = jnp.sum(
                jnp.sum(grad * grad, axis=1, keepdims=True), axis=0, keepdims=True
            )
            scale = jnp.sqrt(weight_sq / entries) / jnp.sqrt(grad_sq / entries + EPSILON)
            moved = weight - scale * grad
            ratio = jnp.sqrt(row_sq) / jnp.sqrt(
                jnp.sum(moved * moved, axis=1, keepdims=True) + EPSILON
            )
            fresh[which * hid : (which + 1) * hid, :] = (moved * ratio).astype(BF16)

    q = q_ref[...]
    h_one = dot_bt(q, fresh[0:hid, :])
    h_three = dot_bt(q, fresh[hid : 2 * hid, :])
    active = (h_one * jax.nn.sigmoid(h_one) * h_three).astype(BF16)
    y = dot_bt(active, fresh[2 * hid :, :])
    y_ref[...] = y
    square = y * y
    high = square.astype(BF16)
    low = (square - high.astype(F32)).astype(BF16)
    ones = jnp.ones((8, width), BF16)
    sq_ref[...] = (dot_bt(ones, high) + dot_bt(ones, low))[0:1, :]


def read_out(q, one, three, two, grads):
    count, width = q.shape
    hid = one.shape[1]
    tile = min(count, 512)
    weight = pl.BlockSpec((1, hid, width), lambda i: (0, 0, 0))
    parts = len(grads)
    return pl.pallas_call(
        functools.partial(readout_kernel, parts),
        grid=(count // tile,),
        out_shape=[
            jax.ShapeDtypeStruct((count, width), F32),
            jax.ShapeDtypeStruct((1, count), F32),
        ],
        in_specs=[pl.BlockSpec((tile, width), lambda i: (i, 0)), weight, weight, weight]
        + [pl.BlockSpec(grads[0].shape, lambda i: (0, 0))] * parts,
        out_specs=[
            pl.BlockSpec((tile, width), lambda i: (i, 0)),
            pl.BlockSpec((1, tile), lambda i: (0, i)),
        ],
        scratch_shapes=[pltpu.VMEM((3 * hid, width), F32), pltpu.VMEM((3 * hid, width), BF16)],
        compiler_params=params(),
        cost_estimate=cost(6 * count * width * hid, 8 * count * width, count * hid),
        name="read_out",
    )(q, one, three, two, *grads)


def slot_row(n, start, rows, owned_rows):
    me = lax.axis_index("cam")
    at = lax.broadcasted_iota(jnp.int32, (8, n * rows), 1)
    step = jnp.zeros_like(at)
    for cut in range(1, n):
        step = step + (at >= cut * rows).astype(jnp.int32)
    return peer(me, step, n) * owned_rows + start + at - step * rows


def placed(order_ref, low, slots, onehot, joined):
    tile = onehot.shape[0]
    for at in range(0, tile, LANES):
        wanted = column(order_ref[:, low + at : low + at + LANES].astype(F32))
        for lane in range(0, onehot.shape[1], LANES):
            hit = wanted == slots[:, lane : lane + LANES]
            onehot[at : at + LANES, lane : lane + LANES] = hit.astype(F32).astype(BF16)
    return dot(onehot[...], joined[...])


def unsort_kernel(n, start, rows, owned_rows, order_ref, *rest):
    blocks, (out_ref, onehot, joined) = rest[:n], rest[n:]
    for at in range(n):
        joined[at * rows : (at + 1) * rows, :] = blocks[at][...]
    slots = slot_row(n, start, rows, owned_rows)[0:1, :].astype(F32)
    tile = onehot.shape[0]
    for low in range(0, out_ref.shape[0], tile):
        part = placed(order_ref, low, slots, onehot, joined)
        out_ref[low : low + tile, :] = part.astype(BF16)


def unsort(order, blocks, n, start, owned_rows, count):
    rows, width = blocks[0].shape
    tile = min(count, 512)
    return pl.pallas_call(
        functools.partial(unsort_kernel, n, start, rows, owned_rows),
        out_shape=jax.ShapeDtypeStruct((count, width), BF16),
        in_specs=full(1 + n),
        out_specs=pl.BlockSpec(memory_space=pltpu.VMEM),
        scratch_shapes=[
            pltpu.VMEM((tile, n * rows), BF16),
            pltpu.VMEM((n * rows, width), BF16),
        ],
        compiler_params=params(),
        cost_estimate=cost(2 * count * n * rows * width, 4 * count * width),
        name="unsort",
    )(order, *blocks)


def mix_kernel(n, heads, start, rows, owned_rows, order_ref, gain_ref, y_ref, acc_ref, *rest):
    squares, blocks = rest[:heads], rest[heads : heads + n]
    out_ref, onehot, joined = rest[heads + n :]
    count, width = y_ref.shape
    for at in range(n):
        joined[at * rows : (at + 1) * rows, :] = blocks[at][...]
    slots = slot_row(n, start, rows, owned_rows)[0:1, :].astype(F32)
    total = squares[0][...]
    for ref in squares[1:]:
        total = total + ref[...]
    inverse = 1.0 / jnp.sqrt(total / (width * heads) + EPSILON)
    tile = onehot.shape[0]
    gain = gain_ref[...]
    for low in range(0, count, tile):
        part = placed(order_ref, low, slots, onehot, joined)
        for at in range(0, tile, LANES):
            here = slice(low + at, low + at + LANES)
            norm = column(inverse[:, here])
            norm = jnp.concatenate([norm] * (width // LANES), axis=1)
            rest_part = part[at : at + LANES] + acc_ref[here, :].astype(F32)
            out_ref[here, :] = (y_ref[here, :] * norm * gain + rest_part).astype(BF16)


def mix(order, gain, y, acc, squares, blocks, n, start, owned_rows):
    count, width = y.shape
    rows = blocks[0].shape[0]
    tile = min(count, 512)
    heads = len(squares)
    return pl.pallas_call(
        functools.partial(mix_kernel, n, heads, start, rows, owned_rows),
        out_shape=jax.ShapeDtypeStruct((count, width), BF16),
        in_specs=full(4 + heads + n),
        out_specs=pl.BlockSpec(memory_space=pltpu.VMEM),
        scratch_shapes=[
            pltpu.VMEM((tile, n * rows), BF16),
            pltpu.VMEM((n * rows, width), BF16),
        ],
        compiler_params=params(),
        cost_estimate=cost(2 * count * n * rows * width, 8 * count * width),
        name="mix",
    )(order, gain, y, acc, *squares, *blocks)


def exchange(blocks, n):
    return [blocks[0]] + [
        lax.ppermute(blocks[step], "cam", routes(step, n)) for step in range(1, n)
    ]


def give_back(blocks, n):
    moved = [blocks[0]]
    for step in range(1, n):
        pairs = [(target, at) for at, target in routes(step, n)]
        moved.append(lax.ppermute(blocks[step], "cam", pairs))
    return moved


def per_device(queries, keys, values, rates, w_one, w_three, w_two, gain, order):
    count, width = queries.shape
    n = lax.axis_size("cam")
    heads = lax.axis_size("head")
    owned_rows = count // n
    chunks = CHUNKS if (owned_rows // PATCHES) % CHUNKS == 0 else 1
    rows = owned_rows // chunks
    arrived = []
    for at in range(chunks):
        blocks = sort_tokens(order, queries, keys, values, n, at * rows, rows, owned_rows)
        arrived.append(exchange(blocks, n))
    parts = gradients(keys, values, rates.reshape(1, count), w_one, w_three, w_two, n)
    summed = sum_over_cams(parts, n)
    y, square = read_out(queries, w_one, w_three, w_two, summed)
    squares = [square] + [
        lax.ppermute(square, "head", [(at, (at + step) % heads) for at in range(heads)])
        for step in range(1, heads)
    ]
    acc = jnp.zeros((count, width), BF16) if chunks == 1 else None
    for at in range(chunks):
        returned = give_back(attend(arrived[at], n, width), n)
        if at == chunks - 1:
            gain_row = gain.reshape(1, width)
            return mix(order, gain_row, y, acc, squares, returned, n, at * rows, owned_rows)
        part = unsort(order, returned, n, at * rows, owned_rows, count)
        acc = part if acc is None else acc + part


def solution(mesh):
    in_specs = (
        P("cam", "head"),
        P("cam", "head"),
        P("cam", "head"),
        P("cam", "head"),
        P("head", None, None),
        P("head", None, None),
        P("head", None, None),
        P("head"),
        P("cam", None),
    )
    out_specs = P("cam", "head")
    return jax.shard_map(
        per_device, mesh=mesh, in_specs=in_specs, out_specs=out_specs, check_vma=False
    )
```

time: 212 us -> 92.1 us (0.43)
  local copies, waits for them, and re-layouts: 65.4 us -> 5.88 us
  waiting for transfers between devices: 66.9 us -> 23.3 us
  starting transfers between devices: 17.4 us -> 41.2 us
  Pallas kernels: 0 us -> 21.1 us
  between operations: 17.5 us -> 0.2 us
  matrix products: 16.5 us -> 0 us
  other arithmetic: 15.1 us -> 0.15 us
  blocking collectives: 11.8 us -> 0 us
    psum x1 -> x0, waiting for transfers between devices: 47.8 us -> none  [per_device(): summed = lax.psum((grad_first, grad_third, grad_second), 'cam')]
    ppermute x0 -> x35, starting transfers between devices: none -> 41.2 us  [the longest x14 17.1 us: exchange(): lax.ppermute(blocks[step], 'cam', routes(step, n))]
    gather x5 -> x0, local copies, waits for them, and re-layouts: 34.3 us -> none  [the longest x1 9.05 us: per_device(): jnp.take(keys, inverse, axis=0).reshape(cams, owned, PATCHES, width)]
    ppermute x0 -> x35, waiting for transfers between devices: none -> 23.3 us  [the longest x14 18.8 us: exchange(): lax.ppermute(blocks[step], 'cam', routes(step, n))]
    pallas_call x0 -> x8, Pallas kernels: none -> 21.1 us  [the longest x2 6.81 us: sort_tokens(): pl.pallas_call(functools.partial(sort_kernel, n, start, rows, owned_rows)...]
    all_to_all x4 -> x0, waiting for transfers between devices: 19 us -> none  [the longest x1 13.8 us: per_device(): lax.all_to_all(sorted_keys, 'cam', split_axis=0, concat_axis=0, tiled=True)]
    all_to_all x4 -> x0, starting transfers between devices: 17.4 us -> none  [the longest x1 5.31 us: per_device(): lax.all_to_all(sorted_value, 'cam', split_axis=0, concat_axis=0, tiled=True)]
    dot_general x24 -> x0, matrix products: 16.5 us -> none  [the longest x1 4.22 us: per_device(): jnp.einsum('nhk,hdk->nhd', q_active, new_second, preferred_element_type=j...]
  transfers between devices with their start and end apart: 5 -> 35, of which waited for: 3 -> 11; matrix products, arithmetic and copies ran while one was open for 10% -> 0% of each run, Pallas kernels for 0% -> 16%
where the time goes in v1:
time: 92.1 us; the launch traced here: 91.8 us
  starting transfers between devices  41.2 us (45%)
  waiting for transfers between devices  23.3 us (25%)
  Pallas kernels  21.1 us (23%)
  local copies, waits for them, and re-layouts  5.88 us (6%)
    ppermute x14, waiting for transfers between devices, exchange(): lax.ppermute(blocks[step], 'cam', routes(step, n))  18.8 us
    ppermute x14, starting transfers between devices, exchange(): lax.ppermute(blocks[step], 'cam', routes(step, n))  17.1 us
    ppermute x14, starting transfers between devices, give_back(): moved.append(lax.ppermute(blocks[step], 'cam', pairs))  12.6 us
    pallas_call x2, Pallas kernels, sort_tokens(): pl.pallas_call(functools.partial(sort_kernel, n, start, rows, owned_rows)...  6.81 us
    unnamed x24, local copies, waits for them, and re-layouts  5.88 us
    ppermute x2, starting transfers between devices, sum_over_cams(): mine = mine + lax.ppermute(mine, 'cam', pairs)  5.32 us
    ppermute x3, starting transfers between devices, per_device(): lax.ppermute(square, 'head', [(at, (at + step) % heads) for at in range(h...  5.3 us
    pallas_call x1, Pallas kernels, gradients(): pl.pallas_call(functools.partial(grads_kernel, n, split), grid=(count //...  3.8 us
  transfers between devices with their start and end apart: 35, of which 11 were waited for; matrix products, arithmetic and copies ran while one was open for 0% of the time, Pallas kernels for 16%

profile of v1, /device:TPU:0, one launch (start us, length us, event | category | flops | bytes accessed | tf_op | source)
XLA Modules:
  0.0 91.8 jit_solution(16293405974735724338)
XLA Ops:
  0.0 1.2 %copy-done.2 = bf16[2048,256]{1,0:T(8,128)(2,1)S(1)} copy-done((bf16[2048,256]{1,0:T(8,128)(2,1)S(1)}, bf16[2048,256]{1,0:T(8,128)(2,1)}, u32[]{:S(2)}) %copy-start.2) | copy-done | bytes 1048600
  1.2 1.2 %copy-done.3 = bf16[2048,256]{1,0:T(8,128)(2,1)S(1)} copy-done((bf16[2048,256]{1,0:T(8,128)(2,1)S(1)}, bf16[2048,256]{1,0:T(8,128)(2,1)}, u32[]{:S(2)}) %copy-start.3) | copy-done | bytes 1048600
  5.9 3.8 %gradients.1 = (f32[384,256]{1,0:T(8,128)S(1)}, f32[384,256]{1,0:T(8,128)S(1)}) custom-call(bf16[2048,256]{1,0:T(8,128)(2,1)S(1)} %copy-done.2, bf16[2048,256]{1,0:T(8,128)(2,1)S(1)} %copy-done.3, f32[1,2048]{1,0:T(1,128)S(1)} %bitcast.3, bf16[1,256,256]{2,1,0:T(8,128)(2,1)S(1)} %copy-done.5, bf16[1,256,256]{2,1,0:T(8,128)(2,1)S(1)} %copy-done.7, ...), custom_call_target="tpu_custom_call" | custom-call | flops 1610612736 | bytes 4194304 | tf_op jit(solution)/shard_map/gradients/pallas_call | solution.py:191
  10.2 1.3 %collective-permute-done = f32[384,256]{1,0:T(8,128)S(1)} collective-permute-done((f32[384,256]{1,0:T(8,128)S(1)}, f32[384,256]{1,0:T(8,128)S(1)}, u32[]{:S(2)}, u32[]{:S(2)}) %collective-permute-start) | collective-permute-done | bytes 393248 | tf_op jit(solution)/shard_map/ppermute | solution.py:216
  11.6 2.9 %collective-permute-start.1 = (f32[384,256]{1,0:T(8,128)S(1)}, f32[384,256]{1,0:T(8,128)S(1)}, u32[]{:S(2)}, u32[]{:S(2)}) collective-permute-start(f32[384,256]{1,0:T(8,128)S(1)} %add.9), channel_id=1, source_target_pairs={{0,8},{4,20},{8,0},{12,28},{16,24},{20,4},{24,16},{28,12},{1,9},{5... | collective-permute-start | bytes 1179656 | tf_op jit(solution)/shard_map/ppermute | solution.py:223
  14.5 3.4 %sort_tokens.2 = (bf16[128,768]{1,0:T(8,128)(2,1)S(1)}, bf16[128,768]{1,0:T(8,128)(2,1)S(1)}, bf16[128,768]{1,0:T(8,128)(2,1)S(1)}, bf16[128,768]{1,0:T(8,128)(2...) custom-call(s32[1,2048]{1,0:T(1,128)S(1)} %copy-done, ...), custom_call_target="tpu_custom_call" | custom-call | flops 3221225472 | bytes 3145728 | tf_op jit(solution)/shard_map/sort_tokens/pallas_call | solution.py:88
  20.3 2.4 %collective-permute-start.2 = (f32[384,256]{1,0:T(8,128)S(1)}, f32[384,256]{1,0:T(8,128)S(1)}, u32[]{:S(2)}, u32[]{:S(2)}) collective-permute-start(f32[384,256]{1,0:T(8,128)S(1)} %add.10), channel_id=1, source_target_pairs={{0,16},{4,12},{8,24},{12,4},{16,0},{20,28},{24,8},{28,20},{1,17},{... | collective-permute-start | bytes 1179656 | tf_op jit(solution)/shard_map/ppermute | solution.py:223
  22.7 2.5 %collective-permute-start.5 = (bf16[128,768]{1,0:T(8,128)(2,1)S(1)}, bf16[128,768]{1,0:T(8,128)(2,1)S(1)}, u32[]{:S(2)}, u32[]{:S(2)}) collective-permute-start(bf16[128,768]{1,0:T(8,128)(2,1)S(1)} %get-tuple-element.46), channel_id=1, source_target_pairs={{0,8},{4,12},{8,0},{12,4},{16,24},{20,28},{24,16},{28,20},{1,9},{5... | collective-permute-start | bytes 589832 | tf_op jit(solution)/shard_map/ppermute | solution.py:389
  27.5 3.4 %sort_tokens.3 = (bf16[128,768]{1,0:T(8,128)(2,1)S(1)}, bf16[128,768]{1,0:T(8,128)(2,1)S(1)}, bf16[128,768]{1,0:T(8,128)(2,1)S(1)}, bf16[128,768]{1,0:T(8,128)(2...) custom-call(s32[1,2048]{1,0:T(1,128)S(1)} %copy-done, ...), custom_call_target="tpu_custom_call" | custom-call | flops 3221225472 | bytes 3145728 | tf_op jit(solution)/shard_map/sort_tokens/pallas_call | solution.py:88
  31.0 2.1 %collective-permute-start.9 = (bf16[128,768]{1,0:T(8,128)(2,1)S(1)}, bf16[128,768]{1,0:T(8,128)(2,1)S(1)}, u32[]{:S(2)}, u32[]{:S(2)}) collective-permute-start(bf16[128,768]{1,0:T(8,128)(2,1)S(1)} %get-tuple-element.50), channel_id=1, source_target_pairs={{0,24},{4,28},{8,16},{12,20},{16,8},{20,12},{24,0},{28,4},{1,25},{... | collective-permute-start | bytes 589832 | tf_op jit(solution)/shard_map/ppermute | solution.py:389
  33.2 6.6 %collective-permute-done.6.refs_3_ = bf16[128,768]{1,0:T(8,128)(2,1)S(1)} collective-permute-done((bf16[128,768]{1,0:T(8,128)(2,1)S(1)}, bf16[128,768]{1,0:T(8,128)(2,1)S(1)}, u32[]{:S(2)}, u32[]{:S(2)}) %collective-permute-start.6) | collective-permute-done | bytes 196640 | tf_op jit(solution)/shard_map/ppermute | solution.py:389
  39.8 1.6 %collective-permute-start.22 = (bf16[128,768]{1,0:T(8,128)(2,1)S(1)}, bf16[128,768]{1,0:T(8,128)(2,1)S(1)}, u32[]{:S(2)}, u32[]{:S(2)}) collective-permute-start(bf16[128,768]{1,0:T(8,128)(2,1)S(1)} %get-tuple-element.63), channel_id=1, source_target_pairs={{0,8},{4,12},{8,0},{12,4},{16,24},{20,28},{24,16},{28,20},{1,9},{5... | collective-permute-start | bytes 589832 | tf_op jit(solution)/shard_map/ppermute | solution.py:389
  42.1 1.7 %collective-permute-start.24 = (bf16[128,768]{1,0:T(8,128)(2,1)S(1)}, bf16[128,768]{1,0:T(8,128)(2,1)S(1)}, u32[]{:S(2)}, u32[]{:S(2)}) collective-permute-start(bf16[128,768]{1,0:T(8,128)(2,1)S(1)} %get-tuple-element.65), channel_id=1, source_target_pairs={{0,16},{4,20},{8,24},{12,28},{16,0},{20,4},{24,8},{28,12},{1,17},{... | collective-permute-start | bytes 589832 | tf_op jit(solution)/shard_map/ppermute | solution.py:389
  44.2 3.3 %collective-permute-done.22.refs_2_ = bf16[128,768]{1,0:T(8,128)(2,1)S(1)} collective-permute-done((bf16[128,768]{1,0:T(8,128)(2,1)S(1)}, bf16[128,768]{1,0:T(8,128)(2,1)S(1)}, u32[]{:S(2)}, u32[]{:S(2)}) %collective-permute-start.22) | collective-permute-done | bytes 196640 | tf_op jit(solution)/shard_map/ppermute | solution.py:389
  47.5 2.5 %collective-permute-start.26 = (bf16[128,768]{1,0:T(8,128)(2,1)S(1)}, bf16[128,768]{1,0:T(8,128)(2,1)S(1)}, u32[]{:S(2)}, u32[]{:S(2)}) collective-permute-start(bf16[128,768]{1,0:T(8,128)(2,1)S(1)} %get-tuple-element.67), channel_id=1, source_target_pairs={{0,24},{4,28},{8,16},{12,20},{16,8},{20,12},{24,0},{28,4},{1,25},{... | collective-permute-start | bytes 589832 | tf_op jit(solution)/shard_map/ppermute | solution.py:389
  50.9 2.9 %collective-permute-start.27 = (bf16[128,768]{1,0:T(8,128)(2,1)S(1)}, bf16[128,768]{1,0:T(8,128)(2,1)S(1)}, u32[]{:S(2)}, u32[]{:S(2)}) collective-permute-start(bf16[128,768]{1,0:T(8,128)(2,1)S(1)} %get-tuple-element.68), channel_id=1, source_target_pairs={{0,28},{4,24},{8,20},{12,16},{16,12},{20,8},{24,4},{28,0},{1,29},{... | collective-permute-start | bytes 589832 | tf_op jit(solution)/shard_map/ppermute | solution.py:389
  53.9 1.1 %attend.2 = (bf16[128,256]{1,0:T(8,128)(2,1)S(1)}, bf16[128,256]{1,0:T(8,128)(2,1)S(1)}, bf16[128,256]{1,0:T(8,128)(2,1)S(1)}, bf16[128,256]{1,0:T(8,128)(2,1)S(...) custom-call(bf16[128,768]{1,0:T(8,128)(2,1)S(1)} %get-tuple-element., ...), custom_call_target="tpu_custom_call" | custom-call | flops 268435456 | bytes 2097152 | tf_op jit(solution)/shard_map/attend/pallas_call | solution.py:128
  55.1 6.9 %collective-permute-done.25.refs_5_ = bf16[128,768]{1,0:T(8,128)(2,1)S(1)} collective-permute-done((bf16[128,768]{1,0:T(8,128)(2,1)S(1)}, bf16[128,768]{1,0:T(8,128)(2,1)S(1)}, u32[]{:S(2)}, u32[]{:S(2)}) %collective-permute-start.25) | collective-permute-done | bytes 196640 | tf_op jit(solution)/shard_map/ppermute | solution.py:389
  63.4 1.2 %collective-permute-start.14 = (bf16[128,256]{1,0:T(8,128)(2,1)S(1)}, bf16[128,256]{1,0:T(8,128)(2,1)S(1)}, u32[]{:S(2)}, u32[]{:S(2)}) collective-permute-start(bf16[128,256]{1,0:T(8,128)(2,1)S(1)} %get-tuple-element.56), channel_id=1, source_target_pairs={{16,0},{20,4},{24,8},{28,12},{0,16},{4,20},{8,24},{12,28},{17,1},{... | collective-permute-start | bytes 196616 | tf_op jit(solution)/shard_map/ppermute | solution.py:397
  65.5 1.1 %collective-permute-done.12.rest_2_ = bf16[128,256]{1,0:T(8,128)(2,1)S(1)} collective-permute-done((bf16[128,256]{1,0:T(8,128)(2,1)S(1)}, bf16[128,256]{1,0:T(8,128)(2,1)S(1)}, u32[]{:S(2)}, u32[]{:S(2)}) %collective-permute-start.12) | collective-permute-done | bytes 65568 | tf_op jit(solution)/shard_map/ppermute | solution.py:397
  66.6 1.7 %collective-permute-start.16 = (bf16[128,256]{1,0:T(8,128)(2,1)S(1)}, bf16[128,256]{1,0:T(8,128)(2,1)S(1)}, u32[]{:S(2)}, u32[]{:S(2)}) collective-permute-start(bf16[128,256]{1,0:T(8,128)(2,1)S(1)} %get-tuple-element.58), channel_id=1, source_target_pairs={{24,0},{28,4},{16,8},{20,12},{8,16},{12,20},{0,24},{4,28},{25,1},{... | collective-permute-start | bytes 196616 | tf_op jit(solution)/shard_map/ppermute | solution.py:397
  69.3 1.1 %attend.3 = (bf16[128,256]{1,0:T(8,128)(2,1)S(1)}, bf16[128,256]{1,0:T(8,128)(2,1)S(1)}, bf16[128,256]{1,0:T(8,128)(2,1)S(1)}, bf16[128,256]{1,0:T(8,128)(2,1)S(...) custom-call(bf16[128,768]{1,0:T(8,128)(2,1)S(1)} %get-tuple-element., ...), custom_call_target="tpu_custom_call" | custom-call | flops 268435456 | bytes 2097152 | tf_op jit(solution)/shard_map/attend/pallas_call | solution.py:128
  70.9 1.2 %collective-permute-start.29 = (bf16[128,256]{1,0:T(8,128)(2,1)S(1)}, bf16[128,256]{1,0:T(8,128)(2,1)S(1)}, u32[]{:S(2)}, u32[]{:S(2)}) collective-permute-start(bf16[128,256]{1,0:T(8,128)(2,1)S(1)} %get-tuple-element.71), channel_id=1, source_target_pairs={{8,0},{12,4},{0,8},{4,12},{24,16},{28,20},{16,24},{20,28},{9,1},{1... | collective-permute-start | bytes 196616 | tf_op jit(solution)/shard_map/ppermute | solution.py:397
  73.3 1.0 %collective-permute-start.31 = (bf16[128,256]{1,0:T(8,128)(2,1)S(1)}, bf16[128,256]{1,0:T(8,128)(2,1)S(1)}, u32[]{:S(2)}, u32[]{:S(2)}) collective-permute-start(bf16[128,256]{1,0:T(8,128)(2,1)S(1)} %get-tuple-element.73), channel_id=1, source_target_pairs={{16,0},{20,4},{24,8},{28,12},{0,16},{4,20},{8,24},{12,28},{17,1},{... | collective-permute-start | bytes 196616 | tf_op jit(solution)/shard_map/ppermute | solution.py:397
  74.6 3.6 %read_out.1 = (f32[2048,256]{1,0:T(8,128)S(1)}, f32[1,2048]{1,0:T(1,128)S(1)}) custom-call(bf16[2048,256]{1,0:T(8,128)(2,1)S(1)} %copy-done.4, bf16[1,256,256]{2,1,0:T(8,128)(2,1)S(1)} %copy-done.6, bf16[1,256,256]{2,1,0:T(8,128)(2,1)S(1)} %copy-done.8, bf16[1,256,256]{2,1,0:T(8,128)(2,1)S(1)} %copy-done.10, f32[384,256]{1,0:T(8,128)S(1)} %add.11.rest_0_, ...), custom_call_target="tpu_custom_call" | custom-call | flops 805306368 | bytes 4194304 | tf_op jit(solution)/shard_map/read_out/pallas_call | solution.py:276
  78.2 1.6 %collective-permute-start.33 = (bf16[128,256]{1,0:T(8,128)(2,1)S(1)}, bf16[128,256]{1,0:T(8,128)(2,1)S(1)}, u32[]{:S(2)}, u32[]{:S(2)}) collective-permute-start(bf16[128,256]{1,0:T(8,128)(2,1)S(1)} %get-tuple-element.75), channel_id=1, source_target_pairs={{24,0},{28,4},{16,8},{20,12},{8,16},{12,20},{0,24},{4,28},{25,1},{... | collective-permute-start | bytes 196616 | tf_op jit(solution)/shard_map/ppermute | solution.py:397
  79.8 1.5 %collective-permute-start.34 = (bf16[128,256]{1,0:T(8,128)(2,1)S(1)}, bf16[128,256]{1,0:T(8,128)(2,1)S(1)}, u32[]{:S(2)}, u32[]{:S(2)}) collective-permute-start(bf16[128,256]{1,0:T(8,128)(2,1)S(1)} %get-tuple-element.76), channel_id=1, source_target_pairs={{28,0},{24,4},{20,8},{16,12},{12,16},{8,20},{4,24},{0,28},{29,1},{... | collective-permute-start | bytes 196616 | tf_op jit(solution)/shard_map/ppermute | solution.py:397
  81.4 1.3 %collective-permute-start.18 = (f32[1,2048]{1,0:T(1,128)S(1)}, f32[1,2048]{1,0:T(1,128)S(1)}, u32[]{:S(2)}, u32[]{:S(2)}) collective-permute-start(f32[1,2048]{1,0:T(1,128)S(1)} %get-tuple-element.60.rest_0_), channel_id=1, source_target_pairs={{0,1},{1,2},{2,3},{3,0},{4,5},{5,6},{6,7},{7,4},{8,9},{9,10},{10,1... | collective-permute-start | bytes 24584 | tf_op jit(solution)/shard_map/ppermute | solution.py:416
  82.7 2.6 %collective-permute-start.19 = (f32[1,2048]{1,0:T(1,128)S(1)}, f32[1,2048]{1,0:T(1,128)S(1)}, u32[]{:S(2)}, u32[]{:S(2)}) collective-permute-start(f32[1,2048]{1,0:T(1,128)S(1)} %get-tuple-element.60.rest_0_), channel_id=1, source_target_pairs={{0,2},{1,3},{2,0},{3,1},{4,6},{5,7},{6,4},{7,5},{8,10},{9,11},{10,... | collective-permute-start | bytes 24584 | tf_op jit(solution)/shard_map/ppermute | solution.py:416
  85.3 1.4 %collective-permute-start.20 = (f32[1,2048]{1,0:T(1,128)S(1)}, f32[1,2048]{1,0:T(1,128)S(1)}, u32[]{:S(2)}, u32[]{:S(2)}) collective-permute-start(f32[1,2048]{1,0:T(1,128)S(1)} %get-tuple-element.60.rest_0_), channel_id=1, source_target_pairs={{0,3},{1,0},{2,1},{3,2},{4,7},{5,4},{6,5},{7,6},{8,11},{9,8},{10,9... | collective-permute-start | bytes 24584 | tf_op jit(solution)/shard_map/ppermute | solution.py:416
  86.7 1.9 %unsort.1.acc_ref = bf16[2048,256]{1,0:T(8,128)(2,1)S(1)} custom-call(s32[1,2048]{1,0:T(1,128)S(1)} %copy-done, bf16[128,256]{1,0:T(8,128)(2,1)S(1)} %get-tuple-element.52.rest_0_, bf16[128,256]{1,0:T(8,128)(2,1)S(1)} %collective-permute-done.11.rest_1_, bf16[128,256]{1,0:T(8,128)(2,1)S(1)} %collective-permute-done.12.rest_2_, ...), custom_call_target="tpu_custom_call" | custom-call | flops 1073741824 | bytes 2097152 | tf_op jit(solution)/shard_map/unsort/pallas_call | solution.py:329
  89.0 2.9 %mix.1 = bf16[2048,256]{1,0:T(8,128)(2,1)} custom-call(s32[1,2048]{1,0:T(1,128)S(1)} %copy-done, f32[1,256]{1,0:T(1,128)S(1)} %bitcast.2, f32[2048,256]{1,0:T(8,128)S(1)} %get-tuple-element.43.y_ref, bf16[2048,256]{1,0:T(8,128)(2,1)S(1)} %unsort.1.acc_ref, f32[1,2048]{1,0:T(1,128)S(1)} %get-tuple-element.60.rest_0_, ...), custom_call_target="tpu_custom_call" | custom-call | flops 1073741824 | bytes 4194304 | tf_op jit(solution)/shard_map/mix/pallas_call | solution.py:372
  (73 shorter events, 16.5 us)
Async XLA Ops:
  11.6 8.7 %collective-permute-start.1 = (f32[384,256]{1,0:T(8,128)S(1)}, f32[384,256]{1,0:T(8,128)S(1)}, u32[]{:S(2)}, u32[]{:S(2)}) collective-permute-start(f32[384,256]{1,0:T(8,128)S(1)} %add.9), channel_id=1, source_target_pairs={{0,8},{4,20},{8,0},{12,28},{16,24},{20,4},{24,16},{28,12},{1,9},{5... | collective-permute-start | bytes 1179656 | tf_op jit(solution)/shard_map/ppermute | solution.py:223
  17.9 8.2 %collective-permute-start.10 = (bf16[128,768]{1,0:T(8,128)(2,1)S(1)}, bf16[128,768]{1,0:T(8,128)(2,1)S(1)}, u32[]{:S(2)}, u32[]{:S(2)}) collective-permute-start(bf16[128,768]{1,0:T(8,128)(2,1)S(1)} %get-tuple-element.51), channel_id=1, source_target_pairs={{0,28},{4,24},{8,20},{12,16},{16,12},{20,8},{24,4},{28,0},{1,29},{... | collective-permute-start | bytes 589832 | tf_op jit(solution)/shard_map/ppermute | solution.py:389
  18.9 7.9 %collective-permute-start.4 = (bf16[128,768]{1,0:T(8,128)(2,1)S(1)}, bf16[128,768]{1,0:T(8,128)(2,1)S(1)}, u32[]{:S(2)}, u32[]{:S(2)}) collective-permute-start(bf16[128,768]{1,0:T(8,128)(2,1)S(1)} %get-tuple-element.45), channel_id=1, source_target_pairs={{0,4},{4,0},{8,12},{12,8},{16,20},{20,16},{24,28},{28,24},{1,5},{5... | collective-permute-start | bytes 589832 | tf_op jit(solution)/shard_map/ppermute | solution.py:389
  20.3 21.1 %collective-permute-start.2 = (f32[384,256]{1,0:T(8,128)S(1)}, f32[384,256]{1,0:T(8,128)S(1)}, u32[]{:S(2)}, u32[]{:S(2)}) collective-permute-start(f32[384,256]{1,0:T(8,128)S(1)} %add.10), channel_id=1, source_target_pairs={{0,16},{4,12},{8,24},{12,4},{16,0},{20,28},{24,8},{28,20},{1,17},{... | collective-permute-start | bytes 1179656 | tf_op jit(solution)/shard_map/ppermute | solution.py:223
  22.7 8.3 %collective-permute-start.5 = (bf16[128,768]{1,0:T(8,128)(2,1)S(1)}, bf16[128,768]{1,0:T(8,128)(2,1)S(1)}, u32[]{:S(2)}, u32[]{:S(2)}) collective-permute-start(bf16[128,768]{1,0:T(8,128)(2,1)S(1)} %get-tuple-element.46), channel_id=1, source_target_pairs={{0,8},{4,12},{8,0},{12,4},{16,24},{20,28},{24,16},{28,20},{1,9},{5... | collective-permute-start | bytes 589832 | tf_op jit(solution)/shard_map/ppermute | solution.py:389
  25.2 14.5 %collective-permute-start.6 = (bf16[128,768]{1,0:T(8,128)(2,1)S(1)}, bf16[128,768]{1,0:T(8,128)(2,1)S(1)}, u32[]{:S(2)}, u32[]{:S(2)}) collective-permute-start(bf16[128,768]{1,0:T(8,128)(2,1)S(1)} %get-tuple-element.47), channel_id=1, source_target_pairs={{0,12},{4,8},{8,4},{12,0},{16,28},{20,24},{24,20},{28,16},{1,13},{... | collective-permute-start | bytes 589832 | tf_op jit(solution)/shard_map/ppermute | solution.py:389
  26.1 13.6 %collective-permute-start.7 = (bf16[128,768]{1,0:T(8,128)(2,1)S(1)}, bf16[128,768]{1,0:T(8,128)(2,1)S(1)}, u32[]{:S(2)}, u32[]{:S(2)}) collective-permute-start(bf16[128,768]{1,0:T(8,128)(2,1)S(1)} %get-tuple-element.48), channel_id=1, source_target_pairs={{0,16},{4,20},{8,24},{12,28},{16,0},{20,4},{24,8},{28,12},{1,17},{... | collective-permute-start | bytes 589832 | tf_op jit(solution)/shard_map/ppermute | solution.py:389
  26.8 14.9 %collective-permute-start.8 = (bf16[128,768]{1,0:T(8,128)(2,1)S(1)}, bf16[128,768]{1,0:T(8,128)(2,1)S(1)}, u32[]{:S(2)}, u32[]{:S(2)}) collective-permute-start(bf16[128,768]{1,0:T(8,128)(2,1)S(1)} %get-tuple-element.49), channel_id=1, source_target_pairs={{0,20},{4,16},{8,28},{12,24},{16,4},{20,0},{24,12},{28,8},{1,21},{... | collective-permute-start | bytes 589832 | tf_op jit(solution)/shard_map/ppermute | solution.py:389
  31.0 11.1 %collective-permute-start.9 = (bf16[128,768]{1,0:T(8,128)(2,1)S(1)}, bf16[128,768]{1,0:T(8,128)(2,1)S(1)}, u32[]{:S(2)}, u32[]{:S(2)}) collective-permute-start(bf16[128,768]{1,0:T(8,128)(2,1)S(1)} %get-tuple-element.50), channel_id=1, source_target_pairs={{0,24},{4,28},{8,16},{12,20},{16,8},{20,12},{24,0},{28,4},{1,25},{... | collective-permute-start | bytes 589832 | tf_op jit(solution)/shard_map/ppermute | solution.py:389
  39.8 7.7 %collective-permute-start.22 = (bf16[128,768]{1,0:T(8,128)(2,1)S(1)}, bf16[128,768]{1,0:T(8,128)(2,1)S(1)}, u32[]{:S(2)}, u32[]{:S(2)}) collective-permute-start(bf16[128,768]{1,0:T(8,128)(2,1)S(1)} %get-tuple-element.63), channel_id=1, source_target_pairs={{0,8},{4,12},{8,0},{12,4},{16,24},{20,28},{24,16},{28,20},{1,9},{5... | collective-permute-start | bytes 589832 | tf_op jit(solution)/shard_map/ppermute | solution.py:389
  41.4 9.5 %collective-permute-start.23 = (bf16[128,768]{1,0:T(8,128)(2,1)S(1)}, bf16[128,768]{1,0:T(8,128)(2,1)S(1)}, u32[]{:S(2)}, u32[]{:S(2)}) collective-permute-start(bf16[128,768]{1,0:T(8,128)(2,1)S(1)} %get-tuple-element.64), channel_id=1, source_target_pairs={{0,12},{4,8},{8,4},{12,0},{16,28},{20,24},{24,20},{28,16},{1,13},{... | collective-permute-start | bytes 589832 | tf_op jit(solution)/shard_map/ppermute | solution.py:389
  41.8 32.5 %collective-permute-start.3 = (f32[384,256]{1,0:T(8,128)S(1)}, f32[384,256]{1,0:T(8,128)S(1)}, u32[]{:S(2)}, u32[]{:S(2)}) collective-permute-start(f32[384,256]{1,0:T(8,128)S(1)} %add.11.rest_0_), channel_id=1, source_target_pairs={{0,4},{4,0},{8,12},{12,8},{16,20},{20,16},{24,28},{28,24},{1,5},{5... | collective-permute-start | bytes 1179656 | tf_op jit(solution)/shard_map/ppermute | solution.py:224
  42.1 12.9 %collective-permute-start.24 = (bf16[128,768]{1,0:T(8,128)(2,1)S(1)}, bf16[128,768]{1,0:T(8,128)(2,1)S(1)}, u32[]{:S(2)}, u32[]{:S(2)}) collective-permute-start(bf16[128,768]{1,0:T(8,128)(2,1)S(1)} %get-tuple-element.65), channel_id=1, source_target_pairs={{0,16},{4,20},{8,24},{12,28},{16,0},{20,4},{24,8},{28,12},{1,17},{... | collective-permute-start | bytes 589832 | tf_op jit(solution)/shard_map/ppermute | solution.py:389
  43.8 18.2 %collective-permute-start.25 = (bf16[128,768]{1,0:T(8,128)(2,1)S(1)}, bf16[128,768]{1,0:T(8,128)(2,1)S(1)}, u32[]{:S(2)}, u32[]{:S(2)}) collective-permute-start(bf16[128,768]{1,0:T(8,128)(2,1)S(1)} %get-tuple-element.66), channel_id=1, source_target_pairs={{0,20},{4,16},{8,28},{12,24},{16,4},{20,0},{24,12},{28,8},{1,21},{... | collective-permute-start | bytes 589832 | tf_op jit(solution)/shard_map/ppermute | solution.py:389
  47.5 15.5 %collective-permute-start.26 = (bf16[128,768]{1,0:T(8,128)(2,1)S(1)}, bf16[128,768]{1,0:T(8,128)(2,1)S(1)}, u32[]{:S(2)}, u32[]{:S(2)}) collective-permute-start(bf16[128,768]{1,0:T(8,128)(2,1)S(1)} %get-tuple-element.67), channel_id=1, source_target_pairs={{0,24},{4,28},{8,16},{12,20},{16,8},{20,12},{24,0},{28,4},{1,25},{... | collective-permute-start | bytes 589832 | tf_op jit(solution)/shard_map/ppermute | solution.py:389
  50.9 12.5 %collective-permute-start.27 = (bf16[128,768]{1,0:T(8,128)(2,1)S(1)}, bf16[128,768]{1,0:T(8,128)(2,1)S(1)}, u32[]{:S(2)}, u32[]{:S(2)}) collective-permute-start(bf16[128,768]{1,0:T(8,128)(2,1)S(1)} %get-tuple-element.68), channel_id=1, source_target_pairs={{0,28},{4,24},{8,20},{12,16},{16,12},{20,8},{24,4},{28,0},{1,29},{... | collective-permute-start | bytes 589832 | tf_op jit(solution)/shard_map/ppermute | solution.py:389
  55.0 9.7 %collective-permute-start.11 = (bf16[128,256]{1,0:T(8,128)(2,1)S(1)}, bf16[128,256]{1,0:T(8,128)(2,1)S(1)}, u32[]{:S(2)}, u32[]{:S(2)}) collective-permute-start(bf16[128,256]{1,0:T(8,128)(2,1)S(1)} %get-tuple-element.53), channel_id=1, source_target_pairs={{4,0},{0,4},{12,8},{8,12},{20,16},{16,20},{28,24},{24,28},{5,1},{1... | collective-permute-start | bytes 196616 | tf_op jit(solution)/shard_map/ppermute | solution.py:397
  62.0 4.7 %collective-permute-start.12 = (bf16[128,256]{1,0:T(8,128)(2,1)S(1)}, bf16[128,256]{1,0:T(8,128)(2,1)S(1)}, u32[]{:S(2)}, u32[]{:S(2)}) collective-permute-start(bf16[128,256]{1,0:T(8,128)(2,1)S(1)} %get-tuple-element.54), channel_id=1, source_target_pairs={{8,0},{12,4},{0,8},{4,12},{24,16},{28,20},{16,24},{20,28},{9,1},{1... | collective-permute-start | bytes 196616 | tf_op jit(solution)/shard_map/ppermute | solution.py:397
  62.9 5.4 %collective-permute-start.13 = (bf16[128,256]{1,0:T(8,128)(2,1)S(1)}, bf16[128,256]{1,0:T(8,128)(2,1)S(1)}, u32[]{:S(2)}, u32[]{:S(2)}) collective-permute-start(bf16[128,256]{1,0:T(8,128)(2,1)S(1)} %get-tuple-element.55), channel_id=1, source_target_pairs={{12,0},{8,4},{4,8},{0,12},{28,16},{24,20},{20,24},{16,28},{13,1},{... | collective-permute-start | bytes 196616 | tf_op jit(solution)/shard_map/ppermute | solution.py:397
  63.4 7.0 %collective-permute-start.14 = (bf16[128,256]{1,0:T(8,128)(2,1)S(1)}, bf16[128,256]{1,0:T(8,128)(2,1)S(1)}, u32[]{:S(2)}, u32[]{:S(2)}) collective-permute-start(bf16[128,256]{1,0:T(8,128)(2,1)S(1)} %get-tuple-element.56), channel_id=1, source_target_pairs={{16,0},{20,4},{24,8},{28,12},{0,16},{4,20},{8,24},{12,28},{17,1},{... | collective-permute-start | bytes 196616 | tf_op jit(solution)/shard_map/ppermute | solution.py:397
  64.7 6.2 %collective-permute-start.15 = (bf16[128,256]{1,0:T(8,128)(2,1)S(1)}, bf16[128,256]{1,0:T(8,128)(2,1)S(1)}, u32[]{:S(2)}, u32[]{:S(2)}) collective-permute-start(bf16[128,256]{1,0:T(8,128)(2,1)S(1)} %get-tuple-element.57), channel_id=1, source_target_pairs={{20,0},{16,4},{28,8},{24,12},{4,16},{0,20},{12,24},{8,28},{21,1},{... | collective-permute-start | bytes 196616 | tf_op jit(solution)/shard_map/ppermute | solution.py:397
  66.6 5.5 %collective-permute-start.16 = (bf16[128,256]{1,0:T(8,128)(2,1)S(1)}, bf16[128,256]{1,0:T(8,128)(2,1)S(1)}, u32[]{:S(2)}, u32[]{:S(2)}) collective-permute-start(bf16[128,256]{1,0:T(8,128)(2,1)S(1)} %get-tuple-element.58), channel_id=1, source_target_pairs={{24,0},{28,4},{16,8},{20,12},{8,16},{12,20},{0,24},{4,28},{25,1},{... | collective-permute-start | bytes 196616 | tf_op jit(solution)/shard_map/ppermute | solution.py:397
  68.3 4.9 %collective-permute-start.17 = (bf16[128,256]{1,0:T(8,128)(2,1)S(1)}, bf16[128,256]{1,0:T(8,128)(2,1)S(1)}, u32[]{:S(2)}, u32[]{:S(2)}) collective-permute-start(bf16[128,256]{1,0:T(8,128)(2,1)S(1)} %get-tuple-element.59), channel_id=1, source_target_pairs={{28,0},{24,4},{20,8},{16,12},{12,16},{8,20},{4,24},{0,28},{29,1},{... | collective-permute-start | bytes 196616 | tf_op jit(solution)/shard_map/ppermute | solution.py:397
  70.4 7.8 %collective-permute-start.28 = (bf16[128,256]{1,0:T(8,128)(2,1)S(1)}, bf16[128,256]{1,0:T(8,128)(2,1)S(1)}, u32[]{:S(2)}, u32[]{:S(2)}) collective-permute-start(bf16[128,256]{1,0:T(8,128)(2,1)S(1)} %get-tuple-element.70), channel_id=1, source_target_pairs={{4,0},{0,4},{12,8},{8,12},{20,16},{16,20},{28,24},{24,28},{5,1},{1... | collective-permute-start | bytes 196616 | tf_op jit(solution)/shard_map/ppermute | solution.py:397
  70.9 9.0 %collective-permute-start.29 = (bf16[128,256]{1,0:T(8,128)(2,1)S(1)}, bf16[128,256]{1,0:T(8,128)(2,1)S(1)}, u32[]{:S(2)}, u32[]{:S(2)}) collective-permute-start(bf16[128,256]{1,0:T(8,128)(2,1)S(1)} %get-tuple-element.71), channel_id=1, source_target_pairs={{8,0},{12,4},{0,8},{4,12},{24,16},{28,20},{16,24},{20,28},{9,1},{1... | collective-permute-start | bytes 196616 | tf_op jit(solution)/shard_map/ppermute | solution.py:397
  72.1 9.2 %collective-permute-start.30 = (bf16[128,256]{1,0:T(8,128)(2,1)S(1)}, bf16[128,256]{1,0:T(8,128)(2,1)S(1)}, u32[]{:S(2)}, u32[]{:S(2)}) collective-permute-start(bf16[128,256]{1,0:T(8,128)(2,1)S(1)} %get-tuple-element.72), channel_id=1, source_target_pairs={{12,0},{8,4},{4,8},{0,12},{28,16},{24,20},{20,24},{16,28},{13,1},{... | collective-permute-start | bytes 196616 | tf_op jit(solution)/shard_map/ppermute | solution.py:397
  73.3 9.4 %collective-permute-start.31 = (bf16[128,256]{1,0:T(8,128)(2,1)S(1)}, bf16[128,256]{1,0:T(8,128)(2,1)S(1)}, u32[]{:S(2)}, u32[]{:S(2)}) collective-permute-start(bf16[128,256]{1,0:T(8,128)(2,1)S(1)} %get-tuple-element.73), channel_id=1, source_target_pairs={{16,0},{20,4},{24,8},{28,12},{0,16},{4,20},{8,24},{12,28},{17,1},{... | collective-permute-start | bytes 196616 | tf_op jit(solution)/shard_map/ppermute | solution.py:397
  74.3 11.0 %collective-permute-start.32 = (bf16[128,256]{1,0:T(8,128)(2,1)S(1)}, bf16[128,256]{1,0:T(8,128)(2,1)S(1)}, u32[]{:S(2)}, u32[]{:S(2)}) collective-permute-start(bf16[128,256]{1,0:T(8,128)(2,1)S(1)} %get-tuple-element.74), channel_id=1, source_target_pairs={{20,0},{16,4},{28,8},{24,12},{4,16},{0,20},{12,24},{8,28},{21,1},{... | collective-permute-start | bytes 196616 | tf_op jit(solution)/shard_map/ppermute | solution.py:397
  78.2 10.3 %collective-permute-start.33 = (bf16[128,256]{1,0:T(8,128)(2,1)S(1)}, bf16[128,256]{1,0:T(8,128)(2,1)S(1)}, u32[]{:S(2)}, u32[]{:S(2)}) collective-permute-start(bf16[128,256]{1,0:T(8,128)(2,1)S(1)} %get-tuple-element.75), channel_id=1, source_target_pairs={{24,0},{28,4},{16,8},{20,12},{8,16},{12,20},{0,24},{4,28},{25,1},{... | collective-permute-start | bytes 196616 | tf_op jit(solution)/shard_map/ppermute | solution.py:397
  79.8 8.7 %collective-permute-start.34 = (bf16[128,256]{1,0:T(8,128)(2,1)S(1)}, bf16[128,256]{1,0:T(8,128)(2,1)S(1)}, u32[]{:S(2)}, u32[]{:S(2)}) collective-permute-start(bf16[128,256]{1,0:T(8,128)(2,1)S(1)} %get-tuple-element.76), channel_id=1, source_target_pairs={{28,0},{24,4},{20,8},{16,12},{12,16},{8,20},{4,24},{0,28},{29,1},{... | collective-permute-start | bytes 196616 | tf_op jit(solution)/shard_map/ppermute | solution.py:397
  81.4 7.2 %collective-permute-start.18 = (f32[1,2048]{1,0:T(1,128)S(1)}, f32[1,2048]{1,0:T(1,128)S(1)}, u32[]{:S(2)}, u32[]{:S(2)}) collective-permute-start(f32[1,2048]{1,0:T(1,128)S(1)} %get-tuple-element.60.rest_0_), channel_id=1, source_target_pairs={{0,1},{1,2},{2,3},{3,0},{4,5},{5,6},{6,7},{7,4},{8,9},{9,10},{10,1... | collective-permute-start | bytes 24584 | tf_op jit(solution)/shard_map/ppermute | solution.py:416
  82.7 5.9 %collective-permute-start.19 = (f32[1,2048]{1,0:T(1,128)S(1)}, f32[1,2048]{1,0:T(1,128)S(1)}, u32[]{:S(2)}, u32[]{:S(2)}) collective-permute-start(f32[1,2048]{1,0:T(1,128)S(1)} %get-tuple-element.60.rest_0_), channel_id=1, source_target_pairs={{0,2},{1,3},{2,0},{3,1},{4,6},{5,7},{6,4},{7,5},{8,10},{9,11},{10,... | collective-permute-start | bytes 24584 | tf_op jit(solution)/shard_map/ppermute | solution.py:416
  (15 other events, 143.1 us)

commit v2 on v1

v2 whole, which is shorter than its diff:
```python
import functools

import jax
import jax.numpy as jnp
from jax import lax
from jax.experimental import pallas as pl
from jax.experimental.pallas import tpu as pltpu
from jax.sharding import PartitionSpec as P

PATCHES = 32
EPSILON = 1e-06
LANES = 128
CHUNKS = 2
TILE = 512
MIB = 1024 * 1024
F32 = jnp.float32
BF16 = jnp.bfloat16


def dot(a, b):
    return lax.dot_general(a, b, (((1,), (0,)), ((), ())), preferred_element_type=F32)


def dot_bt(a, b):
    return lax.dot_general(a, b, (((1,), (1,)), ((), ())), preferred_element_type=F32)


def dot_at(a, b):
    return lax.dot_general(a, b, (((0,), (0,)), ((), ())), preferred_element_type=F32)


def params():
    return pltpu.CompilerParams(vmem_limit_bytes=40 * MIB)


def full(count):
    return [pl.BlockSpec(memory_space=pltpu.VMEM)] * count


def cost(flops, moved, exps=0):
    return pl.CostEstimate(flops=int(flops), bytes_accessed=int(moved), transcendentals=int(exps))


def power_of_two(n):
    return n & (n - 1) == 0


def crossed(step):
    return (step & ~6) | ((step & 2) << 1) | ((step & 4) >> 1)


def peer(me, step, n):
    if power_of_two(n):
        if n < 8:
            return me ^ step
        odd = me & 1
        return me ^ (step * (1 - odd) + crossed(step) * odd)
    ahead = me + step
    wrap = ahead - n
    return wrap * (wrap >= 0) + ahead * (wrap < 0)


def routes(step, n):
    return [(at, int(peer(at, step, n))) for at in range(n)]


def column(row):
    return jnp.broadcast_to(row, (LANES, LANES)).T


def sort_into(n, start, rows, owned_rows, order, sources, outs, onehot):
    me = lax.axis_index("cam")
    group = onehot.shape[0] // rows
    count = onehot.shape[1]
    for first in range(0, n, group):
        for at in range(group):
            base = peer(me, first + at, n) * owned_rows + start
            slot = lax.broadcasted_iota(jnp.int32, (rows, count), 0) + base
            onehot[at * rows : (at + 1) * rows, :] = (slot == order).astype(F32).astype(BF16)
        for which, source in sources:
            ref = source(first == 0)
            width = ref.shape[1]
            picked = dot(onehot[...], ref[...]).astype(BF16)
            for at in range(group):
                outs[first + at][:, which * width : (which + 1) * width] = picked[
                    at * rows : (at + 1) * rows
                ]


def first_sort_kernel(n, start, rows, owned_rows, order_in, q_in, k_in, v_in, *rest):
    outs, (order_ref, q_ref, k_ref, v_ref, onehot, sems) = rest[:n], rest[n:]
    copies = [
        pltpu.make_async_copy(source, target, sems.at[at])
        for at, (source, target) in enumerate(
            ((order_in, order_ref), (k_in, k_ref), (v_in, v_ref), (q_in, q_ref))
        )
    ]
    for copy in copies:
        copy.start()
    copies[0].wait()

    def arrives(ref, copy):
        def get(first):
            if first:
                copy.wait()
            return ref

        return get

    sources = (
        (1, arrives(k_ref, copies[1])),
        (2, arrives(v_ref, copies[2])),
        (0, arrives(q_ref, copies[3])),
    )
    sort_into(n, start, rows, owned_rows, order_ref[...], sources, outs, onehot)


def sort_kernel(n, start, rows, owned_rows, order_ref, q_ref, k_ref, v_ref, *rest):
    outs, onehot = rest[:n], rest[n]
    sources = ((0, lambda _: q_ref), (1, lambda _: k_ref), (2, lambda _: v_ref))
    sort_into(n, start, rows, owned_rows, order_ref[...], sources, outs, onehot)


def sort_tokens(order, q, k, v, n, start, rows, owned_rows, first):
    count, width = q.shape
    group = max(1, min(n, 512 // rows))
    while n % group:
        group -= 1
    shapes = [jax.ShapeDtypeStruct((rows, 3 * width), BF16)] * n
    scratch = [pltpu.VMEM((group * rows, count), BF16)]
    if first:
        shapes = shapes + [
            jax.ShapeDtypeStruct(array.shape, array.dtype) for array in (order, q, k, v)
        ]
        scratch = scratch + [pltpu.SemaphoreType.DMA((4,))]
    return pl.pallas_call(
        functools.partial(
            first_sort_kernel if first else sort_kernel, n, start, rows, owned_rows
        ),
        out_shape=shapes,
        in_specs=[pl.BlockSpec(memory_space=pltpu.HBM)] * 4 if first else full(4),
        out_specs=full(len(shapes)),
        scratch_shapes=scratch,
        compiler_params=params(),
        cost_estimate=cost(6 * n * rows * count * width, 6 * count * width),
        name="sort_tokens",
    )(order, q, k, v)


def attend_kernel(n, scale, *refs):
    ins, outs = refs[:n], refs[-3 - n : -3]
    q_all, k_all, v_all = refs[-3:]
    rows = ins[0].shape[0]
    width = outs[0].shape[1]
    group = n * PATCHES
    block = min(group, 256)
    for stamp in range(rows // PATCHES):
        here = slice(stamp * PATCHES, (stamp + 1) * PATCHES)
        for cam in range(n):
            there = slice(cam * PATCHES, (cam + 1) * PATCHES)
            q_all[there, :] = ins[cam][here, 0:width]
            k_all[there, :] = ins[cam][here, width : 2 * width]
            v_all[there, :] = ins[cam][here, 2 * width : 3 * width]
        for low in range(0, group, block):
            scores = dot_bt(q_all[low : low + block, :], k_all[...]) * scale
            scores = scores - jnp.max(scores, axis=-1, keepdims=True)
            expo = jnp.exp(scores)
            probs = (expo / jnp.sum(expo, axis=-1, keepdims=True)).astype(BF16)
            result = dot(probs, v_all[...]).astype(BF16)
            for cam in range(low // PATCHES, (low + block) // PATCHES):
                at = cam * PATCHES - low
                outs[cam][here, :] = result[at : at + PATCHES]


def attend(blocks, after, n, width):
    rows = blocks[0].shape[0]
    group = n * PATCHES
    return pl.pallas_call(
        functools.partial(attend_kernel, n, width**-0.5),
        out_shape=[jax.ShapeDtypeStruct((rows, width), BF16)] * n,
        in_specs=full(n) + [pl.BlockSpec(memory_space=pl.ANY)] * len(after),
        out_specs=full(n),
        scratch_shapes=[pltpu.VMEM((group, width), BF16)] * 3,
        compiler_params=params(),
        cost_estimate=cost(
            4 * n * rows * group * width, 8 * n * rows * width, n * rows * group
        ),
        name="attend",
    )(*blocks, *after)


def grads_kernel(n, split, k_ref, v_ref, rate_ref, one_ref, three_ref, two_ref, *rest):
    outs, total = rest[:-1], rest[-1]
    count, width = k_ref.shape
    hid = one_ref.shape[1]
    one, three, two = one_ref[0], three_ref[0], two_ref[0]
    tile = min(count, TILE)
    for start in range(0, count, tile):
        k = k_ref[start : start + tile, :]
        h_one = dot_bt(k, one)
        h_three = dot_bt(k, three)
        sigma = jax.nn.sigmoid(h_one)
        gated = h_one * sigma
        active = (gated * h_three).astype(BF16)
        pieces = []
        for low in range(start, start + tile, LANES):
            rate = column(rate_ref[:, low : low + LANES])
            rate = jnp.concatenate([rate] * (width // LANES), axis=1)
            pieces.append((-rate * v_ref[low : low + LANES, :].astype(F32)).astype(BF16))
        error = jnp.concatenate(pieces, axis=0)
        back = dot(error, two)
        back_one = (back * h_three * sigma * (1.0 + h_one * (1.0 - sigma))).astype(BF16)
        back_three = (back * gated).astype(BF16)
        sums = (dot_at(back_one, k), dot_at(back_three, k), dot_at(error, active))
        for which, term in enumerate(sums):
            here = slice(which * hid, (which + 1) * hid)
            total[here, :] = term if start == 0 else total[here, :] + term
    if split:
        half = total.shape[0] // 2
        core = lax.axis_index("cam") & 1
        outs[0][...] = total[pl.ds(pl.multiple_of(core * half, half), half), :]
        outs[1][...] = total[pl.ds(pl.multiple_of((1 - core) * half, half), half), :]
    else:
        outs[0][...] = total[...]


def gradients(k, v, rate, one, three, two, n):
    count, width = k.shape
    hid = one.shape[1]
    split = n > 1 and power_of_two(n)
    assert hid == width
    rows = 3 * hid
    parts = 2 if split else 1
    return pl.pallas_call(
        functools.partial(grads_kernel, n, split),
        out_shape=[jax.ShapeDtypeStruct((rows // parts, width), F32)] * parts,
        in_specs=full(6),
        out_specs=full(parts),
        scratch_shapes=[pltpu.VMEM((rows, width), F32)],
        compiler_params=params(),
        cost_estimate=cost(12 * count * width * hid, 8 * count * width, count * hid),
        name="gradients",
    )(k, v, rate, one, three, two)


def sum_over_cams(parts, n):
    if len(parts) == 1:
        return [lax.psum(parts[0], "cam")]
    keep, send = parts
    bits = n.bit_length() - 1
    pair = [(at, at ^ 1) for at in range(n)]
    mine = keep + lax.ppermute(send, "cam", pair)
    span = bits - 1
    for step in range(span):
        pairs = []
        for at in range(n):
            bit = 1 + (step + (at & 1)) % span
            pairs.append((at, at ^ (1 << bit)))
        mine = mine + lax.ppermute(mine.astype(BF16), "cam", pairs).astype(F32)
    return [mine, lax.ppermute(mine, "cam", pair)]


def readout_kernel(parts, q_ref, one_ref, three_ref, two_ref, *rest):
    grads, (y_ref, sq_ref, total, fresh) = rest[:parts], rest[parts:]
    hid, width = one_ref.shape[1:]
    if parts == 2:
        half = total.shape[0] // 2
        core = lax.axis_index("cam") & 1
        total[pl.ds(pl.multiple_of(core * half, half), half), :] = grads[0][...]
        total[pl.ds(pl.multiple_of((1 - core) * half, half), half), :] = grads[1][...]
    else:
        total[...] = grads[0][...]
    entries = hid * width
    for which, ref in enumerate((one_ref, three_ref, two_ref)):
        grad = total[which * hid : (which + 1) * hid, :]
        weight = ref[0].astype(F32)
        row_sq = jnp.sum(weight * weight, axis=1, keepdims=True)
        weight_sq = jnp.sum(row_sq, axis=0, keepdims=True)
        grad_sq = jnp.sum(jnp.sum(grad * grad, axis=1, keepdims=True), axis=0, keepdims=True)
        scale = jnp.sqrt(weight_sq / entries) / jnp.sqrt(grad_sq / entries + EPSILON)
        moved = weight - scale * grad
        ratio = jnp.sqrt(row_sq) / jnp.sqrt(
            jnp.sum(moved * moved, axis=1, keepdims=True) + EPSILON
        )
        fresh[which * hid : (which + 1) * hid, :] = (moved * ratio).astype(BF16)
    count = q_ref.shape[0]
    tile = min(count, TILE)
    ones = jnp.ones((8, width), BF16)
    for start in range(0, count, tile):
        here = slice(start, start + tile)
        q = q_ref[here, :]
        h_one = dot_bt(q, fresh[0:hid, :])
        h_three = dot_bt(q, fresh[hid : 2 * hid, :])
        active = (h_one * jax.nn.sigmoid(h_one) * h_three).astype(BF16)
        y = dot_bt(active, fresh[2 * hid :, :])
        y_ref[here, :] = y
        square = y * y
        high = square.astype(BF16)
        low = (square - high.astype(F32)).astype(BF16)
        sq_ref[:, here] = (dot_bt(ones, high) + dot_bt(ones, low))[0:1, :]


def read_out(q, one, three, two, grads):
    count, width = q.shape
    hid = one.shape[1]
    parts = len(grads)
    return pl.pallas_call(
        functools.partial(readout_kernel, parts),
        out_shape=[
            jax.ShapeDtypeStruct((count, width), F32),
            jax.ShapeDtypeStruct((1, count), F32),
        ],
        in_specs=full(4 + parts),
        out_specs=full(2),
        scratch_shapes=[pltpu.VMEM((3 * hid, width), F32), pltpu.VMEM((3 * hid, width), BF16)],
        compiler_params=params(),
        cost_estimate=cost(6 * count * width * hid, 8 * count * width, count * hid),
        name="read_out",
    )(q, one, three, two, *grads)


def slot_row(n, start, rows, owned_rows):
    me = lax.axis_index("cam")
    at = lax.broadcasted_iota(jnp.int32, (8, n * rows), 1)
    step = jnp.zeros_like(at)
    for cut in range(1, n):
        step = step + (at >= cut * rows).astype(jnp.int32)
    return peer(me, step, n) * owned_rows + start + at - step * rows


def placed(order_ref, low, slots, onehot, joined):
    tile = onehot.shape[0]
    for at in range(0, tile, LANES):
        wanted = column(order_ref[:, low + at : low + at + LANES].astype(F32))
        for lane in range(0, onehot.shape[1], LANES):
            hit = wanted == slots[:, lane : lane + LANES]
            onehot[at : at + LANES, lane : lane + LANES] = hit.astype(F32).astype(BF16)
    return dot(onehot[...], joined[...])


def base_kernel(heads, shapes, order_ref, gain_ref, y_ref, *rest):
    squares, rest = rest[:heads], rest[heads:]
    count, width = y_ref.shape
    n, given = shapes
    groups = [rest[at * n : (at + 1) * n] for at in range(len(given))]
    out_ref = rest[len(given) * n]
    scratch = rest[len(given) * n + 1 :]
    total = squares[0][...]
    for ref in squares[1:]:
        total = total + ref[...]
    inverse = 1.0 / jnp.sqrt(total / (width * heads) + EPSILON)
    gain = gain_ref[...]
    owned_rows = count // n
    tile = min(count, TILE)
    laid = []
    for at, (start, rows) in enumerate(given):
        onehot, joined = scratch[2 * at : 2 * at + 2]
        for cam in range(n):
            joined[cam * rows : (cam + 1) * rows, :] = groups[at][cam][...]
        laid.append((slot_row(n, start, rows, owned_rows)[0:1, :].astype(F32), onehot, joined))
    for low in range(0, count, tile):
        parts = [placed(order_ref, low, *entry) for entry in laid]
        for at in range(0, tile, LANES):
            here = slice(low + at, low + at + LANES)
            norm = column(inverse[:, here])
            norm = jnp.concatenate([norm] * (width // LANES), axis=1)
            value = y_ref[here, :] * norm * gain
            for part in parts:
                value = value + part[at : at + LANES]
            out_ref[here, :] = value


def base(order, gain, y, squares, groups, starts, n):
    count, width = y.shape
    heads = len(squares)
    tile = min(count, TILE)
    scratch = []
    for _, rows in starts:
        scratch.append(pltpu.VMEM((tile, n * rows), BF16))
        scratch.append(pltpu.VMEM((n * rows, width), BF16))
    blocks = [block for group in groups for block in group]
    moved = sum(n * rows for _, rows in starts)
    return pl.pallas_call(
        functools.partial(base_kernel, heads, (n, tuple(starts))),
        out_shape=jax.ShapeDtypeStruct((count, width), F32),
        in_specs=full(3 + heads + len(blocks)),
        out_specs=pl.BlockSpec(memory_space=pltpu.VMEM),
        scratch_shapes=scratch,
        compiler_params=params(),
        cost_estimate=cost(2 * count * moved * width, 8 * count * width),
        name="base",
    )(order, gain, y, *squares, *blocks)


def mix_kernel(n, start, rows, owned_rows, order_ref, base_ref, *rest):
    blocks, (out_ref, onehot, joined) = rest[:n], rest[n:]
    step = pl.program_id(0)

    @pl.when(step == 0)
    def _():
        for at in range(n):
            joined[at * rows : (at + 1) * rows, :] = blocks[at][...]

    slots = slot_row(n, start, rows, owned_rows)[0:1, :].astype(F32)
    part = placed(order_ref, 0, slots, onehot, joined)
    out_ref[...] = (base_ref[...] + part).astype(BF16)


def mix(order, given, blocks, n, start, owned_rows):
    count, width = given.shape
    rows = blocks[0].shape[0]
    tile = min(count, TILE)
    return pl.pallas_call(
        functools.partial(mix_kernel, n, start, rows, owned_rows),
        grid=(count // tile,),
        out_shape=jax.ShapeDtypeStruct((count, width), BF16),
        in_specs=[
            pl.BlockSpec((1, tile), lambda i: (0, i)),
            pl.BlockSpec((tile, width), lambda i: (i, 0)),
        ]
        + full(n),
        out_specs=pl.BlockSpec((tile, width), lambda i: (i, 0)),
        scratch_shapes=[
            pltpu.VMEM((tile, n * rows), BF16),
            pltpu.VMEM((n * rows, width), BF16),
        ],
        compiler_params=params(),
        cost_estimate=cost(2 * count * n * rows * width, 8 * count * width),
        name="mix",
    )(order, given, *blocks)


def exchange(blocks, n):
    return [blocks[0]] + [
        lax.ppermute(blocks[step], "cam", routes(step, n)) for step in range(1, n)
    ]


def give_back(blocks, n):
    moved = [blocks[0]]
    for step in range(1, n):
        pairs = [(target, at) for at, target in routes(step, n)]
        moved.append(lax.ppermute(blocks[step], "cam", pairs))
    return moved


def per_device(queries, keys, values, rates, w_one, w_three, w_two, gain, order):
    count, width = queries.shape
    n = lax.axis_size("cam")
    heads = lax.axis_size("head")
    owned_rows = count // n
    chunks = CHUNKS if (owned_rows // PATCHES) % CHUNKS == 0 else 1
    rows = owned_rows // chunks
    arrived = []
    for at in range(chunks):
        blocks = sort_tokens(
            order, queries, keys, values, n, at * rows, rows, owned_rows, at == 0
        )
        if at == 0:
            order, queries, keys, values = blocks[n:]
            blocks = blocks[:n]
        arrived.append(exchange(blocks, n))
    parts = gradients(keys, values, rates.reshape(1, count), w_one, w_three, w_two, n)
    summed = sum_over_cams(parts, n)
    y, square = read_out(queries, w_one, w_three, w_two, summed)
    squares = [square] + [
        lax.ppermute(square, "head", [(at, (at + step) % heads) for at in range(heads)])
        for step in range(1, heads)
    ]
    returned = []
    for at in range(chunks):
        after = [square] if at == chunks - 1 else []
        returned.append(give_back(attend(arrived[at], after, n, width), n))
    starts = [(at * rows, rows) for at in range(chunks)]
    given = base(order, gain.reshape(1, width), y, squares, returned[:-1], starts[:-1], n)
    return mix(order, given, returned[-1], n, starts[-1][0], owned_rows)


def solution(mesh):
    in_specs = (
        P("cam", "head"),
        P("cam", "head"),
        P("cam", "head"),
        P("cam", "head"),
        P("head", None, None),
        P("head", None, None),
        P("head", None, None),
        P("head"),
        P("cam", None),
    )
    out_specs = P("cam", "head")
    return jax.shard_map(
        per_device, mesh=mesh, in_specs=in_specs, out_specs=out_specs, check_vma=False
    )
```

time: 92.1 us -> 89.6 us (0.973)
  waiting for transfers between devices: 23.3 us -> 21.1 us
  local copies, waits for them, and re-layouts: 5.88 us -> 4.39 us
    ppermute x14, waiting for transfers between devices: 18.8 us -> 13.7 us  [exchange(): lax.ppermute(blocks[step], 'cam', routes(step, n))]
    ppermute x3, waiting for transfers between devices: 0.37 us -> 3.68 us  [per_device(): lax.ppermute(square, 'head', [(at, (at + step) % heads) for at in range(h...]
    unnamed x24 -> x18, local copies, waits for them, and re-layouts: 5.88 us -> 4.39 us
    ppermute x14, starting transfers between devices: 17.1 us -> 18.1 us  [exchange(): lax.ppermute(blocks[step], 'cam', routes(step, n))]
    ppermute x14, starting transfers between devices: 12.6 us -> 13.6 us  [give_back(): moved.append(lax.ppermute(blocks[step], 'cam', pairs))]
  transfers between devices with their start and end apart: 35 -> 35, of which waited for: 11 -> 12; matrix products, arithmetic and copies ran while one was open for 0% -> 0% of each run, Pallas kernels for 16% -> 12%
where the time goes in v2:
time: 89.6 us; the launch traced here: 89.4 us
  starting transfers between devices  41.8 us (47%)
  Pallas kernels  21.6 us (24%)
  waiting for transfers between devices  21.1 us (24%)
  local copies, waits for them, and re-layouts  4.39 us (5%)
    ppermute x14, starting transfers between devices, exchange(): lax.ppermute(blocks[step], 'cam', routes(step, n))  18.1 us
    ppermute x14, waiting for transfers between devices, exchange(): lax.ppermute(blocks[step], 'cam', routes(step, n))  13.7 us
    ppermute x14, starting transfers between devices, give_back(): moved.append(lax.ppermute(blocks[step], 'cam', pairs))  13.6 us
    pallas_call x2, Pallas kernels, sort_tokens(): pl.pallas_call(functools.partial(first_sort_kernel if first else sort_ker...  8.59 us
    ppermute x2, starting transfers between devices, sum_over_cams(): mine = mine + lax.ppermute(mine.astype(BF16), 'cam', pairs).astype(F32)  5.03 us
    ppermute x3, starting transfers between devices, per_device(): lax.ppermute(square, 'head', [(at, (at + step) % heads) for at in range(h...  4.61 us
    unnamed x18, local copies, waits for them, and re-layouts  4.39 us
    ppermute x3, waiting for transfers between devices, per_device(): lax.ppermute(square, 'head', [(at, (at + step) % heads) for at in range(h...  3.68 us
  transfers between devices with their start and end apart: 35, of which 12 were waited for; matrix products, arithmetic and copies ran while one was open for 0% of the time, Pallas kernels for 12%

profile of v2, /device:TPU:0, one launch (start us, length us, event | category | flops | bytes accessed | tf_op | source)
XLA Modules:
  0.0 89.4 jit_solution(10514161196486920570)
XLA Ops:
  0.0 1.2 %copy-done.1 = bf16[2048,256]{1,0:T(8,128)(2,1)S(1)} copy-done((bf16[2048,256]{1,0:T(8,128)(2,1)S(1)}, bf16[2048,256]{1,0:T(8,128)(2,1)}, u32[]{:S(2)}) %copy-start.1) | copy-done | bytes 1048600
  1.2 1.2 %copy-done.2 = bf16[2048,256]{1,0:T(8,128)(2,1)S(1)} copy-done((bf16[2048,256]{1,0:T(8,128)(2,1)S(1)}, bf16[2048,256]{1,0:T(8,128)(2,1)}, u32[]{:S(2)}) %copy-start.2) | copy-done | bytes 1048600
  2.5 1.2 %copy-done.3 = bf16[2048,256]{1,0:T(8,128)(2,1)S(1)} copy-done((bf16[2048,256]{1,0:T(8,128)(2,1)S(1)}, bf16[2048,256]{1,0:T(8,128)(2,1)}, u32[]{:S(2)}) %copy-start.3) | copy-done | bytes 1048600
  4.4 5.1 %sort_tokens.2 = (bf16[128,768]{1,0:T(8,128)(2,1)S(1)}, bf16[128,768]{1,0:T(8,128)(2,1)S(1)}, bf16[128,768]{1,0:T(8,128)(2,1)S(1)}, bf16[128,768]{1,0:T(8,128)(2...) custom-call(s32[1,2048]{1,0:T(1,128)S(1)} %copy-done.7, ...), custom_call_target="tpu_custom_call" | custom-call | flops 3221225472 | bytes 3145728 | tf_op jit(solution)/shard_map/sort_tokens/pallas_call | solution.py:136
  9.6 2.9 %gradients.1 = (f32[384,256]{1,0:T(8,128)S(1)}, f32[384,256]{1,0:T(8,128)S(1)}) custom-call(bf16[2048,256]{1,0:T(8,128)(2,1)S(1)} %get-tuple-element.47.k_ref, bf16[2048,256]{1,0:T(8,128)(2,1)S(1)} %get-tuple-element.48.v_ref, f32[1,2048]{1,0:T(1,128)S(1)} %bitcast.3, bf16[1,256,256]{2,1,0:T(8,128)(2,1)S(1)} %copy-done.4, ...), custom_call_target="tpu_custom_call" | custom-call | flops 1610612736 | bytes 4194304 | tf_op jit(solution)/shard_map/gradients/pallas_call | solution.py:234
  13.0 1.3 %collective-permute-done = f32[384,256]{1,0:T(8,128)S(1)} collective-permute-done((f32[384,256]{1,0:T(8,128)S(1)}, f32[384,256]{1,0:T(8,128)S(1)}, u32[]{:S(2)}, u32[]{:S(2)}) %collective-permute-start) | collective-permute-done | bytes 393248 | tf_op jit(solution)/shard_map/ppermute | solution.py:252
  14.4 2.9 %collective-permute-start.1 = (bf16[384,256]{1,0:T(8,128)(2,1)S(1)}, bf16[384,256]{1,0:T(8,128)(2,1)S(1)}, u32[]{:S(2)}, u32[]{:S(2)}) collective-permute-start(bf16[384,256]{1,0:T(8,128)(2,1)S(1)} %get-tuple-element.85), channel_id=1, source_target_pairs={{0,8},{4,20},{8,0},{12,28},{16,24},{20,4},{24,16},{28,12},{1,9},{5... | collective-permute-start | bytes 589832 | tf_op jit(solution)/shard_map/ppermute | solution.py:259
  17.3 1.4 %collective-permute-start.8 = (bf16[128,768]{1,0:T(8,128)(2,1)S(1)}, bf16[128,768]{1,0:T(8,128)(2,1)S(1)}, u32[]{:S(2)}, u32[]{:S(2)}) collective-permute-start(bf16[128,768]{1,0:T(8,128)(2,1)S(1)} %get-tuple-element.55), channel_id=1, source_target_pairs={{0,8},{4,20},{8,0},{12,28},{16,24},{20,4},{24,16},{28,12},{1,9},{5... | collective-permute-start | bytes 589832 | tf_op jit(solution)/shard_map/ppermute | solution.py:435
  21.0 2.1 %collective-permute-start.2 = (bf16[384,256]{1,0:T(8,128)(2,1)S(1)}, bf16[384,256]{1,0:T(8,128)(2,1)S(1)}, u32[]{:S(2)}, u32[]{:S(2)}) collective-permute-start(bf16[384,256]{1,0:T(8,128)(2,1)S(1)} %fusion), channel_id=1, source_target_pairs={{0,16},{4,12},{8,24},{12,4},{16,0},{20,28},{24,8},{28,20},{1,17},{... | collective-permute-start | bytes 589832 | tf_op jit(solution)/shard_map/ppermute | solution.py:259
  23.1 3.5 %sort_tokens.3 = (bf16[128,768]{1,0:T(8,128)(2,1)S(1)}, bf16[128,768]{1,0:T(8,128)(2,1)S(1)}, bf16[128,768]{1,0:T(8,128)(2,1)S(1)}, bf16[128,768]{1,0:T(8,128)(2...) custom-call(s32[1,2048]{1,0:T(1,128)S(1)} %get-tuple-element.45.orde, ...), custom_call_target="tpu_custom_call" | custom-call | flops 3221225472 | bytes 3145728 | tf_op jit(solution)/shard_map/sort_tokens/pallas_call | solution.py:136
  26.8 1.8 %collective-permute-start.12 = (bf16[128,768]{1,0:T(8,128)(2,1)S(1)}, bf16[128,768]{1,0:T(8,128)(2,1)S(1)}, u32[]{:S(2)}, u32[]{:S(2)}) collective-permute-start(bf16[128,768]{1,0:T(8,128)(2,1)S(1)} %get-tuple-element.59), channel_id=1, source_target_pairs={{0,24},{4,28},{8,16},{12,20},{16,8},{20,12},{24,0},{28,4},{1,25},{... | collective-permute-start | bytes 589832 | tf_op jit(solution)/shard_map/ppermute | solution.py:435
  28.5 3.9 %collective-permute-start.13 = (bf16[128,768]{1,0:T(8,128)(2,1)S(1)}, bf16[128,768]{1,0:T(8,128)(2,1)S(1)}, u32[]{:S(2)}, u32[]{:S(2)}) collective-permute-start(bf16[128,768]{1,0:T(8,128)(2,1)S(1)} %get-tuple-element.60), channel_id=1, source_target_pairs={{0,28},{4,24},{8,20},{12,16},{16,12},{20,8},{24,4},{28,0},{1,29},{... | collective-permute-start | bytes 589832 | tf_op jit(solution)/shard_map/ppermute | solution.py:435
  33.3 2.2 %collective-permute-done.12.refs_6_ = bf16[128,768]{1,0:T(8,128)(2,1)S(1)} collective-permute-done((bf16[128,768]{1,0:T(8,128)(2,1)S(1)}, bf16[128,768]{1,0:T(8,128)(2,1)S(1)}, u32[]{:S(2)}, u32[]{:S(2)}) %collective-permute-start.12) | collective-permute-done | bytes 196640 | tf_op jit(solution)/shard_map/ppermute | solution.py:435
  35.5 4.1 %collective-permute-start.23 = (bf16[128,768]{1,0:T(8,128)(2,1)S(1)}, bf16[128,768]{1,0:T(8,128)(2,1)S(1)}, u32[]{:S(2)}, u32[]{:S(2)}) collective-permute-start(bf16[128,768]{1,0:T(8,128)(2,1)S(1)} %get-tuple-element.72), channel_id=1, source_target_pairs={{0,12},{4,16},{8,4},{12,24},{16,28},{20,0},{24,20},{28,8},{1,13},{... | collective-permute-start | bytes 589832 | tf_op jit(solution)/shard_map/ppermute | solution.py:435
  39.6 3.6 %collective-permute-done.13.refs_7_ = bf16[128,768]{1,0:T(8,128)(2,1)S(1)} collective-permute-done((bf16[128,768]{1,0:T(8,128)(2,1)S(1)}, bf16[128,768]{1,0:T(8,128)(2,1)S(1)}, u32[]{:S(2)}, u32[]{:S(2)}) %collective-permute-start.13) | collective-permute-done | bytes 196640 | tf_op jit(solution)/shard_map/ppermute | solution.py:435
  43.2 2.6 %collective-permute-start.26 = (bf16[128,768]{1,0:T(8,128)(2,1)S(1)}, bf16[128,768]{1,0:T(8,128)(2,1)S(1)}, u32[]{:S(2)}, u32[]{:S(2)}) collective-permute-start(bf16[128,768]{1,0:T(8,128)(2,1)S(1)} %get-tuple-element.75), channel_id=1, source_target_pairs={{0,24},{4,28},{8,16},{12,20},{16,8},{20,12},{24,0},{28,4},{1,25},{... | collective-permute-start | bytes 589832 | tf_op jit(solution)/shard_map/ppermute | solution.py:435
  45.8 2.7 %collective-permute-start.27 = (bf16[128,768]{1,0:T(8,128)(2,1)S(1)}, bf16[128,768]{1,0:T(8,128)(2,1)S(1)}, u32[]{:S(2)}, u32[]{:S(2)}) collective-permute-start(bf16[128,768]{1,0:T(8,128)(2,1)S(1)} %get-tuple-element.76), channel_id=1, source_target_pairs={{0,28},{4,24},{8,20},{12,16},{16,12},{20,8},{24,4},{28,0},{1,29},{... | collective-permute-start | bytes 589832 | tf_op jit(solution)/shard_map/ppermute | solution.py:435
  49.8 7.1 %collective-permute-done.25.refs_5_ = bf16[128,768]{1,0:T(8,128)(2,1)S(1)} collective-permute-done((bf16[128,768]{1,0:T(8,128)(2,1)S(1)}, bf16[128,768]{1,0:T(8,128)(2,1)S(1)}, u32[]{:S(2)}, u32[]{:S(2)}) %collective-permute-start.25) | collective-permute-done | bytes 196640 | tf_op jit(solution)/shard_map/ppermute | solution.py:435
  56.9 1.9 %collective-permute-start.15 = (bf16[128,256]{1,0:T(8,128)(2,1)S(1)}, bf16[128,256]{1,0:T(8,128)(2,1)S(1)}, u32[]{:S(2)}, u32[]{:S(2)}) collective-permute-start(bf16[128,256]{1,0:T(8,128)(2,1)S(1)} %get-tuple-element.63), channel_id=1, source_target_pairs={{8,0},{20,4},{0,8},{28,12},{24,16},{4,20},{16,24},{12,28},{9,1},{2... | collective-permute-start | bytes 196616 | tf_op jit(solution)/shard_map/ppermute | solution.py:443
  58.8 1.7 %collective-permute-start.16 = (bf16[128,256]{1,0:T(8,128)(2,1)S(1)}, bf16[128,256]{1,0:T(8,128)(2,1)S(1)}, u32[]{:S(2)}, u32[]{:S(2)}) collective-permute-start(bf16[128,256]{1,0:T(8,128)(2,1)S(1)} %get-tuple-element.64), channel_id=1, source_target_pairs={{12,0},{16,4},{4,8},{24,12},{28,16},{0,20},{20,24},{8,28},{13,1},{... | collective-permute-start | bytes 196616 | tf_op jit(solution)/shard_map/ppermute | solution.py:443
  60.8 2.7 %read_out.1 = (f32[2048,256]{1,0:T(8,128)S(1)}, f32[1,2048]{1,0:T(1,128)S(1)}) custom-call(bf16[2048,256]{1,0:T(8,128)(2,1)S(1)} %get-tuple-element.46.q_ref, bf16[1,256,256]{2,1,0:T(8,128)(2,1)S(1)} %copy-done.4, bf16[1,256,256]{2,1,0:T(8,128)(2,1)S(1)} %copy-done.5, bf16[1,256,256]{2,1,0:T(8,128)(2,1)S(1)} %copy-done.6, ...), custom_call_target="tpu_custom_call" | custom-call | flops 805306368 | bytes 4194304 | tf_op jit(solution)/shard_map/read_out/pallas_call | solution.py:307
  63.6 2.4 %collective-permute-start.19 = (bf16[128,256]{1,0:T(8,128)(2,1)S(1)}, bf16[128,256]{1,0:T(8,128)(2,1)S(1)}, u32[]{:S(2)}, u32[]{:S(2)}) collective-permute-start(bf16[128,256]{1,0:T(8,128)(2,1)S(1)} %get-tuple-element.67), channel_id=1, source_target_pairs={{24,0},{28,4},{16,8},{20,12},{8,16},{12,20},{0,24},{4,28},{25,1},{... | collective-permute-start | bytes 196616 | tf_op jit(solution)/shard_map/ppermute | solution.py:443
  66.0 1.7 %collective-permute-start.20 = (bf16[128,256]{1,0:T(8,128)(2,1)S(1)}, bf16[128,256]{1,0:T(8,128)(2,1)S(1)}, u32[]{:S(2)}, u32[]{:S(2)}) collective-permute-start(bf16[128,256]{1,0:T(8,128)(2,1)S(1)} %get-tuple-element.68), channel_id=1, source_target_pairs={{28,0},{24,4},{20,8},{16,12},{12,16},{8,20},{4,24},{0,28},{29,1},{... | collective-permute-start | bytes 196616 | tf_op jit(solution)/shard_map/ppermute | solution.py:443
  67.7 1.1 %attend.3 = (bf16[128,256]{1,0:T(8,128)(2,1)S(1)}, bf16[128,256]{1,0:T(8,128)(2,1)S(1)}, bf16[128,256]{1,0:T(8,128)(2,1)S(1)}, bf16[128,256]{1,0:T(8,128)(2,1)S(...) custom-call(bf16[128,768]{1,0:T(8,128)(2,1)S(1)} %get-tuple-element., ...), custom_call_target="tpu_custom_call" | custom-call | flops 268435456 | bytes 2097152 | tf_op jit(solution)/shard_map/attend/pallas_call | solution.py:178
  68.9 1.2 %collective-permute-start.29 = (bf16[128,256]{1,0:T(8,128)(2,1)S(1)}, bf16[128,256]{1,0:T(8,128)(2,1)S(1)}, u32[]{:S(2)}, u32[]{:S(2)}) collective-permute-start(bf16[128,256]{1,0:T(8,128)(2,1)S(1)} %get-tuple-element.79), channel_id=1, source_target_pairs={{8,0},{20,4},{0,8},{28,12},{24,16},{4,20},{16,24},{12,28},{9,1},{2... | collective-permute-start | bytes 196616 | tf_op jit(solution)/shard_map/ppermute | solution.py:443
  70.1 3.6 %collective-permute-start.6 = (f32[1,2048]{1,0:T(1,128)S(1)}, f32[1,2048]{1,0:T(1,128)S(1)}, u32[]{:S(2)}, u32[]{:S(2)}) collective-permute-start(f32[1,2048]{1,0:T(1,128)S(1)} %get-tuple-element.52.rest_0_.refs_8_), channel_id=1, source_target_pairs={{0,3},{1,0},{2,1},{3,2},{4,7},{5,4},{6,5},{7,6},{8,11},{9,8},{10,9... | collective-permute-start | bytes 24584 | tf_op jit(solution)/shard_map/ppermute | solution.py:467
  75.1 3.2 %collective-permute-done.5.rest_2_ = f32[1,2048]{1,0:T(1,128)S(1)} collective-permute-done((f32[1,2048]{1,0:T(1,128)S(1)}, f32[1,2048]{1,0:T(1,128)S(1)}, u32[]{:S(2)}, u32[]{:S(2)}) %collective-permute-start.5) | collective-permute-done | bytes 8224 | tf_op jit(solution)/shard_map/ppermute | solution.py:467
  79.2 1.4 %collective-permute-start.33 = (bf16[128,256]{1,0:T(8,128)(2,1)S(1)}, bf16[128,256]{1,0:T(8,128)(2,1)S(1)}, u32[]{:S(2)}, u32[]{:S(2)}) collective-permute-start(bf16[128,256]{1,0:T(8,128)(2,1)S(1)} %get-tuple-element.83), channel_id=1, source_target_pairs={{24,0},{28,4},{16,8},{20,12},{8,16},{12,20},{0,24},{4,28},{25,1},{... | collective-permute-start | bytes 196616 | tf_op jit(solution)/shard_map/ppermute | solution.py:443
  80.7 2.0 %collective-permute-start.34 = (bf16[128,256]{1,0:T(8,128)(2,1)S(1)}, bf16[128,256]{1,0:T(8,128)(2,1)S(1)}, u32[]{:S(2)}, u32[]{:S(2)}) collective-permute-start(bf16[128,256]{1,0:T(8,128)(2,1)S(1)} %get-tuple-element.84), channel_id=1, source_target_pairs={{28,0},{24,4},{20,8},{16,12},{12,16},{8,20},{4,24},{0,28},{29,1},{... | collective-permute-start | bytes 196616 | tf_op jit(solution)/shard_map/ppermute | solution.py:443
  82.7 1.9 %base.1.base_ref = f32[2048,256]{1,0:T(8,128)S(1)} custom-call(s32[1,2048]{1,0:T(1,128)S(1)} %get-tuple-element.45.order_ref, f32[1,256]{1,0:T(1,128)S(1)} %bitcast.2, f32[2048,256]{1,0:T(8,128)S(1)} %get-tuple-element.51.y_ref, f32[1,2048]{1,0:T(1,128)S(1)} %get-tuple-element.52.rest_0_.refs_8_, f32[1,2048]{1,0:T(1,128)S(1)} %collective-permute-done.4.rest_1_, ...), custom_call_target="tpu_custom_call" | custom-call | flops 1073741824 | bytes 4194304 | tf_op jit(solution)/shard_map/base/pallas_call | solution.py:383
  84.9 1.2 %collective-permute-done.34.rest_7_ = bf16[128,256]{1,0:T(8,128)(2,1)S(1)} collective-permute-done((bf16[128,256]{1,0:T(8,128)(2,1)S(1)}, bf16[128,256]{1,0:T(8,128)(2,1)S(1)}, u32[]{:S(2)}, u32[]{:S(2)}) %collective-permute-start.34) | collective-permute-done | bytes 65568 | tf_op jit(solution)/shard_map/ppermute | solution.py:443
  86.1 3.3 %mix.1 = bf16[2048,256]{1,0:T(8,128)(2,1)} custom-call(s32[1,2048]{1,0:T(1,128)S(1)} %get-tuple-element.45.order_ref, f32[2048,256]{1,0:T(8,128)S(1)} %base.1.base_ref, bf16[128,256]{1,0:T(8,128)(2,1)S(1)} %get-tuple-element.77.rest_0_, bf16[128,256]{1,0:T(8,128)(2,1)S(1)} %collective-permute-done.28.rest_1_, ...), custom_call_target="tpu_custom_call" | custom-call | flops 1073741824 | bytes 4194304 | tf_op jit(solution)/shard_map/mix/pallas_call | solution.py:413
  (67 shorter events, 8.9 us)
Async XLA Ops:
  14.4 6.6 %collective-permute-start.1 = (bf16[384,256]{1,0:T(8,128)(2,1)S(1)}, bf16[384,256]{1,0:T(8,128)(2,1)S(1)}, u32[]{:S(2)}, u32[]{:S(2)}) collective-permute-start(bf16[384,256]{1,0:T(8,128)(2,1)S(1)} %get-tuple-element.85), channel_id=1, source_target_pairs={{0,8},{4,20},{8,0},{12,28},{16,24},{20,4},{24,16},{28,12},{1,9},{5... | collective-permute-start | bytes 589832 | tf_op jit(solution)/shard_map/ppermute | solution.py:259
  17.3 9.3 %collective-permute-start.7 = (bf16[128,768]{1,0:T(8,128)(2,1)S(1)}, bf16[128,768]{1,0:T(8,128)(2,1)S(1)}, u32[]{:S(2)}, u32[]{:S(2)}) collective-permute-start(bf16[128,768]{1,0:T(8,128)(2,1)S(1)} %get-tuple-element.54), channel_id=1, source_target_pairs={{0,4},{4,0},{8,12},{12,8},{16,20},{20,16},{24,28},{28,24},{1,5},{5... | collective-permute-start | bytes 589832 | tf_op jit(solution)/shard_map/ppermute | solution.py:435
  17.3 9.4 %collective-permute-start.8 = (bf16[128,768]{1,0:T(8,128)(2,1)S(1)}, bf16[128,768]{1,0:T(8,128)(2,1)S(1)}, u32[]{:S(2)}, u32[]{:S(2)}) collective-permute-start(bf16[128,768]{1,0:T(8,128)(2,1)S(1)} %get-tuple-element.55), channel_id=1, source_target_pairs={{0,8},{4,20},{8,0},{12,28},{16,24},{20,4},{24,16},{28,12},{1,9},{5... | collective-permute-start | bytes 589832 | tf_op jit(solution)/shard_map/ppermute | solution.py:435
  18.7 9.8 %collective-permute-start.9 = (bf16[128,768]{1,0:T(8,128)(2,1)S(1)}, bf16[128,768]{1,0:T(8,128)(2,1)S(1)}, u32[]{:S(2)}, u32[]{:S(2)}) collective-permute-start(bf16[128,768]{1,0:T(8,128)(2,1)S(1)} %get-tuple-element.56), channel_id=1, source_target_pairs={{0,12},{4,16},{8,4},{12,24},{16,28},{20,0},{24,20},{28,8},{1,13},{... | collective-permute-start | bytes 589832 | tf_op jit(solution)/shard_map/ppermute | solution.py:435
  19.2 13.2 %collective-permute-start.10 = (bf16[128,768]{1,0:T(8,128)(2,1)S(1)}, bf16[128,768]{1,0:T(8,128)(2,1)S(1)}, u32[]{:S(2)}, u32[]{:S(2)}) collective-permute-start(bf16[128,768]{1,0:T(8,128)(2,1)S(1)} %get-tuple-element.57), channel_id=1, source_target_pairs={{0,16},{4,12},{8,24},{12,4},{16,0},{20,28},{24,8},{28,20},{1,17},{... | collective-permute-start | bytes 589832 | tf_op jit(solution)/shard_map/ppermute | solution.py:435
  21.0 11.4 %collective-permute-start.2 = (bf16[384,256]{1,0:T(8,128)(2,1)S(1)}, bf16[384,256]{1,0:T(8,128)(2,1)S(1)}, u32[]{:S(2)}, u32[]{:S(2)}) collective-permute-start(bf16[384,256]{1,0:T(8,128)(2,1)S(1)} %fusion), channel_id=1, source_target_pairs={{0,16},{4,12},{8,24},{12,4},{16,0},{20,28},{24,8},{28,20},{1,17},{... | collective-permute-start | bytes 589832 | tf_op jit(solution)/shard_map/ppermute | solution.py:259
  26.6 6.7 %collective-permute-start.11 = (bf16[128,768]{1,0:T(8,128)(2,1)S(1)}, bf16[128,768]{1,0:T(8,128)(2,1)S(1)}, u32[]{:S(2)}, u32[]{:S(2)}) collective-permute-start(bf16[128,768]{1,0:T(8,128)(2,1)S(1)} %get-tuple-element.58), channel_id=1, source_target_pairs={{0,20},{4,8},{8,28},{12,0},{16,4},{20,24},{24,12},{28,16},{1,21},{... | collective-permute-start | bytes 589832 | tf_op jit(solution)/shard_map/ppermute | solution.py:435
  26.8 8.7 %collective-permute-start.12 = (bf16[128,768]{1,0:T(8,128)(2,1)S(1)}, bf16[128,768]{1,0:T(8,128)(2,1)S(1)}, u32[]{:S(2)}, u32[]{:S(2)}) collective-permute-start(bf16[128,768]{1,0:T(8,128)(2,1)S(1)} %get-tuple-element.59), channel_id=1, source_target_pairs={{0,24},{4,28},{8,16},{12,20},{16,8},{20,12},{24,0},{28,4},{1,25},{... | collective-permute-start | bytes 589832 | tf_op jit(solution)/shard_map/ppermute | solution.py:435
  28.5 14.6 %collective-permute-start.13 = (bf16[128,768]{1,0:T(8,128)(2,1)S(1)}, bf16[128,768]{1,0:T(8,128)(2,1)S(1)}, u32[]{:S(2)}, u32[]{:S(2)}) collective-permute-start(bf16[128,768]{1,0:T(8,128)(2,1)S(1)} %get-tuple-element.60), channel_id=1, source_target_pairs={{0,28},{4,24},{8,20},{12,16},{16,12},{20,8},{24,4},{28,0},{1,29},{... | collective-permute-start | bytes 589832 | tf_op jit(solution)/shard_map/ppermute | solution.py:435
  32.5 10.7 %collective-permute-start.21 = (bf16[128,768]{1,0:T(8,128)(2,1)S(1)}, bf16[128,768]{1,0:T(8,128)(2,1)S(1)}, u32[]{:S(2)}, u32[]{:S(2)}) collective-permute-start(bf16[128,768]{1,0:T(8,128)(2,1)S(1)} %get-tuple-element.70), channel_id=1, source_target_pairs={{0,4},{4,0},{8,12},{12,8},{16,20},{20,16},{24,28},{28,24},{1,5},{5... | collective-permute-start | bytes 589832 | tf_op jit(solution)/shard_map/ppermute | solution.py:435
  32.5 10.7 %collective-permute-start.22 = (bf16[128,768]{1,0:T(8,128)(2,1)S(1)}, bf16[128,768]{1,0:T(8,128)(2,1)S(1)}, u32[]{:S(2)}, u32[]{:S(2)}) collective-permute-start(bf16[128,768]{1,0:T(8,128)(2,1)S(1)} %get-tuple-element.71), channel_id=1, source_target_pairs={{0,8},{4,20},{8,0},{12,28},{16,24},{20,4},{24,16},{28,12},{1,9},{5... | collective-permute-start | bytes 589832 | tf_op jit(solution)/shard_map/ppermute | solution.py:435
  33.3 27.2 %collective-permute-start.3 = (f32[384,256]{1,0:T(8,128)S(1)}, f32[384,256]{1,0:T(8,128)S(1)}, u32[]{:S(2)}, u32[]{:S(2)}) collective-permute-start(f32[384,256]{1,0:T(8,128)S(1)} %convert_add_fusion.rest_0_), channel_id=1, source_target_pairs={{0,4},{4,0},{8,12},{12,8},{16,20},{20,16},{24,28},{28,24},{1,5},{5... | collective-permute-start | bytes 1179656 | tf_op jit(solution)/shard_map/ppermute | solution.py:260
  35.5 10.3 %collective-permute-start.23 = (bf16[128,768]{1,0:T(8,128)(2,1)S(1)}, bf16[128,768]{1,0:T(8,128)(2,1)S(1)}, u32[]{:S(2)}, u32[]{:S(2)}) collective-permute-start(bf16[128,768]{1,0:T(8,128)(2,1)S(1)} %get-tuple-element.72), channel_id=1, source_target_pairs={{0,12},{4,16},{8,4},{12,24},{16,28},{20,0},{24,20},{28,8},{1,13},{... | collective-permute-start | bytes 589832 | tf_op jit(solution)/shard_map/ppermute | solution.py:435
  43.2 6.7 %collective-permute-start.24 = (bf16[128,768]{1,0:T(8,128)(2,1)S(1)}, bf16[128,768]{1,0:T(8,128)(2,1)S(1)}, u32[]{:S(2)}, u32[]{:S(2)}) collective-permute-start(bf16[128,768]{1,0:T(8,128)(2,1)S(1)} %get-tuple-element.73), channel_id=1, source_target_pairs={{0,16},{4,12},{8,24},{12,4},{16,0},{20,28},{24,8},{28,20},{1,17},{... | collective-permute-start | bytes 589832 | tf_op jit(solution)/shard_map/ppermute | solution.py:435
  43.2 13.7 %collective-permute-start.25 = (bf16[128,768]{1,0:T(8,128)(2,1)S(1)}, bf16[128,768]{1,0:T(8,128)(2,1)S(1)}, u32[]{:S(2)}, u32[]{:S(2)}) collective-permute-start(bf16[128,768]{1,0:T(8,128)(2,1)S(1)} %get-tuple-element.74), channel_id=1, source_target_pairs={{0,20},{4,8},{8,28},{12,0},{16,4},{20,24},{24,12},{28,16},{1,21},{... | collective-permute-start | bytes 589832 | tf_op jit(solution)/shard_map/ppermute | solution.py:435
  43.2 15.6 %collective-permute-start.26 = (bf16[128,768]{1,0:T(8,128)(2,1)S(1)}, bf16[128,768]{1,0:T(8,128)(2,1)S(1)}, u32[]{:S(2)}, u32[]{:S(2)}) collective-permute-start(bf16[128,768]{1,0:T(8,128)(2,1)S(1)} %get-tuple-element.75), channel_id=1, source_target_pairs={{0,24},{4,28},{8,16},{12,20},{16,8},{20,12},{24,0},{28,4},{1,25},{... | collective-permute-start | bytes 589832 | tf_op jit(solution)/shard_map/ppermute | solution.py:435
  45.8 17.7 %collective-permute-start.27 = (bf16[128,768]{1,0:T(8,128)(2,1)S(1)}, bf16[128,768]{1,0:T(8,128)(2,1)S(1)}, u32[]{:S(2)}, u32[]{:S(2)}) collective-permute-start(bf16[128,768]{1,0:T(8,128)(2,1)S(1)} %get-tuple-element.76), channel_id=1, source_target_pairs={{0,28},{4,24},{8,20},{12,16},{16,12},{20,8},{24,4},{28,0},{1,29},{... | collective-permute-start | bytes 589832 | tf_op jit(solution)/shard_map/ppermute | solution.py:435
  49.8 13.7 %collective-permute-start.14 = (bf16[128,256]{1,0:T(8,128)(2,1)S(1)}, bf16[128,256]{1,0:T(8,128)(2,1)S(1)}, u32[]{:S(2)}, u32[]{:S(2)}) collective-permute-start(bf16[128,256]{1,0:T(8,128)(2,1)S(1)} %get-tuple-element.62), channel_id=1, source_target_pairs={{4,0},{0,4},{12,8},{8,12},{20,16},{16,20},{28,24},{24,28},{5,1},{1... | collective-permute-start | bytes 196616 | tf_op jit(solution)/shard_map/ppermute | solution.py:443
  56.9 9.0 %collective-permute-start.15 = (bf16[128,256]{1,0:T(8,128)(2,1)S(1)}, bf16[128,256]{1,0:T(8,128)(2,1)S(1)}, u32[]{:S(2)}, u32[]{:S(2)}) collective-permute-start(bf16[128,256]{1,0:T(8,128)(2,1)S(1)} %get-tuple-element.63), channel_id=1, source_target_pairs={{8,0},{20,4},{0,8},{28,12},{24,16},{4,20},{16,24},{12,28},{9,1},{2... | collective-permute-start | bytes 196616 | tf_op jit(solution)/shard_map/ppermute | solution.py:443
  58.8 10.0 %collective-permute-start.16 = (bf16[128,256]{1,0:T(8,128)(2,1)S(1)}, bf16[128,256]{1,0:T(8,128)(2,1)S(1)}, u32[]{:S(2)}, u32[]{:S(2)}) collective-permute-start(bf16[128,256]{1,0:T(8,128)(2,1)S(1)} %get-tuple-element.64), channel_id=1, source_target_pairs={{12,0},{16,4},{4,8},{24,12},{28,16},{0,20},{20,24},{8,28},{13,1},{... | collective-permute-start | bytes 196616 | tf_op jit(solution)/shard_map/ppermute | solution.py:443
  60.5 8.3 %collective-permute-start.17 = (bf16[128,256]{1,0:T(8,128)(2,1)S(1)}, bf16[128,256]{1,0:T(8,128)(2,1)S(1)}, u32[]{:S(2)}, u32[]{:S(2)}) collective-permute-start(bf16[128,256]{1,0:T(8,128)(2,1)S(1)} %get-tuple-element.65), channel_id=1, source_target_pairs={{16,0},{12,4},{24,8},{4,12},{0,16},{28,20},{8,24},{20,28},{17,1},{... | collective-permute-start | bytes 196616 | tf_op jit(solution)/shard_map/ppermute | solution.py:443
  63.5 6.6 %collective-permute-start.18 = (bf16[128,256]{1,0:T(8,128)(2,1)S(1)}, bf16[128,256]{1,0:T(8,128)(2,1)S(1)}, u32[]{:S(2)}, u32[]{:S(2)}) collective-permute-start(bf16[128,256]{1,0:T(8,128)(2,1)S(1)} %get-tuple-element.66), channel_id=1, source_target_pairs={{20,0},{8,4},{28,8},{0,12},{4,16},{24,20},{12,24},{16,28},{21,1},{... | collective-permute-start | bytes 196616 | tf_op jit(solution)/shard_map/ppermute | solution.py:443
  63.6 10.1 %collective-permute-start.19 = (bf16[128,256]{1,0:T(8,128)(2,1)S(1)}, bf16[128,256]{1,0:T(8,128)(2,1)S(1)}, u32[]{:S(2)}, u32[]{:S(2)}) collective-permute-start(bf16[128,256]{1,0:T(8,128)(2,1)S(1)} %get-tuple-element.67), channel_id=1, source_target_pairs={{24,0},{28,4},{16,8},{20,12},{8,16},{12,20},{0,24},{4,28},{25,1},{... | collective-permute-start | bytes 196616 | tf_op jit(solution)/shard_map/ppermute | solution.py:443
  66.0 7.8 %collective-permute-start.20 = (bf16[128,256]{1,0:T(8,128)(2,1)S(1)}, bf16[128,256]{1,0:T(8,128)(2,1)S(1)}, u32[]{:S(2)}, u32[]{:S(2)}) collective-permute-start(bf16[128,256]{1,0:T(8,128)(2,1)S(1)} %get-tuple-element.68), channel_id=1, source_target_pairs={{28,0},{24,4},{20,8},{16,12},{12,16},{8,20},{4,24},{0,28},{29,1},{... | collective-permute-start | bytes 196616 | tf_op jit(solution)/shard_map/ppermute | solution.py:443
  68.8 10.4 %collective-permute-start.28 = (bf16[128,256]{1,0:T(8,128)(2,1)S(1)}, bf16[128,256]{1,0:T(8,128)(2,1)S(1)}, u32[]{:S(2)}, u32[]{:S(2)}) collective-permute-start(bf16[128,256]{1,0:T(8,128)(2,1)S(1)} %get-tuple-element.78), channel_id=1, source_target_pairs={{4,0},{0,4},{12,8},{8,12},{20,16},{16,20},{28,24},{24,28},{5,1},{1... | collective-permute-start | bytes 196616 | tf_op jit(solution)/shard_map/ppermute | solution.py:443
  68.9 11.8 %collective-permute-start.29 = (bf16[128,256]{1,0:T(8,128)(2,1)S(1)}, bf16[128,256]{1,0:T(8,128)(2,1)S(1)}, u32[]{:S(2)}, u32[]{:S(2)}) collective-permute-start(bf16[128,256]{1,0:T(8,128)(2,1)S(1)} %get-tuple-element.79), channel_id=1, source_target_pairs={{8,0},{20,4},{0,8},{28,12},{24,16},{4,20},{16,24},{12,28},{9,1},{2... | collective-permute-start | bytes 196616 | tf_op jit(solution)/shard_map/ppermute | solution.py:443
  73.7 5.5 %collective-permute-start.4 = (f32[1,2048]{1,0:T(1,128)S(1)}, f32[1,2048]{1,0:T(1,128)S(1)}, u32[]{:S(2)}, u32[]{:S(2)}) collective-permute-start(f32[1,2048]{1,0:T(1,128)S(1)} %get-tuple-element.52.rest_0_.refs_8_), channel_id=1, source_target_pairs={{0,1},{1,2},{2,3},{3,0},{4,5},{5,6},{6,7},{7,4},{8,9},{9,10},{10,1... | collective-permute-start | bytes 24584 | tf_op jit(solution)/shard_map/ppermute | solution.py:467
  75.1 9.5 %collective-permute-start.30 = (bf16[128,256]{1,0:T(8,128)(2,1)S(1)}, bf16[128,256]{1,0:T(8,128)(2,1)S(1)}, u32[]{:S(2)}, u32[]{:S(2)}) collective-permute-start(bf16[128,256]{1,0:T(8,128)(2,1)S(1)} %get-tuple-element.80), channel_id=1, source_target_pairs={{12,0},{16,4},{4,8},{24,12},{28,16},{0,20},{20,24},{8,28},{13,1},{... | collective-permute-start | bytes 196616 | tf_op jit(solution)/shard_map/ppermute | solution.py:443
  78.3 6.4 %collective-permute-start.31 = (bf16[128,256]{1,0:T(8,128)(2,1)S(1)}, bf16[128,256]{1,0:T(8,128)(2,1)S(1)}, u32[]{:S(2)}, u32[]{:S(2)}) collective-permute-start(bf16[128,256]{1,0:T(8,128)(2,1)S(1)} %get-tuple-element.81), channel_id=1, source_target_pairs={{16,0},{12,4},{24,8},{4,12},{0,16},{28,20},{8,24},{20,28},{17,1},{... | collective-permute-start | bytes 196616 | tf_op jit(solution)/shard_map/ppermute | solution.py:443
  79.2 5.4 %collective-permute-start.32 = (bf16[128,256]{1,0:T(8,128)(2,1)S(1)}, bf16[128,256]{1,0:T(8,128)(2,1)S(1)}, u32[]{:S(2)}, u32[]{:S(2)}) collective-permute-start(bf16[128,256]{1,0:T(8,128)(2,1)S(1)} %get-tuple-element.82), channel_id=1, source_target_pairs={{20,0},{8,4},{28,8},{0,12},{4,16},{24,20},{12,24},{16,28},{21,1},{... | collective-permute-start | bytes 196616 | tf_op jit(solution)/shard_map/ppermute | solution.py:443
  79.2 5.7 %collective-permute-start.33 = (bf16[128,256]{1,0:T(8,128)(2,1)S(1)}, bf16[128,256]{1,0:T(8,128)(2,1)S(1)}, u32[]{:S(2)}, u32[]{:S(2)}) collective-permute-start(bf16[128,256]{1,0:T(8,128)(2,1)S(1)} %get-tuple-element.83), channel_id=1, source_target_pairs={{24,0},{28,4},{16,8},{20,12},{8,16},{12,20},{0,24},{4,28},{25,1},{... | collective-permute-start | bytes 196616 | tf_op jit(solution)/shard_map/ppermute | solution.py:443
  80.7 5.4 %collective-permute-start.34 = (bf16[128,256]{1,0:T(8,128)(2,1)S(1)}, bf16[128,256]{1,0:T(8,128)(2,1)S(1)}, u32[]{:S(2)}, u32[]{:S(2)}) collective-permute-start(bf16[128,256]{1,0:T(8,128)(2,1)S(1)} %get-tuple-element.84), channel_id=1, source_target_pairs={{28,0},{24,4},{20,8},{16,12},{12,16},{8,20},{4,24},{0,28},{29,1},{... | collective-permute-start | bytes 196616 | tf_op jit(solution)/shard_map/ppermute | solution.py:443
  (12 other events, 58.6 us)

commit v3 on v2

--- a/solution.py
+++ b/solution.py
@@ -10,11 +10,14 @@
 PATCHES = 32
 EPSILON = 1e-06
 LANES = 128
-CHUNKS = 2
 TILE = 512
+LIMIT = 24
+FIRST_LIMIT = 54
+COST = 8
 MIB = 1024 * 1024
 F32 = jnp.float32
 BF16 = jnp.bfloat16
+TOKEN = jax.ShapeDtypeStruct((8, LANES), F32)
 
 
 def dot(a, b):
@@ -29,8 +32,8 @@
     return lax.dot_general(a, b, (((0,), (0,)), ((), ())), preferred_element_type=F32)
 
 
-def params():
-    return pltpu.CompilerParams(vmem_limit_bytes=40 * MIB)
+def params(limit=LIMIT):
+    return pltpu.CompilerParams(vmem_limit_bytes=limit * MIB)
 
 
 def full(count):
@@ -38,7 +41,11 @@
 
 
 def cost(flops, moved, exps=0):
-    return pl.CostEstimate(flops=int(flops), bytes_accessed=int(moved), transcendentals=int(exps))
+    return pl.CostEstimate(
+        flops=int(flops) // COST,
+        bytes_accessed=int(moved) // COST,
+        transcendentals=int(exps) // COST,
+    )
 
 
 def power_of_two(n):
@@ -68,13 +75,26 @@
     return jnp.broadcast_to(row, (LANES, LANES)).T
 
 
-def sort_into(n, start, rows, owned_rows, order, sources, outs, onehot):
+def far_first(n):
+    return sorted(range(n), key=lambda step: (-(step >> 1).bit_count(), -step))
+
+
+def fetch(pairs, sems):
+    copies = []
+    for at, (source, target) in enumerate(pairs):
+        copies.append(pltpu.make_async_copy(source, target, sems.at[at]))
+        copies[-1].start()
+    return copies
+
+
+def sort_into(n, steps, order, sources, outs, onehot):
     me = lax.axis_index("cam")
+    count = onehot.shape[1]
+    rows = count // n
     group = onehot.shape[0] // rows
-    count = onehot.shape[1]
-    for first in range(0, n, group):
+    for first in range(0, len(steps), group):
         for at in range(group):
-            base = peer(me, first + at, n) * owned_rows + start
+            base = peer(me, steps[first + at], n) * rows
             slot = lax.broadcasted_iota(jnp.int32, (rows, count), 0) + base
             onehot[at * rows : (at + 1) * rows, :] = (slot == order).astype(F32).astype(BF16)
         for which, source in sources:
@@ -87,16 +107,13 @@
                 ]
 
 
-def first_sort_kernel(n, start, rows, owned_rows, order_in, q_in, k_in, v_in, *rest):
-    outs, (order_ref, q_ref, k_ref, v_ref, onehot, sems) = rest[:n], rest[n:]
-    copies = [
-        pltpu.make_async_copy(source, target, sems.at[at])
-        for at, (source, target) in enumerate(
-            ((order_in, order_ref), (k_in, k_ref), (v_in, v_ref), (q_in, q_ref))
-        )
-    ]
-    for copy in copies:
-        copy.start()
+def first_sort_kernel(n, steps, order_in, q_in, k_in, v_in, *rest):
+    outs, rest = rest[: len(steps)], rest[len(steps) :]
+    token, onehot, order_ref, k_ref, v_ref, q_ref, sems = rest
+    token[...] = jnp.zeros_like(token)
+    copies = fetch(
+        ((order_in, order_ref), (k_in, k_ref), (v_in, v_ref), (q_in, q_ref)), sems
+    )
     copies[0].wait()
 
     def arrives(ref, copy):
@@ -112,37 +129,36 @@
         (2, arrives(v_ref, copies[2])),
         (0, arrives(q_ref, copies[3])),
     )
-    sort_into(n, start, rows, owned_rows, order_ref[...], sources, outs, onehot)
-
-
-def sort_kernel(n, start, rows, owned_rows, order_ref, q_ref, k_ref, v_ref, *rest):
-    outs, onehot = rest[:n], rest[n]
+    sort_into(n, steps, order_ref[...], sources, outs, onehot)
+
+
+def sort_kernel(n, steps, order_ref, q_ref, k_ref, v_ref, *rest):
+    outs, (token, onehot) = rest[: len(steps)], rest[len(steps) :]
+    token[...] = jnp.zeros_like(token)
     sources = ((0, lambda _: q_ref), (1, lambda _: k_ref), (2, lambda _: v_ref))
-    sort_into(n, start, rows, owned_rows, order_ref[...], sources, outs, onehot)
-
-
-def sort_tokens(order, q, k, v, n, start, rows, owned_rows, first):
+    sort_into(n, steps, order_ref[...], sources, outs, onehot)
+
+
+def sort_tokens(order, q, k, v, n, steps, first):
     count, width = q.shape
-    group = max(1, min(n, 512 // rows))
-    while n % group:
+    rows = count // n
+    size = len(steps)
+    group = max(1, min(size, TILE // rows))
+    while size % group:
         group -= 1
-    shapes = [jax.ShapeDtypeStruct((rows, 3 * width), BF16)] * n
+    shapes = [jax.ShapeDtypeStruct((rows, 3 * width), BF16)] * size + [TOKEN]
     scratch = [pltpu.VMEM((group * rows, count), BF16)]
     if first:
-        shapes = shapes + [
-            jax.ShapeDtypeStruct(array.shape, array.dtype) for array in (order, q, k, v)
-        ]
+        scratch = scratch + [pltpu.VMEM(array.shape, array.dtype) for array in (order, k, v, q)]
         scratch = scratch + [pltpu.SemaphoreType.DMA((4,))]
     return pl.pallas_call(
-        functools.partial(
-            first_sort_kernel if first else sort_kernel, n, start, rows, owned_rows
-        ),
+        functools.partial(first_sort_kernel if first else sort_kernel, n, tuple(steps)),
         out_shape=shapes,
         in_specs=[pl.BlockSpec(memory_space=pltpu.HBM)] * 4 if first else full(4),
         out_specs=full(len(shapes)),
         scratch_shapes=scratch,
-        compiler_params=params(),
-        cost_estimate=cost(6 * n * rows * count * width, 6 * count * width),
+        compiler_params=params(FIRST_LIMIT if first else LIMIT),
+        cost_estimate=cost(6 * size * rows * count * width, 6 * count * width),
         name="sort_tokens",
     )(order, q, k, v)
 
@@ -189,13 +205,25 @@
     )(*blocks, *after)
 
 
-def grads_kernel(n, split, k_ref, v_ref, rate_ref, one_ref, three_ref, two_ref, *rest):
-    outs, total = rest[:-1], rest[-1]
+def grads_kernel(n, split, parts, k_in, v_in, rate_in, one_in, three_in, two_in, *rest):
+    outs, rest = rest[:parts], rest[parts:]
+    total, one_ref, three_ref, two_ref, rate_ref, k_ref, v_ref, sems = rest
     count, width = k_ref.shape
     hid = one_ref.shape[1]
+    tile = min(count, TILE)
+    tiles = [slice(start, start + tile) for start in range(0, count, tile)]
+    pairs = [(one_in, one_ref), (three_in, three_ref), (k_in.at[tiles[0]], k_ref.at[tiles[0]])]
+    pairs += [(rate_in, rate_ref), (v_in.at[tiles[0]], v_ref.at[tiles[0]]), (two_in, two_ref)]
+    for here in tiles[1:]:
+        pairs += [(k_in.at[here], k_ref.at[here]), (v_in.at[here], v_ref.at[here])]
+    copies = fetch(pairs, sems)
+    for copy in copies[:6]:
+        copy.wait()
     one, three, two = one_ref[0], three_ref[0], two_ref[0]
-    tile = min(count, TILE)
     for start in range(0, count, tile):
+        if start:
+            copies[4 + 2 * (start // tile)].wait()
+            copies[5 + 2 * (start // tile)].wait()
         k = k_ref[start : start + tile, :]
         h_one = dot_bt(k, one)
         h_three = dot_bt(k, three)
@@ -231,32 +259,56 @@
     assert hid == width
     rows = 3 * hid
     parts = 2 if split else 1
-    return pl.pallas_call(
-        functools.partial(grads_kernel, n, split),
+    tiles = count // min(count, TILE)
+    held = (one, three, two, rate, k, v)
+    return pl.pallas_call(
+        functools.partial(grads_kernel, n, split, parts),
         out_shape=[jax.ShapeDtypeStruct((rows // parts, width), F32)] * parts,
-        in_specs=full(6),
+        in_specs=[pl.BlockSpec(memory_space=pltpu.HBM)] * 6,
         out_specs=full(parts),
-        scratch_shapes=[pltpu.VMEM((rows, width), F32)],
-        compiler_params=params(),
+        scratch_shapes=[pltpu.VMEM((rows, width), F32)]
+        + [pltpu.VMEM(array.shape, array.dtype) for array in held]
+        + [pltpu.SemaphoreType.DMA((4 + 2 * tiles,))],
+        compiler_params=params(58),
         cost_estimate=cost(12 * count * width * hid, 8 * count * width, count * hid),
         name="gradients",
     )(k, v, rate, one, three, two)
 
 
-def sum_over_cams(parts, n):
+def merge_kernel(keep_ref, got_ref, *rest):
+    rest[-1][...] = keep_ref[...] + got_ref[...].astype(F32)
+
+
+def merge(keep, got, after):
+    return pl.pallas_call(
+        merge_kernel,
+        out_shape=jax.ShapeDtypeStruct(keep.shape, F32),
+        in_specs=full(2) + [pl.BlockSpec(memory_space=pl.ANY)] * len(after),
+        out_specs=pl.BlockSpec(memory_space=pltpu.VMEM),
+        compiler_params=params(),
+        cost_estimate=cost(keep.size, 12 * keep.size),
+        name="merge",
+    )(keep, got, *after)
+
+
+def sum_over_cams(parts, after, n):
     if len(parts) == 1:
         return [lax.psum(parts[0], "cam")]
     keep, send = parts
     bits = n.bit_length() - 1
     pair = [(at, at ^ 1) for at in range(n)]
-    mine = keep + lax.ppermute(send, "cam", pair)
+    mine = merge(keep, lax.ppermute(send, "cam", pair), after[0])
     span = bits - 1
     for step in range(span):
         pairs = []
         for at in range(n):
             bit = 1 + (step + (at & 1)) % span
             pairs.append((at, at ^ (1 << bit)))
-        mine = mine + lax.ppermute(mine.astype(BF16), "cam", pairs).astype(F32)
+        got = lax.ppermute(mine.astype(BF16), "cam", pairs)
+        if step + 1 < len(after):
+            mine = merge(mine, got, after[step + 1])
+        else:
+            mine = mine + got.astype(F32)
     return [mine, lax.ppermute(mine, "cam", pair)]
 
 
@@ -319,161 +371,155 @@
     )(q, one, three, two, *grads)
 
 
-def slot_row(n, start, rows, owned_rows):
+def place_kernel(n, steps, order_ref, *outs):
     me = lax.axis_index("cam")
-    at = lax.broadcasted_iota(jnp.int32, (8, n * rows), 1)
-    step = jnp.zeros_like(at)
-    for cut in range(1, n):
-        step = step + (at >= cut * rows).astype(jnp.int32)
-    return peer(me, step, n) * owned_rows + start + at - step * rows
-
-
-def placed(order_ref, low, slots, onehot, joined):
-    tile = onehot.shape[0]
-    for at in range(0, tile, LANES):
-        wanted = column(order_ref[:, low + at : low + at + LANES].astype(F32))
-        for lane in range(0, onehot.shape[1], LANES):
+    count = order_ref.shape[1]
+    rows = count // n
+    size = len(steps) * rows
+    at = lax.broadcasted_iota(jnp.int32, (8, size), 1)
+    slots = at * 0
+    for which, step in enumerate(steps):
+        inside = jnp.logical_and(at >= which * rows, at < (which + 1) * rows)
+        slots = jnp.where(inside, peer(me, step, n) * rows + at - which * rows, slots)
+    slots = slots[0:1, :].astype(F32)
+    each = outs[0].shape[1]
+    for low in range(0, count, LANES):
+        wanted = column(order_ref[:, low : low + LANES].astype(F32))
+        for lane in range(0, size, LANES):
             hit = wanted == slots[:, lane : lane + LANES]
-            onehot[at : at + LANES, lane : lane + LANES] = hit.astype(F32).astype(BF16)
-    return dot(onehot[...], joined[...])
-
-
-def base_kernel(heads, shapes, order_ref, gain_ref, y_ref, *rest):
-    squares, rest = rest[:heads], rest[heads:]
+            out = outs[lane // each]
+            start = lane % each
+            out[low : low + LANES, start : start + LANES] = hit.astype(F32).astype(BF16)
+
+
+def place(order, n, steps):
+    count = order.shape[1]
+    shape = jax.ShapeDtypeStruct((count, count // 2), BF16)
+    return pl.pallas_call(
+        functools.partial(place_kernel, n, tuple(steps)),
+        out_shape=[shape, shape],
+        in_specs=full(1),
+        out_specs=full(2),
+        compiler_params=params(),
+        cost_estimate=cost(count * count, 2 * count * count),
+        name="place",
+    )(order)
+
+
+def gathered(onehot, here, blocks):
+    rows = blocks[0].shape[0]
+    total = None
+    for at, block in enumerate(blocks):
+        part = dot(onehot[here, at * rows : (at + 1) * rows], block[...])
+        total = part if total is None else total + part
+    return total
+
+
+def base_kernel(heads, gain_ref, y_ref, onehot, *rest):
+    squares, blocks, out_ref = rest[:heads], rest[heads:-1], rest[-1]
     count, width = y_ref.shape
-    n, given = shapes
-    groups = [rest[at * n : (at + 1) * n] for at in range(len(given))]
-    out_ref = rest[len(given) * n]
-    scratch = rest[len(given) * n + 1 :]
     total = squares[0][...]
     for ref in squares[1:]:
         total = total + ref[...]
     inverse = 1.0 / jnp.sqrt(total / (width * heads) + EPSILON)
     gain = gain_ref[...]
-    owned_rows = count // n
     tile = min(count, TILE)
-    laid = []
-    for at, (start, rows) in enumerate(given):
-        onehot, joined = scratch[2 * at : 2 * at + 2]
-        for cam in range(n):
-            joined[cam * rows : (cam + 1) * rows, :] = groups[at][cam][...]
-        laid.append((slot_row(n, start, rows, owned_rows)[0:1, :].astype(F32), onehot, joined))
     for low in range(0, count, tile):
-        parts = [placed(order_ref, low, *entry) for entry in laid]
+        part = gathered(onehot, slice(low, low + tile), blocks)
         for at in range(0, tile, LANES):
             here = slice(low + at, low + at + LANES)
             norm = column(inverse[:, here])
             norm = jnp.concatenate([norm] * (width // LANES), axis=1)
-            value = y_ref[here, :] * norm * gain
-            for part in parts:
-                value = value + part[at : at + LANES]
-            out_ref[here, :] = value
-
-
-def base(order, gain, y, squares, groups, starts, n):
+            out_ref[here, :] = y_ref[here, :] * norm * gain + part[at : at + LANES]
+
+
+def base(gain, y, onehot, squares, blocks):
     count, width = y.shape
     heads = len(squares)
-    tile = min(count, TILE)
-    scratch = []
-    for _, rows in starts:
-        scratch.append(pltpu.VMEM((tile, n * rows), BF16))
-        scratch.append(pltpu.VMEM((n * rows, width), BF16))
-    blocks = [block for group in groups for block in group]
-    moved = sum(n * rows for _, rows in starts)
-    return pl.pallas_call(
-        functools.partial(base_kernel, heads, (n, tuple(starts))),
+    moved = len(blocks) * blocks[0].shape[0]
+    return pl.pallas_call(
+        functools.partial(base_kernel, heads),
         out_shape=jax.ShapeDtypeStruct((count, width), F32),
         in_specs=full(3 + heads + len(blocks)),
         out_specs=pl.BlockSpec(memory_space=pltpu.VMEM),
-        scratch_shapes=scratch,
         compiler_params=params(),
         cost_estimate=cost(2 * count * moved * width, 8 * count * width),
         name="base",
-    )(order, gain, y, *squares, *blocks)
-
-
-def mix_kernel(n, start, rows, owned_rows, order_ref, base_ref, *rest):
-    blocks, (out_ref, onehot, joined) = rest[:n], rest[n:]
-    step = pl.program_id(0)
-
-    @pl.when(step == 0)
-    def _():
-        for at in range(n):
-            joined[at * rows : (at + 1) * rows, :] = blocks[at][...]
-
-    slots = slot_row(n, start, rows, owned_rows)[0:1, :].astype(F32)
-    part = placed(order_ref, 0, slots, onehot, joined)
-    out_ref[...] = (base_ref[...] + part).astype(BF16)
-
-
-def mix(order, given, blocks, n, start, owned_rows):
+    )(gain, y, onehot, *squares, *blocks)
+
+
+def mix_kernel(base_ref, onehot, *rest):
+    blocks, (out_ref, held, sems) = rest[:-3], rest[-3:]
+    count = base_ref.shape[0]
+    tile = min(count, TILE)
+    copies = []
+    for at in range(count // tile):
+        here = slice(at * tile, (at + 1) * tile)
+        held[here, :] = (base_ref[here, :] + gathered(onehot, here, blocks)).astype(BF16)
+        copies += fetch([(held.at[here], out_ref.at[here])], sems.at[at : at + 1])
+    for copy in copies:
+        copy.wait()
+
+
+def mix(given, onehot, blocks):
     count, width = given.shape
-    rows = blocks[0].shape[0]
+    moved = len(blocks) * blocks[0].shape[0]
     tile = min(count, TILE)
     return pl.pallas_call(
-        functools.partial(mix_kernel, n, start, rows, owned_rows),
-        grid=(count // tile,),
+        mix_kernel,
         out_shape=jax.ShapeDtypeStruct((count, width), BF16),
-        in_specs=[
-            pl.BlockSpec((1, tile), lambda i: (0, i)),
-            pl.BlockSpec((tile, width), lambda i: (i, 0)),
-        ]
-        + full(n),
-        out_specs=pl.BlockSpec((tile, width), lambda i: (i, 0)),
+        in_specs=full(2 + len(blocks)),
+        out_specs=pl.BlockSpec(memory_space=pltpu.HBM),
         scratch_shapes=[
-            pltpu.VMEM((tile, n * rows), BF16),
-            pltpu.VMEM((n * rows, width), BF16),
+            pltpu.VMEM((count, width), BF16),
+            pltpu.SemaphoreType.DMA((count // tile,)),
         ],
         compiler_params=params(),
-        cost_estimate=cost(2 * count * n * rows * width, 8 * count * width),
+        cost_estimate=cost(2 * count * moved * width, 8 * count * width),
         name="mix",
-    )(order, given, *blocks)
-
-
-def exchange(blocks, n):
-    return [blocks[0]] + [
-        lax.ppermute(blocks[step], "cam", routes(step, n)) for step in range(1, n)
-    ]
-
-
-def give_back(blocks, n):
-    moved = [blocks[0]]
-    for step in range(1, n):
-        pairs = [(target, at) for at, target in routes(step, n)]
-        moved.append(lax.ppermute(blocks[step], "cam", pairs))
-    return moved
+    )(given, onehot, *blocks)
+
+
+def exchange(block, step, n):
+    return lax.ppermute(block, "cam", routes(step, n)) if step else block
+
+
+def give_back(block, step, n):
+    pairs = [(target, at) for at, target in routes(step, n)]
+    return lax.ppermute(block, "cam", pairs) if step else block
 
 
 def per_device(queries, keys, values, rates, w_one, w_three, w_two, gain, order):
     count, width = queries.shape
     n = lax.axis_size("cam")
     heads = lax.axis_size("head")
-    owned_rows = count // n
-    chunks = CHUNKS if (owned_rows // PATCHES) % CHUNKS == 0 else 1
-    rows = owned_rows // chunks
-    arrived = []
-    for at in range(chunks):
-        blocks = sort_tokens(
-            order, queries, keys, values, n, at * rows, rows, owned_rows, at == 0
-        )
-        if at == 0:
-            order, queries, keys, values = blocks[n:]
-            blocks = blocks[:n]
-        arrived.append(exchange(blocks, n))
+    steps = far_first(n)
+    few = max(1, n // 4)
     parts = gradients(keys, values, rates.reshape(1, count), w_one, w_three, w_two, n)
-    summed = sum_over_cams(parts, n)
+    arrived = {}
+    after = []
+    for at, group in enumerate((steps[:few], steps[few:])):
+        blocks = sort_tokens(order, queries, keys, values, n, group, True)
+        after.append(blocks[-1])
+        for step, block in zip(group, blocks):
+            arrived[step] = exchange(block, step, n)
+    summed = sum_over_cams(parts, [after[:1], after[1:], [arrived[step] for step in steps[: 2 * few]]], n)
     y, square = read_out(queries, w_one, w_three, w_two, summed)
     squares = [square] + [
         lax.ppermute(square, "head", [(at, (at + step) % heads) for at in range(heads)])
         for step in range(1, heads)
     ]
-    returned = []
-    for at in range(chunks):
-        after = [square] if at == chunks - 1 else []
-        returned.append(give_back(attend(arrived[at], after, n, width), n))
-    starts = [(at * rows, rows) for at in range(chunks)]
-    given = base(order, gain.reshape(1, width), y, squares, returned[:-1], starts[:-1], n)
-    return mix(order, given, returned[-1], n, starts[-1][0], owned_rows)
+    early = steps[:few] + steps[n - few :]
+    late = steps[few : n - few]
+    early_places, late_places = place(order, n, early + late)
+    attended = attend(
+        [arrived[step] for step in range(n)], squares + [late_places], n, width
+    )
+    returned = {step: give_back(attended[step], step, n) for step in early + late}
+    given = base(
+        gain.reshape(1, width), y, early_places, squares, [returned[step] for step in early]
+    )
+    return mix(given, late_places, [returned[step] for step in late])
 
 
 def solution(mesh):

time: 89.6 us -> 78.1 us (0.87)
  starting transfers between devices: 41.8 us -> 23.1 us
  Pallas kernels: 21.6 us -> 28.9 us
  waiting for transfers between devices: 21.1 us -> 24.1 us
  local copies, waits for them, and re-layouts: 4.39 us -> 1.45 us
    ppermute x31 -> x17, starting transfers between devices: 37.2 us -> 17.4 us  [the longest x7 8.16 us: exchange(): return lax.ppermute(block, 'cam', routes(step, n)) if step else block]
    ppermute x31 -> x17, waiting for transfers between devices: 17.4 us -> 23.5 us  [the longest x2 12.4 us: sum_over_cams(): got = lax.ppermute(mine.astype(BF16), 'cam', pairs)]
    pallas_call x2, Pallas kernels: 8.59 us -> 13.9 us  [sort_tokens(): pl.pallas_call(functools.partial(first_sort_kernel if first else sort_ker...]
    ppermute x3, waiting for transfers between devices: 3.68 us -> 0.57 us  [per_device(): lax.ppermute(square, 'head', [(at, (at + step) % heads) for at in range(h...]
    unnamed x18 -> x26, local copies, waits for them, and re-layouts: 4.39 us -> 1.45 us
    pallas_call x3 -> x7, Pallas kernels: 8.15 us -> 10.8 us  [the longest x1 5.61 us: gradients(): pl.pallas_call(functools.partial(grads_kernel, n, split, parts), out_shap...]
    ppermute x3, starting transfers between devices: 4.61 us -> 5.55 us  [per_device(): lax.ppermute(square, 'head', [(at, (at + step) % heads) for at in range(h...]
    pallas_call x2 -> x1, Pallas kernels: 2.22 us -> 1.52 us  [attend(): pl.pallas_call(functools.partial(attend_kernel, n, width ** (-0.5)), out_...]
  transfers between devices with their start and end apart: 35 -> 21, of which waited for: 12 -> 11; matrix products, arithmetic and copies ran while one was open for 0% -> 0% of each run, Pallas kernels for 12% -> 25%
where the time goes in v3:
time: 78.1 us; the launch traced here: 77.9 us
  Pallas kernels  28.9 us (37%)
  waiting for transfers between devices  24.1 us (31%)
  starting transfers between devices  23.1 us (30%)
  local copies, waits for them, and re-layouts  1.45 us (2%)
    pallas_call x2, Pallas kernels, sort_tokens(): pl.pallas_call(functools.partial(first_sort_kernel if first else sort_ker...  13.9 us
    ppermute x2, waiting for transfers between devices, sum_over_cams(): got = lax.ppermute(mine.astype(BF16), 'cam', pairs)  12.4 us
    ppermute x7, starting transfers between devices, exchange(): return lax.ppermute(block, 'cam', routes(step, n)) if step else block  8.16 us
    ppermute x7, starting transfers between devices, give_back(): return lax.ppermute(block, 'cam', pairs) if step else block  6.65 us
    ppermute x7, waiting for transfers between devices, give_back(): return lax.ppermute(block, 'cam', pairs) if step else block  6.43 us
    pallas_call x1, Pallas kernels, gradients(): pl.pallas_call(functools.partial(grads_kernel, n, split, parts), out_shap...  5.61 us
    ppermute x3, starting transfers between devices, per_device(): lax.ppermute(square, 'head', [(at, (at + step) % heads) for at in range(h...  5.55 us
    ppermute x7, waiting for transfers between devices, exchange(): return lax.ppermute(block, 'cam', routes(step, n)) if step else block  4.68 us
  transfers between devices with their start and end apart: 21, of which 11 were waited for; matrix products, arithmetic and copies ran while one was open for 0% of the time, Pallas kernels for 25%

profile of v3, /device:TPU:0, one launch (start us, length us, event | category | flops | bytes accessed | tf_op | source)
XLA Modules:
  0.0 77.9 jit_solution(13445546432789708980)
XLA Ops:
  0.0 5.6 %gradients.1 = (f32[384,256]{1,0:T(8,128)}, f32[384,256]{1,0:T(8,128)}) custom-call(bf16[2048,256]{1,0:T(8,128)(2,1)} %k_in.5, bf16[2048,256]{1,0:T(8,128)(2,1)} %v_in.5, f32[1,2048]{1,0:T(1,128)} %bitcast.3, bf16[1,256,256]{2,1,0:T(8,128)(2,1)} %one_ref.1, bf16[1,256,256]{2,1,0:T(8,128)(2,1)} %three_ref.1, bf16[1,256,256]{2,1,0:T(8,128)(2,1)} %two_ref.1), custom_call_target="tpu_custom_call" | custom-call | flops 201326592 | bytes 524288 | tf_op jit(solution)/shard_map/gradients/pallas_call | solution.py:264
  6.2 5.3 %sort_tokens.2 = (bf16[256,768]{1,0:T(8,128)(2,1)}, bf16[256,768]{1,0:T(8,128)(2,1)}, f32[8,128]{1,0:T(8,128)}) custom-call(s32[1,2048]{1,0:T(1,128)} %order_ref.1, bf16[2048,256]{1,0:T(8,128)(2,1)} %q_ref.1, bf16[2048,256]{1,0:T(8,128)(2,1)} %k_in.5, bf16[2048,256]{1,0:T(8,128)(2,1)} %v_in.5), custom_call_target="tpu_custom_call" | custom-call | flops 201326592 | bytes 393216 | tf_op jit(solution)/shard_map/sort_tokens/pallas_call | solution.py:154
  11.4 3.6 %collective-permute-start.3 = (bf16[256,768]{1,0:T(8,128)(2,1)}, bf16[256,768]{1,0:T(8,128)(2,1)S(1)}, u32[]{:S(2)}, u32[]{:S(2)}) collective-permute-start(bf16[256,768]{1,0:T(8,128)(2,1)} %get-tuple-element.33), channel_id=1, source_target_pairs={{0,28},{4,24},{8,20},{12,16},{16,12},{20,8},{24,4},{28,0},{1,29},{... | collective-permute-start | bytes 1179656 | tf_op jit(solution)/shard_map/ppermute | solution.py:484
  15.1 8.6 %sort_tokens.3 = (bf16[256,768]{1,0:T(8,128)(2,1)}, bf16[256,768]{1,0:T(8,128)(2,1)}, bf16[256,768]{1,0:T(8,128)(2,1)}, bf16[256,768]{1,0:T(8,128)(2,1)}, bf16[2...) custom-call(s32[1,2048]{1,0:T(1,128)} %order_ref.1, bf16[2048,256]{1,0:T(8,128)(2,1)} %q_ref.1, ...), custom_call_target="tpu_custom_call" | custom-call | flops 603979776 | bytes 393216 | tf_op jit(solution)/shard_map/sort_tokens/pallas_call | solution.py:154
  23.8 0.7 copy-done.8
  24.6 1.9 %collective-permute-start.1 = (bf16[384,256]{1,0:T(8,128)(2,1)S(1)}, bf16[384,256]{1,0:T(8,128)(2,1)S(1)}, u32[]{:S(2)}, u32[]{:S(2)}) collective-permute-start(bf16[384,256]{1,0:T(8,128)(2,1)S(1)} %convert_element_type.6), channel_id=1, source_target_pairs={{0,8},{4,20},{8,0},{12,28},{16,24},{20,4},{24,16},{28,12},{1,9},{5... | collective-permute-start | bytes 589832 | tf_op jit(solution)/shard_map/ppermute | solution.py:307
  26.6 1.5 %collective-permute-start.6 = (bf16[256,768]{1,0:T(8,128)(2,1)}, bf16[256,768]{1,0:T(8,128)(2,1)S(1)}, u32[]{:S(2)}, u32[]{:S(2)}) collective-permute-start(bf16[256,768]{1,0:T(8,128)(2,1)} %get-tuple-element.36), channel_id=1, source_target_pairs={{0,16},{4,12},{8,24},{12,4},{16,0},{20,28},{24,8},{28,20},{1,17},{... | collective-permute-start | bytes 1179656 | tf_op jit(solution)/shard_map/ppermute | solution.py:484
  28.1 10.3 %collective-permute-done.1.got_ref = bf16[384,256]{1,0:T(8,128)(2,1)S(1)} collective-permute-done((bf16[384,256]{1,0:T(8,128)(2,1)S(1)}, bf16[384,256]{1,0:T(8,128)(2,1)S(1)}, u32[]{:S(2)}, u32[]{:S(2)}) %collective-permute-start.1) | collective-permute-done | bytes 196640 | tf_op jit(solution)/shard_map/ppermute | solution.py:307
  38.4 0.7 copy-done.7
  39.2 0.7 collective-permute-done.5.rest_2_.refs_5_
  39.9 4.0 %collective-permute-done.6.rest_3_.refs_4_ = bf16[256,768]{1,0:T(8,128)(2,1)S(1)} collective-permute-done((bf16[256,768]{1,0:T(8,128)(2,1)}, bf16[256,768]{1,0:T(8,128)(2,1)S(1)}, u32[]{:S(2)}, u32[]{:S(2)}) %collective-permute-start.6) | collective-permute-done | bytes 393248 | tf_op jit(solution)/shard_map/ppermute | solution.py:484
  43.9 2.1 %collective-permute-done.2.got_ref = bf16[384,256]{1,0:T(8,128)(2,1)S(1)} collective-permute-done((bf16[384,256]{1,0:T(8,128)(2,1)S(1)}, bf16[384,256]{1,0:T(8,128)(2,1)S(1)}, u32[]{:S(2)}, u32[]{:S(2)}) %collective-permute-start.2) | collective-permute-done | bytes 196640 | tf_op jit(solution)/shard_map/ppermute | solution.py:307
  46.6 1.6 %collective-permute-start.12 = (bf16[256,768]{1,0:T(8,128)(2,1)S(1)}, bf16[256,768]{1,0:T(8,128)(2,1)S(1)}, u32[]{:S(2)}, u32[]{:S(2)}) collective-permute-start(bf16[256,768]{1,0:T(8,128)(2,1)S(1)} %copy-done.11), channel_id=1, source_target_pairs={{0,8},{4,20},{8,0},{12,28},{16,24},{20,4},{24,16},{28,12},{1,9},{5... | collective-permute-start | bytes 1179656 | tf_op jit(solution)/shard_map/ppermute | solution.py:484
  48.2 0.9 %collective-permute-start.13 = (bf16[256,768]{1,0:T(8,128)(2,1)S(1)}, bf16[256,768]{1,0:T(8,128)(2,1)S(1)}, u32[]{:S(2)}, u32[]{:S(2)}) collective-permute-start(bf16[256,768]{1,0:T(8,128)(2,1)S(1)} %copy-done.10), channel_id=1, source_target_pairs={{0,12},{4,16},{8,4},{12,24},{16,28},{20,0},{24,20},{28,8},{1,13},{... | collective-permute-start | bytes 1179656 | tf_op jit(solution)/shard_map/ppermute | solution.py:484
  49.2 2.7 %read_out.1 = (f32[2048,256]{1,0:T(8,128)S(1)}, f32[1,2048]{1,0:T(1,128)S(1)}) custom-call(bf16[2048,256]{1,0:T(8,128)(2,1)S(1)} %copy-done, bf16[1,256,256]{2,1,0:T(8,128)(2,1)S(1)} %copy-done.1, bf16[1,256,256]{2,1,0:T(8,128)(2,1)S(1)} %copy-done.2, bf16[1,256,256]{2,1,0:T(8,128)(2,1)S(1)} %copy-done.3, f32[384,256]{1,0:T(8,128)S(1)} %merge.5.rest_0_, ...), custom_call_target="tpu_custom_call" | custom-call | flops 100663296 | bytes 524288 | tf_op jit(solution)/shard_map/read_out/pallas_call | solution.py:359
  51.9 1.6 %collective-permute-start.8 = (f32[1,2048]{1,0:T(1,128)S(1)}, f32[1,2048]{1,0:T(1,128)S(1)}, u32[]{:S(2)}, u32[]{:S(2)}) collective-permute-start(f32[1,2048]{1,0:T(1,128)S(1)} %get-tuple-element.39.refs_8_.rest_0_), channel_id=1, source_target_pairs={{0,1},{1,2},{2,3},{3,0},{4,5},{5,6},{6,7},{7,4},{8,9},{9,10},{10,1... | collective-permute-start | bytes 24584 | tf_op jit(solution)/shard_map/ppermute | solution.py:509
  53.5 2.6 %collective-permute-start.9 = (f32[1,2048]{1,0:T(1,128)S(1)}, f32[1,2048]{1,0:T(1,128)S(1)}, u32[]{:S(2)}, u32[]{:S(2)}) collective-permute-start(f32[1,2048]{1,0:T(1,128)S(1)} %get-tuple-element.39.refs_8_.rest_0_), channel_id=1, source_target_pairs={{0,2},{1,3},{2,0},{3,1},{4,6},{5,7},{6,4},{7,5},{8,10},{9,11},{10,... | collective-permute-start | bytes 24584 | tf_op jit(solution)/shard_map/ppermute | solution.py:509
  56.1 1.3 %collective-permute-start.10 = (f32[1,2048]{1,0:T(1,128)S(1)}, f32[1,2048]{1,0:T(1,128)S(1)}, u32[]{:S(2)}, u32[]{:S(2)}) collective-permute-start(f32[1,2048]{1,0:T(1,128)S(1)} %get-tuple-element.39.refs_8_.rest_0_), channel_id=1, source_target_pairs={{0,3},{1,0},{2,1},{3,2},{4,7},{5,4},{6,5},{7,6},{8,11},{9,8},{10,9... | collective-permute-start | bytes 24584 | tf_op jit(solution)/shard_map/ppermute | solution.py:509
  57.4 1.7 %place.1 = (bf16[2048,1024]{1,0:T(8,128)(2,1)S(1)}, bf16[2048,1024]{1,0:T(8,128)(2,1)S(1)}) custom-call(s32[1,2048]{1,0:T(1,128)S(1)} %copy-done.6), custom_call_target="tpu_custom_call" | custom-call | flops 524288 | bytes 1048576 | tf_op jit(solution)/shard_map/place/pallas_call | solution.py:398
  59.2 0.6 collective-permute-done.10.refs_11_.rest_3_
  59.7 1.5 %attend.1 = (bf16[256,256]{1,0:T(8,128)(2,1)S(1)}, bf16[256,256]{1,0:T(8,128)(2,1)S(1)}, bf16[256,256]{1,0:T(8,128)(2,1)S(1)}, bf16[256,256]{1,0:T(8,128)(2,1)S(...) custom-call(bf16[256,768]{1,0:T(8,128)(2,1)S(1)} %copy-done.4, ...), custom_call_target="tpu_custom_call" | custom-call | flops 67108864 | bytes 524288 | tf_op jit(solution)/shard_map/attend/pallas_call | solution.py:194
  61.3 1.0 %collective-permute-start.14 = (bf16[256,256]{1,0:T(8,128)(2,1)S(1)}, bf16[256,256]{1,0:T(8,128)(2,1)S(1)}, u32[]{:S(2)}, u32[]{:S(2)}) collective-permute-start(bf16[256,256]{1,0:T(8,128)(2,1)S(1)} %get-tuple-element.45), channel_id=1, source_target_pairs={{28,0},{24,4},{20,8},{16,12},{12,16},{8,20},{4,24},{0,28},{29,1},{... | collective-permute-start | bytes 393224 | tf_op jit(solution)/shard_map/ppermute | solution.py:489
  62.3 0.9 %collective-permute-start.15 = (bf16[256,256]{1,0:T(8,128)(2,1)S(1)}, bf16[256,256]{1,0:T(8,128)(2,1)S(1)}, u32[]{:S(2)}, u32[]{:S(2)}) collective-permute-start(bf16[256,256]{1,0:T(8,128)(2,1)S(1)} %get-tuple-element.46), channel_id=1, source_target_pairs={{24,0},{28,4},{16,8},{20,12},{8,16},{12,20},{0,24},{4,28},{25,1},{... | collective-permute-start | bytes 393224 | tf_op jit(solution)/shard_map/ppermute | solution.py:489
  63.2 0.9 %collective-permute-start.16 = (bf16[256,256]{1,0:T(8,128)(2,1)S(1)}, bf16[256,256]{1,0:T(8,128)(2,1)S(1)}, u32[]{:S(2)}, u32[]{:S(2)}) collective-permute-start(bf16[256,256]{1,0:T(8,128)(2,1)S(1)} %get-tuple-element.47), channel_id=1, source_target_pairs={{4,0},{0,4},{12,8},{8,12},{20,16},{16,20},{28,24},{24,28},{5,1},{1... | collective-permute-start | bytes 393224 | tf_op jit(solution)/shard_map/ppermute | solution.py:489
  64.6 1.3 %collective-permute-start.18 = (bf16[256,256]{1,0:T(8,128)(2,1)S(1)}, bf16[256,256]{1,0:T(8,128)(2,1)S(1)}, u32[]{:S(2)}, u32[]{:S(2)}) collective-permute-start(bf16[256,256]{1,0:T(8,128)(2,1)S(1)} %get-tuple-element.50), channel_id=1, source_target_pairs={{16,0},{12,4},{24,8},{4,12},{0,16},{28,20},{8,24},{20,28},{17,1},{... | collective-permute-start | bytes 393224 | tf_op jit(solution)/shard_map/ppermute | solution.py:489
  65.9 2.1 %collective-permute-done.14.rest_4_ = bf16[256,256]{1,0:T(8,128)(2,1)S(1)} collective-permute-done((bf16[256,256]{1,0:T(8,128)(2,1)S(1)}, bf16[256,256]{1,0:T(8,128)(2,1)S(1)}, u32[]{:S(2)}, u32[]{:S(2)}) %collective-permute-start.14) | collective-permute-done | bytes 131104 | tf_op jit(solution)/shard_map/ppermute | solution.py:489
  68.4 1.7 %collective-permute-done.15.rest_5_ = bf16[256,256]{1,0:T(8,128)(2,1)S(1)} collective-permute-done((bf16[256,256]{1,0:T(8,128)(2,1)S(1)}, bf16[256,256]{1,0:T(8,128)(2,1)S(1)}, u32[]{:S(2)}, u32[]{:S(2)}) %collective-permute-start.15) | collective-permute-done | bytes 131104 | tf_op jit(solution)/shard_map/ppermute | solution.py:489
  70.0 1.7 %collective-permute-start.20 = (bf16[256,256]{1,0:T(8,128)(2,1)S(1)}, bf16[256,256]{1,0:T(8,128)(2,1)S(1)}, u32[]{:S(2)}, u32[]{:S(2)}) collective-permute-start(bf16[256,256]{1,0:T(8,128)(2,1)S(1)} %get-tuple-element.52), channel_id=1, source_target_pairs={{8,0},{20,4},{0,8},{28,12},{24,16},{4,20},{16,24},{12,28},{9,1},{2... | collective-permute-start | bytes 393224 | tf_op jit(solution)/shard_map/ppermute | solution.py:489
  71.7 1.3 %base.1.base_ref = f32[2048,256]{1,0:T(8,128)S(1)} custom-call(f32[1,256]{1,0:T(1,128)S(1)} %bitcast.2, f32[2048,256]{1,0:T(8,128)S(1)} %get-tuple-element.37.y_ref, bf16[2048,1024]{1,0:T(8,128)(2,1)S(1)} %get-tuple-element.38.onehot, f32[1,2048]{1,0:T(1,128)S(1)} %get-tuple-element.39.refs_8_.rest_0_, f32[1,2048]{1,0:T(1,128)S(1)} %collective-permute-done.8.refs_9_.rest_1_, ...), custom_call_target="tpu_custom_call" | custom-call | flops 134217728 | bytes 524288 | tf_op jit(solution)/shard_map/base/pallas_call | solution.py:440
  73.2 1.6 %collective-permute-done.19.rest_2_ = bf16[256,256]{1,0:T(8,128)(2,1)S(1)} collective-permute-done((bf16[256,256]{1,0:T(8,128)(2,1)S(1)}, bf16[256,256]{1,0:T(8,128)(2,1)S(1)}, u32[]{:S(2)}, u32[]{:S(2)}) %collective-permute-start.19) | collective-permute-done | bytes 131104 | tf_op jit(solution)/shard_map/ppermute | solution.py:489
  74.8 0.8 %collective-permute-done.20.rest_3_ = bf16[256,256]{1,0:T(8,128)(2,1)S(1)} collective-permute-done((bf16[256,256]{1,0:T(8,128)(2,1)S(1)}, bf16[256,256]{1,0:T(8,128)(2,1)S(1)}, u32[]{:S(2)}, u32[]{:S(2)}) %collective-permute-start.20) | collective-permute-done | bytes 131104 | tf_op jit(solution)/shard_map/ppermute | solution.py:489
  75.6 2.1 %mix.1 = bf16[2048,256]{1,0:T(8,128)(2,1)} custom-call(f32[2048,256]{1,0:T(8,128)S(1)} %base.1.base_ref, bf16[2048,1024]{1,0:T(8,128)(2,1)S(1)} %get-tuple-element.44.refs_12_.onehot, bf16[256,256]{1,0:T(8,128)(2,1)S(1)} %collective-permute-done.17.rest_0_, bf16[256,256]{1,0:T(8,128)(2,1)S(1)} %collective-permute-done.18.rest_1_, ...), custom_call_target="tpu_custom_call" | custom-call | flops 134217728 | bytes 524288 | tf_op jit(solution)/shard_map/mix/pallas_call | solution.py:468
  (49 shorter events, 2.6 us)
Async XLA Ops:
  5.6 18.2 %copy-start.5 = (f32[384,256]{1,0:T(8,128)S(1)}, f32[384,256]{1,0:T(8,128)}, u32[]{:S(2)}) copy-start(f32[384,256]{1,0:T(8,128)} %get-tuple-element.29.keep_ref) | copy-start | bytes 1179652
  5.6 18.2 %collective-permute-start = (f32[384,256]{1,0:T(8,128)}, f32[384,256]{1,0:T(8,128)S(1)}, u32[]{:S(2)}, u32[]{:S(2)}) collective-permute-start(f32[384,256]{1,0:T(8,128)} %get-tuple-element.30), channel_id=1, source_target_pairs={{0,4},{4,0},{8,12},{12,8},{16,20},{20,16},{24,28},{28,24},{1,5},{5... | collective-permute-start | bytes 1179656 | tf_op jit(solution)/shard_map/ppermute | solution.py:300
  11.4 27.8 %collective-permute-start.3 = (bf16[256,768]{1,0:T(8,128)(2,1)}, bf16[256,768]{1,0:T(8,128)(2,1)S(1)}, u32[]{:S(2)}, u32[]{:S(2)}) collective-permute-start(bf16[256,768]{1,0:T(8,128)(2,1)} %get-tuple-element.33), channel_id=1, source_target_pairs={{0,28},{4,24},{8,20},{12,16},{16,12},{20,8},{24,4},{28,0},{1,29},{... | collective-permute-start | bytes 1179656 | tf_op jit(solution)/shard_map/ppermute | solution.py:484
  15.1 34.1 %copy-start = (bf16[2048,256]{1,0:T(8,128)(2,1)S(1)}, bf16[2048,256]{1,0:T(8,128)(2,1)}, u32[]{:S(2)}) copy-start(bf16[2048,256]{1,0:T(8,128)(2,1)} %q_ref.1) | copy-start | bytes 3145732
  15.1 34.1 %copy-start.1 = (bf16[1,256,256]{2,1,0:T(8,128)(2,1)S(1)}, bf16[1,256,256]{2,1,0:T(8,128)(2,1)}, u32[]{:S(2)}) copy-start(bf16[1,256,256]{2,1,0:T(8,128)(2,1)} %one_ref.1) | copy-start | bytes 393220
  15.1 34.1 %copy-start.2 = (bf16[1,256,256]{2,1,0:T(8,128)(2,1)S(1)}, bf16[1,256,256]{2,1,0:T(8,128)(2,1)}, u32[]{:S(2)}) copy-start(bf16[1,256,256]{2,1,0:T(8,128)(2,1)} %three_ref.1) | copy-start | bytes 393220
  15.1 34.1 %copy-start.3 = (bf16[1,256,256]{2,1,0:T(8,128)(2,1)S(1)}, bf16[1,256,256]{2,1,0:T(8,128)(2,1)}, u32[]{:S(2)}) copy-start(bf16[1,256,256]{2,1,0:T(8,128)(2,1)} %two_ref.1) | copy-start | bytes 393220
  15.1 24.2 %collective-permute-start.4 = (bf16[256,768]{1,0:T(8,128)(2,1)}, bf16[256,768]{1,0:T(8,128)(2,1)S(1)}, u32[]{:S(2)}, u32[]{:S(2)}) collective-permute-start(bf16[256,768]{1,0:T(8,128)(2,1)} %get-tuple-element.34), channel_id=1, source_target_pairs={{0,24},{4,28},{8,16},{12,20},{16,8},{20,12},{24,0},{28,4},{1,25},{... | collective-permute-start | bytes 1179656 | tf_op jit(solution)/shard_map/ppermute | solution.py:484
  23.8 33.6 %copy-start.6 = (s32[1,2048]{1,0:T(1,128)S(1)}, s32[1,2048]{1,0:T(1,128)}, u32[]{:S(2)}) copy-start(s32[1,2048]{1,0:T(1,128)} %order_ref.1) | copy-start | bytes 24580
  23.8 35.9 %copy-start.4 = (bf16[256,768]{1,0:T(8,128)(2,1)S(1)}, bf16[256,768]{1,0:T(8,128)(2,1)}, u32[]{:S(2)}) copy-start(bf16[256,768]{1,0:T(8,128)(2,1)} %get-tuple-element.40.refs_0_) | copy-start | bytes 1179652
  24.6 21.7 %copy-start.12 = (bf16[256,768]{1,0:T(8,128)(2,1)S(1)}, bf16[256,768]{1,0:T(8,128)(2,1)}, u32[]{:S(2)}) copy-start(bf16[256,768]{1,0:T(8,128)(2,1)} %get-tuple-element.41) | copy-start | bytes 1179652
  24.6 22.1 %copy-start.11 = (bf16[256,768]{1,0:T(8,128)(2,1)S(1)}, bf16[256,768]{1,0:T(8,128)(2,1)}, u32[]{:S(2)}) copy-start(bf16[256,768]{1,0:T(8,128)(2,1)} %get-tuple-element.42) | copy-start | bytes 1179652
  24.6 23.7 %copy-start.10 = (bf16[256,768]{1,0:T(8,128)(2,1)S(1)}, bf16[256,768]{1,0:T(8,128)(2,1)}, u32[]{:S(2)}) copy-start(bf16[256,768]{1,0:T(8,128)(2,1)} %get-tuple-element.43) | copy-start | bytes 1179652
  24.6 13.7 %collective-permute-start.1 = (bf16[384,256]{1,0:T(8,128)(2,1)S(1)}, bf16[384,256]{1,0:T(8,128)(2,1)S(1)}, u32[]{:S(2)}, u32[]{:S(2)}) collective-permute-start(bf16[384,256]{1,0:T(8,128)(2,1)S(1)} %convert_element_type.6), channel_id=1, source_target_pairs={{0,8},{4,20},{8,0},{12,28},{16,24},{20,4},{24,16},{28,12},{1,9},{5... | collective-permute-start | bytes 589832 | tf_op jit(solution)/shard_map/ppermute | solution.py:307
  26.6 13.3 %collective-permute-start.5 = (bf16[256,768]{1,0:T(8,128)(2,1)}, bf16[256,768]{1,0:T(8,128)(2,1)S(1)}, u32[]{:S(2)}, u32[]{:S(2)}) collective-permute-start(bf16[256,768]{1,0:T(8,128)(2,1)} %get-tuple-element.35), channel_id=1, source_target_pairs={{0,20},{4,8},{8,28},{12,0},{16,4},{20,24},{24,12},{28,16},{1,21},{... | collective-permute-start | bytes 1179656 | tf_op jit(solution)/shard_map/ppermute | solution.py:484
  26.6 17.3 %collective-permute-start.6 = (bf16[256,768]{1,0:T(8,128)(2,1)}, bf16[256,768]{1,0:T(8,128)(2,1)S(1)}, u32[]{:S(2)}, u32[]{:S(2)}) collective-permute-start(bf16[256,768]{1,0:T(8,128)(2,1)} %get-tuple-element.36), channel_id=1, source_target_pairs={{0,16},{4,12},{8,24},{12,4},{16,0},{20,28},{24,8},{28,20},{1,17},{... | collective-permute-start | bytes 1179656 | tf_op jit(solution)/shard_map/ppermute | solution.py:484
  39.1 6.9 %collective-permute-start.2 = (bf16[384,256]{1,0:T(8,128)(2,1)S(1)}, bf16[384,256]{1,0:T(8,128)(2,1)S(1)}, u32[]{:S(2)}, u32[]{:S(2)}) collective-permute-start(bf16[384,256]{1,0:T(8,128)(2,1)S(1)} %convert_element_type.7), channel_id=1, source_target_pairs={{0,16},{4,12},{8,24},{12,4},{16,0},{20,28},{24,8},{28,20},{1,17},{... | collective-permute-start | bytes 589832 | tf_op jit(solution)/shard_map/ppermute | solution.py:307
  46.0 3.1 %collective-permute-start.7 = (f32[384,256]{1,0:T(8,128)S(1)}, f32[384,256]{1,0:T(8,128)S(1)}, u32[]{:S(2)}, u32[]{:S(2)}) collective-permute-start(f32[384,256]{1,0:T(8,128)S(1)} %merge.5.rest_0_), channel_id=1, source_target_pairs={{0,4},{4,0},{8,12},{12,8},{16,20},{20,16},{24,28},{28,24},{1,5},{5... | collective-permute-start | bytes 1179656 | tf_op jit(solution)/shard_map/ppermute | solution.py:312
  46.2 9.9 %collective-permute-start.11 = (bf16[256,768]{1,0:T(8,128)(2,1)S(1)}, bf16[256,768]{1,0:T(8,128)(2,1)S(1)}, u32[]{:S(2)}, u32[]{:S(2)}) collective-permute-start(bf16[256,768]{1,0:T(8,128)(2,1)S(1)} %copy-done.12), channel_id=1, source_target_pairs={{0,4},{4,0},{8,12},{12,8},{16,20},{20,16},{24,28},{28,24},{1,5},{5... | collective-permute-start | bytes 1179656 | tf_op jit(solution)/shard_map/ppermute | solution.py:484
  46.6 12.5 %collective-permute-start.12 = (bf16[256,768]{1,0:T(8,128)(2,1)S(1)}, bf16[256,768]{1,0:T(8,128)(2,1)S(1)}, u32[]{:S(2)}, u32[]{:S(2)}) collective-permute-start(bf16[256,768]{1,0:T(8,128)(2,1)S(1)} %copy-done.11), channel_id=1, source_target_pairs={{0,8},{4,20},{8,0},{12,28},{16,24},{20,4},{24,16},{28,12},{1,9},{5... | collective-permute-start | bytes 1179656 | tf_op jit(solution)/shard_map/ppermute | solution.py:484
  48.2 10.9 %collective-permute-start.13 = (bf16[256,768]{1,0:T(8,128)(2,1)S(1)}, bf16[256,768]{1,0:T(8,128)(2,1)S(1)}, u32[]{:S(2)}, u32[]{:S(2)}) collective-permute-start(bf16[256,768]{1,0:T(8,128)(2,1)S(1)} %copy-done.10), channel_id=1, source_target_pairs={{0,12},{4,16},{8,4},{12,24},{16,28},{20,0},{24,20},{28,8},{1,13},{... | collective-permute-start | bytes 1179656 | tf_op jit(solution)/shard_map/ppermute | solution.py:484
  51.9 19.8 %copy-start.9 = (f32[256]{0:T(256)S(1)}, f32[256]{0:T(256)}, u32[]{:S(2)}) copy-start(f32[256]{0:T(256)} %param.16) | copy-start | bytes 3076
  51.9 7.3 %collective-permute-start.8 = (f32[1,2048]{1,0:T(1,128)S(1)}, f32[1,2048]{1,0:T(1,128)S(1)}, u32[]{:S(2)}, u32[]{:S(2)}) collective-permute-start(f32[1,2048]{1,0:T(1,128)S(1)} %get-tuple-element.39.refs_8_.rest_0_), channel_id=1, source_target_pairs={{0,1},{1,2},{2,3},{3,0},{4,5},{5,6},{6,7},{7,4},{8,9},{9,10},{10,1... | collective-permute-start | bytes 24584 | tf_op jit(solution)/shard_map/ppermute | solution.py:509
  53.5 5.7 %collective-permute-start.9 = (f32[1,2048]{1,0:T(1,128)S(1)}, f32[1,2048]{1,0:T(1,128)S(1)}, u32[]{:S(2)}, u32[]{:S(2)}) collective-permute-start(f32[1,2048]{1,0:T(1,128)S(1)} %get-tuple-element.39.refs_8_.rest_0_), channel_id=1, source_target_pairs={{0,2},{1,3},{2,0},{3,1},{4,6},{5,7},{6,4},{7,5},{8,10},{9,11},{10,... | collective-permute-start | bytes 24584 | tf_op jit(solution)/shard_map/ppermute | solution.py:509
  56.1 3.7 %collective-permute-start.10 = (f32[1,2048]{1,0:T(1,128)S(1)}, f32[1,2048]{1,0:T(1,128)S(1)}, u32[]{:S(2)}, u32[]{:S(2)}) collective-permute-start(f32[1,2048]{1,0:T(1,128)S(1)} %get-tuple-element.39.refs_8_.rest_0_), channel_id=1, source_target_pairs={{0,3},{1,0},{2,1},{3,2},{4,7},{5,4},{6,5},{7,6},{8,11},{9,8},{10,9... | collective-permute-start | bytes 24584 | tf_op jit(solution)/shard_map/ppermute | solution.py:509
  61.3 6.8 %collective-permute-start.14 = (bf16[256,256]{1,0:T(8,128)(2,1)S(1)}, bf16[256,256]{1,0:T(8,128)(2,1)S(1)}, u32[]{:S(2)}, u32[]{:S(2)}) collective-permute-start(bf16[256,256]{1,0:T(8,128)(2,1)S(1)} %get-tuple-element.45), channel_id=1, source_target_pairs={{28,0},{24,4},{20,8},{16,12},{12,16},{8,20},{4,24},{0,28},{29,1},{... | collective-permute-start | bytes 393224 | tf_op jit(solution)/shard_map/ppermute | solution.py:489
  62.3 7.8 %collective-permute-start.15 = (bf16[256,256]{1,0:T(8,128)(2,1)S(1)}, bf16[256,256]{1,0:T(8,128)(2,1)S(1)}, u32[]{:S(2)}, u32[]{:S(2)}) collective-permute-start(bf16[256,256]{1,0:T(8,128)(2,1)S(1)} %get-tuple-element.46), channel_id=1, source_target_pairs={{24,0},{28,4},{16,8},{20,12},{8,16},{12,20},{0,24},{4,28},{25,1},{... | collective-permute-start | bytes 393224 | tf_op jit(solution)/shard_map/ppermute | solution.py:489
  63.2 8.5 %collective-permute-start.16 = (bf16[256,256]{1,0:T(8,128)(2,1)S(1)}, bf16[256,256]{1,0:T(8,128)(2,1)S(1)}, u32[]{:S(2)}, u32[]{:S(2)}) collective-permute-start(bf16[256,256]{1,0:T(8,128)(2,1)S(1)} %get-tuple-element.47), channel_id=1, source_target_pairs={{4,0},{0,4},{12,8},{8,12},{20,16},{16,20},{28,24},{24,28},{5,1},{1... | collective-permute-start | bytes 393224 | tf_op jit(solution)/shard_map/ppermute | solution.py:489
  64.1 9.0 %collective-permute-start.17 = (bf16[256,256]{1,0:T(8,128)(2,1)S(1)}, bf16[256,256]{1,0:T(8,128)(2,1)S(1)}, u32[]{:S(2)}, u32[]{:S(2)}) collective-permute-start(bf16[256,256]{1,0:T(8,128)(2,1)S(1)} %get-tuple-element.49), channel_id=1, source_target_pairs={{20,0},{8,4},{28,8},{0,12},{4,16},{24,20},{12,24},{16,28},{21,1},{... | collective-permute-start | bytes 393224 | tf_op jit(solution)/shard_map/ppermute | solution.py:489
  64.6 8.5 %collective-permute-start.18 = (bf16[256,256]{1,0:T(8,128)(2,1)S(1)}, bf16[256,256]{1,0:T(8,128)(2,1)S(1)}, u32[]{:S(2)}, u32[]{:S(2)}) collective-permute-start(bf16[256,256]{1,0:T(8,128)(2,1)S(1)} %get-tuple-element.50), channel_id=1, source_target_pairs={{16,0},{12,4},{24,8},{4,12},{0,16},{28,20},{8,24},{20,28},{17,1},{... | collective-permute-start | bytes 393224 | tf_op jit(solution)/shard_map/ppermute | solution.py:489
  68.0 6.7 %collective-permute-start.19 = (bf16[256,256]{1,0:T(8,128)(2,1)S(1)}, bf16[256,256]{1,0:T(8,128)(2,1)S(1)}, u32[]{:S(2)}, u32[]{:S(2)}) collective-permute-start(bf16[256,256]{1,0:T(8,128)(2,1)S(1)} %get-tuple-element.51), channel_id=1, source_target_pairs={{12,0},{16,4},{4,8},{24,12},{28,16},{0,20},{20,24},{8,28},{13,1},{... | collective-permute-start | bytes 393224 | tf_op jit(solution)/shard_map/ppermute | solution.py:489
  70.0 5.6 %collective-permute-start.20 = (bf16[256,256]{1,0:T(8,128)(2,1)S(1)}, bf16[256,256]{1,0:T(8,128)(2,1)S(1)}, u32[]{:S(2)}, u32[]{:S(2)}) collective-permute-start(bf16[256,256]{1,0:T(8,128)(2,1)S(1)} %get-tuple-element.52), channel_id=1, source_target_pairs={{8,0},{20,4},{0,8},{28,12},{24,16},{4,20},{16,24},{12,28},{9,1},{2... | collective-permute-start | bytes 393224 | tf_op jit(solution)/shard_map/ppermute | solution.py:489
  (2 other events, 1.4 us)

commit v4 on v3

--- a/solution.py
+++ b/solution.py
@@ -12,8 +12,8 @@
 LANES = 128
 TILE = 512
 LIMIT = 24
-FIRST_LIMIT = 54
-COST = 8
+COST = 1
+FIRST_COST = pl.CostEstimate(flops=10**12, bytes_accessed=1024, transcendentals=0)
 MIB = 1024 * 1024
 F32 = jnp.float32
 BF16 = jnp.bfloat16
@@ -33,7 +33,7 @@
 
 
 def params(limit=LIMIT):
-    return pltpu.CompilerParams(vmem_limit_bytes=limit * MIB)
+    return pltpu.CompilerParams(vmem_limit_bytes=int(limit * MIB))
 
 
 def full(count):
@@ -87,80 +87,65 @@
     return copies
 
 
-def sort_into(n, steps, order, sources, outs, onehot):
+def mark_kernel(n, steps, order_ref, *rest):
+    outs, token = rest[:-1], rest[-1]
+    token[...] = jnp.zeros_like(token)
     me = lax.axis_index("cam")
-    count = onehot.shape[1]
+    count = order_ref.shape[1]
     rows = count // n
-    group = onehot.shape[0] // rows
-    for first in range(0, len(steps), group):
-        for at in range(group):
-            base = peer(me, steps[first + at], n) * rows
-            slot = lax.broadcasted_iota(jnp.int32, (rows, count), 0) + base
-            onehot[at * rows : (at + 1) * rows, :] = (slot == order).astype(F32).astype(BF16)
-        for which, source in sources:
-            ref = source(first == 0)
-            width = ref.shape[1]
-            picked = dot(onehot[...], ref[...]).astype(BF16)
+    order = order_ref[...]
+    slot = lax.broadcasted_iota(jnp.int32, (rows, count), 0)
+    for group, out in zip(steps, outs):
+        for at, step in enumerate(group):
+            hit = slot + peer(me, step, n) * rows == order
+            out[at * rows : (at + 1) * rows, :] = hit.astype(F32).astype(BF16)
+
+
+def mark(order, n, steps):
+    count = order.shape[1]
+    rows = count // n
+    return pl.pallas_call(
+        functools.partial(mark_kernel, n, steps),
+        out_shape=[jax.ShapeDtypeStruct((len(group) * rows, count), BF16) for group in steps]
+        + [TOKEN],
+        in_specs=full(1),
+        out_specs=full(len(steps) + 1),
+        compiler_params=params(),
+        cost_estimate=FIRST_COST,
+        name="mark",
+    )(order)
+
+
+def sort_kernel(onehot, q_ref, k_ref, v_ref, *rest):
+    outs, token = rest[:-1], rest[-1]
+    token[...] = jnp.zeros_like(token)
+    rows, width = outs[0].shape[0], q_ref.shape[1]
+    group = max(1, min(len(outs), TILE // rows))
+    while len(outs) % group:
+        group -= 1
+    for first in range(0, len(outs), group):
+        marks = onehot[first * rows : (first + group) * rows, :]
+        for which, ref in enumerate((q_ref, k_ref, v_ref)):
+            picked = dot(marks, ref[...]).astype(BF16)
             for at in range(group):
                 outs[first + at][:, which * width : (which + 1) * width] = picked[
                     at * rows : (at + 1) * rows
                 ]
 
 
-def first_sort_kernel(n, steps, order_in, q_in, k_in, v_in, *rest):
-    outs, rest = rest[: len(steps)], rest[len(steps) :]
-    token, onehot, order_ref, k_ref, v_ref, q_ref, sems = rest
-    token[...] = jnp.zeros_like(token)
-    copies = fetch(
-        ((order_in, order_ref), (k_in, k_ref), (v_in, v_ref), (q_in, q_ref)), sems
-    )
-    copies[0].wait()
-
-    def arrives(ref, copy):
-        def get(first):
-            if first:
-                copy.wait()
-            return ref
-
-        return get
-
-    sources = (
-        (1, arrives(k_ref, copies[1])),
-        (2, arrives(v_ref, copies[2])),
-        (0, arrives(q_ref, copies[3])),
-    )
-    sort_into(n, steps, order_ref[...], sources, outs, onehot)
-
-
-def sort_kernel(n, steps, order_ref, q_ref, k_ref, v_ref, *rest):
-    outs, (token, onehot) = rest[: len(steps)], rest[len(steps) :]
-    token[...] = jnp.zeros_like(token)
-    sources = ((0, lambda _: q_ref), (1, lambda _: k_ref), (2, lambda _: v_ref))
-    sort_into(n, steps, order_ref[...], sources, outs, onehot)
-
-
-def sort_tokens(order, q, k, v, n, steps, first):
+def sort_tokens(onehot, q, k, v, n):
     count, width = q.shape
     rows = count // n
-    size = len(steps)
-    group = max(1, min(size, TILE // rows))
-    while size % group:
-        group -= 1
-    shapes = [jax.ShapeDtypeStruct((rows, 3 * width), BF16)] * size + [TOKEN]
-    scratch = [pltpu.VMEM((group * rows, count), BF16)]
-    if first:
-        scratch = scratch + [pltpu.VMEM(array.shape, array.dtype) for array in (order, k, v, q)]
-        scratch = scratch + [pltpu.SemaphoreType.DMA((4,))]
-    return pl.pallas_call(
-        functools.partial(first_sort_kernel if first else sort_kernel, n, tuple(steps)),
-        out_shape=shapes,
-        in_specs=[pl.BlockSpec(memory_space=pltpu.HBM)] * 4 if first else full(4),
-        out_specs=full(len(shapes)),
-        scratch_shapes=scratch,
-        compiler_params=params(FIRST_LIMIT if first else LIMIT),
+    size = onehot.shape[0] // rows
+    return pl.pallas_call(
+        sort_kernel,
+        out_shape=[jax.ShapeDtypeStruct((rows, 3 * width), BF16)] * size + [TOKEN],
+        in_specs=full(4),
+        out_specs=full(size + 1),
+        compiler_params=params(),
         cost_estimate=cost(6 * size * rows * count * width, 6 * count * width),
         name="sort_tokens",
-    )(order, q, k, v)
+    )(onehot, q, k, v)
 
 
 def attend_kernel(n, scale, *refs):
@@ -205,25 +190,13 @@
     )(*blocks, *after)
 
 
-def grads_kernel(n, split, parts, k_in, v_in, rate_in, one_in, three_in, two_in, *rest):
-    outs, rest = rest[:parts], rest[parts:]
-    total, one_ref, three_ref, two_ref, rate_ref, k_ref, v_ref, sems = rest
+def grads_kernel(n, split, k_ref, v_ref, rate_ref, one_ref, three_ref, two_ref, *rest):
+    outs, total = rest[1:-1], rest[-1]
     count, width = k_ref.shape
     hid = one_ref.shape[1]
+    one, three, two = one_ref[0], three_ref[0], two_ref[0]
     tile = min(count, TILE)
-    tiles = [slice(start, start + tile) for start in range(0, count, tile)]
-    pairs = [(one_in, one_ref), (three_in, three_ref), (k_in.at[tiles[0]], k_ref.at[tiles[0]])]
-    pairs += [(rate_in, rate_ref), (v_in.at[tiles[0]], v_ref.at[tiles[0]]), (two_in, two_ref)]
-    for here in tiles[1:]:
-        pairs += [(k_in.at[here], k_ref.at[here]), (v_in.at[here], v_ref.at[here])]
-    copies = fetch(pairs, sems)
-    for copy in copies[:6]:
-        copy.wait()
-    one, three, two = one_ref[0], three_ref[0], two_ref[0]
     for start in range(0, count, tile):
-        if start:
-            copies[4 + 2 * (start // tile)].wait()
-            copies[5 + 2 * (start // tile)].wait()
         k = k_ref[start : start + tile, :]
         h_one = dot_bt(k, one)
         h_three = dot_bt(k, three)
@@ -252,27 +225,23 @@
         outs[0][...] = total[...]
 
 
-def gradients(k, v, rate, one, three, two, n):
+def gradients(k, v, rate, one, three, two, after, n):
     count, width = k.shape
     hid = one.shape[1]
     split = n > 1 and power_of_two(n)
     assert hid == width
     rows = 3 * hid
     parts = 2 if split else 1
-    tiles = count // min(count, TILE)
-    held = (one, three, two, rate, k, v)
-    return pl.pallas_call(
-        functools.partial(grads_kernel, n, split, parts),
+    return pl.pallas_call(
+        functools.partial(grads_kernel, n, split),
         out_shape=[jax.ShapeDtypeStruct((rows // parts, width), F32)] * parts,
-        in_specs=[pl.BlockSpec(memory_space=pltpu.HBM)] * 6,
+        in_specs=full(6) + [pl.BlockSpec(memory_space=pl.ANY)],
         out_specs=full(parts),
-        scratch_shapes=[pltpu.VMEM((rows, width), F32)]
-        + [pltpu.VMEM(array.shape, array.dtype) for array in held]
-        + [pltpu.SemaphoreType.DMA((4 + 2 * tiles,))],
-        compiler_params=params(58),
+        scratch_shapes=[pltpu.VMEM((rows, width), F32)],
+        compiler_params=params(),
         cost_estimate=cost(12 * count * width * hid, 8 * count * width, count * hid),
         name="gradients",
-    )(k, v, rate, one, three, two)
+    )(k, v, rate, one, three, two, after)
 
 
 def merge_kernel(keep_ref, got_ref, *rest):
@@ -495,16 +464,19 @@
     heads = lax.axis_size("head")
     steps = far_first(n)
     few = max(1, n // 4)
-    parts = gradients(keys, values, rates.reshape(1, count), w_one, w_three, w_two, n)
+    weights = (w_one, w_three, w_two)
+    groups = (tuple(steps[:few]), tuple(steps[few:]))
+    marks = mark(order, n, groups)
+    parts = gradients(keys, values, rates.reshape(1, count), *weights, marks[-1], n)
     arrived = {}
     after = []
-    for at, group in enumerate((steps[:few], steps[few:])):
-        blocks = sort_tokens(order, queries, keys, values, n, group, True)
+    for group, onehot in zip(groups, marks):
+        blocks = sort_tokens(onehot, queries, keys, values, n)
         after.append(blocks[-1])
         for step, block in zip(group, blocks):
             arrived[step] = exchange(block, step, n)
-    summed = sum_over_cams(parts, [after[:1], after[1:], [arrived[step] for step in steps[: 2 * few]]], n)
-    y, square = read_out(queries, w_one, w_three, w_two, summed)
+    summed = sum_over_cams(parts, [after[:1], after[1:], [arrived[step] for step in steps[:few+1]]], n)
+    y, square = read_out(queries, *weights, summed)
     squares = [square] + [
         lax.ppermute(square, "head", [(at, (at + step) % heads) for at in range(heads)])
         for step in range(1, heads)

time: 78.1 us -> 75.6 us (0.968)
  Pallas kernels: 28.9 us -> 20.6 us
  waiting for transfers between devices: 24.1 us -> 30.4 us
    pallas_call x3 -> x4, Pallas kernels: 19.5 us -> 11.2 us  [the longest x2 6.92 us: sort_tokens(): pl.pallas_call(sort_kernel, out_shape=[jax.ShapeDtypeStruct((rows, 3 * wi...]
    ppermute x2, waiting for transfers between devices: 12.4 us -> 20.1 us  [sum_over_cams(): got = lax.ppermute(mine.astype(BF16), 'cam', pairs)]
    ppermute x7, waiting for transfers between devices: 4.68 us -> 2.44 us  [exchange(): return lax.ppermute(block, 'cam', routes(step, n)) if step else block]
    ppermute x3, starting transfers between devices: 5.55 us -> 7.69 us  [per_device(): lax.ppermute(square, 'head', [(at, (at + step) % heads) for at in range(h...]
    ppermute x7, waiting for transfers between devices: 6.43 us -> 7.79 us  [give_back(): return lax.ppermute(block, 'cam', pairs) if step else block]
    ppermute x7, starting transfers between devices: 6.65 us -> 5.55 us  [give_back(): return lax.ppermute(block, 'cam', pairs) if step else block]
    ppermute x7, starting transfers between devices: 8.16 us -> 7.14 us  [exchange(): return lax.ppermute(block, 'cam', routes(step, n)) if step else block]
  transfers between devices with their start and end apart: 21 -> 21, of which waited for: 11 -> 10; matrix products, arithmetic and copies ran while one was open for 0% -> 0% of each run, Pallas kernels for 25% -> 17%
where the time goes in v4:
time: 75.6 us; the launch traced here: 75.4 us
  waiting for transfers between devices  30.4 us (40%)
  starting transfers between devices  23 us (30%)
  Pallas kernels  20.6 us (27%)
  local copies, waits for them, and re-layouts  0.87 us (1%)
    ppermute x2, waiting for transfers between devices, sum_over_cams(): got = lax.ppermute(mine.astype(BF16), 'cam', pairs)  20.1 us
    ppermute x7, waiting for transfers between devices, give_back(): return lax.ppermute(block, 'cam', pairs) if step else block  7.79 us
    ppermute x3, starting transfers between devices, per_device(): lax.ppermute(square, 'head', [(at, (at + step) % heads) for at in range(h...  7.69 us
    ppermute x7, starting transfers between devices, exchange(): return lax.ppermute(block, 'cam', routes(step, n)) if step else block  7.14 us
    pallas_call x2, Pallas kernels, sort_tokens(): pl.pallas_call(sort_kernel, out_shape=[jax.ShapeDtypeStruct((rows, 3 * wi...  6.92 us
    ppermute x7, starting transfers between devices, give_back(): return lax.ppermute(block, 'cam', pairs) if step else block  5.55 us
    pallas_call x1, Pallas kernels, gradients(): pl.pallas_call(functools.partial(grads_kernel, n, split), out_shape=[jax....  2.9 us
    pallas_call x1, Pallas kernels, read_out(): pl.pallas_call(functools.partial(readout_kernel, parts), out_shape=[jax.S...  2.67 us
  transfers between devices with their start and end apart: 21, of which 10 were waited for; matrix products, arithmetic and copies ran while one was open for 0% of the time, Pallas kernels for 17%

profile of v4, /device:TPU:0, one launch (start us, length us, event | category | flops | bytes accessed | tf_op | source)
XLA Modules:
  0.0 75.4 jit_solution(6740258796555920751)
XLA Ops:
  0.0 0.7 copy-done.8
  0.7 1.4 %mark.1 = (bf16[512,2048]{1,0:T(8,128)(2,1)S(1)}, bf16[1536,2048]{1,0:T(8,128)(2,1)S(1)}, f32[8,128]{1,0:T(8,128)S(1)}) custom-call(s32[1,2048]{1,0:T(1,128)S(1)} %copy-done.8), custom_call_target="tpu_custom_call" | custom-call | flops 999999995904 | bytes 1024 | tf_op jit(solution)/shard_map/mark/pallas_call | solution.py:107
  2.3 2.9 %gradients.1 = (f32[384,256]{1,0:T(8,128)S(1)}, f32[384,256]{1,0:T(8,128)S(1)}) custom-call(bf16[2048,256]{1,0:T(8,128)(2,1)S(1)} %copy-done.1, bf16[2048,256]{1,0:T(8,128)(2,1)S(1)} %copy-done.2, f32[1,2048]{1,0:T(1,128)S(1)} %bitcast.3, bf16[1,256,256]{2,1,0:T(8,128)(2,1)S(1)} %copy-done.4, bf16[1,256,256]{2,1,0:T(8,128)(2,1)S(1)} %copy-done.5, ...), custom_call_target="tpu_custom_call" | custom-call | flops 1610612736 | bytes 4194304 | tf_op jit(solution)/shard_map/gradients/pallas_call | solution.py:235
  5.2 0.5 collective-permute-start
  5.7 1.8 %sort_tokens.2 = (bf16[256,768]{1,0:T(8,128)(2,1)S(1)}, bf16[256,768]{1,0:T(8,128)(2,1)S(1)}, f32[8,128]{1,0:T(8,128)S(1)}) custom-call(bf16[512,2048]{1,0:T(8,128)(2,1)S(1)} %get-tuple-element.35.onehot, bf16[2048,256]{1,0:T(8,128)(2,1)S(1)} %copy-done.3, bf16[2048,256]{1,0:T(8,128)(2,1)S(1)} %copy-done.1, bf16[2048,256]{1,0:T(8,128)(2,1)S(1)} %copy-done.2), custom_call_target="tpu_custom_call" | custom-call | flops 1610612736 | bytes 3145728 | tf_op jit(solution)/shard_map/sort_tokens/pallas_call | solution.py:140
  7.5 3.6 %collective-permute-start.3 = (bf16[256,768]{1,0:T(8,128)(2,1)S(1)}, bf16[256,768]{1,0:T(8,128)(2,1)S(1)}, u32[]{:S(2)}, u32[]{:S(2)}) collective-permute-start(bf16[256,768]{1,0:T(8,128)(2,1)S(1)} %get-tuple-element.39), channel_id=1, source_target_pairs={{0,28},{4,24},{8,20},{12,16},{16,12},{20,8},{24,4},{28,0},{1,29},{... | collective-permute-start | bytes 1179656 | tf_op jit(solution)/shard_map/ppermute | solution.py:453
  11.3 2.0 %collective-permute-start.1 = (bf16[384,256]{1,0:T(8,128)(2,1)S(1)}, bf16[384,256]{1,0:T(8,128)(2,1)S(1)}, u32[]{:S(2)}, u32[]{:S(2)}) collective-permute-start(bf16[384,256]{1,0:T(8,128)(2,1)S(1)} %convert_element_type.6), channel_id=1, source_target_pairs={{0,8},{4,20},{8,0},{12,28},{16,24},{20,4},{24,16},{28,12},{1,9},{5... | collective-permute-start | bytes 589832 | tf_op jit(solution)/shard_map/ppermute | solution.py:276
  13.3 5.1 %sort_tokens.3 = (bf16[256,768]{1,0:T(8,128)(2,1)S(1)}, bf16[256,768]{1,0:T(8,128)(2,1)S(1)}, bf16[256,768]{1,0:T(8,128)(2,1)S(1)}, bf16[256,768]{1,0:T(8,128)(2...) custom-call(bf16[1536,2048]{1,0:T(8,128)(2,1)S(1)} %get-tuple-element.37.onehot, ...), custom_call_target="tpu_custom_call" | custom-call | flops 4831838208 | bytes 3145728 | tf_op jit(solution)/shard_map/sort_tokens/pallas_call | solution.py:140
  18.5 15.8 %collective-permute-done.1.got_ref = bf16[384,256]{1,0:T(8,128)(2,1)S(1)} collective-permute-done((bf16[384,256]{1,0:T(8,128)(2,1)S(1)}, bf16[384,256]{1,0:T(8,128)(2,1)S(1)}, u32[]{:S(2)}, u32[]{:S(2)}) %collective-permute-start.1) | collective-permute-done | bytes 196640 | tf_op jit(solution)/shard_map/ppermute | solution.py:276
  34.5 1.3 %collective-permute-done.5.rest_2_.refs_5_ = bf16[256,768]{1,0:T(8,128)(2,1)S(1)} collective-permute-done((bf16[256,768]{1,0:T(8,128)(2,1)S(1)}, bf16[256,768]{1,0:T(8,128)(2,1)S(1)}, u32[]{:S(2)}, u32[]{:S(2)}) %collective-permute-start.5) | collective-permute-done | bytes 393248 | tf_op jit(solution)/shard_map/ppermute | solution.py:453
  35.8 4.3 %collective-permute-done.2.got_ref = bf16[384,256]{1,0:T(8,128)(2,1)S(1)} collective-permute-done((bf16[384,256]{1,0:T(8,128)(2,1)S(1)}, bf16[384,256]{1,0:T(8,128)(2,1)S(1)}, u32[]{:S(2)}, u32[]{:S(2)}) %collective-permute-start.2) | collective-permute-done | bytes 196640 | tf_op jit(solution)/shard_map/ppermute | solution.py:276
  40.2 0.5 collective-permute-start.10
  40.7 1.5 %collective-permute-start.11 = (bf16[256,768]{1,0:T(8,128)(2,1)S(1)}, bf16[256,768]{1,0:T(8,128)(2,1)S(1)}, u32[]{:S(2)}, u32[]{:S(2)}) collective-permute-start(bf16[256,768]{1,0:T(8,128)(2,1)S(1)} %get-tuple-element.47), channel_id=1, source_target_pairs={{0,8},{4,20},{8,0},{12,28},{16,24},{20,4},{24,16},{28,12},{1,9},{5... | collective-permute-start | bytes 1179656 | tf_op jit(solution)/shard_map/ppermute | solution.py:453
  42.2 1.4 %collective-permute-start.13 = (bf16[256,768]{1,0:T(8,128)(2,1)S(1)}, bf16[256,768]{1,0:T(8,128)(2,1)S(1)}, u32[]{:S(2)}, u32[]{:S(2)}) collective-permute-start(bf16[256,768]{1,0:T(8,128)(2,1)S(1)} %get-tuple-element.49), channel_id=1, source_target_pairs={{0,16},{4,12},{8,24},{12,4},{16,0},{20,28},{24,8},{28,20},{1,17},{... | collective-permute-start | bytes 1179656 | tf_op jit(solution)/shard_map/ppermute | solution.py:453
  43.7 2.7 %read_out.1 = (f32[2048,256]{1,0:T(8,128)S(1)}, f32[1,2048]{1,0:T(1,128)S(1)}) custom-call(bf16[2048,256]{1,0:T(8,128)(2,1)S(1)} %copy-done.3, bf16[1,256,256]{2,1,0:T(8,128)(2,1)S(1)} %copy-done.4, bf16[1,256,256]{2,1,0:T(8,128)(2,1)S(1)} %copy-done.5, bf16[1,256,256]{2,1,0:T(8,128)(2,1)S(1)} %copy-done.6, f32[384,256]{1,0:T(8,128)S(1)} %merge.5.rest_0_, ...), custom_call_target="tpu_custom_call" | custom-call | flops 805306368 | bytes 4194304 | tf_op jit(solution)/shard_map/read_out/pallas_call | solution.py:328
  46.3 1.6 %collective-permute-start.7 = (f32[1,2048]{1,0:T(1,128)S(1)}, f32[1,2048]{1,0:T(1,128)S(1)}, u32[]{:S(2)}, u32[]{:S(2)}) collective-permute-start(f32[1,2048]{1,0:T(1,128)S(1)} %get-tuple-element.44.refs_8_.rest_0_), channel_id=1, source_target_pairs={{0,1},{1,2},{2,3},{3,0},{4,5},{5,6},{6,7},{7,4},{8,9},{9,10},{10,1... | collective-permute-start | bytes 24584 | tf_op jit(solution)/shard_map/ppermute | solution.py:481
  47.9 2.6 %collective-permute-start.8 = (f32[1,2048]{1,0:T(1,128)S(1)}, f32[1,2048]{1,0:T(1,128)S(1)}, u32[]{:S(2)}, u32[]{:S(2)}) collective-permute-start(f32[1,2048]{1,0:T(1,128)S(1)} %get-tuple-element.44.refs_8_.rest_0_), channel_id=1, source_target_pairs={{0,2},{1,3},{2,0},{3,1},{4,6},{5,7},{6,4},{7,5},{8,10},{9,11},{10,... | collective-permute-start | bytes 24584 | tf_op jit(solution)/shard_map/ppermute | solution.py:481
  50.5 1.1 %collective-permute-done.11.refs_2_ = bf16[256,768]{1,0:T(8,128)(2,1)S(1)} collective-permute-done((bf16[256,768]{1,0:T(8,128)(2,1)S(1)}, bf16[256,768]{1,0:T(8,128)(2,1)S(1)}, u32[]{:S(2)}, u32[]{:S(2)}) %collective-permute-start.11) | collective-permute-done | bytes 393248 | tf_op jit(solution)/shard_map/ppermute | solution.py:453
  51.7 3.5 %collective-permute-start.9 = (f32[1,2048]{1,0:T(1,128)S(1)}, f32[1,2048]{1,0:T(1,128)S(1)}, u32[]{:S(2)}, u32[]{:S(2)}) collective-permute-start(f32[1,2048]{1,0:T(1,128)S(1)} %get-tuple-element.44.refs_8_.rest_0_), channel_id=1, source_target_pairs={{0,3},{1,0},{2,1},{3,2},{4,7},{5,4},{6,5},{7,6},{8,11},{9,8},{10,9... | collective-permute-start | bytes 24584 | tf_op jit(solution)/shard_map/ppermute | solution.py:481
  55.2 1.7 %place.1 = (bf16[2048,1024]{1,0:T(8,128)(2,1)S(1)}, bf16[2048,1024]{1,0:T(8,128)(2,1)S(1)}) custom-call(s32[1,2048]{1,0:T(1,128)S(1)} %copy-done.9), custom_call_target="tpu_custom_call" | custom-call | flops 4194304 | bytes 8388608 | tf_op jit(solution)/shard_map/place/pallas_call | solution.py:367
  56.9 1.5 %attend.1 = (bf16[256,256]{1,0:T(8,128)(2,1)S(1)}, bf16[256,256]{1,0:T(8,128)(2,1)S(1)}, bf16[256,256]{1,0:T(8,128)(2,1)S(1)}, bf16[256,256]{1,0:T(8,128)(2,1)S(...) custom-call(bf16[256,768]{1,0:T(8,128)(2,1)S(1)} %get-tuple-element., ...), custom_call_target="tpu_custom_call" | custom-call | flops 536870912 | bytes 4194304 | tf_op jit(solution)/shard_map/attend/pallas_call | solution.py:179
  58.5 1.0 %collective-permute-start.14 = (bf16[256,256]{1,0:T(8,128)(2,1)S(1)}, bf16[256,256]{1,0:T(8,128)(2,1)S(1)}, u32[]{:S(2)}, u32[]{:S(2)}) collective-permute-start(bf16[256,256]{1,0:T(8,128)(2,1)S(1)} %get-tuple-element.51), channel_id=1, source_target_pairs={{28,0},{24,4},{20,8},{16,12},{12,16},{8,20},{4,24},{0,28},{29,1},{... | collective-permute-start | bytes 393224 | tf_op jit(solution)/shard_map/ppermute | solution.py:458
  59.4 1.5 %collective-permute-start.15 = (bf16[256,256]{1,0:T(8,128)(2,1)S(1)}, bf16[256,256]{1,0:T(8,128)(2,1)S(1)}, u32[]{:S(2)}, u32[]{:S(2)}) collective-permute-start(bf16[256,256]{1,0:T(8,128)(2,1)S(1)} %get-tuple-element.52), channel_id=1, source_target_pairs={{24,0},{28,4},{16,8},{20,12},{8,16},{12,20},{0,24},{4,28},{25,1},{... | collective-permute-start | bytes 393224 | tf_op jit(solution)/shard_map/ppermute | solution.py:458
  60.9 0.4 collective-permute-start.16
  61.3 2.1 %collective-permute-start.17 = (bf16[256,256]{1,0:T(8,128)(2,1)S(1)}, bf16[256,256]{1,0:T(8,128)(2,1)S(1)}, u32[]{:S(2)}, u32[]{:S(2)}) collective-permute-start(bf16[256,256]{1,0:T(8,128)(2,1)S(1)} %get-tuple-element.55), channel_id=1, source_target_pairs={{20,0},{8,4},{28,8},{0,12},{4,16},{24,20},{12,24},{16,28},{21,1},{... | collective-permute-start | bytes 393224 | tf_op jit(solution)/shard_map/ppermute | solution.py:458
  63.4 1.9 %collective-permute-done.14.rest_4_ = bf16[256,256]{1,0:T(8,128)(2,1)S(1)} collective-permute-done((bf16[256,256]{1,0:T(8,128)(2,1)S(1)}, bf16[256,256]{1,0:T(8,128)(2,1)S(1)}, u32[]{:S(2)}, u32[]{:S(2)}) %collective-permute-start.14) | collective-permute-done | bytes 131104 | tf_op jit(solution)/shard_map/ppermute | solution.py:458
  65.5 2.6 %collective-permute-done.15.rest_5_ = bf16[256,256]{1,0:T(8,128)(2,1)S(1)} collective-permute-done((bf16[256,256]{1,0:T(8,128)(2,1)S(1)}, bf16[256,256]{1,0:T(8,128)(2,1)S(1)}, u32[]{:S(2)}, u32[]{:S(2)}) %collective-permute-start.15) | collective-permute-done | bytes 131104 | tf_op jit(solution)/shard_map/ppermute | solution.py:458
  68.1 0.4 collective-permute-start.20
  68.6 1.3 %base.1.base_ref = f32[2048,256]{1,0:T(8,128)S(1)} custom-call(f32[1,256]{1,0:T(1,128)S(1)} %bitcast.2, f32[2048,256]{1,0:T(8,128)S(1)} %get-tuple-element.42.y_ref, bf16[2048,1024]{1,0:T(8,128)(2,1)S(1)} %get-tuple-element.43.onehot, f32[1,2048]{1,0:T(1,128)S(1)} %get-tuple-element.44.refs_8_.rest_0_, f32[1,2048]{1,0:T(1,128)S(1)} %collective-permute-done.7.refs_9_.rest_1_, ...), custom_call_target="tpu_custom_call" | custom-call | flops 1073741824 | bytes 4194304 | tf_op jit(solution)/shard_map/base/pallas_call | solution.py:409
  69.9 0.9 %collective-permute-done.17.rest_0_ = bf16[256,256]{1,0:T(8,128)(2,1)S(1)} collective-permute-done((bf16[256,256]{1,0:T(8,128)(2,1)S(1)}, bf16[256,256]{1,0:T(8,128)(2,1)S(1)}, u32[]{:S(2)}, u32[]{:S(2)}) %collective-permute-start.17) | collective-permute-done | bytes 131104 | tf_op jit(solution)/shard_map/ppermute | solution.py:458
  71.0 2.1 %collective-permute-done.20.rest_3_ = bf16[256,256]{1,0:T(8,128)(2,1)S(1)} collective-permute-done((bf16[256,256]{1,0:T(8,128)(2,1)S(1)}, bf16[256,256]{1,0:T(8,128)(2,1)S(1)}, u32[]{:S(2)}, u32[]{:S(2)}) %collective-permute-start.20) | collective-permute-done | bytes 131104 | tf_op jit(solution)/shard_map/ppermute | solution.py:458
  73.1 2.1 %mix.1 = bf16[2048,256]{1,0:T(8,128)(2,1)} custom-call(f32[2048,256]{1,0:T(8,128)S(1)} %base.1.base_ref, bf16[2048,1024]{1,0:T(8,128)(2,1)S(1)} %get-tuple-element.50.refs_12_.onehot, bf16[256,256]{1,0:T(8,128)(2,1)S(1)} %collective-permute-done.17.rest_0_, bf16[256,256]{1,0:T(8,128)(2,1)S(1)} %collective-permute-done.18.rest_1_, ...), custom_call_target="tpu_custom_call" | custom-call | flops 1073741824 | bytes 4194304 | tf_op jit(solution)/shard_map/mix/pallas_call | solution.py:437
  (44 shorter events, 1.1 us)
Async XLA Ops:
  0.0 0.7 copy-start.8
  0.7 1.5 %copy-start.1 = (bf16[2048,256]{1,0:T(8,128)(2,1)S(1)}, bf16[2048,256]{1,0:T(8,128)(2,1)}, u32[]{:S(2)}) copy-start(bf16[2048,256]{1,0:T(8,128)(2,1)} %k_ref.5) | copy-start | bytes 3145732
  0.7 1.5 %copy-start.2 = (bf16[2048,256]{1,0:T(8,128)(2,1)S(1)}, bf16[2048,256]{1,0:T(8,128)(2,1)}, u32[]{:S(2)}) copy-start(bf16[2048,256]{1,0:T(8,128)(2,1)} %v_ref.5) | copy-start | bytes 3145732
  0.7 1.5 %copy-start.4 = (bf16[1,256,256]{2,1,0:T(8,128)(2,1)S(1)}, bf16[1,256,256]{2,1,0:T(8,128)(2,1)}, u32[]{:S(2)}) copy-start(bf16[1,256,256]{2,1,0:T(8,128)(2,1)} %one_ref.3) | copy-start | bytes 393220
  0.7 1.6 %copy-start.5 = (bf16[1,256,256]{2,1,0:T(8,128)(2,1)S(1)}, bf16[1,256,256]{2,1,0:T(8,128)(2,1)}, u32[]{:S(2)}) copy-start(bf16[1,256,256]{2,1,0:T(8,128)(2,1)} %three_ref.3) | copy-start | bytes 393220
  0.7 1.6 %copy-start.6 = (bf16[1,256,256]{2,1,0:T(8,128)(2,1)S(1)}, bf16[1,256,256]{2,1,0:T(8,128)(2,1)}, u32[]{:S(2)}) copy-start(bf16[1,256,256]{2,1,0:T(8,128)(2,1)} %two_ref.3) | copy-start | bytes 393220
  0.7 1.6 %copy-start.7 = (f32[2048,1]{0,1:T(1,128)S(1)}, f32[2048,1]{0,1:T(1,128)}, u32[]{:S(2)}) copy-start(f32[2048,1]{0,1:T(1,128)} %param.12) | copy-start | bytes 24580
  2.1 3.6 %copy-start.3 = (bf16[2048,256]{1,0:T(8,128)(2,1)S(1)}, bf16[2048,256]{1,0:T(8,128)(2,1)}, u32[]{:S(2)}) copy-start(bf16[2048,256]{1,0:T(8,128)(2,1)} %q_ref.5) | copy-start | bytes 3145732
  5.2 6.0 %collective-permute-start = (f32[384,256]{1,0:T(8,128)S(1)}, f32[384,256]{1,0:T(8,128)S(1)}, u32[]{:S(2)}, u32[]{:S(2)}) collective-permute-start(f32[384,256]{1,0:T(8,128)S(1)} %get-tuple-element.34), channel_id=1, source_target_pairs={{0,4},{4,0},{8,12},{12,8},{16,20},{20,16},{24,28},{28,24},{1,5},{5... | collective-permute-start | bytes 1179656 | tf_op jit(solution)/shard_map/ppermute | solution.py:269
  7.5 26.9 %collective-permute-start.3 = (bf16[256,768]{1,0:T(8,128)(2,1)S(1)}, bf16[256,768]{1,0:T(8,128)(2,1)S(1)}, u32[]{:S(2)}, u32[]{:S(2)}) collective-permute-start(bf16[256,768]{1,0:T(8,128)(2,1)S(1)} %get-tuple-element.39), channel_id=1, source_target_pairs={{0,28},{4,24},{8,20},{12,16},{16,12},{20,8},{24,4},{28,0},{1,29},{... | collective-permute-start | bytes 1179656 | tf_op jit(solution)/shard_map/ppermute | solution.py:453
  11.2 23.3 %collective-permute-start.4 = (bf16[256,768]{1,0:T(8,128)(2,1)S(1)}, bf16[256,768]{1,0:T(8,128)(2,1)S(1)}, u32[]{:S(2)}, u32[]{:S(2)}) collective-permute-start(bf16[256,768]{1,0:T(8,128)(2,1)S(1)} %get-tuple-element.40), channel_id=1, source_target_pairs={{0,24},{4,28},{8,16},{12,20},{16,8},{20,12},{24,0},{28,4},{1,25},{... | collective-permute-start | bytes 1179656 | tf_op jit(solution)/shard_map/ppermute | solution.py:453
  11.3 23.0 %collective-permute-start.1 = (bf16[384,256]{1,0:T(8,128)(2,1)S(1)}, bf16[384,256]{1,0:T(8,128)(2,1)S(1)}, u32[]{:S(2)}, u32[]{:S(2)}) collective-permute-start(bf16[384,256]{1,0:T(8,128)(2,1)S(1)} %convert_element_type.6), channel_id=1, source_target_pairs={{0,8},{4,20},{8,0},{12,28},{16,24},{20,4},{24,16},{28,12},{1,9},{5... | collective-permute-start | bytes 589832 | tf_op jit(solution)/shard_map/ppermute | solution.py:276
  18.4 36.8 %copy-start.9 = (s32[1,2048]{1,0:T(1,128)S(1)}, s32[1,2048]{1,0:T(1,128)}, u32[]{:S(2)}) copy-start(s32[1,2048]{1,0:T(1,128)} %order_ref.3) | copy-start | bytes 24580
  18.4 17.4 %collective-permute-start.5 = (bf16[256,768]{1,0:T(8,128)(2,1)S(1)}, bf16[256,768]{1,0:T(8,128)(2,1)S(1)}, u32[]{:S(2)}, u32[]{:S(2)}) collective-permute-start(bf16[256,768]{1,0:T(8,128)(2,1)S(1)} %get-tuple-element.41), channel_id=1, source_target_pairs={{0,20},{4,8},{8,28},{12,0},{16,4},{20,24},{24,12},{28,16},{1,21},{... | collective-permute-start | bytes 1179656 | tf_op jit(solution)/shard_map/ppermute | solution.py:453
  34.4 5.7 %collective-permute-start.2 = (bf16[384,256]{1,0:T(8,128)(2,1)S(1)}, bf16[384,256]{1,0:T(8,128)(2,1)S(1)}, u32[]{:S(2)}, u32[]{:S(2)}) collective-permute-start(bf16[384,256]{1,0:T(8,128)(2,1)S(1)} %convert_element_type.7), channel_id=1, source_target_pairs={{0,16},{4,12},{8,24},{12,4},{16,0},{20,28},{24,8},{28,20},{1,17},{... | collective-permute-start | bytes 589832 | tf_op jit(solution)/shard_map/ppermute | solution.py:276
  40.2 3.5 %collective-permute-start.6 = (f32[384,256]{1,0:T(8,128)S(1)}, f32[384,256]{1,0:T(8,128)S(1)}, u32[]{:S(2)}, u32[]{:S(2)}) collective-permute-start(f32[384,256]{1,0:T(8,128)S(1)} %merge.5.rest_0_), channel_id=1, source_target_pairs={{0,4},{4,0},{8,12},{12,8},{16,20},{20,16},{24,28},{28,24},{1,5},{5... | collective-permute-start | bytes 1179656 | tf_op jit(solution)/shard_map/ppermute | solution.py:281
  40.2 7.7 %collective-permute-start.10 = (bf16[256,768]{1,0:T(8,128)(2,1)S(1)}, bf16[256,768]{1,0:T(8,128)(2,1)S(1)}, u32[]{:S(2)}, u32[]{:S(2)}) collective-permute-start(bf16[256,768]{1,0:T(8,128)(2,1)S(1)} %get-tuple-element.46), channel_id=1, source_target_pairs={{0,4},{4,0},{8,12},{12,8},{16,20},{20,16},{24,28},{28,24},{1,5},{5... | collective-permute-start | bytes 1179656 | tf_op jit(solution)/shard_map/ppermute | solution.py:453
  40.7 10.9 %collective-permute-start.11 = (bf16[256,768]{1,0:T(8,128)(2,1)S(1)}, bf16[256,768]{1,0:T(8,128)(2,1)S(1)}, u32[]{:S(2)}, u32[]{:S(2)}) collective-permute-start(bf16[256,768]{1,0:T(8,128)(2,1)S(1)} %get-tuple-element.47), channel_id=1, source_target_pairs={{0,8},{4,20},{8,0},{12,28},{16,24},{20,4},{24,16},{28,12},{1,9},{5... | collective-permute-start | bytes 1179656 | tf_op jit(solution)/shard_map/ppermute | solution.py:453
  42.2 14.6 %collective-permute-start.12 = (bf16[256,768]{1,0:T(8,128)(2,1)S(1)}, bf16[256,768]{1,0:T(8,128)(2,1)S(1)}, u32[]{:S(2)}, u32[]{:S(2)}) collective-permute-start(bf16[256,768]{1,0:T(8,128)(2,1)S(1)} %get-tuple-element.48), channel_id=1, source_target_pairs={{0,12},{4,16},{8,4},{12,24},{16,28},{20,0},{24,20},{28,8},{1,13},{... | collective-permute-start | bytes 1179656 | tf_op jit(solution)/shard_map/ppermute | solution.py:453
  42.2 14.6 %collective-permute-start.13 = (bf16[256,768]{1,0:T(8,128)(2,1)S(1)}, bf16[256,768]{1,0:T(8,128)(2,1)S(1)}, u32[]{:S(2)}, u32[]{:S(2)}) collective-permute-start(bf16[256,768]{1,0:T(8,128)(2,1)S(1)} %get-tuple-element.49), channel_id=1, source_target_pairs={{0,16},{4,12},{8,24},{12,4},{16,0},{20,28},{24,8},{28,20},{1,17},{... | collective-permute-start | bytes 1179656 | tf_op jit(solution)/shard_map/ppermute | solution.py:453
  46.3 22.2 %copy-start = (f32[256]{0:T(256)S(1)}, f32[256]{0:T(256)}, u32[]{:S(2)}) copy-start(f32[256]{0:T(256)} %param.16) | copy-start | bytes 3076
  46.3 10.5 %collective-permute-start.7 = (f32[1,2048]{1,0:T(1,128)S(1)}, f32[1,2048]{1,0:T(1,128)S(1)}, u32[]{:S(2)}, u32[]{:S(2)}) collective-permute-start(f32[1,2048]{1,0:T(1,128)S(1)} %get-tuple-element.44.refs_8_.rest_0_), channel_id=1, source_target_pairs={{0,1},{1,2},{2,3},{3,0},{4,5},{5,6},{6,7},{7,4},{8,9},{9,10},{10,1... | collective-permute-start | bytes 24584 | tf_op jit(solution)/shard_map/ppermute | solution.py:481
  47.9 9.0 %collective-permute-start.8 = (f32[1,2048]{1,0:T(1,128)S(1)}, f32[1,2048]{1,0:T(1,128)S(1)}, u32[]{:S(2)}, u32[]{:S(2)}) collective-permute-start(f32[1,2048]{1,0:T(1,128)S(1)} %get-tuple-element.44.refs_8_.rest_0_), channel_id=1, source_target_pairs={{0,2},{1,3},{2,0},{3,1},{4,6},{5,7},{6,4},{7,5},{8,10},{9,11},{10,... | collective-permute-start | bytes 24584 | tf_op jit(solution)/shard_map/ppermute | solution.py:481
  51.7 5.2 %collective-permute-start.9 = (f32[1,2048]{1,0:T(1,128)S(1)}, f32[1,2048]{1,0:T(1,128)S(1)}, u32[]{:S(2)}, u32[]{:S(2)}) collective-permute-start(f32[1,2048]{1,0:T(1,128)S(1)} %get-tuple-element.44.refs_8_.rest_0_), channel_id=1, source_target_pairs={{0,3},{1,0},{2,1},{3,2},{4,7},{5,4},{6,5},{7,6},{8,11},{9,8},{10,9... | collective-permute-start | bytes 24584 | tf_op jit(solution)/shard_map/ppermute | solution.py:481
  58.5 6.8 %collective-permute-start.14 = (bf16[256,256]{1,0:T(8,128)(2,1)S(1)}, bf16[256,256]{1,0:T(8,128)(2,1)S(1)}, u32[]{:S(2)}, u32[]{:S(2)}) collective-permute-start(bf16[256,256]{1,0:T(8,128)(2,1)S(1)} %get-tuple-element.51), channel_id=1, source_target_pairs={{28,0},{24,4},{20,8},{16,12},{12,16},{8,20},{4,24},{0,28},{29,1},{... | collective-permute-start | bytes 393224 | tf_op jit(solution)/shard_map/ppermute | solution.py:458
  59.4 8.7 %collective-permute-start.15 = (bf16[256,256]{1,0:T(8,128)(2,1)S(1)}, bf16[256,256]{1,0:T(8,128)(2,1)S(1)}, u32[]{:S(2)}, u32[]{:S(2)}) collective-permute-start(bf16[256,256]{1,0:T(8,128)(2,1)S(1)} %get-tuple-element.52), channel_id=1, source_target_pairs={{24,0},{28,4},{16,8},{20,12},{8,16},{12,20},{0,24},{4,28},{25,1},{... | collective-permute-start | bytes 393224 | tf_op jit(solution)/shard_map/ppermute | solution.py:458
  60.9 7.7 %collective-permute-start.16 = (bf16[256,256]{1,0:T(8,128)(2,1)S(1)}, bf16[256,256]{1,0:T(8,128)(2,1)S(1)}, u32[]{:S(2)}, u32[]{:S(2)}) collective-permute-start(bf16[256,256]{1,0:T(8,128)(2,1)S(1)} %get-tuple-element.53), channel_id=1, source_target_pairs={{4,0},{0,4},{12,8},{8,12},{20,16},{16,20},{28,24},{24,28},{5,1},{1... | collective-permute-start | bytes 393224 | tf_op jit(solution)/shard_map/ppermute | solution.py:458
  61.3 9.5 %collective-permute-start.17 = (bf16[256,256]{1,0:T(8,128)(2,1)S(1)}, bf16[256,256]{1,0:T(8,128)(2,1)S(1)}, u32[]{:S(2)}, u32[]{:S(2)}) collective-permute-start(bf16[256,256]{1,0:T(8,128)(2,1)S(1)} %get-tuple-element.55), channel_id=1, source_target_pairs={{20,0},{8,4},{28,8},{0,12},{4,16},{24,20},{12,24},{16,28},{21,1},{... | collective-permute-start | bytes 393224 | tf_op jit(solution)/shard_map/ppermute | solution.py:458
  63.4 7.6 %collective-permute-start.18 = (bf16[256,256]{1,0:T(8,128)(2,1)S(1)}, bf16[256,256]{1,0:T(8,128)(2,1)S(1)}, u32[]{:S(2)}, u32[]{:S(2)}) collective-permute-start(bf16[256,256]{1,0:T(8,128)(2,1)S(1)} %get-tuple-element.56), channel_id=1, source_target_pairs={{16,0},{12,4},{24,8},{4,12},{0,16},{28,20},{8,24},{20,28},{17,1},{... | collective-permute-start | bytes 393224 | tf_op jit(solution)/shard_map/ppermute | solution.py:458
  65.3 5.7 %collective-permute-start.19 = (bf16[256,256]{1,0:T(8,128)(2,1)S(1)}, bf16[256,256]{1,0:T(8,128)(2,1)S(1)}, u32[]{:S(2)}, u32[]{:S(2)}) collective-permute-start(bf16[256,256]{1,0:T(8,128)(2,1)S(1)} %get-tuple-element.57), channel_id=1, source_target_pairs={{12,0},{16,4},{4,8},{24,12},{28,16},{0,20},{20,24},{8,28},{13,1},{... | collective-permute-start | bytes 393224 | tf_op jit(solution)/shard_map/ppermute | solution.py:458
  68.1 5.0 %collective-permute-start.20 = (bf16[256,256]{1,0:T(8,128)(2,1)S(1)}, bf16[256,256]{1,0:T(8,128)(2,1)S(1)}, u32[]{:S(2)}, u32[]{:S(2)}) collective-permute-start(bf16[256,256]{1,0:T(8,128)(2,1)S(1)} %get-tuple-element.58), channel_id=1, source_target_pairs={{8,0},{20,4},{0,8},{28,12},{24,16},{4,20},{16,24},{12,28},{9,1},{2... | collective-permute-start | bytes 393224 | tf_op jit(solution)/shard_map/ppermute | solution.py:458

commit v5 on v4

--- a/solution.py
+++ b/solution.py
@@ -116,8 +116,8 @@
     )(order)
 
 
-def sort_kernel(onehot, q_ref, k_ref, v_ref, *rest):
-    outs, token = rest[:-1], rest[-1]
+def sort_kernel(size, onehot, q_ref, k_ref, v_ref, *rest):
+    outs, token = rest[-1 - size : -1], rest[-1]
     token[...] = jnp.zeros_like(token)
     rows, width = outs[0].shape[0], q_ref.shape[1]
     group = max(1, min(len(outs), TILE // rows))
@@ -133,19 +133,19 @@
                 ]
 
 
-def sort_tokens(onehot, q, k, v, n):
+def sort_tokens(onehot, q, k, v, after, n):
     count, width = q.shape
     rows = count // n
     size = onehot.shape[0] // rows
     return pl.pallas_call(
-        sort_kernel,
+        functools.partial(sort_kernel, size),
         out_shape=[jax.ShapeDtypeStruct((rows, 3 * width), BF16)] * size + [TOKEN],
-        in_specs=full(4),
+        in_specs=full(4) + [pl.BlockSpec(memory_space=pl.ANY)] * len(after),
         out_specs=full(size + 1),
         compiler_params=params(),
         cost_estimate=cost(6 * size * rows * count * width, 6 * count * width),
         name="sort_tokens",
-    )(onehot, q, k, v)
+    )(onehot, q, k, v, *after)
 
 
 def attend_kernel(n, scale, *refs):
@@ -260,25 +260,28 @@
     )(keep, got, *after)
 
 
-def sum_over_cams(parts, after, n):
+def core_step(parts, after, n):
     if len(parts) == 1:
-        return [lax.psum(parts[0], "cam")]
-    keep, send = parts
-    bits = n.bit_length() - 1
+        return parts[0]
     pair = [(at, at ^ 1) for at in range(n)]
-    mine = merge(keep, lax.ppermute(send, "cam", pair), after[0])
-    span = bits - 1
+    return merge(parts[0], lax.ppermute(parts[1], "cam", pair), after)
+
+
+def sum_over_chips(mine, split, after, n):
+    if not split:
+        return [lax.psum(mine, "cam")]
+    span = n.bit_length() - 2
     for step in range(span):
         pairs = []
         for at in range(n):
             bit = 1 + (step + (at & 1)) % span
             pairs.append((at, at ^ (1 << bit)))
         got = lax.ppermute(mine.astype(BF16), "cam", pairs)
-        if step + 1 < len(after):
-            mine = merge(mine, got, after[step + 1])
+        if step < len(after):
+            mine = merge(mine, got, after[step])
         else:
             mine = mine + got.astype(F32)
-    return [mine, lax.ppermute(mine, "cam", pair)]
+    return [mine, lax.ppermute(mine, "cam", [(at, at ^ 1) for at in range(n)])]
 
 
 def readout_kernel(parts, q_ref, one_ref, three_ref, two_ref, *rest):
@@ -468,25 +471,24 @@
     groups = (tuple(steps[:few]), tuple(steps[few:]))
     marks = mark(order, n, groups)
     parts = gradients(keys, values, rates.reshape(1, count), *weights, marks[-1], n)
+    early = steps[:few] + steps[n - few :]
+    late = steps[few : n - few]
+    early_places, late_places = place(order, n, early + late)
+    mine = core_step(parts, [late_places], n)
     arrived = {}
-    after = []
-    for group, onehot in zip(groups, marks):
-        blocks = sort_tokens(onehot, queries, keys, values, n)
-        after.append(blocks[-1])
+    tokens = []
+    for group, onehot, after in zip(groups, marks, ([mine], [])):
+        blocks = sort_tokens(onehot, queries, keys, values, after + tokens, n)
+        tokens.append(blocks[-1])
         for step, block in zip(group, blocks):
             arrived[step] = exchange(block, step, n)
-    summed = sum_over_cams(parts, [after[:1], after[1:], [arrived[step] for step in steps[:few+1]]], n)
+    summed = sum_over_chips(mine, len(parts) == 2, [tokens[1:] + [arrived[steps[0]], arrived[steps[1]]], [arrived[step] for step in steps[: 2 * few + 1]]], n)
     y, square = read_out(queries, *weights, summed)
     squares = [square] + [
         lax.ppermute(square, "head", [(at, (at + step) % heads) for at in range(heads)])
         for step in range(1, heads)
     ]
-    early = steps[:few] + steps[n - few :]
-    late = steps[few : n - few]
-    early_places, late_places = place(order, n, early + late)
-    attended = attend(
-        [arrived[step] for step in range(n)], squares + [late_places], n, width
-    )
+    attended = attend([arrived[step] for step in range(n)], [square], n, width)
     returned = {step: give_back(attended[step], step, n) for step in early + late}
     given = base(
         gain.reshape(1, width), y, early_places, squares, [returned[step] for step in early]

time: 75.6 us -> 80.6 us (1.066)
  waiting for transfers between devices: 30.4 us -> 38.8 us
  starting transfers between devices: 23 us -> 19.2 us
    ppermute x7, waiting for transfers between devices: 2.44 us -> 26.2 us  [exchange(): return lax.ppermute(block, 'cam', routes(step, n)) if step else block]
    ppermute x4, waiting for transfers between devices: 20.1 us -> 2.47 us  [the longest x2 2.11 us: sum_over_chips(): got = lax.ppermute(mine.astype(BF16), 'cam', pairs)]
    ppermute x3, waiting for transfers between devices: 0.01 us -> 6.8 us  [per_device(): lax.ppermute(square, 'head', [(at, (at + step) % heads) for at in range(h...]
    ppermute x7, waiting for transfers between devices: 7.79 us -> 3.28 us  [give_back(): return lax.ppermute(block, 'cam', pairs) if step else block]
    ppermute x3, starting transfers between devices: 7.69 us -> 3.86 us  [per_device(): lax.ppermute(square, 'head', [(at, (at + step) % heads) for at in range(h...]
  transfers between devices with their start and end apart: 21 -> 21, of which waited for: 10 -> 13; matrix products, arithmetic and copies ran while one was open for 0% -> 0% of each run, Pallas kernels for 17% -> 16%
where the time goes in v5:
time: 80.6 us; the launch traced here: 79.9 us
  waiting for transfers between devices  38.8 us (48%)
  Pallas kernels  20.7 us (26%)
  starting transfers between devices  19.2 us (24%)
  local copies, waits for them, and re-layouts  0.88 us (1%)
    ppermute x7, waiting for transfers between devices, exchange(): return lax.ppermute(block, 'cam', routes(step, n)) if step else block  26.2 us
    ppermute x7, starting transfers between devices, exchange(): return lax.ppermute(block, 'cam', routes(step, n)) if step else block  7.18 us
    pallas_call x2, Pallas kernels, sort_tokens(): pl.pallas_call(functools.partial(sort_kernel, size), out_shape=[jax.Shape...  6.93 us
    ppermute x3, waiting for transfers between devices, per_device(): lax.ppermute(square, 'head', [(at, (at + step) % heads) for at in range(h...  6.8 us
    ppermute x7, starting transfers between devices, give_back(): return lax.ppermute(block, 'cam', pairs) if step else block  4.94 us
    ppermute x3, starting transfers between devices, per_device(): lax.ppermute(square, 'head', [(at, (at + step) % heads) for at in range(h...  3.86 us
    ppermute x7, waiting for transfers between devices, give_back(): return lax.ppermute(block, 'cam', pairs) if step else block  3.28 us
    pallas_call x1, Pallas kernels, gradients(): pl.pallas_call(functools.partial(grads_kernel, n, split), out_shape=[jax....  2.9 us
  transfers between devices with their start and end apart: 21, of which 13 were waited for; matrix products, arithmetic and copies ran while one was open for 0% of the time, Pallas kernels for 16%

profile of v5, /device:TPU:0, one launch (start us, length us, event | category | flops | bytes accessed | tf_op | source)
XLA Modules:
  0.0 79.9 jit_solution(11416288176544178339)
XLA Ops:
  0.0 0.7 copy-done.8
  0.7 1.4 %mark.1 = (bf16[512,2048]{1,0:T(8,128)(2,1)S(1)}, bf16[1536,2048]{1,0:T(8,128)(2,1)S(1)}, f32[8,128]{1,0:T(8,128)S(1)}) custom-call(s32[1,2048]{1,0:T(1,128)S(1)} %copy-done.8), custom_call_target="tpu_custom_call" | custom-call | flops 999999995904 | bytes 1024 | tf_op jit(solution)/shard_map/mark/pallas_call | solution.py:107
  2.3 2.9 %gradients.1 = (f32[384,256]{1,0:T(8,128)S(1)}, f32[384,256]{1,0:T(8,128)S(1)}) custom-call(bf16[2048,256]{1,0:T(8,128)(2,1)S(1)} %copy-done.1, bf16[2048,256]{1,0:T(8,128)(2,1)S(1)} %copy-done.2, f32[1,2048]{1,0:T(1,128)S(1)} %bitcast.3, bf16[1,256,256]{2,1,0:T(8,128)(2,1)S(1)} %copy-done.4, bf16[1,256,256]{2,1,0:T(8,128)(2,1)S(1)} %copy-done.5, ...), custom_call_target="tpu_custom_call" | custom-call | flops 1610612736 | bytes 4194304 | tf_op jit(solution)/shard_map/gradients/pallas_call | solution.py:235
  5.8 1.7 %place.1 = (bf16[2048,1024]{1,0:T(8,128)(2,1)S(1)}, bf16[2048,1024]{1,0:T(8,128)(2,1)S(1)}) custom-call(s32[1,2048]{1,0:T(1,128)S(1)} %copy-done.9), custom_call_target="tpu_custom_call" | custom-call | flops 4194304 | bytes 8388608 | tf_op jit(solution)/shard_map/place/pallas_call | solution.py:370
  7.5 2.6 %collective-permute-start.1 = (bf16[384,256]{1,0:T(8,128)(2,1)S(1)}, bf16[384,256]{1,0:T(8,128)(2,1)S(1)}, u32[]{:S(2)}, u32[]{:S(2)}) collective-permute-start(bf16[384,256]{1,0:T(8,128)(2,1)S(1)} %convert_element_type.6), channel_id=1, source_target_pairs={{0,8},{4,20},{8,0},{12,28},{16,24},{20,4},{24,16},{28,12},{1,9},{5... | collective-permute-start | bytes 589832 | tf_op jit(solution)/shard_map/ppermute | solution.py:279
  10.1 1.8 %sort_tokens.2 = (bf16[256,768]{1,0:T(8,128)(2,1)S(1)}, bf16[256,768]{1,0:T(8,128)(2,1)S(1)}, f32[8,128]{1,0:T(8,128)S(1)}) custom-call(bf16[512,2048]{1,0:T(8,128)(2,1)S(1)} %get-tuple-element.37.onehot, bf16[2048,256]{1,0:T(8,128)(2,1)S(1)} %copy-done.3, bf16[2048,256]{1,0:T(8,128)(2,1)S(1)} %copy-done.1, bf16[2048,256]{1,0:T(8,128)(2,1)S(1)} %copy-done.2, ...), custom_call_target="tpu_custom_call" | custom-call | flops 1610612736 | bytes 3145728 | tf_op jit(solution)/shard_map/sort_tokens/pallas_call | solution.py:140
  11.9 1.3 %collective-permute-start.2 = (bf16[256,768]{1,0:T(8,128)(2,1)S(1)}, bf16[256,768]{1,0:T(8,128)(2,1)S(1)}, u32[]{:S(2)}, u32[]{:S(2)}) collective-permute-start(bf16[256,768]{1,0:T(8,128)(2,1)S(1)} %get-tuple-element.40), channel_id=1, source_target_pairs={{0,28},{4,24},{8,20},{12,16},{16,12},{20,8},{24,4},{28,0},{1,29},{... | collective-permute-start | bytes 1179656 | tf_op jit(solution)/shard_map/ppermute | solution.py:456
  13.3 1.5 %collective-permute-start.3 = (bf16[256,768]{1,0:T(8,128)(2,1)S(1)}, bf16[256,768]{1,0:T(8,128)(2,1)S(1)}, u32[]{:S(2)}, u32[]{:S(2)}) collective-permute-start(bf16[256,768]{1,0:T(8,128)(2,1)S(1)} %get-tuple-element.41), channel_id=1, source_target_pairs={{0,24},{4,28},{8,16},{12,20},{16,8},{20,12},{24,0},{28,4},{1,25},{... | collective-permute-start | bytes 1179656 | tf_op jit(solution)/shard_map/ppermute | solution.py:456
  14.8 5.1 %sort_tokens.3 = (bf16[256,768]{1,0:T(8,128)(2,1)S(1)}, bf16[256,768]{1,0:T(8,128)(2,1)S(1)}, bf16[256,768]{1,0:T(8,128)(2,1)S(1)}, bf16[256,768]{1,0:T(8,128)(2...) custom-call(bf16[1536,2048]{1,0:T(8,128)(2,1)S(1)} %get-tuple-element.36.onehot, ...), custom_call_target="tpu_custom_call" | custom-call | flops 4831838208 | bytes 3145728 | tf_op jit(solution)/shard_map/sort_tokens/pallas_call | solution.py:140
  19.9 1.2 %collective-permute-start.5 = (bf16[256,768]{1,0:T(8,128)(2,1)S(1)}, bf16[256,768]{1,0:T(8,128)(2,1)S(1)}, u32[]{:S(2)}, u32[]{:S(2)}) collective-permute-start(bf16[256,768]{1,0:T(8,128)(2,1)S(1)} %get-tuple-element.42), channel_id=1, source_target_pairs={{0,20},{4,8},{8,28},{12,0},{16,4},{20,24},{24,12},{28,16},{1,21},{... | collective-permute-start | bytes 1179656 | tf_op jit(solution)/shard_map/ppermute | solution.py:456
  21.6 1.3 %collective-permute-start.7 = (bf16[256,768]{1,0:T(8,128)(2,1)S(1)}, bf16[256,768]{1,0:T(8,128)(2,1)S(1)}, u32[]{:S(2)}, u32[]{:S(2)}) collective-permute-start(bf16[256,768]{1,0:T(8,128)(2,1)S(1)} %get-tuple-element.44), channel_id=1, source_target_pairs={{0,12},{4,16},{8,4},{12,24},{16,28},{20,0},{24,20},{28,8},{1,13},{... | collective-permute-start | bytes 1179656 | tf_op jit(solution)/shard_map/ppermute | solution.py:456
  22.9 1.2 %collective-permute-done.2.rest_1_.rest_0_.refs_7_ = bf16[256,768]{1,0:T(8,128)(2,1)S(1)} collective-permute-done((bf16[256,768]{1,0:T(8,128)(2,1)S(1)}, bf16[256,768]{1,0:T(8,128)(2,1)S(1)}, u32[]{:S(2)}, u32[]{:S(2)}) %collective-permute-start.2) | collective-permute-done | bytes 393248 | tf_op jit(solution)/shard_map/ppermute | solution.py:456
  24.1 9.0 %collective-permute-done.3.rest_2_.rest_1_.refs_6_ = bf16[256,768]{1,0:T(8,128)(2,1)S(1)} collective-permute-done((bf16[256,768]{1,0:T(8,128)(2,1)S(1)}, bf16[256,768]{1,0:T(8,128)(2,1)S(1)}, u32[]{:S(2)}, u32[]{:S(2)}) %collective-permute-start.3) | collective-permute-done | bytes 393248 | tf_op jit(solution)/shard_map/ppermute | solution.py:456
  33.3 7.2 %collective-permute-done.5.rest_2_.refs_5_ = bf16[256,768]{1,0:T(8,128)(2,1)S(1)} collective-permute-done((bf16[256,768]{1,0:T(8,128)(2,1)S(1)}, bf16[256,768]{1,0:T(8,128)(2,1)S(1)}, u32[]{:S(2)}, u32[]{:S(2)}) %collective-permute-start.5) | collective-permute-done | bytes 393248 | tf_op jit(solution)/shard_map/ppermute | solution.py:456
  40.5 4.9 %collective-permute-done.6.rest_3_.refs_4_ = bf16[256,768]{1,0:T(8,128)(2,1)S(1)} collective-permute-done((bf16[256,768]{1,0:T(8,128)(2,1)S(1)}, bf16[256,768]{1,0:T(8,128)(2,1)S(1)}, u32[]{:S(2)}, u32[]{:S(2)}) %collective-permute-start.6) | collective-permute-done | bytes 393248 | tf_op jit(solution)/shard_map/ppermute | solution.py:456
  45.4 2.1 %collective-permute-done.4.got_ref = bf16[384,256]{1,0:T(8,128)(2,1)S(1)} collective-permute-done((bf16[384,256]{1,0:T(8,128)(2,1)S(1)}, bf16[384,256]{1,0:T(8,128)(2,1)S(1)}, u32[]{:S(2)}, u32[]{:S(2)}) %collective-permute-start.4) | collective-permute-done | bytes 196640 | tf_op jit(solution)/shard_map/ppermute | solution.py:279
  48.1 0.8 %collective-permute-start.13 = (bf16[256,768]{1,0:T(8,128)(2,1)S(1)}, bf16[256,768]{1,0:T(8,128)(2,1)S(1)}, u32[]{:S(2)}, u32[]{:S(2)}) collective-permute-start(bf16[256,768]{1,0:T(8,128)(2,1)S(1)} %get-tuple-element.50), channel_id=1, source_target_pairs={{0,8},{4,20},{8,0},{12,28},{16,24},{20,4},{24,16},{28,12},{1,9},{5... | collective-permute-start | bytes 1179656 | tf_op jit(solution)/shard_map/ppermute | solution.py:456
  49.3 2.7 %read_out.1 = (f32[2048,256]{1,0:T(8,128)S(1)}, f32[1,2048]{1,0:T(1,128)S(1)}) custom-call(bf16[2048,256]{1,0:T(8,128)(2,1)S(1)} %copy-done.3, bf16[1,256,256]{2,1,0:T(8,128)(2,1)S(1)} %copy-done.4, bf16[1,256,256]{2,1,0:T(8,128)(2,1)S(1)} %copy-done.5, bf16[1,256,256]{2,1,0:T(8,128)(2,1)S(1)} %copy-done.6, f32[384,256]{1,0:T(8,128)S(1)} %merge.5.rest_0_, ...), custom_call_target="tpu_custom_call" | custom-call | flops 805306368 | bytes 4194304 | tf_op jit(solution)/shard_map/read_out/pallas_call | solution.py:331
  52.0 3.9 %collective-permute-done.13.refs_2_ = bf16[256,768]{1,0:T(8,128)(2,1)S(1)} collective-permute-done((bf16[256,768]{1,0:T(8,128)(2,1)S(1)}, bf16[256,768]{1,0:T(8,128)(2,1)S(1)}, u32[]{:S(2)}, u32[]{:S(2)}) %collective-permute-start.13) | collective-permute-done | bytes 393248 | tf_op jit(solution)/shard_map/ppermute | solution.py:456
  55.9 1.5 %attend.1 = (bf16[256,256]{1,0:T(8,128)(2,1)S(1)}, bf16[256,256]{1,0:T(8,128)(2,1)S(1)}, bf16[256,256]{1,0:T(8,128)(2,1)S(1)}, bf16[256,256]{1,0:T(8,128)(2,1)S(...) custom-call(bf16[256,768]{1,0:T(8,128)(2,1)S(1)} %get-tuple-element., ...), custom_call_target="tpu_custom_call" | custom-call | flops 536870912 | bytes 4194304 | tf_op jit(solution)/shard_map/attend/pallas_call | solution.py:179
  57.8 1.4 %collective-permute-start.15 = (bf16[256,256]{1,0:T(8,128)(2,1)S(1)}, bf16[256,256]{1,0:T(8,128)(2,1)S(1)}, u32[]{:S(2)}, u32[]{:S(2)}) collective-permute-start(bf16[256,256]{1,0:T(8,128)(2,1)S(1)} %get-tuple-element.52), channel_id=1, source_target_pairs={{24,0},{28,4},{16,8},{20,12},{8,16},{12,20},{0,24},{4,28},{25,1},{... | collective-permute-start | bytes 393224 | tf_op jit(solution)/shard_map/ppermute | solution.py:461
  59.2 1.0 %collective-permute-start.16 = (bf16[256,256]{1,0:T(8,128)(2,1)S(1)}, bf16[256,256]{1,0:T(8,128)(2,1)S(1)}, u32[]{:S(2)}, u32[]{:S(2)}) collective-permute-start(bf16[256,256]{1,0:T(8,128)(2,1)S(1)} %get-tuple-element.53), channel_id=1, source_target_pairs={{4,0},{0,4},{12,8},{8,12},{20,16},{16,20},{28,24},{24,28},{5,1},{1... | collective-permute-start | bytes 393224 | tf_op jit(solution)/shard_map/ppermute | solution.py:461
  60.3 3.6 %collective-permute-start.11 = (f32[1,2048]{1,0:T(1,128)S(1)}, f32[1,2048]{1,0:T(1,128)S(1)}, u32[]{:S(2)}, u32[]{:S(2)}) collective-permute-start(f32[1,2048]{1,0:T(1,128)S(1)} %get-tuple-element.47.refs_8_.rest_0_), channel_id=1, source_target_pairs={{0,3},{1,0},{2,1},{3,2},{4,7},{5,4},{6,5},{7,6},{8,11},{9,8},{10,9... | collective-permute-start | bytes 24584 | tf_op jit(solution)/shard_map/ppermute | solution.py:488
  63.9 1.4 %collective-permute-done.11.rest_3_ = f32[1,2048]{1,0:T(1,128)S(1)} collective-permute-done((f32[1,2048]{1,0:T(1,128)S(1)}, f32[1,2048]{1,0:T(1,128)S(1)}, u32[]{:S(2)}, u32[]{:S(2)}) %collective-permute-start.11) | collective-permute-done | bytes 8224 | tf_op jit(solution)/shard_map/ppermute | solution.py:488
  65.5 2.9 %collective-permute-done.10.rest_2_ = f32[1,2048]{1,0:T(1,128)S(1)} collective-permute-done((f32[1,2048]{1,0:T(1,128)S(1)}, f32[1,2048]{1,0:T(1,128)S(1)}, u32[]{:S(2)}, u32[]{:S(2)}) %collective-permute-start.10) | collective-permute-done | bytes 8224 | tf_op jit(solution)/shard_map/ppermute | solution.py:488
  68.4 2.5 %collective-permute-done.9.rest_1_ = f32[1,2048]{1,0:T(1,128)S(1)} collective-permute-done((f32[1,2048]{1,0:T(1,128)S(1)}, f32[1,2048]{1,0:T(1,128)S(1)}, u32[]{:S(2)}, u32[]{:S(2)}) %collective-permute-start.9) | collective-permute-done | bytes 8224 | tf_op jit(solution)/shard_map/ppermute | solution.py:488
  70.9 0.9 %collective-permute-start.18 = (bf16[256,256]{1,0:T(8,128)(2,1)S(1)}, bf16[256,256]{1,0:T(8,128)(2,1)S(1)}, u32[]{:S(2)}, u32[]{:S(2)}) collective-permute-start(bf16[256,256]{1,0:T(8,128)(2,1)S(1)} %get-tuple-element.56), channel_id=1, source_target_pairs={{16,0},{12,4},{24,8},{4,12},{0,16},{28,20},{8,24},{20,28},{17,1},{... | collective-permute-start | bytes 393224 | tf_op jit(solution)/shard_map/ppermute | solution.py:461
  71.9 1.2 %collective-permute-start.20 = (bf16[256,256]{1,0:T(8,128)(2,1)S(1)}, bf16[256,256]{1,0:T(8,128)(2,1)S(1)}, u32[]{:S(2)}, u32[]{:S(2)}) collective-permute-start(bf16[256,256]{1,0:T(8,128)(2,1)S(1)} %get-tuple-element.58), channel_id=1, source_target_pairs={{8,0},{20,4},{0,8},{28,12},{24,16},{4,20},{16,24},{12,28},{9,1},{2... | collective-permute-start | bytes 393224 | tf_op jit(solution)/shard_map/ppermute | solution.py:461
  73.1 1.3 %base.1.base_ref = f32[2048,256]{1,0:T(8,128)S(1)} custom-call(f32[1,256]{1,0:T(1,128)S(1)} %bitcast.2, f32[2048,256]{1,0:T(8,128)S(1)} %get-tuple-element.45.y_ref, bf16[2048,1024]{1,0:T(8,128)(2,1)S(1)} %get-tuple-element.46.onehot, f32[1,2048]{1,0:T(1,128)S(1)} %get-tuple-element.47.refs_8_.rest_0_, f32[1,2048]{1,0:T(1,128)S(1)} %collective-permute-done.9.rest_1_, ...), custom_call_target="tpu_custom_call" | custom-call | flops 1073741824 | bytes 4194304 | tf_op jit(solution)/shard_map/base/pallas_call | solution.py:412
  74.4 1.7 %collective-permute-done.18.rest_1_ = bf16[256,256]{1,0:T(8,128)(2,1)S(1)} collective-permute-done((bf16[256,256]{1,0:T(8,128)(2,1)S(1)}, bf16[256,256]{1,0:T(8,128)(2,1)S(1)}, u32[]{:S(2)}, u32[]{:S(2)}) %collective-permute-start.18) | collective-permute-done | bytes 131104 | tf_op jit(solution)/shard_map/ppermute | solution.py:461
  76.1 1.1 %collective-permute-done.19.rest_2_ = bf16[256,256]{1,0:T(8,128)(2,1)S(1)} collective-permute-done((bf16[256,256]{1,0:T(8,128)(2,1)S(1)}, bf16[256,256]{1,0:T(8,128)(2,1)S(1)}, u32[]{:S(2)}, u32[]{:S(2)}) %collective-permute-start.19) | collective-permute-done | bytes 131104 | tf_op jit(solution)/shard_map/ppermute | solution.py:461
  77.7 2.1 %mix.1 = bf16[2048,256]{1,0:T(8,128)(2,1)} custom-call(f32[2048,256]{1,0:T(8,128)S(1)} %base.1.base_ref, bf16[2048,1024]{1,0:T(8,128)(2,1)S(1)} %get-tuple-element.35.rest_0_.onehot, bf16[256,256]{1,0:T(8,128)(2,1)S(1)} %collective-permute-done.17.rest_0_, bf16[256,256]{1,0:T(8,128)(2,1)S(1)} %collective-permute-done.18.rest_1_, ...), custom_call_target="tpu_custom_call" | custom-call | flops 1073741824 | bytes 4194304 | tf_op jit(solution)/shard_map/mix/pallas_call | solution.py:440
  (44 shorter events, 3.6 us)
Async XLA Ops:
  0.0 0.7 copy-start.8
  0.7 1.5 %copy-start.1 = (bf16[2048,256]{1,0:T(8,128)(2,1)S(1)}, bf16[2048,256]{1,0:T(8,128)(2,1)}, u32[]{:S(2)}) copy-start(bf16[2048,256]{1,0:T(8,128)(2,1)} %k_ref.5) | copy-start | bytes 3145732
  0.7 1.5 %copy-start.2 = (bf16[2048,256]{1,0:T(8,128)(2,1)S(1)}, bf16[2048,256]{1,0:T(8,128)(2,1)}, u32[]{:S(2)}) copy-start(bf16[2048,256]{1,0:T(8,128)(2,1)} %v_ref.5) | copy-start | bytes 3145732
  0.7 1.5 %copy-start.4 = (bf16[1,256,256]{2,1,0:T(8,128)(2,1)S(1)}, bf16[1,256,256]{2,1,0:T(8,128)(2,1)}, u32[]{:S(2)}) copy-start(bf16[1,256,256]{2,1,0:T(8,128)(2,1)} %one_ref.3) | copy-start | bytes 393220
  0.7 1.6 %copy-start.5 = (bf16[1,256,256]{2,1,0:T(8,128)(2,1)S(1)}, bf16[1,256,256]{2,1,0:T(8,128)(2,1)}, u32[]{:S(2)}) copy-start(bf16[1,256,256]{2,1,0:T(8,128)(2,1)} %three_ref.3) | copy-start | bytes 393220
  0.7 1.6 %copy-start.6 = (bf16[1,256,256]{2,1,0:T(8,128)(2,1)S(1)}, bf16[1,256,256]{2,1,0:T(8,128)(2,1)}, u32[]{:S(2)}) copy-start(bf16[1,256,256]{2,1,0:T(8,128)(2,1)} %two_ref.3) | copy-start | bytes 393220
  0.7 1.6 %copy-start.7 = (f32[2048,1]{0,1:T(1,128)S(1)}, f32[2048,1]{0,1:T(1,128)}, u32[]{:S(2)}) copy-start(f32[2048,1]{0,1:T(1,128)} %param.12) | copy-start | bytes 24580
  2.1 3.6 %copy-start.9 = (s32[1,2048]{1,0:T(1,128)S(1)}, s32[1,2048]{1,0:T(1,128)}, u32[]{:S(2)}) copy-start(s32[1,2048]{1,0:T(1,128)} %order_ref.3) | copy-start | bytes 24580
  5.2 4.9 %copy-start.3 = (bf16[2048,256]{1,0:T(8,128)(2,1)S(1)}, bf16[2048,256]{1,0:T(8,128)(2,1)}, u32[]{:S(2)}) copy-start(bf16[2048,256]{1,0:T(8,128)(2,1)} %q_ref.5) | copy-start | bytes 3145732
  5.2 2.2 %collective-permute-start = (f32[384,256]{1,0:T(8,128)S(1)}, f32[384,256]{1,0:T(8,128)S(1)}, u32[]{:S(2)}, u32[]{:S(2)}) collective-permute-start(f32[384,256]{1,0:T(8,128)S(1)} %get-tuple-element.34), channel_id=1, source_target_pairs={{0,4},{4,0},{8,12},{12,8},{16,20},{20,16},{24,28},{28,24},{1,5},{5... | collective-permute-start | bytes 1179656 | tf_op jit(solution)/shard_map/ppermute | solution.py:267
  7.5 14.0 %collective-permute-start.1 = (bf16[384,256]{1,0:T(8,128)(2,1)S(1)}, bf16[384,256]{1,0:T(8,128)(2,1)S(1)}, u32[]{:S(2)}, u32[]{:S(2)}) collective-permute-start(bf16[384,256]{1,0:T(8,128)(2,1)S(1)} %convert_element_type.6), channel_id=1, source_target_pairs={{0,8},{4,20},{8,0},{12,28},{16,24},{20,4},{24,16},{28,12},{1,9},{5... | collective-permute-start | bytes 589832 | tf_op jit(solution)/shard_map/ppermute | solution.py:279
  11.9 12.1 %collective-permute-start.2 = (bf16[256,768]{1,0:T(8,128)(2,1)S(1)}, bf16[256,768]{1,0:T(8,128)(2,1)S(1)}, u32[]{:S(2)}, u32[]{:S(2)}) collective-permute-start(bf16[256,768]{1,0:T(8,128)(2,1)S(1)} %get-tuple-element.40), channel_id=1, source_target_pairs={{0,28},{4,24},{8,20},{12,16},{16,12},{20,8},{24,4},{28,0},{1,29},{... | collective-permute-start | bytes 1179656 | tf_op jit(solution)/shard_map/ppermute | solution.py:456
  13.3 19.8 %collective-permute-start.3 = (bf16[256,768]{1,0:T(8,128)(2,1)S(1)}, bf16[256,768]{1,0:T(8,128)(2,1)S(1)}, u32[]{:S(2)}, u32[]{:S(2)}) collective-permute-start(bf16[256,768]{1,0:T(8,128)(2,1)S(1)} %get-tuple-element.41), channel_id=1, source_target_pairs={{0,24},{4,28},{8,16},{12,20},{16,8},{20,12},{24,0},{28,4},{1,25},{... | collective-permute-start | bytes 1179656 | tf_op jit(solution)/shard_map/ppermute | solution.py:456
  19.9 20.6 %collective-permute-start.5 = (bf16[256,768]{1,0:T(8,128)(2,1)S(1)}, bf16[256,768]{1,0:T(8,128)(2,1)S(1)}, u32[]{:S(2)}, u32[]{:S(2)}) collective-permute-start(bf16[256,768]{1,0:T(8,128)(2,1)S(1)} %get-tuple-element.42), channel_id=1, source_target_pairs={{0,20},{4,8},{8,28},{12,0},{16,4},{20,24},{24,12},{28,16},{1,21},{... | collective-permute-start | bytes 1179656 | tf_op jit(solution)/shard_map/ppermute | solution.py:456
  21.1 24.3 %collective-permute-start.6 = (bf16[256,768]{1,0:T(8,128)(2,1)S(1)}, bf16[256,768]{1,0:T(8,128)(2,1)S(1)}, u32[]{:S(2)}, u32[]{:S(2)}) collective-permute-start(bf16[256,768]{1,0:T(8,128)(2,1)S(1)} %get-tuple-element.43), channel_id=1, source_target_pairs={{0,16},{4,12},{8,24},{12,4},{16,0},{20,28},{24,8},{28,20},{1,17},{... | collective-permute-start | bytes 1179656 | tf_op jit(solution)/shard_map/ppermute | solution.py:456
  21.6 23.8 %collective-permute-start.7 = (bf16[256,768]{1,0:T(8,128)(2,1)S(1)}, bf16[256,768]{1,0:T(8,128)(2,1)S(1)}, u32[]{:S(2)}, u32[]{:S(2)}) collective-permute-start(bf16[256,768]{1,0:T(8,128)(2,1)S(1)} %get-tuple-element.44), channel_id=1, source_target_pairs={{0,12},{4,16},{8,4},{12,24},{16,28},{20,0},{24,20},{28,8},{1,13},{... | collective-permute-start | bytes 1179656 | tf_op jit(solution)/shard_map/ppermute | solution.py:456
  33.2 39.9 %copy-start = (f32[256]{0:T(256)S(1)}, f32[256]{0:T(256)}, u32[]{:S(2)}) copy-start(f32[256]{0:T(256)} %param.16) | copy-start | bytes 3076
  33.2 14.3 %collective-permute-start.4 = (bf16[384,256]{1,0:T(8,128)(2,1)S(1)}, bf16[384,256]{1,0:T(8,128)(2,1)S(1)}, u32[]{:S(2)}, u32[]{:S(2)}) collective-permute-start(bf16[384,256]{1,0:T(8,128)(2,1)S(1)} %convert_element_type.7), channel_id=1, source_target_pairs={{0,16},{4,12},{8,24},{12,4},{16,0},{20,28},{24,8},{28,20},{1,17},{... | collective-permute-start | bytes 589832 | tf_op jit(solution)/shard_map/ppermute | solution.py:279
  47.5 1.8 %collective-permute-start.8 = (f32[384,256]{1,0:T(8,128)S(1)}, f32[384,256]{1,0:T(8,128)S(1)}, u32[]{:S(2)}, u32[]{:S(2)}) collective-permute-start(f32[384,256]{1,0:T(8,128)S(1)} %merge.5.rest_0_), channel_id=1, source_target_pairs={{0,4},{4,0},{8,12},{12,8},{16,20},{20,16},{24,28},{28,24},{1,5},{5... | collective-permute-start | bytes 1179656 | tf_op jit(solution)/shard_map/ppermute | solution.py:284
  47.6 4.4 %collective-permute-start.12 = (bf16[256,768]{1,0:T(8,128)(2,1)S(1)}, bf16[256,768]{1,0:T(8,128)(2,1)S(1)}, u32[]{:S(2)}, u32[]{:S(2)}) collective-permute-start(bf16[256,768]{1,0:T(8,128)(2,1)S(1)} %get-tuple-element.49), channel_id=1, source_target_pairs={{0,4},{4,0},{8,12},{12,8},{16,20},{20,16},{24,28},{28,24},{1,5},{5... | collective-permute-start | bytes 1179656 | tf_op jit(solution)/shard_map/ppermute | solution.py:456
  48.1 7.8 %collective-permute-start.13 = (bf16[256,768]{1,0:T(8,128)(2,1)S(1)}, bf16[256,768]{1,0:T(8,128)(2,1)S(1)}, u32[]{:S(2)}, u32[]{:S(2)}) collective-permute-start(bf16[256,768]{1,0:T(8,128)(2,1)S(1)} %get-tuple-element.50), channel_id=1, source_target_pairs={{0,8},{4,20},{8,0},{12,28},{16,24},{20,4},{24,16},{28,12},{1,9},{5... | collective-permute-start | bytes 1179656 | tf_op jit(solution)/shard_map/ppermute | solution.py:456
  57.4 14.4 %collective-permute-start.14 = (bf16[256,256]{1,0:T(8,128)(2,1)S(1)}, bf16[256,256]{1,0:T(8,128)(2,1)S(1)}, u32[]{:S(2)}, u32[]{:S(2)}) collective-permute-start(bf16[256,256]{1,0:T(8,128)(2,1)S(1)} %get-tuple-element.51), channel_id=1, source_target_pairs={{28,0},{24,4},{20,8},{16,12},{12,16},{8,20},{4,24},{0,28},{29,1},{... | collective-permute-start | bytes 393224 | tf_op jit(solution)/shard_map/ppermute | solution.py:461
  57.8 14.0 %collective-permute-start.15 = (bf16[256,256]{1,0:T(8,128)(2,1)S(1)}, bf16[256,256]{1,0:T(8,128)(2,1)S(1)}, u32[]{:S(2)}, u32[]{:S(2)}) collective-permute-start(bf16[256,256]{1,0:T(8,128)(2,1)S(1)} %get-tuple-element.52), channel_id=1, source_target_pairs={{24,0},{28,4},{16,8},{20,12},{8,16},{12,20},{0,24},{4,28},{25,1},{... | collective-permute-start | bytes 393224 | tf_op jit(solution)/shard_map/ppermute | solution.py:461
  59.2 13.8 %collective-permute-start.16 = (bf16[256,256]{1,0:T(8,128)(2,1)S(1)}, bf16[256,256]{1,0:T(8,128)(2,1)S(1)}, u32[]{:S(2)}, u32[]{:S(2)}) collective-permute-start(bf16[256,256]{1,0:T(8,128)(2,1)S(1)} %get-tuple-element.53), channel_id=1, source_target_pairs={{4,0},{0,4},{12,8},{8,12},{20,16},{16,20},{28,24},{24,28},{5,1},{1... | collective-permute-start | bytes 393224 | tf_op jit(solution)/shard_map/ppermute | solution.py:461
  60.3 5.0 %collective-permute-start.11 = (f32[1,2048]{1,0:T(1,128)S(1)}, f32[1,2048]{1,0:T(1,128)S(1)}, u32[]{:S(2)}, u32[]{:S(2)}) collective-permute-start(f32[1,2048]{1,0:T(1,128)S(1)} %get-tuple-element.47.refs_8_.rest_0_), channel_id=1, source_target_pairs={{0,3},{1,0},{2,1},{3,2},{4,7},{5,4},{6,5},{7,6},{8,11},{9,8},{10,9... | collective-permute-start | bytes 24584 | tf_op jit(solution)/shard_map/ppermute | solution.py:488
  63.9 4.5 %collective-permute-start.10 = (f32[1,2048]{1,0:T(1,128)S(1)}, f32[1,2048]{1,0:T(1,128)S(1)}, u32[]{:S(2)}, u32[]{:S(2)}) collective-permute-start(f32[1,2048]{1,0:T(1,128)S(1)} %get-tuple-element.47.refs_8_.rest_0_), channel_id=1, source_target_pairs={{0,2},{1,3},{2,0},{3,1},{4,6},{5,7},{6,4},{7,5},{8,10},{9,11},{10,... | collective-permute-start | bytes 24584 | tf_op jit(solution)/shard_map/ppermute | solution.py:488
  65.2 5.7 %collective-permute-start.9 = (f32[1,2048]{1,0:T(1,128)S(1)}, f32[1,2048]{1,0:T(1,128)S(1)}, u32[]{:S(2)}, u32[]{:S(2)}) collective-permute-start(f32[1,2048]{1,0:T(1,128)S(1)} %get-tuple-element.47.refs_8_.rest_0_), channel_id=1, source_target_pairs={{0,1},{1,2},{2,3},{3,0},{4,5},{5,6},{6,7},{7,4},{8,9},{9,10},{10,1... | collective-permute-start | bytes 24584 | tf_op jit(solution)/shard_map/ppermute | solution.py:488
  68.4 6.0 %collective-permute-start.17 = (bf16[256,256]{1,0:T(8,128)(2,1)S(1)}, bf16[256,256]{1,0:T(8,128)(2,1)S(1)}, u32[]{:S(2)}, u32[]{:S(2)}) collective-permute-start(bf16[256,256]{1,0:T(8,128)(2,1)S(1)} %get-tuple-element.55), channel_id=1, source_target_pairs={{20,0},{8,4},{28,8},{0,12},{4,16},{24,20},{12,24},{16,28},{21,1},{... | collective-permute-start | bytes 393224 | tf_op jit(solution)/shard_map/ppermute | solution.py:461
  70.9 5.1 %collective-permute-start.18 = (bf16[256,256]{1,0:T(8,128)(2,1)S(1)}, bf16[256,256]{1,0:T(8,128)(2,1)S(1)}, u32[]{:S(2)}, u32[]{:S(2)}) collective-permute-start(bf16[256,256]{1,0:T(8,128)(2,1)S(1)} %get-tuple-element.56), channel_id=1, source_target_pairs={{16,0},{12,4},{24,8},{4,12},{0,16},{28,20},{8,24},{20,28},{17,1},{... | collective-permute-start | bytes 393224 | tf_op jit(solution)/shard_map/ppermute | solution.py:461
  71.9 5.3 %collective-permute-start.19 = (bf16[256,256]{1,0:T(8,128)(2,1)S(1)}, bf16[256,256]{1,0:T(8,128)(2,1)S(1)}, u32[]{:S(2)}, u32[]{:S(2)}) collective-permute-start(bf16[256,256]{1,0:T(8,128)(2,1)S(1)} %get-tuple-element.57), channel_id=1, source_target_pairs={{12,0},{16,4},{4,8},{24,12},{28,16},{0,20},{20,24},{8,28},{13,1},{... | collective-permute-start | bytes 393224 | tf_op jit(solution)/shard_map/ppermute | solution.py:461
  71.9 5.8 %collective-permute-start.20 = (bf16[256,256]{1,0:T(8,128)(2,1)S(1)}, bf16[256,256]{1,0:T(8,128)(2,1)S(1)}, u32[]{:S(2)}, u32[]{:S(2)}) collective-permute-start(bf16[256,256]{1,0:T(8,128)(2,1)S(1)} %get-tuple-element.58), channel_id=1, source_target_pairs={{8,0},{20,4},{0,8},{28,12},{24,16},{4,20},{16,24},{12,28},{9,1},{2... | collective-permute-start | bytes 393224 | tf_op jit(solution)/shard_map/ppermute | solution.py:461

commit v6 on v5

--- a/solution.py
+++ b/solution.py
@@ -285,7 +285,7 @@
 
 
 def readout_kernel(parts, q_ref, one_ref, three_ref, two_ref, *rest):
-    grads, (y_ref, sq_ref, total, fresh) = rest[:parts], rest[parts:]
+    grads, (y_ref, sq_ref, total, fresh) = rest[:parts], rest[-4:]
     hid, width = one_ref.shape[1:]
     if parts == 2:
         half = total.shape[0] // 2
@@ -324,7 +324,7 @@
         sq_ref[:, here] = (dot_bt(ones, high) + dot_bt(ones, low))[0:1, :]
 
 
-def read_out(q, one, three, two, grads):
+def read_out(q, one, three, two, grads, after):
     count, width = q.shape
     hid = one.shape[1]
     parts = len(grads)
@@ -334,13 +334,13 @@
             jax.ShapeDtypeStruct((count, width), F32),
             jax.ShapeDtypeStruct((1, count), F32),
         ],
-        in_specs=full(4 + parts),
+        in_specs=full(4 + parts) + [pl.BlockSpec(memory_space=pl.ANY)] * len(after),
         out_specs=full(2),
         scratch_shapes=[pltpu.VMEM((3 * hid, width), F32), pltpu.VMEM((3 * hid, width), BF16)],
         compiler_params=params(),
         cost_estimate=cost(6 * count * width * hid, 8 * count * width, count * hid),
         name="read_out",
-    )(q, one, three, two, *grads)
+    )(q, one, three, two, *grads, *after)
 
 
 def place_kernel(n, steps, order_ref, *outs):
@@ -468,27 +468,27 @@
     steps = far_first(n)
     few = max(1, n // 4)
     weights = (w_one, w_three, w_two)
-    groups = (tuple(steps[:few]), tuple(steps[few:]))
+    groups = (tuple(steps[:few]), tuple(steps[few : 2 * few]), tuple(steps[2 * few :]))
     marks = mark(order, n, groups)
     parts = gradients(keys, values, rates.reshape(1, count), *weights, marks[-1], n)
+    arrived = {}
+    tokens = []
+    for group, onehot in zip(groups, marks):
+        blocks = sort_tokens(onehot, queries, keys, values, [], n)
+        tokens.append(blocks[-1])
+        for step, block in zip(group, blocks):
+            arrived[step] = exchange(block, step, n)
+    mine = core_step(parts, tokens[:1], n)
+    summed = sum_over_chips(mine, len(parts) == 2, [tokens[1:2], [arrived[s] for s in steps[:2]] + tokens[2:]], n)
     early = steps[:few] + steps[n - few :]
     late = steps[few : n - few]
     early_places, late_places = place(order, n, early + late)
-    mine = core_step(parts, [late_places], n)
-    arrived = {}
-    tokens = []
-    for group, onehot, after in zip(groups, marks, ([mine], [])):
-        blocks = sort_tokens(onehot, queries, keys, values, after + tokens, n)
-        tokens.append(blocks[-1])
-        for step, block in zip(group, blocks):
-            arrived[step] = exchange(block, step, n)
-    summed = sum_over_chips(mine, len(parts) == 2, [tokens[1:] + [arrived[steps[0]], arrived[steps[1]]], [arrived[step] for step in steps[: 2 * few + 1]]], n)
-    y, square = read_out(queries, *weights, summed)
+    y, square = read_out(queries, *weights, summed, [late_places])
     squares = [square] + [
         lax.ppermute(square, "head", [(at, (at + step) % heads) for at in range(heads)])
         for step in range(1, heads)
     ]
-    attended = attend([arrived[step] for step in range(n)], [square], n, width)
+    attended = attend([arrived[step] for step in range(n)], squares, n, width)
     returned = {step: give_back(attended[step], step, n) for step in early + late}
     given = base(
         gain.reshape(1, width), y, early_places, squares, [returned[step] for step in early]

time: 80.6 us -> 77.3 us (0.959)
  waiting for transfers between devices: 38.8 us -> 25 us
  starting transfers between devices: 19.2 us -> 29.7 us
    ppermute x7, waiting for transfers between devices: 26.2 us -> 16 us  [exchange(): return lax.ppermute(block, 'cam', routes(step, n)) if step else block]
    ppermute x3, starting transfers between devices: 3.86 us -> 10.3 us  [per_device(): lax.ppermute(square, 'head', [(at, (at + step) % heads) for at in range(h...]
    ppermute x3, waiting for transfers between devices: 6.8 us -> 1.35 us  [per_device(): lax.ppermute(square, 'head', [(at, (at + step) % heads) for at in range(h...]
    ppermute x2, starting transfers between devices: 2.64 us -> 5.03 us  [sum_over_chips(): got = lax.ppermute(mine.astype(BF16), 'cam', pairs)]
    ppermute x7, waiting for transfers between devices: 3.28 us -> 5.62 us  [give_back(): return lax.ppermute(block, 'cam', pairs) if step else block]
    ppermute x7, starting transfers between devices: 4.94 us -> 7.09 us  [give_back(): return lax.ppermute(block, 'cam', pairs) if step else block]
    pallas_call x2 -> x3, Pallas kernels: 6.93 us -> 7.01 us  [sort_tokens(): pl.pallas_call(functools.partial(sort_kernel, size), out_shape=[jax.Shape...]
  transfers between devices with their start and end apart: 21 -> 21, of which waited for: 13 -> 10; matrix products, arithmetic and copies ran while one was open for 0% -> 0% of each run, Pallas kernels for 16% -> 17%
where the time goes in v6:
time: 77.3 us; the launch traced here: 76.9 us
  starting transfers between devices  29.7 us (38%)
  waiting for transfers between devices  25 us (32%)
  Pallas kernels  20.7 us (27%)
  local copies, waits for them, and re-layouts  0.99 us (1%)
    ppermute x7, waiting for transfers between devices, exchange(): return lax.ppermute(block, 'cam', routes(step, n)) if step else block  16 us
    ppermute x3, starting transfers between devices, per_device(): lax.ppermute(square, 'head', [(at, (at + step) % heads) for at in range(h...  10.3 us
    ppermute x7, starting transfers between devices, give_back(): return lax.ppermute(block, 'cam', pairs) if step else block  7.09 us
    pallas_call x3, Pallas kernels, sort_tokens(): pl.pallas_call(functools.partial(sort_kernel, size), out_shape=[jax.Shape...  7.01 us
    ppermute x7, starting transfers between devices, exchange(): return lax.ppermute(block, 'cam', routes(step, n)) if step else block  6.76 us
    ppermute x7, waiting for transfers between devices, give_back(): return lax.ppermute(block, 'cam', pairs) if step else block  5.62 us
    ppermute x2, starting transfers between devices, sum_over_chips(): got = lax.ppermute(mine.astype(BF16), 'cam', pairs)  5.03 us
    pallas_call x1, Pallas kernels, gradients(): pl.pallas_call(functools.partial(grads_kernel, n, split), out_shape=[jax....  2.87 us
  transfers between devices with their start and end apart: 21, of which 10 were waited for; matrix products, arithmetic and copies ran while one was open for 0% of the time, Pallas kernels for 17%

profile of v6, /device:TPU:0, one launch (start us, length us, event | category | flops | bytes accessed | tf_op | source)
XLA Modules:
  0.0 76.9 jit_solution(14250445532602683589)
XLA Ops:
  0.7 1.4 %mark.1 = (bf16[512,2048]{1,0:T(8,128)(2,1)S(1)}, bf16[512,2048]{1,0:T(8,128)(2,1)S(1)}, bf16[1024,2048]{1,0:T(8,128)(2,1)S(1)}, f32[8,128]{1,0:T(8,128)S(1)}) custom-call(s32[1,2048]{1,0:T(1,128)S(1)} %copy-done.8), custom_call_target="tpu_custom_call" | custom-call | flops 999999995904 | bytes 1024 | tf_op jit(solution)/shard_map/mark/pallas_call | solution.py:107
  2.5 2.9 %gradients.1 = (f32[384,256]{1,0:T(8,128)S(1)}, f32[384,256]{1,0:T(8,128)S(1)}) custom-call(bf16[2048,256]{1,0:T(8,128)(2,1)S(1)} %copy-done.5, bf16[2048,256]{1,0:T(8,128)(2,1)S(1)} %copy-done.6, f32[1,2048]{1,0:T(1,128)S(1)} %bitcast.3, bf16[1,256,256]{2,1,0:T(8,128)(2,1)S(1)} %copy-done.1, bf16[1,256,256]{2,1,0:T(8,128)(2,1)S(1)} %copy-done.2, ...), custom_call_target="tpu_custom_call" | custom-call | flops 1610612736 | bytes 4194304 | tf_op jit(solution)/shard_map/gradients/pallas_call | solution.py:235
  5.8 1.8 %sort_tokens.3 = (bf16[256,768]{1,0:T(8,128)(2,1)S(1)}, bf16[256,768]{1,0:T(8,128)(2,1)S(1)}, f32[8,128]{1,0:T(8,128)S(1)}) custom-call(bf16[512,2048]{1,0:T(8,128)(2,1)S(1)} %get-tuple-element.37.onehot, bf16[2048,256]{1,0:T(8,128)(2,1)S(1)} %copy-done, bf16[2048,256]{1,0:T(8,128)(2,1)S(1)} %copy-done.5, bf16[2048,256]{1,0:T(8,128)(2,1)S(1)} %copy-done.6), custom_call_target="tpu_custom_call" | custom-call | flops 1610612736 | bytes 3145728 | tf_op jit(solution)/shard_map/sort_tokens/pallas_call | solution.py:140
  7.7 2.6 %collective-permute-start.1 = (bf16[384,256]{1,0:T(8,128)(2,1)S(1)}, bf16[384,256]{1,0:T(8,128)(2,1)S(1)}, u32[]{:S(2)}, u32[]{:S(2)}) collective-permute-start(bf16[384,256]{1,0:T(8,128)(2,1)S(1)} %convert_element_type.6), channel_id=1, source_target_pairs={{0,8},{4,20},{8,0},{12,28},{16,24},{20,4},{24,16},{28,12},{1,9},{5... | collective-permute-start | bytes 589832 | tf_op jit(solution)/shard_map/ppermute | solution.py:279
  10.3 1.3 %collective-permute-start.3 = (bf16[256,768]{1,0:T(8,128)(2,1)S(1)}, bf16[256,768]{1,0:T(8,128)(2,1)S(1)}, u32[]{:S(2)}, u32[]{:S(2)}) collective-permute-start(bf16[256,768]{1,0:T(8,128)(2,1)S(1)} %get-tuple-element.41), channel_id=1, source_target_pairs={{0,28},{4,24},{8,20},{12,16},{16,12},{20,8},{24,4},{28,0},{1,29},{... | collective-permute-start | bytes 1179656 | tf_op jit(solution)/shard_map/ppermute | solution.py:456
  11.6 1.5 %collective-permute-start.4 = (bf16[256,768]{1,0:T(8,128)(2,1)S(1)}, bf16[256,768]{1,0:T(8,128)(2,1)S(1)}, u32[]{:S(2)}, u32[]{:S(2)}) collective-permute-start(bf16[256,768]{1,0:T(8,128)(2,1)S(1)} %get-tuple-element.42), channel_id=1, source_target_pairs={{0,24},{4,28},{8,16},{12,20},{16,8},{20,12},{24,0},{28,4},{1,25},{... | collective-permute-start | bytes 1179656 | tf_op jit(solution)/shard_map/ppermute | solution.py:456
  13.1 1.8 %sort_tokens.4 = (bf16[256,768]{1,0:T(8,128)(2,1)S(1)}, bf16[256,768]{1,0:T(8,128)(2,1)S(1)}, f32[8,128]{1,0:T(8,128)S(1)}) custom-call(bf16[512,2048]{1,0:T(8,128)(2,1)S(1)} %get-tuple-element.39.onehot, bf16[2048,256]{1,0:T(8,128)(2,1)S(1)} %copy-done, bf16[2048,256]{1,0:T(8,128)(2,1)S(1)} %copy-done.5, bf16[2048,256]{1,0:T(8,128)(2,1)S(1)} %copy-done.6), custom_call_target="tpu_custom_call" | custom-call | flops 1610612736 | bytes 3145728 | tf_op jit(solution)/shard_map/sort_tokens/pallas_call | solution.py:140
  15.0 2.5 %collective-permute-start.2 = (bf16[384,256]{1,0:T(8,128)(2,1)S(1)}, bf16[384,256]{1,0:T(8,128)(2,1)S(1)}, u32[]{:S(2)}, u32[]{:S(2)}) collective-permute-start(bf16[384,256]{1,0:T(8,128)(2,1)S(1)} %convert_element_type.7), channel_id=1, source_target_pairs={{0,16},{4,12},{8,24},{12,4},{16,0},{20,28},{24,8},{28,20},{1,17},{... | collective-permute-start | bytes 589832 | tf_op jit(solution)/shard_map/ppermute | solution.py:279
  17.4 3.4 %sort_tokens.5 = (bf16[256,768]{1,0:T(8,128)(2,1)S(1)}, bf16[256,768]{1,0:T(8,128)(2,1)S(1)}, bf16[256,768]{1,0:T(8,128)(2,1)S(1)}, bf16[256,768]{1,0:T(8,128)(2,1)S(1)}, f32[8,128]{1,0:T(8,128)S(1)}) custom-call(bf16[1024,2048]{1,0:T(8,128)(2,1)S(1)} %get-tuple-element.43.onehot, bf16[2048,256]{1,0:T(8,128)(2,1)S(1)} %copy-done, ...), custom_call_target="tpu_custom_call" | custom-call | flops 3221225472 | bytes 3145728 | tf_op jit(solution)/shard_map/sort_tokens/pallas_call | solution.py:140
  20.9 2.3 %collective-permute-done.3.rest_0_.refs_7_ = bf16[256,768]{1,0:T(8,128)(2,1)S(1)} collective-permute-done((bf16[256,768]{1,0:T(8,128)(2,1)S(1)}, bf16[256,768]{1,0:T(8,128)(2,1)S(1)}, u32[]{:S(2)}, u32[]{:S(2)}) %collective-permute-start.3) | collective-permute-done | bytes 393248 | tf_op jit(solution)/shard_map/ppermute | solution.py:456
  23.1 9.3 %collective-permute-done.4.rest_1_.refs_6_ = bf16[256,768]{1,0:T(8,128)(2,1)S(1)} collective-permute-done((bf16[256,768]{1,0:T(8,128)(2,1)S(1)}, bf16[256,768]{1,0:T(8,128)(2,1)S(1)}, u32[]{:S(2)}, u32[]{:S(2)}) %collective-permute-start.4) | collective-permute-done | bytes 393248 | tf_op jit(solution)/shard_map/ppermute | solution.py:456
  32.4 2.0 %collective-permute-done.2.got_ref = bf16[384,256]{1,0:T(8,128)(2,1)S(1)} collective-permute-done((bf16[384,256]{1,0:T(8,128)(2,1)S(1)}, bf16[384,256]{1,0:T(8,128)(2,1)S(1)}, u32[]{:S(2)}, u32[]{:S(2)}) %collective-permute-start.2) | collective-permute-done | bytes 196640 | tf_op jit(solution)/shard_map/ppermute | solution.py:279
  35.0 0.9 %collective-permute-start.10 = (bf16[256,768]{1,0:T(8,128)(2,1)S(1)}, bf16[256,768]{1,0:T(8,128)(2,1)S(1)}, u32[]{:S(2)}, u32[]{:S(2)}) collective-permute-start(bf16[256,768]{1,0:T(8,128)(2,1)S(1)} %get-tuple-element.51), channel_id=1, source_target_pairs={{0,8},{4,20},{8,0},{12,28},{16,24},{20,4},{24,16},{28,12},{1,9},{5... | collective-permute-start | bytes 1179656 | tf_op jit(solution)/shard_map/ppermute | solution.py:456
  36.0 1.5 %collective-permute-start.11 = (bf16[256,768]{1,0:T(8,128)(2,1)S(1)}, bf16[256,768]{1,0:T(8,128)(2,1)S(1)}, u32[]{:S(2)}, u32[]{:S(2)}) collective-permute-start(bf16[256,768]{1,0:T(8,128)(2,1)S(1)} %get-tuple-element.52), channel_id=1, source_target_pairs={{0,12},{4,16},{8,4},{12,24},{16,28},{20,0},{24,20},{28,8},{1,13},{... | collective-permute-start | bytes 1179656 | tf_op jit(solution)/shard_map/ppermute | solution.py:456
  37.8 0.7 collective-permute-start.13
  38.5 1.7 %place.1 = (bf16[2048,1024]{1,0:T(8,128)(2,1)S(1)}, bf16[2048,1024]{1,0:T(8,128)(2,1)S(1)}) custom-call(s32[1,2048]{1,0:T(1,128)S(1)} %copy-done.9), custom_call_target="tpu_custom_call" | custom-call | flops 4194304 | bytes 8388608 | tf_op jit(solution)/shard_map/place/pallas_call | solution.py:370
  40.2 2.7 %read_out.1 = (f32[2048,256]{1,0:T(8,128)S(1)}, f32[1,2048]{1,0:T(1,128)S(1)}) custom-call(bf16[2048,256]{1,0:T(8,128)(2,1)S(1)} %copy-done, bf16[1,256,256]{2,1,0:T(8,128)(2,1)S(1)} %copy-done.1, bf16[1,256,256]{2,1,0:T(8,128)(2,1)S(1)} %copy-done.2, bf16[1,256,256]{2,1,0:T(8,128)(2,1)S(1)} %copy-done.3, f32[384,256]{1,0:T(8,128)S(1)} %merge.5.rest_0_, ...), custom_call_target="tpu_custom_call" | custom-call | flops 805306368 | bytes 4194304 | tf_op jit(solution)/shard_map/read_out/pallas_call | solution.py:331
  42.9 1.6 %collective-permute-start.6 = (f32[1,2048]{1,0:T(1,128)S(1)}, f32[1,2048]{1,0:T(1,128)S(1)}, u32[]{:S(2)}, u32[]{:S(2)}) collective-permute-start(f32[1,2048]{1,0:T(1,128)S(1)} %get-tuple-element.48.refs_8_.rest_0_), channel_id=1, source_target_pairs={{0,1},{1,2},{2,3},{3,0},{4,5},{5,6},{6,7},{7,4},{8,9},{9,10},{10,1... | collective-permute-start | bytes 24584 | tf_op jit(solution)/shard_map/ppermute | solution.py:488
  45.1 3.4 %collective-permute-start.7 = (f32[1,2048]{1,0:T(1,128)S(1)}, f32[1,2048]{1,0:T(1,128)S(1)}, u32[]{:S(2)}, u32[]{:S(2)}) collective-permute-start(f32[1,2048]{1,0:T(1,128)S(1)} %get-tuple-element.48.refs_8_.rest_0_), channel_id=1, source_target_pairs={{0,2},{1,3},{2,0},{3,1},{4,6},{5,7},{6,4},{7,5},{8,10},{9,11},{10,... | collective-permute-start | bytes 24584 | tf_op jit(solution)/shard_map/ppermute | solution.py:488
  48.5 3.9 %collective-permute-done.11.refs_3_ = bf16[256,768]{1,0:T(8,128)(2,1)S(1)} collective-permute-done((bf16[256,768]{1,0:T(8,128)(2,1)S(1)}, bf16[256,768]{1,0:T(8,128)(2,1)S(1)}, u32[]{:S(2)}, u32[]{:S(2)}) %collective-permute-start.11) | collective-permute-done | bytes 393248 | tf_op jit(solution)/shard_map/ppermute | solution.py:456
  52.4 5.3 %collective-permute-start.8 = (f32[1,2048]{1,0:T(1,128)S(1)}, f32[1,2048]{1,0:T(1,128)S(1)}, u32[]{:S(2)}, u32[]{:S(2)}) collective-permute-start(f32[1,2048]{1,0:T(1,128)S(1)} %get-tuple-element.48.refs_8_.rest_0_), channel_id=1, source_target_pairs={{0,3},{1,0},{2,1},{3,2},{4,7},{5,4},{6,5},{7,6},{8,11},{9,8},{10,9... | collective-permute-start | bytes 24584 | tf_op jit(solution)/shard_map/ppermute | solution.py:488
  57.7 1.3 %collective-permute-done.8.refs_11_.rest_3_ = f32[1,2048]{1,0:T(1,128)S(1)} collective-permute-done((f32[1,2048]{1,0:T(1,128)S(1)}, f32[1,2048]{1,0:T(1,128)S(1)}, u32[]{:S(2)}, u32[]{:S(2)}) %collective-permute-start.8) | collective-permute-done | bytes 8224 | tf_op jit(solution)/shard_map/ppermute | solution.py:488
  59.1 1.5 %attend.1 = (bf16[256,256]{1,0:T(8,128)(2,1)S(1)}, bf16[256,256]{1,0:T(8,128)(2,1)S(1)}, bf16[256,256]{1,0:T(8,128)(2,1)S(1)}, bf16[256,256]{1,0:T(8,128)(2,1)S(...) custom-call(bf16[256,768]{1,0:T(8,128)(2,1)S(1)} %get-tuple-element., ...), custom_call_target="tpu_custom_call" | custom-call | flops 536870912 | bytes 4194304 | tf_op jit(solution)/shard_map/attend/pallas_call | solution.py:179
  61.3 1.3 %collective-permute-start.15 = (bf16[256,256]{1,0:T(8,128)(2,1)S(1)}, bf16[256,256]{1,0:T(8,128)(2,1)S(1)}, u32[]{:S(2)}, u32[]{:S(2)}) collective-permute-start(bf16[256,256]{1,0:T(8,128)(2,1)S(1)} %get-tuple-element.56), channel_id=1, source_target_pairs={{24,0},{28,4},{16,8},{20,12},{8,16},{12,20},{0,24},{4,28},{25,1},{... | collective-permute-start | bytes 393224 | tf_op jit(solution)/shard_map/ppermute | solution.py:461
  62.7 0.8 collective-permute-start.16
  63.4 1.6 %collective-permute-start.17 = (bf16[256,256]{1,0:T(8,128)(2,1)S(1)}, bf16[256,256]{1,0:T(8,128)(2,1)S(1)}, u32[]{:S(2)}, u32[]{:S(2)}) collective-permute-start(bf16[256,256]{1,0:T(8,128)(2,1)S(1)} %get-tuple-element.59), channel_id=1, source_target_pairs={{20,0},{8,4},{28,8},{0,12},{4,16},{24,20},{12,24},{16,28},{21,1},{... | collective-permute-start | bytes 393224 | tf_op jit(solution)/shard_map/ppermute | solution.py:461
  65.1 2.3 %collective-permute-done.14.rest_4_ = bf16[256,256]{1,0:T(8,128)(2,1)S(1)} collective-permute-done((bf16[256,256]{1,0:T(8,128)(2,1)S(1)}, bf16[256,256]{1,0:T(8,128)(2,1)S(1)}, u32[]{:S(2)}, u32[]{:S(2)}) %collective-permute-start.14) | collective-permute-done | bytes 131104 | tf_op jit(solution)/shard_map/ppermute | solution.py:461
  68.0 1.7 %collective-permute-done.15.rest_5_ = bf16[256,256]{1,0:T(8,128)(2,1)S(1)} collective-permute-done((bf16[256,256]{1,0:T(8,128)(2,1)S(1)}, bf16[256,256]{1,0:T(8,128)(2,1)S(1)}, u32[]{:S(2)}, u32[]{:S(2)}) %collective-permute-start.15) | collective-permute-done | bytes 131104 | tf_op jit(solution)/shard_map/ppermute | solution.py:461
  69.7 2.0 %collective-permute-start.20 = (bf16[256,256]{1,0:T(8,128)(2,1)S(1)}, bf16[256,256]{1,0:T(8,128)(2,1)S(1)}, u32[]{:S(2)}, u32[]{:S(2)}) collective-permute-start(bf16[256,256]{1,0:T(8,128)(2,1)S(1)} %get-tuple-element.62), channel_id=1, source_target_pairs={{8,0},{20,4},{0,8},{28,12},{24,16},{4,20},{16,24},{12,28},{9,1},{2... | collective-permute-start | bytes 393224 | tf_op jit(solution)/shard_map/ppermute | solution.py:461
  71.7 1.3 %base.1.base_ref = f32[2048,256]{1,0:T(8,128)S(1)} custom-call(f32[1,256]{1,0:T(1,128)S(1)} %bitcast.2, f32[2048,256]{1,0:T(8,128)S(1)} %get-tuple-element.46.y_ref, bf16[2048,1024]{1,0:T(8,128)(2,1)S(1)} %get-tuple-element.47.onehot, f32[1,2048]{1,0:T(1,128)S(1)} %get-tuple-element.48.refs_8_.rest_0_, f32[1,2048]{1,0:T(1,128)S(1)} %collective-permute-done.6.refs_9_.rest_1_, ...), custom_call_target="tpu_custom_call" | custom-call | flops 1073741824 | bytes 4194304 | tf_op jit(solution)/shard_map/base/pallas_call | solution.py:412
  73.5 1.1 %collective-permute-done.20.rest_3_ = bf16[256,256]{1,0:T(8,128)(2,1)S(1)} collective-permute-done((bf16[256,256]{1,0:T(8,128)(2,1)S(1)}, bf16[256,256]{1,0:T(8,128)(2,1)S(1)}, u32[]{:S(2)}, u32[]{:S(2)}) %collective-permute-start.20) | collective-permute-done | bytes 131104 | tf_op jit(solution)/shard_map/ppermute | solution.py:461
  74.6 2.1 %mix.1 = bf16[2048,256]{1,0:T(8,128)(2,1)} custom-call(f32[2048,256]{1,0:T(8,128)S(1)} %base.1.base_ref, bf16[2048,1024]{1,0:T(8,128)(2,1)S(1)} %get-tuple-element.45.rest_2_.onehot, bf16[256,256]{1,0:T(8,128)(2,1)S(1)} %collective-permute-done.17.rest_0_, bf16[256,256]{1,0:T(8,128)(2,1)S(1)} %collective-permute-done.18.rest_1_, ...), custom_call_target="tpu_custom_call" | custom-call | flops 1073741824 | bytes 4194304 | tf_op jit(solution)/shard_map/mix/pallas_call | solution.py:440
  (45 shorter events, 5.0 us)
Async XLA Ops:
  0.0 0.7 copy-start.8
  0.7 1.4 %copy-start.1 = (bf16[1,256,256]{2,1,0:T(8,128)(2,1)S(1)}, bf16[1,256,256]{2,1,0:T(8,128)(2,1)}, u32[]{:S(2)}) copy-start(bf16[1,256,256]{2,1,0:T(8,128)(2,1)} %one_ref.3) | copy-start | bytes 393220
  0.7 1.5 %copy-start.2 = (bf16[1,256,256]{2,1,0:T(8,128)(2,1)S(1)}, bf16[1,256,256]{2,1,0:T(8,128)(2,1)}, u32[]{:S(2)}) copy-start(bf16[1,256,256]{2,1,0:T(8,128)(2,1)} %three_ref.3) | copy-start | bytes 393220
  0.7 1.5 %copy-start.3 = (bf16[1,256,256]{2,1,0:T(8,128)(2,1)S(1)}, bf16[1,256,256]{2,1,0:T(8,128)(2,1)}, u32[]{:S(2)}) copy-start(bf16[1,256,256]{2,1,0:T(8,128)(2,1)} %two_ref.3) | copy-start | bytes 393220
  0.7 1.5 %copy-start.5 = (bf16[2048,256]{1,0:T(8,128)(2,1)S(1)}, bf16[2048,256]{1,0:T(8,128)(2,1)}, u32[]{:S(2)}) copy-start(bf16[2048,256]{1,0:T(8,128)(2,1)} %k_ref.7) | copy-start | bytes 3145732
  0.7 1.7 %copy-start.6 = (bf16[2048,256]{1,0:T(8,128)(2,1)S(1)}, bf16[2048,256]{1,0:T(8,128)(2,1)}, u32[]{:S(2)}) copy-start(bf16[2048,256]{1,0:T(8,128)(2,1)} %v_ref.7) | copy-start | bytes 3145732
  0.7 1.7 %copy-start.7 = (f32[2048,1]{0,1:T(1,128)S(1)}, f32[2048,1]{0,1:T(1,128)}, u32[]{:S(2)}) copy-start(f32[2048,1]{0,1:T(1,128)} %param.12) | copy-start | bytes 24580
  2.4 3.4 %copy-start = (bf16[2048,256]{1,0:T(8,128)(2,1)S(1)}, bf16[2048,256]{1,0:T(8,128)(2,1)}, u32[]{:S(2)}) copy-start(bf16[2048,256]{1,0:T(8,128)(2,1)} %q_ref.7) | copy-start | bytes 3145732
  5.3 2.3 %collective-permute-start = (f32[384,256]{1,0:T(8,128)S(1)}, f32[384,256]{1,0:T(8,128)S(1)}, u32[]{:S(2)}, u32[]{:S(2)}) collective-permute-start(f32[384,256]{1,0:T(8,128)S(1)} %get-tuple-element.36), channel_id=1, source_target_pairs={{0,4},{4,0},{8,12},{12,8},{16,20},{20,16},{24,28},{28,24},{1,5},{5... | collective-permute-start | bytes 1179656 | tf_op jit(solution)/shard_map/ppermute | solution.py:267
  7.7 7.1 %collective-permute-start.1 = (bf16[384,256]{1,0:T(8,128)(2,1)S(1)}, bf16[384,256]{1,0:T(8,128)(2,1)S(1)}, u32[]{:S(2)}, u32[]{:S(2)}) collective-permute-start(bf16[384,256]{1,0:T(8,128)(2,1)S(1)} %convert_element_type.6), channel_id=1, source_target_pairs={{0,8},{4,20},{8,0},{12,28},{16,24},{20,4},{24,16},{28,12},{1,9},{5... | collective-permute-start | bytes 589832 | tf_op jit(solution)/shard_map/ppermute | solution.py:279
  10.3 12.8 %collective-permute-start.3 = (bf16[256,768]{1,0:T(8,128)(2,1)S(1)}, bf16[256,768]{1,0:T(8,128)(2,1)S(1)}, u32[]{:S(2)}, u32[]{:S(2)}) collective-permute-start(bf16[256,768]{1,0:T(8,128)(2,1)S(1)} %get-tuple-element.41), channel_id=1, source_target_pairs={{0,28},{4,24},{8,20},{12,16},{16,12},{20,8},{24,4},{28,0},{1,29},{... | collective-permute-start | bytes 1179656 | tf_op jit(solution)/shard_map/ppermute | solution.py:456
  11.6 20.8 %collective-permute-start.4 = (bf16[256,768]{1,0:T(8,128)(2,1)S(1)}, bf16[256,768]{1,0:T(8,128)(2,1)S(1)}, u32[]{:S(2)}, u32[]{:S(2)}) collective-permute-start(bf16[256,768]{1,0:T(8,128)(2,1)S(1)} %get-tuple-element.42), channel_id=1, source_target_pairs={{0,24},{4,28},{8,16},{12,20},{16,8},{20,12},{24,0},{28,4},{1,25},{... | collective-permute-start | bytes 1179656 | tf_op jit(solution)/shard_map/ppermute | solution.py:456
  15.0 19.4 %collective-permute-start.2 = (bf16[384,256]{1,0:T(8,128)(2,1)S(1)}, bf16[384,256]{1,0:T(8,128)(2,1)S(1)}, u32[]{:S(2)}, u32[]{:S(2)}) collective-permute-start(bf16[384,256]{1,0:T(8,128)(2,1)S(1)} %convert_element_type.7), channel_id=1, source_target_pairs={{0,16},{4,12},{8,24},{12,4},{16,0},{20,28},{24,8},{28,20},{1,17},{... | collective-permute-start | bytes 589832 | tf_op jit(solution)/shard_map/ppermute | solution.py:279
  17.4 21.1 %copy-start.9 = (s32[1,2048]{1,0:T(1,128)S(1)}, s32[1,2048]{1,0:T(1,128)}, u32[]{:S(2)}) copy-start(s32[1,2048]{1,0:T(1,128)} %order_ref.3) | copy-start | bytes 24580
  34.5 3.3 %collective-permute-start.5 = (f32[384,256]{1,0:T(8,128)S(1)}, f32[384,256]{1,0:T(8,128)S(1)}, u32[]{:S(2)}, u32[]{:S(2)}) collective-permute-start(f32[384,256]{1,0:T(8,128)S(1)} %merge.5.rest_0_), channel_id=1, source_target_pairs={{0,4},{4,0},{8,12},{12,8},{16,20},{20,16},{24,28},{28,24},{1,5},{5... | collective-permute-start | bytes 1179656 | tf_op jit(solution)/shard_map/ppermute | solution.py:284
  34.5 8.4 %collective-permute-start.9 = (bf16[256,768]{1,0:T(8,128)(2,1)S(1)}, bf16[256,768]{1,0:T(8,128)(2,1)S(1)}, u32[]{:S(2)}, u32[]{:S(2)}) collective-permute-start(bf16[256,768]{1,0:T(8,128)(2,1)S(1)} %get-tuple-element.50), channel_id=1, source_target_pairs={{0,4},{4,0},{8,12},{12,8},{16,20},{20,16},{24,28},{28,24},{1,5},{5... | collective-permute-start | bytes 1179656 | tf_op jit(solution)/shard_map/ppermute | solution.py:456
  35.0 10.1 %collective-permute-start.10 = (bf16[256,768]{1,0:T(8,128)(2,1)S(1)}, bf16[256,768]{1,0:T(8,128)(2,1)S(1)}, u32[]{:S(2)}, u32[]{:S(2)}) collective-permute-start(bf16[256,768]{1,0:T(8,128)(2,1)S(1)} %get-tuple-element.51), channel_id=1, source_target_pairs={{0,8},{4,20},{8,0},{12,28},{16,24},{20,4},{24,16},{28,12},{1,9},{5... | collective-permute-start | bytes 1179656 | tf_op jit(solution)/shard_map/ppermute | solution.py:456
  36.0 16.4 %collective-permute-start.11 = (bf16[256,768]{1,0:T(8,128)(2,1)S(1)}, bf16[256,768]{1,0:T(8,128)(2,1)S(1)}, u32[]{:S(2)}, u32[]{:S(2)}) collective-permute-start(bf16[256,768]{1,0:T(8,128)(2,1)S(1)} %get-tuple-element.52), channel_id=1, source_target_pairs={{0,12},{4,16},{8,4},{12,24},{16,28},{20,0},{24,20},{28,8},{1,13},{... | collective-permute-start | bytes 1179656 | tf_op jit(solution)/shard_map/ppermute | solution.py:456
  37.5 20.2 %collective-permute-start.12 = (bf16[256,768]{1,0:T(8,128)(2,1)S(1)}, bf16[256,768]{1,0:T(8,128)(2,1)S(1)}, u32[]{:S(2)}, u32[]{:S(2)}) collective-permute-start(bf16[256,768]{1,0:T(8,128)(2,1)S(1)} %get-tuple-element.53), channel_id=1, source_target_pairs={{0,16},{4,12},{8,24},{12,4},{16,0},{20,28},{24,8},{28,20},{1,17},{... | collective-permute-start | bytes 1179656 | tf_op jit(solution)/shard_map/ppermute | solution.py:456
  37.8 19.9 %collective-permute-start.13 = (bf16[256,768]{1,0:T(8,128)(2,1)S(1)}, bf16[256,768]{1,0:T(8,128)(2,1)S(1)}, u32[]{:S(2)}, u32[]{:S(2)}) collective-permute-start(bf16[256,768]{1,0:T(8,128)(2,1)S(1)} %get-tuple-element.54), channel_id=1, source_target_pairs={{0,20},{4,8},{8,28},{12,0},{16,4},{20,24},{24,12},{28,16},{1,21},{... | collective-permute-start | bytes 1179656 | tf_op jit(solution)/shard_map/ppermute | solution.py:456
  42.9 28.8 %copy-start.4 = (f32[256]{0:T(256)S(1)}, f32[256]{0:T(256)}, u32[]{:S(2)}) copy-start(f32[256]{0:T(256)} %param.16) | copy-start | bytes 3076
  42.9 14.8 %collective-permute-start.6 = (f32[1,2048]{1,0:T(1,128)S(1)}, f32[1,2048]{1,0:T(1,128)S(1)}, u32[]{:S(2)}, u32[]{:S(2)}) collective-permute-start(f32[1,2048]{1,0:T(1,128)S(1)} %get-tuple-element.48.refs_8_.rest_0_), channel_id=1, source_target_pairs={{0,1},{1,2},{2,3},{3,0},{4,5},{5,6},{6,7},{7,4},{8,9},{9,10},{10,1... | collective-permute-start | bytes 24584 | tf_op jit(solution)/shard_map/ppermute | solution.py:488
  45.1 12.6 %collective-permute-start.7 = (f32[1,2048]{1,0:T(1,128)S(1)}, f32[1,2048]{1,0:T(1,128)S(1)}, u32[]{:S(2)}, u32[]{:S(2)}) collective-permute-start(f32[1,2048]{1,0:T(1,128)S(1)} %get-tuple-element.48.refs_8_.rest_0_), channel_id=1, source_target_pairs={{0,2},{1,3},{2,0},{3,1},{4,6},{5,7},{6,4},{7,5},{8,10},{9,11},{10,... | collective-permute-start | bytes 24584 | tf_op jit(solution)/shard_map/ppermute | solution.py:488
  52.4 6.7 %collective-permute-start.8 = (f32[1,2048]{1,0:T(1,128)S(1)}, f32[1,2048]{1,0:T(1,128)S(1)}, u32[]{:S(2)}, u32[]{:S(2)}) collective-permute-start(f32[1,2048]{1,0:T(1,128)S(1)} %get-tuple-element.48.refs_8_.rest_0_), channel_id=1, source_target_pairs={{0,3},{1,0},{2,1},{3,2},{4,7},{5,4},{6,5},{7,6},{8,11},{9,8},{10,9... | collective-permute-start | bytes 24584 | tf_op jit(solution)/shard_map/ppermute | solution.py:488
  60.6 6.8 %collective-permute-start.14 = (bf16[256,256]{1,0:T(8,128)(2,1)S(1)}, bf16[256,256]{1,0:T(8,128)(2,1)S(1)}, u32[]{:S(2)}, u32[]{:S(2)}) collective-permute-start(bf16[256,256]{1,0:T(8,128)(2,1)S(1)} %get-tuple-element.55), channel_id=1, source_target_pairs={{28,0},{24,4},{20,8},{16,12},{12,16},{8,20},{4,24},{0,28},{29,1},{... | collective-permute-start | bytes 393224 | tf_op jit(solution)/shard_map/ppermute | solution.py:461
  61.3 8.3 %collective-permute-start.15 = (bf16[256,256]{1,0:T(8,128)(2,1)S(1)}, bf16[256,256]{1,0:T(8,128)(2,1)S(1)}, u32[]{:S(2)}, u32[]{:S(2)}) collective-permute-start(bf16[256,256]{1,0:T(8,128)(2,1)S(1)} %get-tuple-element.56), channel_id=1, source_target_pairs={{24,0},{28,4},{16,8},{20,12},{8,16},{12,20},{0,24},{4,28},{25,1},{... | collective-permute-start | bytes 393224 | tf_op jit(solution)/shard_map/ppermute | solution.py:461
  62.7 9.0 %collective-permute-start.16 = (bf16[256,256]{1,0:T(8,128)(2,1)S(1)}, bf16[256,256]{1,0:T(8,128)(2,1)S(1)}, u32[]{:S(2)}, u32[]{:S(2)}) collective-permute-start(bf16[256,256]{1,0:T(8,128)(2,1)S(1)} %get-tuple-element.57), channel_id=1, source_target_pairs={{4,0},{0,4},{12,8},{8,12},{20,16},{16,20},{28,24},{24,28},{5,1},{1... | collective-permute-start | bytes 393224 | tf_op jit(solution)/shard_map/ppermute | solution.py:461
  63.4 9.5 %collective-permute-start.17 = (bf16[256,256]{1,0:T(8,128)(2,1)S(1)}, bf16[256,256]{1,0:T(8,128)(2,1)S(1)}, u32[]{:S(2)}, u32[]{:S(2)}) collective-permute-start(bf16[256,256]{1,0:T(8,128)(2,1)S(1)} %get-tuple-element.59), channel_id=1, source_target_pairs={{20,0},{8,4},{28,8},{0,12},{4,16},{24,20},{12,24},{16,28},{21,1},{... | collective-permute-start | bytes 393224 | tf_op jit(solution)/shard_map/ppermute | solution.py:461
  65.1 7.9 %collective-permute-start.18 = (bf16[256,256]{1,0:T(8,128)(2,1)S(1)}, bf16[256,256]{1,0:T(8,128)(2,1)S(1)}, u32[]{:S(2)}, u32[]{:S(2)}) collective-permute-start(bf16[256,256]{1,0:T(8,128)(2,1)S(1)} %get-tuple-element.60), channel_id=1, source_target_pairs={{16,0},{12,4},{24,8},{4,12},{0,16},{28,20},{8,24},{20,28},{17,1},{... | collective-permute-start | bytes 393224 | tf_op jit(solution)/shard_map/ppermute | solution.py:461
  67.4 6.2 %collective-permute-start.19 = (bf16[256,256]{1,0:T(8,128)(2,1)S(1)}, bf16[256,256]{1,0:T(8,128)(2,1)S(1)}, u32[]{:S(2)}, u32[]{:S(2)}) collective-permute-start(bf16[256,256]{1,0:T(8,128)(2,1)S(1)} %get-tuple-element.61), channel_id=1, source_target_pairs={{12,0},{16,4},{4,8},{24,12},{28,16},{0,20},{20,24},{8,28},{13,1},{... | collective-permute-start | bytes 393224 | tf_op jit(solution)/shard_map/ppermute | solution.py:461
  69.7 5.0 %collective-permute-start.20 = (bf16[256,256]{1,0:T(8,128)(2,1)S(1)}, bf16[256,256]{1,0:T(8,128)(2,1)S(1)}, u32[]{:S(2)}, u32[]{:S(2)}) collective-permute-start(bf16[256,256]{1,0:T(8,128)(2,1)S(1)} %get-tuple-element.62), channel_id=1, source_target_pairs={{8,0},{20,4},{0,8},{28,12},{24,16},{4,20},{16,24},{12,28},{9,1},{2... | collective-permute-start | bytes 393224 | tf_op jit(solution)/shard_map/ppermute | solution.py:461

commit v7 on v6

--- a/solution.py
+++ b/solution.py
@@ -387,13 +387,10 @@
     return total
 
 
-def base_kernel(heads, gain_ref, y_ref, onehot, *rest):
-    squares, blocks, out_ref = rest[:heads], rest[heads:-1], rest[-1]
+def base_kernel(heads, gain_ref, y_ref, onehot, total_ref, *rest):
+    blocks, out_ref = rest[:-1], rest[-1]
     count, width = y_ref.shape
-    total = squares[0][...]
-    for ref in squares[1:]:
-        total = total + ref[...]
-    inverse = 1.0 / jnp.sqrt(total / (width * heads) + EPSILON)
+    inverse = 1.0 / jnp.sqrt(total_ref[...] / (width * heads) + EPSILON)
     gain = gain_ref[...]
     tile = min(count, TILE)
     for low in range(0, count, tile):
@@ -405,19 +402,18 @@
             out_ref[here, :] = y_ref[here, :] * norm * gain + part[at : at + LANES]
 
 
-def base(gain, y, onehot, squares, blocks):
+def base(gain, y, onehot, total, heads, blocks):
     count, width = y.shape
-    heads = len(squares)
     moved = len(blocks) * blocks[0].shape[0]
     return pl.pallas_call(
         functools.partial(base_kernel, heads),
         out_shape=jax.ShapeDtypeStruct((count, width), F32),
-        in_specs=full(3 + heads + len(blocks)),
+        in_specs=full(4 + len(blocks)),
         out_specs=pl.BlockSpec(memory_space=pltpu.VMEM),
         compiler_params=params(),
         cost_estimate=cost(2 * count * moved * width, 8 * count * width),
         name="base",
-    )(gain, y, onehot, *squares, *blocks)
+    )(gain, y, onehot, total, *blocks)
 
 
 def mix_kernel(base_ref, onehot, *rest):
@@ -450,6 +446,17 @@
         cost_estimate=cost(2 * count * moved * width, 8 * count * width),
         name="mix",
     )(given, onehot, *blocks)
+
+
+def sum_over_heads(square, heads):
+    if not power_of_two(heads):
+        return lax.psum(square, "head")
+    step = 1
+    while step < heads:
+        pairs = [(at, at ^ step) for at in range(heads)]
+        square = square + lax.ppermute(square, "head", pairs)
+        step *= 2
+    return square
 
 
 def exchange(block, step, n):
@@ -484,14 +491,11 @@
     late = steps[few : n - few]
     early_places, late_places = place(order, n, early + late)
     y, square = read_out(queries, *weights, summed, [late_places])
-    squares = [square] + [
-        lax.ppermute(square, "head", [(at, (at + step) % heads) for at in range(heads)])
-        for step in range(1, heads)
-    ]
-    attended = attend([arrived[step] for step in range(n)], squares, n, width)
+    total = sum_over_heads(square, heads)
+    attended = attend([arrived[step] for step in range(n)], [total], n, width)
     returned = {step: give_back(attended[step], step, n) for step in early + late}
     given = base(
-        gain.reshape(1, width), y, early_places, squares, [returned[step] for step in early]
+        gain.reshape(1, width), y, early_places, total, heads, [returned[step] for step in early]
     )
     return mix(given, late_places, [returned[step] for step in late])
 

time: 77.3 us -> 84.3 us (1.091)
  waiting for transfers between devices: 25 us -> 39.3 us
  starting transfers between devices: 29.7 us -> 22.3 us
    ppermute x7, waiting for transfers between devices: 16 us -> 29.6 us  [exchange(): return lax.ppermute(block, 'cam', routes(step, n)) if step else block]
    ppermute x3 -> x2, starting transfers between devices: 10.3 us -> 4.29 us  [sum_over_heads(): square = square + lax.ppermute(square, 'head', pairs)]
    ppermute x7, waiting for transfers between devices: 5.62 us -> 6.83 us  [give_back(): return lax.ppermute(block, 'cam', pairs) if step else block]
    ppermute x2, waiting for transfers between devices: 2 us -> 0.8 us  [sum_over_chips(): got = lax.ppermute(mine.astype(BF16), 'cam', pairs)]
    ppermute x7, starting transfers between devices: 7.09 us -> 6.16 us  [give_back(): return lax.ppermute(block, 'cam', pairs) if step else block]
    ppermute x3 -> x2, waiting for transfers between devices: 1.35 us -> 2.07 us  [sum_over_heads(): square = square + lax.ppermute(square, 'head', pairs)]
  transfers between devices with their start and end apart: 21 -> 20, of which waited for: 10 -> 11; matrix products, arithmetic and copies ran while one was open for 0% -> 0% of each run, Pallas kernels for 17% -> 12%
where the time goes in v7:
time: 84.3 us; the launch traced here: 84 us
  waiting for transfers between devices  39.3 us (47%)
  starting transfers between devices  22.3 us (26%)
  Pallas kernels  20.9 us (25%)
  local copies, waits for them, and re-layouts  0.99 us (1%)
    ppermute x7, waiting for transfers between devices, exchange(): return lax.ppermute(block, 'cam', routes(step, n)) if step else block  29.6 us
    pallas_call x3, Pallas kernels, sort_tokens(): pl.pallas_call(functools.partial(sort_kernel, size), out_shape=[jax.Shape...  7.06 us
    ppermute x7, waiting for transfers between devices, give_back(): return lax.ppermute(block, 'cam', pairs) if step else block  6.83 us
    ppermute x7, starting transfers between devices, exchange(): return lax.ppermute(block, 'cam', routes(step, n)) if step else block  6.26 us
    ppermute x7, starting transfers between devices, give_back(): return lax.ppermute(block, 'cam', pairs) if step else block  6.16 us
    ppermute x2, starting transfers between devices, sum_over_chips(): got = lax.ppermute(mine.astype(BF16), 'cam', pairs)  5 us
    ppermute x2, starting transfers between devices, sum_over_heads(): square = square + lax.ppermute(square, 'head', pairs)  4.29 us
    pallas_call x1, Pallas kernels, gradients(): pl.pallas_call(functools.partial(grads_kernel, n, split), out_shape=[jax....  2.87 us
  transfers between devices with their start and end apart: 20, of which 11 were waited for; matrix products, arithmetic and copies ran while one was open for 0% of the time, Pallas kernels for 12%

profile of v7, /device:TPU:0, one launch (start us, length us, event | category | flops | bytes accessed | tf_op | source)
XLA Modules:
  0.0 84.0 jit_solution(7667316987899218916)
XLA Ops:
  0.7 1.4 %mark.1 = (bf16[512,2048]{1,0:T(8,128)(2,1)S(1)}, bf16[512,2048]{1,0:T(8,128)(2,1)S(1)}, bf16[1024,2048]{1,0:T(8,128)(2,1)S(1)}, f32[8,128]{1,0:T(8,128)S(1)}) custom-call(s32[1,2048]{1,0:T(1,128)S(1)} %copy-done.8), custom_call_target="tpu_custom_call" | custom-call | flops 999999995904 | bytes 1024 | tf_op jit(solution)/shard_map/mark/pallas_call | solution.py:107
  2.5 2.9 %gradients.1 = (f32[384,256]{1,0:T(8,128)S(1)}, f32[384,256]{1,0:T(8,128)S(1)}) custom-call(bf16[2048,256]{1,0:T(8,128)(2,1)S(1)} %copy-done.5, bf16[2048,256]{1,0:T(8,128)(2,1)S(1)} %copy-done.6, f32[1,2048]{1,0:T(1,128)S(1)} %bitcast.3, bf16[1,256,256]{2,1,0:T(8,128)(2,1)S(1)} %copy-done.1, bf16[1,256,256]{2,1,0:T(8,128)(2,1)S(1)} %copy-done.2, ...), custom_call_target="tpu_custom_call" | custom-call | flops 1610612736 | bytes 4194304 | tf_op jit(solution)/shard_map/gradients/pallas_call | solution.py:235
  5.9 1.8 %sort_tokens.3 = (bf16[256,768]{1,0:T(8,128)(2,1)S(1)}, bf16[256,768]{1,0:T(8,128)(2,1)S(1)}, f32[8,128]{1,0:T(8,128)S(1)}) custom-call(bf16[512,2048]{1,0:T(8,128)(2,1)S(1)} %get-tuple-element.37.onehot, bf16[2048,256]{1,0:T(8,128)(2,1)S(1)} %copy-done, bf16[2048,256]{1,0:T(8,128)(2,1)S(1)} %copy-done.5, bf16[2048,256]{1,0:T(8,128)(2,1)S(1)} %copy-done.6), custom_call_target="tpu_custom_call" | custom-call | flops 1610612736 | bytes 3145728 | tf_op jit(solution)/shard_map/sort_tokens/pallas_call | solution.py:140
  7.8 2.6 %collective-permute-start.1 = (bf16[384,256]{1,0:T(8,128)(2,1)S(1)}, bf16[384,256]{1,0:T(8,128)(2,1)S(1)}, u32[]{:S(2)}, u32[]{:S(2)}) collective-permute-start(bf16[384,256]{1,0:T(8,128)(2,1)S(1)} %convert_element_type.6), channel_id=1, source_target_pairs={{0,8},{4,20},{8,0},{12,28},{16,24},{20,4},{24,16},{28,12},{1,9},{5... | collective-permute-start | bytes 589832 | tf_op jit(solution)/shard_map/ppermute | solution.py:279
  10.3 1.3 %collective-permute-start.3 = (bf16[256,768]{1,0:T(8,128)(2,1)S(1)}, bf16[256,768]{1,0:T(8,128)(2,1)S(1)}, u32[]{:S(2)}, u32[]{:S(2)}) collective-permute-start(bf16[256,768]{1,0:T(8,128)(2,1)S(1)} %get-tuple-element.41), channel_id=1, source_target_pairs={{0,28},{4,24},{8,20},{12,16},{16,12},{20,8},{24,4},{28,0},{1,29},{... | collective-permute-start | bytes 1179656 | tf_op jit(solution)/shard_map/ppermute | solution.py:463
  11.6 1.5 %collective-permute-start.4 = (bf16[256,768]{1,0:T(8,128)(2,1)S(1)}, bf16[256,768]{1,0:T(8,128)(2,1)S(1)}, u32[]{:S(2)}, u32[]{:S(2)}) collective-permute-start(bf16[256,768]{1,0:T(8,128)(2,1)S(1)} %get-tuple-element.42), channel_id=1, source_target_pairs={{0,24},{4,28},{8,16},{12,20},{16,8},{20,12},{24,0},{28,4},{1,25},{... | collective-permute-start | bytes 1179656 | tf_op jit(solution)/shard_map/ppermute | solution.py:463
  13.1 1.8 %sort_tokens.4 = (bf16[256,768]{1,0:T(8,128)(2,1)S(1)}, bf16[256,768]{1,0:T(8,128)(2,1)S(1)}, f32[8,128]{1,0:T(8,128)S(1)}) custom-call(bf16[512,2048]{1,0:T(8,128)(2,1)S(1)} %get-tuple-element.39.onehot, bf16[2048,256]{1,0:T(8,128)(2,1)S(1)} %copy-done, bf16[2048,256]{1,0:T(8,128)(2,1)S(1)} %copy-done.5, bf16[2048,256]{1,0:T(8,128)(2,1)S(1)} %copy-done.6), custom_call_target="tpu_custom_call" | custom-call | flops 1610612736 | bytes 3145728 | tf_op jit(solution)/shard_map/sort_tokens/pallas_call | solution.py:140
  15.0 2.4 %collective-permute-start.2 = (bf16[384,256]{1,0:T(8,128)(2,1)S(1)}, bf16[384,256]{1,0:T(8,128)(2,1)S(1)}, u32[]{:S(2)}, u32[]{:S(2)}) collective-permute-start(bf16[384,256]{1,0:T(8,128)(2,1)S(1)} %convert_element_type.7), channel_id=1, source_target_pairs={{0,16},{4,12},{8,24},{12,4},{16,0},{20,28},{24,8},{28,20},{1,17},{... | collective-permute-start | bytes 589832 | tf_op jit(solution)/shard_map/ppermute | solution.py:279
  17.4 3.5 %sort_tokens.5 = (bf16[256,768]{1,0:T(8,128)(2,1)S(1)}, bf16[256,768]{1,0:T(8,128)(2,1)S(1)}, bf16[256,768]{1,0:T(8,128)(2,1)S(1)}, bf16[256,768]{1,0:T(8,128)(2,1)S(1)}, f32[8,128]{1,0:T(8,128)S(1)}) custom-call(bf16[1024,2048]{1,0:T(8,128)(2,1)S(1)} %get-tuple-element.43.onehot, bf16[2048,256]{1,0:T(8,128)(2,1)S(1)} %copy-done, ...), custom_call_target="tpu_custom_call" | custom-call | flops 3221225472 | bytes 3145728 | tf_op jit(solution)/shard_map/sort_tokens/pallas_call | solution.py:140
  20.9 2.3 %collective-permute-done.3.rest_0_.refs_7_ = bf16[256,768]{1,0:T(8,128)(2,1)S(1)} collective-permute-done((bf16[256,768]{1,0:T(8,128)(2,1)S(1)}, bf16[256,768]{1,0:T(8,128)(2,1)S(1)}, u32[]{:S(2)}, u32[]{:S(2)}) %collective-permute-start.3) | collective-permute-done | bytes 393248 | tf_op jit(solution)/shard_map/ppermute | solution.py:463
  23.1 10.5 %collective-permute-done.4.rest_1_.refs_6_ = bf16[256,768]{1,0:T(8,128)(2,1)S(1)} collective-permute-done((bf16[256,768]{1,0:T(8,128)(2,1)S(1)}, bf16[256,768]{1,0:T(8,128)(2,1)S(1)}, u32[]{:S(2)}, u32[]{:S(2)}) %collective-permute-start.4) | collective-permute-done | bytes 393248 | tf_op jit(solution)/shard_map/ppermute | solution.py:463
  33.6 0.8 collective-permute-done.2.got_ref
  34.6 1.7 %place.1 = (bf16[2048,1024]{1,0:T(8,128)(2,1)S(1)}, bf16[2048,1024]{1,0:T(8,128)(2,1)S(1)}) custom-call(s32[1,2048]{1,0:T(1,128)S(1)} %copy-done.9), custom_call_target="tpu_custom_call" | custom-call | flops 4194304 | bytes 8388608 | tf_op jit(solution)/shard_map/place/pallas_call | solution.py:370
  36.3 2.9 %read_out.1 = (f32[2048,256]{1,0:T(8,128)S(1)}, f32[1,2048]{1,0:T(1,128)S(1)}) custom-call(bf16[2048,256]{1,0:T(8,128)(2,1)S(1)} %copy-done, bf16[1,256,256]{2,1,0:T(8,128)(2,1)S(1)} %copy-done.1, bf16[1,256,256]{2,1,0:T(8,128)(2,1)S(1)} %copy-done.2, bf16[1,256,256]{2,1,0:T(8,128)(2,1)S(1)} %copy-done.3, f32[384,256]{1,0:T(8,128)S(1)} %merge.5.rest_0_, ...), custom_call_target="tpu_custom_call" | custom-call | flops 805306368 | bytes 4194304 | tf_op jit(solution)/shard_map/read_out/pallas_call | solution.py:331
  39.1 1.6 %collective-permute-start.6 = (f32[1,2048]{1,0:T(1,128)S(1)}, f32[1,2048]{1,0:T(1,128)S(1)}, u32[]{:S(2)}, u32[]{:S(2)}) collective-permute-start(f32[1,2048]{1,0:T(1,128)S(1)} %get-tuple-element.48), channel_id=1, source_target_pairs={{0,1},{1,0},{2,3},{3,2},{4,5},{5,4},{6,7},{7,6},{8,9},{9,8},{10,11... | collective-permute-start | bytes 24584 | tf_op jit(solution)/shard_map/ppermute | solution.py:457
  40.7 2.1 %collective-permute-done.6 = f32[1,2048]{1,0:T(1,128)S(1)} collective-permute-done((f32[1,2048]{1,0:T(1,128)S(1)}, f32[1,2048]{1,0:T(1,128)S(1)}, u32[]{:S(2)}, u32[]{:S(2)}) %collective-permute-start.6) | collective-permute-done | bytes 8224 | tf_op jit(solution)/shard_map/ppermute | solution.py:457
  42.8 2.7 %collective-permute-start.7 = (f32[1,2048]{1,0:T(1,128)S(1)}, f32[1,2048]{1,0:T(1,128)S(1)}, u32[]{:S(2)}, u32[]{:S(2)}) collective-permute-start(f32[1,2048]{1,0:T(1,128)S(1)} %add.6), channel_id=1, source_target_pairs={{0,2},{1,3},{2,0},{3,1},{4,6},{5,7},{6,4},{7,5},{8,10},{9,11},{10,... | collective-permute-start | bytes 24584 | tf_op jit(solution)/shard_map/ppermute | solution.py:457
  45.5 1.4 %collective-permute-start.9 = (bf16[256,768]{1,0:T(8,128)(2,1)S(1)}, bf16[256,768]{1,0:T(8,128)(2,1)S(1)}, u32[]{:S(2)}, u32[]{:S(2)}) collective-permute-start(bf16[256,768]{1,0:T(8,128)(2,1)S(1)} %get-tuple-element.51), channel_id=1, source_target_pairs={{0,8},{4,20},{8,0},{12,28},{16,24},{20,4},{24,16},{28,12},{1,9},{5... | collective-permute-start | bytes 1179656 | tf_op jit(solution)/shard_map/ppermute | solution.py:463
  47.3 1.4 %collective-permute-start.11 = (bf16[256,768]{1,0:T(8,128)(2,1)S(1)}, bf16[256,768]{1,0:T(8,128)(2,1)S(1)}, u32[]{:S(2)}, u32[]{:S(2)}) collective-permute-start(bf16[256,768]{1,0:T(8,128)(2,1)S(1)} %get-tuple-element.53), channel_id=1, source_target_pairs={{0,16},{4,12},{8,24},{12,4},{16,0},{20,28},{24,8},{28,20},{1,17},{... | collective-permute-start | bytes 1179656 | tf_op jit(solution)/shard_map/ppermute | solution.py:463
  49.0 7.3 %collective-permute-done.9.refs_2_ = bf16[256,768]{1,0:T(8,128)(2,1)S(1)} collective-permute-done((bf16[256,768]{1,0:T(8,128)(2,1)S(1)}, bf16[256,768]{1,0:T(8,128)(2,1)S(1)}, u32[]{:S(2)}, u32[]{:S(2)}) %collective-permute-start.9) | collective-permute-done | bytes 393248 | tf_op jit(solution)/shard_map/ppermute | solution.py:463
  56.3 8.2 %collective-permute-done.10.refs_3_ = bf16[256,768]{1,0:T(8,128)(2,1)S(1)} collective-permute-done((bf16[256,768]{1,0:T(8,128)(2,1)S(1)}, bf16[256,768]{1,0:T(8,128)(2,1)S(1)}, u32[]{:S(2)}, u32[]{:S(2)}) %collective-permute-start.10) | collective-permute-done | bytes 393248 | tf_op jit(solution)/shard_map/ppermute | solution.py:463
  64.5 1.4 %collective-permute-done.12.refs_5_ = bf16[256,768]{1,0:T(8,128)(2,1)S(1)} collective-permute-done((bf16[256,768]{1,0:T(8,128)(2,1)S(1)}, bf16[256,768]{1,0:T(8,128)(2,1)S(1)}, u32[]{:S(2)}, u32[]{:S(2)}) %collective-permute-start.12) | collective-permute-done | bytes 393248 | tf_op jit(solution)/shard_map/ppermute | solution.py:463
  65.9 1.5 %attend.1 = (bf16[256,256]{1,0:T(8,128)(2,1)S(1)}, bf16[256,256]{1,0:T(8,128)(2,1)S(1)}, bf16[256,256]{1,0:T(8,128)(2,1)S(1)}, bf16[256,256]{1,0:T(8,128)(2,1)S(...) custom-call(bf16[256,768]{1,0:T(8,128)(2,1)S(1)} %get-tuple-element., ...), custom_call_target="tpu_custom_call" | custom-call | flops 536870912 | bytes 4194304 | tf_op jit(solution)/shard_map/attend/pallas_call | solution.py:179
  68.2 1.5 %collective-permute-start.14 = (bf16[256,256]{1,0:T(8,128)(2,1)S(1)}, bf16[256,256]{1,0:T(8,128)(2,1)S(1)}, u32[]{:S(2)}, u32[]{:S(2)}) collective-permute-start(bf16[256,256]{1,0:T(8,128)(2,1)S(1)} %get-tuple-element.56), channel_id=1, source_target_pairs={{24,0},{28,4},{16,8},{20,12},{8,16},{12,20},{0,24},{4,28},{25,1},{... | collective-permute-start | bytes 393224 | tf_op jit(solution)/shard_map/ppermute | solution.py:468
  70.3 1.1 %collective-permute-start.16 = (bf16[256,256]{1,0:T(8,128)(2,1)S(1)}, bf16[256,256]{1,0:T(8,128)(2,1)S(1)}, u32[]{:S(2)}, u32[]{:S(2)}) collective-permute-start(bf16[256,256]{1,0:T(8,128)(2,1)S(1)} %get-tuple-element.59), channel_id=1, source_target_pairs={{20,0},{8,4},{28,8},{0,12},{4,16},{24,20},{12,24},{16,28},{21,1},{... | collective-permute-start | bytes 393224 | tf_op jit(solution)/shard_map/ppermute | solution.py:468
  71.9 2.4 %collective-permute-done.13.rest_0_ = bf16[256,256]{1,0:T(8,128)(2,1)S(1)} collective-permute-done((bf16[256,256]{1,0:T(8,128)(2,1)S(1)}, bf16[256,256]{1,0:T(8,128)(2,1)S(1)}, u32[]{:S(2)}, u32[]{:S(2)}) %collective-permute-start.13) | collective-permute-done | bytes 131104 | tf_op jit(solution)/shard_map/ppermute | solution.py:468
  74.3 2.4 %collective-permute-done.14.rest_1_ = bf16[256,256]{1,0:T(8,128)(2,1)S(1)} collective-permute-done((bf16[256,256]{1,0:T(8,128)(2,1)S(1)}, bf16[256,256]{1,0:T(8,128)(2,1)S(1)}, u32[]{:S(2)}, u32[]{:S(2)}) %collective-permute-start.14) | collective-permute-done | bytes 131104 | tf_op jit(solution)/shard_map/ppermute | solution.py:468
  76.8 1.7 %collective-permute-start.19 = (bf16[256,256]{1,0:T(8,128)(2,1)S(1)}, bf16[256,256]{1,0:T(8,128)(2,1)S(1)}, u32[]{:S(2)}, u32[]{:S(2)}) collective-permute-start(bf16[256,256]{1,0:T(8,128)(2,1)S(1)} %get-tuple-element.62), channel_id=1, source_target_pairs={{8,0},{20,4},{0,8},{28,12},{24,16},{4,20},{16,24},{12,28},{9,1},{2... | collective-permute-start | bytes 393224 | tf_op jit(solution)/shard_map/ppermute | solution.py:468
  78.5 1.3 %base.1.base_ref = f32[2048,256]{1,0:T(8,128)S(1)} custom-call(f32[1,256]{1,0:T(1,128)S(1)} %bitcast.2, f32[2048,256]{1,0:T(8,128)S(1)} %get-tuple-element.46.y_ref, bf16[2048,1024]{1,0:T(8,128)(2,1)S(1)} %get-tuple-element.47.onehot, f32[1,2048]{1,0:T(1,128)S(1)} %add.7.refs_8_.total_ref, bf16[256,256]{1,0:T(8,128)(2,1)S(1)} %collective-permute-done.13.rest_0_, ...), custom_call_target="tpu_custom_call" | custom-call | flops 1073741824 | bytes 4194304 | tf_op jit(solution)/shard_map/base/pallas_call | solution.py:408
  79.8 0.9 %collective-permute-done.18.rest_2_ = bf16[256,256]{1,0:T(8,128)(2,1)S(1)} collective-permute-done((bf16[256,256]{1,0:T(8,128)(2,1)S(1)}, bf16[256,256]{1,0:T(8,128)(2,1)S(1)}, u32[]{:S(2)}, u32[]{:S(2)}) %collective-permute-start.18) | collective-permute-done | bytes 131104 | tf_op jit(solution)/shard_map/ppermute | solution.py:468
  80.7 1.1 %collective-permute-done.19.rest_3_ = bf16[256,256]{1,0:T(8,128)(2,1)S(1)} collective-permute-done((bf16[256,256]{1,0:T(8,128)(2,1)S(1)}, bf16[256,256]{1,0:T(8,128)(2,1)S(1)}, u32[]{:S(2)}, u32[]{:S(2)}) %collective-permute-start.19) | collective-permute-done | bytes 131104 | tf_op jit(solution)/shard_map/ppermute | solution.py:468
  81.7 2.1 %mix.1 = bf16[2048,256]{1,0:T(8,128)(2,1)} custom-call(f32[2048,256]{1,0:T(8,128)S(1)} %base.1.base_ref, bf16[2048,1024]{1,0:T(8,128)(2,1)S(1)} %get-tuple-element.45.rest_2_.onehot, bf16[256,256]{1,0:T(8,128)(2,1)S(1)} %collective-permute-done.16.rest_0_, bf16[256,256]{1,0:T(8,128)(2,1)S(1)} %collective-permute-done.17.rest_1_, ...), custom_call_target="tpu_custom_call" | custom-call | flops 1073741824 | bytes 4194304 | tf_op jit(solution)/shard_map/mix/pallas_call | solution.py:436
  (45 shorter events, 4.4 us)
Async XLA Ops:
  0.0 0.7 copy-start.8
  0.7 1.4 %copy-start.1 = (bf16[1,256,256]{2,1,0:T(8,128)(2,1)S(1)}, bf16[1,256,256]{2,1,0:T(8,128)(2,1)}, u32[]{:S(2)}) copy-start(bf16[1,256,256]{2,1,0:T(8,128)(2,1)} %one_ref.3) | copy-start | bytes 393220
  0.7 1.5 %copy-start.2 = (bf16[1,256,256]{2,1,0:T(8,128)(2,1)S(1)}, bf16[1,256,256]{2,1,0:T(8,128)(2,1)}, u32[]{:S(2)}) copy-start(bf16[1,256,256]{2,1,0:T(8,128)(2,1)} %three_ref.3) | copy-start | bytes 393220
  0.7 1.5 %copy-start.3 = (bf16[1,256,256]{2,1,0:T(8,128)(2,1)S(1)}, bf16[1,256,256]{2,1,0:T(8,128)(2,1)}, u32[]{:S(2)}) copy-start(bf16[1,256,256]{2,1,0:T(8,128)(2,1)} %two_ref.3) | copy-start | bytes 393220
  0.7 1.5 %copy-start.5 = (bf16[2048,256]{1,0:T(8,128)(2,1)S(1)}, bf16[2048,256]{1,0:T(8,128)(2,1)}, u32[]{:S(2)}) copy-start(bf16[2048,256]{1,0:T(8,128)(2,1)} %k_ref.7) | copy-start | bytes 3145732
  0.7 1.7 %copy-start.6 = (bf16[2048,256]{1,0:T(8,128)(2,1)S(1)}, bf16[2048,256]{1,0:T(8,128)(2,1)}, u32[]{:S(2)}) copy-start(bf16[2048,256]{1,0:T(8,128)(2,1)} %v_ref.7) | copy-start | bytes 3145732
  0.7 1.7 %copy-start.7 = (f32[2048,1]{0,1:T(1,128)S(1)}, f32[2048,1]{0,1:T(1,128)}, u32[]{:S(2)}) copy-start(f32[2048,1]{0,1:T(1,128)} %param.12) | copy-start | bytes 24580
  2.4 3.4 %copy-start = (bf16[2048,256]{1,0:T(8,128)(2,1)S(1)}, bf16[2048,256]{1,0:T(8,128)(2,1)}, u32[]{:S(2)}) copy-start(bf16[2048,256]{1,0:T(8,128)(2,1)} %q_ref.7) | copy-start | bytes 3145732
  5.3 2.3 %collective-permute-start = (f32[384,256]{1,0:T(8,128)S(1)}, f32[384,256]{1,0:T(8,128)S(1)}, u32[]{:S(2)}, u32[]{:S(2)}) collective-permute-start(f32[384,256]{1,0:T(8,128)S(1)} %get-tuple-element.36), channel_id=1, source_target_pairs={{0,4},{4,0},{8,12},{12,8},{16,20},{20,16},{24,28},{28,24},{1,5},{5... | collective-permute-start | bytes 1179656 | tf_op jit(solution)/shard_map/ppermute | solution.py:267
  7.8 7.2 %collective-permute-start.1 = (bf16[384,256]{1,0:T(8,128)(2,1)S(1)}, bf16[384,256]{1,0:T(8,128)(2,1)S(1)}, u32[]{:S(2)}, u32[]{:S(2)}) collective-permute-start(bf16[384,256]{1,0:T(8,128)(2,1)S(1)} %convert_element_type.6), channel_id=1, source_target_pairs={{0,8},{4,20},{8,0},{12,28},{16,24},{20,4},{24,16},{28,12},{1,9},{5... | collective-permute-start | bytes 589832 | tf_op jit(solution)/shard_map/ppermute | solution.py:279
  10.3 12.8 %collective-permute-start.3 = (bf16[256,768]{1,0:T(8,128)(2,1)S(1)}, bf16[256,768]{1,0:T(8,128)(2,1)S(1)}, u32[]{:S(2)}, u32[]{:S(2)}) collective-permute-start(bf16[256,768]{1,0:T(8,128)(2,1)S(1)} %get-tuple-element.41), channel_id=1, source_target_pairs={{0,28},{4,24},{8,20},{12,16},{16,12},{20,8},{24,4},{28,0},{1,29},{... | collective-permute-start | bytes 1179656 | tf_op jit(solution)/shard_map/ppermute | solution.py:463
  11.6 22.0 %collective-permute-start.4 = (bf16[256,768]{1,0:T(8,128)(2,1)S(1)}, bf16[256,768]{1,0:T(8,128)(2,1)S(1)}, u32[]{:S(2)}, u32[]{:S(2)}) collective-permute-start(bf16[256,768]{1,0:T(8,128)(2,1)S(1)} %get-tuple-element.42), channel_id=1, source_target_pairs={{0,24},{4,28},{8,16},{12,20},{16,8},{20,12},{24,0},{28,4},{1,25},{... | collective-permute-start | bytes 1179656 | tf_op jit(solution)/shard_map/ppermute | solution.py:463
  15.0 19.4 %collective-permute-start.2 = (bf16[384,256]{1,0:T(8,128)(2,1)S(1)}, bf16[384,256]{1,0:T(8,128)(2,1)S(1)}, u32[]{:S(2)}, u32[]{:S(2)}) collective-permute-start(bf16[384,256]{1,0:T(8,128)(2,1)S(1)} %convert_element_type.7), channel_id=1, source_target_pairs={{0,16},{4,12},{8,24},{12,4},{16,0},{20,28},{24,8},{28,20},{1,17},{... | collective-permute-start | bytes 589832 | tf_op jit(solution)/shard_map/ppermute | solution.py:279
  17.4 17.1 %copy-start.9 = (s32[1,2048]{1,0:T(1,128)S(1)}, s32[1,2048]{1,0:T(1,128)}, u32[]{:S(2)}) copy-start(s32[1,2048]{1,0:T(1,128)} %order_ref.3) | copy-start | bytes 24580
  34.5 1.8 %collective-permute-start.5 = (f32[384,256]{1,0:T(8,128)S(1)}, f32[384,256]{1,0:T(8,128)S(1)}, u32[]{:S(2)}, u32[]{:S(2)}) collective-permute-start(f32[384,256]{1,0:T(8,128)S(1)} %merge.5.rest_0_), channel_id=1, source_target_pairs={{0,4},{4,0},{8,12},{12,8},{16,20},{20,16},{24,28},{28,24},{1,5},{5... | collective-permute-start | bytes 1179656 | tf_op jit(solution)/shard_map/ppermute | solution.py:284
  39.1 39.3 %copy-start.4 = (f32[256]{0:T(256)S(1)}, f32[256]{0:T(256)}, u32[]{:S(2)}) copy-start(f32[256]{0:T(256)} %param.16) | copy-start | bytes 3076
  39.1 3.7 %collective-permute-start.6 = (f32[1,2048]{1,0:T(1,128)S(1)}, f32[1,2048]{1,0:T(1,128)S(1)}, u32[]{:S(2)}, u32[]{:S(2)}) collective-permute-start(f32[1,2048]{1,0:T(1,128)S(1)} %get-tuple-element.48), channel_id=1, source_target_pairs={{0,1},{1,0},{2,3},{3,2},{4,5},{5,4},{6,7},{7,6},{8,9},{9,8},{10,11... | collective-permute-start | bytes 24584 | tf_op jit(solution)/shard_map/ppermute | solution.py:457
  42.8 5.9 %collective-permute-start.7 = (f32[1,2048]{1,0:T(1,128)S(1)}, f32[1,2048]{1,0:T(1,128)S(1)}, u32[]{:S(2)}, u32[]{:S(2)}) collective-permute-start(f32[1,2048]{1,0:T(1,128)S(1)} %add.6), channel_id=1, source_target_pairs={{0,2},{1,3},{2,0},{3,1},{4,6},{5,7},{6,4},{7,5},{8,10},{9,11},{10,... | collective-permute-start | bytes 24584 | tf_op jit(solution)/shard_map/ppermute | solution.py:457
  45.5 3.5 %collective-permute-start.8 = (bf16[256,768]{1,0:T(8,128)(2,1)S(1)}, bf16[256,768]{1,0:T(8,128)(2,1)S(1)}, u32[]{:S(2)}, u32[]{:S(2)}) collective-permute-start(bf16[256,768]{1,0:T(8,128)(2,1)S(1)} %get-tuple-element.50), channel_id=1, source_target_pairs={{0,4},{4,0},{8,12},{12,8},{16,20},{20,16},{24,28},{28,24},{1,5},{5... | collective-permute-start | bytes 1179656 | tf_op jit(solution)/shard_map/ppermute | solution.py:463
  45.5 10.8 %collective-permute-start.9 = (bf16[256,768]{1,0:T(8,128)(2,1)S(1)}, bf16[256,768]{1,0:T(8,128)(2,1)S(1)}, u32[]{:S(2)}, u32[]{:S(2)}) collective-permute-start(bf16[256,768]{1,0:T(8,128)(2,1)S(1)} %get-tuple-element.51), channel_id=1, source_target_pairs={{0,8},{4,20},{8,0},{12,28},{16,24},{20,4},{24,16},{28,12},{1,9},{5... | collective-permute-start | bytes 1179656 | tf_op jit(solution)/shard_map/ppermute | solution.py:463
  46.9 17.6 %collective-permute-start.10 = (bf16[256,768]{1,0:T(8,128)(2,1)S(1)}, bf16[256,768]{1,0:T(8,128)(2,1)S(1)}, u32[]{:S(2)}, u32[]{:S(2)}) collective-permute-start(bf16[256,768]{1,0:T(8,128)(2,1)S(1)} %get-tuple-element.52), channel_id=1, source_target_pairs={{0,12},{4,16},{8,4},{12,24},{16,28},{20,0},{24,20},{28,8},{1,13},{... | collective-permute-start | bytes 1179656 | tf_op jit(solution)/shard_map/ppermute | solution.py:463
  47.3 17.2 %collective-permute-start.11 = (bf16[256,768]{1,0:T(8,128)(2,1)S(1)}, bf16[256,768]{1,0:T(8,128)(2,1)S(1)}, u32[]{:S(2)}, u32[]{:S(2)}) collective-permute-start(bf16[256,768]{1,0:T(8,128)(2,1)S(1)} %get-tuple-element.53), channel_id=1, source_target_pairs={{0,16},{4,12},{8,24},{12,4},{16,0},{20,28},{24,8},{28,20},{1,17},{... | collective-permute-start | bytes 1179656 | tf_op jit(solution)/shard_map/ppermute | solution.py:463
  48.8 17.1 %collective-permute-start.12 = (bf16[256,768]{1,0:T(8,128)(2,1)S(1)}, bf16[256,768]{1,0:T(8,128)(2,1)S(1)}, u32[]{:S(2)}, u32[]{:S(2)}) collective-permute-start(bf16[256,768]{1,0:T(8,128)(2,1)S(1)} %get-tuple-element.54), channel_id=1, source_target_pairs={{0,20},{4,8},{8,28},{12,0},{16,4},{20,24},{24,12},{28,16},{1,21},{... | collective-permute-start | bytes 1179656 | tf_op jit(solution)/shard_map/ppermute | solution.py:463
  67.4 6.9 %collective-permute-start.13 = (bf16[256,256]{1,0:T(8,128)(2,1)S(1)}, bf16[256,256]{1,0:T(8,128)(2,1)S(1)}, u32[]{:S(2)}, u32[]{:S(2)}) collective-permute-start(bf16[256,256]{1,0:T(8,128)(2,1)S(1)} %get-tuple-element.55), channel_id=1, source_target_pairs={{28,0},{24,4},{20,8},{16,12},{12,16},{8,20},{4,24},{0,28},{29,1},{... | collective-permute-start | bytes 393224 | tf_op jit(solution)/shard_map/ppermute | solution.py:468
  68.2 8.6 %collective-permute-start.14 = (bf16[256,256]{1,0:T(8,128)(2,1)S(1)}, bf16[256,256]{1,0:T(8,128)(2,1)S(1)}, u32[]{:S(2)}, u32[]{:S(2)}) collective-permute-start(bf16[256,256]{1,0:T(8,128)(2,1)S(1)} %get-tuple-element.56), channel_id=1, source_target_pairs={{24,0},{28,4},{16,8},{20,12},{8,16},{12,20},{0,24},{4,28},{25,1},{... | collective-permute-start | bytes 393224 | tf_op jit(solution)/shard_map/ppermute | solution.py:468
  69.7 8.8 %collective-permute-start.15 = (bf16[256,256]{1,0:T(8,128)(2,1)S(1)}, bf16[256,256]{1,0:T(8,128)(2,1)S(1)}, u32[]{:S(2)}, u32[]{:S(2)}) collective-permute-start(bf16[256,256]{1,0:T(8,128)(2,1)S(1)} %get-tuple-element.57), channel_id=1, source_target_pairs={{4,0},{0,4},{12,8},{8,12},{20,16},{16,20},{28,24},{24,28},{5,1},{1... | collective-permute-start | bytes 393224 | tf_op jit(solution)/shard_map/ppermute | solution.py:468
  70.3 9.5 %collective-permute-start.16 = (bf16[256,256]{1,0:T(8,128)(2,1)S(1)}, bf16[256,256]{1,0:T(8,128)(2,1)S(1)}, u32[]{:S(2)}, u32[]{:S(2)}) collective-permute-start(bf16[256,256]{1,0:T(8,128)(2,1)S(1)} %get-tuple-element.59), channel_id=1, source_target_pairs={{20,0},{8,4},{28,8},{0,12},{4,16},{24,20},{12,24},{16,28},{21,1},{... | collective-permute-start | bytes 393224 | tf_op jit(solution)/shard_map/ppermute | solution.py:468
  71.3 8.4 %collective-permute-start.17 = (bf16[256,256]{1,0:T(8,128)(2,1)S(1)}, bf16[256,256]{1,0:T(8,128)(2,1)S(1)}, u32[]{:S(2)}, u32[]{:S(2)}) collective-permute-start(bf16[256,256]{1,0:T(8,128)(2,1)S(1)} %get-tuple-element.60), channel_id=1, source_target_pairs={{16,0},{12,4},{24,8},{4,12},{0,16},{28,20},{8,24},{20,28},{17,1},{... | collective-permute-start | bytes 393224 | tf_op jit(solution)/shard_map/ppermute | solution.py:468
  74.3 6.4 %collective-permute-start.18 = (bf16[256,256]{1,0:T(8,128)(2,1)S(1)}, bf16[256,256]{1,0:T(8,128)(2,1)S(1)}, u32[]{:S(2)}, u32[]{:S(2)}) collective-permute-start(bf16[256,256]{1,0:T(8,128)(2,1)S(1)} %get-tuple-element.61), channel_id=1, source_target_pairs={{12,0},{16,4},{4,8},{24,12},{28,16},{0,20},{20,24},{8,28},{13,1},{... | collective-permute-start | bytes 393224 | tf_op jit(solution)/shard_map/ppermute | solution.py:468
  76.8 5.0 %collective-permute-start.19 = (bf16[256,256]{1,0:T(8,128)(2,1)S(1)}, bf16[256,256]{1,0:T(8,128)(2,1)S(1)}, u32[]{:S(2)}, u32[]{:S(2)}) collective-permute-start(bf16[256,256]{1,0:T(8,128)(2,1)S(1)} %get-tuple-element.62), channel_id=1, source_target_pairs={{8,0},{20,4},{0,8},{28,12},{24,16},{4,20},{16,24},{12,28},{9,1},{2... | collective-permute-start | bytes 393224 | tf_op jit(solution)/shard_map/ppermute | solution.py:468

commit v8 on v7

--- a/solution.py
+++ b/solution.py
@@ -477,7 +477,6 @@
     weights = (w_one, w_three, w_two)
     groups = (tuple(steps[:few]), tuple(steps[few : 2 * few]), tuple(steps[2 * few :]))
     marks = mark(order, n, groups)
-    parts = gradients(keys, values, rates.reshape(1, count), *weights, marks[-1], n)
     arrived = {}
     tokens = []
     for group, onehot in zip(groups, marks):
@@ -485,12 +484,14 @@
         tokens.append(blocks[-1])
         for step, block in zip(group, blocks):
             arrived[step] = exchange(block, step, n)
+    came = [arrived[step] for step in steps]
+    parts = gradients(keys, values, rates.reshape(1, count), *weights, marks[-1], n)
     mine = core_step(parts, tokens[:1], n)
-    summed = sum_over_chips(mine, len(parts) == 2, [tokens[1:2], [arrived[s] for s in steps[:2]] + tokens[2:]], n)
+    summed = sum_over_chips(mine, len(parts) == 2, [tokens[1:2], came[:2] + tokens[2:]], n)
     early = steps[:few] + steps[n - few :]
     late = steps[few : n - few]
     early_places, late_places = place(order, n, early + late)
-    y, square = read_out(queries, *weights, summed, [late_places])
+    y, square = read_out(queries, *weights, summed, [late_places] + came[2:4])
     total = sum_over_heads(square, heads)
     attended = attend([arrived[step] for step in range(n)], [total], n, width)
     returned = {step: give_back(attended[step], step, n) for step in early + late}

time: 84.3 us -> 75.5 us (0.90)
  waiting for transfers between devices: 39.3 us -> 32.1 us
  starting transfers between devices: 22.3 us -> 21 us
    ppermute x7, waiting for transfers between devices: 29.6 us -> 11.9 us  [exchange(): return lax.ppermute(block, 'cam', routes(step, n)) if step else block]
    ppermute x2, waiting for transfers between devices: 0.8 us -> 9.22 us  [sum_over_chips(): got = lax.ppermute(mine.astype(BF16), 'cam', pairs)]
    ppermute x2, waiting for transfers between devices: 2.07 us -> 4.01 us  [sum_over_heads(): square = square + lax.ppermute(square, 'head', pairs)]
    ppermute x2, starting transfers between devices: 5 us -> 4.16 us  [sum_over_chips(): got = lax.ppermute(mine.astype(BF16), 'cam', pairs)]
  transfers between devices with their start and end apart: 20 -> 20, of which waited for: 11 -> 11; matrix products, arithmetic and copies ran while one was open for 0% -> 0% of each run, Pallas kernels for 12% -> 17%
where the time goes in v8:
time: 75.5 us; the launch traced here: 75.3 us
  waiting for transfers between devices  32.1 us (43%)
  starting transfers between devices  21 us (28%)
  Pallas kernels  20.8 us (28%)
  local copies, waits for them, and re-layouts  0.99 us (1%)
    ppermute x7, waiting for transfers between devices, exchange(): return lax.ppermute(block, 'cam', routes(step, n)) if step else block  11.9 us
    ppermute x2, waiting for transfers between devices, sum_over_chips(): got = lax.ppermute(mine.astype(BF16), 'cam', pairs)  9.22 us
    pallas_call x3, Pallas kernels, sort_tokens(): pl.pallas_call(functools.partial(sort_kernel, size), out_shape=[jax.Shape...  7.03 us
    ppermute x7, waiting for transfers between devices, give_back(): return lax.ppermute(block, 'cam', pairs) if step else block  6.9 us
    ppermute x7, starting transfers between devices, exchange(): return lax.ppermute(block, 'cam', routes(step, n)) if step else block  6.34 us
    ppermute x7, starting transfers between devices, give_back(): return lax.ppermute(block, 'cam', pairs) if step else block  5.65 us
    ppermute x2, starting transfers between devices, sum_over_heads(): square = square + lax.ppermute(square, 'head', pairs)  4.29 us
    ppermute x2, starting transfers between devices, sum_over_chips(): got = lax.ppermute(mine.astype(BF16), 'cam', pairs)  4.16 us
  transfers between devices with their start and end apart: 20, of which 11 were waited for; matrix products, arithmetic and copies ran while one was open for 0% of the time, Pallas kernels for 17%

profile of v8, /device:TPU:0, one launch (start us, length us, event | category | flops | bytes accessed | tf_op | source)
XLA Modules:
  0.0 75.3 jit_solution(12480811234309158737)
XLA Ops:
  0.0 0.7 copy-done.8
  0.7 1.4 %mark.1 = (bf16[512,2048]{1,0:T(8,128)(2,1)S(1)}, bf16[512,2048]{1,0:T(8,128)(2,1)S(1)}, bf16[1024,2048]{1,0:T(8,128)(2,1)S(1)}, f32[8,128]{1,0:T(8,128)S(1)}) custom-call(s32[1,2048]{1,0:T(1,128)S(1)} %copy-done.8), custom_call_target="tpu_custom_call" | custom-call | flops 999999995904 | bytes 1024 | tf_op jit(solution)/shard_map/mark/pallas_call | solution.py:107
  2.5 2.9 %gradients.1 = (f32[384,256]{1,0:T(8,128)S(1)}, f32[384,256]{1,0:T(8,128)S(1)}) custom-call(bf16[2048,256]{1,0:T(8,128)(2,1)S(1)} %copy-done.5, bf16[2048,256]{1,0:T(8,128)(2,1)S(1)} %copy-done.6, f32[1,2048]{1,0:T(1,128)S(1)} %bitcast.3, bf16[1,256,256]{2,1,0:T(8,128)(2,1)S(1)} %copy-done.1, bf16[1,256,256]{2,1,0:T(8,128)(2,1)S(1)} %copy-done.2, ...), custom_call_target="tpu_custom_call" | custom-call | flops 1610612736 | bytes 4194304 | tf_op jit(solution)/shard_map/gradients/pallas_call | solution.py:235
  5.9 1.8 %sort_tokens.3 = (bf16[256,768]{1,0:T(8,128)(2,1)S(1)}, bf16[256,768]{1,0:T(8,128)(2,1)S(1)}, f32[8,128]{1,0:T(8,128)S(1)}) custom-call(bf16[512,2048]{1,0:T(8,128)(2,1)S(1)} %get-tuple-element.37.onehot, bf16[2048,256]{1,0:T(8,128)(2,1)S(1)} %copy-done, bf16[2048,256]{1,0:T(8,128)(2,1)S(1)} %copy-done.5, bf16[2048,256]{1,0:T(8,128)(2,1)S(1)} %copy-done.6), custom_call_target="tpu_custom_call" | custom-call | flops 1610612736 | bytes 3145728 | tf_op jit(solution)/shard_map/sort_tokens/pallas_call | solution.py:140
  7.8 2.6 %collective-permute-start.1 = (bf16[384,256]{1,0:T(8,128)(2,1)S(1)}, bf16[384,256]{1,0:T(8,128)(2,1)S(1)}, u32[]{:S(2)}, u32[]{:S(2)}) collective-permute-start(bf16[384,256]{1,0:T(8,128)(2,1)S(1)} %convert_element_type.6), channel_id=1, source_target_pairs={{0,8},{4,20},{8,0},{12,28},{16,24},{20,4},{24,16},{28,12},{1,9},{5... | collective-permute-start | bytes 589832 | tf_op jit(solution)/shard_map/ppermute | solution.py:279
  10.3 1.3 %collective-permute-start.3 = (bf16[256,768]{1,0:T(8,128)(2,1)S(1)}, bf16[256,768]{1,0:T(8,128)(2,1)S(1)}, u32[]{:S(2)}, u32[]{:S(2)}) collective-permute-start(bf16[256,768]{1,0:T(8,128)(2,1)S(1)} %get-tuple-element.41), channel_id=1, source_target_pairs={{0,28},{4,24},{8,20},{12,16},{16,12},{20,8},{24,4},{28,0},{1,29},{... | collective-permute-start | bytes 1179656 | tf_op jit(solution)/shard_map/ppermute | solution.py:463
  11.6 1.5 %collective-permute-start.4 = (bf16[256,768]{1,0:T(8,128)(2,1)S(1)}, bf16[256,768]{1,0:T(8,128)(2,1)S(1)}, u32[]{:S(2)}, u32[]{:S(2)}) collective-permute-start(bf16[256,768]{1,0:T(8,128)(2,1)S(1)} %get-tuple-element.42), channel_id=1, source_target_pairs={{0,24},{4,28},{8,16},{12,20},{16,8},{20,12},{24,0},{28,4},{1,25},{... | collective-permute-start | bytes 1179656 | tf_op jit(solution)/shard_map/ppermute | solution.py:463
  13.1 1.8 %sort_tokens.4 = (bf16[256,768]{1,0:T(8,128)(2,1)S(1)}, bf16[256,768]{1,0:T(8,128)(2,1)S(1)}, f32[8,128]{1,0:T(8,128)S(1)}) custom-call(bf16[512,2048]{1,0:T(8,128)(2,1)S(1)} %get-tuple-element.39.onehot, bf16[2048,256]{1,0:T(8,128)(2,1)S(1)} %copy-done, bf16[2048,256]{1,0:T(8,128)(2,1)S(1)} %copy-done.5, bf16[2048,256]{1,0:T(8,128)(2,1)S(1)} %copy-done.6), custom_call_target="tpu_custom_call" | custom-call | flops 1610612736 | bytes 3145728 | tf_op jit(solution)/shard_map/sort_tokens/pallas_call | solution.py:140
  14.9 1.2 %collective-permute-start.6 = (bf16[256,768]{1,0:T(8,128)(2,1)S(1)}, bf16[256,768]{1,0:T(8,128)(2,1)S(1)}, u32[]{:S(2)}, u32[]{:S(2)}) collective-permute-start(bf16[256,768]{1,0:T(8,128)(2,1)S(1)} %get-tuple-element.46), channel_id=1, source_target_pairs={{0,20},{4,8},{8,28},{12,0},{16,4},{20,24},{24,12},{28,16},{1,21},{... | collective-permute-start | bytes 1179656 | tf_op jit(solution)/shard_map/ppermute | solution.py:463
  16.7 1.6 %collective-permute-start.2 = (bf16[384,256]{1,0:T(8,128)(2,1)S(1)}, bf16[384,256]{1,0:T(8,128)(2,1)S(1)}, u32[]{:S(2)}, u32[]{:S(2)}) collective-permute-start(bf16[384,256]{1,0:T(8,128)(2,1)S(1)} %convert_element_type.7), channel_id=1, source_target_pairs={{0,16},{4,12},{8,24},{12,4},{16,0},{20,28},{24,8},{28,20},{1,17},{... | collective-permute-start | bytes 589832 | tf_op jit(solution)/shard_map/ppermute | solution.py:279
  18.3 3.4 %sort_tokens.5 = (bf16[256,768]{1,0:T(8,128)(2,1)S(1)}, bf16[256,768]{1,0:T(8,128)(2,1)S(1)}, bf16[256,768]{1,0:T(8,128)(2,1)S(1)}, bf16[256,768]{1,0:T(8,128)(2,1)S(1)}, f32[8,128]{1,0:T(8,128)S(1)}) custom-call(bf16[1024,2048]{1,0:T(8,128)(2,1)S(1)} %get-tuple-element.43.onehot, bf16[2048,256]{1,0:T(8,128)(2,1)S(1)} %copy-done, ...), custom_call_target="tpu_custom_call" | custom-call | flops 3221225472 | bytes 3145728 | tf_op jit(solution)/shard_map/sort_tokens/pallas_call | solution.py:140
  21.7 1.4 %collective-permute-done.3.rest_0_.refs_7_ = bf16[256,768]{1,0:T(8,128)(2,1)S(1)} collective-permute-done((bf16[256,768]{1,0:T(8,128)(2,1)S(1)}, bf16[256,768]{1,0:T(8,128)(2,1)S(1)}, u32[]{:S(2)}, u32[]{:S(2)}) %collective-permute-start.3) | collective-permute-done | bytes 393248 | tf_op jit(solution)/shard_map/ppermute | solution.py:463
  23.1 10.5 %collective-permute-done.4.rest_1_.refs_6_ = bf16[256,768]{1,0:T(8,128)(2,1)S(1)} collective-permute-done((bf16[256,768]{1,0:T(8,128)(2,1)S(1)}, bf16[256,768]{1,0:T(8,128)(2,1)S(1)}, u32[]{:S(2)}, u32[]{:S(2)}) %collective-permute-start.4) | collective-permute-done | bytes 393248 | tf_op jit(solution)/shard_map/ppermute | solution.py:463
  33.6 9.2 %collective-permute-done.2.got_ref = bf16[384,256]{1,0:T(8,128)(2,1)S(1)} collective-permute-done((bf16[384,256]{1,0:T(8,128)(2,1)S(1)}, bf16[384,256]{1,0:T(8,128)(2,1)S(1)}, u32[]{:S(2)}, u32[]{:S(2)}) %collective-permute-start.2) | collective-permute-done | bytes 196640 | tf_op jit(solution)/shard_map/ppermute | solution.py:279
  44.2 0.7 collective-permute-start.12
  44.9 1.7 %place.1 = (bf16[2048,1024]{1,0:T(8,128)(2,1)S(1)}, bf16[2048,1024]{1,0:T(8,128)(2,1)S(1)}) custom-call(s32[1,2048]{1,0:T(1,128)S(1)} %copy-done.9), custom_call_target="tpu_custom_call" | custom-call | flops 4194304 | bytes 8388608 | tf_op jit(solution)/shard_map/place/pallas_call | solution.py:370
  46.6 2.7 %read_out.1 = (f32[2048,256]{1,0:T(8,128)S(1)}, f32[1,2048]{1,0:T(1,128)S(1)}) custom-call(bf16[2048,256]{1,0:T(8,128)(2,1)S(1)} %copy-done, bf16[1,256,256]{2,1,0:T(8,128)(2,1)S(1)} %copy-done.1, bf16[1,256,256]{2,1,0:T(8,128)(2,1)S(1)} %copy-done.2, bf16[1,256,256]{2,1,0:T(8,128)(2,1)S(1)} %copy-done.3, f32[384,256]{1,0:T(8,128)S(1)} %merge.5.rest_0_, ...), custom_call_target="tpu_custom_call" | custom-call | flops 805306368 | bytes 4194304 | tf_op jit(solution)/shard_map/read_out/pallas_call | solution.py:331
  49.3 1.6 %collective-permute-start.8 = (f32[1,2048]{1,0:T(1,128)S(1)}, f32[1,2048]{1,0:T(1,128)S(1)}, u32[]{:S(2)}, u32[]{:S(2)}) collective-permute-start(f32[1,2048]{1,0:T(1,128)S(1)} %get-tuple-element.50), channel_id=1, source_target_pairs={{0,1},{1,0},{2,3},{3,2},{4,5},{5,4},{6,7},{7,6},{8,9},{9,8},{10,11... | collective-permute-start | bytes 24584 | tf_op jit(solution)/shard_map/ppermute | solution.py:457
  50.9 2.1 %collective-permute-done.8 = f32[1,2048]{1,0:T(1,128)S(1)} collective-permute-done((f32[1,2048]{1,0:T(1,128)S(1)}, f32[1,2048]{1,0:T(1,128)S(1)}, u32[]{:S(2)}, u32[]{:S(2)}) %collective-permute-start.8) | collective-permute-done | bytes 8224 | tf_op jit(solution)/shard_map/ppermute | solution.py:457
  53.0 2.7 %collective-permute-start.9 = (f32[1,2048]{1,0:T(1,128)S(1)}, f32[1,2048]{1,0:T(1,128)S(1)}, u32[]{:S(2)}, u32[]{:S(2)}) collective-permute-start(f32[1,2048]{1,0:T(1,128)S(1)} %add.6), channel_id=1, source_target_pairs={{0,2},{1,3},{2,0},{3,1},{4,6},{5,7},{6,4},{7,5},{8,10},{9,11},{10,... | collective-permute-start | bytes 24584 | tf_op jit(solution)/shard_map/ppermute | solution.py:457
  55.6 1.9 %collective-permute-done.9 = f32[1,2048]{1,0:T(1,128)S(1)} collective-permute-done((f32[1,2048]{1,0:T(1,128)S(1)}, f32[1,2048]{1,0:T(1,128)S(1)}, u32[]{:S(2)}, u32[]{:S(2)}) %collective-permute-start.9) | collective-permute-done | bytes 8224 | tf_op jit(solution)/shard_map/ppermute | solution.py:457
  57.6 1.5 %attend.1 = (bf16[256,256]{1,0:T(8,128)(2,1)S(1)}, bf16[256,256]{1,0:T(8,128)(2,1)S(1)}, bf16[256,256]{1,0:T(8,128)(2,1)S(1)}, bf16[256,256]{1,0:T(8,128)(2,1)S(...) custom-call(bf16[256,768]{1,0:T(8,128)(2,1)S(1)} %get-tuple-element., ...), custom_call_target="tpu_custom_call" | custom-call | flops 536870912 | bytes 4194304 | tf_op jit(solution)/shard_map/attend/pallas_call | solution.py:179
  59.3 1.6 %collective-permute-start.14 = (bf16[256,256]{1,0:T(8,128)(2,1)S(1)}, bf16[256,256]{1,0:T(8,128)(2,1)S(1)}, u32[]{:S(2)}, u32[]{:S(2)}) collective-permute-start(bf16[256,256]{1,0:T(8,128)(2,1)S(1)} %get-tuple-element.56), channel_id=1, source_target_pairs={{24,0},{28,4},{16,8},{20,12},{8,16},{12,20},{0,24},{4,28},{25,1},{... | collective-permute-start | bytes 393224 | tf_op jit(solution)/shard_map/ppermute | solution.py:468
  60.8 1.2 %collective-permute-start.15 = (bf16[256,256]{1,0:T(8,128)(2,1)S(1)}, bf16[256,256]{1,0:T(8,128)(2,1)S(1)}, u32[]{:S(2)}, u32[]{:S(2)}) collective-permute-start(bf16[256,256]{1,0:T(8,128)(2,1)S(1)} %get-tuple-element.57), channel_id=1, source_target_pairs={{4,0},{0,4},{12,8},{8,12},{20,16},{16,20},{28,24},{24,28},{5,1},{1... | collective-permute-start | bytes 393224 | tf_op jit(solution)/shard_map/ppermute | solution.py:468
  62.2 1.4 %collective-permute-start.17 = (bf16[256,256]{1,0:T(8,128)(2,1)S(1)}, bf16[256,256]{1,0:T(8,128)(2,1)S(1)}, u32[]{:S(2)}, u32[]{:S(2)}) collective-permute-start(bf16[256,256]{1,0:T(8,128)(2,1)S(1)} %get-tuple-element.60), channel_id=1, source_target_pairs={{16,0},{12,4},{24,8},{4,12},{0,16},{28,20},{8,24},{20,28},{17,1},{... | collective-permute-start | bytes 393224 | tf_op jit(solution)/shard_map/ppermute | solution.py:468
  63.7 2.3 %collective-permute-done.13.rest_0_ = bf16[256,256]{1,0:T(8,128)(2,1)S(1)} collective-permute-done((bf16[256,256]{1,0:T(8,128)(2,1)S(1)}, bf16[256,256]{1,0:T(8,128)(2,1)S(1)}, u32[]{:S(2)}, u32[]{:S(2)}) %collective-permute-start.13) | collective-permute-done | bytes 131104 | tf_op jit(solution)/shard_map/ppermute | solution.py:468
  66.0 1.1 %collective-permute-done.14.rest_1_ = bf16[256,256]{1,0:T(8,128)(2,1)S(1)} collective-permute-done((bf16[256,256]{1,0:T(8,128)(2,1)S(1)}, bf16[256,256]{1,0:T(8,128)(2,1)S(1)}, u32[]{:S(2)}, u32[]{:S(2)}) %collective-permute-start.14) | collective-permute-done | bytes 131104 | tf_op jit(solution)/shard_map/ppermute | solution.py:468
  67.2 1.2 %collective-permute-start.19 = (bf16[256,256]{1,0:T(8,128)(2,1)S(1)}, bf16[256,256]{1,0:T(8,128)(2,1)S(1)}, u32[]{:S(2)}, u32[]{:S(2)}) collective-permute-start(bf16[256,256]{1,0:T(8,128)(2,1)S(1)} %get-tuple-element.62), channel_id=1, source_target_pairs={{8,0},{20,4},{0,8},{28,12},{24,16},{4,20},{16,24},{12,28},{9,1},{2... | collective-permute-start | bytes 393224 | tf_op jit(solution)/shard_map/ppermute | solution.py:468
  68.3 1.3 %base.1.base_ref = f32[2048,256]{1,0:T(8,128)S(1)} custom-call(f32[1,256]{1,0:T(1,128)S(1)} %bitcast.2, f32[2048,256]{1,0:T(8,128)S(1)} %get-tuple-element.48.y_ref, bf16[2048,1024]{1,0:T(8,128)(2,1)S(1)} %get-tuple-element.49.onehot, f32[1,2048]{1,0:T(1,128)S(1)} %add.7.refs_8_.total_ref, bf16[256,256]{1,0:T(8,128)(2,1)S(1)} %collective-permute-done.13.rest_0_, ...), custom_call_target="tpu_custom_call" | custom-call | flops 1073741824 | bytes 4194304 | tf_op jit(solution)/shard_map/base/pallas_call | solution.py:408
  69.6 1.0 %collective-permute-done.16.rest_0_ = bf16[256,256]{1,0:T(8,128)(2,1)S(1)} collective-permute-done((bf16[256,256]{1,0:T(8,128)(2,1)S(1)}, bf16[256,256]{1,0:T(8,128)(2,1)S(1)}, u32[]{:S(2)}, u32[]{:S(2)}) %collective-permute-start.16) | collective-permute-done | bytes 131104 | tf_op jit(solution)/shard_map/ppermute | solution.py:468
  70.7 1.7 %collective-permute-done.18.rest_2_ = bf16[256,256]{1,0:T(8,128)(2,1)S(1)} collective-permute-done((bf16[256,256]{1,0:T(8,128)(2,1)S(1)}, bf16[256,256]{1,0:T(8,128)(2,1)S(1)}, u32[]{:S(2)}, u32[]{:S(2)}) %collective-permute-start.18) | collective-permute-done | bytes 131104 | tf_op jit(solution)/shard_map/ppermute | solution.py:468
  73.0 2.1 %mix.1 = bf16[2048,256]{1,0:T(8,128)(2,1)} custom-call(f32[2048,256]{1,0:T(8,128)S(1)} %base.1.base_ref, bf16[2048,1024]{1,0:T(8,128)(2,1)S(1)} %get-tuple-element.45.rest_2_.onehot, bf16[256,256]{1,0:T(8,128)(2,1)S(1)} %collective-permute-done.16.rest_0_, bf16[256,256]{1,0:T(8,128)(2,1)S(1)} %collective-permute-done.17.rest_1_, ...), custom_call_target="tpu_custom_call" | custom-call | flops 1073741824 | bytes 4194304 | tf_op jit(solution)/shard_map/mix/pallas_call | solution.py:436
  (45 shorter events, 3.8 us)
Async XLA Ops:
  0.0 0.7 copy-start.8
  0.7 1.4 %copy-start.1 = (bf16[1,256,256]{2,1,0:T(8,128)(2,1)S(1)}, bf16[1,256,256]{2,1,0:T(8,128)(2,1)}, u32[]{:S(2)}) copy-start(bf16[1,256,256]{2,1,0:T(8,128)(2,1)} %one_ref.3) | copy-start | bytes 393220
  0.7 1.5 %copy-start.2 = (bf16[1,256,256]{2,1,0:T(8,128)(2,1)S(1)}, bf16[1,256,256]{2,1,0:T(8,128)(2,1)}, u32[]{:S(2)}) copy-start(bf16[1,256,256]{2,1,0:T(8,128)(2,1)} %three_ref.3) | copy-start | bytes 393220
  0.7 1.5 %copy-start.3 = (bf16[1,256,256]{2,1,0:T(8,128)(2,1)S(1)}, bf16[1,256,256]{2,1,0:T(8,128)(2,1)}, u32[]{:S(2)}) copy-start(bf16[1,256,256]{2,1,0:T(8,128)(2,1)} %two_ref.3) | copy-start | bytes 393220
  0.7 1.5 %copy-start.5 = (bf16[2048,256]{1,0:T(8,128)(2,1)S(1)}, bf16[2048,256]{1,0:T(8,128)(2,1)}, u32[]{:S(2)}) copy-start(bf16[2048,256]{1,0:T(8,128)(2,1)} %k_ref.7) | copy-start | bytes 3145732
  0.7 1.7 %copy-start.6 = (bf16[2048,256]{1,0:T(8,128)(2,1)S(1)}, bf16[2048,256]{1,0:T(8,128)(2,1)}, u32[]{:S(2)}) copy-start(bf16[2048,256]{1,0:T(8,128)(2,1)} %v_ref.7) | copy-start | bytes 3145732
  0.7 1.7 %copy-start.7 = (f32[2048,1]{0,1:T(1,128)S(1)}, f32[2048,1]{0,1:T(1,128)}, u32[]{:S(2)}) copy-start(f32[2048,1]{0,1:T(1,128)} %param.12) | copy-start | bytes 24580
  2.4 3.4 %copy-start = (bf16[2048,256]{1,0:T(8,128)(2,1)S(1)}, bf16[2048,256]{1,0:T(8,128)(2,1)}, u32[]{:S(2)}) copy-start(bf16[2048,256]{1,0:T(8,128)(2,1)} %q_ref.7) | copy-start | bytes 3145732
  5.3 2.3 %collective-permute-start = (f32[384,256]{1,0:T(8,128)S(1)}, f32[384,256]{1,0:T(8,128)S(1)}, u32[]{:S(2)}, u32[]{:S(2)}) collective-permute-start(f32[384,256]{1,0:T(8,128)S(1)} %get-tuple-element.36), channel_id=1, source_target_pairs={{0,4},{4,0},{8,12},{12,8},{16,20},{20,16},{24,28},{28,24},{1,5},{5... | collective-permute-start | bytes 1179656 | tf_op jit(solution)/shard_map/ppermute | solution.py:267
  7.8 8.8 %collective-permute-start.1 = (bf16[384,256]{1,0:T(8,128)(2,1)S(1)}, bf16[384,256]{1,0:T(8,128)(2,1)S(1)}, u32[]{:S(2)}, u32[]{:S(2)}) collective-permute-start(bf16[384,256]{1,0:T(8,128)(2,1)S(1)} %convert_element_type.6), channel_id=1, source_target_pairs={{0,8},{4,20},{8,0},{12,28},{16,24},{20,4},{24,16},{28,12},{1,9},{5... | collective-permute-start | bytes 589832 | tf_op jit(solution)/shard_map/ppermute | solution.py:279
  10.3 12.8 %collective-permute-start.3 = (bf16[256,768]{1,0:T(8,128)(2,1)S(1)}, bf16[256,768]{1,0:T(8,128)(2,1)S(1)}, u32[]{:S(2)}, u32[]{:S(2)}) collective-permute-start(bf16[256,768]{1,0:T(8,128)(2,1)S(1)} %get-tuple-element.41), channel_id=1, source_target_pairs={{0,28},{4,24},{8,20},{12,16},{16,12},{20,8},{24,4},{28,0},{1,29},{... | collective-permute-start | bytes 1179656 | tf_op jit(solution)/shard_map/ppermute | solution.py:463
  11.6 22.0 %collective-permute-start.4 = (bf16[256,768]{1,0:T(8,128)(2,1)S(1)}, bf16[256,768]{1,0:T(8,128)(2,1)S(1)}, u32[]{:S(2)}, u32[]{:S(2)}) collective-permute-start(bf16[256,768]{1,0:T(8,128)(2,1)S(1)} %get-tuple-element.42), channel_id=1, source_target_pairs={{0,24},{4,28},{8,16},{12,20},{16,8},{20,12},{24,0},{28,4},{1,25},{... | collective-permute-start | bytes 1179656 | tf_op jit(solution)/shard_map/ppermute | solution.py:463
  14.9 29.3 %collective-permute-start.6 = (bf16[256,768]{1,0:T(8,128)(2,1)S(1)}, bf16[256,768]{1,0:T(8,128)(2,1)S(1)}, u32[]{:S(2)}, u32[]{:S(2)}) collective-permute-start(bf16[256,768]{1,0:T(8,128)(2,1)S(1)} %get-tuple-element.46), channel_id=1, source_target_pairs={{0,20},{4,8},{8,28},{12,0},{16,4},{20,24},{24,12},{28,16},{1,21},{... | collective-permute-start | bytes 1179656 | tf_op jit(solution)/shard_map/ppermute | solution.py:463
  16.1 30.5 %collective-permute-start.7 = (bf16[256,768]{1,0:T(8,128)(2,1)S(1)}, bf16[256,768]{1,0:T(8,128)(2,1)S(1)}, u32[]{:S(2)}, u32[]{:S(2)}) collective-permute-start(bf16[256,768]{1,0:T(8,128)(2,1)S(1)} %get-tuple-element.47), channel_id=1, source_target_pairs={{0,16},{4,12},{8,24},{12,4},{16,0},{20,28},{24,8},{28,20},{1,17},{... | collective-permute-start | bytes 1179656 | tf_op jit(solution)/shard_map/ppermute | solution.py:463
  16.7 26.2 %collective-permute-start.2 = (bf16[384,256]{1,0:T(8,128)(2,1)S(1)}, bf16[384,256]{1,0:T(8,128)(2,1)S(1)}, u32[]{:S(2)}, u32[]{:S(2)}) collective-permute-start(bf16[384,256]{1,0:T(8,128)(2,1)S(1)} %convert_element_type.7), channel_id=1, source_target_pairs={{0,16},{4,12},{8,24},{12,4},{16,0},{20,28},{24,8},{28,20},{1,17},{... | collective-permute-start | bytes 589832 | tf_op jit(solution)/shard_map/ppermute | solution.py:279
  18.2 26.6 %copy-start.9 = (s32[1,2048]{1,0:T(1,128)S(1)}, s32[1,2048]{1,0:T(1,128)}, u32[]{:S(2)}) copy-start(s32[1,2048]{1,0:T(1,128)} %order_ref.3) | copy-start | bytes 24580
  42.9 3.7 %collective-permute-start.5 = (f32[384,256]{1,0:T(8,128)S(1)}, f32[384,256]{1,0:T(8,128)S(1)}, u32[]{:S(2)}, u32[]{:S(2)}) collective-permute-start(f32[384,256]{1,0:T(8,128)S(1)} %merge.5.rest_0_), channel_id=1, source_target_pairs={{0,4},{4,0},{8,12},{12,8},{16,20},{20,16},{24,28},{28,24},{1,5},{5... | collective-permute-start | bytes 1179656 | tf_op jit(solution)/shard_map/ppermute | solution.py:284
  43.0 14.6 %collective-permute-start.10 = (bf16[256,768]{1,0:T(8,128)(2,1)S(1)}, bf16[256,768]{1,0:T(8,128)(2,1)S(1)}, u32[]{:S(2)}, u32[]{:S(2)}) collective-permute-start(bf16[256,768]{1,0:T(8,128)(2,1)S(1)} %get-tuple-element.52), channel_id=1, source_target_pairs={{0,4},{4,0},{8,12},{12,8},{16,20},{20,16},{24,28},{28,24},{1,5},{5... | collective-permute-start | bytes 1179656 | tf_op jit(solution)/shard_map/ppermute | solution.py:463
  43.5 14.2 %collective-permute-start.11 = (bf16[256,768]{1,0:T(8,128)(2,1)S(1)}, bf16[256,768]{1,0:T(8,128)(2,1)S(1)}, u32[]{:S(2)}, u32[]{:S(2)}) collective-permute-start(bf16[256,768]{1,0:T(8,128)(2,1)S(1)} %get-tuple-element.53), channel_id=1, source_target_pairs={{0,8},{4,20},{8,0},{12,28},{16,24},{20,4},{24,16},{28,12},{1,9},{5... | collective-permute-start | bytes 1179656 | tf_op jit(solution)/shard_map/ppermute | solution.py:463
  44.2 13.5 %collective-permute-start.12 = (bf16[256,768]{1,0:T(8,128)(2,1)S(1)}, bf16[256,768]{1,0:T(8,128)(2,1)S(1)}, u32[]{:S(2)}, u32[]{:S(2)}) collective-permute-start(bf16[256,768]{1,0:T(8,128)(2,1)S(1)} %get-tuple-element.54), channel_id=1, source_target_pairs={{0,12},{4,16},{8,4},{12,24},{16,28},{20,0},{24,20},{28,8},{1,13},{... | collective-permute-start | bytes 1179656 | tf_op jit(solution)/shard_map/ppermute | solution.py:463
  49.3 19.1 %copy-start.4 = (f32[256]{0:T(256)S(1)}, f32[256]{0:T(256)}, u32[]{:S(2)}) copy-start(f32[256]{0:T(256)} %param.16) | copy-start | bytes 3076
  49.3 3.7 %collective-permute-start.8 = (f32[1,2048]{1,0:T(1,128)S(1)}, f32[1,2048]{1,0:T(1,128)S(1)}, u32[]{:S(2)}, u32[]{:S(2)}) collective-permute-start(f32[1,2048]{1,0:T(1,128)S(1)} %get-tuple-element.50), channel_id=1, source_target_pairs={{0,1},{1,0},{2,3},{3,2},{4,5},{5,4},{6,7},{7,6},{8,9},{9,8},{10,11... | collective-permute-start | bytes 24584 | tf_op jit(solution)/shard_map/ppermute | solution.py:457
  53.0 4.6 %collective-permute-start.9 = (f32[1,2048]{1,0:T(1,128)S(1)}, f32[1,2048]{1,0:T(1,128)S(1)}, u32[]{:S(2)}, u32[]{:S(2)}) collective-permute-start(f32[1,2048]{1,0:T(1,128)S(1)} %add.6), channel_id=1, source_target_pairs={{0,2},{1,3},{2,0},{3,1},{4,6},{5,7},{6,4},{7,5},{8,10},{9,11},{10,... | collective-permute-start | bytes 24584 | tf_op jit(solution)/shard_map/ppermute | solution.py:457
  59.2 6.8 %collective-permute-start.13 = (bf16[256,256]{1,0:T(8,128)(2,1)S(1)}, bf16[256,256]{1,0:T(8,128)(2,1)S(1)}, u32[]{:S(2)}, u32[]{:S(2)}) collective-permute-start(bf16[256,256]{1,0:T(8,128)(2,1)S(1)} %get-tuple-element.55), channel_id=1, source_target_pairs={{28,0},{24,4},{20,8},{16,12},{12,16},{8,20},{4,24},{0,28},{29,1},{... | collective-permute-start | bytes 393224 | tf_op jit(solution)/shard_map/ppermute | solution.py:468
  59.3 7.9 %collective-permute-start.14 = (bf16[256,256]{1,0:T(8,128)(2,1)S(1)}, bf16[256,256]{1,0:T(8,128)(2,1)S(1)}, u32[]{:S(2)}, u32[]{:S(2)}) collective-permute-start(bf16[256,256]{1,0:T(8,128)(2,1)S(1)} %get-tuple-element.56), channel_id=1, source_target_pairs={{24,0},{28,4},{16,8},{20,12},{8,16},{12,20},{0,24},{4,28},{25,1},{... | collective-permute-start | bytes 393224 | tf_op jit(solution)/shard_map/ppermute | solution.py:468
  60.8 7.5 %collective-permute-start.15 = (bf16[256,256]{1,0:T(8,128)(2,1)S(1)}, bf16[256,256]{1,0:T(8,128)(2,1)S(1)}, u32[]{:S(2)}, u32[]{:S(2)}) collective-permute-start(bf16[256,256]{1,0:T(8,128)(2,1)S(1)} %get-tuple-element.57), channel_id=1, source_target_pairs={{4,0},{0,4},{12,8},{8,12},{20,16},{16,20},{28,24},{24,28},{5,1},{1... | collective-permute-start | bytes 393224 | tf_op jit(solution)/shard_map/ppermute | solution.py:468
  62.0 8.6 %collective-permute-start.16 = (bf16[256,256]{1,0:T(8,128)(2,1)S(1)}, bf16[256,256]{1,0:T(8,128)(2,1)S(1)}, u32[]{:S(2)}, u32[]{:S(2)}) collective-permute-start(bf16[256,256]{1,0:T(8,128)(2,1)S(1)} %get-tuple-element.59), channel_id=1, source_target_pairs={{20,0},{8,4},{28,8},{0,12},{4,16},{24,20},{12,24},{16,28},{21,1},{... | collective-permute-start | bytes 393224 | tf_op jit(solution)/shard_map/ppermute | solution.py:468
  62.2 8.5 %collective-permute-start.17 = (bf16[256,256]{1,0:T(8,128)(2,1)S(1)}, bf16[256,256]{1,0:T(8,128)(2,1)S(1)}, u32[]{:S(2)}, u32[]{:S(2)}) collective-permute-start(bf16[256,256]{1,0:T(8,128)(2,1)S(1)} %get-tuple-element.60), channel_id=1, source_target_pairs={{16,0},{12,4},{24,8},{4,12},{0,16},{28,20},{8,24},{20,28},{17,1},{... | collective-permute-start | bytes 393224 | tf_op jit(solution)/shard_map/ppermute | solution.py:468
  66.0 6.4 %collective-permute-start.18 = (bf16[256,256]{1,0:T(8,128)(2,1)S(1)}, bf16[256,256]{1,0:T(8,128)(2,1)S(1)}, u32[]{:S(2)}, u32[]{:S(2)}) collective-permute-start(bf16[256,256]{1,0:T(8,128)(2,1)S(1)} %get-tuple-element.61), channel_id=1, source_target_pairs={{12,0},{16,4},{4,8},{24,12},{28,16},{0,20},{20,24},{8,28},{13,1},{... | collective-permute-start | bytes 393224 | tf_op jit(solution)/shard_map/ppermute | solution.py:468
  67.2 5.9 %collective-permute-start.19 = (bf16[256,256]{1,0:T(8,128)(2,1)S(1)}, bf16[256,256]{1,0:T(8,128)(2,1)S(1)}, u32[]{:S(2)}, u32[]{:S(2)}) collective-permute-start(bf16[256,256]{1,0:T(8,128)(2,1)S(1)} %get-tuple-element.62), channel_id=1, source_target_pairs={{8,0},{20,4},{0,8},{28,12},{24,16},{4,20},{16,24},{12,28},{9,1},{2... | collective-permute-start | bytes 393224 | tf_op jit(solution)/shard_map/ppermute | solution.py:468

commit v9 on v8

--- a/solution.py
+++ b/solution.py
@@ -487,11 +487,11 @@
     came = [arrived[step] for step in steps]
     parts = gradients(keys, values, rates.reshape(1, count), *weights, marks[-1], n)
     mine = core_step(parts, tokens[:1], n)
-    summed = sum_over_chips(mine, len(parts) == 2, [tokens[1:2], came[:2] + tokens[2:]], n)
+    summed = sum_over_chips(mine, len(parts) == 2, [[], came[:2] + tokens[1:2]], n)
     early = steps[:few] + steps[n - few :]
     late = steps[few : n - few]
     early_places, late_places = place(order, n, early + late)
-    y, square = read_out(queries, *weights, summed, [late_places] + came[2:4])
+    y, square = read_out(queries, *weights, summed, [late_places] + came[2:4] + tokens[2:])
     total = sum_over_heads(square, heads)
     attended = attend([arrived[step] for step in range(n)], [total], n, width)
     returned = {step: give_back(attended[step], step, n) for step in early + late}

time: 75.5 us -> 73.3 us (0.971)
  waiting for transfers between devices: 32.1 us -> 29.6 us
    ppermute x2, waiting for transfers between devices: 9.22 us -> 2.43 us  [sum_over_chips(): got = lax.ppermute(mine.astype(BF16), 'cam', pairs)]
    ppermute x7, waiting for transfers between devices: 11.9 us -> 15.6 us  [exchange(): return lax.ppermute(block, 'cam', routes(step, n)) if step else block]
    ppermute x2, starting transfers between devices: 4.16 us -> 5.2 us  [sum_over_chips(): got = lax.ppermute(mine.astype(BF16), 'cam', pairs)]
  transfers between devices with their start and end apart: 20 -> 20, of which waited for: 11 -> 13; matrix products, arithmetic and copies ran while one was open for 0% -> 0% of each run, Pallas kernels for 17% -> 18%
where the time goes in v9:
time: 73.3 us; the launch traced here: 73.1 us
  waiting for transfers between devices  29.6 us (40%)
  starting transfers between devices  21.3 us (29%)
  Pallas kernels  20.7 us (28%)
  local copies, waits for them, and re-layouts  0.99 us (1%)
    ppermute x7, waiting for transfers between devices, exchange(): return lax.ppermute(block, 'cam', routes(step, n)) if step else block  15.6 us
    ppermute x7, waiting for transfers between devices, give_back(): return lax.ppermute(block, 'cam', pairs) if step else block  7.56 us
    pallas_call x3, Pallas kernels, sort_tokens(): pl.pallas_call(functools.partial(sort_kernel, size), out_shape=[jax.Shape...  7.07 us
    ppermute x7, starting transfers between devices, exchange(): return lax.ppermute(block, 'cam', routes(step, n)) if step else block  6.21 us
    ppermute x2, starting transfers between devices, sum_over_chips(): got = lax.ppermute(mine.astype(BF16), 'cam', pairs)  5.2 us
    ppermute x7, starting transfers between devices, give_back(): return lax.ppermute(block, 'cam', pairs) if step else block  5.03 us
    ppermute x2, starting transfers between devices, sum_over_heads(): square = square + lax.ppermute(square, 'head', pairs)  4.29 us
    ppermute x2, waiting for transfers between devices, sum_over_heads(): square = square + lax.ppermute(square, 'head', pairs)  4.02 us
  transfers between devices with their start and end apart: 20, of which 13 were waited for; matrix products, arithmetic and copies ran while one was open for 0% of the time, Pallas kernels for 18%

profile of v9, /device:TPU:0, one launch (start us, length us, event | category | flops | bytes accessed | tf_op | source)
XLA Modules:
  0.0 73.1 jit_solution(17584674670034465830)
XLA Ops:
  0.7 1.4 %mark.1 = (bf16[512,2048]{1,0:T(8,128)(2,1)S(1)}, bf16[512,2048]{1,0:T(8,128)(2,1)S(1)}, bf16[1024,2048]{1,0:T(8,128)(2,1)S(1)}, f32[8,128]{1,0:T(8,128)S(1)}) custom-call(s32[1,2048]{1,0:T(1,128)S(1)} %copy-done.8), custom_call_target="tpu_custom_call" | custom-call | flops 999999995904 | bytes 1024 | tf_op jit(solution)/shard_map/mark/pallas_call | solution.py:107
  2.5 2.9 %gradients.1 = (f32[384,256]{1,0:T(8,128)S(1)}, f32[384,256]{1,0:T(8,128)S(1)}) custom-call(bf16[2048,256]{1,0:T(8,128)(2,1)S(1)} %copy-done.5, bf16[2048,256]{1,0:T(8,128)(2,1)S(1)} %copy-done.6, f32[1,2048]{1,0:T(1,128)S(1)} %bitcast.3, bf16[1,256,256]{2,1,0:T(8,128)(2,1)S(1)} %copy-done.1, bf16[1,256,256]{2,1,0:T(8,128)(2,1)S(1)} %copy-done.2, ...), custom_call_target="tpu_custom_call" | custom-call | flops 1610612736 | bytes 4194304 | tf_op jit(solution)/shard_map/gradients/pallas_call | solution.py:235
  5.9 1.8 %sort_tokens.3 = (bf16[256,768]{1,0:T(8,128)(2,1)S(1)}, bf16[256,768]{1,0:T(8,128)(2,1)S(1)}, f32[8,128]{1,0:T(8,128)S(1)}) custom-call(bf16[512,2048]{1,0:T(8,128)(2,1)S(1)} %get-tuple-element.37.onehot, bf16[2048,256]{1,0:T(8,128)(2,1)S(1)} %copy-done, bf16[2048,256]{1,0:T(8,128)(2,1)S(1)} %copy-done.5, bf16[2048,256]{1,0:T(8,128)(2,1)S(1)} %copy-done.6), custom_call_target="tpu_custom_call" | custom-call | flops 1610612736 | bytes 3145728 | tf_op jit(solution)/shard_map/sort_tokens/pallas_call | solution.py:140
  7.8 2.6 %collective-permute-start.1 = (bf16[384,256]{1,0:T(8,128)(2,1)S(1)}, bf16[384,256]{1,0:T(8,128)(2,1)S(1)}, u32[]{:S(2)}, u32[]{:S(2)}) collective-permute-start(bf16[384,256]{1,0:T(8,128)(2,1)S(1)} %convert_element_type.6), channel_id=1, source_target_pairs={{0,8},{4,20},{8,0},{12,28},{16,24},{20,4},{24,16},{28,12},{1,9},{5... | collective-permute-start | bytes 589832 | tf_op jit(solution)/shard_map/ppermute | solution.py:279
  10.3 1.3 %collective-permute-start.3 = (bf16[256,768]{1,0:T(8,128)(2,1)S(1)}, bf16[256,768]{1,0:T(8,128)(2,1)S(1)}, u32[]{:S(2)}, u32[]{:S(2)}) collective-permute-start(bf16[256,768]{1,0:T(8,128)(2,1)S(1)} %get-tuple-element.39), channel_id=1, source_target_pairs={{0,28},{4,24},{8,20},{12,16},{16,12},{20,8},{24,4},{28,0},{1,29},{... | collective-permute-start | bytes 1179656 | tf_op jit(solution)/shard_map/ppermute | solution.py:463
  11.6 1.5 %collective-permute-start.4 = (bf16[256,768]{1,0:T(8,128)(2,1)S(1)}, bf16[256,768]{1,0:T(8,128)(2,1)S(1)}, u32[]{:S(2)}, u32[]{:S(2)}) collective-permute-start(bf16[256,768]{1,0:T(8,128)(2,1)S(1)} %get-tuple-element.40), channel_id=1, source_target_pairs={{0,24},{4,28},{8,16},{12,20},{16,8},{20,12},{24,0},{28,4},{1,25},{... | collective-permute-start | bytes 1179656 | tf_op jit(solution)/shard_map/ppermute | solution.py:463
  13.1 1.6 %collective-permute-done.1.got_ref = bf16[384,256]{1,0:T(8,128)(2,1)S(1)} collective-permute-done((bf16[384,256]{1,0:T(8,128)(2,1)S(1)}, bf16[384,256]{1,0:T(8,128)(2,1)S(1)}, u32[]{:S(2)}, u32[]{:S(2)}) %collective-permute-start.1) | collective-permute-done | bytes 196640 | tf_op jit(solution)/shard_map/ppermute | solution.py:279
  14.8 2.6 %collective-permute-start.2 = (bf16[384,256]{1,0:T(8,128)(2,1)S(1)}, bf16[384,256]{1,0:T(8,128)(2,1)S(1)}, u32[]{:S(2)}, u32[]{:S(2)}) collective-permute-start(bf16[384,256]{1,0:T(8,128)(2,1)S(1)} %convert_element_type.7), channel_id=1, source_target_pairs={{0,16},{4,12},{8,24},{12,4},{16,0},{20,28},{24,8},{28,20},{1,17},{... | collective-permute-start | bytes 589832 | tf_op jit(solution)/shard_map/ppermute | solution.py:279
  17.4 1.8 %sort_tokens.4 = (bf16[256,768]{1,0:T(8,128)(2,1)S(1)}, bf16[256,768]{1,0:T(8,128)(2,1)S(1)}, f32[8,128]{1,0:T(8,128)S(1)}) custom-call(bf16[512,2048]{1,0:T(8,128)(2,1)S(1)} %get-tuple-element.41.onehot, bf16[2048,256]{1,0:T(8,128)(2,1)S(1)} %copy-done, bf16[2048,256]{1,0:T(8,128)(2,1)S(1)} %copy-done.5, bf16[2048,256]{1,0:T(8,128)(2,1)S(1)} %copy-done.6), custom_call_target="tpu_custom_call" | custom-call | flops 1610612736 | bytes 3145728 | tf_op jit(solution)/shard_map/sort_tokens/pallas_call | solution.py:140
  19.3 1.4 %collective-permute-start.7 = (bf16[256,768]{1,0:T(8,128)(2,1)S(1)}, bf16[256,768]{1,0:T(8,128)(2,1)S(1)}, u32[]{:S(2)}, u32[]{:S(2)}) collective-permute-start(bf16[256,768]{1,0:T(8,128)(2,1)S(1)} %get-tuple-element.45), channel_id=1, source_target_pairs={{0,16},{4,12},{8,24},{12,4},{16,0},{20,28},{24,8},{28,20},{1,17},{... | collective-permute-start | bytes 1179656 | tf_op jit(solution)/shard_map/ppermute | solution.py:463
  20.7 2.5 %collective-permute-done.3.rest_0_.refs_7_ = bf16[256,768]{1,0:T(8,128)(2,1)S(1)} collective-permute-done((bf16[256,768]{1,0:T(8,128)(2,1)S(1)}, bf16[256,768]{1,0:T(8,128)(2,1)S(1)}, u32[]{:S(2)}, u32[]{:S(2)}) %collective-permute-start.3) | collective-permute-done | bytes 393248 | tf_op jit(solution)/shard_map/ppermute | solution.py:463
  23.2 10.5 %collective-permute-done.4.rest_1_.refs_6_ = bf16[256,768]{1,0:T(8,128)(2,1)S(1)} collective-permute-done((bf16[256,768]{1,0:T(8,128)(2,1)S(1)}, bf16[256,768]{1,0:T(8,128)(2,1)S(1)}, u32[]{:S(2)}, u32[]{:S(2)}) %collective-permute-start.4) | collective-permute-done | bytes 393248 | tf_op jit(solution)/shard_map/ppermute | solution.py:463
  33.6 0.8 %collective-permute-done.2.got_ref = bf16[384,256]{1,0:T(8,128)(2,1)S(1)} collective-permute-done((bf16[384,256]{1,0:T(8,128)(2,1)S(1)}, bf16[384,256]{1,0:T(8,128)(2,1)S(1)}, u32[]{:S(2)}, u32[]{:S(2)}) %collective-permute-start.2) | collective-permute-done | bytes 196640 | tf_op jit(solution)/shard_map/ppermute | solution.py:279
  34.6 3.5 %sort_tokens.5 = (bf16[256,768]{1,0:T(8,128)(2,1)S(1)}, bf16[256,768]{1,0:T(8,128)(2,1)S(1)}, bf16[256,768]{1,0:T(8,128)(2,1)S(1)}, bf16[256,768]{1,0:T(8,128)(2,1)S(1)}, f32[8,128]{1,0:T(8,128)S(1)}) custom-call(bf16[1024,2048]{1,0:T(8,128)(2,1)S(1)} %get-tuple-element.46.onehot, bf16[2048,256]{1,0:T(8,128)(2,1)S(1)} %copy-done, ...), custom_call_target="tpu_custom_call" | custom-call | flops 3221225472 | bytes 3145728 | tf_op jit(solution)/shard_map/sort_tokens/pallas_call | solution.py:140
  38.6 1.5 %collective-permute-start.11 = (bf16[256,768]{1,0:T(8,128)(2,1)S(1)}, bf16[256,768]{1,0:T(8,128)(2,1)S(1)}, u32[]{:S(2)}, u32[]{:S(2)}) collective-permute-start(bf16[256,768]{1,0:T(8,128)(2,1)S(1)} %get-tuple-element.53), channel_id=1, source_target_pairs={{0,8},{4,20},{8,0},{12,28},{16,24},{20,4},{24,16},{28,12},{1,9},{5... | collective-permute-start | bytes 1179656 | tf_op jit(solution)/shard_map/ppermute | solution.py:463
  40.0 1.7 %place.1 = (bf16[2048,1024]{1,0:T(8,128)(2,1)S(1)}, bf16[2048,1024]{1,0:T(8,128)(2,1)S(1)}) custom-call(s32[1,2048]{1,0:T(1,128)S(1)} %copy-done.9), custom_call_target="tpu_custom_call" | custom-call | flops 4194304 | bytes 8388608 | tf_op jit(solution)/shard_map/place/pallas_call | solution.py:370
  41.7 2.6 %collective-permute-done.7.rest_4_.refs_4_ = bf16[256,768]{1,0:T(8,128)(2,1)S(1)} collective-permute-done((bf16[256,768]{1,0:T(8,128)(2,1)S(1)}, bf16[256,768]{1,0:T(8,128)(2,1)S(1)}, u32[]{:S(2)}, u32[]{:S(2)}) %collective-permute-start.7) | collective-permute-done | bytes 393248 | tf_op jit(solution)/shard_map/ppermute | solution.py:463
  44.4 2.7 %read_out.1 = (f32[2048,256]{1,0:T(8,128)S(1)}, f32[1,2048]{1,0:T(1,128)S(1)}) custom-call(bf16[2048,256]{1,0:T(8,128)(2,1)S(1)} %copy-done, bf16[1,256,256]{2,1,0:T(8,128)(2,1)S(1)} %copy-done.1, bf16[1,256,256]{2,1,0:T(8,128)(2,1)S(1)} %copy-done.2, bf16[1,256,256]{2,1,0:T(8,128)(2,1)S(1)} %copy-done.3, f32[384,256]{1,0:T(8,128)S(1)} %merge.5.rest_0_, ...), custom_call_target="tpu_custom_call" | custom-call | flops 805306368 | bytes 4194304 | tf_op jit(solution)/shard_map/read_out/pallas_call | solution.py:331
  47.1 1.6 %collective-permute-start.8 = (f32[1,2048]{1,0:T(1,128)S(1)}, f32[1,2048]{1,0:T(1,128)S(1)}, u32[]{:S(2)}, u32[]{:S(2)}) collective-permute-start(f32[1,2048]{1,0:T(1,128)S(1)} %get-tuple-element.50), channel_id=1, source_target_pairs={{0,1},{1,0},{2,3},{3,2},{4,5},{5,4},{6,7},{7,6},{8,9},{9,8},{10,11... | collective-permute-start | bytes 24584 | tf_op jit(solution)/shard_map/ppermute | solution.py:457
  48.7 2.1 %collective-permute-done.8 = f32[1,2048]{1,0:T(1,128)S(1)} collective-permute-done((f32[1,2048]{1,0:T(1,128)S(1)}, f32[1,2048]{1,0:T(1,128)S(1)}, u32[]{:S(2)}, u32[]{:S(2)}) %collective-permute-start.8) | collective-permute-done | bytes 8224 | tf_op jit(solution)/shard_map/ppermute | solution.py:457
  50.8 2.7 %collective-permute-start.9 = (f32[1,2048]{1,0:T(1,128)S(1)}, f32[1,2048]{1,0:T(1,128)S(1)}, u32[]{:S(2)}, u32[]{:S(2)}) collective-permute-start(f32[1,2048]{1,0:T(1,128)S(1)} %add.6), channel_id=1, source_target_pairs={{0,2},{1,3},{2,0},{3,1},{4,6},{5,7},{6,4},{7,5},{8,10},{9,11},{10,... | collective-permute-start | bytes 24584 | tf_op jit(solution)/shard_map/ppermute | solution.py:457
  53.4 2.0 %collective-permute-done.9 = f32[1,2048]{1,0:T(1,128)S(1)} collective-permute-done((f32[1,2048]{1,0:T(1,128)S(1)}, f32[1,2048]{1,0:T(1,128)S(1)}, u32[]{:S(2)}, u32[]{:S(2)}) %collective-permute-start.9) | collective-permute-done | bytes 8224 | tf_op jit(solution)/shard_map/ppermute | solution.py:457
  55.4 1.5 %attend.1 = (bf16[256,256]{1,0:T(8,128)(2,1)S(1)}, bf16[256,256]{1,0:T(8,128)(2,1)S(1)}, bf16[256,256]{1,0:T(8,128)(2,1)S(1)}, bf16[256,256]{1,0:T(8,128)(2,1)S(...) custom-call(bf16[256,768]{1,0:T(8,128)(2,1)S(1)} %get-tuple-element., ...), custom_call_target="tpu_custom_call" | custom-call | flops 536870912 | bytes 4194304 | tf_op jit(solution)/shard_map/attend/pallas_call | solution.py:179
  57.0 1.5 %collective-permute-start.14 = (bf16[256,256]{1,0:T(8,128)(2,1)S(1)}, bf16[256,256]{1,0:T(8,128)(2,1)S(1)}, u32[]{:S(2)}, u32[]{:S(2)}) collective-permute-start(bf16[256,256]{1,0:T(8,128)(2,1)S(1)} %get-tuple-element.56), channel_id=1, source_target_pairs={{24,0},{28,4},{16,8},{20,12},{8,16},{12,20},{0,24},{4,28},{25,1},{... | collective-permute-start | bytes 393224 | tf_op jit(solution)/shard_map/ppermute | solution.py:468
  58.5 1.2 %collective-permute-start.15 = (bf16[256,256]{1,0:T(8,128)(2,1)S(1)}, bf16[256,256]{1,0:T(8,128)(2,1)S(1)}, u32[]{:S(2)}, u32[]{:S(2)}) collective-permute-start(bf16[256,256]{1,0:T(8,128)(2,1)S(1)} %get-tuple-element.57), channel_id=1, source_target_pairs={{4,0},{0,4},{12,8},{8,12},{20,16},{16,20},{28,24},{24,28},{5,1},{1... | collective-permute-start | bytes 393224 | tf_op jit(solution)/shard_map/ppermute | solution.py:468
  60.4 1.0 %collective-permute-start.17 = (bf16[256,256]{1,0:T(8,128)(2,1)S(1)}, bf16[256,256]{1,0:T(8,128)(2,1)S(1)}, u32[]{:S(2)}, u32[]{:S(2)}) collective-permute-start(bf16[256,256]{1,0:T(8,128)(2,1)S(1)} %get-tuple-element.60), channel_id=1, source_target_pairs={{16,0},{12,4},{24,8},{4,12},{0,16},{28,20},{8,24},{20,28},{17,1},{... | collective-permute-start | bytes 393224 | tf_op jit(solution)/shard_map/ppermute | solution.py:468
  61.4 2.4 %collective-permute-done.13.rest_0_ = bf16[256,256]{1,0:T(8,128)(2,1)S(1)} collective-permute-done((bf16[256,256]{1,0:T(8,128)(2,1)S(1)}, bf16[256,256]{1,0:T(8,128)(2,1)S(1)}, u32[]{:S(2)}, u32[]{:S(2)}) %collective-permute-start.13) | collective-permute-done | bytes 131104 | tf_op jit(solution)/shard_map/ppermute | solution.py:468
  63.8 1.0 %collective-permute-done.14.rest_1_ = bf16[256,256]{1,0:T(8,128)(2,1)S(1)} collective-permute-done((bf16[256,256]{1,0:T(8,128)(2,1)S(1)}, bf16[256,256]{1,0:T(8,128)(2,1)S(1)}, u32[]{:S(2)}, u32[]{:S(2)}) %collective-permute-start.14) | collective-permute-done | bytes 131104 | tf_op jit(solution)/shard_map/ppermute | solution.py:468
  65.4 1.3 %base.1.base_ref = f32[2048,256]{1,0:T(8,128)S(1)} custom-call(f32[1,256]{1,0:T(1,128)S(1)} %bitcast.2, f32[2048,256]{1,0:T(8,128)S(1)} %get-tuple-element.48.y_ref, bf16[2048,1024]{1,0:T(8,128)(2,1)S(1)} %get-tuple-element.49.onehot, f32[1,2048]{1,0:T(1,128)S(1)} %add.7.refs_8_.total_ref, bf16[256,256]{1,0:T(8,128)(2,1)S(1)} %collective-permute-done.13.rest_0_, ...), custom_call_target="tpu_custom_call" | custom-call | flops 1073741824 | bytes 4194304 | tf_op jit(solution)/shard_map/base/pallas_call | solution.py:408
  66.7 1.6 %collective-permute-done.16.rest_0_ = bf16[256,256]{1,0:T(8,128)(2,1)S(1)} collective-permute-done((bf16[256,256]{1,0:T(8,128)(2,1)S(1)}, bf16[256,256]{1,0:T(8,128)(2,1)S(1)}, u32[]{:S(2)}, u32[]{:S(2)}) %collective-permute-start.16) | collective-permute-done | bytes 131104 | tf_op jit(solution)/shard_map/ppermute | solution.py:468
  68.4 2.0 %collective-permute-done.18.rest_2_ = bf16[256,256]{1,0:T(8,128)(2,1)S(1)} collective-permute-done((bf16[256,256]{1,0:T(8,128)(2,1)S(1)}, bf16[256,256]{1,0:T(8,128)(2,1)S(1)}, u32[]{:S(2)}, u32[]{:S(2)}) %collective-permute-start.18) | collective-permute-done | bytes 131104 | tf_op jit(solution)/shard_map/ppermute | solution.py:468
  70.8 2.1 %mix.1 = bf16[2048,256]{1,0:T(8,128)(2,1)} custom-call(f32[2048,256]{1,0:T(8,128)S(1)} %base.1.base_ref, bf16[2048,1024]{1,0:T(8,128)(2,1)S(1)} %get-tuple-element.43.rest_2_.onehot, bf16[256,256]{1,0:T(8,128)(2,1)S(1)} %collective-permute-done.16.rest_0_, bf16[256,256]{1,0:T(8,128)(2,1)S(1)} %collective-permute-done.17.rest_1_, ...), custom_call_target="tpu_custom_call" | custom-call | flops 1073741824 | bytes 4194304 | tf_op jit(solution)/shard_map/mix/pallas_call | solution.py:436
  (45 shorter events, 4.2 us)
Async XLA Ops:
  0.0 0.7 copy-start.8
  0.7 1.4 %copy-start.1 = (bf16[1,256,256]{2,1,0:T(8,128)(2,1)S(1)}, bf16[1,256,256]{2,1,0:T(8,128)(2,1)}, u32[]{:S(2)}) copy-start(bf16[1,256,256]{2,1,0:T(8,128)(2,1)} %one_ref.3) | copy-start | bytes 393220
  0.7 1.5 %copy-start.2 = (bf16[1,256,256]{2,1,0:T(8,128)(2,1)S(1)}, bf16[1,256,256]{2,1,0:T(8,128)(2,1)}, u32[]{:S(2)}) copy-start(bf16[1,256,256]{2,1,0:T(8,128)(2,1)} %three_ref.3) | copy-start | bytes 393220
  0.7 1.5 %copy-start.3 = (bf16[1,256,256]{2,1,0:T(8,128)(2,1)S(1)}, bf16[1,256,256]{2,1,0:T(8,128)(2,1)}, u32[]{:S(2)}) copy-start(bf16[1,256,256]{2,1,0:T(8,128)(2,1)} %two_ref.3) | copy-start | bytes 393220
  0.7 1.5 %copy-start.5 = (bf16[2048,256]{1,0:T(8,128)(2,1)S(1)}, bf16[2048,256]{1,0:T(8,128)(2,1)}, u32[]{:S(2)}) copy-start(bf16[2048,256]{1,0:T(8,128)(2,1)} %k_ref.7) | copy-start | bytes 3145732
  0.7 1.7 %copy-start.6 = (bf16[2048,256]{1,0:T(8,128)(2,1)S(1)}, bf16[2048,256]{1,0:T(8,128)(2,1)}, u32[]{:S(2)}) copy-start(bf16[2048,256]{1,0:T(8,128)(2,1)} %v_ref.7) | copy-start | bytes 3145732
  0.7 1.7 %copy-start.7 = (f32[2048,1]{0,1:T(1,128)S(1)}, f32[2048,1]{0,1:T(1,128)}, u32[]{:S(2)}) copy-start(f32[2048,1]{0,1:T(1,128)} %param.12) | copy-start | bytes 24580
  2.4 3.4 %copy-start = (bf16[2048,256]{1,0:T(8,128)(2,1)S(1)}, bf16[2048,256]{1,0:T(8,128)(2,1)}, u32[]{:S(2)}) copy-start(bf16[2048,256]{1,0:T(8,128)(2,1)} %q_ref.7) | copy-start | bytes 3145732
  5.3 2.3 %collective-permute-start = (f32[384,256]{1,0:T(8,128)S(1)}, f32[384,256]{1,0:T(8,128)S(1)}, u32[]{:S(2)}, u32[]{:S(2)}) collective-permute-start(f32[384,256]{1,0:T(8,128)S(1)} %get-tuple-element.36), channel_id=1, source_target_pairs={{0,4},{4,0},{8,12},{12,8},{16,20},{20,16},{24,28},{28,24},{1,5},{5... | collective-permute-start | bytes 1179656 | tf_op jit(solution)/shard_map/ppermute | solution.py:267
  7.8 7.0 %collective-permute-start.1 = (bf16[384,256]{1,0:T(8,128)(2,1)S(1)}, bf16[384,256]{1,0:T(8,128)(2,1)S(1)}, u32[]{:S(2)}, u32[]{:S(2)}) collective-permute-start(bf16[384,256]{1,0:T(8,128)(2,1)S(1)} %convert_element_type.6), channel_id=1, source_target_pairs={{0,8},{4,20},{8,0},{12,28},{16,24},{20,4},{24,16},{28,12},{1,9},{5... | collective-permute-start | bytes 589832 | tf_op jit(solution)/shard_map/ppermute | solution.py:279
  10.3 12.8 %collective-permute-start.3 = (bf16[256,768]{1,0:T(8,128)(2,1)S(1)}, bf16[256,768]{1,0:T(8,128)(2,1)S(1)}, u32[]{:S(2)}, u32[]{:S(2)}) collective-permute-start(bf16[256,768]{1,0:T(8,128)(2,1)S(1)} %get-tuple-element.39), channel_id=1, source_target_pairs={{0,28},{4,24},{8,20},{12,16},{16,12},{20,8},{24,4},{28,0},{1,29},{... | collective-permute-start | bytes 1179656 | tf_op jit(solution)/shard_map/ppermute | solution.py:463
  11.6 22.0 %collective-permute-start.4 = (bf16[256,768]{1,0:T(8,128)(2,1)S(1)}, bf16[256,768]{1,0:T(8,128)(2,1)S(1)}, u32[]{:S(2)}, u32[]{:S(2)}) collective-permute-start(bf16[256,768]{1,0:T(8,128)(2,1)S(1)} %get-tuple-element.40), channel_id=1, source_target_pairs={{0,24},{4,28},{8,16},{12,20},{16,8},{20,12},{24,0},{28,4},{1,25},{... | collective-permute-start | bytes 1179656 | tf_op jit(solution)/shard_map/ppermute | solution.py:463
  14.8 19.6 %collective-permute-start.2 = (bf16[384,256]{1,0:T(8,128)(2,1)S(1)}, bf16[384,256]{1,0:T(8,128)(2,1)S(1)}, u32[]{:S(2)}, u32[]{:S(2)}) collective-permute-start(bf16[384,256]{1,0:T(8,128)(2,1)S(1)} %convert_element_type.7), channel_id=1, source_target_pairs={{0,16},{4,12},{8,24},{12,4},{16,0},{20,28},{24,8},{28,20},{1,17},{... | collective-permute-start | bytes 589832 | tf_op jit(solution)/shard_map/ppermute | solution.py:279
  19.2 20.8 %collective-permute-start.6 = (bf16[256,768]{1,0:T(8,128)(2,1)S(1)}, bf16[256,768]{1,0:T(8,128)(2,1)S(1)}, u32[]{:S(2)}, u32[]{:S(2)}) collective-permute-start(bf16[256,768]{1,0:T(8,128)(2,1)S(1)} %get-tuple-element.44), channel_id=1, source_target_pairs={{0,20},{4,8},{8,28},{12,0},{16,4},{20,24},{24,12},{28,16},{1,21},{... | collective-permute-start | bytes 1179656 | tf_op jit(solution)/shard_map/ppermute | solution.py:463
  19.3 25.1 %collective-permute-start.7 = (bf16[256,768]{1,0:T(8,128)(2,1)S(1)}, bf16[256,768]{1,0:T(8,128)(2,1)S(1)}, u32[]{:S(2)}, u32[]{:S(2)}) collective-permute-start(bf16[256,768]{1,0:T(8,128)(2,1)S(1)} %get-tuple-element.45), channel_id=1, source_target_pairs={{0,16},{4,12},{8,24},{12,4},{16,0},{20,28},{24,8},{28,20},{1,17},{... | collective-permute-start | bytes 1179656 | tf_op jit(solution)/shard_map/ppermute | solution.py:463
  34.5 9.9 %collective-permute-start.5 = (f32[384,256]{1,0:T(8,128)S(1)}, f32[384,256]{1,0:T(8,128)S(1)}, u32[]{:S(2)}, u32[]{:S(2)}) collective-permute-start(f32[384,256]{1,0:T(8,128)S(1)} %merge.5.rest_0_), channel_id=1, source_target_pairs={{0,4},{4,0},{8,12},{12,8},{16,20},{20,16},{24,28},{28,24},{1,5},{5... | collective-permute-start | bytes 1179656 | tf_op jit(solution)/shard_map/ppermute | solution.py:284
  34.5 5.5 %copy-start.9 = (s32[1,2048]{1,0:T(1,128)S(1)}, s32[1,2048]{1,0:T(1,128)}, u32[]{:S(2)}) copy-start(s32[1,2048]{1,0:T(1,128)} %order_ref.3) | copy-start | bytes 24580
  38.0 17.4 %collective-permute-start.10 = (bf16[256,768]{1,0:T(8,128)(2,1)S(1)}, bf16[256,768]{1,0:T(8,128)(2,1)S(1)}, u32[]{:S(2)}, u32[]{:S(2)}) collective-permute-start(bf16[256,768]{1,0:T(8,128)(2,1)S(1)} %get-tuple-element.52), channel_id=1, source_target_pairs={{0,4},{4,0},{8,12},{12,8},{16,20},{20,16},{24,28},{28,24},{1,5},{5... | collective-permute-start | bytes 1179656 | tf_op jit(solution)/shard_map/ppermute | solution.py:463
  38.6 16.8 %collective-permute-start.11 = (bf16[256,768]{1,0:T(8,128)(2,1)S(1)}, bf16[256,768]{1,0:T(8,128)(2,1)S(1)}, u32[]{:S(2)}, u32[]{:S(2)}) collective-permute-start(bf16[256,768]{1,0:T(8,128)(2,1)S(1)} %get-tuple-element.53), channel_id=1, source_target_pairs={{0,8},{4,20},{8,0},{12,28},{16,24},{20,4},{24,16},{28,12},{1,9},{5... | collective-permute-start | bytes 1179656 | tf_op jit(solution)/shard_map/ppermute | solution.py:463
  40.0 15.4 %collective-permute-start.12 = (bf16[256,768]{1,0:T(8,128)(2,1)S(1)}, bf16[256,768]{1,0:T(8,128)(2,1)S(1)}, u32[]{:S(2)}, u32[]{:S(2)}) collective-permute-start(bf16[256,768]{1,0:T(8,128)(2,1)S(1)} %get-tuple-element.54), channel_id=1, source_target_pairs={{0,12},{4,16},{8,4},{12,24},{16,28},{20,0},{24,20},{28,8},{1,13},{... | collective-permute-start | bytes 1179656 | tf_op jit(solution)/shard_map/ppermute | solution.py:463
  47.1 18.4 %copy-start.4 = (f32[256]{0:T(256)S(1)}, f32[256]{0:T(256)}, u32[]{:S(2)}) copy-start(f32[256]{0:T(256)} %param.16) | copy-start | bytes 3076
  47.1 3.7 %collective-permute-start.8 = (f32[1,2048]{1,0:T(1,128)S(1)}, f32[1,2048]{1,0:T(1,128)S(1)}, u32[]{:S(2)}, u32[]{:S(2)}) collective-permute-start(f32[1,2048]{1,0:T(1,128)S(1)} %get-tuple-element.50), channel_id=1, source_target_pairs={{0,1},{1,0},{2,3},{3,2},{4,5},{5,4},{6,7},{7,6},{8,9},{9,8},{10,11... | collective-permute-start | bytes 24584 | tf_op jit(solution)/shard_map/ppermute | solution.py:457
  50.8 4.6 %collective-permute-start.9 = (f32[1,2048]{1,0:T(1,128)S(1)}, f32[1,2048]{1,0:T(1,128)S(1)}, u32[]{:S(2)}, u32[]{:S(2)}) collective-permute-start(f32[1,2048]{1,0:T(1,128)S(1)} %add.6), channel_id=1, source_target_pairs={{0,2},{1,3},{2,0},{3,1},{4,6},{5,7},{6,4},{7,5},{8,10},{9,11},{10,... | collective-permute-start | bytes 24584 | tf_op jit(solution)/shard_map/ppermute | solution.py:457
  57.0 6.8 %collective-permute-start.13 = (bf16[256,256]{1,0:T(8,128)(2,1)S(1)}, bf16[256,256]{1,0:T(8,128)(2,1)S(1)}, u32[]{:S(2)}, u32[]{:S(2)}) collective-permute-start(bf16[256,256]{1,0:T(8,128)(2,1)S(1)} %get-tuple-element.55), channel_id=1, source_target_pairs={{28,0},{24,4},{20,8},{16,12},{12,16},{8,20},{4,24},{0,28},{29,1},{... | collective-permute-start | bytes 393224 | tf_op jit(solution)/shard_map/ppermute | solution.py:468
  57.0 7.8 %collective-permute-start.14 = (bf16[256,256]{1,0:T(8,128)(2,1)S(1)}, bf16[256,256]{1,0:T(8,128)(2,1)S(1)}, u32[]{:S(2)}, u32[]{:S(2)}) collective-permute-start(bf16[256,256]{1,0:T(8,128)(2,1)S(1)} %get-tuple-element.56), channel_id=1, source_target_pairs={{24,0},{28,4},{16,8},{20,12},{8,16},{12,20},{0,24},{4,28},{25,1},{... | collective-permute-start | bytes 393224 | tf_op jit(solution)/shard_map/ppermute | solution.py:468
  58.5 6.9 %collective-permute-start.15 = (bf16[256,256]{1,0:T(8,128)(2,1)S(1)}, bf16[256,256]{1,0:T(8,128)(2,1)S(1)}, u32[]{:S(2)}, u32[]{:S(2)}) collective-permute-start(bf16[256,256]{1,0:T(8,128)(2,1)S(1)} %get-tuple-element.57), channel_id=1, source_target_pairs={{4,0},{0,4},{12,8},{8,12},{20,16},{16,20},{28,24},{24,28},{5,1},{1... | collective-permute-start | bytes 393224 | tf_op jit(solution)/shard_map/ppermute | solution.py:468
  59.8 8.5 %collective-permute-start.16 = (bf16[256,256]{1,0:T(8,128)(2,1)S(1)}, bf16[256,256]{1,0:T(8,128)(2,1)S(1)}, u32[]{:S(2)}, u32[]{:S(2)}) collective-permute-start(bf16[256,256]{1,0:T(8,128)(2,1)S(1)} %get-tuple-element.59), channel_id=1, source_target_pairs={{20,0},{8,4},{28,8},{0,12},{4,16},{24,20},{12,24},{16,28},{21,1},{... | collective-permute-start | bytes 393224 | tf_op jit(solution)/shard_map/ppermute | solution.py:468
  60.4 8.0 %collective-permute-start.17 = (bf16[256,256]{1,0:T(8,128)(2,1)S(1)}, bf16[256,256]{1,0:T(8,128)(2,1)S(1)}, u32[]{:S(2)}, u32[]{:S(2)}) collective-permute-start(bf16[256,256]{1,0:T(8,128)(2,1)S(1)} %get-tuple-element.60), channel_id=1, source_target_pairs={{16,0},{12,4},{24,8},{4,12},{0,16},{28,20},{8,24},{20,28},{17,1},{... | collective-permute-start | bytes 393224 | tf_op jit(solution)/shard_map/ppermute | solution.py:468
  63.8 6.6 %collective-permute-start.18 = (bf16[256,256]{1,0:T(8,128)(2,1)S(1)}, bf16[256,256]{1,0:T(8,128)(2,1)S(1)}, u32[]{:S(2)}, u32[]{:S(2)}) collective-permute-start(bf16[256,256]{1,0:T(8,128)(2,1)S(1)} %get-tuple-element.61), channel_id=1, source_target_pairs={{12,0},{16,4},{4,8},{24,12},{28,16},{0,20},{20,24},{8,28},{13,1},{... | collective-permute-start | bytes 393224 | tf_op jit(solution)/shard_map/ppermute | solution.py:468
  64.8 6.0 %collective-permute-start.19 = (bf16[256,256]{1,0:T(8,128)(2,1)S(1)}, bf16[256,256]{1,0:T(8,128)(2,1)S(1)}, u32[]{:S(2)}, u32[]{:S(2)}) collective-permute-start(bf16[256,256]{1,0:T(8,128)(2,1)S(1)} %get-tuple-element.62), channel_id=1, source_target_pairs={{8,0},{20,4},{0,8},{28,12},{24,16},{4,20},{16,24},{12,28},{9,1},{2... | collective-permute-start | bytes 393224 | tf_op jit(solution)/shard_map/ppermute | solution.py:468

commit v10 on v9

--- a/solution.py
+++ b/solution.py
@@ -220,7 +220,8 @@
         half = total.shape[0] // 2
         core = lax.axis_index("cam") & 1
         outs[0][...] = total[pl.ds(pl.multiple_of(core * half, half), half), :]
-        outs[1][...] = total[pl.ds(pl.multiple_of((1 - core) * half, half), half), :]
+        other = total[pl.ds(pl.multiple_of((1 - core) * half, half), half), :]
+        outs[1][...] = other.astype(BF16)
     else:
         outs[0][...] = total[...]
 
@@ -234,7 +235,9 @@
     parts = 2 if split else 1
     return pl.pallas_call(
         functools.partial(grads_kernel, n, split),
-        out_shape=[jax.ShapeDtypeStruct((rows // parts, width), F32)] * parts,
+        out_shape=[
+            jax.ShapeDtypeStruct((rows // parts, width), kind) for kind in (F32, BF16)[:parts]
+        ],
         in_specs=full(6) + [pl.BlockSpec(memory_space=pl.ANY)],
         out_specs=full(parts),
         scratch_shapes=[pltpu.VMEM((rows, width), F32)],
@@ -485,13 +488,13 @@
         for step, block in zip(group, blocks):
             arrived[step] = exchange(block, step, n)
     came = [arrived[step] for step in steps]
-    parts = gradients(keys, values, rates.reshape(1, count), *weights, marks[-1], n)
-    mine = core_step(parts, tokens[:1], n)
-    summed = sum_over_chips(mine, len(parts) == 2, [[], came[:2] + tokens[1:2]], n)
+    parts = gradients(keys, values, rates.reshape(1, count), *weights, tokens[0], n)
     early = steps[:few] + steps[n - few :]
     late = steps[few : n - few]
     early_places, late_places = place(order, n, early + late)
-    y, square = read_out(queries, *weights, summed, [late_places] + came[2:4] + tokens[2:])
+    mine = core_step(parts, [came[0]], n)
+    summed = sum_over_chips(mine, len(parts) == 2, [tokens[1:2], came[1:3] + tokens[2:] + [late_places]], n)
+    y, square = read_out(queries, *weights, summed, came[3:4])
     total = sum_over_heads(square, heads)
     attended = attend([arrived[step] for step in range(n)], [total], n, width)
     returned = {step: give_back(attended[step], step, n) for step in early + late}

time: 73.3 us -> 71.2 us (0.971)
  waiting for transfers between devices: 29.6 us -> 26.9 us
    ppermute x7, waiting for transfers between devices: 15.6 us -> 4.77 us  [exchange(): return lax.ppermute(block, 'cam', routes(step, n)) if step else block]
    ppermute x2, waiting for transfers between devices: 2.43 us -> 9.93 us  [sum_over_chips(): got = lax.ppermute(mine.astype(BF16), 'cam', pairs)]
    ppermute x2, starting transfers between devices: 5.2 us -> 2.53 us  [sum_over_chips(): got = lax.ppermute(mine.astype(BF16), 'cam', pairs)]
    ppermute x7, starting transfers between devices: 6.21 us -> 8.05 us  [exchange(): return lax.ppermute(block, 'cam', routes(step, n)) if step else block]
    ppermute x1, waiting for transfers between devices: 0.01 us -> 1.07 us  [core_step(): return merge(parts[0], lax.ppermute(parts[1], 'cam', pair), after)]
  transfers between devices with their start and end apart: 20 -> 20, of which waited for: 13 -> 12; matrix products, arithmetic and copies ran while one was open for 0% -> 0% of each run, Pallas kernels for 18% -> 20%
where the time goes in v10:
time: 71.2 us; the launch traced here: 71 us
  waiting for transfers between devices  26.9 us (38%)
  starting transfers between devices  21.8 us (31%)
  Pallas kernels  20.7 us (29%)
  local copies, waits for them, and re-layouts  1.16 us (2%)
    ppermute x2, waiting for transfers between devices, sum_over_chips(): got = lax.ppermute(mine.astype(BF16), 'cam', pairs)  9.93 us
    ppermute x7, starting transfers between devices, exchange(): return lax.ppermute(block, 'cam', routes(step, n)) if step else block  8.05 us
    ppermute x7, waiting for transfers between devices, give_back(): return lax.ppermute(block, 'cam', pairs) if step else block  7.08 us
    pallas_call x3, Pallas kernels, sort_tokens(): pl.pallas_call(functools.partial(sort_kernel, size), out_shape=[jax.Shape...  7.03 us
    ppermute x7, starting transfers between devices, give_back(): return lax.ppermute(block, 'cam', pairs) if step else block  5.43 us
    ppermute x7, waiting for transfers between devices, exchange(): return lax.ppermute(block, 'cam', routes(step, n)) if step else block  4.77 us
    ppermute x2, starting transfers between devices, sum_over_heads(): square = square + lax.ppermute(square, 'head', pairs)  4.27 us
    ppermute x2, waiting for transfers between devices, sum_over_heads(): square = square + lax.ppermute(square, 'head', pairs)  4.03 us
  transfers between devices with their start and end apart: 20, of which 12 were waited for; matrix products, arithmetic and copies ran while one was open for 0% of the time, Pallas kernels for 20%

profile of v10, /device:TPU:0, one launch (start us, length us, event | category | flops | bytes accessed | tf_op | source)
XLA Modules:
  0.0 71.0 jit_solution(228407077242259276)
XLA Ops:
  0.7 1.4 %mark.1 = (bf16[512,2048]{1,0:T(8,128)(2,1)S(1)}, bf16[512,2048]{1,0:T(8,128)(2,1)S(1)}, bf16[1024,2048]{1,0:T(8,128)(2,1)S(1)}, f32[8,128]{1,0:T(8,128)}) custom-call(s32[1,2048]{1,0:T(1,128)S(1)} %copy-done.8), custom_call_target="tpu_custom_call" | custom-call | flops 999999995904 | bytes 1024 | tf_op jit(solution)/shard_map/mark/pallas_call | solution.py:107
  2.6 1.8 %sort_tokens.3 = (bf16[256,768]{1,0:T(8,128)(2,1)S(1)}, bf16[256,768]{1,0:T(8,128)(2,1)S(1)}, f32[8,128]{1,0:T(8,128)S(1)}) custom-call(bf16[512,2048]{1,0:T(8,128)(2,1)S(1)} %get-tuple-element.33.onehot, bf16[2048,256]{1,0:T(8,128)(2,1)S(1)} %copy-done.3, bf16[2048,256]{1,0:T(8,128)(2,1)S(1)} %copy-done.1, bf16[2048,256]{1,0:T(8,128)(2,1)S(1)} %copy-done.2), custom_call_target="tpu_custom_call" | custom-call | flops 1610612736 | bytes 3145728 | tf_op jit(solution)/shard_map/sort_tokens/pallas_call | solution.py:140
  4.4 3.4 %collective-permute-start.1 = (bf16[256,768]{1,0:T(8,128)(2,1)S(1)}, bf16[256,768]{1,0:T(8,128)(2,1)S(1)}, u32[]{:S(2)}, u32[]{:S(2)}) collective-permute-start(bf16[256,768]{1,0:T(8,128)(2,1)S(1)} %get-tuple-element.37), channel_id=1, source_target_pairs={{0,28},{4,24},{8,20},{12,16},{16,12},{20,8},{24,4},{28,0},{1,29},{... | collective-permute-start | bytes 1179656 | tf_op jit(solution)/shard_map/ppermute | solution.py:466
  7.8 2.9 %gradients.1 = (f32[384,256]{1,0:T(8,128)S(1)}, bf16[384,256]{1,0:T(8,128)(2,1)S(1)}) custom-call(bf16[2048,256]{1,0:T(8,128)(2,1)S(1)} %copy-done.1, bf16[2048,256]{1,0:T(8,128)(2,1)S(1)} %copy-done.2, f32[1,2048]{1,0:T(1,128)S(1)} %bitcast.3, bf16[1,256,256]{2,1,0:T(8,128)(2,1)S(1)} %copy-done.4, bf16[1,256,256]{2,1,0:T(8,128)(2,1)S(1)} %copy-done.5, ...), custom_call_target="tpu_custom_call" | custom-call | flops 1610612736 | bytes 4194304 | tf_op jit(solution)/shard_map/gradients/pallas_call | solution.py:236
  10.7 0.7 %collective-permute-start = (bf16[384,256]{1,0:T(8,128)(2,1)S(1)}, bf16[384,256]{1,0:T(8,128)(2,1)S(1)}, u32[]{:S(2)}, u32[]{:S(2)}) collective-permute-start(bf16[384,256]{1,0:T(8,128)(2,1)S(1)} %get-tuple-element.36), channel_id=1, source_target_pairs={{0,4},{4,0},{8,12},{12,8},{16,20},{20,16},{24,28},{28,24},{1,5},{5... | collective-permute-start | bytes 589832 | tf_op jit(solution)/shard_map/ppermute | solution.py:270
  11.5 1.1 %collective-permute-done.got_ref = bf16[384,256]{1,0:T(8,128)(2,1)S(1)} collective-permute-done((bf16[384,256]{1,0:T(8,128)(2,1)S(1)}, bf16[384,256]{1,0:T(8,128)(2,1)S(1)}, u32[]{:S(2)}, u32[]{:S(2)}) %collective-permute-start) | collective-permute-done | bytes 196640 | tf_op jit(solution)/shard_map/ppermute | solution.py:270
  12.5 4.8 %collective-permute-done.1.rest_0_.refs_7_ = bf16[256,768]{1,0:T(8,128)(2,1)S(1)} collective-permute-done((bf16[256,768]{1,0:T(8,128)(2,1)S(1)}, bf16[256,768]{1,0:T(8,128)(2,1)S(1)}, u32[]{:S(2)}, u32[]{:S(2)}) %collective-permute-start.1) | collective-permute-done | bytes 393248 | tf_op jit(solution)/shard_map/ppermute | solution.py:466
  17.4 2.5 %collective-permute-start.2 = (bf16[384,256]{1,0:T(8,128)(2,1)S(1)}, bf16[384,256]{1,0:T(8,128)(2,1)S(1)}, u32[]{:S(2)}, u32[]{:S(2)}) collective-permute-start(bf16[384,256]{1,0:T(8,128)(2,1)S(1)} %convert_element_type.6), channel_id=1, source_target_pairs={{0,8},{4,20},{8,0},{12,28},{16,24},{20,4},{24,16},{28,12},{1,9},{5... | collective-permute-start | bytes 589832 | tf_op jit(solution)/shard_map/ppermute | solution.py:282
  19.8 1.8 %sort_tokens.4 = (bf16[256,768]{1,0:T(8,128)(2,1)S(1)}, bf16[256,768]{1,0:T(8,128)(2,1)S(1)}, f32[8,128]{1,0:T(8,128)S(1)}) custom-call(bf16[512,2048]{1,0:T(8,128)(2,1)S(1)} %get-tuple-element.38.onehot, bf16[2048,256]{1,0:T(8,128)(2,1)S(1)} %copy-done.3, bf16[2048,256]{1,0:T(8,128)(2,1)S(1)} %copy-done.1, bf16[2048,256]{1,0:T(8,128)(2,1)S(1)} %copy-done.2), custom_call_target="tpu_custom_call" | custom-call | flops 1610612736 | bytes 3145728 | tf_op jit(solution)/shard_map/sort_tokens/pallas_call | solution.py:140
  21.7 1.6 %collective-permute-start.7 = (bf16[256,768]{1,0:T(8,128)(2,1)S(1)}, bf16[256,768]{1,0:T(8,128)(2,1)S(1)}, u32[]{:S(2)}, u32[]{:S(2)}) collective-permute-start(bf16[256,768]{1,0:T(8,128)(2,1)S(1)} %get-tuple-element.45), channel_id=1, source_target_pairs={{0,16},{4,12},{8,24},{12,4},{16,0},{20,28},{24,8},{28,20},{1,17},{... | collective-permute-start | bytes 1179656 | tf_op jit(solution)/shard_map/ppermute | solution.py:466
  23.3 1.7 %place.1 = (bf16[2048,1024]{1,0:T(8,128)(2,1)S(1)}, bf16[2048,1024]{1,0:T(8,128)(2,1)S(1)}) custom-call(s32[1,2048]{1,0:T(1,128)S(1)} %copy-done.9), custom_call_target="tpu_custom_call" | custom-call | flops 4194304 | bytes 8388608 | tf_op jit(solution)/shard_map/place/pallas_call | solution.py:373
  25.0 6.0 %collective-permute-done.2.got_ref = bf16[384,256]{1,0:T(8,128)(2,1)S(1)} collective-permute-done((bf16[384,256]{1,0:T(8,128)(2,1)S(1)}, bf16[384,256]{1,0:T(8,128)(2,1)S(1)}, u32[]{:S(2)}, u32[]{:S(2)}) %collective-permute-start.2) | collective-permute-done | bytes 196640 | tf_op jit(solution)/shard_map/ppermute | solution.py:282
  31.1 3.4 %sort_tokens.5 = (bf16[256,768]{1,0:T(8,128)(2,1)S(1)}, bf16[256,768]{1,0:T(8,128)(2,1)S(1)}, bf16[256,768]{1,0:T(8,128)(2,1)S(1)}, bf16[256,768]{1,0:T(8,128)(2,1)S(1)}, f32[8,128]{1,0:T(8,128)S(1)}) custom-call(bf16[1024,2048]{1,0:T(8,128)(2,1)S(1)} %get-tuple-element.42.onehot, bf16[2048,256]{1,0:T(8,128)(2,1)S(1)} %copy-done.3, ...), custom_call_target="tpu_custom_call" | custom-call | flops 3221225472 | bytes 3145728 | tf_op jit(solution)/shard_map/sort_tokens/pallas_call | solution.py:140
  34.6 3.9 %collective-permute-done.3.got_ref = bf16[384,256]{1,0:T(8,128)(2,1)S(1)} collective-permute-done((bf16[384,256]{1,0:T(8,128)(2,1)S(1)}, bf16[384,256]{1,0:T(8,128)(2,1)S(1)}, u32[]{:S(2)}, u32[]{:S(2)}) %collective-permute-start.3) | collective-permute-done | bytes 196640 | tf_op jit(solution)/shard_map/ppermute | solution.py:282
  39.4 2.0 %collective-permute-start.11 = (bf16[256,768]{1,0:T(8,128)(2,1)S(1)}, bf16[256,768]{1,0:T(8,128)(2,1)S(1)}, u32[]{:S(2)}, u32[]{:S(2)}) collective-permute-start(bf16[256,768]{1,0:T(8,128)(2,1)S(1)} %get-tuple-element.51), channel_id=1, source_target_pairs={{0,8},{4,20},{8,0},{12,28},{16,24},{20,4},{24,16},{28,12},{1,9},{5... | collective-permute-start | bytes 1179656 | tf_op jit(solution)/shard_map/ppermute | solution.py:466
  41.4 0.9 %collective-permute-start.12 = (bf16[256,768]{1,0:T(8,128)(2,1)S(1)}, bf16[256,768]{1,0:T(8,128)(2,1)S(1)}, u32[]{:S(2)}, u32[]{:S(2)}) collective-permute-start(bf16[256,768]{1,0:T(8,128)(2,1)S(1)} %get-tuple-element.52), channel_id=1, source_target_pairs={{0,12},{4,16},{8,4},{12,24},{16,28},{20,0},{24,20},{28,8},{1,13},{... | collective-permute-start | bytes 1179656 | tf_op jit(solution)/shard_map/ppermute | solution.py:466
  42.3 2.7 %read_out.1 = (f32[2048,256]{1,0:T(8,128)S(1)}, f32[1,2048]{1,0:T(1,128)S(1)}) custom-call(bf16[2048,256]{1,0:T(8,128)(2,1)S(1)} %copy-done.3, bf16[1,256,256]{2,1,0:T(8,128)(2,1)S(1)} %copy-done.4, bf16[1,256,256]{2,1,0:T(8,128)(2,1)S(1)} %copy-done.5, bf16[1,256,256]{2,1,0:T(8,128)(2,1)S(1)} %copy-done.6, f32[384,256]{1,0:T(8,128)S(1)} %merge.5.rest_0_, ...), custom_call_target="tpu_custom_call" | custom-call | flops 805306368 | bytes 4194304 | tf_op jit(solution)/shard_map/read_out/pallas_call | solution.py:334
  45.0 1.6 %collective-permute-start.8 = (f32[1,2048]{1,0:T(1,128)S(1)}, f32[1,2048]{1,0:T(1,128)S(1)}, u32[]{:S(2)}, u32[]{:S(2)}) collective-permute-start(f32[1,2048]{1,0:T(1,128)S(1)} %get-tuple-element.48), channel_id=1, source_target_pairs={{0,1},{1,0},{2,3},{3,2},{4,5},{5,4},{6,7},{7,6},{8,9},{9,8},{10,11... | collective-permute-start | bytes 24584 | tf_op jit(solution)/shard_map/ppermute | solution.py:460
  46.6 2.1 %collective-permute-done.8 = f32[1,2048]{1,0:T(1,128)S(1)} collective-permute-done((f32[1,2048]{1,0:T(1,128)S(1)}, f32[1,2048]{1,0:T(1,128)S(1)}, u32[]{:S(2)}, u32[]{:S(2)}) %collective-permute-start.8) | collective-permute-done | bytes 8224 | tf_op jit(solution)/shard_map/ppermute | solution.py:460
  48.7 2.7 %collective-permute-start.9 = (f32[1,2048]{1,0:T(1,128)S(1)}, f32[1,2048]{1,0:T(1,128)S(1)}, u32[]{:S(2)}, u32[]{:S(2)}) collective-permute-start(f32[1,2048]{1,0:T(1,128)S(1)} %add.6), channel_id=1, source_target_pairs={{0,2},{1,3},{2,0},{3,1},{4,6},{5,7},{6,4},{7,5},{8,10},{9,11},{10,... | collective-permute-start | bytes 24584 | tf_op jit(solution)/shard_map/ppermute | solution.py:460
  51.3 2.0 %collective-permute-done.9 = f32[1,2048]{1,0:T(1,128)S(1)} collective-permute-done((f32[1,2048]{1,0:T(1,128)S(1)}, f32[1,2048]{1,0:T(1,128)S(1)}, u32[]{:S(2)}, u32[]{:S(2)}) %collective-permute-start.9) | collective-permute-done | bytes 8224 | tf_op jit(solution)/shard_map/ppermute | solution.py:460
  53.4 1.5 %attend.1 = (bf16[256,256]{1,0:T(8,128)(2,1)S(1)}, bf16[256,256]{1,0:T(8,128)(2,1)S(1)}, bf16[256,256]{1,0:T(8,128)(2,1)S(1)}, bf16[256,256]{1,0:T(8,128)(2,1)S(...) custom-call(bf16[256,768]{1,0:T(8,128)(2,1)S(1)} %get-tuple-element., ...), custom_call_target="tpu_custom_call" | custom-call | flops 536870912 | bytes 4194304 | tf_op jit(solution)/shard_map/attend/pallas_call | solution.py:179
  54.9 0.8 %collective-permute-start.13 = (bf16[256,256]{1,0:T(8,128)(2,1)S(1)}, bf16[256,256]{1,0:T(8,128)(2,1)S(1)}, u32[]{:S(2)}, u32[]{:S(2)}) collective-permute-start(bf16[256,256]{1,0:T(8,128)(2,1)S(1)} %get-tuple-element.53), channel_id=1, source_target_pairs={{28,0},{24,4},{20,8},{16,12},{12,16},{8,20},{4,24},{0,28},{29,1},{... | collective-permute-start | bytes 393224 | tf_op jit(solution)/shard_map/ppermute | solution.py:471
  56.3 1.4 %collective-permute-start.15 = (bf16[256,256]{1,0:T(8,128)(2,1)S(1)}, bf16[256,256]{1,0:T(8,128)(2,1)S(1)}, u32[]{:S(2)}, u32[]{:S(2)}) collective-permute-start(bf16[256,256]{1,0:T(8,128)(2,1)S(1)} %get-tuple-element.55), channel_id=1, source_target_pairs={{4,0},{0,4},{12,8},{8,12},{20,16},{16,20},{28,24},{24,28},{5,1},{1... | collective-permute-start | bytes 393224 | tf_op jit(solution)/shard_map/ppermute | solution.py:471
  57.9 1.4 %collective-permute-start.17 = (bf16[256,256]{1,0:T(8,128)(2,1)S(1)}, bf16[256,256]{1,0:T(8,128)(2,1)S(1)}, u32[]{:S(2)}, u32[]{:S(2)}) collective-permute-start(bf16[256,256]{1,0:T(8,128)(2,1)S(1)} %get-tuple-element.58), channel_id=1, source_target_pairs={{16,0},{12,4},{24,8},{4,12},{0,16},{28,20},{8,24},{20,28},{17,1},{... | collective-permute-start | bytes 393224 | tf_op jit(solution)/shard_map/ppermute | solution.py:471
  59.3 1.7 %collective-permute-done.13.rest_0_ = bf16[256,256]{1,0:T(8,128)(2,1)S(1)} collective-permute-done((bf16[256,256]{1,0:T(8,128)(2,1)S(1)}, bf16[256,256]{1,0:T(8,128)(2,1)S(1)}, u32[]{:S(2)}, u32[]{:S(2)}) %collective-permute-start.13) | collective-permute-done | bytes 131104 | tf_op jit(solution)/shard_map/ppermute | solution.py:471
  61.0 2.1 %collective-permute-done.14.rest_1_ = bf16[256,256]{1,0:T(8,128)(2,1)S(1)} collective-permute-done((bf16[256,256]{1,0:T(8,128)(2,1)S(1)}, bf16[256,256]{1,0:T(8,128)(2,1)S(1)}, u32[]{:S(2)}, u32[]{:S(2)}) %collective-permute-start.14) | collective-permute-done | bytes 131104 | tf_op jit(solution)/shard_map/ppermute | solution.py:471
  63.0 1.1 %collective-permute-start.19 = (bf16[256,256]{1,0:T(8,128)(2,1)S(1)}, bf16[256,256]{1,0:T(8,128)(2,1)S(1)}, u32[]{:S(2)}, u32[]{:S(2)}) collective-permute-start(bf16[256,256]{1,0:T(8,128)(2,1)S(1)} %get-tuple-element.60), channel_id=1, source_target_pairs={{8,0},{20,4},{0,8},{28,12},{24,16},{4,20},{16,24},{12,28},{9,1},{2... | collective-permute-start | bytes 393224 | tf_op jit(solution)/shard_map/ppermute | solution.py:471
  64.1 1.3 %base.1.base_ref = f32[2048,256]{1,0:T(8,128)S(1)} custom-call(f32[1,256]{1,0:T(1,128)S(1)} %bitcast.2, f32[2048,256]{1,0:T(8,128)S(1)} %get-tuple-element.46.y_ref, bf16[2048,1024]{1,0:T(8,128)(2,1)S(1)} %get-tuple-element.47.onehot, f32[1,2048]{1,0:T(1,128)S(1)} %add.7.refs_8_.total_ref, bf16[256,256]{1,0:T(8,128)(2,1)S(1)} %collective-permute-done.13.rest_0_, ...), custom_call_target="tpu_custom_call" | custom-call | flops 1073741824 | bytes 4194304 | tf_op jit(solution)/shard_map/base/pallas_call | solution.py:411
  66.2 1.8 %collective-permute-done.18.rest_2_ = bf16[256,256]{1,0:T(8,128)(2,1)S(1)} collective-permute-done((bf16[256,256]{1,0:T(8,128)(2,1)S(1)}, bf16[256,256]{1,0:T(8,128)(2,1)S(1)}, u32[]{:S(2)}, u32[]{:S(2)}) %collective-permute-start.18) | collective-permute-done | bytes 131104 | tf_op jit(solution)/shard_map/ppermute | solution.py:471
  67.9 0.8 %collective-permute-done.19.rest_3_ = bf16[256,256]{1,0:T(8,128)(2,1)S(1)} collective-permute-done((bf16[256,256]{1,0:T(8,128)(2,1)S(1)}, bf16[256,256]{1,0:T(8,128)(2,1)S(1)}, u32[]{:S(2)}, u32[]{:S(2)}) %collective-permute-start.19) | collective-permute-done | bytes 131104 | tf_op jit(solution)/shard_map/ppermute | solution.py:471
  68.7 2.1 %mix.1 = bf16[2048,256]{1,0:T(8,128)(2,1)} custom-call(f32[2048,256]{1,0:T(8,128)S(1)} %base.1.base_ref, bf16[2048,1024]{1,0:T(8,128)(2,1)S(1)} %get-tuple-element.44.rest_3_.onehot, bf16[256,256]{1,0:T(8,128)(2,1)S(1)} %collective-permute-done.16.rest_0_, bf16[256,256]{1,0:T(8,128)(2,1)S(1)} %collective-permute-done.17.rest_1_, ...), custom_call_target="tpu_custom_call" | custom-call | flops 1073741824 | bytes 4194304 | tf_op jit(solution)/shard_map/mix/pallas_call | solution.py:439
  (45 shorter events, 3.8 us)
Async XLA Ops:
  0.0 0.7 copy-start.8
  0.7 1.4 %copy-start.1 = (bf16[2048,256]{1,0:T(8,128)(2,1)S(1)}, bf16[2048,256]{1,0:T(8,128)(2,1)}, u32[]{:S(2)}) copy-start(bf16[2048,256]{1,0:T(8,128)(2,1)} %k_ref.7) | copy-start | bytes 3145732
  0.7 1.5 %copy-start.2 = (bf16[2048,256]{1,0:T(8,128)(2,1)S(1)}, bf16[2048,256]{1,0:T(8,128)(2,1)}, u32[]{:S(2)}) copy-start(bf16[2048,256]{1,0:T(8,128)(2,1)} %v_ref.7) | copy-start | bytes 3145732
  0.7 1.9 %copy-start.3 = (bf16[2048,256]{1,0:T(8,128)(2,1)S(1)}, bf16[2048,256]{1,0:T(8,128)(2,1)}, u32[]{:S(2)}) copy-start(bf16[2048,256]{1,0:T(8,128)(2,1)} %q_ref.7) | copy-start | bytes 3145732
  2.6 5.2 %copy-start.4 = (bf16[1,256,256]{2,1,0:T(8,128)(2,1)S(1)}, bf16[1,256,256]{2,1,0:T(8,128)(2,1)}, u32[]{:S(2)}) copy-start(bf16[1,256,256]{2,1,0:T(8,128)(2,1)} %one_ref.3) | copy-start | bytes 393220
  2.6 5.2 %copy-start.5 = (bf16[1,256,256]{2,1,0:T(8,128)(2,1)S(1)}, bf16[1,256,256]{2,1,0:T(8,128)(2,1)}, u32[]{:S(2)}) copy-start(bf16[1,256,256]{2,1,0:T(8,128)(2,1)} %three_ref.3) | copy-start | bytes 393220
  2.6 5.2 %copy-start.6 = (bf16[1,256,256]{2,1,0:T(8,128)(2,1)S(1)}, bf16[1,256,256]{2,1,0:T(8,128)(2,1)}, u32[]{:S(2)}) copy-start(bf16[1,256,256]{2,1,0:T(8,128)(2,1)} %two_ref.3) | copy-start | bytes 393220
  2.6 5.2 %copy-start.7 = (f32[2048,1]{0,1:T(1,128)S(1)}, f32[2048,1]{0,1:T(1,128)}, u32[]{:S(2)}) copy-start(f32[2048,1]{0,1:T(1,128)} %param.12) | copy-start | bytes 24580
  4.4 12.9 %collective-permute-start.1 = (bf16[256,768]{1,0:T(8,128)(2,1)S(1)}, bf16[256,768]{1,0:T(8,128)(2,1)S(1)}, u32[]{:S(2)}, u32[]{:S(2)}) collective-permute-start(bf16[256,768]{1,0:T(8,128)(2,1)S(1)} %get-tuple-element.37), channel_id=1, source_target_pairs={{0,28},{4,24},{8,20},{12,16},{16,12},{20,8},{24,4},{28,0},{1,29},{... | collective-permute-start | bytes 1179656 | tf_op jit(solution)/shard_map/ppermute | solution.py:466
  10.7 1.8 %collective-permute-start = (bf16[384,256]{1,0:T(8,128)(2,1)S(1)}, bf16[384,256]{1,0:T(8,128)(2,1)S(1)}, u32[]{:S(2)}, u32[]{:S(2)}) collective-permute-start(bf16[384,256]{1,0:T(8,128)(2,1)S(1)} %get-tuple-element.36), channel_id=1, source_target_pairs={{0,4},{4,0},{8,12},{12,8},{16,20},{20,16},{24,28},{28,24},{1,5},{5... | collective-permute-start | bytes 589832 | tf_op jit(solution)/shard_map/ppermute | solution.py:270
  11.5 23.1 %collective-permute-start.4 = (bf16[256,768]{1,0:T(8,128)(2,1)S(1)}, bf16[256,768]{1,0:T(8,128)(2,1)S(1)}, u32[]{:S(2)}, u32[]{:S(2)}) collective-permute-start(bf16[256,768]{1,0:T(8,128)(2,1)S(1)} %get-tuple-element.40), channel_id=1, source_target_pairs={{0,24},{4,28},{8,16},{12,20},{16,8},{20,12},{24,0},{28,4},{1,25},{... | collective-permute-start | bytes 1179656 | tf_op jit(solution)/shard_map/ppermute | solution.py:466
  17.4 13.6 %collective-permute-start.2 = (bf16[384,256]{1,0:T(8,128)(2,1)S(1)}, bf16[384,256]{1,0:T(8,128)(2,1)S(1)}, u32[]{:S(2)}, u32[]{:S(2)}) collective-permute-start(bf16[384,256]{1,0:T(8,128)(2,1)S(1)} %convert_element_type.6), channel_id=1, source_target_pairs={{0,8},{4,20},{8,0},{12,28},{16,24},{20,4},{24,16},{28,12},{1,9},{5... | collective-permute-start | bytes 589832 | tf_op jit(solution)/shard_map/ppermute | solution.py:282
  19.8 3.5 %copy-start.9 = (s32[1,2048]{1,0:T(1,128)S(1)}, s32[1,2048]{1,0:T(1,128)}, u32[]{:S(2)}) copy-start(s32[1,2048]{1,0:T(1,128)} %order_ref.3) | copy-start | bytes 24580
  21.6 13.0 %collective-permute-start.5 = (bf16[256,768]{1,0:T(8,128)(2,1)S(1)}, bf16[256,768]{1,0:T(8,128)(2,1)S(1)}, u32[]{:S(2)}, u32[]{:S(2)}) collective-permute-start(bf16[256,768]{1,0:T(8,128)(2,1)S(1)} %get-tuple-element.41), channel_id=1, source_target_pairs={{0,20},{4,8},{8,28},{12,0},{16,4},{20,24},{24,12},{28,16},{1,21},{... | collective-permute-start | bytes 1179656 | tf_op jit(solution)/shard_map/ppermute | solution.py:466
  21.7 20.6 %collective-permute-start.7 = (bf16[256,768]{1,0:T(8,128)(2,1)S(1)}, bf16[256,768]{1,0:T(8,128)(2,1)S(1)}, u32[]{:S(2)}, u32[]{:S(2)}) collective-permute-start(bf16[256,768]{1,0:T(8,128)(2,1)S(1)} %get-tuple-element.45), channel_id=1, source_target_pairs={{0,16},{4,12},{8,24},{12,4},{16,0},{20,28},{24,8},{28,20},{1,17},{... | collective-permute-start | bytes 1179656 | tf_op jit(solution)/shard_map/ppermute | solution.py:466
  31.0 7.5 %collective-permute-start.3 = (bf16[384,256]{1,0:T(8,128)(2,1)S(1)}, bf16[384,256]{1,0:T(8,128)(2,1)S(1)}, u32[]{:S(2)}, u32[]{:S(2)}) collective-permute-start(bf16[384,256]{1,0:T(8,128)(2,1)S(1)} %convert_element_type.7), channel_id=1, source_target_pairs={{0,16},{4,12},{8,24},{12,4},{16,0},{20,28},{24,8},{28,20},{1,17},{... | collective-permute-start | bytes 589832 | tf_op jit(solution)/shard_map/ppermute | solution.py:282
  38.6 3.8 %collective-permute-start.6 = (f32[384,256]{1,0:T(8,128)S(1)}, f32[384,256]{1,0:T(8,128)S(1)}, u32[]{:S(2)}, u32[]{:S(2)}) collective-permute-start(f32[384,256]{1,0:T(8,128)S(1)} %merge.5.rest_0_), channel_id=1, source_target_pairs={{0,4},{4,0},{8,12},{12,8},{16,20},{20,16},{24,28},{28,24},{1,5},{5... | collective-permute-start | bytes 1179656 | tf_op jit(solution)/shard_map/ppermute | solution.py:287
  39.3 14.0 %collective-permute-start.10 = (bf16[256,768]{1,0:T(8,128)(2,1)S(1)}, bf16[256,768]{1,0:T(8,128)(2,1)S(1)}, u32[]{:S(2)}, u32[]{:S(2)}) collective-permute-start(bf16[256,768]{1,0:T(8,128)(2,1)S(1)} %get-tuple-element.50), channel_id=1, source_target_pairs={{0,4},{4,0},{8,12},{12,8},{16,20},{20,16},{24,28},{28,24},{1,5},{5... | collective-permute-start | bytes 1179656 | tf_op jit(solution)/shard_map/ppermute | solution.py:466
  39.4 14.0 %collective-permute-start.11 = (bf16[256,768]{1,0:T(8,128)(2,1)S(1)}, bf16[256,768]{1,0:T(8,128)(2,1)S(1)}, u32[]{:S(2)}, u32[]{:S(2)}) collective-permute-start(bf16[256,768]{1,0:T(8,128)(2,1)S(1)} %get-tuple-element.51), channel_id=1, source_target_pairs={{0,8},{4,20},{8,0},{12,28},{16,24},{20,4},{24,16},{28,12},{1,9},{5... | collective-permute-start | bytes 1179656 | tf_op jit(solution)/shard_map/ppermute | solution.py:466
  41.4 12.0 %collective-permute-start.12 = (bf16[256,768]{1,0:T(8,128)(2,1)S(1)}, bf16[256,768]{1,0:T(8,128)(2,1)S(1)}, u32[]{:S(2)}, u32[]{:S(2)}) collective-permute-start(bf16[256,768]{1,0:T(8,128)(2,1)S(1)} %get-tuple-element.52), channel_id=1, source_target_pairs={{0,12},{4,16},{8,4},{12,24},{16,28},{20,0},{24,20},{28,8},{1,13},{... | collective-permute-start | bytes 1179656 | tf_op jit(solution)/shard_map/ppermute | solution.py:466
  45.0 19.1 %copy-start = (f32[256]{0:T(256)S(1)}, f32[256]{0:T(256)}, u32[]{:S(2)}) copy-start(f32[256]{0:T(256)} %param.16) | copy-start | bytes 3076
  45.0 3.7 %collective-permute-start.8 = (f32[1,2048]{1,0:T(1,128)S(1)}, f32[1,2048]{1,0:T(1,128)S(1)}, u32[]{:S(2)}, u32[]{:S(2)}) collective-permute-start(f32[1,2048]{1,0:T(1,128)S(1)} %get-tuple-element.48), channel_id=1, source_target_pairs={{0,1},{1,0},{2,3},{3,2},{4,5},{5,4},{6,7},{7,6},{8,9},{9,8},{10,11... | collective-permute-start | bytes 24584 | tf_op jit(solution)/shard_map/ppermute | solution.py:460
  48.7 4.6 %collective-permute-start.9 = (f32[1,2048]{1,0:T(1,128)S(1)}, f32[1,2048]{1,0:T(1,128)S(1)}, u32[]{:S(2)}, u32[]{:S(2)}) collective-permute-start(f32[1,2048]{1,0:T(1,128)S(1)} %add.6), channel_id=1, source_target_pairs={{0,2},{1,3},{2,0},{3,1},{4,6},{5,7},{6,4},{7,5},{8,10},{9,11},{10,... | collective-permute-start | bytes 24584 | tf_op jit(solution)/shard_map/ppermute | solution.py:460
  54.9 6.1 %collective-permute-start.13 = (bf16[256,256]{1,0:T(8,128)(2,1)S(1)}, bf16[256,256]{1,0:T(8,128)(2,1)S(1)}, u32[]{:S(2)}, u32[]{:S(2)}) collective-permute-start(bf16[256,256]{1,0:T(8,128)(2,1)S(1)} %get-tuple-element.53), channel_id=1, source_target_pairs={{28,0},{24,4},{20,8},{16,12},{12,16},{8,20},{4,24},{0,28},{29,1},{... | collective-permute-start | bytes 393224 | tf_op jit(solution)/shard_map/ppermute | solution.py:471
  55.6 7.4 %collective-permute-start.14 = (bf16[256,256]{1,0:T(8,128)(2,1)S(1)}, bf16[256,256]{1,0:T(8,128)(2,1)S(1)}, u32[]{:S(2)}, u32[]{:S(2)}) collective-permute-start(bf16[256,256]{1,0:T(8,128)(2,1)S(1)} %get-tuple-element.54), channel_id=1, source_target_pairs={{24,0},{28,4},{16,8},{20,12},{8,16},{12,20},{0,24},{4,28},{25,1},{... | collective-permute-start | bytes 393224 | tf_op jit(solution)/shard_map/ppermute | solution.py:471
  56.3 7.8 %collective-permute-start.15 = (bf16[256,256]{1,0:T(8,128)(2,1)S(1)}, bf16[256,256]{1,0:T(8,128)(2,1)S(1)}, u32[]{:S(2)}, u32[]{:S(2)}) collective-permute-start(bf16[256,256]{1,0:T(8,128)(2,1)S(1)} %get-tuple-element.55), channel_id=1, source_target_pairs={{4,0},{0,4},{12,8},{8,12},{20,16},{16,20},{28,24},{24,28},{5,1},{1... | collective-permute-start | bytes 393224 | tf_op jit(solution)/shard_map/ppermute | solution.py:471
  57.7 8.4 %collective-permute-start.16 = (bf16[256,256]{1,0:T(8,128)(2,1)S(1)}, bf16[256,256]{1,0:T(8,128)(2,1)S(1)}, u32[]{:S(2)}, u32[]{:S(2)}) collective-permute-start(bf16[256,256]{1,0:T(8,128)(2,1)S(1)} %get-tuple-element.57), channel_id=1, source_target_pairs={{20,0},{8,4},{28,8},{0,12},{4,16},{24,20},{12,24},{16,28},{21,1},{... | collective-permute-start | bytes 393224 | tf_op jit(solution)/shard_map/ppermute | solution.py:471
  57.9 8.3 %collective-permute-start.17 = (bf16[256,256]{1,0:T(8,128)(2,1)S(1)}, bf16[256,256]{1,0:T(8,128)(2,1)S(1)}, u32[]{:S(2)}, u32[]{:S(2)}) collective-permute-start(bf16[256,256]{1,0:T(8,128)(2,1)S(1)} %get-tuple-element.58), channel_id=1, source_target_pairs={{16,0},{12,4},{24,8},{4,12},{0,16},{28,20},{8,24},{20,28},{17,1},{... | collective-permute-start | bytes 393224 | tf_op jit(solution)/shard_map/ppermute | solution.py:471
  61.0 6.9 %collective-permute-start.18 = (bf16[256,256]{1,0:T(8,128)(2,1)S(1)}, bf16[256,256]{1,0:T(8,128)(2,1)S(1)}, u32[]{:S(2)}, u32[]{:S(2)}) collective-permute-start(bf16[256,256]{1,0:T(8,128)(2,1)S(1)} %get-tuple-element.59), channel_id=1, source_target_pairs={{12,0},{16,4},{4,8},{24,12},{28,16},{0,20},{20,24},{8,28},{13,1},{... | collective-permute-start | bytes 393224 | tf_op jit(solution)/shard_map/ppermute | solution.py:471
  63.0 5.7 %collective-permute-start.19 = (bf16[256,256]{1,0:T(8,128)(2,1)S(1)}, bf16[256,256]{1,0:T(8,128)(2,1)S(1)}, u32[]{:S(2)}, u32[]{:S(2)}) collective-permute-start(bf16[256,256]{1,0:T(8,128)(2,1)S(1)} %get-tuple-element.60), channel_id=1, source_target_pairs={{8,0},{20,4},{0,8},{28,12},{24,16},{4,20},{16,24},{12,28},{9,1},{2... | collective-permute-start | bytes 393224 | tf_op jit(solution)/shard_map/ppermute | solution.py:471

commit v11 on v10

--- a/solution.py
+++ b/solution.py
@@ -116,40 +116,44 @@
     )(order)
 
 
-def sort_kernel(size, onehot, q_ref, k_ref, v_ref, *rest):
-    outs, token = rest[-1 - size : -1], rest[-1]
+def sort_kernel(size, cut, onehot, q_ref, k_ref, v_ref, *rest):
+    width = q_ref.shape[1]
+    outs, token = rest[-1 - size - cut : -1], rest[-1]
+    places = [[(out, at * width) for at in range(3)] for out in outs[cut:]]
+    if cut:
+        places[0] = [(outs[0], 0), (outs[0], width), (outs[1], 0)]
     token[...] = jnp.zeros_like(token)
-    rows, width = outs[0].shape[0], q_ref.shape[1]
-    group = max(1, min(len(outs), TILE // rows))
-    while len(outs) % group:
+    rows = outs[0].shape[0]
+    group = max(1, min(size, TILE // rows))
+    while size % group:
         group -= 1
-    for first in range(0, len(outs), group):
+    for first in range(0, size, group):
         marks = onehot[first * rows : (first + group) * rows, :]
         for which, ref in enumerate((q_ref, k_ref, v_ref)):
             picked = dot(marks, ref[...]).astype(BF16)
             for at in range(group):
-                outs[first + at][:, which * width : (which + 1) * width] = picked[
-                    at * rows : (at + 1) * rows
-                ]
-
-
-def sort_tokens(onehot, q, k, v, after, n):
+                out, low = places[first + at][which]
+                out[:, low : low + width] = picked[at * rows : (at + 1) * rows]
+
+
+def sort_tokens(onehot, q, k, v, cut, n):
     count, width = q.shape
     rows = count // n
     size = onehot.shape[0] // rows
-    return pl.pallas_call(
-        functools.partial(sort_kernel, size),
-        out_shape=[jax.ShapeDtypeStruct((rows, 3 * width), BF16)] * size + [TOKEN],
-        in_specs=full(4) + [pl.BlockSpec(memory_space=pl.ANY)] * len(after),
-        out_specs=full(size + 1),
+    widths = [2 * width, width] * cut + [3 * width] * (size - cut)
+    return pl.pallas_call(
+        functools.partial(sort_kernel, size, cut),
+        out_shape=[jax.ShapeDtypeStruct((rows, each), BF16) for each in widths] + [TOKEN],
+        in_specs=full(4),
+        out_specs=full(len(widths) + 1),
         compiler_params=params(),
         cost_estimate=cost(6 * size * rows * count * width, 6 * count * width),
         name="sort_tokens",
-    )(onehot, q, k, v, *after)
-
-
-def attend_kernel(n, scale, *refs):
-    ins, outs = refs[:n], refs[-3 - n : -3]
+    )(onehot, q, k, v)
+
+
+def attend_kernel(n, scale, cut, *refs):
+    ins, outs = list(refs[:n]), refs[-3 - n : -3]
     q_all, k_all, v_all = refs[-3:]
     rows = ins[0].shape[0]
     width = outs[0].shape[1]
@@ -161,7 +165,10 @@
             there = slice(cam * PATCHES, (cam + 1) * PATCHES)
             q_all[there, :] = ins[cam][here, 0:width]
             k_all[there, :] = ins[cam][here, width : 2 * width]
-            v_all[there, :] = ins[cam][here, 2 * width : 3 * width]
+            if cam == cut:
+                v_all[there, :] = refs[n][here, :]
+            else:
+                v_all[there, :] = ins[cam][here, 2 * width : 3 * width]
         for low in range(0, group, block):
             scores = dot_bt(q_all[low : low + block, :], k_all[...]) * scale
             scores = scores - jnp.max(scores, axis=-1, keepdims=True)
@@ -173,13 +180,13 @@
                 outs[cam][here, :] = result[at : at + PATCHES]
 
 
-def attend(blocks, after, n, width):
+def attend(blocks, cut, rest, after, n, width):
     rows = blocks[0].shape[0]
     group = n * PATCHES
     return pl.pallas_call(
-        functools.partial(attend_kernel, n, width**-0.5),
+        functools.partial(attend_kernel, n, width**-0.5, cut),
         out_shape=[jax.ShapeDtypeStruct((rows, width), BF16)] * n,
-        in_specs=full(n) + [pl.BlockSpec(memory_space=pl.ANY)] * len(after),
+        in_specs=full(n + 1) + [pl.BlockSpec(memory_space=pl.ANY)] * len(after),
         out_specs=full(n),
         scratch_shapes=[pltpu.VMEM((group, width), BF16)] * 3,
         compiler_params=params(),
@@ -187,7 +194,7 @@
             4 * n * rows * group * width, 8 * n * rows * width, n * rows * group
         ),
         name="attend",
-    )(*blocks, *after)
+    )(*blocks, rest, *after)
 
 
 def grads_kernel(n, split, k_ref, v_ref, rate_ref, one_ref, three_ref, two_ref, *rest):
@@ -284,7 +291,7 @@
             mine = merge(mine, got, after[step])
         else:
             mine = mine + got.astype(F32)
-    return [mine, lax.ppermute(mine, "cam", [(at, at ^ 1) for at in range(n)])]
+    return [mine, lax.ppermute(mine.astype(BF16), "cam", [(at, at ^ 1) for at in range(n)])]
 
 
 def readout_kernel(parts, q_ref, one_ref, three_ref, two_ref, *rest):
@@ -294,7 +301,7 @@
         half = total.shape[0] // 2
         core = lax.axis_index("cam") & 1
         total[pl.ds(pl.multiple_of(core * half, half), half), :] = grads[0][...]
-        total[pl.ds(pl.multiple_of((1 - core) * half, half), half), :] = grads[1][...]
+        total[pl.ds(pl.multiple_of((1 - core) * half, half), half), :] = grads[1][...].astype(F32)
     else:
         total[...] = grads[0][...]
     entries = hid * width
@@ -451,9 +458,12 @@
     )(given, onehot, *blocks)
 
 
-def sum_over_heads(square, heads):
-    if not power_of_two(heads):
-        return lax.psum(square, "head")
+def sum_over_heads(square, heads, direct):
+    if not power_of_two(heads) or direct:
+        return square + sum(
+            lax.ppermute(square, "head", [(at, (at + step) % heads) for at in range(heads)])
+            for step in range(1, heads)
+        )
     step = 1
     while step < heads:
         pairs = [(at, at ^ step) for at in range(heads)]
@@ -478,13 +488,16 @@
     steps = far_first(n)
     few = max(1, n // 4)
     weights = (w_one, w_three, w_two)
-    groups = (tuple(steps[:few]), tuple(steps[few : 2 * few]), tuple(steps[2 * few :]))
+    groups = (tuple(steps[:few]), (*steps[few : 2 * few], 1), (*steps[2 * few : -2], 0))
     marks = mark(order, n, groups)
     arrived = {}
     tokens = []
-    for group, onehot in zip(groups, marks):
-        blocks = sort_tokens(onehot, queries, keys, values, [], n)
-        tokens.append(blocks[-1])
+    for which, (group, onehot) in enumerate(zip(groups, marks)):
+        cut = 1 if which == 0 else 0
+        blocks = list(sort_tokens(onehot, queries, keys, values, cut, n))
+        tokens.append(blocks.pop())
+        if cut:
+            rest = exchange(blocks.pop(1), group[0], n)
         for step, block in zip(group, blocks):
             arrived[step] = exchange(block, step, n)
     came = [arrived[step] for step in steps]
@@ -493,10 +506,11 @@
     late = steps[few : n - few]
     early_places, late_places = place(order, n, early + late)
     mine = core_step(parts, [came[0]], n)
-    summed = sum_over_chips(mine, len(parts) == 2, [tokens[1:2], came[1:3] + tokens[2:] + [late_places]], n)
+    summed = sum_over_chips(mine, len(parts) == 2, [tokens[1:2], [rest] + came[1:3] + tokens[2:] + [late_places]], n)
     y, square = read_out(queries, *weights, summed, came[3:4])
-    total = sum_over_heads(square, heads)
-    attended = attend([arrived[step] for step in range(n)], [total], n, width)
+    total = sum_over_heads(square, heads, False)
+    blocks = [arrived[step] for step in range(n)]
+    attended = attend(blocks, steps[0], rest, [total], n, width)
     returned = {step: give_back(attended[step], step, n) for step in early + late}
     given = base(
         gain.reshape(1, width), y, early_places, total, heads, [returned[step] for step in early]

time: 71.2 us -> 73.6 us (1.034)
  starting transfers between devices: 21.8 us -> 23.9 us
    ppermute x7 -> x8, starting transfers between devices: 8.05 us -> 9.88 us  [exchange(): return lax.ppermute(block, 'cam', routes(step, n)) if step else block]
    ppermute x7 -> x8, waiting for transfers between devices: 4.77 us -> 3.67 us  [exchange(): return lax.ppermute(block, 'cam', routes(step, n)) if step else block]
    ppermute x1, waiting for transfers between devices: 0.01 us -> 1.07 us  [sum_over_chips(): lax.ppermute(mine.astype(BF16), 'cam', [(at, at ^ 1) for at in range(n)])]
    ppermute x7, waiting for transfers between devices: 7.08 us -> 7.94 us  [give_back(): return lax.ppermute(block, 'cam', pairs) if step else block]
  transfers between devices with their start and end apart: 20 -> 21, of which waited for: 12 -> 14; matrix products, arithmetic and copies ran while one was open for 0% -> 0% of each run, Pallas kernels for 20% -> 19%
where the time goes in v11:
time: 73.6 us; the launch traced here: 73.4 us
  waiting for transfers between devices  27 us (37%)
  starting transfers between devices  23.9 us (32%)
  Pallas kernels  20.9 us (28%)
  local copies, waits for them, and re-layouts  1.13 us (2%)
    ppermute x8, starting transfers between devices, exchange(): return lax.ppermute(block, 'cam', routes(step, n)) if step else block  9.88 us
    ppermute x2, waiting for transfers between devices, sum_over_chips(): got = lax.ppermute(mine.astype(BF16), 'cam', pairs)  9.24 us
    ppermute x7, waiting for transfers between devices, give_back(): return lax.ppermute(block, 'cam', pairs) if step else block  7.94 us
    pallas_call x3, Pallas kernels, sort_tokens(): pl.pallas_call(functools.partial(sort_kernel, size, cut), out_shape=[jax....  7.22 us
    ppermute x7, starting transfers between devices, give_back(): return lax.ppermute(block, 'cam', pairs) if step else block  5.48 us
    ppermute x2, starting transfers between devices, sum_over_heads(): square = square + lax.ppermute(square, 'head', pairs)  4.35 us
    ppermute x2, waiting for transfers between devices, sum_over_heads(): square = square + lax.ppermute(square, 'head', pairs)  3.97 us
    ppermute x8, waiting for transfers between devices, exchange(): return lax.ppermute(block, 'cam', routes(step, n)) if step else block  3.67 us
  transfers between devices with their start and end apart: 21, of which 14 were waited for; matrix products, arithmetic and copies ran while one was open for 0% of the time, Pallas kernels for 19%

profile of v11, /device:TPU:0, one launch (start us, length us, event | category | flops | bytes accessed | tf_op | source)
XLA Modules:
  0.0 73.4 jit_solution(588969662358762927)
XLA Ops:
  0.7 1.4 %mark.1 = (bf16[512,2048]{1,0:T(8,128)(2,1)S(1)}, bf16[768,2048]{1,0:T(8,128)(2,1)S(1)}, bf16[768,2048]{1,0:T(8,128)(2,1)S(1)}, f32[8,128]{1,0:T(8,128)}) custom-call(s32[1,2048]{1,0:T(1,128)S(1)} %copy-done.8), custom_call_target="tpu_custom_call" | custom-call | flops 999999995904 | bytes 1024 | tf_op jit(solution)/shard_map/mark/pallas_call | solution.py:107
  2.6 1.8 %sort_tokens.3 = (bf16[256,512]{1,0:T(8,128)(2,1)S(1)}, bf16[256,256]{1,0:T(8,128)(2,1)S(1)}, bf16[256,768]{1,0:T(8,128)(2,1)S(1)}, f32[8,128]{1,0:T(8,128)S(1)}) custom-call(bf16[512,2048]{1,0:T(8,128)(2,1)S(1)} %get-tuple-element.34.onehot, bf16[2048,256]{1,0:T(8,128)(2,1)S(1)} %copy-done.3, bf16[2048,256]{1,0:T(8,128)(2,1)S(1)} %copy-done.1, ...), custom_call_target="tpu_custom_call" | custom-call | flops 1610612736 | bytes 3145728 | tf_op jit(solution)/shard_map/sort_tokens/pallas_call | solution.py:144
  4.4 3.4 %collective-permute-start.1 = (bf16[256,512]{1,0:T(8,128)(2,1)S(1)}, bf16[256,512]{1,0:T(8,128)(2,1)S(1)}, u32[]{:S(2)}, u32[]{:S(2)}) collective-permute-start(bf16[256,512]{1,0:T(8,128)(2,1)S(1)} %get-tuple-element.38), channel_id=1, source_target_pairs={{0,28},{4,24},{8,20},{12,16},{16,12},{20,8},{24,4},{28,0},{1,29},{... | collective-permute-start | bytes 786440 | tf_op jit(solution)/shard_map/ppermute | solution.py:476
  7.8 2.9 %gradients.1 = (f32[384,256]{1,0:T(8,128)S(1)}, bf16[384,256]{1,0:T(8,128)(2,1)S(1)}) custom-call(bf16[2048,256]{1,0:T(8,128)(2,1)S(1)} %copy-done.1, bf16[2048,256]{1,0:T(8,128)(2,1)S(1)} %copy-done.2, f32[1,2048]{1,0:T(1,128)S(1)} %bitcast.3, bf16[1,256,256]{2,1,0:T(8,128)(2,1)S(1)} %copy-done.4, bf16[1,256,256]{2,1,0:T(8,128)(2,1)S(1)} %copy-done.5, ...), custom_call_target="tpu_custom_call" | custom-call | flops 1610612736 | bytes 4194304 | tf_op jit(solution)/shard_map/gradients/pallas_call | solution.py:243
  11.4 1.1 %collective-permute-done.got_ref = bf16[384,256]{1,0:T(8,128)(2,1)S(1)} collective-permute-done((bf16[384,256]{1,0:T(8,128)(2,1)S(1)}, bf16[384,256]{1,0:T(8,128)(2,1)S(1)}, u32[]{:S(2)}, u32[]{:S(2)}) %collective-permute-start) | collective-permute-done | bytes 196640 | tf_op jit(solution)/shard_map/ppermute | solution.py:277
  12.5 2.0 %collective-permute-done.1.rest_0_.refs_7_ = bf16[256,512]{1,0:T(8,128)(2,1)S(1)} collective-permute-done((bf16[256,512]{1,0:T(8,128)(2,1)S(1)}, bf16[256,512]{1,0:T(8,128)(2,1)S(1)}, u32[]{:S(2)}, u32[]{:S(2)}) %collective-permute-start.1) | collective-permute-done | bytes 262176 | tf_op jit(solution)/shard_map/ppermute | solution.py:476
  14.5 2.5 %collective-permute-start.2 = (bf16[384,256]{1,0:T(8,128)(2,1)S(1)}, bf16[384,256]{1,0:T(8,128)(2,1)S(1)}, u32[]{:S(2)}, u32[]{:S(2)}) collective-permute-start(bf16[384,256]{1,0:T(8,128)(2,1)S(1)} %convert_element_type.9), channel_id=1, source_target_pairs={{0,8},{4,20},{8,0},{12,28},{16,24},{20,4},{24,16},{28,12},{1,9},{5... | collective-permute-start | bytes 589832 | tf_op jit(solution)/shard_map/ppermute | solution.py:289
  17.0 2.7 %sort_tokens.4 = (bf16[256,768]{1,0:T(8,128)(2,1)S(1)}, bf16[256,768]{1,0:T(8,128)(2,1)S(1)}, bf16[256,768]{1,0:T(8,128)(2,1)S(1)}, f32[8,128]{1,0:T(8,128)S(1)}) custom-call(bf16[768,2048]{1,0:T(8,128)(2,1)S(1)} %get-tuple-element.39.onehot, bf16[2048,256]{1,0:T(8,128)(2,1)S(1)} %copy-done.3, bf16[2048,256]{1,0:T(8,128)(2,1)S(1)} %copy-done.1, ...), custom_call_target="tpu_custom_call" | custom-call | flops 2415919104 | bytes 3145728 | tf_op jit(solution)/shard_map/sort_tokens/pallas_call | solution.py:144
  19.8 2.7 %collective-permute-start.4 = (bf16[256,256]{1,0:T(8,128)(2,1)S(1)}, bf16[256,256]{1,0:T(8,128)(2,1)S(1)}, u32[]{:S(2)}, u32[]{:S(2)}) collective-permute-start(bf16[256,256]{1,0:T(8,128)(2,1)S(1)} %get-tuple-element.41), channel_id=1, source_target_pairs={{0,28},{4,24},{8,20},{12,16},{16,12},{20,8},{24,4},{28,0},{1,29},{... | collective-permute-start | bytes 393224 | tf_op jit(solution)/shard_map/ppermute | solution.py:476
  23.0 5.2 %collective-permute-done.2.got_ref = bf16[384,256]{1,0:T(8,128)(2,1)S(1)} collective-permute-done((bf16[384,256]{1,0:T(8,128)(2,1)S(1)}, bf16[384,256]{1,0:T(8,128)(2,1)S(1)}, u32[]{:S(2)}, u32[]{:S(2)}) %collective-permute-start.2) | collective-permute-done | bytes 196640 | tf_op jit(solution)/shard_map/ppermute | solution.py:289
  28.3 2.7 %sort_tokens.5 = (bf16[256,768]{1,0:T(8,128)(2,1)S(1)}, bf16[256,768]{1,0:T(8,128)(2,1)S(1)}, bf16[256,768]{1,0:T(8,128)(2,1)S(1)}, f32[8,128]{1,0:T(8,128)S(1)}) custom-call(bf16[768,2048]{1,0:T(8,128)(2,1)S(1)} %get-tuple-element.44.onehot, bf16[2048,256]{1,0:T(8,128)(2,1)S(1)} %copy-done.3, bf16[2048,256]{1,0:T(8,128)(2,1)S(1)} %copy-done.1, ...), custom_call_target="tpu_custom_call" | custom-call | flops 2415919104 | bytes 3145728 | tf_op jit(solution)/shard_map/sort_tokens/pallas_call | solution.py:144
  31.0 1.7 %collective-permute-done.4.rest_0_.refs_8_ = bf16[256,256]{1,0:T(8,128)(2,1)S(1)} collective-permute-done((bf16[256,256]{1,0:T(8,128)(2,1)S(1)}, bf16[256,256]{1,0:T(8,128)(2,1)S(1)}, u32[]{:S(2)}, u32[]{:S(2)}) %collective-permute-start.4) | collective-permute-done | bytes 131104 | tf_op jit(solution)/shard_map/ppermute | solution.py:476
  32.7 1.9 %collective-permute-start.12 = (bf16[256,768]{1,0:T(8,128)(2,1)S(1)}, bf16[256,768]{1,0:T(8,128)(2,1)S(1)}, u32[]{:S(2)}, u32[]{:S(2)}) collective-permute-start(bf16[256,768]{1,0:T(8,128)(2,1)S(1)} %get-tuple-element.53), channel_id=1, source_target_pairs={{0,8},{4,20},{8,0},{12,28},{16,24},{20,4},{24,16},{28,12},{1,9},{5... | collective-permute-start | bytes 1179656 | tf_op jit(solution)/shard_map/ppermute | solution.py:476
  34.6 1.4 %collective-permute-start.13 = (bf16[256,768]{1,0:T(8,128)(2,1)S(1)}, bf16[256,768]{1,0:T(8,128)(2,1)S(1)}, u32[]{:S(2)}, u32[]{:S(2)}) collective-permute-start(bf16[256,768]{1,0:T(8,128)(2,1)S(1)} %get-tuple-element.54), channel_id=1, source_target_pairs={{0,12},{4,16},{8,4},{12,24},{16,28},{20,0},{24,20},{28,8},{1,13},{... | collective-permute-start | bytes 1179656 | tf_op jit(solution)/shard_map/ppermute | solution.py:476
  36.0 1.7 %place.1 = (bf16[2048,1024]{1,0:T(8,128)(2,1)S(1)}, bf16[2048,1024]{1,0:T(8,128)(2,1)S(1)}) custom-call(s32[1,2048]{1,0:T(1,128)S(1)} %copy-done.9), custom_call_target="tpu_custom_call" | custom-call | flops 4194304 | bytes 8388608 | tf_op jit(solution)/shard_map/place/pallas_call | solution.py:380
  37.6 4.1 %collective-permute-done.3.got_ref = bf16[384,256]{1,0:T(8,128)(2,1)S(1)} collective-permute-done((bf16[384,256]{1,0:T(8,128)(2,1)S(1)}, bf16[384,256]{1,0:T(8,128)(2,1)S(1)}, u32[]{:S(2)}, u32[]{:S(2)}) %collective-permute-start.3) | collective-permute-done | bytes 196640 | tf_op jit(solution)/shard_map/ppermute | solution.py:289
  42.7 1.1 %collective-permute-done.7.rest_1_ = bf16[384,256]{1,0:T(8,128)(2,1)S(1)} collective-permute-done((bf16[384,256]{1,0:T(8,128)(2,1)S(1)}, bf16[384,256]{1,0:T(8,128)(2,1)S(1)}, u32[]{:S(2)}, u32[]{:S(2)}) %collective-permute-start.7) | collective-permute-done | bytes 196640 | tf_op jit(solution)/shard_map/ppermute | solution.py:294
  43.8 2.7 %read_out.1 = (f32[2048,256]{1,0:T(8,128)S(1)}, f32[1,2048]{1,0:T(1,128)S(1)}) custom-call(bf16[2048,256]{1,0:T(8,128)(2,1)S(1)} %copy-done.3, bf16[1,256,256]{2,1,0:T(8,128)(2,1)S(1)} %copy-done.4, bf16[1,256,256]{2,1,0:T(8,128)(2,1)S(1)} %copy-done.5, bf16[1,256,256]{2,1,0:T(8,128)(2,1)S(1)} %copy-done.6, f32[384,256]{1,0:T(8,128)S(1)} %merge.5.rest_0_, ...), custom_call_target="tpu_custom_call" | custom-call | flops 805306368 | bytes 4194304 | tf_op jit(solution)/shard_map/read_out/pallas_call | solution.py:341
  46.5 1.7 %collective-permute-start.9 = (f32[1,2048]{1,0:T(1,128)S(1)}, f32[1,2048]{1,0:T(1,128)S(1)}, u32[]{:S(2)}, u32[]{:S(2)}) collective-permute-start(f32[1,2048]{1,0:T(1,128)S(1)} %get-tuple-element.50), channel_id=1, source_target_pairs={{0,1},{1,0},{2,3},{3,2},{4,5},{5,4},{6,7},{7,6},{8,9},{9,8},{10,11... | collective-permute-start | bytes 24584 | tf_op jit(solution)/shard_map/ppermute | solution.py:470
  48.1 2.0 %collective-permute-done.9 = f32[1,2048]{1,0:T(1,128)S(1)} collective-permute-done((f32[1,2048]{1,0:T(1,128)S(1)}, f32[1,2048]{1,0:T(1,128)S(1)}, u32[]{:S(2)}, u32[]{:S(2)}) %collective-permute-start.9) | collective-permute-done | bytes 8224 | tf_op jit(solution)/shard_map/ppermute | solution.py:470
  50.2 2.7 %collective-permute-start.10 = (f32[1,2048]{1,0:T(1,128)S(1)}, f32[1,2048]{1,0:T(1,128)S(1)}, u32[]{:S(2)}, u32[]{:S(2)}) collective-permute-start(f32[1,2048]{1,0:T(1,128)S(1)} %add.6), channel_id=1, source_target_pairs={{0,2},{1,3},{2,0},{3,1},{4,6},{5,7},{6,4},{7,5},{8,10},{9,11},{10,... | collective-permute-start | bytes 24584 | tf_op jit(solution)/shard_map/ppermute | solution.py:470
  52.9 1.9 %collective-permute-done.10 = f32[1,2048]{1,0:T(1,128)S(1)} collective-permute-done((f32[1,2048]{1,0:T(1,128)S(1)}, f32[1,2048]{1,0:T(1,128)S(1)}, u32[]{:S(2)}, u32[]{:S(2)}) %collective-permute-start.10) | collective-permute-done | bytes 8224 | tf_op jit(solution)/shard_map/ppermute | solution.py:470
  54.9 1.5 %attend.1 = (bf16[256,256]{1,0:T(8,128)(2,1)S(1)}, bf16[256,256]{1,0:T(8,128)(2,1)S(1)}, bf16[256,256]{1,0:T(8,128)(2,1)S(1)}, bf16[256,256]{1,0:T(8,128)(2,1)S(...) custom-call(bf16[256,768]{1,0:T(8,128)(2,1)S(1)} %get-tuple-element., ...), custom_call_target="tpu_custom_call" | custom-call | flops 536870912 | bytes 4194304 | tf_op jit(solution)/shard_map/attend/pallas_call | solution.py:186
  56.5 2.5 %collective-permute-start.15 = (bf16[256,256]{1,0:T(8,128)(2,1)S(1)}, bf16[256,256]{1,0:T(8,128)(2,1)S(1)}, u32[]{:S(2)}, u32[]{:S(2)}) collective-permute-start(bf16[256,256]{1,0:T(8,128)(2,1)S(1)} %get-tuple-element.56), channel_id=1, source_target_pairs={{24,0},{28,4},{16,8},{20,12},{8,16},{12,20},{0,24},{4,28},{25,1},{... | collective-permute-start | bytes 393224 | tf_op jit(solution)/shard_map/ppermute | solution.py:481
  59.2 1.1 %collective-permute-start.17 = (bf16[256,256]{1,0:T(8,128)(2,1)S(1)}, bf16[256,256]{1,0:T(8,128)(2,1)S(1)}, u32[]{:S(2)}, u32[]{:S(2)}) collective-permute-start(bf16[256,256]{1,0:T(8,128)(2,1)S(1)} %get-tuple-element.59), channel_id=1, source_target_pairs={{20,0},{8,4},{28,8},{0,12},{4,16},{24,20},{12,24},{16,28},{21,1},{... | collective-permute-start | bytes 393224 | tf_op jit(solution)/shard_map/ppermute | solution.py:481
  60.3 1.5 %collective-permute-start.18 = (bf16[256,256]{1,0:T(8,128)(2,1)S(1)}, bf16[256,256]{1,0:T(8,128)(2,1)S(1)}, u32[]{:S(2)}, u32[]{:S(2)}) collective-permute-start(bf16[256,256]{1,0:T(8,128)(2,1)S(1)} %get-tuple-element.60), channel_id=1, source_target_pairs={{16,0},{12,4},{24,8},{4,12},{0,16},{28,20},{8,24},{20,28},{17,1},{... | collective-permute-start | bytes 393224 | tf_op jit(solution)/shard_map/ppermute | solution.py:481
  61.9 1.2 %collective-permute-done.14.rest_0_ = bf16[256,256]{1,0:T(8,128)(2,1)S(1)} collective-permute-done((bf16[256,256]{1,0:T(8,128)(2,1)S(1)}, bf16[256,256]{1,0:T(8,128)(2,1)S(1)}, u32[]{:S(2)}, u32[]{:S(2)}) %collective-permute-start.14) | collective-permute-done | bytes 131104 | tf_op jit(solution)/shard_map/ppermute | solution.py:481
  63.1 3.0 %collective-permute-done.15.rest_1_ = bf16[256,256]{1,0:T(8,128)(2,1)S(1)} collective-permute-done((bf16[256,256]{1,0:T(8,128)(2,1)S(1)}, bf16[256,256]{1,0:T(8,128)(2,1)S(1)}, u32[]{:S(2)}, u32[]{:S(2)}) %collective-permute-start.15) | collective-permute-done | bytes 131104 | tf_op jit(solution)/shard_map/ppermute | solution.py:481
  66.2 1.3 %base.1.base_ref = f32[2048,256]{1,0:T(8,128)S(1)} custom-call(f32[1,256]{1,0:T(1,128)S(1)} %bitcast.2, f32[2048,256]{1,0:T(8,128)S(1)} %get-tuple-element.48.y_ref, bf16[2048,1024]{1,0:T(8,128)(2,1)S(1)} %get-tuple-element.49.onehot, f32[1,2048]{1,0:T(1,128)S(1)} %add.7.refs_9_.total_ref, bf16[256,256]{1,0:T(8,128)(2,1)S(1)} %collective-permute-done.14.rest_0_, ...), custom_call_target="tpu_custom_call" | custom-call | flops 1073741824 | bytes 4194304 | tf_op jit(solution)/shard_map/base/pallas_call | solution.py:418
  67.4 1.2 %collective-permute-done.17.rest_0_ = bf16[256,256]{1,0:T(8,128)(2,1)S(1)} collective-permute-done((bf16[256,256]{1,0:T(8,128)(2,1)S(1)}, bf16[256,256]{1,0:T(8,128)(2,1)S(1)}, u32[]{:S(2)}, u32[]{:S(2)}) %collective-permute-start.17) | collective-permute-done | bytes 131104 | tf_op jit(solution)/shard_map/ppermute | solution.py:481
  69.4 1.7 %collective-permute-done.20.rest_3_ = bf16[256,256]{1,0:T(8,128)(2,1)S(1)} collective-permute-done((bf16[256,256]{1,0:T(8,128)(2,1)S(1)}, bf16[256,256]{1,0:T(8,128)(2,1)S(1)}, u32[]{:S(2)}, u32[]{:S(2)}) %collective-permute-start.20) | collective-permute-done | bytes 131104 | tf_op jit(solution)/shard_map/ppermute | solution.py:481
  71.1 2.1 %mix.1 = bf16[2048,256]{1,0:T(8,128)(2,1)} custom-call(f32[2048,256]{1,0:T(8,128)S(1)} %base.1.base_ref, bf16[2048,1024]{1,0:T(8,128)(2,1)S(1)} %get-tuple-element.46.rest_4_.onehot, bf16[256,256]{1,0:T(8,128)(2,1)S(1)} %collective-permute-done.17.rest_0_, bf16[256,256]{1,0:T(8,128)(2,1)S(1)} %collective-permute-done.18.rest_1_, ...), custom_call_target="tpu_custom_call" | custom-call | flops 1073741824 | bytes 4194304 | tf_op jit(solution)/shard_map/mix/pallas_call | solution.py:446
  (48 shorter events, 4.7 us)
Async XLA Ops:
  0.0 0.7 copy-start.8
  0.7 1.5 %copy-start.1 = (bf16[2048,256]{1,0:T(8,128)(2,1)S(1)}, bf16[2048,256]{1,0:T(8,128)(2,1)}, u32[]{:S(2)}) copy-start(bf16[2048,256]{1,0:T(8,128)(2,1)} %k_ref.7) | copy-start | bytes 3145732
  0.7 1.5 %copy-start.2 = (bf16[2048,256]{1,0:T(8,128)(2,1)S(1)}, bf16[2048,256]{1,0:T(8,128)(2,1)}, u32[]{:S(2)}) copy-start(bf16[2048,256]{1,0:T(8,128)(2,1)} %v_ref.7) | copy-start | bytes 3145732
  0.7 1.9 %copy-start.3 = (bf16[2048,256]{1,0:T(8,128)(2,1)S(1)}, bf16[2048,256]{1,0:T(8,128)(2,1)}, u32[]{:S(2)}) copy-start(bf16[2048,256]{1,0:T(8,128)(2,1)} %q_ref.7) | copy-start | bytes 3145732
  2.1 5.7 %copy-start.4 = (bf16[1,256,256]{2,1,0:T(8,128)(2,1)S(1)}, bf16[1,256,256]{2,1,0:T(8,128)(2,1)}, u32[]{:S(2)}) copy-start(bf16[1,256,256]{2,1,0:T(8,128)(2,1)} %one_ref.3) | copy-start | bytes 393220
  2.1 5.7 %copy-start.5 = (bf16[1,256,256]{2,1,0:T(8,128)(2,1)S(1)}, bf16[1,256,256]{2,1,0:T(8,128)(2,1)}, u32[]{:S(2)}) copy-start(bf16[1,256,256]{2,1,0:T(8,128)(2,1)} %three_ref.3) | copy-start | bytes 393220
  2.1 5.6 %copy-start.6 = (bf16[1,256,256]{2,1,0:T(8,128)(2,1)S(1)}, bf16[1,256,256]{2,1,0:T(8,128)(2,1)}, u32[]{:S(2)}) copy-start(bf16[1,256,256]{2,1,0:T(8,128)(2,1)} %two_ref.3) | copy-start | bytes 393220
  2.1 5.6 %copy-start.7 = (f32[2048,1]{0,1:T(1,128)S(1)}, f32[2048,1]{0,1:T(1,128)}, u32[]{:S(2)}) copy-start(f32[2048,1]{0,1:T(1,128)} %param.12) | copy-start | bytes 24580
  4.4 10.1 %collective-permute-start.1 = (bf16[256,512]{1,0:T(8,128)(2,1)S(1)}, bf16[256,512]{1,0:T(8,128)(2,1)S(1)}, u32[]{:S(2)}, u32[]{:S(2)}) collective-permute-start(bf16[256,512]{1,0:T(8,128)(2,1)S(1)} %get-tuple-element.38), channel_id=1, source_target_pairs={{0,28},{4,24},{8,20},{12,16},{16,12},{20,8},{24,4},{28,0},{1,29},{... | collective-permute-start | bytes 786440 | tf_op jit(solution)/shard_map/ppermute | solution.py:476
  10.7 1.8 %collective-permute-start = (bf16[384,256]{1,0:T(8,128)(2,1)S(1)}, bf16[384,256]{1,0:T(8,128)(2,1)S(1)}, u32[]{:S(2)}, u32[]{:S(2)}) collective-permute-start(bf16[384,256]{1,0:T(8,128)(2,1)S(1)} %get-tuple-element.37), channel_id=1, source_target_pairs={{0,4},{4,0},{8,12},{12,8},{16,20},{20,16},{24,28},{28,24},{1,5},{5... | collective-permute-start | bytes 589832 | tf_op jit(solution)/shard_map/ppermute | solution.py:277
  11.4 21.3 %collective-permute-start.5 = (bf16[256,768]{1,0:T(8,128)(2,1)S(1)}, bf16[256,768]{1,0:T(8,128)(2,1)S(1)}, u32[]{:S(2)}, u32[]{:S(2)}) collective-permute-start(bf16[256,768]{1,0:T(8,128)(2,1)S(1)} %get-tuple-element.42), channel_id=1, source_target_pairs={{0,24},{4,28},{8,16},{12,20},{16,8},{20,12},{24,0},{28,4},{1,25},{... | collective-permute-start | bytes 1179656 | tf_op jit(solution)/shard_map/ppermute | solution.py:476
  14.5 13.6 %collective-permute-start.2 = (bf16[384,256]{1,0:T(8,128)(2,1)S(1)}, bf16[384,256]{1,0:T(8,128)(2,1)S(1)}, u32[]{:S(2)}, u32[]{:S(2)}) collective-permute-start(bf16[384,256]{1,0:T(8,128)(2,1)S(1)} %convert_element_type.9), channel_id=1, source_target_pairs={{0,8},{4,20},{8,0},{12,28},{16,24},{20,4},{24,16},{28,12},{1,9},{5... | collective-permute-start | bytes 589832 | tf_op jit(solution)/shard_map/ppermute | solution.py:289
  19.7 14.9 %collective-permute-start.6 = (bf16[256,768]{1,0:T(8,128)(2,1)S(1)}, bf16[256,768]{1,0:T(8,128)(2,1)S(1)}, u32[]{:S(2)}, u32[]{:S(2)}) collective-permute-start(bf16[256,768]{1,0:T(8,128)(2,1)S(1)} %get-tuple-element.43), channel_id=1, source_target_pairs={{0,20},{4,8},{8,28},{12,0},{16,4},{20,24},{24,12},{28,16},{1,21},{... | collective-permute-start | bytes 1179656 | tf_op jit(solution)/shard_map/ppermute | solution.py:476
  19.8 12.9 %collective-permute-start.4 = (bf16[256,256]{1,0:T(8,128)(2,1)S(1)}, bf16[256,256]{1,0:T(8,128)(2,1)S(1)}, u32[]{:S(2)}, u32[]{:S(2)}) collective-permute-start(bf16[256,256]{1,0:T(8,128)(2,1)S(1)} %get-tuple-element.41), channel_id=1, source_target_pairs={{0,28},{4,24},{8,20},{12,16},{16,12},{20,8},{24,4},{28,0},{1,29},{... | collective-permute-start | bytes 393224 | tf_op jit(solution)/shard_map/ppermute | solution.py:476
  22.5 20.3 %collective-permute-start.8 = (bf16[256,768]{1,0:T(8,128)(2,1)S(1)}, bf16[256,768]{1,0:T(8,128)(2,1)S(1)}, u32[]{:S(2)}, u32[]{:S(2)}) collective-permute-start(bf16[256,768]{1,0:T(8,128)(2,1)S(1)} %get-tuple-element.47), channel_id=1, source_target_pairs={{0,16},{4,12},{8,24},{12,4},{16,0},{20,28},{24,8},{28,20},{1,17},{... | collective-permute-start | bytes 1179656 | tf_op jit(solution)/shard_map/ppermute | solution.py:476
  28.2 13.5 %collective-permute-start.3 = (bf16[384,256]{1,0:T(8,128)(2,1)S(1)}, bf16[384,256]{1,0:T(8,128)(2,1)S(1)}, u32[]{:S(2)}, u32[]{:S(2)}) collective-permute-start(bf16[384,256]{1,0:T(8,128)(2,1)S(1)} %convert_element_type.10), channel_id=1, source_target_pairs={{0,16},{4,12},{8,24},{12,4},{16,0},{20,28},{24,8},{28,20},{1,17},{... | collective-permute-start | bytes 589832 | tf_op jit(solution)/shard_map/ppermute | solution.py:289
  28.3 7.7 %copy-start.9 = (s32[1,2048]{1,0:T(1,128)S(1)}, s32[1,2048]{1,0:T(1,128)}, u32[]{:S(2)}) copy-start(s32[1,2048]{1,0:T(1,128)} %order_ref.3) | copy-start | bytes 24580
  32.7 22.1 %collective-permute-start.11 = (bf16[256,768]{1,0:T(8,128)(2,1)S(1)}, bf16[256,768]{1,0:T(8,128)(2,1)S(1)}, u32[]{:S(2)}, u32[]{:S(2)}) collective-permute-start(bf16[256,768]{1,0:T(8,128)(2,1)S(1)} %get-tuple-element.52), channel_id=1, source_target_pairs={{0,4},{4,0},{8,12},{12,8},{16,20},{20,16},{24,28},{28,24},{1,5},{5... | collective-permute-start | bytes 1179656 | tf_op jit(solution)/shard_map/ppermute | solution.py:476
  32.7 22.1 %collective-permute-start.12 = (bf16[256,768]{1,0:T(8,128)(2,1)S(1)}, bf16[256,768]{1,0:T(8,128)(2,1)S(1)}, u32[]{:S(2)}, u32[]{:S(2)}) collective-permute-start(bf16[256,768]{1,0:T(8,128)(2,1)S(1)} %get-tuple-element.53), channel_id=1, source_target_pairs={{0,8},{4,20},{8,0},{12,28},{16,24},{20,4},{24,16},{28,12},{1,9},{5... | collective-permute-start | bytes 1179656 | tf_op jit(solution)/shard_map/ppermute | solution.py:476
  34.6 20.3 %collective-permute-start.13 = (bf16[256,768]{1,0:T(8,128)(2,1)S(1)}, bf16[256,768]{1,0:T(8,128)(2,1)S(1)}, u32[]{:S(2)}, u32[]{:S(2)}) collective-permute-start(bf16[256,768]{1,0:T(8,128)(2,1)S(1)} %get-tuple-element.54), channel_id=1, source_target_pairs={{0,12},{4,16},{8,4},{12,24},{16,28},{20,0},{24,20},{28,8},{1,13},{... | collective-permute-start | bytes 1179656 | tf_op jit(solution)/shard_map/ppermute | solution.py:476
  41.8 24.3 %copy-start = (f32[256]{0:T(256)S(1)}, f32[256]{0:T(256)}, u32[]{:S(2)}) copy-start(f32[256]{0:T(256)} %param.16) | copy-start | bytes 3076
  41.8 2.0 %collective-permute-start.7 = (bf16[384,256]{1,0:T(8,128)(2,1)S(1)}, bf16[384,256]{1,0:T(8,128)(2,1)S(1)}, u32[]{:S(2)}, u32[]{:S(2)}) collective-permute-start(bf16[384,256]{1,0:T(8,128)(2,1)S(1)} %convert_element_type.11), channel_id=1, source_target_pairs={{0,4},{4,0},{8,12},{12,8},{16,20},{20,16},{24,28},{28,24},{1,5},{5... | collective-permute-start | bytes 589832 | tf_op jit(solution)/shard_map/ppermute | solution.py:294
  46.5 3.7 %collective-permute-start.9 = (f32[1,2048]{1,0:T(1,128)S(1)}, f32[1,2048]{1,0:T(1,128)S(1)}, u32[]{:S(2)}, u32[]{:S(2)}) collective-permute-start(f32[1,2048]{1,0:T(1,128)S(1)} %get-tuple-element.50), channel_id=1, source_target_pairs={{0,1},{1,0},{2,3},{3,2},{4,5},{5,4},{6,7},{7,6},{8,9},{9,8},{10,11... | collective-permute-start | bytes 24584 | tf_op jit(solution)/shard_map/ppermute | solution.py:470
  50.2 4.6 %collective-permute-start.10 = (f32[1,2048]{1,0:T(1,128)S(1)}, f32[1,2048]{1,0:T(1,128)S(1)}, u32[]{:S(2)}, u32[]{:S(2)}) collective-permute-start(f32[1,2048]{1,0:T(1,128)S(1)} %add.6), channel_id=1, source_target_pairs={{0,2},{1,3},{2,0},{3,1},{4,6},{5,7},{6,4},{7,5},{8,10},{9,11},{10,... | collective-permute-start | bytes 24584 | tf_op jit(solution)/shard_map/ppermute | solution.py:470
  56.4 6.7 %collective-permute-start.14 = (bf16[256,256]{1,0:T(8,128)(2,1)S(1)}, bf16[256,256]{1,0:T(8,128)(2,1)S(1)}, u32[]{:S(2)}, u32[]{:S(2)}) collective-permute-start(bf16[256,256]{1,0:T(8,128)(2,1)S(1)} %get-tuple-element.55), channel_id=1, source_target_pairs={{28,0},{24,4},{20,8},{16,12},{12,16},{8,20},{4,24},{0,28},{29,1},{... | collective-permute-start | bytes 393224 | tf_op jit(solution)/shard_map/ppermute | solution.py:481
  56.5 9.7 %collective-permute-start.15 = (bf16[256,256]{1,0:T(8,128)(2,1)S(1)}, bf16[256,256]{1,0:T(8,128)(2,1)S(1)}, u32[]{:S(2)}, u32[]{:S(2)}) collective-permute-start(bf16[256,256]{1,0:T(8,128)(2,1)S(1)} %get-tuple-element.56), channel_id=1, source_target_pairs={{24,0},{28,4},{16,8},{20,12},{8,16},{12,20},{0,24},{4,28},{25,1},{... | collective-permute-start | bytes 393224 | tf_op jit(solution)/shard_map/ppermute | solution.py:481
  59.0 7.1 %collective-permute-start.16 = (bf16[256,256]{1,0:T(8,128)(2,1)S(1)}, bf16[256,256]{1,0:T(8,128)(2,1)S(1)}, u32[]{:S(2)}, u32[]{:S(2)}) collective-permute-start(bf16[256,256]{1,0:T(8,128)(2,1)S(1)} %get-tuple-element.57), channel_id=1, source_target_pairs={{4,0},{0,4},{12,8},{8,12},{20,16},{16,20},{28,24},{24,28},{5,1},{1... | collective-permute-start | bytes 393224 | tf_op jit(solution)/shard_map/ppermute | solution.py:481
  59.2 9.5 %collective-permute-start.17 = (bf16[256,256]{1,0:T(8,128)(2,1)S(1)}, bf16[256,256]{1,0:T(8,128)(2,1)S(1)}, u32[]{:S(2)}, u32[]{:S(2)}) collective-permute-start(bf16[256,256]{1,0:T(8,128)(2,1)S(1)} %get-tuple-element.59), channel_id=1, source_target_pairs={{20,0},{8,4},{28,8},{0,12},{4,16},{24,20},{12,24},{16,28},{21,1},{... | collective-permute-start | bytes 393224 | tf_op jit(solution)/shard_map/ppermute | solution.py:481
  60.3 8.5 %collective-permute-start.18 = (bf16[256,256]{1,0:T(8,128)(2,1)S(1)}, bf16[256,256]{1,0:T(8,128)(2,1)S(1)}, u32[]{:S(2)}, u32[]{:S(2)}) collective-permute-start(bf16[256,256]{1,0:T(8,128)(2,1)S(1)} %get-tuple-element.60), channel_id=1, source_target_pairs={{16,0},{12,4},{24,8},{4,12},{0,16},{28,20},{8,24},{20,28},{17,1},{... | collective-permute-start | bytes 393224 | tf_op jit(solution)/shard_map/ppermute | solution.py:481
  63.1 6.3 %collective-permute-start.19 = (bf16[256,256]{1,0:T(8,128)(2,1)S(1)}, bf16[256,256]{1,0:T(8,128)(2,1)S(1)}, u32[]{:S(2)}, u32[]{:S(2)}) collective-permute-start(bf16[256,256]{1,0:T(8,128)(2,1)S(1)} %get-tuple-element.61), channel_id=1, source_target_pairs={{12,0},{16,4},{4,8},{24,12},{28,16},{0,20},{20,24},{8,28},{13,1},{... | collective-permute-start | bytes 393224 | tf_op jit(solution)/shard_map/ppermute | solution.py:481
  66.1 5.0 %collective-permute-start.20 = (bf16[256,256]{1,0:T(8,128)(2,1)S(1)}, bf16[256,256]{1,0:T(8,128)(2,1)S(1)}, u32[]{:S(2)}, u32[]{:S(2)}) collective-permute-start(bf16[256,256]{1,0:T(8,128)(2,1)S(1)} %get-tuple-element.62), channel_id=1, source_target_pairs={{8,0},{20,4},{0,8},{28,12},{24,16},{4,20},{16,24},{12,28},{9,1},{2... | collective-permute-start | bytes 393224 | tf_op jit(solution)/shard_map/ppermute | solution.py:481

commit v12 on v10

--- a/solution.py
+++ b/solution.py
@@ -270,7 +270,7 @@
     return merge(parts[0], lax.ppermute(parts[1], "cam", pair), after)
 
 
-def sum_over_chips(mine, split, after, n):
+def sum_over_chips(mine, split, before, n):
     if not split:
         return [lax.psum(mine, "cam")]
     span = n.bit_length() - 2
@@ -280,11 +280,8 @@
             bit = 1 + (step + (at & 1)) % span
             pairs.append((at, at ^ (1 << bit)))
         got = lax.ppermute(mine.astype(BF16), "cam", pairs)
-        if step < len(after):
-            mine = merge(mine, got, after[step])
-        else:
-            mine = mine + got.astype(F32)
-    return [mine, lax.ppermute(mine, "cam", [(at, at ^ 1) for at in range(n)])]
+        mine = merge(mine, got, before(step, mine))
+    return [mine, lax.ppermute(mine.astype(BF16), "cam", [(at, at ^ 1) for at in range(n)])]
 
 
 def readout_kernel(parts, q_ref, one_ref, three_ref, two_ref, *rest):
@@ -294,7 +291,7 @@
         half = total.shape[0] // 2
         core = lax.axis_index("cam") & 1
         total[pl.ds(pl.multiple_of(core * half, half), half), :] = grads[0][...]
-        total[pl.ds(pl.multiple_of((1 - core) * half, half), half), :] = grads[1][...]
+        total[pl.ds(pl.multiple_of((1 - core) * half, half), half), :] = grads[1][...].astype(F32)
     else:
         total[...] = grads[0][...]
     entries = hid * width
@@ -451,9 +448,12 @@
     )(given, onehot, *blocks)
 
 
-def sum_over_heads(square, heads):
-    if not power_of_two(heads):
-        return lax.psum(square, "head")
+def sum_over_heads(square, heads, direct):
+    if not power_of_two(heads) or direct:
+        return square + sum(
+            lax.ppermute(square, "head", [(at, (at + step) % heads) for at in range(heads)])
+            for step in range(1, heads)
+        )
     step = 1
     while step < heads:
         pairs = [(at, at ^ step) for at in range(heads)]
@@ -476,26 +476,41 @@
     n = lax.axis_size("cam")
     heads = lax.axis_size("head")
     steps = far_first(n)
-    few = max(1, n // 4)
+    few = max(2, n // 4)
+    half = few // 2
     weights = (w_one, w_three, w_two)
-    groups = (tuple(steps[:few]), tuple(steps[few : 2 * few]), tuple(steps[2 * few :]))
+    groups = ((*steps[:half],), (*steps[half:few],), (*steps[few : 2 * few], 1), (*steps[2 * few : -2], 0))
     marks = mark(order, n, groups)
     arrived = {}
     tokens = []
-    for group, onehot in zip(groups, marks):
-        blocks = sort_tokens(onehot, queries, keys, values, [], n)
+
+    def send(which, after):
+        blocks = sort_tokens(marks[which], queries, keys, values, after, n)
         tokens.append(blocks[-1])
-        for step, block in zip(group, blocks):
+        for step, block in zip(groups[which], blocks):
             arrived[step] = exchange(block, step, n)
-    came = [arrived[step] for step in steps]
+
+    send(0, [])
     parts = gradients(keys, values, rates.reshape(1, count), *weights, tokens[0], n)
     early = steps[:few] + steps[n - few :]
     late = steps[few : n - few]
     early_places, late_places = place(order, n, early + late)
-    mine = core_step(parts, [came[0]], n)
-    summed = sum_over_chips(mine, len(parts) == 2, [tokens[1:2], came[1:3] + tokens[2:] + [late_places]], n)
-    y, square = read_out(queries, *weights, summed, came[3:4])
-    total = sum_over_heads(square, heads)
+    mine = core_step(parts, [arrived[step] for step in steps[:half]], n)
+    send(1, [mine])
+
+    def before(step, mine):
+        if step != 1:
+            return []
+        send(2, [mine])
+        send(3, [])
+        return [arrived[steps[1]], late_places] + tokens[2:3]
+
+    summed = sum_over_chips(mine, len(parts) == 2, before, n)
+    for which in range(len(tokens), len(groups)):
+        send(which, [])
+    came = [arrived[step] for step in steps]
+    y, square = read_out(queries, *weights, summed, came[2:4] + tokens[3:])
+    total = sum_over_heads(square, heads, False)
     attended = attend([arrived[step] for step in range(n)], [total], n, width)
     returned = {step: give_back(attended[step], step, n) for step in early + late}
     given = base(

time: 71.2 us -> 74.4 us (1.045)
  waiting for transfers between devices: 26.9 us -> 28.6 us
  starting transfers between devices: 21.8 us -> 22.6 us
    ppermute x7, waiting for transfers between devices: 4.77 us -> 10.5 us  [exchange(): return lax.ppermute(block, 'cam', routes(step, n)) if step else block]
    ppermute x2, waiting for transfers between devices: 9.93 us -> 5.96 us  [sum_over_chips(): got = lax.ppermute(mine.astype(BF16), 'cam', pairs)]
    ppermute x2, starting transfers between devices: 2.53 us -> 3.97 us  [sum_over_chips(): got = lax.ppermute(mine.astype(BF16), 'cam', pairs)]
    pallas_call x3 -> x4, Pallas kernels: 7.03 us -> 7.67 us  [sort_tokens(): pl.pallas_call(functools.partial(sort_kernel, size), out_shape=[jax.Shape...]
  transfers between devices with their start and end apart: 20 -> 20, of which waited for: 12 -> 12; matrix products, arithmetic and copies ran while one was open for 0% -> 0% of each run, Pallas kernels for 20% -> 21%
where the time goes in v12:
time: 74.4 us; the launch traced here: 74.2 us
  waiting for transfers between devices  28.6 us (38%)
  starting transfers between devices  22.6 us (30%)
  Pallas kernels  21.4 us (29%)
  local copies, waits for them, and re-layouts  1.13 us (2%)
    ppermute x7, waiting for transfers between devices, exchange(): return lax.ppermute(block, 'cam', routes(step, n)) if step else block  10.5 us
    ppermute x7, starting transfers between devices, exchange(): return lax.ppermute(block, 'cam', routes(step, n)) if step else block  8.05 us
    pallas_call x4, Pallas kernels, sort_tokens(): pl.pallas_call(functools.partial(sort_kernel, size), out_shape=[jax.Shape...  7.67 us
    ppermute x7, waiting for transfers between devices, give_back(): return lax.ppermute(block, 'cam', pairs) if step else block  7.02 us
    ppermute x2, waiting for transfers between devices, sum_over_chips(): got = lax.ppermute(mine.astype(BF16), 'cam', pairs)  5.96 us
    ppermute x7, starting transfers between devices, give_back(): return lax.ppermute(block, 'cam', pairs) if step else block  5.52 us
    ppermute x2, starting transfers between devices, sum_over_heads(): square = square + lax.ppermute(square, 'head', pairs)  4.25 us
    ppermute x2, waiting for transfers between devices, sum_over_heads(): square = square + lax.ppermute(square, 'head', pairs)  4.05 us
  transfers between devices with their start and end apart: 20, of which 12 were waited for; matrix products, arithmetic and copies ran while one was open for 0% of the time, Pallas kernels for 21%

profile of v12, /device:TPU:0, one launch (start us, length us, event | category | flops | bytes accessed | tf_op | source)
XLA Modules:
  0.0 74.2 jit_solution(11825664905940038824)
XLA Ops:
  0.7 1.4 %mark.1 = (bf16[256,2048]{1,0:T(8,128)(2,1)S(1)}, bf16[256,2048]{1,0:T(8,128)(2,1)S(1)}, bf16[768,2048]{1,0:T(8,128)(2,1)S(1)}, bf16[768,2048]{1,0:T(8,128)(2,1)S(1)}, f32[8,128]{1,0:T(8,128)}) custom-call(s32[1,2048]{1,0:T(1,128)S(1)} %copy-done.8), custom_call_target="tpu_custom_call" | custom-call | flops 999999995904 | bytes 1024 | tf_op jit(solution)/shard_map/mark/pallas_call | solution.py:107
  2.6 1.0 %sort_tokens.4 = (bf16[256,768]{1,0:T(8,128)(2,1)S(1)}, f32[8,128]{1,0:T(8,128)S(1)}) custom-call(bf16[256,2048]{1,0:T(8,128)(2,1)S(1)} %get-tuple-element.34.onehot, bf16[2048,256]{1,0:T(8,128)(2,1)S(1)} %copy-done.2, bf16[2048,256]{1,0:T(8,128)(2,1)S(1)} %copy-done, bf16[2048,256]{1,0:T(8,128)(2,1)S(1)} %copy-done.1), custom_call_target="tpu_custom_call" | custom-call | flops 805306368 | bytes 3145728 | tf_op jit(solution)/shard_map/sort_tokens/pallas_call | solution.py:140
  3.6 3.4 %collective-permute-start.1 = (bf16[256,768]{1,0:T(8,128)(2,1)S(1)}, bf16[256,768]{1,0:T(8,128)(2,1)S(1)}, u32[]{:S(2)}, u32[]{:S(2)}) collective-permute-start(bf16[256,768]{1,0:T(8,128)(2,1)S(1)} %get-tuple-element.38), channel_id=1, source_target_pairs={{0,28},{4,24},{8,20},{12,16},{16,12},{20,8},{24,4},{28,0},{1,29},{... | collective-permute-start | bytes 1179656 | tf_op jit(solution)/shard_map/ppermute | solution.py:466
  7.0 2.9 %gradients.1 = (f32[384,256]{1,0:T(8,128)S(1)}, bf16[384,256]{1,0:T(8,128)(2,1)S(1)}) custom-call(bf16[2048,256]{1,0:T(8,128)(2,1)S(1)} %copy-done, bf16[2048,256]{1,0:T(8,128)(2,1)S(1)} %copy-done.1, f32[1,2048]{1,0:T(1,128)S(1)} %bitcast.3, bf16[1,256,256]{2,1,0:T(8,128)(2,1)S(1)} %copy-done.4, bf16[1,256,256]{2,1,0:T(8,128)(2,1)S(1)} %copy-done.5, ...), custom_call_target="tpu_custom_call" | custom-call | flops 1610612736 | bytes 4194304 | tf_op jit(solution)/shard_map/gradients/pallas_call | solution.py:236
  10.7 1.1 %collective-permute-done.got_ref = bf16[384,256]{1,0:T(8,128)(2,1)S(1)} collective-permute-done((bf16[384,256]{1,0:T(8,128)(2,1)S(1)}, bf16[384,256]{1,0:T(8,128)(2,1)S(1)}, u32[]{:S(2)}, u32[]{:S(2)}) %collective-permute-start) | collective-permute-done | bytes 196640 | tf_op jit(solution)/shard_map/ppermute | solution.py:270
  11.7 4.7 %collective-permute-done.1.rest_0_.refs_7_ = bf16[256,768]{1,0:T(8,128)(2,1)S(1)} collective-permute-done((bf16[256,768]{1,0:T(8,128)(2,1)S(1)}, bf16[256,768]{1,0:T(8,128)(2,1)S(1)}, u32[]{:S(2)}, u32[]{:S(2)}) %collective-permute-start.1) | collective-permute-done | bytes 393248 | tf_op jit(solution)/shard_map/ppermute | solution.py:466
  16.5 2.5 %collective-permute-start.2 = (bf16[384,256]{1,0:T(8,128)(2,1)S(1)}, bf16[384,256]{1,0:T(8,128)(2,1)S(1)}, u32[]{:S(2)}, u32[]{:S(2)}) collective-permute-start(bf16[384,256]{1,0:T(8,128)(2,1)S(1)} %convert_element_type.9), channel_id=1, source_target_pairs={{0,8},{4,20},{8,0},{12,28},{16,24},{20,4},{24,16},{28,12},{1,9},{5... | collective-permute-start | bytes 589832 | tf_op jit(solution)/shard_map/ppermute | solution.py:282
  19.0 1.4 %sort_tokens.5 = (bf16[256,768]{1,0:T(8,128)(2,1)S(1)}, f32[8,128]{1,0:T(8,128)}) custom-call(bf16[256,2048]{1,0:T(8,128)(2,1)S(1)} %get-tuple-element.39.onehot, bf16[2048,256]{1,0:T(8,128)(2,1)S(1)} %copy-done.2, bf16[2048,256]{1,0:T(8,128)(2,1)S(1)} %copy-done, bf16[2048,256]{1,0:T(8,128)(2,1)S(1)} %copy-done.1, f32[384,256]{1,0:T(8,128)S(1)} %merge.3.keep_ref.rest_0_), custom_call_target="tpu_custom_call" | custom-call | flops 805306368 | bytes 3145728 | tf_op jit(solution)/shard_map/sort_tokens/pallas_call | solution.py:140
  20.4 1.5 %collective-permute-start.4 = (bf16[256,768]{1,0:T(8,128)(2,1)S(1)}, bf16[256,768]{1,0:T(8,128)(2,1)S(1)}, u32[]{:S(2)}, u32[]{:S(2)}) collective-permute-start(bf16[256,768]{1,0:T(8,128)(2,1)S(1)} %get-tuple-element.40), channel_id=1, source_target_pairs={{0,24},{4,28},{8,16},{12,20},{16,8},{20,12},{24,0},{28,4},{1,25},{... | collective-permute-start | bytes 1179656 | tf_op jit(solution)/shard_map/ppermute | solution.py:466
  21.9 1.7 %place.1 = (bf16[2048,1024]{1,0:T(8,128)(2,1)S(1)}, bf16[2048,1024]{1,0:T(8,128)(2,1)S(1)}) custom-call(s32[1,2048]{1,0:T(1,128)S(1)} %copy-done.9), custom_call_target="tpu_custom_call" | custom-call | flops 4194304 | bytes 8388608 | tf_op jit(solution)/shard_map/place/pallas_call | solution.py:370
  23.7 1.5 %collective-permute-start.3 = (bf16[384,256]{1,0:T(8,128)(2,1)S(1)}, bf16[384,256]{1,0:T(8,128)(2,1)S(1)}, u32[]{:S(2)}, u32[]{:S(2)}) collective-permute-start(bf16[384,256]{1,0:T(8,128)(2,1)S(1)} %convert_element_type.10), channel_id=1, source_target_pairs={{0,16},{4,12},{8,24},{12,4},{16,0},{20,28},{24,8},{28,20},{1,17},{... | collective-permute-start | bytes 589832 | tf_op jit(solution)/shard_map/ppermute | solution.py:282
  25.2 2.6 %sort_tokens.6 = (bf16[256,768]{1,0:T(8,128)(2,1)S(1)}, bf16[256,768]{1,0:T(8,128)(2,1)S(1)}, bf16[256,768]{1,0:T(8,128)(2,1)S(1)}, f32[8,128]{1,0:T(8,128)S(1)}) custom-call(bf16[768,2048]{1,0:T(8,128)(2,1)S(1)} %get-tuple-element.42.onehot, bf16[2048,256]{1,0:T(8,128)(2,1)S(1)} %copy-done.2, bf16[2048,256]{1,0:T(8,128)(2,1)S(1)} %copy-done, ...), custom_call_target="tpu_custom_call" | custom-call | flops 2415919104 | bytes 3145728 | tf_op jit(solution)/shard_map/sort_tokens/pallas_call | solution.py:140
  28.7 6.0 %collective-permute-done.3.got_ref = bf16[384,256]{1,0:T(8,128)(2,1)S(1)} collective-permute-done((bf16[384,256]{1,0:T(8,128)(2,1)S(1)}, bf16[384,256]{1,0:T(8,128)(2,1)S(1)}, u32[]{:S(2)}, u32[]{:S(2)}) %collective-permute-start.3) | collective-permute-done | bytes 196640 | tf_op jit(solution)/shard_map/ppermute | solution.py:282
  34.8 2.6 %sort_tokens.7 = (bf16[256,768]{1,0:T(8,128)(2,1)S(1)}, bf16[256,768]{1,0:T(8,128)(2,1)S(1)}, bf16[256,768]{1,0:T(8,128)(2,1)S(1)}, f32[8,128]{1,0:T(8,128)S(1)}) custom-call(bf16[768,2048]{1,0:T(8,128)(2,1)S(1)} %get-tuple-element.46.onehot, bf16[2048,256]{1,0:T(8,128)(2,1)S(1)} %copy-done.2, bf16[2048,256]{1,0:T(8,128)(2,1)S(1)} %copy-done, ...), custom_call_target="tpu_custom_call" | custom-call | flops 2415919104 | bytes 3145728 | tf_op jit(solution)/shard_map/sort_tokens/pallas_call | solution.py:140
  37.5 1.6 %collective-permute-start.11 = (bf16[256,768]{1,0:T(8,128)(2,1)S(1)}, bf16[256,768]{1,0:T(8,128)(2,1)S(1)}, u32[]{:S(2)}, u32[]{:S(2)}) collective-permute-start(bf16[256,768]{1,0:T(8,128)(2,1)S(1)} %get-tuple-element.53), channel_id=1, source_target_pairs={{0,8},{4,20},{8,0},{12,28},{16,24},{20,4},{24,16},{28,12},{1,9},{5... | collective-permute-start | bytes 1179656 | tf_op jit(solution)/shard_map/ppermute | solution.py:466
  39.8 5.7 %collective-permute-done.7.rest_3_.refs_4_ = bf16[256,768]{1,0:T(8,128)(2,1)S(1)} collective-permute-done((bf16[256,768]{1,0:T(8,128)(2,1)S(1)}, bf16[256,768]{1,0:T(8,128)(2,1)S(1)}, u32[]{:S(2)}, u32[]{:S(2)}) %collective-permute-start.7) | collective-permute-done | bytes 393248 | tf_op jit(solution)/shard_map/ppermute | solution.py:466
  45.5 2.7 %read_out.1 = (f32[2048,256]{1,0:T(8,128)S(1)}, f32[1,2048]{1,0:T(1,128)S(1)}) custom-call(bf16[2048,256]{1,0:T(8,128)(2,1)S(1)} %copy-done.2, bf16[1,256,256]{2,1,0:T(8,128)(2,1)S(1)} %copy-done.4, bf16[1,256,256]{2,1,0:T(8,128)(2,1)S(1)} %copy-done.5, bf16[1,256,256]{2,1,0:T(8,128)(2,1)S(1)} %copy-done.6, f32[384,256]{1,0:T(8,128)S(1)} %merge.5.rest_0_, ...), custom_call_target="tpu_custom_call" | custom-call | flops 805306368 | bytes 4194304 | tf_op jit(solution)/shard_map/read_out/pallas_call | solution.py:331
  48.2 1.6 %collective-permute-start.8 = (f32[1,2048]{1,0:T(1,128)S(1)}, f32[1,2048]{1,0:T(1,128)S(1)}, u32[]{:S(2)}, u32[]{:S(2)}) collective-permute-start(f32[1,2048]{1,0:T(1,128)S(1)} %get-tuple-element.50), channel_id=1, source_target_pairs={{0,1},{1,0},{2,3},{3,2},{4,5},{5,4},{6,7},{7,6},{8,9},{9,8},{10,11... | collective-permute-start | bytes 24584 | tf_op jit(solution)/shard_map/ppermute | solution.py:460
  49.8 2.1 %collective-permute-done.8 = f32[1,2048]{1,0:T(1,128)S(1)} collective-permute-done((f32[1,2048]{1,0:T(1,128)S(1)}, f32[1,2048]{1,0:T(1,128)S(1)}, u32[]{:S(2)}, u32[]{:S(2)}) %collective-permute-start.8) | collective-permute-done | bytes 8224 | tf_op jit(solution)/shard_map/ppermute | solution.py:460
  51.9 2.6 %collective-permute-start.9 = (f32[1,2048]{1,0:T(1,128)S(1)}, f32[1,2048]{1,0:T(1,128)S(1)}, u32[]{:S(2)}, u32[]{:S(2)}) collective-permute-start(f32[1,2048]{1,0:T(1,128)S(1)} %add.6), channel_id=1, source_target_pairs={{0,2},{1,3},{2,0},{3,1},{4,6},{5,7},{6,4},{7,5},{8,10},{9,11},{10,... | collective-permute-start | bytes 24584 | tf_op jit(solution)/shard_map/ppermute | solution.py:460
  54.5 2.0 %collective-permute-done.9 = f32[1,2048]{1,0:T(1,128)S(1)} collective-permute-done((f32[1,2048]{1,0:T(1,128)S(1)}, f32[1,2048]{1,0:T(1,128)S(1)}, u32[]{:S(2)}, u32[]{:S(2)}) %collective-permute-start.9) | collective-permute-done | bytes 8224 | tf_op jit(solution)/shard_map/ppermute | solution.py:460
  56.5 1.5 %attend.1 = (bf16[256,256]{1,0:T(8,128)(2,1)S(1)}, bf16[256,256]{1,0:T(8,128)(2,1)S(1)}, bf16[256,256]{1,0:T(8,128)(2,1)S(1)}, bf16[256,256]{1,0:T(8,128)(2,1)S(...) custom-call(bf16[256,768]{1,0:T(8,128)(2,1)S(1)} %get-tuple-element., ...), custom_call_target="tpu_custom_call" | custom-call | flops 536870912 | bytes 4194304 | tf_op jit(solution)/shard_map/attend/pallas_call | solution.py:179
  58.1 1.5 %collective-permute-start.14 = (bf16[256,256]{1,0:T(8,128)(2,1)S(1)}, bf16[256,256]{1,0:T(8,128)(2,1)S(1)}, u32[]{:S(2)}, u32[]{:S(2)}) collective-permute-start(bf16[256,256]{1,0:T(8,128)(2,1)S(1)} %get-tuple-element.56), channel_id=1, source_target_pairs={{24,0},{28,4},{16,8},{20,12},{8,16},{12,20},{0,24},{4,28},{25,1},{... | collective-permute-start | bytes 393224 | tf_op jit(solution)/shard_map/ppermute | solution.py:471
  59.6 1.3 %collective-permute-start.15 = (bf16[256,256]{1,0:T(8,128)(2,1)S(1)}, bf16[256,256]{1,0:T(8,128)(2,1)S(1)}, u32[]{:S(2)}, u32[]{:S(2)}) collective-permute-start(bf16[256,256]{1,0:T(8,128)(2,1)S(1)} %get-tuple-element.57), channel_id=1, source_target_pairs={{4,0},{0,4},{12,8},{8,12},{20,16},{16,20},{28,24},{24,28},{5,1},{1... | collective-permute-start | bytes 393224 | tf_op jit(solution)/shard_map/ppermute | solution.py:471
  60.9 1.1 %collective-permute-start.16 = (bf16[256,256]{1,0:T(8,128)(2,1)S(1)}, bf16[256,256]{1,0:T(8,128)(2,1)S(1)}, u32[]{:S(2)}, u32[]{:S(2)}) collective-permute-start(bf16[256,256]{1,0:T(8,128)(2,1)S(1)} %get-tuple-element.59), channel_id=1, source_target_pairs={{20,0},{8,4},{28,8},{0,12},{4,16},{24,20},{12,24},{16,28},{21,1},{... | collective-permute-start | bytes 393224 | tf_op jit(solution)/shard_map/ppermute | solution.py:471
  62.5 2.4 %collective-permute-done.13.rest_0_ = bf16[256,256]{1,0:T(8,128)(2,1)S(1)} collective-permute-done((bf16[256,256]{1,0:T(8,128)(2,1)S(1)}, bf16[256,256]{1,0:T(8,128)(2,1)S(1)}, u32[]{:S(2)}, u32[]{:S(2)}) %collective-permute-start.13) | collective-permute-done | bytes 131104 | tf_op jit(solution)/shard_map/ppermute | solution.py:471
  64.9 1.0 %collective-permute-done.14.rest_1_ = bf16[256,256]{1,0:T(8,128)(2,1)S(1)} collective-permute-done((bf16[256,256]{1,0:T(8,128)(2,1)S(1)}, bf16[256,256]{1,0:T(8,128)(2,1)S(1)}, u32[]{:S(2)}, u32[]{:S(2)}) %collective-permute-start.14) | collective-permute-done | bytes 131104 | tf_op jit(solution)/shard_map/ppermute | solution.py:471
  65.9 1.1 %collective-permute-start.19 = (bf16[256,256]{1,0:T(8,128)(2,1)S(1)}, bf16[256,256]{1,0:T(8,128)(2,1)S(1)}, u32[]{:S(2)}, u32[]{:S(2)}) collective-permute-start(bf16[256,256]{1,0:T(8,128)(2,1)S(1)} %get-tuple-element.62), channel_id=1, source_target_pairs={{8,0},{20,4},{0,8},{28,12},{24,16},{4,20},{16,24},{12,28},{9,1},{2... | collective-permute-start | bytes 393224 | tf_op jit(solution)/shard_map/ppermute | solution.py:471
  67.0 1.3 %base.1.base_ref = f32[2048,256]{1,0:T(8,128)S(1)} custom-call(f32[1,256]{1,0:T(1,128)S(1)} %bitcast.2, f32[2048,256]{1,0:T(8,128)S(1)} %get-tuple-element.48.y_ref, bf16[2048,1024]{1,0:T(8,128)(2,1)S(1)} %get-tuple-element.49.onehot, f32[1,2048]{1,0:T(1,128)S(1)} %add.7.refs_8_.total_ref, bf16[256,256]{1,0:T(8,128)(2,1)S(1)} %collective-permute-done.13.rest_0_, ...), custom_call_target="tpu_custom_call" | custom-call | flops 1073741824 | bytes 4194304 | tf_op jit(solution)/shard_map/base/pallas_call | solution.py:408
  68.3 1.1 %collective-permute-done.16.rest_0_ = bf16[256,256]{1,0:T(8,128)(2,1)S(1)} collective-permute-done((bf16[256,256]{1,0:T(8,128)(2,1)S(1)}, bf16[256,256]{1,0:T(8,128)(2,1)S(1)}, u32[]{:S(2)}, u32[]{:S(2)}) %collective-permute-start.16) | collective-permute-done | bytes 131104 | tf_op jit(solution)/shard_map/ppermute | solution.py:471
  69.5 1.9 %collective-permute-done.18.rest_2_ = bf16[256,256]{1,0:T(8,128)(2,1)S(1)} collective-permute-done((bf16[256,256]{1,0:T(8,128)(2,1)S(1)}, bf16[256,256]{1,0:T(8,128)(2,1)S(1)}, u32[]{:S(2)}, u32[]{:S(2)}) %collective-permute-start.18) | collective-permute-done | bytes 131104 | tf_op jit(solution)/shard_map/ppermute | solution.py:471
  71.9 2.1 %mix.1 = bf16[2048,256]{1,0:T(8,128)(2,1)} custom-call(f32[2048,256]{1,0:T(8,128)S(1)} %base.1.base_ref, bf16[2048,1024]{1,0:T(8,128)(2,1)S(1)} %get-tuple-element.41.rest_1_.onehot, bf16[256,256]{1,0:T(8,128)(2,1)S(1)} %collective-permute-done.16.rest_0_, bf16[256,256]{1,0:T(8,128)(2,1)S(1)} %collective-permute-done.17.rest_1_, ...), custom_call_target="tpu_custom_call" | custom-call | flops 1073741824 | bytes 4194304 | tf_op jit(solution)/shard_map/mix/pallas_call | solution.py:436
  (47 shorter events, 4.9 us)
Async XLA Ops:
  0.0 0.7 copy-start.8
  0.7 1.5 %copy-start = (bf16[2048,256]{1,0:T(8,128)(2,1)S(1)}, bf16[2048,256]{1,0:T(8,128)(2,1)}, u32[]{:S(2)}) copy-start(bf16[2048,256]{1,0:T(8,128)(2,1)} %k_ref.9) | copy-start | bytes 3145732
  0.7 1.5 %copy-start.1 = (bf16[2048,256]{1,0:T(8,128)(2,1)S(1)}, bf16[2048,256]{1,0:T(8,128)(2,1)}, u32[]{:S(2)}) copy-start(bf16[2048,256]{1,0:T(8,128)(2,1)} %v_ref.9) | copy-start | bytes 3145732
  0.7 1.9 %copy-start.2 = (bf16[2048,256]{1,0:T(8,128)(2,1)S(1)}, bf16[2048,256]{1,0:T(8,128)(2,1)}, u32[]{:S(2)}) copy-start(bf16[2048,256]{1,0:T(8,128)(2,1)} %q_ref.9) | copy-start | bytes 3145732
  2.1 4.9 %copy-start.4 = (bf16[1,256,256]{2,1,0:T(8,128)(2,1)S(1)}, bf16[1,256,256]{2,1,0:T(8,128)(2,1)}, u32[]{:S(2)}) copy-start(bf16[1,256,256]{2,1,0:T(8,128)(2,1)} %one_ref.3) | copy-start | bytes 393220
  2.1 4.8 %copy-start.5 = (bf16[1,256,256]{2,1,0:T(8,128)(2,1)S(1)}, bf16[1,256,256]{2,1,0:T(8,128)(2,1)}, u32[]{:S(2)}) copy-start(bf16[1,256,256]{2,1,0:T(8,128)(2,1)} %three_ref.3) | copy-start | bytes 393220
  2.1 4.8 %copy-start.6 = (bf16[1,256,256]{2,1,0:T(8,128)(2,1)S(1)}, bf16[1,256,256]{2,1,0:T(8,128)(2,1)}, u32[]{:S(2)}) copy-start(bf16[1,256,256]{2,1,0:T(8,128)(2,1)} %two_ref.3) | copy-start | bytes 393220
  2.1 4.8 %copy-start.7 = (f32[2048,1]{0,1:T(1,128)S(1)}, f32[2048,1]{0,1:T(1,128)}, u32[]{:S(2)}) copy-start(f32[2048,1]{0,1:T(1,128)} %param.12) | copy-start | bytes 24580
  3.6 12.9 %collective-permute-start.1 = (bf16[256,768]{1,0:T(8,128)(2,1)S(1)}, bf16[256,768]{1,0:T(8,128)(2,1)S(1)}, u32[]{:S(2)}, u32[]{:S(2)}) collective-permute-start(bf16[256,768]{1,0:T(8,128)(2,1)S(1)} %get-tuple-element.38), channel_id=1, source_target_pairs={{0,28},{4,24},{8,20},{12,16},{16,12},{20,8},{24,4},{28,0},{1,29},{... | collective-permute-start | bytes 1179656 | tf_op jit(solution)/shard_map/ppermute | solution.py:466
  9.9 1.8 %collective-permute-start = (bf16[384,256]{1,0:T(8,128)(2,1)S(1)}, bf16[384,256]{1,0:T(8,128)(2,1)S(1)}, u32[]{:S(2)}, u32[]{:S(2)}) collective-permute-start(bf16[384,256]{1,0:T(8,128)(2,1)S(1)} %get-tuple-element.37), channel_id=1, source_target_pairs={{0,4},{4,0},{8,12},{12,8},{16,20},{20,16},{24,28},{28,24},{1,5},{5... | collective-permute-start | bytes 589832 | tf_op jit(solution)/shard_map/ppermute | solution.py:270
  16.5 5.4 %copy-start.9 = (s32[1,2048]{1,0:T(1,128)S(1)}, s32[1,2048]{1,0:T(1,128)}, u32[]{:S(2)}) copy-start(s32[1,2048]{1,0:T(1,128)} %order_ref.3) | copy-start | bytes 24580
  16.5 7.0 %collective-permute-start.2 = (bf16[384,256]{1,0:T(8,128)(2,1)S(1)}, bf16[384,256]{1,0:T(8,128)(2,1)S(1)}, u32[]{:S(2)}, u32[]{:S(2)}) collective-permute-start(bf16[384,256]{1,0:T(8,128)(2,1)S(1)} %convert_element_type.9), channel_id=1, source_target_pairs={{0,8},{4,20},{8,0},{12,28},{16,24},{20,4},{24,16},{28,12},{1,9},{5... | collective-permute-start | bytes 589832 | tf_op jit(solution)/shard_map/ppermute | solution.py:282
  20.4 14.3 %collective-permute-start.4 = (bf16[256,768]{1,0:T(8,128)(2,1)S(1)}, bf16[256,768]{1,0:T(8,128)(2,1)S(1)}, u32[]{:S(2)}, u32[]{:S(2)}) collective-permute-start(bf16[256,768]{1,0:T(8,128)(2,1)S(1)} %get-tuple-element.40), channel_id=1, source_target_pairs={{0,24},{4,28},{8,16},{12,20},{16,8},{20,12},{24,0},{28,4},{1,25},{... | collective-permute-start | bytes 1179656 | tf_op jit(solution)/shard_map/ppermute | solution.py:466
  23.7 11.0 %collective-permute-start.3 = (bf16[384,256]{1,0:T(8,128)(2,1)S(1)}, bf16[384,256]{1,0:T(8,128)(2,1)S(1)}, u32[]{:S(2)}, u32[]{:S(2)}) collective-permute-start(bf16[384,256]{1,0:T(8,128)(2,1)S(1)} %convert_element_type.10), channel_id=1, source_target_pairs={{0,16},{4,12},{8,24},{12,4},{16,0},{20,28},{24,8},{28,20},{1,17},{... | collective-permute-start | bytes 589832 | tf_op jit(solution)/shard_map/ppermute | solution.py:282
  27.8 12.0 %collective-permute-start.6 = (bf16[256,768]{1,0:T(8,128)(2,1)S(1)}, bf16[256,768]{1,0:T(8,128)(2,1)S(1)}, u32[]{:S(2)}, u32[]{:S(2)}) collective-permute-start(bf16[256,768]{1,0:T(8,128)(2,1)S(1)} %get-tuple-element.44), channel_id=1, source_target_pairs={{0,20},{4,8},{8,28},{12,0},{16,4},{20,24},{24,12},{28,16},{1,21},{... | collective-permute-start | bytes 1179656 | tf_op jit(solution)/shard_map/ppermute | solution.py:466
  28.1 17.4 %collective-permute-start.7 = (bf16[256,768]{1,0:T(8,128)(2,1)S(1)}, bf16[256,768]{1,0:T(8,128)(2,1)S(1)}, u32[]{:S(2)}, u32[]{:S(2)}) collective-permute-start(bf16[256,768]{1,0:T(8,128)(2,1)S(1)} %get-tuple-element.45), channel_id=1, source_target_pairs={{0,16},{4,12},{8,24},{12,4},{16,0},{20,28},{24,8},{28,20},{1,17},{... | collective-permute-start | bytes 1179656 | tf_op jit(solution)/shard_map/ppermute | solution.py:466
  34.8 4.6 %collective-permute-start.5 = (bf16[384,256]{1,0:T(8,128)(2,1)S(1)}, bf16[384,256]{1,0:T(8,128)(2,1)S(1)}, u32[]{:S(2)}, u32[]{:S(2)}) collective-permute-start(bf16[384,256]{1,0:T(8,128)(2,1)S(1)} %convert_element_type.11), channel_id=1, source_target_pairs={{0,4},{4,0},{8,12},{12,8},{16,20},{20,16},{24,28},{28,24},{1,5},{5... | collective-permute-start | bytes 589832 | tf_op jit(solution)/shard_map/ppermute | solution.py:284
  37.5 29.5 %copy-start.3 = (f32[256]{0:T(256)S(1)}, f32[256]{0:T(256)}, u32[]{:S(2)}) copy-start(f32[256]{0:T(256)} %param.16) | copy-start | bytes 3076
  37.5 19.0 %collective-permute-start.11 = (bf16[256,768]{1,0:T(8,128)(2,1)S(1)}, bf16[256,768]{1,0:T(8,128)(2,1)S(1)}, u32[]{:S(2)}, u32[]{:S(2)}) collective-permute-start(bf16[256,768]{1,0:T(8,128)(2,1)S(1)} %get-tuple-element.53), channel_id=1, source_target_pairs={{0,8},{4,20},{8,0},{12,28},{16,24},{20,4},{24,16},{28,12},{1,9},{5... | collective-permute-start | bytes 1179656 | tf_op jit(solution)/shard_map/ppermute | solution.py:466
  39.1 17.4 %collective-permute-start.12 = (bf16[256,768]{1,0:T(8,128)(2,1)S(1)}, bf16[256,768]{1,0:T(8,128)(2,1)S(1)}, u32[]{:S(2)}, u32[]{:S(2)}) collective-permute-start(bf16[256,768]{1,0:T(8,128)(2,1)S(1)} %get-tuple-element.54), channel_id=1, source_target_pairs={{0,12},{4,16},{8,4},{12,24},{16,28},{20,0},{24,20},{28,8},{1,13},{... | collective-permute-start | bytes 1179656 | tf_op jit(solution)/shard_map/ppermute | solution.py:466
  39.4 17.1 %collective-permute-start.10 = (bf16[256,768]{1,0:T(8,128)(2,1)S(1)}, bf16[256,768]{1,0:T(8,128)(2,1)S(1)}, u32[]{:S(2)}, u32[]{:S(2)}) collective-permute-start(bf16[256,768]{1,0:T(8,128)(2,1)S(1)} %get-tuple-element.52), channel_id=1, source_target_pairs={{0,4},{4,0},{8,12},{12,8},{16,20},{20,16},{24,28},{28,24},{1,5},{5... | collective-permute-start | bytes 1179656 | tf_op jit(solution)/shard_map/ppermute | solution.py:466
  48.2 3.7 %collective-permute-start.8 = (f32[1,2048]{1,0:T(1,128)S(1)}, f32[1,2048]{1,0:T(1,128)S(1)}, u32[]{:S(2)}, u32[]{:S(2)}) collective-permute-start(f32[1,2048]{1,0:T(1,128)S(1)} %get-tuple-element.50), channel_id=1, source_target_pairs={{0,1},{1,0},{2,3},{3,2},{4,5},{5,4},{6,7},{7,6},{8,9},{9,8},{10,11... | collective-permute-start | bytes 24584 | tf_op jit(solution)/shard_map/ppermute | solution.py:460
  51.9 4.6 %collective-permute-start.9 = (f32[1,2048]{1,0:T(1,128)S(1)}, f32[1,2048]{1,0:T(1,128)S(1)}, u32[]{:S(2)}, u32[]{:S(2)}) collective-permute-start(f32[1,2048]{1,0:T(1,128)S(1)} %add.6), channel_id=1, source_target_pairs={{0,2},{1,3},{2,0},{3,1},{4,6},{5,7},{6,4},{7,5},{8,10},{9,11},{10,... | collective-permute-start | bytes 24584 | tf_op jit(solution)/shard_map/ppermute | solution.py:460
  58.1 6.8 %collective-permute-start.13 = (bf16[256,256]{1,0:T(8,128)(2,1)S(1)}, bf16[256,256]{1,0:T(8,128)(2,1)S(1)}, u32[]{:S(2)}, u32[]{:S(2)}) collective-permute-start(bf16[256,256]{1,0:T(8,128)(2,1)S(1)} %get-tuple-element.55), channel_id=1, source_target_pairs={{28,0},{24,4},{20,8},{16,12},{12,16},{8,20},{4,24},{0,28},{29,1},{... | collective-permute-start | bytes 393224 | tf_op jit(solution)/shard_map/ppermute | solution.py:471
  58.1 7.8 %collective-permute-start.14 = (bf16[256,256]{1,0:T(8,128)(2,1)S(1)}, bf16[256,256]{1,0:T(8,128)(2,1)S(1)}, u32[]{:S(2)}, u32[]{:S(2)}) collective-permute-start(bf16[256,256]{1,0:T(8,128)(2,1)S(1)} %get-tuple-element.56), channel_id=1, source_target_pairs={{24,0},{28,4},{16,8},{20,12},{8,16},{12,20},{0,24},{4,28},{25,1},{... | collective-permute-start | bytes 393224 | tf_op jit(solution)/shard_map/ppermute | solution.py:471
  59.6 7.4 %collective-permute-start.15 = (bf16[256,256]{1,0:T(8,128)(2,1)S(1)}, bf16[256,256]{1,0:T(8,128)(2,1)S(1)}, u32[]{:S(2)}, u32[]{:S(2)}) collective-permute-start(bf16[256,256]{1,0:T(8,128)(2,1)S(1)} %get-tuple-element.57), channel_id=1, source_target_pairs={{4,0},{0,4},{12,8},{8,12},{20,16},{16,20},{28,24},{24,28},{5,1},{1... | collective-permute-start | bytes 393224 | tf_op jit(solution)/shard_map/ppermute | solution.py:471
  60.9 8.5 %collective-permute-start.16 = (bf16[256,256]{1,0:T(8,128)(2,1)S(1)}, bf16[256,256]{1,0:T(8,128)(2,1)S(1)}, u32[]{:S(2)}, u32[]{:S(2)}) collective-permute-start(bf16[256,256]{1,0:T(8,128)(2,1)S(1)} %get-tuple-element.59), channel_id=1, source_target_pairs={{20,0},{8,4},{28,8},{0,12},{4,16},{24,20},{12,24},{16,28},{21,1},{... | collective-permute-start | bytes 393224 | tf_op jit(solution)/shard_map/ppermute | solution.py:471
  62.0 7.5 %collective-permute-start.17 = (bf16[256,256]{1,0:T(8,128)(2,1)S(1)}, bf16[256,256]{1,0:T(8,128)(2,1)S(1)}, u32[]{:S(2)}, u32[]{:S(2)}) collective-permute-start(bf16[256,256]{1,0:T(8,128)(2,1)S(1)} %get-tuple-element.60), channel_id=1, source_target_pairs={{16,0},{12,4},{24,8},{4,12},{0,16},{28,20},{8,24},{20,28},{17,1},{... | collective-permute-start | bytes 393224 | tf_op jit(solution)/shard_map/ppermute | solution.py:471
  64.9 6.5 %collective-permute-start.18 = (bf16[256,256]{1,0:T(8,128)(2,1)S(1)}, bf16[256,256]{1,0:T(8,128)(2,1)S(1)}, u32[]{:S(2)}, u32[]{:S(2)}) collective-permute-start(bf16[256,256]{1,0:T(8,128)(2,1)S(1)} %get-tuple-element.61), channel_id=1, source_target_pairs={{12,0},{16,4},{4,8},{24,12},{28,16},{0,20},{20,24},{8,28},{13,1},{... | collective-permute-start | bytes 393224 | tf_op jit(solution)/shard_map/ppermute | solution.py:471
  65.9 6.0 %collective-permute-start.19 = (bf16[256,256]{1,0:T(8,128)(2,1)S(1)}, bf16[256,256]{1,0:T(8,128)(2,1)S(1)}, u32[]{:S(2)}, u32[]{:S(2)}) collective-permute-start(bf16[256,256]{1,0:T(8,128)(2,1)S(1)} %get-tuple-element.62), channel_id=1, source_target_pairs={{8,0},{20,4},{0,8},{28,12},{24,16},{4,20},{16,24},{12,28},{9,1},{2... | collective-permute-start | bytes 393224 | tf_op jit(solution)/shard_map/ppermute | solution.py:471

commit v13 on v10

--- a/solution.py
+++ b/solution.py
@@ -453,13 +453,14 @@
 
 def sum_over_heads(square, heads):
     if not power_of_two(heads):
-        return lax.psum(square, "head")
+        return [lax.psum(square, "head")]
+    sums = [square]
     step = 1
     while step < heads:
         pairs = [(at, at ^ step) for at in range(heads)]
-        square = square + lax.ppermute(square, "head", pairs)
+        sums.append(sums[-1] + lax.ppermute(sums[-1], "head", pairs))
         step *= 2
-    return square
+    return sums
 
 
 def exchange(block, step, n):
@@ -495,8 +496,9 @@
     mine = core_step(parts, [came[0]], n)
     summed = sum_over_chips(mine, len(parts) == 2, [tokens[1:2], came[1:3] + tokens[2:] + [late_places]], n)
     y, square = read_out(queries, *weights, summed, came[3:4])
-    total = sum_over_heads(square, heads)
-    attended = attend([arrived[step] for step in range(n)], [total], n, width)
+    sums = sum_over_heads(square, heads)
+    total = sums[-1]
+    attended = attend([arrived[step] for step in range(n)], [sums[len(sums) // 2]], n, width)
     returned = {step: give_back(attended[step], step, n) for step in early + late}
     given = base(
         gain.reshape(1, width), y, early_places, total, heads, [returned[step] for step in early]

time: 71.2 us -> 70.3 us (0.987)
  waiting for transfers between devices: 26.9 us -> 23.4 us
  starting transfers between devices: 21.8 us -> 24.4 us
    ppermute x7, waiting for transfers between devices: 7.08 us -> 2.95 us  [give_back(): return lax.ppermute(block, 'cam', pairs) if step else block]
    ppermute x7, starting transfers between devices: 5.43 us -> 7.83 us  [give_back(): return lax.ppermute(block, 'cam', pairs) if step else block]
    ppermute x7, waiting for transfers between devices: 4.77 us -> 6.98 us  [exchange(): return lax.ppermute(block, 'cam', routes(step, n)) if step else block]
    ppermute x2, waiting for transfers between devices: 4.03 us -> 2.42 us  [sum_over_heads(): sums.append(sums[-1] + lax.ppermute(sums[-1], 'head', pairs))]
  transfers between devices with their start and end apart: 20 -> 20, of which waited for: 12 -> 10; matrix products, arithmetic and copies ran while one was open for 0% -> 0% of each run, Pallas kernels for 20% -> 20%
where the time goes in v13:
time: 70.3 us; the launch traced here: 70 us
  starting transfers between devices  24.4 us (35%)
  waiting for transfers between devices  23.4 us (33%)
  Pallas kernels  20.7 us (29%)
  local copies, waits for them, and re-layouts  1.16 us (2%)
    ppermute x2, waiting for transfers between devices, sum_over_chips(): got = lax.ppermute(mine.astype(BF16), 'cam', pairs)  9.93 us
    ppermute x7, starting transfers between devices, exchange(): return lax.ppermute(block, 'cam', routes(step, n)) if step else block  8.05 us
    ppermute x7, starting transfers between devices, give_back(): return lax.ppermute(block, 'cam', pairs) if step else block  7.83 us
    pallas_call x3, Pallas kernels, sort_tokens(): pl.pallas_call(functools.partial(sort_kernel, size), out_shape=[jax.Shape...  7.03 us
    ppermute x7, waiting for transfers between devices, exchange(): return lax.ppermute(block, 'cam', routes(step, n)) if step else block  6.98 us
    ppermute x2, starting transfers between devices, sum_over_heads(): sums.append(sums[-1] + lax.ppermute(sums[-1], 'head', pairs))  4.49 us
    ppermute x7, waiting for transfers between devices, give_back(): return lax.ppermute(block, 'cam', pairs) if step else block  2.95 us
    pallas_call x1, Pallas kernels, gradients(): pl.pallas_call(functools.partial(grads_kernel, n, split), out_shape=[jax....  2.89 us
  transfers between devices with their start and end apart: 20, of which 10 were waited for; matrix products, arithmetic and copies ran while one was open for 0% of the time, Pallas kernels for 20%

profile of v13, /device:TPU:0, one launch (start us, length us, event | category | flops | bytes accessed | tf_op | source)
XLA Modules:
  0.0 70.0 jit_solution(8364410246717644972)
XLA Ops:
  0.0 0.7 copy-done.8
  0.7 1.4 %mark.1 = (bf16[512,2048]{1,0:T(8,128)(2,1)S(1)}, bf16[512,2048]{1,0:T(8,128)(2,1)S(1)}, bf16[1024,2048]{1,0:T(8,128)(2,1)S(1)}, f32[8,128]{1,0:T(8,128)}) custom-call(s32[1,2048]{1,0:T(1,128)S(1)} %copy-done.8), custom_call_target="tpu_custom_call" | custom-call | flops 999999995904 | bytes 1024 | tf_op jit(solution)/shard_map/mark/pallas_call | solution.py:107
  2.6 1.8 %sort_tokens.3 = (bf16[256,768]{1,0:T(8,128)(2,1)S(1)}, bf16[256,768]{1,0:T(8,128)(2,1)S(1)}, f32[8,128]{1,0:T(8,128)S(1)}) custom-call(bf16[512,2048]{1,0:T(8,128)(2,1)S(1)} %get-tuple-element.33.onehot, bf16[2048,256]{1,0:T(8,128)(2,1)S(1)} %copy-done.3, bf16[2048,256]{1,0:T(8,128)(2,1)S(1)} %copy-done.1, bf16[2048,256]{1,0:T(8,128)(2,1)S(1)} %copy-done.2), custom_call_target="tpu_custom_call" | custom-call | flops 1610612736 | bytes 3145728 | tf_op jit(solution)/shard_map/sort_tokens/pallas_call | solution.py:140
  4.4 3.4 %collective-permute-start.1 = (bf16[256,768]{1,0:T(8,128)(2,1)S(1)}, bf16[256,768]{1,0:T(8,128)(2,1)S(1)}, u32[]{:S(2)}, u32[]{:S(2)}) collective-permute-start(bf16[256,768]{1,0:T(8,128)(2,1)S(1)} %get-tuple-element.37), channel_id=1, source_target_pairs={{0,28},{4,24},{8,20},{12,16},{16,12},{20,8},{24,4},{28,0},{1,29},{... | collective-permute-start | bytes 1179656 | tf_op jit(solution)/shard_map/ppermute | solution.py:467
  7.8 2.9 %gradients.1 = (f32[384,256]{1,0:T(8,128)S(1)}, bf16[384,256]{1,0:T(8,128)(2,1)S(1)}) custom-call(bf16[2048,256]{1,0:T(8,128)(2,1)S(1)} %copy-done.1, bf16[2048,256]{1,0:T(8,128)(2,1)S(1)} %copy-done.2, f32[1,2048]{1,0:T(1,128)S(1)} %bitcast.3, bf16[1,256,256]{2,1,0:T(8,128)(2,1)S(1)} %copy-done.4, bf16[1,256,256]{2,1,0:T(8,128)(2,1)S(1)} %copy-done.5, ...), custom_call_target="tpu_custom_call" | custom-call | flops 1610612736 | bytes 4194304 | tf_op jit(solution)/shard_map/gradients/pallas_call | solution.py:236
  10.7 0.7 %collective-permute-start = (bf16[384,256]{1,0:T(8,128)(2,1)S(1)}, bf16[384,256]{1,0:T(8,128)(2,1)S(1)}, u32[]{:S(2)}, u32[]{:S(2)}) collective-permute-start(bf16[384,256]{1,0:T(8,128)(2,1)S(1)} %get-tuple-element.36), channel_id=1, source_target_pairs={{0,4},{4,0},{8,12},{12,8},{16,20},{20,16},{24,28},{28,24},{1,5},{5... | collective-permute-start | bytes 589832 | tf_op jit(solution)/shard_map/ppermute | solution.py:270
  11.4 1.1 %collective-permute-done.got_ref = bf16[384,256]{1,0:T(8,128)(2,1)S(1)} collective-permute-done((bf16[384,256]{1,0:T(8,128)(2,1)S(1)}, bf16[384,256]{1,0:T(8,128)(2,1)S(1)}, u32[]{:S(2)}, u32[]{:S(2)}) %collective-permute-start) | collective-permute-done | bytes 196640 | tf_op jit(solution)/shard_map/ppermute | solution.py:270
  12.5 4.8 %collective-permute-done.1.rest_0_.refs_7_ = bf16[256,768]{1,0:T(8,128)(2,1)S(1)} collective-permute-done((bf16[256,768]{1,0:T(8,128)(2,1)S(1)}, bf16[256,768]{1,0:T(8,128)(2,1)S(1)}, u32[]{:S(2)}, u32[]{:S(2)}) %collective-permute-start.1) | collective-permute-done | bytes 393248 | tf_op jit(solution)/shard_map/ppermute | solution.py:467
  17.4 2.5 %collective-permute-start.2 = (bf16[384,256]{1,0:T(8,128)(2,1)S(1)}, bf16[384,256]{1,0:T(8,128)(2,1)S(1)}, u32[]{:S(2)}, u32[]{:S(2)}) collective-permute-start(bf16[384,256]{1,0:T(8,128)(2,1)S(1)} %convert_element_type.6), channel_id=1, source_target_pairs={{0,8},{4,20},{8,0},{12,28},{16,24},{20,4},{24,16},{28,12},{1,9},{5... | collective-permute-start | bytes 589832 | tf_op jit(solution)/shard_map/ppermute | solution.py:282
  19.8 1.8 %sort_tokens.4 = (bf16[256,768]{1,0:T(8,128)(2,1)S(1)}, bf16[256,768]{1,0:T(8,128)(2,1)S(1)}, f32[8,128]{1,0:T(8,128)S(1)}) custom-call(bf16[512,2048]{1,0:T(8,128)(2,1)S(1)} %get-tuple-element.38.onehot, bf16[2048,256]{1,0:T(8,128)(2,1)S(1)} %copy-done.3, bf16[2048,256]{1,0:T(8,128)(2,1)S(1)} %copy-done.1, bf16[2048,256]{1,0:T(8,128)(2,1)S(1)} %copy-done.2), custom_call_target="tpu_custom_call" | custom-call | flops 1610612736 | bytes 3145728 | tf_op jit(solution)/shard_map/sort_tokens/pallas_call | solution.py:140
  21.7 1.6 %collective-permute-start.7 = (bf16[256,768]{1,0:T(8,128)(2,1)S(1)}, bf16[256,768]{1,0:T(8,128)(2,1)S(1)}, u32[]{:S(2)}, u32[]{:S(2)}) collective-permute-start(bf16[256,768]{1,0:T(8,128)(2,1)S(1)} %get-tuple-element.45), channel_id=1, source_target_pairs={{0,16},{4,12},{8,24},{12,4},{16,0},{20,28},{24,8},{28,20},{1,17},{... | collective-permute-start | bytes 1179656 | tf_op jit(solution)/shard_map/ppermute | solution.py:467
  23.3 1.7 %place.1 = (bf16[2048,1024]{1,0:T(8,128)(2,1)S(1)}, bf16[2048,1024]{1,0:T(8,128)(2,1)S(1)}) custom-call(s32[1,2048]{1,0:T(1,128)S(1)} %copy-done.9), custom_call_target="tpu_custom_call" | custom-call | flops 4194304 | bytes 8388608 | tf_op jit(solution)/shard_map/place/pallas_call | solution.py:373
  25.0 6.0 %collective-permute-done.2.got_ref = bf16[384,256]{1,0:T(8,128)(2,1)S(1)} collective-permute-done((bf16[384,256]{1,0:T(8,128)(2,1)S(1)}, bf16[384,256]{1,0:T(8,128)(2,1)S(1)}, u32[]{:S(2)}, u32[]{:S(2)}) %collective-permute-start.2) | collective-permute-done | bytes 196640 | tf_op jit(solution)/shard_map/ppermute | solution.py:282
  31.1 3.4 %sort_tokens.5 = (bf16[256,768]{1,0:T(8,128)(2,1)S(1)}, bf16[256,768]{1,0:T(8,128)(2,1)S(1)}, bf16[256,768]{1,0:T(8,128)(2,1)S(1)}, bf16[256,768]{1,0:T(8,128)(2,1)S(1)}, f32[8,128]{1,0:T(8,128)S(1)}) custom-call(bf16[1024,2048]{1,0:T(8,128)(2,1)S(1)} %get-tuple-element.42.onehot, bf16[2048,256]{1,0:T(8,128)(2,1)S(1)} %copy-done.3, ...), custom_call_target="tpu_custom_call" | custom-call | flops 3221225472 | bytes 3145728 | tf_op jit(solution)/shard_map/sort_tokens/pallas_call | solution.py:140
  34.6 3.9 %collective-permute-done.3.got_ref = bf16[384,256]{1,0:T(8,128)(2,1)S(1)} collective-permute-done((bf16[384,256]{1,0:T(8,128)(2,1)S(1)}, bf16[384,256]{1,0:T(8,128)(2,1)S(1)}, u32[]{:S(2)}, u32[]{:S(2)}) %collective-permute-start.3) | collective-permute-done | bytes 196640 | tf_op jit(solution)/shard_map/ppermute | solution.py:282
  38.6 0.7 %collective-permute-start.6 = (f32[384,256]{1,0:T(8,128)S(1)}, f32[384,256]{1,0:T(8,128)S(1)}, u32[]{:S(2)}, u32[]{:S(2)}) collective-permute-start(f32[384,256]{1,0:T(8,128)S(1)} %merge.5.rest_0_), channel_id=1, source_target_pairs={{0,4},{4,0},{8,12},{12,8},{16,20},{20,16},{24,28},{28,24},{1,5},{5... | collective-permute-start | bytes 1179656 | tf_op jit(solution)/shard_map/ppermute | solution.py:287
  39.4 2.0 %collective-permute-start.11 = (bf16[256,768]{1,0:T(8,128)(2,1)S(1)}, bf16[256,768]{1,0:T(8,128)(2,1)S(1)}, u32[]{:S(2)}, u32[]{:S(2)}) collective-permute-start(bf16[256,768]{1,0:T(8,128)(2,1)S(1)} %get-tuple-element.51), channel_id=1, source_target_pairs={{0,8},{4,20},{8,0},{12,28},{16,24},{20,4},{24,16},{28,12},{1,9},{5... | collective-permute-start | bytes 1179656 | tf_op jit(solution)/shard_map/ppermute | solution.py:467
  41.4 0.9 %collective-permute-start.12 = (bf16[256,768]{1,0:T(8,128)(2,1)S(1)}, bf16[256,768]{1,0:T(8,128)(2,1)S(1)}, u32[]{:S(2)}, u32[]{:S(2)}) collective-permute-start(bf16[256,768]{1,0:T(8,128)(2,1)S(1)} %get-tuple-element.52), channel_id=1, source_target_pairs={{0,12},{4,16},{8,4},{12,24},{16,28},{20,0},{24,20},{28,8},{1,13},{... | collective-permute-start | bytes 1179656 | tf_op jit(solution)/shard_map/ppermute | solution.py:467
  42.3 2.7 %read_out.1 = (f32[2048,256]{1,0:T(8,128)S(1)}, f32[1,2048]{1,0:T(1,128)S(1)}) custom-call(bf16[2048,256]{1,0:T(8,128)(2,1)S(1)} %copy-done.3, bf16[1,256,256]{2,1,0:T(8,128)(2,1)S(1)} %copy-done.4, bf16[1,256,256]{2,1,0:T(8,128)(2,1)S(1)} %copy-done.5, bf16[1,256,256]{2,1,0:T(8,128)(2,1)S(1)} %copy-done.6, f32[384,256]{1,0:T(8,128)S(1)} %merge.5.rest_0_, ...), custom_call_target="tpu_custom_call" | custom-call | flops 805306368 | bytes 4194304 | tf_op jit(solution)/shard_map/read_out/pallas_call | solution.py:334
  45.0 1.6 %collective-permute-start.8 = (f32[1,2048]{1,0:T(1,128)S(1)}, f32[1,2048]{1,0:T(1,128)S(1)}, u32[]{:S(2)}, u32[]{:S(2)}) collective-permute-start(f32[1,2048]{1,0:T(1,128)S(1)} %get-tuple-element.48), channel_id=1, source_target_pairs={{0,1},{1,0},{2,3},{3,2},{4,5},{5,4},{6,7},{7,6},{8,9},{9,8},{10,11... | collective-permute-start | bytes 24584 | tf_op jit(solution)/shard_map/ppermute | solution.py:461
  46.6 2.1 %collective-permute-done.8 = f32[1,2048]{1,0:T(1,128)S(1)} collective-permute-done((f32[1,2048]{1,0:T(1,128)S(1)}, f32[1,2048]{1,0:T(1,128)S(1)}, u32[]{:S(2)}, u32[]{:S(2)}) %collective-permute-start.8) | collective-permute-done | bytes 8224 | tf_op jit(solution)/shard_map/ppermute | solution.py:461
  48.7 2.2 %collective-permute-done.12.refs_3_ = bf16[256,768]{1,0:T(8,128)(2,1)S(1)} collective-permute-done((bf16[256,768]{1,0:T(8,128)(2,1)S(1)}, bf16[256,768]{1,0:T(8,128)(2,1)S(1)}, u32[]{:S(2)}, u32[]{:S(2)}) %collective-permute-start.12) | collective-permute-done | bytes 393248 | tf_op jit(solution)/shard_map/ppermute | solution.py:467
  50.9 1.5 %attend.1 = (bf16[256,256]{1,0:T(8,128)(2,1)S(1)}, bf16[256,256]{1,0:T(8,128)(2,1)S(1)}, bf16[256,256]{1,0:T(8,128)(2,1)S(1)}, bf16[256,256]{1,0:T(8,128)(2,1)S(...) custom-call(bf16[256,768]{1,0:T(8,128)(2,1)S(1)} %get-tuple-element., ...), custom_call_target="tpu_custom_call" | custom-call | flops 536870912 | bytes 4194304 | tf_op jit(solution)/shard_map/attend/pallas_call | solution.py:179
  52.4 2.9 %collective-permute-start.13 = (bf16[256,256]{1,0:T(8,128)(2,1)S(1)}, bf16[256,256]{1,0:T(8,128)(2,1)S(1)}, u32[]{:S(2)}, u32[]{:S(2)}) collective-permute-start(bf16[256,256]{1,0:T(8,128)(2,1)S(1)} %get-tuple-element.53), channel_id=1, source_target_pairs={{28,0},{24,4},{20,8},{16,12},{12,16},{8,20},{4,24},{0,28},{29,1},{... | collective-permute-start | bytes 393224 | tf_op jit(solution)/shard_map/ppermute | solution.py:472
  55.5 2.9 %collective-permute-start.9 = (f32[1,2048]{1,0:T(1,128)S(1)}, f32[1,2048]{1,0:T(1,128)S(1)}, u32[]{:S(2)}, u32[]{:S(2)}) collective-permute-start(f32[1,2048]{1,0:T(1,128)S(1)} %add.6.refs_8_), channel_id=1, source_target_pairs={{0,2},{1,3},{2,0},{3,1},{4,6},{5,7},{6,4},{7,5},{8,10},{9,11},{10,... | collective-permute-start | bytes 24584 | tf_op jit(solution)/shard_map/ppermute | solution.py:461
  58.4 1.3 %collective-permute-start.16 = (bf16[256,256]{1,0:T(8,128)(2,1)S(1)}, bf16[256,256]{1,0:T(8,128)(2,1)S(1)}, u32[]{:S(2)}, u32[]{:S(2)}) collective-permute-start(bf16[256,256]{1,0:T(8,128)(2,1)S(1)} %get-tuple-element.57), channel_id=1, source_target_pairs={{20,0},{8,4},{28,8},{0,12},{4,16},{24,20},{12,24},{16,28},{21,1},{... | collective-permute-start | bytes 393224 | tf_op jit(solution)/shard_map/ppermute | solution.py:472
  60.1 1.8 %collective-permute-start.17 = (bf16[256,256]{1,0:T(8,128)(2,1)S(1)}, bf16[256,256]{1,0:T(8,128)(2,1)S(1)}, u32[]{:S(2)}, u32[]{:S(2)}) collective-permute-start(bf16[256,256]{1,0:T(8,128)(2,1)S(1)} %get-tuple-element.58), channel_id=1, source_target_pairs={{16,0},{12,4},{24,8},{4,12},{0,16},{28,20},{8,24},{20,28},{17,1},{... | collective-permute-start | bytes 393224 | tf_op jit(solution)/shard_map/ppermute | solution.py:472
  62.3 1.4 %collective-permute-start.19 = (bf16[256,256]{1,0:T(8,128)(2,1)S(1)}, bf16[256,256]{1,0:T(8,128)(2,1)S(1)}, u32[]{:S(2)}, u32[]{:S(2)}) collective-permute-start(bf16[256,256]{1,0:T(8,128)(2,1)S(1)} %get-tuple-element.60), channel_id=1, source_target_pairs={{8,0},{20,4},{0,8},{28,12},{24,16},{4,20},{16,24},{12,28},{9,1},{2... | collective-permute-start | bytes 393224 | tf_op jit(solution)/shard_map/ppermute | solution.py:472
  63.7 1.3 %base.1.base_ref = f32[2048,256]{1,0:T(8,128)S(1)} custom-call(f32[1,256]{1,0:T(1,128)S(1)} %bitcast.2, f32[2048,256]{1,0:T(8,128)S(1)} %get-tuple-element.46.y_ref, bf16[2048,1024]{1,0:T(8,128)(2,1)S(1)} %get-tuple-element.47.onehot, f32[1,2048]{1,0:T(1,128)S(1)} %add.7.total_ref, bf16[256,256]{1,0:T(8,128)(2,1)S(1)} %collective-permute-done.13.rest_0_, ...), custom_call_target="tpu_custom_call" | custom-call | flops 1073741824 | bytes 4194304 | tf_op jit(solution)/shard_map/base/pallas_call | solution.py:411
  65.1 2.1 %collective-permute-done.18.rest_2_ = bf16[256,256]{1,0:T(8,128)(2,1)S(1)} collective-permute-done((bf16[256,256]{1,0:T(8,128)(2,1)S(1)}, bf16[256,256]{1,0:T(8,128)(2,1)S(1)}, u32[]{:S(2)}, u32[]{:S(2)}) %collective-permute-start.18) | collective-permute-done | bytes 131104 | tf_op jit(solution)/shard_map/ppermute | solution.py:472
  67.2 0.6 collective-permute-done.19.rest_3_
  67.8 2.1 %mix.1 = bf16[2048,256]{1,0:T(8,128)(2,1)} custom-call(f32[2048,256]{1,0:T(8,128)S(1)} %base.1.base_ref, bf16[2048,1024]{1,0:T(8,128)(2,1)S(1)} %get-tuple-element.44.rest_3_.onehot, bf16[256,256]{1,0:T(8,128)(2,1)S(1)} %collective-permute-done.16.rest_0_, bf16[256,256]{1,0:T(8,128)(2,1)S(1)} %collective-permute-done.17.rest_1_, ...), custom_call_target="tpu_custom_call" | custom-call | flops 1073741824 | bytes 4194304 | tf_op jit(solution)/shard_map/mix/pallas_call | solution.py:439
  (45 shorter events, 1.9 us)
Async XLA Ops:
  0.0 0.7 copy-start.8
  0.7 1.4 %copy-start.1 = (bf16[2048,256]{1,0:T(8,128)(2,1)S(1)}, bf16[2048,256]{1,0:T(8,128)(2,1)}, u32[]{:S(2)}) copy-start(bf16[2048,256]{1,0:T(8,128)(2,1)} %k_ref.7) | copy-start | bytes 3145732
  0.7 1.5 %copy-start.2 = (bf16[2048,256]{1,0:T(8,128)(2,1)S(1)}, bf16[2048,256]{1,0:T(8,128)(2,1)}, u32[]{:S(2)}) copy-start(bf16[2048,256]{1,0:T(8,128)(2,1)} %v_ref.7) | copy-start | bytes 3145732
  0.7 1.9 %copy-start.3 = (bf16[2048,256]{1,0:T(8,128)(2,1)S(1)}, bf16[2048,256]{1,0:T(8,128)(2,1)}, u32[]{:S(2)}) copy-start(bf16[2048,256]{1,0:T(8,128)(2,1)} %q_ref.7) | copy-start | bytes 3145732
  2.6 5.2 %copy-start.4 = (bf16[1,256,256]{2,1,0:T(8,128)(2,1)S(1)}, bf16[1,256,256]{2,1,0:T(8,128)(2,1)}, u32[]{:S(2)}) copy-start(bf16[1,256,256]{2,1,0:T(8,128)(2,1)} %one_ref.3) | copy-start | bytes 393220
  2.6 5.2 %copy-start.5 = (bf16[1,256,256]{2,1,0:T(8,128)(2,1)S(1)}, bf16[1,256,256]{2,1,0:T(8,128)(2,1)}, u32[]{:S(2)}) copy-start(bf16[1,256,256]{2,1,0:T(8,128)(2,1)} %three_ref.3) | copy-start | bytes 393220
  2.6 5.2 %copy-start.6 = (bf16[1,256,256]{2,1,0:T(8,128)(2,1)S(1)}, bf16[1,256,256]{2,1,0:T(8,128)(2,1)}, u32[]{:S(2)}) copy-start(bf16[1,256,256]{2,1,0:T(8,128)(2,1)} %two_ref.3) | copy-start | bytes 393220
  2.6 5.2 %copy-start.7 = (f32[2048,1]{0,1:T(1,128)S(1)}, f32[2048,1]{0,1:T(1,128)}, u32[]{:S(2)}) copy-start(f32[2048,1]{0,1:T(1,128)} %param.12) | copy-start | bytes 24580
  4.4 12.9 %collective-permute-start.1 = (bf16[256,768]{1,0:T(8,128)(2,1)S(1)}, bf16[256,768]{1,0:T(8,128)(2,1)S(1)}, u32[]{:S(2)}, u32[]{:S(2)}) collective-permute-start(bf16[256,768]{1,0:T(8,128)(2,1)S(1)} %get-tuple-element.37), channel_id=1, source_target_pairs={{0,28},{4,24},{8,20},{12,16},{16,12},{20,8},{24,4},{28,0},{1,29},{... | collective-permute-start | bytes 1179656 | tf_op jit(solution)/shard_map/ppermute | solution.py:467
  10.7 1.8 %collective-permute-start = (bf16[384,256]{1,0:T(8,128)(2,1)S(1)}, bf16[384,256]{1,0:T(8,128)(2,1)S(1)}, u32[]{:S(2)}, u32[]{:S(2)}) collective-permute-start(bf16[384,256]{1,0:T(8,128)(2,1)S(1)} %get-tuple-element.36), channel_id=1, source_target_pairs={{0,4},{4,0},{8,12},{12,8},{16,20},{20,16},{24,28},{28,24},{1,5},{5... | collective-permute-start | bytes 589832 | tf_op jit(solution)/shard_map/ppermute | solution.py:270
  11.4 23.1 %collective-permute-start.4 = (bf16[256,768]{1,0:T(8,128)(2,1)S(1)}, bf16[256,768]{1,0:T(8,128)(2,1)S(1)}, u32[]{:S(2)}, u32[]{:S(2)}) collective-permute-start(bf16[256,768]{1,0:T(8,128)(2,1)S(1)} %get-tuple-element.40), channel_id=1, source_target_pairs={{0,24},{4,28},{8,16},{12,20},{16,8},{20,12},{24,0},{28,4},{1,25},{... | collective-permute-start | bytes 1179656 | tf_op jit(solution)/shard_map/ppermute | solution.py:467
  17.4 13.6 %collective-permute-start.2 = (bf16[384,256]{1,0:T(8,128)(2,1)S(1)}, bf16[384,256]{1,0:T(8,128)(2,1)S(1)}, u32[]{:S(2)}, u32[]{:S(2)}) collective-permute-start(bf16[384,256]{1,0:T(8,128)(2,1)S(1)} %convert_element_type.6), channel_id=1, source_target_pairs={{0,8},{4,20},{8,0},{12,28},{16,24},{20,4},{24,16},{28,12},{1,9},{5... | collective-permute-start | bytes 589832 | tf_op jit(solution)/shard_map/ppermute | solution.py:282
  19.8 3.5 %copy-start.9 = (s32[1,2048]{1,0:T(1,128)S(1)}, s32[1,2048]{1,0:T(1,128)}, u32[]{:S(2)}) copy-start(s32[1,2048]{1,0:T(1,128)} %order_ref.3) | copy-start | bytes 24580
  21.6 13.0 %collective-permute-start.5 = (bf16[256,768]{1,0:T(8,128)(2,1)S(1)}, bf16[256,768]{1,0:T(8,128)(2,1)S(1)}, u32[]{:S(2)}, u32[]{:S(2)}) collective-permute-start(bf16[256,768]{1,0:T(8,128)(2,1)S(1)} %get-tuple-element.41), channel_id=1, source_target_pairs={{0,20},{4,8},{8,28},{12,0},{16,4},{20,24},{24,12},{28,16},{1,21},{... | collective-permute-start | bytes 1179656 | tf_op jit(solution)/shard_map/ppermute | solution.py:467
  21.7 20.6 %collective-permute-start.7 = (bf16[256,768]{1,0:T(8,128)(2,1)S(1)}, bf16[256,768]{1,0:T(8,128)(2,1)S(1)}, u32[]{:S(2)}, u32[]{:S(2)}) collective-permute-start(bf16[256,768]{1,0:T(8,128)(2,1)S(1)} %get-tuple-element.45), channel_id=1, source_target_pairs={{0,16},{4,12},{8,24},{12,4},{16,0},{20,28},{24,8},{28,20},{1,17},{... | collective-permute-start | bytes 1179656 | tf_op jit(solution)/shard_map/ppermute | solution.py:467
  31.0 7.5 %collective-permute-start.3 = (bf16[384,256]{1,0:T(8,128)(2,1)S(1)}, bf16[384,256]{1,0:T(8,128)(2,1)S(1)}, u32[]{:S(2)}, u32[]{:S(2)}) collective-permute-start(bf16[384,256]{1,0:T(8,128)(2,1)S(1)} %convert_element_type.7), channel_id=1, source_target_pairs={{0,16},{4,12},{8,24},{12,4},{16,0},{20,28},{24,8},{28,20},{1,17},{... | collective-permute-start | bytes 589832 | tf_op jit(solution)/shard_map/ppermute | solution.py:282
  38.6 3.8 %collective-permute-start.6 = (f32[384,256]{1,0:T(8,128)S(1)}, f32[384,256]{1,0:T(8,128)S(1)}, u32[]{:S(2)}, u32[]{:S(2)}) collective-permute-start(f32[384,256]{1,0:T(8,128)S(1)} %merge.5.rest_0_), channel_id=1, source_target_pairs={{0,4},{4,0},{8,12},{12,8},{16,20},{20,16},{24,28},{28,24},{1,5},{5... | collective-permute-start | bytes 1179656 | tf_op jit(solution)/shard_map/ppermute | solution.py:287
  39.3 9.4 %collective-permute-start.10 = (bf16[256,768]{1,0:T(8,128)(2,1)S(1)}, bf16[256,768]{1,0:T(8,128)(2,1)S(1)}, u32[]{:S(2)}, u32[]{:S(2)}) collective-permute-start(bf16[256,768]{1,0:T(8,128)(2,1)S(1)} %get-tuple-element.50), channel_id=1, source_target_pairs={{0,4},{4,0},{8,12},{12,8},{16,20},{20,16},{24,28},{28,24},{1,5},{5... | collective-permute-start | bytes 1179656 | tf_op jit(solution)/shard_map/ppermute | solution.py:467
  39.4 9.3 %collective-permute-start.11 = (bf16[256,768]{1,0:T(8,128)(2,1)S(1)}, bf16[256,768]{1,0:T(8,128)(2,1)S(1)}, u32[]{:S(2)}, u32[]{:S(2)}) collective-permute-start(bf16[256,768]{1,0:T(8,128)(2,1)S(1)} %get-tuple-element.51), channel_id=1, source_target_pairs={{0,8},{4,20},{8,0},{12,28},{16,24},{20,4},{24,16},{28,12},{1,9},{5... | collective-permute-start | bytes 1179656 | tf_op jit(solution)/shard_map/ppermute | solution.py:467
  41.4 9.5 %collective-permute-start.12 = (bf16[256,768]{1,0:T(8,128)(2,1)S(1)}, bf16[256,768]{1,0:T(8,128)(2,1)S(1)}, u32[]{:S(2)}, u32[]{:S(2)}) collective-permute-start(bf16[256,768]{1,0:T(8,128)(2,1)S(1)} %get-tuple-element.52), channel_id=1, source_target_pairs={{0,12},{4,16},{8,4},{12,24},{16,28},{20,0},{24,20},{28,8},{1,13},{... | collective-permute-start | bytes 1179656 | tf_op jit(solution)/shard_map/ppermute | solution.py:467
  45.0 18.7 %copy-start = (f32[256]{0:T(256)S(1)}, f32[256]{0:T(256)}, u32[]{:S(2)}) copy-start(f32[256]{0:T(256)} %param.16) | copy-start | bytes 3076
  45.0 3.7 %collective-permute-start.8 = (f32[1,2048]{1,0:T(1,128)S(1)}, f32[1,2048]{1,0:T(1,128)S(1)}, u32[]{:S(2)}, u32[]{:S(2)}) collective-permute-start(f32[1,2048]{1,0:T(1,128)S(1)} %get-tuple-element.48), channel_id=1, source_target_pairs={{0,1},{1,0},{2,3},{3,2},{4,5},{5,4},{6,7},{7,6},{8,9},{9,8},{10,11... | collective-permute-start | bytes 24584 | tf_op jit(solution)/shard_map/ppermute | solution.py:461
  52.4 9.5 %collective-permute-start.13 = (bf16[256,256]{1,0:T(8,128)(2,1)S(1)}, bf16[256,256]{1,0:T(8,128)(2,1)S(1)}, u32[]{:S(2)}, u32[]{:S(2)}) collective-permute-start(bf16[256,256]{1,0:T(8,128)(2,1)S(1)} %get-tuple-element.53), channel_id=1, source_target_pairs={{28,0},{24,4},{20,8},{16,12},{12,16},{8,20},{4,24},{0,28},{29,1},{... | collective-permute-start | bytes 393224 | tf_op jit(solution)/shard_map/ppermute | solution.py:472
  55.4 6.9 %collective-permute-start.14 = (bf16[256,256]{1,0:T(8,128)(2,1)S(1)}, bf16[256,256]{1,0:T(8,128)(2,1)S(1)}, u32[]{:S(2)}, u32[]{:S(2)}) collective-permute-start(bf16[256,256]{1,0:T(8,128)(2,1)S(1)} %get-tuple-element.54), channel_id=1, source_target_pairs={{24,0},{28,4},{16,8},{20,12},{8,16},{12,20},{0,24},{4,28},{25,1},{... | collective-permute-start | bytes 393224 | tf_op jit(solution)/shard_map/ppermute | solution.py:472
  55.4 8.3 %collective-permute-start.15 = (bf16[256,256]{1,0:T(8,128)(2,1)S(1)}, bf16[256,256]{1,0:T(8,128)(2,1)S(1)}, u32[]{:S(2)}, u32[]{:S(2)}) collective-permute-start(bf16[256,256]{1,0:T(8,128)(2,1)S(1)} %get-tuple-element.55), channel_id=1, source_target_pairs={{4,0},{0,4},{12,8},{8,12},{20,16},{16,20},{28,24},{24,28},{5,1},{1... | collective-permute-start | bytes 393224 | tf_op jit(solution)/shard_map/ppermute | solution.py:472
  55.5 4.5 %collective-permute-start.9 = (f32[1,2048]{1,0:T(1,128)S(1)}, f32[1,2048]{1,0:T(1,128)S(1)}, u32[]{:S(2)}, u32[]{:S(2)}) collective-permute-start(f32[1,2048]{1,0:T(1,128)S(1)} %add.6.refs_8_), channel_id=1, source_target_pairs={{0,2},{1,3},{2,0},{3,1},{4,6},{5,7},{6,4},{7,5},{8,10},{9,11},{10,... | collective-permute-start | bytes 24584 | tf_op jit(solution)/shard_map/ppermute | solution.py:461
  58.4 6.6 %collective-permute-start.16 = (bf16[256,256]{1,0:T(8,128)(2,1)S(1)}, bf16[256,256]{1,0:T(8,128)(2,1)S(1)}, u32[]{:S(2)}, u32[]{:S(2)}) collective-permute-start(bf16[256,256]{1,0:T(8,128)(2,1)S(1)} %get-tuple-element.57), channel_id=1, source_target_pairs={{20,0},{8,4},{28,8},{0,12},{4,16},{24,20},{12,24},{16,28},{21,1},{... | collective-permute-start | bytes 393224 | tf_op jit(solution)/shard_map/ppermute | solution.py:472
  60.1 5.0 %collective-permute-start.17 = (bf16[256,256]{1,0:T(8,128)(2,1)S(1)}, bf16[256,256]{1,0:T(8,128)(2,1)S(1)}, u32[]{:S(2)}, u32[]{:S(2)}) collective-permute-start(bf16[256,256]{1,0:T(8,128)(2,1)S(1)} %get-tuple-element.58), channel_id=1, source_target_pairs={{16,0},{12,4},{24,8},{4,12},{0,16},{28,20},{8,24},{20,28},{17,1},{... | collective-permute-start | bytes 393224 | tf_op jit(solution)/shard_map/ppermute | solution.py:472
  61.9 5.3 %collective-permute-start.18 = (bf16[256,256]{1,0:T(8,128)(2,1)S(1)}, bf16[256,256]{1,0:T(8,128)(2,1)S(1)}, u32[]{:S(2)}, u32[]{:S(2)}) collective-permute-start(bf16[256,256]{1,0:T(8,128)(2,1)S(1)} %get-tuple-element.59), channel_id=1, source_target_pairs={{12,0},{16,4},{4,8},{24,12},{28,16},{0,20},{20,24},{8,28},{13,1},{... | collective-permute-start | bytes 393224 | tf_op jit(solution)/shard_map/ppermute | solution.py:472
  62.3 5.5 %collective-permute-start.19 = (bf16[256,256]{1,0:T(8,128)(2,1)S(1)}, bf16[256,256]{1,0:T(8,128)(2,1)S(1)}, u32[]{:S(2)}, u32[]{:S(2)}) collective-permute-start(bf16[256,256]{1,0:T(8,128)(2,1)S(1)} %get-tuple-element.60), channel_id=1, source_target_pairs={{8,0},{20,4},{0,8},{28,12},{24,16},{4,20},{16,24},{12,28},{9,1},{2... | collective-permute-start | bytes 393224 | tf_op jit(solution)/shard_map/ppermute | solution.py:472

commit v14 on v10

--- a/solution.py
+++ b/solution.py
@@ -357,22 +357,23 @@
         inside = jnp.logical_and(at >= which * rows, at < (which + 1) * rows)
         slots = jnp.where(inside, peer(me, step, n) * rows + at - which * rows, slots)
     slots = slots[0:1, :].astype(F32)
-    each = outs[0].shape[1]
+    split = outs[0].shape[1]
     for low in range(0, count, LANES):
         wanted = column(order_ref[:, low : low + LANES].astype(F32))
         for lane in range(0, size, LANES):
             hit = wanted == slots[:, lane : lane + LANES]
-            out = outs[lane // each]
-            start = lane % each
+            out = outs[0] if lane < split else outs[1]
+            start = lane if lane < split else lane - split
             out[low : low + LANES, start : start + LANES] = hit.astype(F32).astype(BF16)
 
 
-def place(order, n, steps):
+def place(order, n, early, late):
     count = order.shape[1]
-    shape = jax.ShapeDtypeStruct((count, count // 2), BF16)
-    return pl.pallas_call(
-        functools.partial(place_kernel, n, tuple(steps)),
-        out_shape=[shape, shape],
+    rows = count // n
+    shapes = [jax.ShapeDtypeStruct((count, len(each) * rows), BF16) for each in (early, late)]
+    return pl.pallas_call(
+        functools.partial(place_kernel, n, (*early, *late)),
+        out_shape=shapes,
         in_specs=full(1),
         out_specs=full(2),
         compiler_params=params(),
@@ -451,15 +452,22 @@
     )(given, onehot, *blocks)
 
 
-def sum_over_heads(square, heads):
-    if not power_of_two(heads):
-        return lax.psum(square, "head")
-    step = 1
-    while step < heads:
-        pairs = [(at, at ^ step) for at in range(heads)]
-        square = square + lax.ppermute(square, "head", pairs)
-        step *= 2
+def head_steps(heads):
+    return heads.bit_length() - 1 if power_of_two(heads) else 0
+
+
+def head_sum(square, heads, low, high):
+    if head_steps(heads) == 0:
+        return square if low else lax.psum(square, "head")
+    for step in range(low, high):
+        pairs = [(at, at ^ (1 << step)) for at in range(heads)]
+        got = lax.ppermute(square, "head", pairs)
+        square = square + got
     return square
+
+
+def held(array, after):
+    return merge(array, jnp.zeros_like(array), after)
 
 
 def exchange(block, step, n):
@@ -489,15 +497,18 @@
             arrived[step] = exchange(block, step, n)
     came = [arrived[step] for step in steps]
     parts = gradients(keys, values, rates.reshape(1, count), *weights, tokens[0], n)
-    early = steps[:few] + steps[n - few :]
-    late = steps[few : n - few]
-    early_places, late_places = place(order, n, early + late)
+    early = steps[: 2 * few] + steps[n - few :]
+    late = steps[2 * few : n - few]
+    early_places, late_places = place(order, n, early, late)
     mine = core_step(parts, [came[0]], n)
     summed = sum_over_chips(mine, len(parts) == 2, [tokens[1:2], came[1:3] + tokens[2:] + [late_places]], n)
     y, square = read_out(queries, *weights, summed, came[3:4])
-    total = sum_over_heads(square, heads)
-    attended = attend([arrived[step] for step in range(n)], [total], n, width)
+    half = head_steps(heads) // 2
+    square = head_sum(square, heads, 0, half)
+    attended = attend([arrived[step] for step in range(n)], [square], n, width)
     returned = {step: give_back(attended[step], step, n) for step in early + late}
+    square = held(square, [returned[steps[0]]])
+    total = head_sum(square, heads, half, head_steps(heads))
     given = base(
         gain.reshape(1, width), y, early_places, total, heads, [returned[step] for step in early]
     )

time: 71.2 us -> 71.2 us (level)
  waiting for transfers between devices: 26.9 us -> 23.5 us
  starting transfers between devices: 21.8 us -> 25.1 us
    ppermute x7, waiting for transfers between devices: 7.08 us -> 2.12 us  [give_back(): return lax.ppermute(block, 'cam', pairs) if step else block]
    ppermute x7, starting transfers between devices: 5.43 us -> 8.41 us  [give_back(): return lax.ppermute(block, 'cam', pairs) if step else block]
    ppermute x7, waiting for transfers between devices: 4.77 us -> 6.46 us  [exchange(): return lax.ppermute(block, 'cam', routes(step, n)) if step else block]
  transfers between devices with their start and end apart: 20 -> 20, of which waited for: 12 -> 10; matrix products, arithmetic and copies ran while one was open for 0% -> 0% of each run, Pallas kernels for 20% -> 20%
where the time goes in v14:
time: 71.2 us; the launch traced here: 71 us
  starting transfers between devices  25.1 us (35%)
  waiting for transfers between devices  23.5 us (33%)
  Pallas kernels  20.8 us (29%)
  local copies, waits for them, and re-layouts  1.17 us (2%)
    ppermute x2, waiting for transfers between devices, sum_over_chips(): got = lax.ppermute(mine.astype(BF16), 'cam', pairs)  9.92 us
    ppermute x7, starting transfers between devices, give_back(): return lax.ppermute(block, 'cam', pairs) if step else block  8.41 us
    ppermute x7, starting transfers between devices, exchange(): return lax.ppermute(block, 'cam', routes(step, n)) if step else block  8.33 us
    pallas_call x3, Pallas kernels, sort_tokens(): pl.pallas_call(functools.partial(sort_kernel, size), out_shape=[jax.Shape...  7.05 us
    ppermute x7, waiting for transfers between devices, exchange(): return lax.ppermute(block, 'cam', routes(step, n)) if step else block  6.46 us
    ppermute x2, starting transfers between devices, head_sum(): got = lax.ppermute(square, 'head', pairs)  4.33 us
    ppermute x2, waiting for transfers between devices, head_sum(): got = lax.ppermute(square, 'head', pairs)  3.97 us
    pallas_call x1, Pallas kernels, gradients(): pl.pallas_call(functools.partial(grads_kernel, n, split), out_shape=[jax....  2.92 us
  transfers between devices with their start and end apart: 20, of which 10 were waited for; matrix products, arithmetic and copies ran while one was open for 0% of the time, Pallas kernels for 20%

profile of v14, /device:TPU:0, one launch (start us, length us, event | category | flops | bytes accessed | tf_op | source)
XLA Modules:
  0.0 71.0 jit_solution(13695385852104775483)
XLA Ops:
  0.7 1.4 %mark.1 = (bf16[512,2048]{1,0:T(8,128)(2,1)S(1)}, bf16[512,2048]{1,0:T(8,128)(2,1)S(1)}, bf16[1024,2048]{1,0:T(8,128)(2,1)S(1)}, f32[8,128]{1,0:T(8,128)}) custom-call(s32[1,2048]{1,0:T(1,128)S(1)} %copy-done.8), custom_call_target="tpu_custom_call" | custom-call | flops 999999995904 | bytes 1024 | tf_op jit(solution)/shard_map/mark/pallas_call | solution.py:107
  2.6 1.8 %sort_tokens.3 = (bf16[256,768]{1,0:T(8,128)(2,1)S(1)}, bf16[256,768]{1,0:T(8,128)(2,1)S(1)}, f32[8,128]{1,0:T(8,128)S(1)}) custom-call(bf16[512,2048]{1,0:T(8,128)(2,1)S(1)} %get-tuple-element.33.onehot, bf16[2048,256]{1,0:T(8,128)(2,1)S(1)} %copy-done.3, bf16[2048,256]{1,0:T(8,128)(2,1)S(1)} %copy-done.1, bf16[2048,256]{1,0:T(8,128)(2,1)S(1)} %copy-done.2), custom_call_target="tpu_custom_call" | custom-call | flops 1610612736 | bytes 3145728 | tf_op jit(solution)/shard_map/sort_tokens/pallas_call | solution.py:140
  4.4 3.4 %collective-permute-start.1 = (bf16[256,768]{1,0:T(8,128)(2,1)S(1)}, bf16[256,768]{1,0:T(8,128)(2,1)S(1)}, u32[]{:S(2)}, u32[]{:S(2)}) collective-permute-start(bf16[256,768]{1,0:T(8,128)(2,1)S(1)} %get-tuple-element.37), channel_id=1, source_target_pairs={{0,28},{4,24},{8,20},{12,16},{16,12},{20,8},{24,4},{28,0},{1,29},{... | collective-permute-start | bytes 1179656 | tf_op jit(solution)/shard_map/ppermute | solution.py:474
  7.8 2.9 %gradients.1 = (f32[384,256]{1,0:T(8,128)S(1)}, bf16[384,256]{1,0:T(8,128)(2,1)S(1)}) custom-call(bf16[2048,256]{1,0:T(8,128)(2,1)S(1)} %copy-done.1, bf16[2048,256]{1,0:T(8,128)(2,1)S(1)} %copy-done.2, f32[1,2048]{1,0:T(1,128)S(1)} %bitcast.3, bf16[1,256,256]{2,1,0:T(8,128)(2,1)S(1)} %copy-done.4, bf16[1,256,256]{2,1,0:T(8,128)(2,1)S(1)} %copy-done.5, ...), custom_call_target="tpu_custom_call" | custom-call | flops 1610612736 | bytes 4194304 | tf_op jit(solution)/shard_map/gradients/pallas_call | solution.py:236
  10.7 0.7 %collective-permute-start = (bf16[384,256]{1,0:T(8,128)(2,1)S(1)}, bf16[384,256]{1,0:T(8,128)(2,1)S(1)}, u32[]{:S(2)}, u32[]{:S(2)}) collective-permute-start(bf16[384,256]{1,0:T(8,128)(2,1)S(1)} %get-tuple-element.36), channel_id=1, source_target_pairs={{0,4},{4,0},{8,12},{12,8},{16,20},{20,16},{24,28},{28,24},{1,5},{5... | collective-permute-start | bytes 589832 | tf_op jit(solution)/shard_map/ppermute | solution.py:270
  11.5 1.1 %collective-permute-done.got_ref = bf16[384,256]{1,0:T(8,128)(2,1)S(1)} collective-permute-done((bf16[384,256]{1,0:T(8,128)(2,1)S(1)}, bf16[384,256]{1,0:T(8,128)(2,1)S(1)}, u32[]{:S(2)}, u32[]{:S(2)}) %collective-permute-start) | collective-permute-done | bytes 196640 | tf_op jit(solution)/shard_map/ppermute | solution.py:270
  12.5 4.8 %collective-permute-done.1.rest_0_.refs_7_ = bf16[256,768]{1,0:T(8,128)(2,1)S(1)} collective-permute-done((bf16[256,768]{1,0:T(8,128)(2,1)S(1)}, bf16[256,768]{1,0:T(8,128)(2,1)S(1)}, u32[]{:S(2)}, u32[]{:S(2)}) %collective-permute-start.1) | collective-permute-done | bytes 393248 | tf_op jit(solution)/shard_map/ppermute | solution.py:474
  17.4 2.5 %collective-permute-start.2 = (bf16[384,256]{1,0:T(8,128)(2,1)S(1)}, bf16[384,256]{1,0:T(8,128)(2,1)S(1)}, u32[]{:S(2)}, u32[]{:S(2)}) collective-permute-start(bf16[384,256]{1,0:T(8,128)(2,1)S(1)} %convert_element_type.6), channel_id=1, source_target_pairs={{0,8},{4,20},{8,0},{12,28},{16,24},{20,4},{24,16},{28,12},{1,9},{5... | collective-permute-start | bytes 589832 | tf_op jit(solution)/shard_map/ppermute | solution.py:282
  19.8 1.8 %sort_tokens.4 = (bf16[256,768]{1,0:T(8,128)(2,1)S(1)}, bf16[256,768]{1,0:T(8,128)(2,1)S(1)}, f32[8,128]{1,0:T(8,128)S(1)}) custom-call(bf16[512,2048]{1,0:T(8,128)(2,1)S(1)} %get-tuple-element.38.onehot, bf16[2048,256]{1,0:T(8,128)(2,1)S(1)} %copy-done.3, bf16[2048,256]{1,0:T(8,128)(2,1)S(1)} %copy-done.1, bf16[2048,256]{1,0:T(8,128)(2,1)S(1)} %copy-done.2), custom_call_target="tpu_custom_call" | custom-call | flops 1610612736 | bytes 3145728 | tf_op jit(solution)/shard_map/sort_tokens/pallas_call | solution.py:140
  21.7 1.6 %collective-permute-start.7 = (bf16[256,768]{1,0:T(8,128)(2,1)S(1)}, bf16[256,768]{1,0:T(8,128)(2,1)S(1)}, u32[]{:S(2)}, u32[]{:S(2)}) collective-permute-start(bf16[256,768]{1,0:T(8,128)(2,1)S(1)} %get-tuple-element.45), channel_id=1, source_target_pairs={{0,16},{4,12},{8,24},{12,4},{16,0},{20,28},{24,8},{28,20},{1,17},{... | collective-permute-start | bytes 1179656 | tf_op jit(solution)/shard_map/ppermute | solution.py:474
  23.3 1.7 %place.1 = (bf16[2048,1536]{1,0:T(8,128)(2,1)S(1)}, bf16[2048,512]{1,0:T(8,128)(2,1)S(1)}) custom-call(s32[1,2048]{1,0:T(1,128)S(1)} %copy-done.9), custom_call_target="tpu_custom_call" | custom-call | flops 4194304 | bytes 8388608 | tf_op jit(solution)/shard_map/place/pallas_call | solution.py:374
  25.0 6.0 %collective-permute-done.2.got_ref = bf16[384,256]{1,0:T(8,128)(2,1)S(1)} collective-permute-done((bf16[384,256]{1,0:T(8,128)(2,1)S(1)}, bf16[384,256]{1,0:T(8,128)(2,1)S(1)}, u32[]{:S(2)}, u32[]{:S(2)}) %collective-permute-start.2) | collective-permute-done | bytes 196640 | tf_op jit(solution)/shard_map/ppermute | solution.py:282
  31.1 3.4 %sort_tokens.5 = (bf16[256,768]{1,0:T(8,128)(2,1)S(1)}, bf16[256,768]{1,0:T(8,128)(2,1)S(1)}, bf16[256,768]{1,0:T(8,128)(2,1)S(1)}, bf16[256,768]{1,0:T(8,128)(2,1)S(1)}, f32[8,128]{1,0:T(8,128)S(1)}) custom-call(bf16[1024,2048]{1,0:T(8,128)(2,1)S(1)} %get-tuple-element.42.onehot, bf16[2048,256]{1,0:T(8,128)(2,1)S(1)} %copy-done.3, ...), custom_call_target="tpu_custom_call" | custom-call | flops 3221225472 | bytes 3145728 | tf_op jit(solution)/shard_map/sort_tokens/pallas_call | solution.py:140
  34.6 4.0 %collective-permute-done.3.got_ref = bf16[384,256]{1,0:T(8,128)(2,1)S(1)} collective-permute-done((bf16[384,256]{1,0:T(8,128)(2,1)S(1)}, bf16[384,256]{1,0:T(8,128)(2,1)S(1)}, u32[]{:S(2)}, u32[]{:S(2)}) %collective-permute-start.3) | collective-permute-done | bytes 196640 | tf_op jit(solution)/shard_map/ppermute | solution.py:282
  38.6 0.7 %collective-permute-start.6 = (f32[384,256]{1,0:T(8,128)S(1)}, f32[384,256]{1,0:T(8,128)S(1)}, u32[]{:S(2)}, u32[]{:S(2)}) collective-permute-start(f32[384,256]{1,0:T(8,128)S(1)} %merge.6.rest_0_), channel_id=1, source_target_pairs={{0,4},{4,0},{8,12},{12,8},{16,20},{20,16},{24,28},{28,24},{1,5},{5... | collective-permute-start | bytes 1179656 | tf_op jit(solution)/shard_map/ppermute | solution.py:287
  39.3 1.7 %collective-permute-start.10 = (bf16[256,768]{1,0:T(8,128)(2,1)S(1)}, bf16[256,768]{1,0:T(8,128)(2,1)S(1)}, u32[]{:S(2)}, u32[]{:S(2)}) collective-permute-start(bf16[256,768]{1,0:T(8,128)(2,1)S(1)} %get-tuple-element.51), channel_id=1, source_target_pairs={{0,8},{4,20},{8,0},{12,28},{16,24},{20,4},{24,16},{28,12},{1,9},{5... | collective-permute-start | bytes 1179656 | tf_op jit(solution)/shard_map/ppermute | solution.py:474
  41.0 1.2 %collective-permute-start.11 = (bf16[256,768]{1,0:T(8,128)(2,1)S(1)}, bf16[256,768]{1,0:T(8,128)(2,1)S(1)}, u32[]{:S(2)}, u32[]{:S(2)}) collective-permute-start(bf16[256,768]{1,0:T(8,128)(2,1)S(1)} %get-tuple-element.52), channel_id=1, source_target_pairs={{0,12},{4,16},{8,4},{12,24},{16,28},{20,0},{24,20},{28,8},{1,13},{... | collective-permute-start | bytes 1179656 | tf_op jit(solution)/shard_map/ppermute | solution.py:474
  42.6 2.7 %read_out.1 = (f32[2048,256]{1,0:T(8,128)S(1)}, f32[1,2048]{1,0:T(1,128)S(1)}) custom-call(bf16[2048,256]{1,0:T(8,128)(2,1)S(1)} %copy-done.3, bf16[1,256,256]{2,1,0:T(8,128)(2,1)S(1)} %copy-done.4, bf16[1,256,256]{2,1,0:T(8,128)(2,1)S(1)} %copy-done.5, bf16[1,256,256]{2,1,0:T(8,128)(2,1)S(1)} %copy-done.6, f32[384,256]{1,0:T(8,128)S(1)} %merge.6.rest_0_, ...), custom_call_target="tpu_custom_call" | custom-call | flops 805306368 | bytes 4194304 | tf_op jit(solution)/shard_map/read_out/pallas_call | solution.py:334
  45.3 1.6 %collective-permute-start.8 = (f32[1,2048]{1,0:T(1,128)S(1)}, f32[1,2048]{1,0:T(1,128)S(1)}, u32[]{:S(2)}, u32[]{:S(2)}) collective-permute-start(f32[1,2048]{1,0:T(1,128)S(1)} %get-tuple-element.48), channel_id=1, source_target_pairs={{0,1},{1,0},{2,3},{3,2},{4,5},{5,4},{6,7},{7,6},{8,9},{9,8},{10,11... | collective-permute-start | bytes 24584 | tf_op jit(solution)/shard_map/ppermute | solution.py:464
  46.9 2.1 %collective-permute-done.8 = f32[1,2048]{1,0:T(1,128)S(1)} collective-permute-done((f32[1,2048]{1,0:T(1,128)S(1)}, f32[1,2048]{1,0:T(1,128)S(1)}, u32[]{:S(2)}, u32[]{:S(2)}) %collective-permute-start.8) | collective-permute-done | bytes 8224 | tf_op jit(solution)/shard_map/ppermute | solution.py:464
  49.0 1.7 %collective-permute-done.11.refs_3_ = bf16[256,768]{1,0:T(8,128)(2,1)S(1)} collective-permute-done((bf16[256,768]{1,0:T(8,128)(2,1)S(1)}, bf16[256,768]{1,0:T(8,128)(2,1)S(1)}, u32[]{:S(2)}, u32[]{:S(2)}) %collective-permute-start.11) | collective-permute-done | bytes 393248 | tf_op jit(solution)/shard_map/ppermute | solution.py:474
  50.7 1.5 %attend.1 = (bf16[256,256]{1,0:T(8,128)(2,1)S(1)}, bf16[256,256]{1,0:T(8,128)(2,1)S(1)}, bf16[256,256]{1,0:T(8,128)(2,1)S(1)}, bf16[256,256]{1,0:T(8,128)(2,1)S(...) custom-call(bf16[256,768]{1,0:T(8,128)(2,1)S(1)} %get-tuple-element., ...), custom_call_target="tpu_custom_call" | custom-call | flops 536870912 | bytes 4194304 | tf_op jit(solution)/shard_map/attend/pallas_call | solution.py:179
  52.2 2.7 %collective-permute-start.12 = (bf16[256,256]{1,0:T(8,128)(2,1)S(1)}, bf16[256,256]{1,0:T(8,128)(2,1)S(1)}, u32[]{:S(2)}, u32[]{:S(2)}) collective-permute-start(bf16[256,256]{1,0:T(8,128)(2,1)S(1)} %get-tuple-element.53), channel_id=1, source_target_pairs={{28,0},{24,4},{20,8},{16,12},{12,16},{8,20},{4,24},{0,28},{29,1},{... | collective-permute-start | bytes 393224 | tf_op jit(solution)/shard_map/ppermute | solution.py:479
  55.3 1.1 %collective-permute-start.15 = (bf16[256,256]{1,0:T(8,128)(2,1)S(1)}, bf16[256,256]{1,0:T(8,128)(2,1)S(1)}, u32[]{:S(2)}, u32[]{:S(2)}) collective-permute-start(bf16[256,256]{1,0:T(8,128)(2,1)S(1)} %get-tuple-element.55), channel_id=1, source_target_pairs={{20,0},{8,4},{28,8},{0,12},{4,16},{24,20},{12,24},{16,28},{21,1},{... | collective-permute-start | bytes 393224 | tf_op jit(solution)/shard_map/ppermute | solution.py:479
  56.4 1.5 %collective-permute-start.16 = (bf16[256,256]{1,0:T(8,128)(2,1)S(1)}, bf16[256,256]{1,0:T(8,128)(2,1)S(1)}, u32[]{:S(2)}, u32[]{:S(2)}) collective-permute-start(bf16[256,256]{1,0:T(8,128)(2,1)S(1)} %get-tuple-element.56), channel_id=1, source_target_pairs={{16,0},{12,4},{24,8},{4,12},{0,16},{28,20},{8,24},{20,28},{17,1},{... | collective-permute-start | bytes 393224 | tf_op jit(solution)/shard_map/ppermute | solution.py:479
  58.8 2.7 %collective-permute-start.13 = (f32[1,2048]{1,0:T(1,128)S(1)}, f32[1,2048]{1,0:T(1,128)S(1)}, u32[]{:S(2)}, u32[]{:S(2)}) collective-permute-start(f32[1,2048]{1,0:T(1,128)S(1)} %merge.7), channel_id=1, source_target_pairs={{0,2},{1,3},{2,0},{3,1},{4,6},{5,7},{6,4},{7,5},{8,10},{9,11},{10,... | collective-permute-start | bytes 24584 | tf_op jit(solution)/shard_map/ppermute | solution.py:464
  61.5 1.9 %collective-permute-done.13 = f32[1,2048]{1,0:T(1,128)S(1)} collective-permute-done((f32[1,2048]{1,0:T(1,128)S(1)}, f32[1,2048]{1,0:T(1,128)S(1)}, u32[]{:S(2)}, u32[]{:S(2)}) %collective-permute-start.13) | collective-permute-done | bytes 8224 | tf_op jit(solution)/shard_map/ppermute | solution.py:464
  63.4 0.8 %collective-permute-start.18 = (bf16[256,256]{1,0:T(8,128)(2,1)S(1)}, bf16[256,256]{1,0:T(8,128)(2,1)S(1)}, u32[]{:S(2)}, u32[]{:S(2)}) collective-permute-start(bf16[256,256]{1,0:T(8,128)(2,1)S(1)} %get-tuple-element.59), channel_id=1, source_target_pairs={{12,0},{16,4},{4,8},{24,12},{28,16},{0,20},{20,24},{8,28},{13,1},{... | collective-permute-start | bytes 393224 | tf_op jit(solution)/shard_map/ppermute | solution.py:479
  64.2 1.6 %collective-permute-start.19 = (bf16[256,256]{1,0:T(8,128)(2,1)S(1)}, bf16[256,256]{1,0:T(8,128)(2,1)S(1)}, u32[]{:S(2)}, u32[]{:S(2)}) collective-permute-start(bf16[256,256]{1,0:T(8,128)(2,1)S(1)} %get-tuple-element.60), channel_id=1, source_target_pairs={{8,0},{20,4},{0,8},{28,12},{24,16},{4,20},{16,24},{12,28},{9,1},{2... | collective-permute-start | bytes 393224 | tf_op jit(solution)/shard_map/ppermute | solution.py:479
  65.8 1.8 %base.1.base_ref = f32[2048,256]{1,0:T(8,128)S(1)} custom-call(f32[1,256]{1,0:T(1,128)S(1)} %bitcast.2, f32[2048,256]{1,0:T(8,128)S(1)} %get-tuple-element.46.y_ref, bf16[2048,1536]{1,0:T(8,128)(2,1)S(1)} %get-tuple-element.47.onehot, f32[1,2048]{1,0:T(1,128)S(1)} %add.7.total_ref, bf16[256,256]{1,0:T(8,128)(2,1)S(1)} %collective-permute-done.12.rest_0_, ...), custom_call_target="tpu_custom_call" | custom-call | flops 1610612736 | bytes 4194304 | tf_op jit(solution)/shard_map/base/pallas_call | solution.py:412
  67.8 1.5 %collective-permute-done.19.rest_1_ = bf16[256,256]{1,0:T(8,128)(2,1)S(1)} collective-permute-done((bf16[256,256]{1,0:T(8,128)(2,1)S(1)}, bf16[256,256]{1,0:T(8,128)(2,1)S(1)}, u32[]{:S(2)}, u32[]{:S(2)}) %collective-permute-start.19) | collective-permute-done | bytes 131104 | tf_op jit(solution)/shard_map/ppermute | solution.py:479
  69.3 1.6 %mix.1 = bf16[2048,256]{1,0:T(8,128)(2,1)} custom-call(f32[2048,256]{1,0:T(8,128)S(1)} %base.1.base_ref, bf16[2048,512]{1,0:T(8,128)(2,1)S(1)} %get-tuple-element.44.rest_3_.onehot, bf16[256,256]{1,0:T(8,128)(2,1)S(1)} %collective-permute-done.18.rest_0_, bf16[256,256]{1,0:T(8,128)(2,1)S(1)} %collective-permute-done.19.rest_1_), custom_call_target="tpu_custom_call" | custom-call | flops 536870912 | bytes 4194304 | tf_op jit(solution)/shard_map/mix/pallas_call | solution.py:440
  (47 shorter events, 3.2 us)
Async XLA Ops:
  0.0 0.7 copy-start.8
  0.7 1.4 %copy-start.1 = (bf16[2048,256]{1,0:T(8,128)(2,1)S(1)}, bf16[2048,256]{1,0:T(8,128)(2,1)}, u32[]{:S(2)}) copy-start(bf16[2048,256]{1,0:T(8,128)(2,1)} %k_ref.7) | copy-start | bytes 3145732
  0.7 1.5 %copy-start.2 = (bf16[2048,256]{1,0:T(8,128)(2,1)S(1)}, bf16[2048,256]{1,0:T(8,128)(2,1)}, u32[]{:S(2)}) copy-start(bf16[2048,256]{1,0:T(8,128)(2,1)} %v_ref.7) | copy-start | bytes 3145732
  0.7 1.9 %copy-start.3 = (bf16[2048,256]{1,0:T(8,128)(2,1)S(1)}, bf16[2048,256]{1,0:T(8,128)(2,1)}, u32[]{:S(2)}) copy-start(bf16[2048,256]{1,0:T(8,128)(2,1)} %q_ref.7) | copy-start | bytes 3145732
  2.6 5.2 %copy-start.4 = (bf16[1,256,256]{2,1,0:T(8,128)(2,1)S(1)}, bf16[1,256,256]{2,1,0:T(8,128)(2,1)}, u32[]{:S(2)}) copy-start(bf16[1,256,256]{2,1,0:T(8,128)(2,1)} %one_ref.3) | copy-start | bytes 393220
  2.6 5.2 %copy-start.5 = (bf16[1,256,256]{2,1,0:T(8,128)(2,1)S(1)}, bf16[1,256,256]{2,1,0:T(8,128)(2,1)}, u32[]{:S(2)}) copy-start(bf16[1,256,256]{2,1,0:T(8,128)(2,1)} %three_ref.3) | copy-start | bytes 393220
  2.6 5.2 %copy-start.6 = (bf16[1,256,256]{2,1,0:T(8,128)(2,1)S(1)}, bf16[1,256,256]{2,1,0:T(8,128)(2,1)}, u32[]{:S(2)}) copy-start(bf16[1,256,256]{2,1,0:T(8,128)(2,1)} %two_ref.3) | copy-start | bytes 393220
  2.6 5.2 %copy-start.7 = (f32[2048,1]{0,1:T(1,128)S(1)}, f32[2048,1]{0,1:T(1,128)}, u32[]{:S(2)}) copy-start(f32[2048,1]{0,1:T(1,128)} %param.12) | copy-start | bytes 24580
  4.4 12.9 %collective-permute-start.1 = (bf16[256,768]{1,0:T(8,128)(2,1)S(1)}, bf16[256,768]{1,0:T(8,128)(2,1)S(1)}, u32[]{:S(2)}, u32[]{:S(2)}) collective-permute-start(bf16[256,768]{1,0:T(8,128)(2,1)S(1)} %get-tuple-element.37), channel_id=1, source_target_pairs={{0,28},{4,24},{8,20},{12,16},{16,12},{20,8},{24,4},{28,0},{1,29},{... | collective-permute-start | bytes 1179656 | tf_op jit(solution)/shard_map/ppermute | solution.py:474
  10.7 1.8 %collective-permute-start = (bf16[384,256]{1,0:T(8,128)(2,1)S(1)}, bf16[384,256]{1,0:T(8,128)(2,1)S(1)}, u32[]{:S(2)}, u32[]{:S(2)}) collective-permute-start(bf16[384,256]{1,0:T(8,128)(2,1)S(1)} %get-tuple-element.36), channel_id=1, source_target_pairs={{0,4},{4,0},{8,12},{12,8},{16,20},{20,16},{24,28},{28,24},{1,5},{5... | collective-permute-start | bytes 589832 | tf_op jit(solution)/shard_map/ppermute | solution.py:270
  11.5 23.1 %collective-permute-start.4 = (bf16[256,768]{1,0:T(8,128)(2,1)S(1)}, bf16[256,768]{1,0:T(8,128)(2,1)S(1)}, u32[]{:S(2)}, u32[]{:S(2)}) collective-permute-start(bf16[256,768]{1,0:T(8,128)(2,1)S(1)} %get-tuple-element.40), channel_id=1, source_target_pairs={{0,24},{4,28},{8,16},{12,20},{16,8},{20,12},{24,0},{28,4},{1,25},{... | collective-permute-start | bytes 1179656 | tf_op jit(solution)/shard_map/ppermute | solution.py:474
  17.4 13.6 %collective-permute-start.2 = (bf16[384,256]{1,0:T(8,128)(2,1)S(1)}, bf16[384,256]{1,0:T(8,128)(2,1)S(1)}, u32[]{:S(2)}, u32[]{:S(2)}) collective-permute-start(bf16[384,256]{1,0:T(8,128)(2,1)S(1)} %convert_element_type.6), channel_id=1, source_target_pairs={{0,8},{4,20},{8,0},{12,28},{16,24},{20,4},{24,16},{28,12},{1,9},{5... | collective-permute-start | bytes 589832 | tf_op jit(solution)/shard_map/ppermute | solution.py:282
  19.8 3.5 %copy-start.9 = (s32[1,2048]{1,0:T(1,128)S(1)}, s32[1,2048]{1,0:T(1,128)}, u32[]{:S(2)}) copy-start(s32[1,2048]{1,0:T(1,128)} %order_ref.3) | copy-start | bytes 24580
  21.6 12.9 %collective-permute-start.5 = (bf16[256,768]{1,0:T(8,128)(2,1)S(1)}, bf16[256,768]{1,0:T(8,128)(2,1)S(1)}, u32[]{:S(2)}, u32[]{:S(2)}) collective-permute-start(bf16[256,768]{1,0:T(8,128)(2,1)S(1)} %get-tuple-element.41), channel_id=1, source_target_pairs={{0,20},{4,8},{8,28},{12,0},{16,4},{20,24},{24,12},{28,16},{1,21},{... | collective-permute-start | bytes 1179656 | tf_op jit(solution)/shard_map/ppermute | solution.py:474
  21.7 20.9 %collective-permute-start.7 = (bf16[256,768]{1,0:T(8,128)(2,1)S(1)}, bf16[256,768]{1,0:T(8,128)(2,1)S(1)}, u32[]{:S(2)}, u32[]{:S(2)}) collective-permute-start(bf16[256,768]{1,0:T(8,128)(2,1)S(1)} %get-tuple-element.45), channel_id=1, source_target_pairs={{0,16},{4,12},{8,24},{12,4},{16,0},{20,28},{24,8},{28,20},{1,17},{... | collective-permute-start | bytes 1179656 | tf_op jit(solution)/shard_map/ppermute | solution.py:474
  31.0 7.5 %collective-permute-start.3 = (bf16[384,256]{1,0:T(8,128)(2,1)S(1)}, bf16[384,256]{1,0:T(8,128)(2,1)S(1)}, u32[]{:S(2)}, u32[]{:S(2)}) collective-permute-start(bf16[384,256]{1,0:T(8,128)(2,1)S(1)} %convert_element_type.7), channel_id=1, source_target_pairs={{0,16},{4,12},{8,24},{12,4},{16,0},{20,28},{24,8},{28,20},{1,17},{... | collective-permute-start | bytes 589832 | tf_op jit(solution)/shard_map/ppermute | solution.py:282
  38.6 4.0 %collective-permute-start.6 = (f32[384,256]{1,0:T(8,128)S(1)}, f32[384,256]{1,0:T(8,128)S(1)}, u32[]{:S(2)}, u32[]{:S(2)}) collective-permute-start(f32[384,256]{1,0:T(8,128)S(1)} %merge.6.rest_0_), channel_id=1, source_target_pairs={{0,4},{4,0},{8,12},{12,8},{16,20},{20,16},{24,28},{28,24},{1,5},{5... | collective-permute-start | bytes 1179656 | tf_op jit(solution)/shard_map/ppermute | solution.py:287
  39.3 9.7 %collective-permute-start.10 = (bf16[256,768]{1,0:T(8,128)(2,1)S(1)}, bf16[256,768]{1,0:T(8,128)(2,1)S(1)}, u32[]{:S(2)}, u32[]{:S(2)}) collective-permute-start(bf16[256,768]{1,0:T(8,128)(2,1)S(1)} %get-tuple-element.51), channel_id=1, source_target_pairs={{0,8},{4,20},{8,0},{12,28},{16,24},{20,4},{24,16},{28,12},{1,9},{5... | collective-permute-start | bytes 1179656 | tf_op jit(solution)/shard_map/ppermute | solution.py:474
  41.0 9.7 %collective-permute-start.11 = (bf16[256,768]{1,0:T(8,128)(2,1)S(1)}, bf16[256,768]{1,0:T(8,128)(2,1)S(1)}, u32[]{:S(2)}, u32[]{:S(2)}) collective-permute-start(bf16[256,768]{1,0:T(8,128)(2,1)S(1)} %get-tuple-element.52), channel_id=1, source_target_pairs={{0,12},{4,16},{8,4},{12,24},{16,28},{20,0},{24,20},{28,8},{1,13},{... | collective-permute-start | bytes 1179656 | tf_op jit(solution)/shard_map/ppermute | solution.py:474
  42.2 8.5 %collective-permute-start.9 = (bf16[256,768]{1,0:T(8,128)(2,1)S(1)}, bf16[256,768]{1,0:T(8,128)(2,1)S(1)}, u32[]{:S(2)}, u32[]{:S(2)}) collective-permute-start(bf16[256,768]{1,0:T(8,128)(2,1)S(1)} %get-tuple-element.50), channel_id=1, source_target_pairs={{0,4},{4,0},{8,12},{12,8},{16,20},{20,16},{24,28},{28,24},{1,5},{5... | collective-permute-start | bytes 1179656 | tf_op jit(solution)/shard_map/ppermute | solution.py:474
  45.3 20.5 %copy-start = (f32[256]{0:T(256)S(1)}, f32[256]{0:T(256)}, u32[]{:S(2)}) copy-start(f32[256]{0:T(256)} %param.16) | copy-start | bytes 3076
  45.3 3.7 %collective-permute-start.8 = (f32[1,2048]{1,0:T(1,128)S(1)}, f32[1,2048]{1,0:T(1,128)S(1)}, u32[]{:S(2)}, u32[]{:S(2)}) collective-permute-start(f32[1,2048]{1,0:T(1,128)S(1)} %get-tuple-element.48), channel_id=1, source_target_pairs={{0,1},{1,0},{2,3},{3,2},{4,5},{5,4},{6,7},{7,6},{8,9},{9,8},{10,11... | collective-permute-start | bytes 24584 | tf_op jit(solution)/shard_map/ppermute | solution.py:464
  52.2 6.5 %collective-permute-start.12 = (bf16[256,256]{1,0:T(8,128)(2,1)S(1)}, bf16[256,256]{1,0:T(8,128)(2,1)S(1)}, u32[]{:S(2)}, u32[]{:S(2)}) collective-permute-start(bf16[256,256]{1,0:T(8,128)(2,1)S(1)} %get-tuple-element.53), channel_id=1, source_target_pairs={{28,0},{24,4},{20,8},{16,12},{12,16},{8,20},{4,24},{0,28},{29,1},{... | collective-permute-start | bytes 393224 | tf_op jit(solution)/shard_map/ppermute | solution.py:479
  54.9 9.3 %collective-permute-start.14 = (bf16[256,256]{1,0:T(8,128)(2,1)S(1)}, bf16[256,256]{1,0:T(8,128)(2,1)S(1)}, u32[]{:S(2)}, u32[]{:S(2)}) collective-permute-start(bf16[256,256]{1,0:T(8,128)(2,1)S(1)} %get-tuple-element.54), channel_id=1, source_target_pairs={{24,0},{28,4},{16,8},{20,12},{8,16},{12,20},{0,24},{4,28},{25,1},{... | collective-permute-start | bytes 393224 | tf_op jit(solution)/shard_map/ppermute | solution.py:479
  55.3 10.5 %collective-permute-start.15 = (bf16[256,256]{1,0:T(8,128)(2,1)S(1)}, bf16[256,256]{1,0:T(8,128)(2,1)S(1)}, u32[]{:S(2)}, u32[]{:S(2)}) collective-permute-start(bf16[256,256]{1,0:T(8,128)(2,1)S(1)} %get-tuple-element.55), channel_id=1, source_target_pairs={{20,0},{8,4},{28,8},{0,12},{4,16},{24,20},{12,24},{16,28},{21,1},{... | collective-permute-start | bytes 393224 | tf_op jit(solution)/shard_map/ppermute | solution.py:479
  56.4 9.4 %collective-permute-start.16 = (bf16[256,256]{1,0:T(8,128)(2,1)S(1)}, bf16[256,256]{1,0:T(8,128)(2,1)S(1)}, u32[]{:S(2)}, u32[]{:S(2)}) collective-permute-start(bf16[256,256]{1,0:T(8,128)(2,1)S(1)} %get-tuple-element.56), channel_id=1, source_target_pairs={{16,0},{12,4},{24,8},{4,12},{0,16},{28,20},{8,24},{20,28},{17,1},{... | collective-permute-start | bytes 393224 | tf_op jit(solution)/shard_map/ppermute | solution.py:479
  57.9 7.9 %collective-permute-start.17 = (bf16[256,256]{1,0:T(8,128)(2,1)S(1)}, bf16[256,256]{1,0:T(8,128)(2,1)S(1)}, u32[]{:S(2)}, u32[]{:S(2)}) collective-permute-start(bf16[256,256]{1,0:T(8,128)(2,1)S(1)} %get-tuple-element.57), channel_id=1, source_target_pairs={{4,0},{0,4},{12,8},{8,12},{20,16},{16,20},{28,24},{24,28},{5,1},{1... | collective-permute-start | bytes 393224 | tf_op jit(solution)/shard_map/ppermute | solution.py:479
  58.8 4.6 %collective-permute-start.13 = (f32[1,2048]{1,0:T(1,128)S(1)}, f32[1,2048]{1,0:T(1,128)S(1)}, u32[]{:S(2)}, u32[]{:S(2)}) collective-permute-start(f32[1,2048]{1,0:T(1,128)S(1)} %merge.7), channel_id=1, source_target_pairs={{0,2},{1,3},{2,0},{3,1},{4,6},{5,7},{6,4},{7,5},{8,10},{9,11},{10,... | collective-permute-start | bytes 24584 | tf_op jit(solution)/shard_map/ppermute | solution.py:464
  63.4 4.4 %collective-permute-start.18 = (bf16[256,256]{1,0:T(8,128)(2,1)S(1)}, bf16[256,256]{1,0:T(8,128)(2,1)S(1)}, u32[]{:S(2)}, u32[]{:S(2)}) collective-permute-start(bf16[256,256]{1,0:T(8,128)(2,1)S(1)} %get-tuple-element.59), channel_id=1, source_target_pairs={{12,0},{16,4},{4,8},{24,12},{28,16},{0,20},{20,24},{8,28},{13,1},{... | collective-permute-start | bytes 393224 | tf_op jit(solution)/shard_map/ppermute | solution.py:479
  64.2 5.0 %collective-permute-start.19 = (bf16[256,256]{1,0:T(8,128)(2,1)S(1)}, bf16[256,256]{1,0:T(8,128)(2,1)S(1)}, u32[]{:S(2)}, u32[]{:S(2)}) collective-permute-start(bf16[256,256]{1,0:T(8,128)(2,1)S(1)} %get-tuple-element.60), channel_id=1, source_target_pairs={{8,0},{20,4},{0,8},{28,12},{24,16},{4,20},{16,24},{12,28},{9,1},{2... | collective-permute-start | bytes 393224 | tf_op jit(solution)/shard_map/ppermute | solution.py:479

commit v15 on v14

--- a/solution.py
+++ b/solution.py
@@ -148,43 +148,48 @@
     )(onehot, q, k, v, *after)
 
 
-def attend_kernel(n, scale, *refs):
-    ins, outs = refs[:n], refs[-3 - n : -3]
+def attend_kernel(n, scale, chosen, *refs):
+    ins, outs = refs[:n], refs[-3 - len(chosen) : -3]
     q_all, k_all, v_all = refs[-3:]
     rows = ins[0].shape[0]
     width = outs[0].shape[1]
-    group = n * PATCHES
-    block = min(group, 256)
+    asked = len(chosen) * PATCHES
+    block = min(asked, 256)
+    while asked % block:
+        block -= PATCHES
     for stamp in range(rows // PATCHES):
         here = slice(stamp * PATCHES, (stamp + 1) * PATCHES)
+        for at, cam in enumerate(chosen):
+            q_all[at * PATCHES : (at + 1) * PATCHES, :] = ins[cam][here, 0:width]
         for cam in range(n):
             there = slice(cam * PATCHES, (cam + 1) * PATCHES)
-            q_all[there, :] = ins[cam][here, 0:width]
             k_all[there, :] = ins[cam][here, width : 2 * width]
             v_all[there, :] = ins[cam][here, 2 * width : 3 * width]
-        for low in range(0, group, block):
+        for low in range(0, asked, block):
             scores = dot_bt(q_all[low : low + block, :], k_all[...]) * scale
             scores = scores - jnp.max(scores, axis=-1, keepdims=True)
             expo = jnp.exp(scores)
             probs = (expo / jnp.sum(expo, axis=-1, keepdims=True)).astype(BF16)
             result = dot(probs, v_all[...]).astype(BF16)
-            for cam in range(low // PATCHES, (low + block) // PATCHES):
-                at = cam * PATCHES - low
-                outs[cam][here, :] = result[at : at + PATCHES]
-
-
-def attend(blocks, after, n, width):
+            for at in range(low // PATCHES, (low + block) // PATCHES):
+                start = at * PATCHES - low
+                outs[at][here, :] = result[start : start + PATCHES]
+
+
+def attend(blocks, chosen, after, n, width):
     rows = blocks[0].shape[0]
     group = n * PATCHES
-    return pl.pallas_call(
-        functools.partial(attend_kernel, n, width**-0.5),
-        out_shape=[jax.ShapeDtypeStruct((rows, width), BF16)] * n,
+    asked = len(chosen)
+    return pl.pallas_call(
+        functools.partial(attend_kernel, n, width**-0.5, tuple(chosen)),
+        out_shape=[jax.ShapeDtypeStruct((rows, width), BF16)] * asked,
         in_specs=full(n) + [pl.BlockSpec(memory_space=pl.ANY)] * len(after),
-        out_specs=full(n),
-        scratch_shapes=[pltpu.VMEM((group, width), BF16)] * 3,
+        out_specs=full(asked),
+        scratch_shapes=[pltpu.VMEM((asked * PATCHES, width), BF16)]
+        + [pltpu.VMEM((group, width), BF16)] * 2,
         compiler_params=params(),
         cost_estimate=cost(
-            4 * n * rows * group * width, 8 * n * rows * width, n * rows * group
+            4 * asked * rows * group * width, 8 * n * rows * width, asked * rows * group
         ),
         name="attend",
     )(*blocks, *after)
@@ -466,10 +471,6 @@
     return square
 
 
-def held(array, after):
-    return merge(array, jnp.zeros_like(array), after)
-
-
 def exchange(block, step, n):
     return lax.ppermute(block, "cam", routes(step, n)) if step else block
 
@@ -505,10 +506,12 @@
     y, square = read_out(queries, *weights, summed, came[3:4])
     half = head_steps(heads) // 2
     square = head_sum(square, heads, 0, half)
-    attended = attend([arrived[step] for step in range(n)], [square], n, width)
-    returned = {step: give_back(attended[step], step, n) for step in early + late}
-    square = held(square, [returned[steps[0]]])
     total = head_sum(square, heads, half, head_steps(heads))
+    blocks = [arrived[step] for step in range(n)]
+    returned = {}
+    for chosen, after in ((steps[: n // 2], square), (steps[n // 2 :], total)):
+        for step, block in zip(chosen, attend(blocks, chosen, [after], n, width)):
+            returned[step] = give_back(block, step, n)
     given = base(
         gain.reshape(1, width), y, early_places, total, heads, [returned[step] for step in early]
     )

time: 71.2 us -> 71.7 us (level)
  Pallas kernels: 20.8 us -> 25.6 us
  waiting for transfers between devices: 23.5 us -> 20.4 us
  starting transfers between devices: 25.1 us -> 23.9 us
    pallas_call x1 -> x2, Pallas kernels: 1.52 us -> 6.45 us  [attend(): pl.pallas_call(functools.partial(attend_kernel, n, width ** (-0.5), tuple...]
    ppermute x2, waiting for transfers between devices: 3.97 us -> 2.07 us  [head_sum(): got = lax.ppermute(square, 'head', pairs)]
    ppermute x7, waiting for transfers between devices: 6.46 us -> 4.79 us  [exchange(): return lax.ppermute(block, 'cam', routes(step, n)) if step else block]
    ppermute x7, starting transfers between devices: 8.41 us -> 7.61 us  [give_back(): return lax.ppermute(block, 'cam', pairs) if step else block]
  transfers between devices with their start and end apart: 20 -> 20, of which waited for: 10 -> 9; matrix products, arithmetic and copies ran while one was open for 0% -> 0% of each run, Pallas kernels for 20% -> 29%
where the time goes in v15:
time: 71.7 us; the launch traced here: 71.5 us
  Pallas kernels  25.6 us (36%)
  starting transfers between devices  23.9 us (33%)
  waiting for transfers between devices  20.4 us (28%)
  local copies, waits for them, and re-layouts  1.17 us (2%)
    ppermute x2, waiting for transfers between devices, sum_over_chips(): got = lax.ppermute(mine.astype(BF16), 'cam', pairs)  9.95 us
    ppermute x7, starting transfers between devices, exchange(): return lax.ppermute(block, 'cam', routes(step, n)) if step else block  8.04 us
    ppermute x7, starting transfers between devices, give_back(): return lax.ppermute(block, 'cam', pairs) if step else block  7.61 us
    pallas_call x3, Pallas kernels, sort_tokens(): pl.pallas_call(functools.partial(sort_kernel, size), out_shape=[jax.Shape...  7.02 us
    pallas_call x2, Pallas kernels, attend(): pl.pallas_call(functools.partial(attend_kernel, n, width ** (-0.5), tuple...  6.45 us
    ppermute x7, waiting for transfers between devices, exchange(): return lax.ppermute(block, 'cam', routes(step, n)) if step else block  4.79 us
    ppermute x2, starting transfers between devices, head_sum(): got = lax.ppermute(square, 'head', pairs)  4.28 us
    pallas_call x1, Pallas kernels, gradients(): pl.pallas_call(functools.partial(grads_kernel, n, split), out_shape=[jax....  2.9 us
  transfers between devices with their start and end apart: 20, of which 9 were waited for; matrix products, arithmetic and copies ran while one was open for 0% of the time, Pallas kernels for 29%

profile of v15, /device:TPU:0, one launch (start us, length us, event | category | flops | bytes accessed | tf_op | source)
XLA Modules:
  0.0 71.5 jit_solution(17522756894706750658)
XLA Ops:
  0.7 1.4 %mark.1 = (bf16[512,2048]{1,0:T(8,128)(2,1)S(1)}, bf16[512,2048]{1,0:T(8,128)(2,1)S(1)}, bf16[1024,2048]{1,0:T(8,128)(2,1)S(1)}, f32[8,128]{1,0:T(8,128)}) custom-call(s32[1,2048]{1,0:T(1,128)S(1)} %copy-done.8), custom_call_target="tpu_custom_call" | custom-call | flops 999999995904 | bytes 1024 | tf_op jit(solution)/shard_map/mark/pallas_call | solution.py:107
  2.6 1.8 %sort_tokens.3 = (bf16[256,768]{1,0:T(8,128)(2,1)S(1)}, bf16[256,768]{1,0:T(8,128)(2,1)S(1)}, f32[8,128]{1,0:T(8,128)S(1)}) custom-call(bf16[512,2048]{1,0:T(8,128)(2,1)S(1)} %get-tuple-element.33.onehot, bf16[2048,256]{1,0:T(8,128)(2,1)S(1)} %copy-done.3, bf16[2048,256]{1,0:T(8,128)(2,1)S(1)} %copy-done.1, bf16[2048,256]{1,0:T(8,128)(2,1)S(1)} %copy-done.2), custom_call_target="tpu_custom_call" | custom-call | flops 1610612736 | bytes 3145728 | tf_op jit(solution)/shard_map/sort_tokens/pallas_call | solution.py:140
  4.4 3.4 %collective-permute-start.1 = (bf16[256,768]{1,0:T(8,128)(2,1)S(1)}, bf16[256,768]{1,0:T(8,128)(2,1)S(1)}, u32[]{:S(2)}, u32[]{:S(2)}) collective-permute-start(bf16[256,768]{1,0:T(8,128)(2,1)S(1)} %get-tuple-element.37), channel_id=1, source_target_pairs={{0,28},{4,24},{8,20},{12,16},{16,12},{20,8},{24,4},{28,0},{1,29},{... | collective-permute-start | bytes 1179656 | tf_op jit(solution)/shard_map/ppermute | solution.py:475
  7.8 2.9 %gradients.1 = (f32[384,256]{1,0:T(8,128)S(1)}, bf16[384,256]{1,0:T(8,128)(2,1)S(1)}) custom-call(bf16[2048,256]{1,0:T(8,128)(2,1)S(1)} %copy-done.1, bf16[2048,256]{1,0:T(8,128)(2,1)S(1)} %copy-done.2, f32[1,2048]{1,0:T(1,128)S(1)} %bitcast.3, bf16[1,256,256]{2,1,0:T(8,128)(2,1)S(1)} %copy-done.4, bf16[1,256,256]{2,1,0:T(8,128)(2,1)S(1)} %copy-done.5, ...), custom_call_target="tpu_custom_call" | custom-call | flops 1610612736 | bytes 4194304 | tf_op jit(solution)/shard_map/gradients/pallas_call | solution.py:241
  10.7 0.7 %collective-permute-start = (bf16[384,256]{1,0:T(8,128)(2,1)S(1)}, bf16[384,256]{1,0:T(8,128)(2,1)S(1)}, u32[]{:S(2)}, u32[]{:S(2)}) collective-permute-start(bf16[384,256]{1,0:T(8,128)(2,1)S(1)} %get-tuple-element.36), channel_id=1, source_target_pairs={{0,4},{4,0},{8,12},{12,8},{16,20},{20,16},{24,28},{28,24},{1,5},{5... | collective-permute-start | bytes 589832 | tf_op jit(solution)/shard_map/ppermute | solution.py:275
  11.4 1.1 %collective-permute-done.got_ref = bf16[384,256]{1,0:T(8,128)(2,1)S(1)} collective-permute-done((bf16[384,256]{1,0:T(8,128)(2,1)S(1)}, bf16[384,256]{1,0:T(8,128)(2,1)S(1)}, u32[]{:S(2)}, u32[]{:S(2)}) %collective-permute-start) | collective-permute-done | bytes 196640 | tf_op jit(solution)/shard_map/ppermute | solution.py:275
  12.5 4.8 %collective-permute-done.1.rest_0_.refs_7_ = bf16[256,768]{1,0:T(8,128)(2,1)S(1)} collective-permute-done((bf16[256,768]{1,0:T(8,128)(2,1)S(1)}, bf16[256,768]{1,0:T(8,128)(2,1)S(1)}, u32[]{:S(2)}, u32[]{:S(2)}) %collective-permute-start.1) | collective-permute-done | bytes 393248 | tf_op jit(solution)/shard_map/ppermute | solution.py:475
  17.4 2.5 %collective-permute-start.2 = (bf16[384,256]{1,0:T(8,128)(2,1)S(1)}, bf16[384,256]{1,0:T(8,128)(2,1)S(1)}, u32[]{:S(2)}, u32[]{:S(2)}) collective-permute-start(bf16[384,256]{1,0:T(8,128)(2,1)S(1)} %convert_element_type.6), channel_id=1, source_target_pairs={{0,8},{4,20},{8,0},{12,28},{16,24},{20,4},{24,16},{28,12},{1,9},{5... | collective-permute-start | bytes 589832 | tf_op jit(solution)/shard_map/ppermute | solution.py:287
  19.8 1.8 %sort_tokens.4 = (bf16[256,768]{1,0:T(8,128)(2,1)S(1)}, bf16[256,768]{1,0:T(8,128)(2,1)S(1)}, f32[8,128]{1,0:T(8,128)S(1)}) custom-call(bf16[512,2048]{1,0:T(8,128)(2,1)S(1)} %get-tuple-element.38.onehot, bf16[2048,256]{1,0:T(8,128)(2,1)S(1)} %copy-done.3, bf16[2048,256]{1,0:T(8,128)(2,1)S(1)} %copy-done.1, bf16[2048,256]{1,0:T(8,128)(2,1)S(1)} %copy-done.2), custom_call_target="tpu_custom_call" | custom-call | flops 1610612736 | bytes 3145728 | tf_op jit(solution)/shard_map/sort_tokens/pallas_call | solution.py:140
  21.7 1.6 %collective-permute-start.7 = (bf16[256,768]{1,0:T(8,128)(2,1)S(1)}, bf16[256,768]{1,0:T(8,128)(2,1)S(1)}, u32[]{:S(2)}, u32[]{:S(2)}) collective-permute-start(bf16[256,768]{1,0:T(8,128)(2,1)S(1)} %get-tuple-element.45), channel_id=1, source_target_pairs={{0,16},{4,12},{8,24},{12,4},{16,0},{20,28},{24,8},{28,20},{1,17},{... | collective-permute-start | bytes 1179656 | tf_op jit(solution)/shard_map/ppermute | solution.py:475
  23.3 1.7 %place.1 = (bf16[2048,1536]{1,0:T(8,128)(2,1)S(1)}, bf16[2048,512]{1,0:T(8,128)(2,1)S(1)}) custom-call(s32[1,2048]{1,0:T(1,128)S(1)} %copy-done.9), custom_call_target="tpu_custom_call" | custom-call | flops 4194304 | bytes 8388608 | tf_op jit(solution)/shard_map/place/pallas_call | solution.py:379
  25.0 6.0 %collective-permute-done.2.got_ref = bf16[384,256]{1,0:T(8,128)(2,1)S(1)} collective-permute-done((bf16[384,256]{1,0:T(8,128)(2,1)S(1)}, bf16[384,256]{1,0:T(8,128)(2,1)S(1)}, u32[]{:S(2)}, u32[]{:S(2)}) %collective-permute-start.2) | collective-permute-done | bytes 196640 | tf_op jit(solution)/shard_map/ppermute | solution.py:287
  31.1 3.4 %sort_tokens.5 = (bf16[256,768]{1,0:T(8,128)(2,1)S(1)}, bf16[256,768]{1,0:T(8,128)(2,1)S(1)}, bf16[256,768]{1,0:T(8,128)(2,1)S(1)}, bf16[256,768]{1,0:T(8,128)(2,1)S(1)}, f32[8,128]{1,0:T(8,128)S(1)}) custom-call(bf16[1024,2048]{1,0:T(8,128)(2,1)S(1)} %get-tuple-element.42.onehot, bf16[2048,256]{1,0:T(8,128)(2,1)S(1)} %copy-done.3, ...), custom_call_target="tpu_custom_call" | custom-call | flops 3221225472 | bytes 3145728 | tf_op jit(solution)/shard_map/sort_tokens/pallas_call | solution.py:140
  34.6 4.0 %collective-permute-done.3.got_ref = bf16[384,256]{1,0:T(8,128)(2,1)S(1)} collective-permute-done((bf16[384,256]{1,0:T(8,128)(2,1)S(1)}, bf16[384,256]{1,0:T(8,128)(2,1)S(1)}, u32[]{:S(2)}, u32[]{:S(2)}) %collective-permute-start.3) | collective-permute-done | bytes 196640 | tf_op jit(solution)/shard_map/ppermute | solution.py:287
  38.6 0.7 %collective-permute-start.6 = (f32[384,256]{1,0:T(8,128)S(1)}, f32[384,256]{1,0:T(8,128)S(1)}, u32[]{:S(2)}, u32[]{:S(2)}) collective-permute-start(f32[384,256]{1,0:T(8,128)S(1)} %merge.5.rest_0_), channel_id=1, source_target_pairs={{0,4},{4,0},{8,12},{12,8},{16,20},{20,16},{24,28},{28,24},{1,5},{5... | collective-permute-start | bytes 1179656 | tf_op jit(solution)/shard_map/ppermute | solution.py:292
  39.4 2.0 %collective-permute-start.11 = (bf16[256,768]{1,0:T(8,128)(2,1)S(1)}, bf16[256,768]{1,0:T(8,128)(2,1)S(1)}, u32[]{:S(2)}, u32[]{:S(2)}) collective-permute-start(bf16[256,768]{1,0:T(8,128)(2,1)S(1)} %get-tuple-element.51), channel_id=1, source_target_pairs={{0,8},{4,20},{8,0},{12,28},{16,24},{20,4},{24,16},{28,12},{1,9},{5... | collective-permute-start | bytes 1179656 | tf_op jit(solution)/shard_map/ppermute | solution.py:475
  41.4 0.9 %collective-permute-start.12 = (bf16[256,768]{1,0:T(8,128)(2,1)S(1)}, bf16[256,768]{1,0:T(8,128)(2,1)S(1)}, u32[]{:S(2)}, u32[]{:S(2)}) collective-permute-start(bf16[256,768]{1,0:T(8,128)(2,1)S(1)} %get-tuple-element.52), channel_id=1, source_target_pairs={{0,12},{4,16},{8,4},{12,24},{16,28},{20,0},{24,20},{28,8},{1,13},{... | collective-permute-start | bytes 1179656 | tf_op jit(solution)/shard_map/ppermute | solution.py:475
  42.3 2.7 %read_out.1 = (f32[2048,256]{1,0:T(8,128)S(1)}, f32[1,2048]{1,0:T(1,128)S(1)}) custom-call(bf16[2048,256]{1,0:T(8,128)(2,1)S(1)} %copy-done.3, bf16[1,256,256]{2,1,0:T(8,128)(2,1)S(1)} %copy-done.4, bf16[1,256,256]{2,1,0:T(8,128)(2,1)S(1)} %copy-done.5, bf16[1,256,256]{2,1,0:T(8,128)(2,1)S(1)} %copy-done.6, f32[384,256]{1,0:T(8,128)S(1)} %merge.5.rest_0_, ...), custom_call_target="tpu_custom_call" | custom-call | flops 805306368 | bytes 4194304 | tf_op jit(solution)/shard_map/read_out/pallas_call | solution.py:339
  45.0 1.6 %collective-permute-start.8 = (f32[1,2048]{1,0:T(1,128)S(1)}, f32[1,2048]{1,0:T(1,128)S(1)}, u32[]{:S(2)}, u32[]{:S(2)}) collective-permute-start(f32[1,2048]{1,0:T(1,128)S(1)} %get-tuple-element.48), channel_id=1, source_target_pairs={{0,1},{1,0},{2,3},{3,2},{4,5},{5,4},{6,7},{7,6},{8,9},{9,8},{10,11... | collective-permute-start | bytes 24584 | tf_op jit(solution)/shard_map/ppermute | solution.py:469
  46.6 2.1 %collective-permute-done.8 = f32[1,2048]{1,0:T(1,128)S(1)} collective-permute-done((f32[1,2048]{1,0:T(1,128)S(1)}, f32[1,2048]{1,0:T(1,128)S(1)}, u32[]{:S(2)}, u32[]{:S(2)}) %collective-permute-start.8) | collective-permute-done | bytes 8224 | tf_op jit(solution)/shard_map/ppermute | solution.py:469
  48.7 2.7 %collective-permute-start.9 = (f32[1,2048]{1,0:T(1,128)S(1)}, f32[1,2048]{1,0:T(1,128)S(1)}, u32[]{:S(2)}, u32[]{:S(2)}) collective-permute-start(f32[1,2048]{1,0:T(1,128)S(1)} %add.6.refs_8_), channel_id=1, source_target_pairs={{0,2},{1,3},{2,0},{3,1},{4,6},{5,7},{6,4},{7,5},{8,10},{9,11},{10,... | collective-permute-start | bytes 24584 | tf_op jit(solution)/shard_map/ppermute | solution.py:469
  51.3 3.2 %attend.2 = (bf16[256,256]{1,0:T(8,128)(2,1)S(1)}, bf16[256,256]{1,0:T(8,128)(2,1)S(1)}, bf16[256,256]{1,0:T(8,128)(2,1)S(1)}, bf16[256,256]{1,0:T(8,128)(2,1)S(1)}) custom-call(bf16[256,768]{1,0:T(8,128)(2,1)S(1)} %get-tuple-element.49.refs_0_, bf16[256,768]{1,0:T(8,128)(2,1)S(1)} %collective-permute-done.10.refs_1_, ...), custom_call_target="tpu_custom_call" | custom-call | flops 268435456 | bytes 4194304 | tf_op jit(solution)/shard_map/attend/pallas_call | solution.py:183
  54.6 2.8 %collective-permute-start.13 = (bf16[256,256]{1,0:T(8,128)(2,1)S(1)}, bf16[256,256]{1,0:T(8,128)(2,1)S(1)}, u32[]{:S(2)}, u32[]{:S(2)}) collective-permute-start(bf16[256,256]{1,0:T(8,128)(2,1)S(1)} %get-tuple-element.53), channel_id=1, source_target_pairs={{28,0},{24,4},{20,8},{16,12},{12,16},{8,20},{4,24},{0,28},{29,1},{... | collective-permute-start | bytes 393224 | tf_op jit(solution)/shard_map/ppermute | solution.py:480
  57.3 0.8 %collective-permute-start.15 = (bf16[256,256]{1,0:T(8,128)(2,1)S(1)}, bf16[256,256]{1,0:T(8,128)(2,1)S(1)}, u32[]{:S(2)}, u32[]{:S(2)}) collective-permute-start(bf16[256,256]{1,0:T(8,128)(2,1)S(1)} %get-tuple-element.55), channel_id=1, source_target_pairs={{20,0},{8,4},{28,8},{0,12},{4,16},{24,20},{12,24},{16,28},{21,1},{... | collective-permute-start | bytes 393224 | tf_op jit(solution)/shard_map/ppermute | solution.py:480
  58.2 1.5 %collective-permute-start.16 = (bf16[256,256]{1,0:T(8,128)(2,1)S(1)}, bf16[256,256]{1,0:T(8,128)(2,1)S(1)}, u32[]{:S(2)}, u32[]{:S(2)}) collective-permute-start(bf16[256,256]{1,0:T(8,128)(2,1)S(1)} %get-tuple-element.56), channel_id=1, source_target_pairs={{16,0},{12,4},{24,8},{4,12},{0,16},{28,20},{8,24},{20,28},{17,1},{... | collective-permute-start | bytes 393224 | tf_op jit(solution)/shard_map/ppermute | solution.py:480
  59.7 3.2 %attend.3 = (bf16[256,256]{1,0:T(8,128)(2,1)S(1)}, bf16[256,256]{1,0:T(8,128)(2,1)S(1)}, bf16[256,256]{1,0:T(8,128)(2,1)S(1)}, bf16[256,256]{1,0:T(8,128)(2,1)S(1)}) custom-call(bf16[256,768]{1,0:T(8,128)(2,1)S(1)} %get-tuple-element.49.refs_0_, bf16[256,768]{1,0:T(8,128)(2,1)S(1)} %collective-permute-done.10.refs_1_, ...), custom_call_target="tpu_custom_call" | custom-call | flops 268435456 | bytes 4194304 | tf_op jit(solution)/shard_map/attend/pallas_call | solution.py:183
  62.9 1.1 %collective-permute-start.17 = (bf16[256,256]{1,0:T(8,128)(2,1)S(1)}, bf16[256,256]{1,0:T(8,128)(2,1)S(1)}, u32[]{:S(2)}, u32[]{:S(2)}) collective-permute-start(bf16[256,256]{1,0:T(8,128)(2,1)S(1)} %get-tuple-element.57), channel_id=1, source_target_pairs={{4,0},{0,4},{12,8},{8,12},{20,16},{16,20},{28,24},{24,28},{5,1},{1... | collective-permute-start | bytes 393224 | tf_op jit(solution)/shard_map/ppermute | solution.py:480
  64.0 0.7 %collective-permute-done.14.rest_1_ = bf16[256,256]{1,0:T(8,128)(2,1)S(1)} collective-permute-done((bf16[256,256]{1,0:T(8,128)(2,1)S(1)}, bf16[256,256]{1,0:T(8,128)(2,1)S(1)}, u32[]{:S(2)}, u32[]{:S(2)}) %collective-permute-start.14) | collective-permute-done | bytes 131104 | tf_op jit(solution)/shard_map/ppermute | solution.py:480
  64.7 1.5 %collective-permute-start.19 = (bf16[256,256]{1,0:T(8,128)(2,1)S(1)}, bf16[256,256]{1,0:T(8,128)(2,1)S(1)}, u32[]{:S(2)}, u32[]{:S(2)}) collective-permute-start(bf16[256,256]{1,0:T(8,128)(2,1)S(1)} %get-tuple-element.60), channel_id=1, source_target_pairs={{8,0},{20,4},{0,8},{28,12},{24,16},{4,20},{16,24},{12,28},{9,1},{2... | collective-permute-start | bytes 393224 | tf_op jit(solution)/shard_map/ppermute | solution.py:480
  67.0 1.8 %base.1.base_ref = f32[2048,256]{1,0:T(8,128)S(1)} custom-call(f32[1,256]{1,0:T(1,128)S(1)} %bitcast.2, f32[2048,256]{1,0:T(8,128)S(1)} %get-tuple-element.46.y_ref, bf16[2048,1536]{1,0:T(8,128)(2,1)S(1)} %get-tuple-element.47.onehot, f32[1,2048]{1,0:T(1,128)S(1)} %add.7.refs_8_.total_ref, bf16[256,256]{1,0:T(8,128)(2,1)S(1)} %collective-permute-done.13.rest_0_, ...), custom_call_target="tpu_custom_call" | custom-call | flops 1610612736 | bytes 4194304 | tf_op jit(solution)/shard_map/base/pallas_call | solution.py:417
  68.8 0.9 %collective-permute-done.19.rest_1_ = bf16[256,256]{1,0:T(8,128)(2,1)S(1)} collective-permute-done((bf16[256,256]{1,0:T(8,128)(2,1)S(1)}, bf16[256,256]{1,0:T(8,128)(2,1)S(1)}, u32[]{:S(2)}, u32[]{:S(2)}) %collective-permute-start.19) | collective-permute-done | bytes 131104 | tf_op jit(solution)/shard_map/ppermute | solution.py:480
  69.8 1.6 %mix.1 = bf16[2048,256]{1,0:T(8,128)(2,1)} custom-call(f32[2048,256]{1,0:T(8,128)S(1)} %base.1.base_ref, bf16[2048,512]{1,0:T(8,128)(2,1)S(1)} %get-tuple-element.44.rest_3_.onehot, bf16[256,256]{1,0:T(8,128)(2,1)S(1)} %collective-permute-done.18.rest_0_, bf16[256,256]{1,0:T(8,128)(2,1)S(1)} %collective-permute-done.19.rest_1_), custom_call_target="tpu_custom_call" | custom-call | flops 536870912 | bytes 4194304 | tf_op jit(solution)/shard_map/mix/pallas_call | solution.py:445
  (46 shorter events, 2.4 us)
Async XLA Ops:
  0.0 0.7 copy-start.8
  0.7 1.4 %copy-start.1 = (bf16[2048,256]{1,0:T(8,128)(2,1)S(1)}, bf16[2048,256]{1,0:T(8,128)(2,1)}, u32[]{:S(2)}) copy-start(bf16[2048,256]{1,0:T(8,128)(2,1)} %k_ref.7) | copy-start | bytes 3145732
  0.7 1.5 %copy-start.2 = (bf16[2048,256]{1,0:T(8,128)(2,1)S(1)}, bf16[2048,256]{1,0:T(8,128)(2,1)}, u32[]{:S(2)}) copy-start(bf16[2048,256]{1,0:T(8,128)(2,1)} %v_ref.7) | copy-start | bytes 3145732
  0.7 1.9 %copy-start.3 = (bf16[2048,256]{1,0:T(8,128)(2,1)S(1)}, bf16[2048,256]{1,0:T(8,128)(2,1)}, u32[]{:S(2)}) copy-start(bf16[2048,256]{1,0:T(8,128)(2,1)} %q_ref.7) | copy-start | bytes 3145732
  2.6 5.2 %copy-start.4 = (bf16[1,256,256]{2,1,0:T(8,128)(2,1)S(1)}, bf16[1,256,256]{2,1,0:T(8,128)(2,1)}, u32[]{:S(2)}) copy-start(bf16[1,256,256]{2,1,0:T(8,128)(2,1)} %one_ref.3) | copy-start | bytes 393220
  2.6 5.2 %copy-start.5 = (bf16[1,256,256]{2,1,0:T(8,128)(2,1)S(1)}, bf16[1,256,256]{2,1,0:T(8,128)(2,1)}, u32[]{:S(2)}) copy-start(bf16[1,256,256]{2,1,0:T(8,128)(2,1)} %three_ref.3) | copy-start | bytes 393220
  2.6 5.2 %copy-start.6 = (bf16[1,256,256]{2,1,0:T(8,128)(2,1)S(1)}, bf16[1,256,256]{2,1,0:T(8,128)(2,1)}, u32[]{:S(2)}) copy-start(bf16[1,256,256]{2,1,0:T(8,128)(2,1)} %two_ref.3) | copy-start | bytes 393220
  2.6 5.2 %copy-start.7 = (f32[2048,1]{0,1:T(1,128)S(1)}, f32[2048,1]{0,1:T(1,128)}, u32[]{:S(2)}) copy-start(f32[2048,1]{0,1:T(1,128)} %param.12) | copy-start | bytes 24580
  4.4 12.9 %collective-permute-start.1 = (bf16[256,768]{1,0:T(8,128)(2,1)S(1)}, bf16[256,768]{1,0:T(8,128)(2,1)S(1)}, u32[]{:S(2)}, u32[]{:S(2)}) collective-permute-start(bf16[256,768]{1,0:T(8,128)(2,1)S(1)} %get-tuple-element.37), channel_id=1, source_target_pairs={{0,28},{4,24},{8,20},{12,16},{16,12},{20,8},{24,4},{28,0},{1,29},{... | collective-permute-start | bytes 1179656 | tf_op jit(solution)/shard_map/ppermute | solution.py:475
  10.7 1.8 %collective-permute-start = (bf16[384,256]{1,0:T(8,128)(2,1)S(1)}, bf16[384,256]{1,0:T(8,128)(2,1)S(1)}, u32[]{:S(2)}, u32[]{:S(2)}) collective-permute-start(bf16[384,256]{1,0:T(8,128)(2,1)S(1)} %get-tuple-element.36), channel_id=1, source_target_pairs={{0,4},{4,0},{8,12},{12,8},{16,20},{20,16},{24,28},{28,24},{1,5},{5... | collective-permute-start | bytes 589832 | tf_op jit(solution)/shard_map/ppermute | solution.py:275
  11.4 23.1 %collective-permute-start.4 = (bf16[256,768]{1,0:T(8,128)(2,1)S(1)}, bf16[256,768]{1,0:T(8,128)(2,1)S(1)}, u32[]{:S(2)}, u32[]{:S(2)}) collective-permute-start(bf16[256,768]{1,0:T(8,128)(2,1)S(1)} %get-tuple-element.40), channel_id=1, source_target_pairs={{0,24},{4,28},{8,16},{12,20},{16,8},{20,12},{24,0},{28,4},{1,25},{... | collective-permute-start | bytes 1179656 | tf_op jit(solution)/shard_map/ppermute | solution.py:475
  17.4 13.6 %collective-permute-start.2 = (bf16[384,256]{1,0:T(8,128)(2,1)S(1)}, bf16[384,256]{1,0:T(8,128)(2,1)S(1)}, u32[]{:S(2)}, u32[]{:S(2)}) collective-permute-start(bf16[384,256]{1,0:T(8,128)(2,1)S(1)} %convert_element_type.6), channel_id=1, source_target_pairs={{0,8},{4,20},{8,0},{12,28},{16,24},{20,4},{24,16},{28,12},{1,9},{5... | collective-permute-start | bytes 589832 | tf_op jit(solution)/shard_map/ppermute | solution.py:287
  19.8 3.4 %copy-start.9 = (s32[1,2048]{1,0:T(1,128)S(1)}, s32[1,2048]{1,0:T(1,128)}, u32[]{:S(2)}) copy-start(s32[1,2048]{1,0:T(1,128)} %order_ref.3) | copy-start | bytes 24580
  21.6 12.9 %collective-permute-start.5 = (bf16[256,768]{1,0:T(8,128)(2,1)S(1)}, bf16[256,768]{1,0:T(8,128)(2,1)S(1)}, u32[]{:S(2)}, u32[]{:S(2)}) collective-permute-start(bf16[256,768]{1,0:T(8,128)(2,1)S(1)} %get-tuple-element.41), channel_id=1, source_target_pairs={{0,20},{4,8},{8,28},{12,0},{16,4},{20,24},{24,12},{28,16},{1,21},{... | collective-permute-start | bytes 1179656 | tf_op jit(solution)/shard_map/ppermute | solution.py:475
  21.7 20.6 %collective-permute-start.7 = (bf16[256,768]{1,0:T(8,128)(2,1)S(1)}, bf16[256,768]{1,0:T(8,128)(2,1)S(1)}, u32[]{:S(2)}, u32[]{:S(2)}) collective-permute-start(bf16[256,768]{1,0:T(8,128)(2,1)S(1)} %get-tuple-element.45), channel_id=1, source_target_pairs={{0,16},{4,12},{8,24},{12,4},{16,0},{20,28},{24,8},{28,20},{1,17},{... | collective-permute-start | bytes 1179656 | tf_op jit(solution)/shard_map/ppermute | solution.py:475
  31.0 7.5 %collective-permute-start.3 = (bf16[384,256]{1,0:T(8,128)(2,1)S(1)}, bf16[384,256]{1,0:T(8,128)(2,1)S(1)}, u32[]{:S(2)}, u32[]{:S(2)}) collective-permute-start(bf16[384,256]{1,0:T(8,128)(2,1)S(1)} %convert_element_type.7), channel_id=1, source_target_pairs={{0,16},{4,12},{8,24},{12,4},{16,0},{20,28},{24,8},{28,20},{1,17},{... | collective-permute-start | bytes 589832 | tf_op jit(solution)/shard_map/ppermute | solution.py:287
  38.6 3.7 %collective-permute-start.6 = (f32[384,256]{1,0:T(8,128)S(1)}, f32[384,256]{1,0:T(8,128)S(1)}, u32[]{:S(2)}, u32[]{:S(2)}) collective-permute-start(f32[384,256]{1,0:T(8,128)S(1)} %merge.5.rest_0_), channel_id=1, source_target_pairs={{0,4},{4,0},{8,12},{12,8},{16,20},{20,16},{24,28},{28,24},{1,5},{5... | collective-permute-start | bytes 1179656 | tf_op jit(solution)/shard_map/ppermute | solution.py:292
  39.3 12.0 %collective-permute-start.10 = (bf16[256,768]{1,0:T(8,128)(2,1)S(1)}, bf16[256,768]{1,0:T(8,128)(2,1)S(1)}, u32[]{:S(2)}, u32[]{:S(2)}) collective-permute-start(bf16[256,768]{1,0:T(8,128)(2,1)S(1)} %get-tuple-element.50), channel_id=1, source_target_pairs={{0,4},{4,0},{8,12},{12,8},{16,20},{20,16},{24,28},{28,24},{1,5},{5... | collective-permute-start | bytes 1179656 | tf_op jit(solution)/shard_map/ppermute | solution.py:475
  39.4 12.0 %collective-permute-start.11 = (bf16[256,768]{1,0:T(8,128)(2,1)S(1)}, bf16[256,768]{1,0:T(8,128)(2,1)S(1)}, u32[]{:S(2)}, u32[]{:S(2)}) collective-permute-start(bf16[256,768]{1,0:T(8,128)(2,1)S(1)} %get-tuple-element.51), channel_id=1, source_target_pairs={{0,8},{4,20},{8,0},{12,28},{16,24},{20,4},{24,16},{28,12},{1,9},{5... | collective-permute-start | bytes 1179656 | tf_op jit(solution)/shard_map/ppermute | solution.py:475
  41.4 10.0 %collective-permute-start.12 = (bf16[256,768]{1,0:T(8,128)(2,1)S(1)}, bf16[256,768]{1,0:T(8,128)(2,1)S(1)}, u32[]{:S(2)}, u32[]{:S(2)}) collective-permute-start(bf16[256,768]{1,0:T(8,128)(2,1)S(1)} %get-tuple-element.52), channel_id=1, source_target_pairs={{0,12},{4,16},{8,4},{12,24},{16,28},{20,0},{24,20},{28,8},{1,13},{... | collective-permute-start | bytes 1179656 | tf_op jit(solution)/shard_map/ppermute | solution.py:475
  45.0 3.7 %collective-permute-start.8 = (f32[1,2048]{1,0:T(1,128)S(1)}, f32[1,2048]{1,0:T(1,128)S(1)}, u32[]{:S(2)}, u32[]{:S(2)}) collective-permute-start(f32[1,2048]{1,0:T(1,128)S(1)} %get-tuple-element.48), channel_id=1, source_target_pairs={{0,1},{1,0},{2,3},{3,2},{4,5},{5,4},{6,7},{7,6},{8,9},{9,8},{10,11... | collective-permute-start | bytes 24584 | tf_op jit(solution)/shard_map/ppermute | solution.py:469
  48.7 11.0 %collective-permute-start.9 = (f32[1,2048]{1,0:T(1,128)S(1)}, f32[1,2048]{1,0:T(1,128)S(1)}, u32[]{:S(2)}, u32[]{:S(2)}) collective-permute-start(f32[1,2048]{1,0:T(1,128)S(1)} %add.6.refs_8_), channel_id=1, source_target_pairs={{0,2},{1,3},{2,0},{3,1},{4,6},{5,7},{6,4},{7,5},{8,10},{9,11},{10,... | collective-permute-start | bytes 24584 | tf_op jit(solution)/shard_map/ppermute | solution.py:469
  54.6 12.4 %copy-start = (f32[256]{0:T(256)S(1)}, f32[256]{0:T(256)}, u32[]{:S(2)}) copy-start(f32[256]{0:T(256)} %param.16) | copy-start | bytes 3076
  54.6 9.4 %collective-permute-start.13 = (bf16[256,256]{1,0:T(8,128)(2,1)S(1)}, bf16[256,256]{1,0:T(8,128)(2,1)S(1)}, u32[]{:S(2)}, u32[]{:S(2)}) collective-permute-start(bf16[256,256]{1,0:T(8,128)(2,1)S(1)} %get-tuple-element.53), channel_id=1, source_target_pairs={{28,0},{24,4},{20,8},{16,12},{12,16},{8,20},{4,24},{0,28},{29,1},{... | collective-permute-start | bytes 393224 | tf_op jit(solution)/shard_map/ppermute | solution.py:480
  57.3 7.4 %collective-permute-start.14 = (bf16[256,256]{1,0:T(8,128)(2,1)S(1)}, bf16[256,256]{1,0:T(8,128)(2,1)S(1)}, u32[]{:S(2)}, u32[]{:S(2)}) collective-permute-start(bf16[256,256]{1,0:T(8,128)(2,1)S(1)} %get-tuple-element.54), channel_id=1, source_target_pairs={{24,0},{28,4},{16,8},{20,12},{8,16},{12,20},{0,24},{4,28},{25,1},{... | collective-permute-start | bytes 393224 | tf_op jit(solution)/shard_map/ppermute | solution.py:480
  57.3 9.5 %collective-permute-start.15 = (bf16[256,256]{1,0:T(8,128)(2,1)S(1)}, bf16[256,256]{1,0:T(8,128)(2,1)S(1)}, u32[]{:S(2)}, u32[]{:S(2)}) collective-permute-start(bf16[256,256]{1,0:T(8,128)(2,1)S(1)} %get-tuple-element.55), channel_id=1, source_target_pairs={{20,0},{8,4},{28,8},{0,12},{4,16},{24,20},{12,24},{16,28},{21,1},{... | collective-permute-start | bytes 393224 | tf_op jit(solution)/shard_map/ppermute | solution.py:480
  58.2 8.8 %collective-permute-start.16 = (bf16[256,256]{1,0:T(8,128)(2,1)S(1)}, bf16[256,256]{1,0:T(8,128)(2,1)S(1)}, u32[]{:S(2)}, u32[]{:S(2)}) collective-permute-start(bf16[256,256]{1,0:T(8,128)(2,1)S(1)} %get-tuple-element.56), channel_id=1, source_target_pairs={{16,0},{12,4},{24,8},{4,12},{0,16},{28,20},{8,24},{20,28},{17,1},{... | collective-permute-start | bytes 393224 | tf_op jit(solution)/shard_map/ppermute | solution.py:480
  62.9 4.1 %collective-permute-start.17 = (bf16[256,256]{1,0:T(8,128)(2,1)S(1)}, bf16[256,256]{1,0:T(8,128)(2,1)S(1)}, u32[]{:S(2)}, u32[]{:S(2)}) collective-permute-start(bf16[256,256]{1,0:T(8,128)(2,1)S(1)} %get-tuple-element.57), channel_id=1, source_target_pairs={{4,0},{0,4},{12,8},{8,12},{20,16},{16,20},{28,24},{24,28},{5,1},{1... | collective-permute-start | bytes 393224 | tf_op jit(solution)/shard_map/ppermute | solution.py:480
  64.0 4.8 %collective-permute-start.18 = (bf16[256,256]{1,0:T(8,128)(2,1)S(1)}, bf16[256,256]{1,0:T(8,128)(2,1)S(1)}, u32[]{:S(2)}, u32[]{:S(2)}) collective-permute-start(bf16[256,256]{1,0:T(8,128)(2,1)S(1)} %get-tuple-element.59), channel_id=1, source_target_pairs={{12,0},{16,4},{4,8},{24,12},{28,16},{0,20},{20,24},{8,28},{13,1},{... | collective-permute-start | bytes 393224 | tf_op jit(solution)/shard_map/ppermute | solution.py:480
  64.7 5.1 %collective-permute-start.19 = (bf16[256,256]{1,0:T(8,128)(2,1)S(1)}, bf16[256,256]{1,0:T(8,128)(2,1)S(1)}, u32[]{:S(2)}, u32[]{:S(2)}) collective-permute-start(bf16[256,256]{1,0:T(8,128)(2,1)S(1)} %get-tuple-element.60), channel_id=1, source_target_pairs={{8,0},{20,4},{0,8},{28,12},{24,16},{4,20},{16,24},{12,28},{9,1},{2... | collective-permute-start | bytes 393224 | tf_op jit(solution)/shard_map/ppermute | solution.py:480

commit v16 on v14

--- a/solution.py
+++ b/solution.py
@@ -466,8 +466,22 @@
     return square
 
 
-def held(array, after):
-    return merge(array, jnp.zeros_like(array), after)
+def pass_on_kernel(size, *refs):
+    for source, target in zip(refs[:size], refs[size + 1 :]):
+        target[...] = source[...]
+
+
+def pass_on(blocks, after):
+    size = len(blocks)
+    return pl.pallas_call(
+        functools.partial(pass_on_kernel, size),
+        out_shape=[jax.ShapeDtypeStruct(block.shape, block.dtype) for block in blocks],
+        in_specs=full(size) + [pl.BlockSpec(memory_space=pl.ANY)],
+        out_specs=full(size),
+        compiler_params=params(),
+        cost_estimate=cost(0, 4 * size * blocks[0].size),
+        name="pass_on",
+    )(*blocks, after)
 
 
 def exchange(block, step, n):
@@ -505,10 +519,12 @@
     y, square = read_out(queries, *weights, summed, came[3:4])
     half = head_steps(heads) // 2
     square = head_sum(square, heads, 0, half)
-    attended = attend([arrived[step] for step in range(n)], [square], n, width)
-    returned = {step: give_back(attended[step], step, n) for step in early + late}
-    square = held(square, [returned[steps[0]]])
     total = head_sum(square, heads, half, head_steps(heads))
+    blocks = [arrived[step] for step in range(n)]
+    attended = attend(blocks, [square], n, width)
+    later = pass_on([attended[step] for step in steps[n // 2 :]], total)
+    attended = dict(zip(steps, [attended[step] for step in steps[: n // 2]] + list(later)))
+    returned = {step: give_back(attended[step], step, n) for step in steps}
     given = base(
         gain.reshape(1, width), y, early_places, total, heads, [returned[step] for step in early]
     )

time: 71.2 us -> 69.9 us (0.982)
  waiting for transfers between devices: 23.5 us -> 22 us
    ppermute x7, waiting for transfers between devices: 2.12 us -> 4.14 us  [give_back(): return lax.ppermute(block, 'cam', pairs) if step else block]
    ppermute x2, waiting for transfers between devices: 3.97 us -> 2.08 us  [head_sum(): got = lax.ppermute(square, 'head', pairs)]
    ppermute x7, waiting for transfers between devices: 6.46 us -> 4.79 us  [exchange(): return lax.ppermute(block, 'cam', routes(step, n)) if step else block]
  transfers between devices with their start and end apart: 20 -> 20, of which waited for: 10 -> 10; matrix products, arithmetic and copies ran while one was open for 0% -> 0% of each run, Pallas kernels for 20% -> 23%
where the time goes in v16:
time: 69.9 us; the launch traced here: 69.7 us
  starting transfers between devices  25.4 us (36%)
  waiting for transfers between devices  22 us (31%)
  Pallas kernels  20.7 us (30%)
  local copies, waits for them, and re-layouts  1.16 us (2%)
    ppermute x2, waiting for transfers between devices, sum_over_chips(): got = lax.ppermute(mine.astype(BF16), 'cam', pairs)  9.95 us
    ppermute x7, starting transfers between devices, give_back(): return lax.ppermute(block, 'cam', pairs) if step else block  9.04 us
    ppermute x7, starting transfers between devices, exchange(): return lax.ppermute(block, 'cam', routes(step, n)) if step else block  8.04 us
    pallas_call x3, Pallas kernels, sort_tokens(): pl.pallas_call(functools.partial(sort_kernel, size), out_shape=[jax.Shape...  7.02 us
    ppermute x7, waiting for transfers between devices, exchange(): return lax.ppermute(block, 'cam', routes(step, n)) if step else block  4.79 us
    ppermute x2, starting transfers between devices, head_sum(): got = lax.ppermute(square, 'head', pairs)  4.27 us
    ppermute x7, waiting for transfers between devices, give_back(): return lax.ppermute(block, 'cam', pairs) if step else block  4.14 us
    pallas_call x1, Pallas kernels, gradients(): pl.pallas_call(functools.partial(grads_kernel, n, split), out_shape=[jax....  2.9 us
  transfers between devices with their start and end apart: 20, of which 10 were waited for; matrix products, arithmetic and copies ran while one was open for 0% of the time, Pallas kernels for 23%

profile of v16, /device:TPU:0, one launch (start us, length us, event | category | flops | bytes accessed | tf_op | source)
XLA Modules:
  0.0 69.7 jit_solution(2808061976197483298)
XLA Ops:
  0.7 1.4 %mark.1 = (bf16[512,2048]{1,0:T(8,128)(2,1)S(1)}, bf16[512,2048]{1,0:T(8,128)(2,1)S(1)}, bf16[1024,2048]{1,0:T(8,128)(2,1)S(1)}, f32[8,128]{1,0:T(8,128)}) custom-call(s32[1,2048]{1,0:T(1,128)S(1)} %copy-done.8), custom_call_target="tpu_custom_call" | custom-call | flops 999999995904 | bytes 1024 | tf_op jit(solution)/shard_map/mark/pallas_call | solution.py:107
  2.6 1.8 %sort_tokens.3 = (bf16[256,768]{1,0:T(8,128)(2,1)S(1)}, bf16[256,768]{1,0:T(8,128)(2,1)S(1)}, f32[8,128]{1,0:T(8,128)S(1)}) custom-call(bf16[512,2048]{1,0:T(8,128)(2,1)S(1)} %get-tuple-element.37.onehot, bf16[2048,256]{1,0:T(8,128)(2,1)S(1)} %copy-done.3, bf16[2048,256]{1,0:T(8,128)(2,1)S(1)} %copy-done.1, bf16[2048,256]{1,0:T(8,128)(2,1)S(1)} %copy-done.2), custom_call_target="tpu_custom_call" | custom-call | flops 1610612736 | bytes 3145728 | tf_op jit(solution)/shard_map/sort_tokens/pallas_call | solution.py:140
  4.4 3.4 %collective-permute-start.1 = (bf16[256,768]{1,0:T(8,128)(2,1)S(1)}, bf16[256,768]{1,0:T(8,128)(2,1)S(1)}, u32[]{:S(2)}, u32[]{:S(2)}) collective-permute-start(bf16[256,768]{1,0:T(8,128)(2,1)S(1)} %get-tuple-element.41), channel_id=1, source_target_pairs={{0,28},{4,24},{8,20},{12,16},{16,12},{20,8},{24,4},{28,0},{1,29},{... | collective-permute-start | bytes 1179656 | tf_op jit(solution)/shard_map/ppermute | solution.py:488
  7.8 2.9 %gradients.1 = (f32[384,256]{1,0:T(8,128)S(1)}, bf16[384,256]{1,0:T(8,128)(2,1)S(1)}) custom-call(bf16[2048,256]{1,0:T(8,128)(2,1)S(1)} %copy-done.1, bf16[2048,256]{1,0:T(8,128)(2,1)S(1)} %copy-done.2, f32[1,2048]{1,0:T(1,128)S(1)} %bitcast.3, bf16[1,256,256]{2,1,0:T(8,128)(2,1)S(1)} %copy-done.4, bf16[1,256,256]{2,1,0:T(8,128)(2,1)S(1)} %copy-done.5, ...), custom_call_target="tpu_custom_call" | custom-call | flops 1610612736 | bytes 4194304 | tf_op jit(solution)/shard_map/gradients/pallas_call | solution.py:236
  10.7 0.7 %collective-permute-start = (bf16[384,256]{1,0:T(8,128)(2,1)S(1)}, bf16[384,256]{1,0:T(8,128)(2,1)S(1)}, u32[]{:S(2)}, u32[]{:S(2)}) collective-permute-start(bf16[384,256]{1,0:T(8,128)(2,1)S(1)} %get-tuple-element.40), channel_id=1, source_target_pairs={{0,4},{4,0},{8,12},{12,8},{16,20},{20,16},{24,28},{28,24},{1,5},{5... | collective-permute-start | bytes 589832 | tf_op jit(solution)/shard_map/ppermute | solution.py:270
  11.4 1.1 %collective-permute-done.got_ref = bf16[384,256]{1,0:T(8,128)(2,1)S(1)} collective-permute-done((bf16[384,256]{1,0:T(8,128)(2,1)S(1)}, bf16[384,256]{1,0:T(8,128)(2,1)S(1)}, u32[]{:S(2)}, u32[]{:S(2)}) %collective-permute-start) | collective-permute-done | bytes 196640 | tf_op jit(solution)/shard_map/ppermute | solution.py:270
  12.5 4.8 %collective-permute-done.1.rest_0_.refs_7_ = bf16[256,768]{1,0:T(8,128)(2,1)S(1)} collective-permute-done((bf16[256,768]{1,0:T(8,128)(2,1)S(1)}, bf16[256,768]{1,0:T(8,128)(2,1)S(1)}, u32[]{:S(2)}, u32[]{:S(2)}) %collective-permute-start.1) | collective-permute-done | bytes 393248 | tf_op jit(solution)/shard_map/ppermute | solution.py:488
  17.4 2.5 %collective-permute-start.2 = (bf16[384,256]{1,0:T(8,128)(2,1)S(1)}, bf16[384,256]{1,0:T(8,128)(2,1)S(1)}, u32[]{:S(2)}, u32[]{:S(2)}) collective-permute-start(bf16[384,256]{1,0:T(8,128)(2,1)S(1)} %convert_element_type.6), channel_id=1, source_target_pairs={{0,8},{4,20},{8,0},{12,28},{16,24},{20,4},{24,16},{28,12},{1,9},{5... | collective-permute-start | bytes 589832 | tf_op jit(solution)/shard_map/ppermute | solution.py:282
  19.8 1.8 %sort_tokens.4 = (bf16[256,768]{1,0:T(8,128)(2,1)S(1)}, bf16[256,768]{1,0:T(8,128)(2,1)S(1)}, f32[8,128]{1,0:T(8,128)S(1)}) custom-call(bf16[512,2048]{1,0:T(8,128)(2,1)S(1)} %get-tuple-element.42.onehot, bf16[2048,256]{1,0:T(8,128)(2,1)S(1)} %copy-done.3, bf16[2048,256]{1,0:T(8,128)(2,1)S(1)} %copy-done.1, bf16[2048,256]{1,0:T(8,128)(2,1)S(1)} %copy-done.2), custom_call_target="tpu_custom_call" | custom-call | flops 1610612736 | bytes 3145728 | tf_op jit(solution)/shard_map/sort_tokens/pallas_call | solution.py:140
  21.7 1.6 %collective-permute-start.7 = (bf16[256,768]{1,0:T(8,128)(2,1)S(1)}, bf16[256,768]{1,0:T(8,128)(2,1)S(1)}, u32[]{:S(2)}, u32[]{:S(2)}) collective-permute-start(bf16[256,768]{1,0:T(8,128)(2,1)S(1)} %get-tuple-element.49), channel_id=1, source_target_pairs={{0,16},{4,12},{8,24},{12,4},{16,0},{20,28},{24,8},{28,20},{1,17},{... | collective-permute-start | bytes 1179656 | tf_op jit(solution)/shard_map/ppermute | solution.py:488
  23.3 1.7 %place.1 = (bf16[2048,1536]{1,0:T(8,128)(2,1)S(1)}, bf16[2048,512]{1,0:T(8,128)(2,1)S(1)}) custom-call(s32[1,2048]{1,0:T(1,128)S(1)} %copy-done.9), custom_call_target="tpu_custom_call" | custom-call | flops 4194304 | bytes 8388608 | tf_op jit(solution)/shard_map/place/pallas_call | solution.py:374
  25.0 6.0 %collective-permute-done.2.got_ref = bf16[384,256]{1,0:T(8,128)(2,1)S(1)} collective-permute-done((bf16[384,256]{1,0:T(8,128)(2,1)S(1)}, bf16[384,256]{1,0:T(8,128)(2,1)S(1)}, u32[]{:S(2)}, u32[]{:S(2)}) %collective-permute-start.2) | collective-permute-done | bytes 196640 | tf_op jit(solution)/shard_map/ppermute | solution.py:282
  31.1 3.4 %sort_tokens.5 = (bf16[256,768]{1,0:T(8,128)(2,1)S(1)}, bf16[256,768]{1,0:T(8,128)(2,1)S(1)}, bf16[256,768]{1,0:T(8,128)(2,1)S(1)}, bf16[256,768]{1,0:T(8,128)(2,1)S(1)}, f32[8,128]{1,0:T(8,128)S(1)}) custom-call(bf16[1024,2048]{1,0:T(8,128)(2,1)S(1)} %get-tuple-element.46.onehot, bf16[2048,256]{1,0:T(8,128)(2,1)S(1)} %copy-done.3, ...), custom_call_target="tpu_custom_call" | custom-call | flops 3221225472 | bytes 3145728 | tf_op jit(solution)/shard_map/sort_tokens/pallas_call | solution.py:140
  34.6 4.0 %collective-permute-done.3.got_ref = bf16[384,256]{1,0:T(8,128)(2,1)S(1)} collective-permute-done((bf16[384,256]{1,0:T(8,128)(2,1)S(1)}, bf16[384,256]{1,0:T(8,128)(2,1)S(1)}, u32[]{:S(2)}, u32[]{:S(2)}) %collective-permute-start.3) | collective-permute-done | bytes 196640 | tf_op jit(solution)/shard_map/ppermute | solution.py:282
  38.6 0.7 %collective-permute-start.6 = (f32[384,256]{1,0:T(8,128)S(1)}, f32[384,256]{1,0:T(8,128)S(1)}, u32[]{:S(2)}, u32[]{:S(2)}) collective-permute-start(f32[384,256]{1,0:T(8,128)S(1)} %merge.5.rest_0_), channel_id=1, source_target_pairs={{0,4},{4,0},{8,12},{12,8},{16,20},{20,16},{24,28},{28,24},{1,5},{5... | collective-permute-start | bytes 1179656 | tf_op jit(solution)/shard_map/ppermute | solution.py:287
  39.4 2.0 %collective-permute-start.11 = (bf16[256,768]{1,0:T(8,128)(2,1)S(1)}, bf16[256,768]{1,0:T(8,128)(2,1)S(1)}, u32[]{:S(2)}, u32[]{:S(2)}) collective-permute-start(bf16[256,768]{1,0:T(8,128)(2,1)S(1)} %get-tuple-element.55), channel_id=1, source_target_pairs={{0,8},{4,20},{8,0},{12,28},{16,24},{20,4},{24,16},{28,12},{1,9},{5... | collective-permute-start | bytes 1179656 | tf_op jit(solution)/shard_map/ppermute | solution.py:488
  41.4 0.9 %collective-permute-start.12 = (bf16[256,768]{1,0:T(8,128)(2,1)S(1)}, bf16[256,768]{1,0:T(8,128)(2,1)S(1)}, u32[]{:S(2)}, u32[]{:S(2)}) collective-permute-start(bf16[256,768]{1,0:T(8,128)(2,1)S(1)} %get-tuple-element.56), channel_id=1, source_target_pairs={{0,12},{4,16},{8,4},{12,24},{16,28},{20,0},{24,20},{28,8},{1,13},{... | collective-permute-start | bytes 1179656 | tf_op jit(solution)/shard_map/ppermute | solution.py:488
  42.3 2.7 %read_out.1 = (f32[2048,256]{1,0:T(8,128)S(1)}, f32[1,2048]{1,0:T(1,128)S(1)}) custom-call(bf16[2048,256]{1,0:T(8,128)(2,1)S(1)} %copy-done.3, bf16[1,256,256]{2,1,0:T(8,128)(2,1)S(1)} %copy-done.4, bf16[1,256,256]{2,1,0:T(8,128)(2,1)S(1)} %copy-done.5, bf16[1,256,256]{2,1,0:T(8,128)(2,1)S(1)} %copy-done.6, f32[384,256]{1,0:T(8,128)S(1)} %merge.5.rest_0_, ...), custom_call_target="tpu_custom_call" | custom-call | flops 805306368 | bytes 4194304 | tf_op jit(solution)/shard_map/read_out/pallas_call | solution.py:334
  45.0 1.6 %collective-permute-start.8 = (f32[1,2048]{1,0:T(1,128)S(1)}, f32[1,2048]{1,0:T(1,128)S(1)}, u32[]{:S(2)}, u32[]{:S(2)}) collective-permute-start(f32[1,2048]{1,0:T(1,128)S(1)} %get-tuple-element.52), channel_id=1, source_target_pairs={{0,1},{1,0},{2,3},{3,2},{4,5},{5,4},{6,7},{7,6},{8,9},{9,8},{10,11... | collective-permute-start | bytes 24584 | tf_op jit(solution)/shard_map/ppermute | solution.py:464
  46.6 2.1 %collective-permute-done.8 = f32[1,2048]{1,0:T(1,128)S(1)} collective-permute-done((f32[1,2048]{1,0:T(1,128)S(1)}, f32[1,2048]{1,0:T(1,128)S(1)}, u32[]{:S(2)}, u32[]{:S(2)}) %collective-permute-start.8) | collective-permute-done | bytes 8224 | tf_op jit(solution)/shard_map/ppermute | solution.py:464
  48.7 2.7 %collective-permute-start.9 = (f32[1,2048]{1,0:T(1,128)S(1)}, f32[1,2048]{1,0:T(1,128)S(1)}, u32[]{:S(2)}, u32[]{:S(2)}) collective-permute-start(f32[1,2048]{1,0:T(1,128)S(1)} %add.6.refs_8_), channel_id=1, source_target_pairs={{0,2},{1,3},{2,0},{3,1},{4,6},{5,7},{6,4},{7,5},{8,10},{9,11},{10,... | collective-permute-start | bytes 24584 | tf_op jit(solution)/shard_map/ppermute | solution.py:464
  51.4 1.5 %attend.1 = (bf16[256,256]{1,0:T(8,128)(2,1)S(1)}, bf16[256,256]{1,0:T(8,128)(2,1)S(1)}, bf16[256,256]{1,0:T(8,128)(2,1)S(1)}, bf16[256,256]{1,0:T(8,128)(2,1)S(...) custom-call(bf16[256,768]{1,0:T(8,128)(2,1)S(1)} %get-tuple-element., ...), custom_call_target="tpu_custom_call" | custom-call | flops 536870912 | bytes 4194304 | tf_op jit(solution)/shard_map/attend/pallas_call | solution.py:179
  52.9 2.7 %collective-permute-start.13 = (bf16[256,256]{1,0:T(8,128)(2,1)S(1)}, bf16[256,256]{1,0:T(8,128)(2,1)S(1)}, u32[]{:S(2)}, u32[]{:S(2)}) collective-permute-start(bf16[256,256]{1,0:T(8,128)(2,1)S(1)} %get-tuple-element.57), channel_id=1, source_target_pairs={{28,0},{24,4},{20,8},{16,12},{12,16},{8,20},{4,24},{0,28},{29,1},{... | collective-permute-start | bytes 393224 | tf_op jit(solution)/shard_map/ppermute | solution.py:493
  55.6 0.8 %collective-permute-start.15 = (bf16[256,256]{1,0:T(8,128)(2,1)S(1)}, bf16[256,256]{1,0:T(8,128)(2,1)S(1)}, u32[]{:S(2)}, u32[]{:S(2)}) collective-permute-start(bf16[256,256]{1,0:T(8,128)(2,1)S(1)} %get-tuple-element.59), channel_id=1, source_target_pairs={{20,0},{8,4},{28,8},{0,12},{4,16},{24,20},{12,24},{16,28},{21,1},{... | collective-permute-start | bytes 393224 | tf_op jit(solution)/shard_map/ppermute | solution.py:493
  56.5 1.5 %collective-permute-start.16 = (bf16[256,256]{1,0:T(8,128)(2,1)S(1)}, bf16[256,256]{1,0:T(8,128)(2,1)S(1)}, u32[]{:S(2)}, u32[]{:S(2)}) collective-permute-start(bf16[256,256]{1,0:T(8,128)(2,1)S(1)} %get-tuple-element.60), channel_id=1, source_target_pairs={{16,0},{12,4},{24,8},{4,12},{0,16},{28,20},{8,24},{20,28},{17,1},{... | collective-permute-start | bytes 393224 | tf_op jit(solution)/shard_map/ppermute | solution.py:493
  58.0 1.1 %collective-permute-start.17 = (bf16[256,256]{1,0:T(8,128)(2,1)S(1)}, bf16[256,256]{1,0:T(8,128)(2,1)S(1)}, u32[]{:S(2)}, u32[]{:S(2)}) collective-permute-start(bf16[256,256]{1,0:T(8,128)(2,1)S(1)} %get-tuple-element.65), channel_id=1, source_target_pairs={{4,0},{0,4},{12,8},{8,12},{20,16},{16,20},{28,24},{24,28},{5,1},{1... | collective-permute-start | bytes 393224 | tf_op jit(solution)/shard_map/ppermute | solution.py:493
  59.7 1.4 %collective-permute-start.18 = (bf16[256,256]{1,0:T(8,128)(2,1)S(1)}, bf16[256,256]{1,0:T(8,128)(2,1)S(1)}, u32[]{:S(2)}, u32[]{:S(2)}) collective-permute-start(bf16[256,256]{1,0:T(8,128)(2,1)S(1)} %get-tuple-element.67), channel_id=1, source_target_pairs={{12,0},{16,4},{4,8},{24,12},{28,16},{0,20},{20,24},{8,28},{13,1},{... | collective-permute-start | bytes 393224 | tf_op jit(solution)/shard_map/ppermute | solution.py:493
  61.2 1.8 %collective-permute-done.14.rest_1_ = bf16[256,256]{1,0:T(8,128)(2,1)S(1)} collective-permute-done((bf16[256,256]{1,0:T(8,128)(2,1)S(1)}, bf16[256,256]{1,0:T(8,128)(2,1)S(1)}, u32[]{:S(2)}, u32[]{:S(2)}) %collective-permute-start.14) | collective-permute-done | bytes 131104 | tf_op jit(solution)/shard_map/ppermute | solution.py:493
  63.0 1.5 %collective-permute-start.19 = (bf16[256,256]{1,0:T(8,128)(2,1)S(1)}, bf16[256,256]{1,0:T(8,128)(2,1)S(1)}, u32[]{:S(2)}, u32[]{:S(2)}) collective-permute-start(bf16[256,256]{1,0:T(8,128)(2,1)S(1)} %get-tuple-element.68), channel_id=1, source_target_pairs={{8,0},{20,4},{0,8},{28,12},{24,16},{4,20},{16,24},{12,28},{9,1},{2... | collective-permute-start | bytes 393224 | tf_op jit(solution)/shard_map/ppermute | solution.py:493
  65.4 1.8 %base.1.base_ref = f32[2048,256]{1,0:T(8,128)S(1)} custom-call(f32[1,256]{1,0:T(1,128)S(1)} %bitcast.2, f32[2048,256]{1,0:T(8,128)S(1)} %get-tuple-element.50.y_ref, bf16[2048,1536]{1,0:T(8,128)(2,1)S(1)} %get-tuple-element.51.onehot, f32[1,2048]{1,0:T(1,128)S(1)} %add.7.refs_4_.total_ref, bf16[256,256]{1,0:T(8,128)(2,1)S(1)} %collective-permute-done.13.rest_0_, ...), custom_call_target="tpu_custom_call" | custom-call | flops 1610612736 | bytes 4194304 | tf_op jit(solution)/shard_map/base/pallas_call | solution.py:412
  67.2 0.8 %collective-permute-done.19.rest_1_ = bf16[256,256]{1,0:T(8,128)(2,1)S(1)} collective-permute-done((bf16[256,256]{1,0:T(8,128)(2,1)S(1)}, bf16[256,256]{1,0:T(8,128)(2,1)S(1)}, u32[]{:S(2)}, u32[]{:S(2)}) %collective-permute-start.19) | collective-permute-done | bytes 131104 | tf_op jit(solution)/shard_map/ppermute | solution.py:493
  68.0 1.6 %mix.1 = bf16[2048,256]{1,0:T(8,128)(2,1)} custom-call(f32[2048,256]{1,0:T(8,128)S(1)} %base.1.base_ref, bf16[2048,512]{1,0:T(8,128)(2,1)S(1)} %get-tuple-element.48.rest_3_.onehot, bf16[256,256]{1,0:T(8,128)(2,1)S(1)} %collective-permute-done.18.rest_0_, bf16[256,256]{1,0:T(8,128)(2,1)S(1)} %collective-permute-done.19.rest_1_), custom_call_target="tpu_custom_call" | custom-call | flops 536870912 | bytes 4194304 | tf_op jit(solution)/shard_map/mix/pallas_call | solution.py:440
  (46 shorter events, 3.1 us)
Async XLA Ops:
  0.0 0.7 copy-start.8
  0.7 1.4 %copy-start.1 = (bf16[2048,256]{1,0:T(8,128)(2,1)S(1)}, bf16[2048,256]{1,0:T(8,128)(2,1)}, u32[]{:S(2)}) copy-start(bf16[2048,256]{1,0:T(8,128)(2,1)} %k_ref.7) | copy-start | bytes 3145732
  0.7 1.5 %copy-start.2 = (bf16[2048,256]{1,0:T(8,128)(2,1)S(1)}, bf16[2048,256]{1,0:T(8,128)(2,1)}, u32[]{:S(2)}) copy-start(bf16[2048,256]{1,0:T(8,128)(2,1)} %v_ref.7) | copy-start | bytes 3145732
  0.7 1.9 %copy-start.3 = (bf16[2048,256]{1,0:T(8,128)(2,1)S(1)}, bf16[2048,256]{1,0:T(8,128)(2,1)}, u32[]{:S(2)}) copy-start(bf16[2048,256]{1,0:T(8,128)(2,1)} %q_ref.7) | copy-start | bytes 3145732
  2.6 5.2 %copy-start.4 = (bf16[1,256,256]{2,1,0:T(8,128)(2,1)S(1)}, bf16[1,256,256]{2,1,0:T(8,128)(2,1)}, u32[]{:S(2)}) copy-start(bf16[1,256,256]{2,1,0:T(8,128)(2,1)} %one_ref.3) | copy-start | bytes 393220
  2.6 5.2 %copy-start.5 = (bf16[1,256,256]{2,1,0:T(8,128)(2,1)S(1)}, bf16[1,256,256]{2,1,0:T(8,128)(2,1)}, u32[]{:S(2)}) copy-start(bf16[1,256,256]{2,1,0:T(8,128)(2,1)} %three_ref.3) | copy-start | bytes 393220
  2.6 5.2 %copy-start.6 = (bf16[1,256,256]{2,1,0:T(8,128)(2,1)S(1)}, bf16[1,256,256]{2,1,0:T(8,128)(2,1)}, u32[]{:S(2)}) copy-start(bf16[1,256,256]{2,1,0:T(8,128)(2,1)} %two_ref.3) | copy-start | bytes 393220
  2.6 5.2 %copy-start.7 = (f32[2048,1]{0,1:T(1,128)S(1)}, f32[2048,1]{0,1:T(1,128)}, u32[]{:S(2)}) copy-start(f32[2048,1]{0,1:T(1,128)} %param.12) | copy-start | bytes 24580
  4.4 12.9 %collective-permute-start.1 = (bf16[256,768]{1,0:T(8,128)(2,1)S(1)}, bf16[256,768]{1,0:T(8,128)(2,1)S(1)}, u32[]{:S(2)}, u32[]{:S(2)}) collective-permute-start(bf16[256,768]{1,0:T(8,128)(2,1)S(1)} %get-tuple-element.41), channel_id=1, source_target_pairs={{0,28},{4,24},{8,20},{12,16},{16,12},{20,8},{24,4},{28,0},{1,29},{... | collective-permute-start | bytes 1179656 | tf_op jit(solution)/shard_map/ppermute | solution.py:488
  10.7 1.8 %collective-permute-start = (bf16[384,256]{1,0:T(8,128)(2,1)S(1)}, bf16[384,256]{1,0:T(8,128)(2,1)S(1)}, u32[]{:S(2)}, u32[]{:S(2)}) collective-permute-start(bf16[384,256]{1,0:T(8,128)(2,1)S(1)} %get-tuple-element.40), channel_id=1, source_target_pairs={{0,4},{4,0},{8,12},{12,8},{16,20},{20,16},{24,28},{28,24},{1,5},{5... | collective-permute-start | bytes 589832 | tf_op jit(solution)/shard_map/ppermute | solution.py:270
  11.4 23.1 %collective-permute-start.4 = (bf16[256,768]{1,0:T(8,128)(2,1)S(1)}, bf16[256,768]{1,0:T(8,128)(2,1)S(1)}, u32[]{:S(2)}, u32[]{:S(2)}) collective-permute-start(bf16[256,768]{1,0:T(8,128)(2,1)S(1)} %get-tuple-element.44), channel_id=1, source_target_pairs={{0,24},{4,28},{8,16},{12,20},{16,8},{20,12},{24,0},{28,4},{1,25},{... | collective-permute-start | bytes 1179656 | tf_op jit(solution)/shard_map/ppermute | solution.py:488
  17.4 13.6 %collective-permute-start.2 = (bf16[384,256]{1,0:T(8,128)(2,1)S(1)}, bf16[384,256]{1,0:T(8,128)(2,1)S(1)}, u32[]{:S(2)}, u32[]{:S(2)}) collective-permute-start(bf16[384,256]{1,0:T(8,128)(2,1)S(1)} %convert_element_type.6), channel_id=1, source_target_pairs={{0,8},{4,20},{8,0},{12,28},{16,24},{20,4},{24,16},{28,12},{1,9},{5... | collective-permute-start | bytes 589832 | tf_op jit(solution)/shard_map/ppermute | solution.py:282
  19.8 3.4 %copy-start.9 = (s32[1,2048]{1,0:T(1,128)S(1)}, s32[1,2048]{1,0:T(1,128)}, u32[]{:S(2)}) copy-start(s32[1,2048]{1,0:T(1,128)} %order_ref.3) | copy-start | bytes 24580
  21.6 12.9 %collective-permute-start.5 = (bf16[256,768]{1,0:T(8,128)(2,1)S(1)}, bf16[256,768]{1,0:T(8,128)(2,1)S(1)}, u32[]{:S(2)}, u32[]{:S(2)}) collective-permute-start(bf16[256,768]{1,0:T(8,128)(2,1)S(1)} %get-tuple-element.45), channel_id=1, source_target_pairs={{0,20},{4,8},{8,28},{12,0},{16,4},{20,24},{24,12},{28,16},{1,21},{... | collective-permute-start | bytes 1179656 | tf_op jit(solution)/shard_map/ppermute | solution.py:488
  21.7 20.6 %collective-permute-start.7 = (bf16[256,768]{1,0:T(8,128)(2,1)S(1)}, bf16[256,768]{1,0:T(8,128)(2,1)S(1)}, u32[]{:S(2)}, u32[]{:S(2)}) collective-permute-start(bf16[256,768]{1,0:T(8,128)(2,1)S(1)} %get-tuple-element.49), channel_id=1, source_target_pairs={{0,16},{4,12},{8,24},{12,4},{16,0},{20,28},{24,8},{28,20},{1,17},{... | collective-permute-start | bytes 1179656 | tf_op jit(solution)/shard_map/ppermute | solution.py:488
  31.0 7.5 %collective-permute-start.3 = (bf16[384,256]{1,0:T(8,128)(2,1)S(1)}, bf16[384,256]{1,0:T(8,128)(2,1)S(1)}, u32[]{:S(2)}, u32[]{:S(2)}) collective-permute-start(bf16[384,256]{1,0:T(8,128)(2,1)S(1)} %convert_element_type.7), channel_id=1, source_target_pairs={{0,16},{4,12},{8,24},{12,4},{16,0},{20,28},{24,8},{28,20},{1,17},{... | collective-permute-start | bytes 589832 | tf_op jit(solution)/shard_map/ppermute | solution.py:282
  38.6 3.7 %collective-permute-start.6 = (f32[384,256]{1,0:T(8,128)S(1)}, f32[384,256]{1,0:T(8,128)S(1)}, u32[]{:S(2)}, u32[]{:S(2)}) collective-permute-start(f32[384,256]{1,0:T(8,128)S(1)} %merge.5.rest_0_), channel_id=1, source_target_pairs={{0,4},{4,0},{8,12},{12,8},{16,20},{20,16},{24,28},{28,24},{1,5},{5... | collective-permute-start | bytes 1179656 | tf_op jit(solution)/shard_map/ppermute | solution.py:287
  39.3 12.1 %collective-permute-start.10 = (bf16[256,768]{1,0:T(8,128)(2,1)S(1)}, bf16[256,768]{1,0:T(8,128)(2,1)S(1)}, u32[]{:S(2)}, u32[]{:S(2)}) collective-permute-start(bf16[256,768]{1,0:T(8,128)(2,1)S(1)} %get-tuple-element.54), channel_id=1, source_target_pairs={{0,4},{4,0},{8,12},{12,8},{16,20},{20,16},{24,28},{28,24},{1,5},{5... | collective-permute-start | bytes 1179656 | tf_op jit(solution)/shard_map/ppermute | solution.py:488
  39.4 12.0 %collective-permute-start.11 = (bf16[256,768]{1,0:T(8,128)(2,1)S(1)}, bf16[256,768]{1,0:T(8,128)(2,1)S(1)}, u32[]{:S(2)}, u32[]{:S(2)}) collective-permute-start(bf16[256,768]{1,0:T(8,128)(2,1)S(1)} %get-tuple-element.55), channel_id=1, source_target_pairs={{0,8},{4,20},{8,0},{12,28},{16,24},{20,4},{24,16},{28,12},{1,9},{5... | collective-permute-start | bytes 1179656 | tf_op jit(solution)/shard_map/ppermute | solution.py:488
  41.4 10.0 %collective-permute-start.12 = (bf16[256,768]{1,0:T(8,128)(2,1)S(1)}, bf16[256,768]{1,0:T(8,128)(2,1)S(1)}, u32[]{:S(2)}, u32[]{:S(2)}) collective-permute-start(bf16[256,768]{1,0:T(8,128)(2,1)S(1)} %get-tuple-element.56), channel_id=1, source_target_pairs={{0,12},{4,16},{8,4},{12,24},{16,28},{20,0},{24,20},{28,8},{1,13},{... | collective-permute-start | bytes 1179656 | tf_op jit(solution)/shard_map/ppermute | solution.py:488
  45.0 20.4 %copy-start = (f32[256]{0:T(256)S(1)}, f32[256]{0:T(256)}, u32[]{:S(2)}) copy-start(f32[256]{0:T(256)} %param.16) | copy-start | bytes 3076
  45.0 3.7 %collective-permute-start.8 = (f32[1,2048]{1,0:T(1,128)S(1)}, f32[1,2048]{1,0:T(1,128)S(1)}, u32[]{:S(2)}, u32[]{:S(2)}) collective-permute-start(f32[1,2048]{1,0:T(1,128)S(1)} %get-tuple-element.52), channel_id=1, source_target_pairs={{0,1},{1,0},{2,3},{3,2},{4,5},{5,4},{6,7},{7,6},{8,9},{9,8},{10,11... | collective-permute-start | bytes 24584 | tf_op jit(solution)/shard_map/ppermute | solution.py:464
  48.7 9.3 %collective-permute-start.9 = (f32[1,2048]{1,0:T(1,128)S(1)}, f32[1,2048]{1,0:T(1,128)S(1)}, u32[]{:S(2)}, u32[]{:S(2)}) collective-permute-start(f32[1,2048]{1,0:T(1,128)S(1)} %add.6.refs_8_), channel_id=1, source_target_pairs={{0,2},{1,3},{2,0},{3,1},{4,6},{5,7},{6,4},{7,5},{8,10},{9,11},{10,... | collective-permute-start | bytes 24584 | tf_op jit(solution)/shard_map/ppermute | solution.py:464
  52.9 6.9 %collective-permute-start.13 = (bf16[256,256]{1,0:T(8,128)(2,1)S(1)}, bf16[256,256]{1,0:T(8,128)(2,1)S(1)}, u32[]{:S(2)}, u32[]{:S(2)}) collective-permute-start(bf16[256,256]{1,0:T(8,128)(2,1)S(1)} %get-tuple-element.57), channel_id=1, source_target_pairs={{28,0},{24,4},{20,8},{16,12},{12,16},{8,20},{4,24},{0,28},{29,1},{... | collective-permute-start | bytes 393224 | tf_op jit(solution)/shard_map/ppermute | solution.py:493
  55.6 7.4 %collective-permute-start.14 = (bf16[256,256]{1,0:T(8,128)(2,1)S(1)}, bf16[256,256]{1,0:T(8,128)(2,1)S(1)}, u32[]{:S(2)}, u32[]{:S(2)}) collective-permute-start(bf16[256,256]{1,0:T(8,128)(2,1)S(1)} %get-tuple-element.58), channel_id=1, source_target_pairs={{24,0},{28,4},{16,8},{20,12},{8,16},{12,20},{0,24},{4,28},{25,1},{... | collective-permute-start | bytes 393224 | tf_op jit(solution)/shard_map/ppermute | solution.py:493
  55.6 9.6 %collective-permute-start.15 = (bf16[256,256]{1,0:T(8,128)(2,1)S(1)}, bf16[256,256]{1,0:T(8,128)(2,1)S(1)}, u32[]{:S(2)}, u32[]{:S(2)}) collective-permute-start(bf16[256,256]{1,0:T(8,128)(2,1)S(1)} %get-tuple-element.59), channel_id=1, source_target_pairs={{20,0},{8,4},{28,8},{0,12},{4,16},{24,20},{12,24},{16,28},{21,1},{... | collective-permute-start | bytes 393224 | tf_op jit(solution)/shard_map/ppermute | solution.py:493
  56.5 8.9 %collective-permute-start.16 = (bf16[256,256]{1,0:T(8,128)(2,1)S(1)}, bf16[256,256]{1,0:T(8,128)(2,1)S(1)}, u32[]{:S(2)}, u32[]{:S(2)}) collective-permute-start(bf16[256,256]{1,0:T(8,128)(2,1)S(1)} %get-tuple-element.60), channel_id=1, source_target_pairs={{16,0},{12,4},{24,8},{4,12},{0,16},{28,20},{8,24},{20,28},{17,1},{... | collective-permute-start | bytes 393224 | tf_op jit(solution)/shard_map/ppermute | solution.py:493
  58.0 7.3 %collective-permute-start.17 = (bf16[256,256]{1,0:T(8,128)(2,1)S(1)}, bf16[256,256]{1,0:T(8,128)(2,1)S(1)}, u32[]{:S(2)}, u32[]{:S(2)}) collective-permute-start(bf16[256,256]{1,0:T(8,128)(2,1)S(1)} %get-tuple-element.65), channel_id=1, source_target_pairs={{4,0},{0,4},{12,8},{8,12},{20,16},{16,20},{28,24},{24,28},{5,1},{1... | collective-permute-start | bytes 393224 | tf_op jit(solution)/shard_map/ppermute | solution.py:493
  59.7 7.5 %collective-permute-start.18 = (bf16[256,256]{1,0:T(8,128)(2,1)S(1)}, bf16[256,256]{1,0:T(8,128)(2,1)S(1)}, u32[]{:S(2)}, u32[]{:S(2)}) collective-permute-start(bf16[256,256]{1,0:T(8,128)(2,1)S(1)} %get-tuple-element.67), channel_id=1, source_target_pairs={{12,0},{16,4},{4,8},{24,12},{28,16},{0,20},{20,24},{8,28},{13,1},{... | collective-permute-start | bytes 393224 | tf_op jit(solution)/shard_map/ppermute | solution.py:493
  63.0 5.0 %collective-permute-start.19 = (bf16[256,256]{1,0:T(8,128)(2,1)S(1)}, bf16[256,256]{1,0:T(8,128)(2,1)S(1)}, u32[]{:S(2)}, u32[]{:S(2)}) collective-permute-start(bf16[256,256]{1,0:T(8,128)(2,1)S(1)} %get-tuple-element.68), channel_id=1, source_target_pairs={{8,0},{20,4},{0,8},{28,12},{24,16},{4,20},{16,24},{12,28},{9,1},{2... | collective-permute-start | bytes 393224 | tf_op jit(solution)/shard_map/ppermute | solution.py:493

commit v17 on v16

--- a/solution.py
+++ b/solution.py
@@ -511,8 +511,8 @@
             arrived[step] = exchange(block, step, n)
     came = [arrived[step] for step in steps]
     parts = gradients(keys, values, rates.reshape(1, count), *weights, tokens[0], n)
-    early = steps[: 2 * few] + steps[n - few :]
-    late = steps[2 * few : n - few]
+    early = steps[: 2 * few + 1] + steps[-1:]
+    late = steps[2 * few + 1 : -1]
     early_places, late_places = place(order, n, early, late)
     mine = core_step(parts, [came[0]], n)
     summed = sum_over_chips(mine, len(parts) == 2, [tokens[1:2], came[1:3] + tokens[2:] + [late_places]], n)

time: 69.9 us -> 71.3 us (1.020)
  waiting for transfers between devices: 22 us -> 25.7 us
  starting transfers between devices: 25.4 us -> 22.5 us
    ppermute x7, waiting for transfers between devices: 4.14 us -> 7.81 us  [give_back(): return lax.ppermute(block, 'cam', pairs) if step else block]
    ppermute x7, starting transfers between devices: 9.04 us -> 6.16 us  [give_back(): return lax.ppermute(block, 'cam', pairs) if step else block]
where the time goes in v17:
time: 71.3 us; the launch traced here: 70.5 us
  waiting for transfers between devices  25.7 us (36%)
  starting transfers between devices  22.5 us (32%)
  Pallas kernels  20.7 us (29%)
  local copies, waits for them, and re-layouts  1.16 us (2%)
    ppermute x2, waiting for transfers between devices, sum_over_chips(): got = lax.ppermute(mine.astype(BF16), 'cam', pairs)  9.95 us
    ppermute x7, starting transfers between devices, exchange(): return lax.ppermute(block, 'cam', routes(step, n)) if step else block  8.04 us
    ppermute x7, waiting for transfers between devices, give_back(): return lax.ppermute(block, 'cam', pairs) if step else block  7.81 us
    pallas_call x3, Pallas kernels, sort_tokens(): pl.pallas_call(functools.partial(sort_kernel, size), out_shape=[jax.Shape...  7.02 us
    ppermute x7, starting transfers between devices, give_back(): return lax.ppermute(block, 'cam', pairs) if step else block  6.16 us
    ppermute x7, waiting for transfers between devices, exchange(): return lax.ppermute(block, 'cam', routes(step, n)) if step else block  4.79 us
    ppermute x2, starting transfers between devices, head_sum(): got = lax.ppermute(square, 'head', pairs)  4.27 us
    pallas_call x1, Pallas kernels, gradients(): pl.pallas_call(functools.partial(grads_kernel, n, split), out_shape=[jax....  2.9 us
  transfers between devices with their start and end apart: 20, of which 10 were waited for; matrix products, arithmetic and copies ran while one was open for 0% of the time, Pallas kernels for 23%

profile of v17, /device:TPU:0, one launch (start us, length us, event | category | flops | bytes accessed | tf_op | source)
XLA Modules:
  0.0 70.5 jit_solution(5645874026751366710)
XLA Ops:
  0.7 1.4 %mark.1 = (bf16[512,2048]{1,0:T(8,128)(2,1)S(1)}, bf16[512,2048]{1,0:T(8,128)(2,1)S(1)}, bf16[1024,2048]{1,0:T(8,128)(2,1)S(1)}, f32[8,128]{1,0:T(8,128)}) custom-call(s32[1,2048]{1,0:T(1,128)S(1)} %copy-done.8), custom_call_target="tpu_custom_call" | custom-call | flops 999999995904 | bytes 1024 | tf_op jit(solution)/shard_map/mark/pallas_call | solution.py:107
  2.6 1.8 %sort_tokens.3 = (bf16[256,768]{1,0:T(8,128)(2,1)S(1)}, bf16[256,768]{1,0:T(8,128)(2,1)S(1)}, f32[8,128]{1,0:T(8,128)S(1)}) custom-call(bf16[512,2048]{1,0:T(8,128)(2,1)S(1)} %get-tuple-element.37.onehot, bf16[2048,256]{1,0:T(8,128)(2,1)S(1)} %copy-done.3, bf16[2048,256]{1,0:T(8,128)(2,1)S(1)} %copy-done.1, bf16[2048,256]{1,0:T(8,128)(2,1)S(1)} %copy-done.2), custom_call_target="tpu_custom_call" | custom-call | flops 1610612736 | bytes 3145728 | tf_op jit(solution)/shard_map/sort_tokens/pallas_call | solution.py:140
  4.4 3.4 %collective-permute-start.1 = (bf16[256,768]{1,0:T(8,128)(2,1)S(1)}, bf16[256,768]{1,0:T(8,128)(2,1)S(1)}, u32[]{:S(2)}, u32[]{:S(2)}) collective-permute-start(bf16[256,768]{1,0:T(8,128)(2,1)S(1)} %get-tuple-element.41), channel_id=1, source_target_pairs={{0,28},{4,24},{8,20},{12,16},{16,12},{20,8},{24,4},{28,0},{1,29},{... | collective-permute-start | bytes 1179656 | tf_op jit(solution)/shard_map/ppermute | solution.py:488
  7.8 2.9 %gradients.1 = (f32[384,256]{1,0:T(8,128)S(1)}, bf16[384,256]{1,0:T(8,128)(2,1)S(1)}) custom-call(bf16[2048,256]{1,0:T(8,128)(2,1)S(1)} %copy-done.1, bf16[2048,256]{1,0:T(8,128)(2,1)S(1)} %copy-done.2, f32[1,2048]{1,0:T(1,128)S(1)} %bitcast.3, bf16[1,256,256]{2,1,0:T(8,128)(2,1)S(1)} %copy-done.4, bf16[1,256,256]{2,1,0:T(8,128)(2,1)S(1)} %copy-done.5, ...), custom_call_target="tpu_custom_call" | custom-call | flops 1610612736 | bytes 4194304 | tf_op jit(solution)/shard_map/gradients/pallas_call | solution.py:236
  10.7 0.7 %collective-permute-start = (bf16[384,256]{1,0:T(8,128)(2,1)S(1)}, bf16[384,256]{1,0:T(8,128)(2,1)S(1)}, u32[]{:S(2)}, u32[]{:S(2)}) collective-permute-start(bf16[384,256]{1,0:T(8,128)(2,1)S(1)} %get-tuple-element.40), channel_id=1, source_target_pairs={{0,4},{4,0},{8,12},{12,8},{16,20},{20,16},{24,28},{28,24},{1,5},{5... | collective-permute-start | bytes 589832 | tf_op jit(solution)/shard_map/ppermute | solution.py:270
  11.4 1.1 %collective-permute-done.got_ref = bf16[384,256]{1,0:T(8,128)(2,1)S(1)} collective-permute-done((bf16[384,256]{1,0:T(8,128)(2,1)S(1)}, bf16[384,256]{1,0:T(8,128)(2,1)S(1)}, u32[]{:S(2)}, u32[]{:S(2)}) %collective-permute-start) | collective-permute-done | bytes 196640 | tf_op jit(solution)/shard_map/ppermute | solution.py:270
  12.5 4.8 %collective-permute-done.1.rest_0_.refs_7_ = bf16[256,768]{1,0:T(8,128)(2,1)S(1)} collective-permute-done((bf16[256,768]{1,0:T(8,128)(2,1)S(1)}, bf16[256,768]{1,0:T(8,128)(2,1)S(1)}, u32[]{:S(2)}, u32[]{:S(2)}) %collective-permute-start.1) | collective-permute-done | bytes 393248 | tf_op jit(solution)/shard_map/ppermute | solution.py:488
  17.4 2.5 %collective-permute-start.2 = (bf16[384,256]{1,0:T(8,128)(2,1)S(1)}, bf16[384,256]{1,0:T(8,128)(2,1)S(1)}, u32[]{:S(2)}, u32[]{:S(2)}) collective-permute-start(bf16[384,256]{1,0:T(8,128)(2,1)S(1)} %convert_element_type.6), channel_id=1, source_target_pairs={{0,8},{4,20},{8,0},{12,28},{16,24},{20,4},{24,16},{28,12},{1,9},{5... | collective-permute-start | bytes 589832 | tf_op jit(solution)/shard_map/ppermute | solution.py:282
  19.8 1.8 %sort_tokens.4 = (bf16[256,768]{1,0:T(8,128)(2,1)S(1)}, bf16[256,768]{1,0:T(8,128)(2,1)S(1)}, f32[8,128]{1,0:T(8,128)S(1)}) custom-call(bf16[512,2048]{1,0:T(8,128)(2,1)S(1)} %get-tuple-element.42.onehot, bf16[2048,256]{1,0:T(8,128)(2,1)S(1)} %copy-done.3, bf16[2048,256]{1,0:T(8,128)(2,1)S(1)} %copy-done.1, bf16[2048,256]{1,0:T(8,128)(2,1)S(1)} %copy-done.2), custom_call_target="tpu_custom_call" | custom-call | flops 1610612736 | bytes 3145728 | tf_op jit(solution)/shard_map/sort_tokens/pallas_call | solution.py:140
  21.7 1.6 %collective-permute-start.7 = (bf16[256,768]{1,0:T(8,128)(2,1)S(1)}, bf16[256,768]{1,0:T(8,128)(2,1)S(1)}, u32[]{:S(2)}, u32[]{:S(2)}) collective-permute-start(bf16[256,768]{1,0:T(8,128)(2,1)S(1)} %get-tuple-element.49), channel_id=1, source_target_pairs={{0,16},{4,12},{8,24},{12,4},{16,0},{20,28},{24,8},{28,20},{1,17},{... | collective-permute-start | bytes 1179656 | tf_op jit(solution)/shard_map/ppermute | solution.py:488
  23.3 1.7 %place.1 = (bf16[2048,1536]{1,0:T(8,128)(2,1)S(1)}, bf16[2048,512]{1,0:T(8,128)(2,1)S(1)}) custom-call(s32[1,2048]{1,0:T(1,128)S(1)} %copy-done.9), custom_call_target="tpu_custom_call" | custom-call | flops 4194304 | bytes 8388608 | tf_op jit(solution)/shard_map/place/pallas_call | solution.py:374
  25.0 6.0 %collective-permute-done.2.got_ref = bf16[384,256]{1,0:T(8,128)(2,1)S(1)} collective-permute-done((bf16[384,256]{1,0:T(8,128)(2,1)S(1)}, bf16[384,256]{1,0:T(8,128)(2,1)S(1)}, u32[]{:S(2)}, u32[]{:S(2)}) %collective-permute-start.2) | collective-permute-done | bytes 196640 | tf_op jit(solution)/shard_map/ppermute | solution.py:282
  31.1 3.4 %sort_tokens.5 = (bf16[256,768]{1,0:T(8,128)(2,1)S(1)}, bf16[256,768]{1,0:T(8,128)(2,1)S(1)}, bf16[256,768]{1,0:T(8,128)(2,1)S(1)}, bf16[256,768]{1,0:T(8,128)(2,1)S(1)}, f32[8,128]{1,0:T(8,128)S(1)}) custom-call(bf16[1024,2048]{1,0:T(8,128)(2,1)S(1)} %get-tuple-element.46.onehot, bf16[2048,256]{1,0:T(8,128)(2,1)S(1)} %copy-done.3, ...), custom_call_target="tpu_custom_call" | custom-call | flops 3221225472 | bytes 3145728 | tf_op jit(solution)/shard_map/sort_tokens/pallas_call | solution.py:140
  34.6 4.0 %collective-permute-done.3.got_ref = bf16[384,256]{1,0:T(8,128)(2,1)S(1)} collective-permute-done((bf16[384,256]{1,0:T(8,128)(2,1)S(1)}, bf16[384,256]{1,0:T(8,128)(2,1)S(1)}, u32[]{:S(2)}, u32[]{:S(2)}) %collective-permute-start.3) | collective-permute-done | bytes 196640 | tf_op jit(solution)/shard_map/ppermute | solution.py:282
  38.6 0.7 %collective-permute-start.6 = (f32[384,256]{1,0:T(8,128)S(1)}, f32[384,256]{1,0:T(8,128)S(1)}, u32[]{:S(2)}, u32[]{:S(2)}) collective-permute-start(f32[384,256]{1,0:T(8,128)S(1)} %merge.5.rest_0_), channel_id=1, source_target_pairs={{0,4},{4,0},{8,12},{12,8},{16,20},{20,16},{24,28},{28,24},{1,5},{5... | collective-permute-start | bytes 1179656 | tf_op jit(solution)/shard_map/ppermute | solution.py:287
  39.4 2.0 %collective-permute-start.11 = (bf16[256,768]{1,0:T(8,128)(2,1)S(1)}, bf16[256,768]{1,0:T(8,128)(2,1)S(1)}, u32[]{:S(2)}, u32[]{:S(2)}) collective-permute-start(bf16[256,768]{1,0:T(8,128)(2,1)S(1)} %get-tuple-element.55), channel_id=1, source_target_pairs={{0,8},{4,20},{8,0},{12,28},{16,24},{20,4},{24,16},{28,12},{1,9},{5... | collective-permute-start | bytes 1179656 | tf_op jit(solution)/shard_map/ppermute | solution.py:488
  41.4 0.9 %collective-permute-start.12 = (bf16[256,768]{1,0:T(8,128)(2,1)S(1)}, bf16[256,768]{1,0:T(8,128)(2,1)S(1)}, u32[]{:S(2)}, u32[]{:S(2)}) collective-permute-start(bf16[256,768]{1,0:T(8,128)(2,1)S(1)} %get-tuple-element.56), channel_id=1, source_target_pairs={{0,12},{4,16},{8,4},{12,24},{16,28},{20,0},{24,20},{28,8},{1,13},{... | collective-permute-start | bytes 1179656 | tf_op jit(solution)/shard_map/ppermute | solution.py:488
  42.3 2.7 %read_out.1 = (f32[2048,256]{1,0:T(8,128)S(1)}, f32[1,2048]{1,0:T(1,128)S(1)}) custom-call(bf16[2048,256]{1,0:T(8,128)(2,1)S(1)} %copy-done.3, bf16[1,256,256]{2,1,0:T(8,128)(2,1)S(1)} %copy-done.4, bf16[1,256,256]{2,1,0:T(8,128)(2,1)S(1)} %copy-done.5, bf16[1,256,256]{2,1,0:T(8,128)(2,1)S(1)} %copy-done.6, f32[384,256]{1,0:T(8,128)S(1)} %merge.5.rest_0_, ...), custom_call_target="tpu_custom_call" | custom-call | flops 805306368 | bytes 4194304 | tf_op jit(solution)/shard_map/read_out/pallas_call | solution.py:334
  45.0 1.6 %collective-permute-start.8 = (f32[1,2048]{1,0:T(1,128)S(1)}, f32[1,2048]{1,0:T(1,128)S(1)}, u32[]{:S(2)}, u32[]{:S(2)}) collective-permute-start(f32[1,2048]{1,0:T(1,128)S(1)} %get-tuple-element.52), channel_id=1, source_target_pairs={{0,1},{1,0},{2,3},{3,2},{4,5},{5,4},{6,7},{7,6},{8,9},{9,8},{10,11... | collective-permute-start | bytes 24584 | tf_op jit(solution)/shard_map/ppermute | solution.py:464
  46.6 2.1 %collective-permute-done.8 = f32[1,2048]{1,0:T(1,128)S(1)} collective-permute-done((f32[1,2048]{1,0:T(1,128)S(1)}, f32[1,2048]{1,0:T(1,128)S(1)}, u32[]{:S(2)}, u32[]{:S(2)}) %collective-permute-start.8) | collective-permute-done | bytes 8224 | tf_op jit(solution)/shard_map/ppermute | solution.py:464
  48.7 2.7 %collective-permute-start.9 = (f32[1,2048]{1,0:T(1,128)S(1)}, f32[1,2048]{1,0:T(1,128)S(1)}, u32[]{:S(2)}, u32[]{:S(2)}) collective-permute-start(f32[1,2048]{1,0:T(1,128)S(1)} %add.6.refs_8_), channel_id=1, source_target_pairs={{0,2},{1,3},{2,0},{3,1},{4,6},{5,7},{6,4},{7,5},{8,10},{9,11},{10,... | collective-permute-start | bytes 24584 | tf_op jit(solution)/shard_map/ppermute | solution.py:464
  51.4 1.5 %attend.1 = (bf16[256,256]{1,0:T(8,128)(2,1)S(1)}, bf16[256,256]{1,0:T(8,128)(2,1)S(1)}, bf16[256,256]{1,0:T(8,128)(2,1)S(1)}, bf16[256,256]{1,0:T(8,128)(2,1)S(...) custom-call(bf16[256,768]{1,0:T(8,128)(2,1)S(1)} %get-tuple-element., ...), custom_call_target="tpu_custom_call" | custom-call | flops 536870912 | bytes 4194304 | tf_op jit(solution)/shard_map/attend/pallas_call | solution.py:179
  52.9 2.7 %collective-permute-start.13 = (bf16[256,256]{1,0:T(8,128)(2,1)S(1)}, bf16[256,256]{1,0:T(8,128)(2,1)S(1)}, u32[]{:S(2)}, u32[]{:S(2)}) collective-permute-start(bf16[256,256]{1,0:T(8,128)(2,1)S(1)} %get-tuple-element.57), channel_id=1, source_target_pairs={{28,0},{24,4},{20,8},{16,12},{12,16},{8,20},{4,24},{0,28},{29,1},{... | collective-permute-start | bytes 393224 | tf_op jit(solution)/shard_map/ppermute | solution.py:493
  55.6 0.8 %collective-permute-start.15 = (bf16[256,256]{1,0:T(8,128)(2,1)S(1)}, bf16[256,256]{1,0:T(8,128)(2,1)S(1)}, u32[]{:S(2)}, u32[]{:S(2)}) collective-permute-start(bf16[256,256]{1,0:T(8,128)(2,1)S(1)} %get-tuple-element.59), channel_id=1, source_target_pairs={{20,0},{8,4},{28,8},{0,12},{4,16},{24,20},{12,24},{16,28},{21,1},{... | collective-permute-start | bytes 393224 | tf_op jit(solution)/shard_map/ppermute | solution.py:493
  56.5 1.5 %collective-permute-start.16 = (bf16[256,256]{1,0:T(8,128)(2,1)S(1)}, bf16[256,256]{1,0:T(8,128)(2,1)S(1)}, u32[]{:S(2)}, u32[]{:S(2)}) collective-permute-start(bf16[256,256]{1,0:T(8,128)(2,1)S(1)} %get-tuple-element.60), channel_id=1, source_target_pairs={{16,0},{12,4},{24,8},{4,12},{0,16},{28,20},{8,24},{20,28},{17,1},{... | collective-permute-start | bytes 393224 | tf_op jit(solution)/shard_map/ppermute | solution.py:493
  58.0 0.9 %collective-permute-start.17 = (bf16[256,256]{1,0:T(8,128)(2,1)S(1)}, bf16[256,256]{1,0:T(8,128)(2,1)S(1)}, u32[]{:S(2)}, u32[]{:S(2)}) collective-permute-start(bf16[256,256]{1,0:T(8,128)(2,1)S(1)} %get-tuple-element.65), channel_id=1, source_target_pairs={{12,0},{16,4},{4,8},{24,12},{28,16},{0,20},{20,24},{8,28},{13,1},{... | collective-permute-start | bytes 393224 | tf_op jit(solution)/shard_map/ppermute | solution.py:493
  58.9 0.9 %collective-permute-done.13.rest_0_ = bf16[256,256]{1,0:T(8,128)(2,1)S(1)} collective-permute-done((bf16[256,256]{1,0:T(8,128)(2,1)S(1)}, bf16[256,256]{1,0:T(8,128)(2,1)S(1)}, u32[]{:S(2)}, u32[]{:S(2)}) %collective-permute-start.13) | collective-permute-done | bytes 131104 | tf_op jit(solution)/shard_map/ppermute | solution.py:493
  60.0 3.0 %collective-permute-done.14.rest_1_ = bf16[256,256]{1,0:T(8,128)(2,1)S(1)} collective-permute-done((bf16[256,256]{1,0:T(8,128)(2,1)S(1)}, bf16[256,256]{1,0:T(8,128)(2,1)S(1)}, u32[]{:S(2)}, u32[]{:S(2)}) %collective-permute-start.14) | collective-permute-done | bytes 131104 | tf_op jit(solution)/shard_map/ppermute | solution.py:493
  63.0 2.2 %collective-permute-done.15.rest_2_ = bf16[256,256]{1,0:T(8,128)(2,1)S(1)} collective-permute-done((bf16[256,256]{1,0:T(8,128)(2,1)S(1)}, bf16[256,256]{1,0:T(8,128)(2,1)S(1)}, u32[]{:S(2)}, u32[]{:S(2)}) %collective-permute-start.15) | collective-permute-done | bytes 131104 | tf_op jit(solution)/shard_map/ppermute | solution.py:493
  65.4 1.6 %collective-permute-done.17.rest_4_ = bf16[256,256]{1,0:T(8,128)(2,1)S(1)} collective-permute-done((bf16[256,256]{1,0:T(8,128)(2,1)S(1)}, bf16[256,256]{1,0:T(8,128)(2,1)S(1)}, u32[]{:S(2)}, u32[]{:S(2)}) %collective-permute-start.17) | collective-permute-done | bytes 131104 | tf_op jit(solution)/shard_map/ppermute | solution.py:493
  66.9 1.8 %base.1.base_ref = f32[2048,256]{1,0:T(8,128)S(1)} custom-call(f32[1,256]{1,0:T(1,128)S(1)} %bitcast.2, f32[2048,256]{1,0:T(8,128)S(1)} %get-tuple-element.50.y_ref, bf16[2048,1536]{1,0:T(8,128)(2,1)S(1)} %get-tuple-element.51.onehot, f32[1,2048]{1,0:T(1,128)S(1)} %add.7.refs_4_.total_ref, bf16[256,256]{1,0:T(8,128)(2,1)S(1)} %collective-permute-done.13.rest_0_, ...), custom_call_target="tpu_custom_call" | custom-call | flops 1610612736 | bytes 4194304 | tf_op jit(solution)/shard_map/base/pallas_call | solution.py:412
  68.8 1.6 %mix.1 = bf16[2048,256]{1,0:T(8,128)(2,1)} custom-call(f32[2048,256]{1,0:T(8,128)S(1)} %base.1.base_ref, bf16[2048,512]{1,0:T(8,128)(2,1)S(1)} %get-tuple-element.48.rest_3_.onehot, bf16[256,256]{1,0:T(8,128)(2,1)S(1)} %collective-permute-done.18.rest_0_, bf16[256,256]{1,0:T(8,128)(2,1)S(1)} %collective-permute-done.19.rest_1_), custom_call_target="tpu_custom_call" | custom-call | flops 536870912 | bytes 4194304 | tf_op jit(solution)/shard_map/mix/pallas_call | solution.py:440
  (46 shorter events, 2.0 us)
Async XLA Ops:
  0.0 0.7 copy-start.8
  0.7 1.4 %copy-start.1 = (bf16[2048,256]{1,0:T(8,128)(2,1)S(1)}, bf16[2048,256]{1,0:T(8,128)(2,1)}, u32[]{:S(2)}) copy-start(bf16[2048,256]{1,0:T(8,128)(2,1)} %k_ref.7) | copy-start | bytes 3145732
  0.7 1.5 %copy-start.2 = (bf16[2048,256]{1,0:T(8,128)(2,1)S(1)}, bf16[2048,256]{1,0:T(8,128)(2,1)}, u32[]{:S(2)}) copy-start(bf16[2048,256]{1,0:T(8,128)(2,1)} %v_ref.7) | copy-start | bytes 3145732
  0.7 1.9 %copy-start.3 = (bf16[2048,256]{1,0:T(8,128)(2,1)S(1)}, bf16[2048,256]{1,0:T(8,128)(2,1)}, u32[]{:S(2)}) copy-start(bf16[2048,256]{1,0:T(8,128)(2,1)} %q_ref.7) | copy-start | bytes 3145732
  2.6 5.2 %copy-start.4 = (bf16[1,256,256]{2,1,0:T(8,128)(2,1)S(1)}, bf16[1,256,256]{2,1,0:T(8,128)(2,1)}, u32[]{:S(2)}) copy-start(bf16[1,256,256]{2,1,0:T(8,128)(2,1)} %one_ref.3) | copy-start | bytes 393220
  2.6 5.2 %copy-start.5 = (bf16[1,256,256]{2,1,0:T(8,128)(2,1)S(1)}, bf16[1,256,256]{2,1,0:T(8,128)(2,1)}, u32[]{:S(2)}) copy-start(bf16[1,256,256]{2,1,0:T(8,128)(2,1)} %three_ref.3) | copy-start | bytes 393220
  2.6 5.2 %copy-start.6 = (bf16[1,256,256]{2,1,0:T(8,128)(2,1)S(1)}, bf16[1,256,256]{2,1,0:T(8,128)(2,1)}, u32[]{:S(2)}) copy-start(bf16[1,256,256]{2,1,0:T(8,128)(2,1)} %two_ref.3) | copy-start | bytes 393220
  2.6 5.2 %copy-start.7 = (f32[2048,1]{0,1:T(1,128)S(1)}, f32[2048,1]{0,1:T(1,128)}, u32[]{:S(2)}) copy-start(f32[2048,1]{0,1:T(1,128)} %param.12) | copy-start | bytes 24580
  4.4 12.9 %collective-permute-start.1 = (bf16[256,768]{1,0:T(8,128)(2,1)S(1)}, bf16[256,768]{1,0:T(8,128)(2,1)S(1)}, u32[]{:S(2)}, u32[]{:S(2)}) collective-permute-start(bf16[256,768]{1,0:T(8,128)(2,1)S(1)} %get-tuple-element.41), channel_id=1, source_target_pairs={{0,28},{4,24},{8,20},{12,16},{16,12},{20,8},{24,4},{28,0},{1,29},{... | collective-permute-start | bytes 1179656 | tf_op jit(solution)/shard_map/ppermute | solution.py:488
  10.7 1.8 %collective-permute-start = (bf16[384,256]{1,0:T(8,128)(2,1)S(1)}, bf16[384,256]{1,0:T(8,128)(2,1)S(1)}, u32[]{:S(2)}, u32[]{:S(2)}) collective-permute-start(bf16[384,256]{1,0:T(8,128)(2,1)S(1)} %get-tuple-element.40), channel_id=1, source_target_pairs={{0,4},{4,0},{8,12},{12,8},{16,20},{20,16},{24,28},{28,24},{1,5},{5... | collective-permute-start | bytes 589832 | tf_op jit(solution)/shard_map/ppermute | solution.py:270
  11.4 23.1 %collective-permute-start.4 = (bf16[256,768]{1,0:T(8,128)(2,1)S(1)}, bf16[256,768]{1,0:T(8,128)(2,1)S(1)}, u32[]{:S(2)}, u32[]{:S(2)}) collective-permute-start(bf16[256,768]{1,0:T(8,128)(2,1)S(1)} %get-tuple-element.44), channel_id=1, source_target_pairs={{0,24},{4,28},{8,16},{12,20},{16,8},{20,12},{24,0},{28,4},{1,25},{... | collective-permute-start | bytes 1179656 | tf_op jit(solution)/shard_map/ppermute | solution.py:488
  17.4 13.6 %collective-permute-start.2 = (bf16[384,256]{1,0:T(8,128)(2,1)S(1)}, bf16[384,256]{1,0:T(8,128)(2,1)S(1)}, u32[]{:S(2)}, u32[]{:S(2)}) collective-permute-start(bf16[384,256]{1,0:T(8,128)(2,1)S(1)} %convert_element_type.6), channel_id=1, source_target_pairs={{0,8},{4,20},{8,0},{12,28},{16,24},{20,4},{24,16},{28,12},{1,9},{5... | collective-permute-start | bytes 589832 | tf_op jit(solution)/shard_map/ppermute | solution.py:282
  19.8 3.4 %copy-start.9 = (s32[1,2048]{1,0:T(1,128)S(1)}, s32[1,2048]{1,0:T(1,128)}, u32[]{:S(2)}) copy-start(s32[1,2048]{1,0:T(1,128)} %order_ref.3) | copy-start | bytes 24580
  21.6 12.9 %collective-permute-start.5 = (bf16[256,768]{1,0:T(8,128)(2,1)S(1)}, bf16[256,768]{1,0:T(8,128)(2,1)S(1)}, u32[]{:S(2)}, u32[]{:S(2)}) collective-permute-start(bf16[256,768]{1,0:T(8,128)(2,1)S(1)} %get-tuple-element.45), channel_id=1, source_target_pairs={{0,20},{4,8},{8,28},{12,0},{16,4},{20,24},{24,12},{28,16},{1,21},{... | collective-permute-start | bytes 1179656 | tf_op jit(solution)/shard_map/ppermute | solution.py:488
  21.7 20.6 %collective-permute-start.7 = (bf16[256,768]{1,0:T(8,128)(2,1)S(1)}, bf16[256,768]{1,0:T(8,128)(2,1)S(1)}, u32[]{:S(2)}, u32[]{:S(2)}) collective-permute-start(bf16[256,768]{1,0:T(8,128)(2,1)S(1)} %get-tuple-element.49), channel_id=1, source_target_pairs={{0,16},{4,12},{8,24},{12,4},{16,0},{20,28},{24,8},{28,20},{1,17},{... | collective-permute-start | bytes 1179656 | tf_op jit(solution)/shard_map/ppermute | solution.py:488
  31.0 7.5 %collective-permute-start.3 = (bf16[384,256]{1,0:T(8,128)(2,1)S(1)}, bf16[384,256]{1,0:T(8,128)(2,1)S(1)}, u32[]{:S(2)}, u32[]{:S(2)}) collective-permute-start(bf16[384,256]{1,0:T(8,128)(2,1)S(1)} %convert_element_type.7), channel_id=1, source_target_pairs={{0,16},{4,12},{8,24},{12,4},{16,0},{20,28},{24,8},{28,20},{1,17},{... | collective-permute-start | bytes 589832 | tf_op jit(solution)/shard_map/ppermute | solution.py:282
  38.6 3.7 %collective-permute-start.6 = (f32[384,256]{1,0:T(8,128)S(1)}, f32[384,256]{1,0:T(8,128)S(1)}, u32[]{:S(2)}, u32[]{:S(2)}) collective-permute-start(f32[384,256]{1,0:T(8,128)S(1)} %merge.5.rest_0_), channel_id=1, source_target_pairs={{0,4},{4,0},{8,12},{12,8},{16,20},{20,16},{24,28},{28,24},{1,5},{5... | collective-permute-start | bytes 1179656 | tf_op jit(solution)/shard_map/ppermute | solution.py:287
  39.3 12.1 %collective-permute-start.10 = (bf16[256,768]{1,0:T(8,128)(2,1)S(1)}, bf16[256,768]{1,0:T(8,128)(2,1)S(1)}, u32[]{:S(2)}, u32[]{:S(2)}) collective-permute-start(bf16[256,768]{1,0:T(8,128)(2,1)S(1)} %get-tuple-element.54), channel_id=1, source_target_pairs={{0,4},{4,0},{8,12},{12,8},{16,20},{20,16},{24,28},{28,24},{1,5},{5... | collective-permute-start | bytes 1179656 | tf_op jit(solution)/shard_map/ppermute | solution.py:488
  39.4 12.0 %collective-permute-start.11 = (bf16[256,768]{1,0:T(8,128)(2,1)S(1)}, bf16[256,768]{1,0:T(8,128)(2,1)S(1)}, u32[]{:S(2)}, u32[]{:S(2)}) collective-permute-start(bf16[256,768]{1,0:T(8,128)(2,1)S(1)} %get-tuple-element.55), channel_id=1, source_target_pairs={{0,8},{4,20},{8,0},{12,28},{16,24},{20,4},{24,16},{28,12},{1,9},{5... | collective-permute-start | bytes 1179656 | tf_op jit(solution)/shard_map/ppermute | solution.py:488
  41.4 10.0 %collective-permute-start.12 = (bf16[256,768]{1,0:T(8,128)(2,1)S(1)}, bf16[256,768]{1,0:T(8,128)(2,1)S(1)}, u32[]{:S(2)}, u32[]{:S(2)}) collective-permute-start(bf16[256,768]{1,0:T(8,128)(2,1)S(1)} %get-tuple-element.56), channel_id=1, source_target_pairs={{0,12},{4,16},{8,4},{12,24},{16,28},{20,0},{24,20},{28,8},{1,13},{... | collective-permute-start | bytes 1179656 | tf_op jit(solution)/shard_map/ppermute | solution.py:488
  45.0 21.9 %copy-start = (f32[256]{0:T(256)S(1)}, f32[256]{0:T(256)}, u32[]{:S(2)}) copy-start(f32[256]{0:T(256)} %param.16) | copy-start | bytes 3076
  45.0 3.7 %collective-permute-start.8 = (f32[1,2048]{1,0:T(1,128)S(1)}, f32[1,2048]{1,0:T(1,128)S(1)}, u32[]{:S(2)}, u32[]{:S(2)}) collective-permute-start(f32[1,2048]{1,0:T(1,128)S(1)} %get-tuple-element.52), channel_id=1, source_target_pairs={{0,1},{1,0},{2,3},{3,2},{4,5},{5,4},{6,7},{7,6},{8,9},{9,8},{10,11... | collective-permute-start | bytes 24584 | tf_op jit(solution)/shard_map/ppermute | solution.py:464
  48.7 9.3 %collective-permute-start.9 = (f32[1,2048]{1,0:T(1,128)S(1)}, f32[1,2048]{1,0:T(1,128)S(1)}, u32[]{:S(2)}, u32[]{:S(2)}) collective-permute-start(f32[1,2048]{1,0:T(1,128)S(1)} %add.6.refs_8_), channel_id=1, source_target_pairs={{0,2},{1,3},{2,0},{3,1},{4,6},{5,7},{6,4},{7,5},{8,10},{9,11},{10,... | collective-permute-start | bytes 24584 | tf_op jit(solution)/shard_map/ppermute | solution.py:464
  52.9 6.9 %collective-permute-start.13 = (bf16[256,256]{1,0:T(8,128)(2,1)S(1)}, bf16[256,256]{1,0:T(8,128)(2,1)S(1)}, u32[]{:S(2)}, u32[]{:S(2)}) collective-permute-start(bf16[256,256]{1,0:T(8,128)(2,1)S(1)} %get-tuple-element.57), channel_id=1, source_target_pairs={{28,0},{24,4},{20,8},{16,12},{12,16},{8,20},{4,24},{0,28},{29,1},{... | collective-permute-start | bytes 393224 | tf_op jit(solution)/shard_map/ppermute | solution.py:493
  55.6 7.4 %collective-permute-start.14 = (bf16[256,256]{1,0:T(8,128)(2,1)S(1)}, bf16[256,256]{1,0:T(8,128)(2,1)S(1)}, u32[]{:S(2)}, u32[]{:S(2)}) collective-permute-start(bf16[256,256]{1,0:T(8,128)(2,1)S(1)} %get-tuple-element.58), channel_id=1, source_target_pairs={{24,0},{28,4},{16,8},{20,12},{8,16},{12,20},{0,24},{4,28},{25,1},{... | collective-permute-start | bytes 393224 | tf_op jit(solution)/shard_map/ppermute | solution.py:493
  55.6 9.6 %collective-permute-start.15 = (bf16[256,256]{1,0:T(8,128)(2,1)S(1)}, bf16[256,256]{1,0:T(8,128)(2,1)S(1)}, u32[]{:S(2)}, u32[]{:S(2)}) collective-permute-start(bf16[256,256]{1,0:T(8,128)(2,1)S(1)} %get-tuple-element.59), channel_id=1, source_target_pairs={{20,0},{8,4},{28,8},{0,12},{4,16},{24,20},{12,24},{16,28},{21,1},{... | collective-permute-start | bytes 393224 | tf_op jit(solution)/shard_map/ppermute | solution.py:493
  56.5 8.9 %collective-permute-start.16 = (bf16[256,256]{1,0:T(8,128)(2,1)S(1)}, bf16[256,256]{1,0:T(8,128)(2,1)S(1)}, u32[]{:S(2)}, u32[]{:S(2)}) collective-permute-start(bf16[256,256]{1,0:T(8,128)(2,1)S(1)} %get-tuple-element.60), channel_id=1, source_target_pairs={{16,0},{12,4},{24,8},{4,12},{0,16},{28,20},{8,24},{20,28},{17,1},{... | collective-permute-start | bytes 393224 | tf_op jit(solution)/shard_map/ppermute | solution.py:493
  58.0 8.9 %collective-permute-start.17 = (bf16[256,256]{1,0:T(8,128)(2,1)S(1)}, bf16[256,256]{1,0:T(8,128)(2,1)S(1)}, u32[]{:S(2)}, u32[]{:S(2)}) collective-permute-start(bf16[256,256]{1,0:T(8,128)(2,1)S(1)} %get-tuple-element.65), channel_id=1, source_target_pairs={{12,0},{16,4},{4,8},{24,12},{28,16},{0,20},{20,24},{8,28},{13,1},{... | collective-permute-start | bytes 393224 | tf_op jit(solution)/shard_map/ppermute | solution.py:493
  59.7 9.0 %collective-permute-start.18 = (bf16[256,256]{1,0:T(8,128)(2,1)S(1)}, bf16[256,256]{1,0:T(8,128)(2,1)S(1)}, u32[]{:S(2)}, u32[]{:S(2)}) collective-permute-start(bf16[256,256]{1,0:T(8,128)(2,1)S(1)} %get-tuple-element.67), channel_id=1, source_target_pairs={{8,0},{20,4},{0,8},{28,12},{24,16},{4,20},{16,24},{12,28},{9,1},{2... | collective-permute-start | bytes 393224 | tf_op jit(solution)/shard_map/ppermute | solution.py:493
  63.0 5.8 %collective-permute-start.19 = (bf16[256,256]{1,0:T(8,128)(2,1)S(1)}, bf16[256,256]{1,0:T(8,128)(2,1)S(1)}, u32[]{:S(2)}, u32[]{:S(2)}) collective-permute-start(bf16[256,256]{1,0:T(8,128)(2,1)S(1)} %get-tuple-element.68), channel_id=1, source_target_pairs={{4,0},{0,4},{12,8},{8,12},{20,16},{16,20},{28,24},{24,28},{5,1},{1... | collective-permute-start | bytes 393224 | tf_op jit(solution)/shard_map/ppermute | solution.py:493

commit v18 on v16

--- a/solution.py
+++ b/solution.py
@@ -284,7 +284,7 @@
             mine = merge(mine, got, after[step])
         else:
             mine = mine + got.astype(F32)
-    return [mine, lax.ppermute(mine, "cam", [(at, at ^ 1) for at in range(n)])]
+    return [mine, lax.ppermute(mine.astype(BF16), "cam", [(at, at ^ 1) for at in range(n)])]
 
 
 def readout_kernel(parts, q_ref, one_ref, three_ref, two_ref, *rest):
@@ -294,7 +294,7 @@
         half = total.shape[0] // 2
         core = lax.axis_index("cam") & 1
         total[pl.ds(pl.multiple_of(core * half, half), half), :] = grads[0][...]
-        total[pl.ds(pl.multiple_of((1 - core) * half, half), half), :] = grads[1][...]
+        total[pl.ds(pl.multiple_of((1 - core) * half, half), half), :] = grads[1][...].astype(F32)
     else:
         total[...] = grads[0][...]
     entries = hid * width

time: 69.9 us -> 69 us (0.987)
  starting transfers between devices: 25.4 us -> 22.9 us
  waiting for transfers between devices: 22 us -> 23.5 us
    ppermute x7, starting transfers between devices: 9.04 us -> 5.73 us  [give_back(): return lax.ppermute(block, 'cam', pairs) if step else block]
    ppermute x7, waiting for transfers between devices: 4.14 us -> 7.21 us  [give_back(): return lax.ppermute(block, 'cam', pairs) if step else block]
    ppermute x2, waiting for transfers between devices: 9.95 us -> 7.69 us  [sum_over_chips(): got = lax.ppermute(mine.astype(BF16), 'cam', pairs)]
    ppermute x1, waiting for transfers between devices: 0.01 us -> 1.07 us  [sum_over_chips(): lax.ppermute(mine.astype(BF16), 'cam', [(at, at ^ 1) for at in range(n)])]
    ppermute x2, starting transfers between devices: 4.27 us -> 5 us  [head_sum(): got = lax.ppermute(square, 'head', pairs)]
where the time goes in v18:
time: 69 us; the launch traced here: 68.8 us
  waiting for transfers between devices  23.5 us (34%)
  starting transfers between devices  22.9 us (33%)
  Pallas kernels  20.8 us (30%)
  local copies, waits for them, and re-layouts  1.17 us (2%)
    ppermute x7, starting transfers between devices, exchange(): return lax.ppermute(block, 'cam', routes(step, n)) if step else block  8.43 us
    ppermute x2, waiting for transfers between devices, sum_over_chips(): got = lax.ppermute(mine.astype(BF16), 'cam', pairs)  7.69 us
    ppermute x7, waiting for transfers between devices, give_back(): return lax.ppermute(block, 'cam', pairs) if step else block  7.21 us
    pallas_call x3, Pallas kernels, sort_tokens(): pl.pallas_call(functools.partial(sort_kernel, size), out_shape=[jax.Shape...  7.06 us
    ppermute x7, starting transfers between devices, give_back(): return lax.ppermute(block, 'cam', pairs) if step else block  5.73 us
    ppermute x2, starting transfers between devices, head_sum(): got = lax.ppermute(square, 'head', pairs)  5 us
    ppermute x7, waiting for transfers between devices, exchange(): return lax.ppermute(block, 'cam', routes(step, n)) if step else block  4.78 us
    pallas_call x1, Pallas kernels, gradients(): pl.pallas_call(functools.partial(grads_kernel, n, split), out_shape=[jax....  2.91 us
  transfers between devices with their start and end apart: 20, of which 10 were waited for; matrix products, arithmetic and copies ran while one was open for 0% of the time, Pallas kernels for 23%

profile of v18, /device:TPU:0, one launch (start us, length us, event | category | flops | bytes accessed | tf_op | source)
XLA Modules:
  0.0 68.8 jit_solution(8428692331095211048)
XLA Ops:
  0.0 0.7 %copy-done.8 = s32[1,2048]{1,0:T(1,128)S(1)} copy-done((s32[1,2048]{1,0:T(1,128)S(1)}, s32[1,2048]{1,0:T(1,128)}, u32[]{:S(2)}) %copy-start.8) | copy-done | bytes 8216
  0.7 1.4 %mark.1 = (bf16[512,2048]{1,0:T(8,128)(2,1)S(1)}, bf16[512,2048]{1,0:T(8,128)(2,1)S(1)}, bf16[1024,2048]{1,0:T(8,128)(2,1)S(1)}, f32[8,128]{1,0:T(8,128)}) custom-call(s32[1,2048]{1,0:T(1,128)S(1)} %copy-done.8), custom_call_target="tpu_custom_call" | custom-call | flops 999999995904 | bytes 1024 | tf_op jit(solution)/shard_map/mark/pallas_call | solution.py:107
  2.6 1.8 %sort_tokens.3 = (bf16[256,768]{1,0:T(8,128)(2,1)S(1)}, bf16[256,768]{1,0:T(8,128)(2,1)S(1)}, f32[8,128]{1,0:T(8,128)S(1)}) custom-call(bf16[512,2048]{1,0:T(8,128)(2,1)S(1)} %get-tuple-element.37.onehot, bf16[2048,256]{1,0:T(8,128)(2,1)S(1)} %copy-done.3, bf16[2048,256]{1,0:T(8,128)(2,1)S(1)} %copy-done.1, bf16[2048,256]{1,0:T(8,128)(2,1)S(1)} %copy-done.2), custom_call_target="tpu_custom_call" | custom-call | flops 1610612736 | bytes 3145728 | tf_op jit(solution)/shard_map/sort_tokens/pallas_call | solution.py:140
  4.4 3.4 %collective-permute-start.1 = (bf16[256,768]{1,0:T(8,128)(2,1)S(1)}, bf16[256,768]{1,0:T(8,128)(2,1)S(1)}, u32[]{:S(2)}, u32[]{:S(2)}) collective-permute-start(bf16[256,768]{1,0:T(8,128)(2,1)S(1)} %get-tuple-element.41), channel_id=1, source_target_pairs={{0,28},{4,24},{8,20},{12,16},{16,12},{20,8},{24,4},{28,0},{1,29},{... | collective-permute-start | bytes 1179656 | tf_op jit(solution)/shard_map/ppermute | solution.py:488
  7.8 2.9 %gradients.1 = (f32[384,256]{1,0:T(8,128)S(1)}, bf16[384,256]{1,0:T(8,128)(2,1)S(1)}) custom-call(bf16[2048,256]{1,0:T(8,128)(2,1)S(1)} %copy-done.1, bf16[2048,256]{1,0:T(8,128)(2,1)S(1)} %copy-done.2, f32[1,2048]{1,0:T(1,128)S(1)} %bitcast.3, bf16[1,256,256]{2,1,0:T(8,128)(2,1)S(1)} %copy-done.4, bf16[1,256,256]{2,1,0:T(8,128)(2,1)S(1)} %copy-done.5, ...), custom_call_target="tpu_custom_call" | custom-call | flops 1610612736 | bytes 4194304 | tf_op jit(solution)/shard_map/gradients/pallas_call | solution.py:236
  10.7 0.7 %collective-permute-start = (bf16[384,256]{1,0:T(8,128)(2,1)S(1)}, bf16[384,256]{1,0:T(8,128)(2,1)S(1)}, u32[]{:S(2)}, u32[]{:S(2)}) collective-permute-start(bf16[384,256]{1,0:T(8,128)(2,1)S(1)} %get-tuple-element.40), channel_id=1, source_target_pairs={{0,4},{4,0},{8,12},{12,8},{16,20},{20,16},{24,28},{28,24},{1,5},{5... | collective-permute-start | bytes 589832 | tf_op jit(solution)/shard_map/ppermute | solution.py:270
  11.5 1.1 %collective-permute-done.got_ref = bf16[384,256]{1,0:T(8,128)(2,1)S(1)} collective-permute-done((bf16[384,256]{1,0:T(8,128)(2,1)S(1)}, bf16[384,256]{1,0:T(8,128)(2,1)S(1)}, u32[]{:S(2)}, u32[]{:S(2)}) %collective-permute-start) | collective-permute-done | bytes 196640 | tf_op jit(solution)/shard_map/ppermute | solution.py:270
  12.5 4.8 %collective-permute-done.1.rest_0_.refs_7_ = bf16[256,768]{1,0:T(8,128)(2,1)S(1)} collective-permute-done((bf16[256,768]{1,0:T(8,128)(2,1)S(1)}, bf16[256,768]{1,0:T(8,128)(2,1)S(1)}, u32[]{:S(2)}, u32[]{:S(2)}) %collective-permute-start.1) | collective-permute-done | bytes 393248 | tf_op jit(solution)/shard_map/ppermute | solution.py:488
  17.4 2.5 %collective-permute-start.2 = (bf16[384,256]{1,0:T(8,128)(2,1)S(1)}, bf16[384,256]{1,0:T(8,128)(2,1)S(1)}, u32[]{:S(2)}, u32[]{:S(2)}) collective-permute-start(bf16[384,256]{1,0:T(8,128)(2,1)S(1)} %convert_element_type.9), channel_id=1, source_target_pairs={{0,8},{4,20},{8,0},{12,28},{16,24},{20,4},{24,16},{28,12},{1,9},{5... | collective-permute-start | bytes 589832 | tf_op jit(solution)/shard_map/ppermute | solution.py:282
  19.8 1.8 %sort_tokens.4 = (bf16[256,768]{1,0:T(8,128)(2,1)S(1)}, bf16[256,768]{1,0:T(8,128)(2,1)S(1)}, f32[8,128]{1,0:T(8,128)S(1)}) custom-call(bf16[512,2048]{1,0:T(8,128)(2,1)S(1)} %get-tuple-element.42.onehot, bf16[2048,256]{1,0:T(8,128)(2,1)S(1)} %copy-done.3, bf16[2048,256]{1,0:T(8,128)(2,1)S(1)} %copy-done.1, bf16[2048,256]{1,0:T(8,128)(2,1)S(1)} %copy-done.2), custom_call_target="tpu_custom_call" | custom-call | flops 1610612736 | bytes 3145728 | tf_op jit(solution)/shard_map/sort_tokens/pallas_call | solution.py:140
  21.7 1.6 %collective-permute-start.7 = (bf16[256,768]{1,0:T(8,128)(2,1)S(1)}, bf16[256,768]{1,0:T(8,128)(2,1)S(1)}, u32[]{:S(2)}, u32[]{:S(2)}) collective-permute-start(bf16[256,768]{1,0:T(8,128)(2,1)S(1)} %get-tuple-element.49), channel_id=1, source_target_pairs={{0,16},{4,12},{8,24},{12,4},{16,0},{20,28},{24,8},{28,20},{1,17},{... | collective-permute-start | bytes 1179656 | tf_op jit(solution)/shard_map/ppermute | solution.py:488
  23.3 7.7 %collective-permute-done.2.got_ref = bf16[384,256]{1,0:T(8,128)(2,1)S(1)} collective-permute-done((bf16[384,256]{1,0:T(8,128)(2,1)S(1)}, bf16[384,256]{1,0:T(8,128)(2,1)S(1)}, u32[]{:S(2)}, u32[]{:S(2)}) %collective-permute-start.2) | collective-permute-done | bytes 196640 | tf_op jit(solution)/shard_map/ppermute | solution.py:282
  31.1 3.5 %sort_tokens.5 = (bf16[256,768]{1,0:T(8,128)(2,1)S(1)}, bf16[256,768]{1,0:T(8,128)(2,1)S(1)}, bf16[256,768]{1,0:T(8,128)(2,1)S(1)}, bf16[256,768]{1,0:T(8,128)(2,1)S(1)}, f32[8,128]{1,0:T(8,128)S(1)}) custom-call(bf16[1024,2048]{1,0:T(8,128)(2,1)S(1)} %get-tuple-element.46.onehot, bf16[2048,256]{1,0:T(8,128)(2,1)S(1)} %copy-done.3, ...), custom_call_target="tpu_custom_call" | custom-call | flops 3221225472 | bytes 3145728 | tf_op jit(solution)/shard_map/sort_tokens/pallas_call | solution.py:140
  34.6 1.1 %collective-permute-start.10 = (bf16[256,768]{1,0:T(8,128)(2,1)S(1)}, bf16[256,768]{1,0:T(8,128)(2,1)S(1)}, u32[]{:S(2)}, u32[]{:S(2)}) collective-permute-start(bf16[256,768]{1,0:T(8,128)(2,1)S(1)} %get-tuple-element.54), channel_id=1, source_target_pairs={{0,4},{4,0},{8,12},{12,8},{16,20},{20,16},{24,28},{28,24},{1,5},{5... | collective-permute-start | bytes 1179656 | tf_op jit(solution)/shard_map/ppermute | solution.py:488
  35.7 1.0 %collective-permute-start.11 = (bf16[256,768]{1,0:T(8,128)(2,1)S(1)}, bf16[256,768]{1,0:T(8,128)(2,1)S(1)}, u32[]{:S(2)}, u32[]{:S(2)}) collective-permute-start(bf16[256,768]{1,0:T(8,128)(2,1)S(1)} %get-tuple-element.55), channel_id=1, source_target_pairs={{0,8},{4,20},{8,0},{12,28},{16,24},{20,4},{24,16},{28,12},{1,9},{5... | collective-permute-start | bytes 1179656 | tf_op jit(solution)/shard_map/ppermute | solution.py:488
  36.7 1.3 %collective-permute-start.12 = (bf16[256,768]{1,0:T(8,128)(2,1)S(1)}, bf16[256,768]{1,0:T(8,128)(2,1)S(1)}, u32[]{:S(2)}, u32[]{:S(2)}) collective-permute-start(bf16[256,768]{1,0:T(8,128)(2,1)S(1)} %get-tuple-element.56), channel_id=1, source_target_pairs={{0,12},{4,16},{8,4},{12,24},{16,28},{20,0},{24,20},{28,8},{1,13},{... | collective-permute-start | bytes 1179656 | tf_op jit(solution)/shard_map/ppermute | solution.py:488
  38.0 1.7 %place.1 = (bf16[2048,1536]{1,0:T(8,128)(2,1)S(1)}, bf16[2048,512]{1,0:T(8,128)(2,1)S(1)}) custom-call(s32[1,2048]{1,0:T(1,128)S(1)} %copy-done.9), custom_call_target="tpu_custom_call" | custom-call | flops 4194304 | bytes 8388608 | tf_op jit(solution)/shard_map/place/pallas_call | solution.py:374
  40.2 1.1 %collective-permute-done.6.rest_1_ = bf16[384,256]{1,0:T(8,128)(2,1)S(1)} collective-permute-done((bf16[384,256]{1,0:T(8,128)(2,1)S(1)}, bf16[384,256]{1,0:T(8,128)(2,1)S(1)}, u32[]{:S(2)}, u32[]{:S(2)}) %collective-permute-start.6) | collective-permute-done | bytes 196640 | tf_op jit(solution)/shard_map/ppermute | solution.py:287
  41.3 2.7 %read_out.1 = (f32[2048,256]{1,0:T(8,128)S(1)}, f32[1,2048]{1,0:T(1,128)S(1)}) custom-call(bf16[2048,256]{1,0:T(8,128)(2,1)S(1)} %copy-done.3, bf16[1,256,256]{2,1,0:T(8,128)(2,1)S(1)} %copy-done.4, bf16[1,256,256]{2,1,0:T(8,128)(2,1)S(1)} %copy-done.5, bf16[1,256,256]{2,1,0:T(8,128)(2,1)S(1)} %copy-done.6, f32[384,256]{1,0:T(8,128)S(1)} %merge.5.rest_0_, ...), custom_call_target="tpu_custom_call" | custom-call | flops 805306368 | bytes 4194304 | tf_op jit(solution)/shard_map/read_out/pallas_call | solution.py:334
  44.0 2.0 %collective-permute-start.8 = (f32[1,2048]{1,0:T(1,128)S(1)}, f32[1,2048]{1,0:T(1,128)S(1)}, u32[]{:S(2)}, u32[]{:S(2)}) collective-permute-start(f32[1,2048]{1,0:T(1,128)S(1)} %get-tuple-element.52), channel_id=1, source_target_pairs={{0,1},{1,0},{2,3},{3,2},{4,5},{5,4},{6,7},{7,6},{8,9},{9,8},{10,11... | collective-permute-start | bytes 24584 | tf_op jit(solution)/shard_map/ppermute | solution.py:464
  46.0 1.7 %collective-permute-done.8 = f32[1,2048]{1,0:T(1,128)S(1)} collective-permute-done((f32[1,2048]{1,0:T(1,128)S(1)}, f32[1,2048]{1,0:T(1,128)S(1)}, u32[]{:S(2)}, u32[]{:S(2)}) %collective-permute-start.8) | collective-permute-done | bytes 8224 | tf_op jit(solution)/shard_map/ppermute | solution.py:464
  47.7 3.0 %collective-permute-start.9 = (f32[1,2048]{1,0:T(1,128)S(1)}, f32[1,2048]{1,0:T(1,128)S(1)}, u32[]{:S(2)}, u32[]{:S(2)}) collective-permute-start(f32[1,2048]{1,0:T(1,128)S(1)} %add.6.refs_8_), channel_id=1, source_target_pairs={{0,2},{1,3},{2,0},{3,1},{4,6},{5,7},{6,4},{7,5},{8,10},{9,11},{10,... | collective-permute-start | bytes 24584 | tf_op jit(solution)/shard_map/ppermute | solution.py:464
  50.7 1.5 %attend.1 = (bf16[256,256]{1,0:T(8,128)(2,1)S(1)}, bf16[256,256]{1,0:T(8,128)(2,1)S(1)}, bf16[256,256]{1,0:T(8,128)(2,1)S(1)}, bf16[256,256]{1,0:T(8,128)(2,1)S(...) custom-call(bf16[256,768]{1,0:T(8,128)(2,1)S(1)} %get-tuple-element., ...), custom_call_target="tpu_custom_call" | custom-call | flops 536870912 | bytes 4194304 | tf_op jit(solution)/shard_map/attend/pallas_call | solution.py:179
  52.2 1.3 %collective-permute-start.13 = (bf16[256,256]{1,0:T(8,128)(2,1)S(1)}, bf16[256,256]{1,0:T(8,128)(2,1)S(1)}, u32[]{:S(2)}, u32[]{:S(2)}) collective-permute-start(bf16[256,256]{1,0:T(8,128)(2,1)S(1)} %get-tuple-element.57), channel_id=1, source_target_pairs={{28,0},{24,4},{20,8},{16,12},{12,16},{8,20},{4,24},{0,28},{29,1},{... | collective-permute-start | bytes 393224 | tf_op jit(solution)/shard_map/ppermute | solution.py:493
  53.5 1.5 %collective-permute-start.14 = (bf16[256,256]{1,0:T(8,128)(2,1)S(1)}, bf16[256,256]{1,0:T(8,128)(2,1)S(1)}, u32[]{:S(2)}, u32[]{:S(2)}) collective-permute-start(bf16[256,256]{1,0:T(8,128)(2,1)S(1)} %get-tuple-element.58), channel_id=1, source_target_pairs={{24,0},{28,4},{16,8},{20,12},{8,16},{12,20},{0,24},{4,28},{25,1},{... | collective-permute-start | bytes 393224 | tf_op jit(solution)/shard_map/ppermute | solution.py:493
  55.0 1.3 %collective-permute-start.15 = (bf16[256,256]{1,0:T(8,128)(2,1)S(1)}, bf16[256,256]{1,0:T(8,128)(2,1)S(1)}, u32[]{:S(2)}, u32[]{:S(2)}) collective-permute-start(bf16[256,256]{1,0:T(8,128)(2,1)S(1)} %get-tuple-element.59), channel_id=1, source_target_pairs={{20,0},{8,4},{28,8},{0,12},{4,16},{24,20},{12,24},{16,28},{21,1},{... | collective-permute-start | bytes 393224 | tf_op jit(solution)/shard_map/ppermute | solution.py:493
  56.3 1.5 %collective-permute-start.16 = (bf16[256,256]{1,0:T(8,128)(2,1)S(1)}, bf16[256,256]{1,0:T(8,128)(2,1)S(1)}, u32[]{:S(2)}, u32[]{:S(2)}) collective-permute-start(bf16[256,256]{1,0:T(8,128)(2,1)S(1)} %get-tuple-element.60), channel_id=1, source_target_pairs={{16,0},{12,4},{24,8},{4,12},{0,16},{28,20},{8,24},{20,28},{17,1},{... | collective-permute-start | bytes 393224 | tf_op jit(solution)/shard_map/ppermute | solution.py:493
  58.0 0.8 %collective-permute-done.13.rest_0_ = bf16[256,256]{1,0:T(8,128)(2,1)S(1)} collective-permute-done((bf16[256,256]{1,0:T(8,128)(2,1)S(1)}, bf16[256,256]{1,0:T(8,128)(2,1)S(1)}, u32[]{:S(2)}, u32[]{:S(2)}) %collective-permute-start.13) | collective-permute-done | bytes 131104 | tf_op jit(solution)/shard_map/ppermute | solution.py:493
  58.8 3.3 %collective-permute-done.14.rest_1_ = bf16[256,256]{1,0:T(8,128)(2,1)S(1)} collective-permute-done((bf16[256,256]{1,0:T(8,128)(2,1)S(1)}, bf16[256,256]{1,0:T(8,128)(2,1)S(1)}, u32[]{:S(2)}, u32[]{:S(2)}) %collective-permute-start.14) | collective-permute-done | bytes 131104 | tf_op jit(solution)/shard_map/ppermute | solution.py:493
  62.1 2.4 %collective-permute-done.15.rest_2_ = bf16[256,256]{1,0:T(8,128)(2,1)S(1)} collective-permute-done((bf16[256,256]{1,0:T(8,128)(2,1)S(1)}, bf16[256,256]{1,0:T(8,128)(2,1)S(1)}, u32[]{:S(2)}, u32[]{:S(2)}) %collective-permute-start.15) | collective-permute-done | bytes 131104 | tf_op jit(solution)/shard_map/ppermute | solution.py:493
  64.7 1.8 %base.1.base_ref = f32[2048,256]{1,0:T(8,128)S(1)} custom-call(f32[1,256]{1,0:T(1,128)S(1)} %bitcast.2, f32[2048,256]{1,0:T(8,128)S(1)} %get-tuple-element.50.y_ref, bf16[2048,1536]{1,0:T(8,128)(2,1)S(1)} %get-tuple-element.51.onehot, f32[1,2048]{1,0:T(1,128)S(1)} %add.7.refs_4_.total_ref, bf16[256,256]{1,0:T(8,128)(2,1)S(1)} %collective-permute-done.13.rest_0_, ...), custom_call_target="tpu_custom_call" | custom-call | flops 1610612736 | bytes 4194304 | tf_op jit(solution)/shard_map/base/pallas_call | solution.py:412
  67.1 1.6 %mix.1 = bf16[2048,256]{1,0:T(8,128)(2,1)} custom-call(f32[2048,256]{1,0:T(8,128)S(1)} %base.1.base_ref, bf16[2048,512]{1,0:T(8,128)(2,1)S(1)} %get-tuple-element.48.rest_3_.onehot, bf16[256,256]{1,0:T(8,128)(2,1)S(1)} %collective-permute-done.18.rest_0_, bf16[256,256]{1,0:T(8,128)(2,1)S(1)} %collective-permute-done.19.rest_1_), custom_call_target="tpu_custom_call" | custom-call | flops 536870912 | bytes 4194304 | tf_op jit(solution)/shard_map/mix/pallas_call | solution.py:440
  (47 shorter events, 2.2 us)
Async XLA Ops:
  0.0 0.7 %copy-start.8 = (s32[1,2048]{1,0:T(1,128)S(1)}, s32[1,2048]{1,0:T(1,128)}, u32[]{:S(2)}) copy-start(s32[1,2048]{1,0:T(1,128)} %order_ref.3) | copy-start | bytes 24580
  0.7 1.4 %copy-start.1 = (bf16[2048,256]{1,0:T(8,128)(2,1)S(1)}, bf16[2048,256]{1,0:T(8,128)(2,1)}, u32[]{:S(2)}) copy-start(bf16[2048,256]{1,0:T(8,128)(2,1)} %k_ref.7) | copy-start | bytes 3145732
  0.7 1.5 %copy-start.2 = (bf16[2048,256]{1,0:T(8,128)(2,1)S(1)}, bf16[2048,256]{1,0:T(8,128)(2,1)}, u32[]{:S(2)}) copy-start(bf16[2048,256]{1,0:T(8,128)(2,1)} %v_ref.7) | copy-start | bytes 3145732
  0.7 1.9 %copy-start.3 = (bf16[2048,256]{1,0:T(8,128)(2,1)S(1)}, bf16[2048,256]{1,0:T(8,128)(2,1)}, u32[]{:S(2)}) copy-start(bf16[2048,256]{1,0:T(8,128)(2,1)} %q_ref.7) | copy-start | bytes 3145732
  2.6 5.2 %copy-start.4 = (bf16[1,256,256]{2,1,0:T(8,128)(2,1)S(1)}, bf16[1,256,256]{2,1,0:T(8,128)(2,1)}, u32[]{:S(2)}) copy-start(bf16[1,256,256]{2,1,0:T(8,128)(2,1)} %one_ref.3) | copy-start | bytes 393220
  2.6 5.2 %copy-start.5 = (bf16[1,256,256]{2,1,0:T(8,128)(2,1)S(1)}, bf16[1,256,256]{2,1,0:T(8,128)(2,1)}, u32[]{:S(2)}) copy-start(bf16[1,256,256]{2,1,0:T(8,128)(2,1)} %three_ref.3) | copy-start | bytes 393220
  2.6 5.2 %copy-start.6 = (bf16[1,256,256]{2,1,0:T(8,128)(2,1)S(1)}, bf16[1,256,256]{2,1,0:T(8,128)(2,1)}, u32[]{:S(2)}) copy-start(bf16[1,256,256]{2,1,0:T(8,128)(2,1)} %two_ref.3) | copy-start | bytes 393220
  2.6 5.2 %copy-start.7 = (f32[2048,1]{0,1:T(1,128)S(1)}, f32[2048,1]{0,1:T(1,128)}, u32[]{:S(2)}) copy-start(f32[2048,1]{0,1:T(1,128)} %param.12) | copy-start | bytes 24580
  4.4 12.9 %collective-permute-start.1 = (bf16[256,768]{1,0:T(8,128)(2,1)S(1)}, bf16[256,768]{1,0:T(8,128)(2,1)S(1)}, u32[]{:S(2)}, u32[]{:S(2)}) collective-permute-start(bf16[256,768]{1,0:T(8,128)(2,1)S(1)} %get-tuple-element.41), channel_id=1, source_target_pairs={{0,28},{4,24},{8,20},{12,16},{16,12},{20,8},{24,4},{28,0},{1,29},{... | collective-permute-start | bytes 1179656 | tf_op jit(solution)/shard_map/ppermute | solution.py:488
  10.7 1.8 %collective-permute-start = (bf16[384,256]{1,0:T(8,128)(2,1)S(1)}, bf16[384,256]{1,0:T(8,128)(2,1)S(1)}, u32[]{:S(2)}, u32[]{:S(2)}) collective-permute-start(bf16[384,256]{1,0:T(8,128)(2,1)S(1)} %get-tuple-element.40), channel_id=1, source_target_pairs={{0,4},{4,0},{8,12},{12,8},{16,20},{20,16},{24,28},{28,24},{1,5},{5... | collective-permute-start | bytes 589832 | tf_op jit(solution)/shard_map/ppermute | solution.py:270
  11.5 24.3 %collective-permute-start.4 = (bf16[256,768]{1,0:T(8,128)(2,1)S(1)}, bf16[256,768]{1,0:T(8,128)(2,1)S(1)}, u32[]{:S(2)}, u32[]{:S(2)}) collective-permute-start(bf16[256,768]{1,0:T(8,128)(2,1)S(1)} %get-tuple-element.44), channel_id=1, source_target_pairs={{0,24},{4,28},{8,16},{12,20},{16,8},{20,12},{24,0},{28,4},{1,25},{... | collective-permute-start | bytes 1179656 | tf_op jit(solution)/shard_map/ppermute | solution.py:488
  17.4 13.6 %collective-permute-start.2 = (bf16[384,256]{1,0:T(8,128)(2,1)S(1)}, bf16[384,256]{1,0:T(8,128)(2,1)S(1)}, u32[]{:S(2)}, u32[]{:S(2)}) collective-permute-start(bf16[384,256]{1,0:T(8,128)(2,1)S(1)} %convert_element_type.9), channel_id=1, source_target_pairs={{0,8},{4,20},{8,0},{12,28},{16,24},{20,4},{24,16},{28,12},{1,9},{5... | collective-permute-start | bytes 589832 | tf_op jit(solution)/shard_map/ppermute | solution.py:282
  21.6 15.1 %collective-permute-start.5 = (bf16[256,768]{1,0:T(8,128)(2,1)S(1)}, bf16[256,768]{1,0:T(8,128)(2,1)S(1)}, u32[]{:S(2)}, u32[]{:S(2)}) collective-permute-start(bf16[256,768]{1,0:T(8,128)(2,1)S(1)} %get-tuple-element.45), channel_id=1, source_target_pairs={{0,20},{4,8},{8,28},{12,0},{16,4},{20,24},{24,12},{28,16},{1,21},{... | collective-permute-start | bytes 1179656 | tf_op jit(solution)/shard_map/ppermute | solution.py:488
  21.7 18.5 %collective-permute-start.7 = (bf16[256,768]{1,0:T(8,128)(2,1)S(1)}, bf16[256,768]{1,0:T(8,128)(2,1)S(1)}, u32[]{:S(2)}, u32[]{:S(2)}) collective-permute-start(bf16[256,768]{1,0:T(8,128)(2,1)S(1)} %get-tuple-element.49), channel_id=1, source_target_pairs={{0,16},{4,12},{8,24},{12,4},{16,0},{20,28},{24,8},{28,20},{1,17},{... | collective-permute-start | bytes 1179656 | tf_op jit(solution)/shard_map/ppermute | solution.py:488
  31.0 8.7 %collective-permute-start.3 = (bf16[384,256]{1,0:T(8,128)(2,1)S(1)}, bf16[384,256]{1,0:T(8,128)(2,1)S(1)}, u32[]{:S(2)}, u32[]{:S(2)}) collective-permute-start(bf16[384,256]{1,0:T(8,128)(2,1)S(1)} %convert_element_type.10), channel_id=1, source_target_pairs={{0,16},{4,12},{8,24},{12,4},{16,0},{20,28},{24,8},{28,20},{1,17},{... | collective-permute-start | bytes 589832 | tf_op jit(solution)/shard_map/ppermute | solution.py:282
  31.1 6.9 %copy-start.9 = (s32[1,2048]{1,0:T(1,128)S(1)}, s32[1,2048]{1,0:T(1,128)}, u32[]{:S(2)}) copy-start(s32[1,2048]{1,0:T(1,128)} %order_ref.3) | copy-start | bytes 24580
  34.6 16.1 %collective-permute-start.10 = (bf16[256,768]{1,0:T(8,128)(2,1)S(1)}, bf16[256,768]{1,0:T(8,128)(2,1)S(1)}, u32[]{:S(2)}, u32[]{:S(2)}) collective-permute-start(bf16[256,768]{1,0:T(8,128)(2,1)S(1)} %get-tuple-element.54), channel_id=1, source_target_pairs={{0,4},{4,0},{8,12},{12,8},{16,20},{20,16},{24,28},{28,24},{1,5},{5... | collective-permute-start | bytes 1179656 | tf_op jit(solution)/shard_map/ppermute | solution.py:488
  35.7 15.0 %collective-permute-start.11 = (bf16[256,768]{1,0:T(8,128)(2,1)S(1)}, bf16[256,768]{1,0:T(8,128)(2,1)S(1)}, u32[]{:S(2)}, u32[]{:S(2)}) collective-permute-start(bf16[256,768]{1,0:T(8,128)(2,1)S(1)} %get-tuple-element.55), channel_id=1, source_target_pairs={{0,8},{4,20},{8,0},{12,28},{16,24},{20,4},{24,16},{28,12},{1,9},{5... | collective-permute-start | bytes 1179656 | tf_op jit(solution)/shard_map/ppermute | solution.py:488
  36.7 14.0 %collective-permute-start.12 = (bf16[256,768]{1,0:T(8,128)(2,1)S(1)}, bf16[256,768]{1,0:T(8,128)(2,1)S(1)}, u32[]{:S(2)}, u32[]{:S(2)}) collective-permute-start(bf16[256,768]{1,0:T(8,128)(2,1)S(1)} %get-tuple-element.56), channel_id=1, source_target_pairs={{0,12},{4,16},{8,4},{12,24},{16,28},{20,0},{24,20},{28,8},{1,13},{... | collective-permute-start | bytes 1179656 | tf_op jit(solution)/shard_map/ppermute | solution.py:488
  39.8 1.5 %collective-permute-start.6 = (bf16[384,256]{1,0:T(8,128)(2,1)S(1)}, bf16[384,256]{1,0:T(8,128)(2,1)S(1)}, u32[]{:S(2)}, u32[]{:S(2)}) collective-permute-start(bf16[384,256]{1,0:T(8,128)(2,1)S(1)} %convert_element_type.11), channel_id=1, source_target_pairs={{0,4},{4,0},{8,12},{12,8},{16,20},{20,16},{24,28},{28,24},{1,5},{5... | collective-permute-start | bytes 589832 | tf_op jit(solution)/shard_map/ppermute | solution.py:287
  44.0 20.7 %copy-start = (f32[256]{0:T(256)S(1)}, f32[256]{0:T(256)}, u32[]{:S(2)}) copy-start(f32[256]{0:T(256)} %param.16) | copy-start | bytes 3076
  44.0 3.7 %collective-permute-start.8 = (f32[1,2048]{1,0:T(1,128)S(1)}, f32[1,2048]{1,0:T(1,128)S(1)}, u32[]{:S(2)}, u32[]{:S(2)}) collective-permute-start(f32[1,2048]{1,0:T(1,128)S(1)} %get-tuple-element.52), channel_id=1, source_target_pairs={{0,1},{1,0},{2,3},{3,2},{4,5},{5,4},{6,7},{7,6},{8,9},{9,8},{10,11... | collective-permute-start | bytes 24584 | tf_op jit(solution)/shard_map/ppermute | solution.py:464
  47.7 10.2 %collective-permute-start.9 = (f32[1,2048]{1,0:T(1,128)S(1)}, f32[1,2048]{1,0:T(1,128)S(1)}, u32[]{:S(2)}, u32[]{:S(2)}) collective-permute-start(f32[1,2048]{1,0:T(1,128)S(1)} %add.6.refs_8_), channel_id=1, source_target_pairs={{0,2},{1,3},{2,0},{3,1},{4,6},{5,7},{6,4},{7,5},{8,10},{9,11},{10,... | collective-permute-start | bytes 24584 | tf_op jit(solution)/shard_map/ppermute | solution.py:464
  52.2 6.6 %collective-permute-start.13 = (bf16[256,256]{1,0:T(8,128)(2,1)S(1)}, bf16[256,256]{1,0:T(8,128)(2,1)S(1)}, u32[]{:S(2)}, u32[]{:S(2)}) collective-permute-start(bf16[256,256]{1,0:T(8,128)(2,1)S(1)} %get-tuple-element.57), channel_id=1, source_target_pairs={{28,0},{24,4},{20,8},{16,12},{12,16},{8,20},{4,24},{0,28},{29,1},{... | collective-permute-start | bytes 393224 | tf_op jit(solution)/shard_map/ppermute | solution.py:493
  53.5 8.6 %collective-permute-start.14 = (bf16[256,256]{1,0:T(8,128)(2,1)S(1)}, bf16[256,256]{1,0:T(8,128)(2,1)S(1)}, u32[]{:S(2)}, u32[]{:S(2)}) collective-permute-start(bf16[256,256]{1,0:T(8,128)(2,1)S(1)} %get-tuple-element.58), channel_id=1, source_target_pairs={{24,0},{28,4},{16,8},{20,12},{8,16},{12,20},{0,24},{4,28},{25,1},{... | collective-permute-start | bytes 393224 | tf_op jit(solution)/shard_map/ppermute | solution.py:493
  55.0 9.5 %collective-permute-start.15 = (bf16[256,256]{1,0:T(8,128)(2,1)S(1)}, bf16[256,256]{1,0:T(8,128)(2,1)S(1)}, u32[]{:S(2)}, u32[]{:S(2)}) collective-permute-start(bf16[256,256]{1,0:T(8,128)(2,1)S(1)} %get-tuple-element.59), channel_id=1, source_target_pairs={{20,0},{8,4},{28,8},{0,12},{4,16},{24,20},{12,24},{16,28},{21,1},{... | collective-permute-start | bytes 393224 | tf_op jit(solution)/shard_map/ppermute | solution.py:493
  56.3 8.4 %collective-permute-start.16 = (bf16[256,256]{1,0:T(8,128)(2,1)S(1)}, bf16[256,256]{1,0:T(8,128)(2,1)S(1)}, u32[]{:S(2)}, u32[]{:S(2)}) collective-permute-start(bf16[256,256]{1,0:T(8,128)(2,1)S(1)} %get-tuple-element.60), channel_id=1, source_target_pairs={{16,0},{12,4},{24,8},{4,12},{0,16},{28,20},{8,24},{20,28},{17,1},{... | collective-permute-start | bytes 393224 | tf_op jit(solution)/shard_map/ppermute | solution.py:493
  57.9 6.8 %collective-permute-start.17 = (bf16[256,256]{1,0:T(8,128)(2,1)S(1)}, bf16[256,256]{1,0:T(8,128)(2,1)S(1)}, u32[]{:S(2)}, u32[]{:S(2)}) collective-permute-start(bf16[256,256]{1,0:T(8,128)(2,1)S(1)} %get-tuple-element.65), channel_id=1, source_target_pairs={{4,0},{0,4},{12,8},{8,12},{20,16},{16,20},{28,24},{24,28},{5,1},{1... | collective-permute-start | bytes 393224 | tf_op jit(solution)/shard_map/ppermute | solution.py:493
  58.8 7.8 %collective-permute-start.18 = (bf16[256,256]{1,0:T(8,128)(2,1)S(1)}, bf16[256,256]{1,0:T(8,128)(2,1)S(1)}, u32[]{:S(2)}, u32[]{:S(2)}) collective-permute-start(bf16[256,256]{1,0:T(8,128)(2,1)S(1)} %get-tuple-element.67), channel_id=1, source_target_pairs={{12,0},{16,4},{4,8},{24,12},{28,16},{0,20},{20,24},{8,28},{13,1},{... | collective-permute-start | bytes 393224 | tf_op jit(solution)/shard_map/ppermute | solution.py:493
  62.1 5.0 %collective-permute-start.19 = (bf16[256,256]{1,0:T(8,128)(2,1)S(1)}, bf16[256,256]{1,0:T(8,128)(2,1)S(1)}, u32[]{:S(2)}, u32[]{:S(2)}) collective-permute-start(bf16[256,256]{1,0:T(8,128)(2,1)S(1)} %get-tuple-element.68), channel_id=1, source_target_pairs={{8,0},{20,4},{0,8},{28,12},{24,16},{4,20},{16,24},{12,28},{9,1},{2... | collective-permute-start | bytes 393224 | tf_op jit(solution)/shard_map/ppermute | solution.py:493
